TPU v7x, 32 devices: a whole 2x2x4 slice. The times are simulated.
32 devices in a mesh: dp: 4 (over y, core), mp: 8 (over z, x).
Axes of the slice: x: 2, y: 2, z: 4, core: 2. Of those that a mesh axis runs over, the one named last changes fastest.
Arguments:
- skip_stream_arriving: float32 [1024, 2304], P('dp', 'mp'), may hold values from -170 to 170
- chosen_specialists: int32 [1024, 2], P('dp'), may hold values from 0 to 3, all different within a row; in each aligned block of 256 rows (0 to 255, 256 to 511, ...) at most 160 rows name the same one
- sequence_piece_tallies: int32 [4, 4], P('dp'), may hold values from 1 to 128, 256 in all within a row
- premix_rmsnorm_gain: float32 [2304], P('mp'), may hold values from 0.1 to 1.9
- dispatcher_weights: bfloat16 [2304, 4], replicated, may hold values from -0.125 to 0.125
- specialist_switch_weights: bfloat16 [4, 2304, 5760], P(None, 'dp', 'mp'), may hold values from -0.125 to 0.125
- specialist_expand_weights: bfloat16 [4, 2304, 5760], P(None, 'dp', 'mp'), may hold values from -0.125 to 0.125
- specialist_contract_weights: bfloat16 [4, 5760, 2304], P(None, 'mp', 'dp'), may hold values from -0.109375 to 0.109375
- terminal_rmsnorm_gain: float32 [2304], replicated, may hold values from 0.1 to 1.9
- lexicon_projector_weights: bfloat16 [2304, 16384], P(None, ('dp', 'mp')), may hold values from -12 to 12
- softness_per_sequence: float32 [16], replicated, may hold values from 0.02 to 1.5
Outputs:
- new_hidden: float32 [1024, 2304], P('dp', 'mp')
- logprobs: float32 [16, 16384], P(None, ('dp', 'mp'))
Inputs may be any that keep to these rules, and one draw needn't show every extreme that they name: `chosen_specialists`: in the 256 rows of each data group no expert is named by more than 160 rows, a bound that some block reaches. `sequence_piece_tallies`: each row sums to 256; its largest entry is 128.
All inputs are finite; a program needn't handle non-finite values.
Results may differ from a plain program's by a relative error of at most 0.0014.
Values may be sent and summed in bfloat16 or wider, within the bound.
No kernel may reach another device: no remote copies, remote signals or barrier semaphores. Data moves between devices by JAX's collectives and lax.ppermute only.
A program may use at most 128 MiB of HBM per device.

v0:
```python
import math

import jax
import jax.numpy as jnp
from jax import lax
from jax.sharding import PartitionSpec as P

EMBED_DIMENSION = 2304
CAP = 160


branch_scale = 1.4 / math.sqrt(40.0)
epsilon = 1e-05


def slot_tables(routes_grp, expert, capacity):
    count = routes_grp.shape[0]
    hit = jnp.any(routes_grp == expert, axis=1)
    second = (routes_grp[:, 1] == expert).astype(jnp.int32)
    order = jnp.cumsum(hit.astype(jnp.int32), dtype=jnp.int32) - 1
    target = jnp.where(hit, order, capacity)
    tokens = jnp.arange(count, dtype=jnp.int32)
    slot_rows = jnp.zeros((capacity,), jnp.int32).at[target].set(tokens, mode="drop")
    live = jnp.zeros((capacity,), jnp.float32).at[target].set(1.0, mode="drop")
    which = jnp.zeros((capacity,), jnp.int32).at[target].set(second, mode="drop")
    return (slot_rows, live, which)


def body(
    skip_stream_arriving,
    chosen_specialists,
    sequence_piece_tallies,
    premix_rmsnorm_gain,
    dispatcher_weights,
    specialist_switch_weights,
    specialist_expand_weights,
    specialist_contract_weights,
    terminal_rmsnorm_gain,
    lexicon_projector_weights,
    softness_per_sequence,
):
    tok_rows = skip_stream_arriving.shape[0]
    local_width = skip_stream_arriving.shape[1]
    experts = specialist_switch_weights.shape[0]
    unit_cols = specialist_switch_weights.shape[2]
    squares = lax.psum(jnp.sum(skip_stream_arriving * skip_stream_arriving, axis=1), "mp")
    normed_local = (
        skip_stream_arriving
        * lax.rsqrt(squares / EMBED_DIMENSION + epsilon)[:, None]
        * premix_rmsnorm_gain
    ).astype(jnp.bfloat16)
    features = lax.all_gather(normed_local, "mp", axis=1, tiled=True)
    router = jnp.dot(features, dispatcher_weights, preferred_element_type=jnp.float32)
    mixing = jax.nn.softmax(jnp.take_along_axis(router, chosen_specialists, axis=1), axis=1)
    tables = [slot_tables(chosen_specialists, expert, CAP) for expert in range(experts)]
    inputs = jnp.stack([features[table[0]] for table in tables])
    scales = jnp.stack([mixing[table[0], table[2]] * table[1] for table in tables])
    pieces_out = []
    for expert in range(experts):
        rows_in = inputs[expert]

        def add_pair(carry, pieces, start, rows_in=rows_in):
            return (
                jnp.dot(rows_in, pieces[0], preferred_element_type=jnp.float32),
                jnp.dot(rows_in, pieces[1], preferred_element_type=jnp.float32),
            )

        empty = jnp.zeros((CAP, unit_cols), jnp.float32)
        gate, up_part = add_pair(
            (empty, empty),
            (
                lax.all_gather(specialist_switch_weights[expert], "dp", axis=0, tiled=True),
                lax.all_gather(specialist_expand_weights[expert], "dp", axis=0, tiled=True),
            ),
            jnp.int32(0),
        )
        act = (jax.nn.silu(gate) * up_part).astype(jnp.bfloat16)

        def project(piece, start, act=act):
            return jnp.dot(act, piece, preferred_element_type=jnp.float32)

        pieces_out.append(
            project(
                lax.all_gather(specialist_contract_weights[expert], "dp", axis=1, tiled=True),
                jnp.int32(0),
            )
        )
    outputs = jnp.stack(pieces_out)
    combined = jnp.zeros((tok_rows, EMBED_DIMENSION), jnp.float32)
    for expert in range(experts):
        combined = combined.at[tables[expert][0]].add(outputs[expert] * scales[expert][:, None])
    branch = lax.psum_scatter(
        combined.astype(jnp.bfloat16), "mp", scatter_dimension=1, tiled=True
    ).astype(jnp.float32)
    new_hidden = skip_stream_arriving + branch_scale * branch
    ends_index = jnp.cumsum(sequence_piece_tallies[0], dtype=jnp.int32) - 1
    end_local = new_hidden[ends_index]
    groups = lax.axis_size("dp")
    columns_count = lax.axis_size("mp")
    req_count = ends_index.shape[0]
    end_squares = lax.psum(jnp.sum(end_local * end_local, axis=1), "mp")
    gain_local = lax.dynamic_slice_in_dim(
        terminal_rmsnorm_gain, lax.axis_index("mp") * local_width, local_width
    )
    end_normed = (
        end_local * lax.rsqrt(end_squares / EMBED_DIMENSION + epsilon)[:, None] * gain_local
    ).astype(jnp.bfloat16)
    shaped = lax.all_gather(end_normed[None], ("dp", "mp"), axis=0, tiled=True).reshape(
        groups, columns_count, req_count, local_width
    )
    lexicon_projector_feed = shaped.transpose(0, 2, 1, 3).reshape(
        groups * req_count, columns_count * local_width
    )
    lexicon_logit_values = jnp.dot(
        lexicon_projector_feed, lexicon_projector_weights, preferred_element_type=jnp.float32
    ) / (EMBED_DIMENSION / 256.0 * softness_per_sequence[:, None])
    largest = lax.pmax(jnp.max(lexicon_logit_values, axis=1), ("dp", "mp"))
    total_exp = lax.psum(
        jnp.sum(jnp.exp(lexicon_logit_values - largest[:, None]), axis=1), ("dp", "mp")
    )
    logprobs = lexicon_logit_values - largest[:, None] - jnp.log(total_exp)[:, None]
    return (new_hidden, logprobs)


def solution(mesh):
    return jax.shard_map(
        body,
        mesh=mesh,
        in_specs=(
            P("dp", "mp"),
            P("dp", None),
            P("dp", None),
            P("mp"),
            P(),
            P(None, "dp", "mp"),
            P(None, "dp", "mp"),
            P(None, "mp", "dp"),
            P(),
            P(None, ("dp", "mp")),
            P(),
        ),
        out_specs=(P("dp", "mp"), P(None, ("dp", "mp"))),
        check_vma=False,
    )
```

profile of v0, /device:TPU:4, one launch (start us, length us, event | category | flops | bytes accessed | tf_op | source)
XLA Modules:
  0.0 713.5 jit_solution(12775711100678235528)
XLA Ops:
  8.4 21.6 %psum.21 = f32[256]{0:T(256)S(1)} all-reduce(f32[256]{0:T(256)S(1)} %multiply_reduce_fusion), channel_id=1, replica_groups=mesh['dp'=4,'mp'=8] {'mp'}, use_global_device_ids=true, to_apply=%region_5.6 | all-reduce | flops 256 | bytes 2048 | tf_op jit(solution)/shard_map/psum | solution.py:46
  30.0 1.7 multiply_convert_fusion
  31.9 3.8 fusion.124
  35.7 4.0 fusion.125
  39.8 3.8 fusion.126
  56.1 1.9 scatter_custom_fusion.6
  58.0 1.9 scatter_custom_fusion.2
  62.7 2.0 scatter_custom_fusion.10
  67.7 2.0 scatter_custom_fusion.14
  77.0 4.9 gather_fusion.9
  82.1 2.6 gather_fusion.3
  84.7 2.6 gather_fusion.1
  87.3 1.6 copy.22
  88.9 2.1 gather_fusion.2
  91.0 2.1 gather_fusion
  93.1 2.6 gather_fusion.5
  95.7 2.1 gather_fusion.4
  97.8 2.5 gather_fusion.7
  100.3 2.2 gather_fusion.6
  105.3 3.8 fusion.18
  109.1 23.6 %all-gather.30.cloned.1.call-done = bf16[1,2304,720]{2,1,0:T(8,128)(2,1)} async-done(((bf16[1,576,720]{2,1,0:T(8,128)(2,1)}), bf16[1,2304,720]{2,1,0:T(8,128)(2,1)}) %all-gather.30.cloned.1.call-update) | async-done | bytes 3317776 | tf_op jit(solution)/shard_map/all_gather | solution.py:73
  132.7 32.2 %all-gather.32.cloned.1.call-done = bf16[1,720,2304]{1,2,0:T(8,128)(2,1)} async-done(((bf16[1,720,576]{1,2,0:T(8,128)(2,1)}), bf16[1,720,2304]{1,2,0:T(8,128)(2,1)}) %all-gather.32.cloned.1.call-update) | async-done | bytes 3317776 | tf_op jit(solution)/shard_map/all_gather | solution.py:84
  164.9 6.3 convolution_multiply_fusion.3
  171.2 5.2 scatter_custom_fusion.3
  176.5 20.7 %all-gather.34.cloned.1.call-done = bf16[1,2304,720]{2,1,0:T(8,128)(2,1)} async-done(((bf16[1,576,720]{2,1,0:T(8,128)(2,1)}), bf16[1,2304,720]{2,1,0:T(8,128)(2,1)}) %all-gather.34.cloned.1.call-update) | async-done | bytes 3317776 | tf_op jit(solution)/shard_map/all_gather | solution.py:72
  197.1 3.5 fusion.13
  200.7 28.7 %all-gather.36.cloned.1.call-done = bf16[1,2304,720]{2,1,0:T(8,128)(2,1)} async-done(((bf16[1,576,720]{2,1,0:T(8,128)(2,1)}), bf16[1,2304,720]{2,1,0:T(8,128)(2,1)}) %all-gather.36.cloned.1.call-update) | async-done | bytes 3317776 | tf_op jit(solution)/shard_map/all_gather | solution.py:73
  229.3 32.4 %all-gather.38.cloned.1.call-done = bf16[1,720,2304]{1,2,0:T(8,128)(2,1)} async-done(((bf16[1,720,576]{1,2,0:T(8,128)(2,1)}), bf16[1,720,2304]{1,2,0:T(8,128)(2,1)}) %all-gather.38.cloned.1.call-update) | async-done | bytes 3317776 | tf_op jit(solution)/shard_map/all_gather | solution.py:84
  261.7 6.3 convolution_multiply_fusion.2
  268.0 6.7 scatter_fusion
  274.7 19.4 %all-gather.40.cloned.1.call-done = bf16[1,2304,720]{2,1,0:T(8,128)(2,1)} async-done(((bf16[1,576,720]{2,1,0:T(8,128)(2,1)}), bf16[1,2304,720]{2,1,0:T(8,128)(2,1)}) %all-gather.40.cloned.1.call-update) | async-done | bytes 3317776 | tf_op jit(solution)/shard_map/all_gather | solution.py:72
  294.1 3.5 fusion.8
  297.6 28.8 %all-gather.42.cloned.1.call-done = bf16[1,2304,720]{2,1,0:T(8,128)(2,1)} async-done(((bf16[1,576,720]{2,1,0:T(8,128)(2,1)}), bf16[1,2304,720]{2,1,0:T(8,128)(2,1)}) %all-gather.42.cloned.1.call-update) | async-done | bytes 3317776 | tf_op jit(solution)/shard_map/all_gather | solution.py:73
  326.4 32.2 %all-gather.44.cloned.1.call-done = bf16[1,720,2304]{1,2,0:T(8,128)(2,1)} async-done(((bf16[1,720,576]{1,2,0:T(8,128)(2,1)}), bf16[1,720,2304]{1,2,0:T(8,128)(2,1)}) %all-gather.44.cloned.1.call-update) | async-done | bytes 3317776 | tf_op jit(solution)/shard_map/all_gather | solution.py:84
  358.6 6.3 convolution_multiply_fusion.1
  365.0 6.9 scatter_fusion.1
  371.9 19.1 %all-gather.46.cloned.1.call-done = bf16[1,2304,720]{2,1,0:T(8,128)(2,1)} async-done(((bf16[1,576,720]{2,1,0:T(8,128)(2,1)}), bf16[1,2304,720]{2,1,0:T(8,128)(2,1)}) %all-gather.46.cloned.1.call-update) | async-done | bytes 3317776 | tf_op jit(solution)/shard_map/all_gather | solution.py:72
  391.0 3.5 fusion.3
  394.6 28.7 %all-gather.48.cloned.1.call-done = bf16[1,2304,720]{2,1,0:T(8,128)(2,1)} async-done(((bf16[1,576,720]{2,1,0:T(8,128)(2,1)}), bf16[1,2304,720]{2,1,0:T(8,128)(2,1)}) %all-gather.48.cloned.1.call-update) | async-done | bytes 3317776 | tf_op jit(solution)/shard_map/all_gather | solution.py:73
  423.2 32.4 %all-gather.50.cloned.1.call-done = bf16[1,720,2304]{1,2,0:T(8,128)(2,1)} async-done(((bf16[1,720,576]{1,2,0:T(8,128)(2,1)}), bf16[1,720,2304]{1,2,0:T(8,128)(2,1)}) %all-gather.50.cloned.1.call-update) | async-done | bytes 3317776 | tf_op jit(solution)/shard_map/all_gather | solution.py:84
  455.6 6.3 convolution_multiply_fusion
  461.9 6.5 scatter_fusion.2
  468.4 1.8 convert_element_type.104
  473.0 64.5 %reduce-scatter.4.cloned.1.call-done = bf16[288,256]{1,0:T(8,128)(2,1)} async-done(((bf16[2304,256]{1,0:T(8,128)(2,1)}), bf16[288,256]{1,0:T(8,128)(2,1)}) %reduce-scatter.4.cloned.1.call-update) | async-done | bytes 147472
  540.1 19.4 %psum.22 = f32[4]{0:T(128)S(1)} all-reduce(f32[4]{0:T(128)S(1)} %multiply_reduce_fusion.1), channel_id=1, replica_groups=mesh['dp'=4,'mp'=8] {'mp'}, use_global_device_ids=true, to_apply=%region_35.36 | all-reduce | flops 4 | bytes 32 | tf_op jit(solution)/shard_map/psum | solution.py:101
  559.6 63.8 %all_gather.55 = bf16[32,4,288]{2,1,0:T(4,128)(2,1)S(1)} all-gather(bf16[1,4,288]{2,1,0:T(4,128)(2,1)S(1)} %fusion.79), channel_id=1, replica_groups=mesh['dp'=4,'mp'=8] {'dp','mp'}, dimensions={0}, use_global_device_ids=true | all-gather | bytes 76032 | tf_op jit(solution)/shard_map/all_gather | solution.py:108
  624.1 39.4 %pmax.7 = f32[16]{0:T(128)S(1)} all-reduce(f32[16]{0:T(128)S(1)} %get-tuple-element.38), channel_id=1, replica_groups=mesh['dp'=4,'mp'=8] {'dp','mp'}, use_global_device_ids=true, to_apply=%region_37.38 | all-reduce | flops 16 | bytes 128 | tf_op jit(solution)/shard_map/pmax | solution.py:117
  664.5 41.3 %psum.23 = f32[16]{0:T(128)S(1)} all-reduce(f32[16]{0:T(128)S(1)} %exponential_reduce_fusion), channel_id=1, replica_groups=mesh['dp'=4,'mp'=8] {'dp','mp'}, use_global_device_ids=true, to_apply=%region_39.40 | all-reduce | flops 16 | bytes 128 | tf_op jit(solution)/shard_map/psum | solution.py:118
  (154 shorter events, 37.4 us)
Async XLA Ops:
  7.2 616.4 %copy-start = (bf16[2304,512]{1,0:T(8,128)(2,1)S(1)}, bf16[2304,512]{1,0:T(8,128)(2,1)}, u32[]{:S(2)}) copy-start(bf16[2304,512]{1,0:T(8,128)(2,1)} %param.20) | copy-start | bytes 7077892
  7.2 68.3 %all-gather.26.cloned.1.call-start = ((), (), s32[]{:S(2)}) async-start(), calls=%async_computation.1 | async-start | bytes 1327104 | tf_op jit(solution)/shard_map/all_gather | solution.py:52
  31.8 73.5 %all-gather.28.cloned.1.call-start = ((), (), s32[]{:S(2)}) async-start(), calls=%async_computation.2 | async-start | bytes 4423680 | tf_op jit(solution)/shard_map/all_gather | solution.py:72
  35.7 97.0 %all-gather.30.cloned.1.call-start = ((), (), s32[]{:S(2)}) async-start(), calls=%async_computation.3 | async-start | bytes 4423680 | tf_op jit(solution)/shard_map/all_gather | solution.py:73
  39.7 125.2 %all-gather.32.cloned.1.call-start = ((), (), s32[]{:S(2)}) async-start(), calls=%async_computation.4 | async-start | bytes 4423680 | tf_op jit(solution)/shard_map/all_gather | solution.py:84
  43.6 153.5 %all-gather.34.cloned.1.call-start = ((), (), s32[]{:S(2)}) async-start(), calls=%async_computation.5 | async-start | bytes 4423680 | tf_op jit(solution)/shard_map/all_gather | solution.py:72
  44.2 185.1 %all-gather.36.cloned.1.call-start = ((), (), s32[]{:S(2)}) async-start(), calls=%async_computation.6 | async-start | bytes 4423680 | tf_op jit(solution)/shard_map/all_gather | solution.py:73
  44.8 216.9 %all-gather.38.cloned.1.call-start = ((), (), s32[]{:S(2)}) async-start(), calls=%async_computation.7 | async-start | bytes 4423680 | tf_op jit(solution)/shard_map/all_gather | solution.py:84
  45.5 248.5 %all-gather.40.cloned.1.call-start = ((), (), s32[]{:S(2)}) async-start(), calls=%async_computation.8 | async-start | bytes 4423680 | tf_op jit(solution)/shard_map/all_gather | solution.py:72
  46.3 3.4 copy-start.5
  46.3 280.1 %all-gather.42.cloned.1.call-start = ((), (), s32[]{:S(2)}) async-start(), calls=%async_computation.9 | async-start | bytes 4423680 | tf_op jit(solution)/shard_map/all_gather | solution.py:73
  46.3 29.1 %copy-start.6 = (bf16[2304,4]{0,1:T(4,128)(2,1)S(1)}, bf16[2304,4]{0,1:T(4,128)(2,1)}, u32[]{:S(2)}) copy-start(bf16[2304,4]{0,1:T(4,128)(2,1)} %param.15) | copy-start | bytes 55300
  47.0 311.6 %all-gather.44.cloned.1.call-start = ((), (), s32[]{:S(2)}) async-start(), calls=%async_computation.10 | async-start | bytes 4423680 | tf_op jit(solution)/shard_map/all_gather | solution.py:84
  47.6 343.4 %all-gather.46.cloned.1.call-start = ((), (), s32[]{:S(2)}) async-start(), calls=%async_computation.11 | async-start | bytes 4423680 | tf_op jit(solution)/shard_map/all_gather | solution.py:72
  48.4 374.9 %all-gather.48.cloned.1.call-start = ((), (), s32[]{:S(2)}) async-start(), calls=%async_computation.12 | async-start | bytes 4423680 | tf_op jit(solution)/shard_map/all_gather | solution.py:73
  48.9 406.7 %all-gather.50.cloned.1.call-start = ((), (), s32[]{:S(2)}) async-start(), calls=%async_computation.13 | async-start | bytes 4423680 | tf_op jit(solution)/shard_map/all_gather | solution.py:84
  49.7 487.8 %reduce-scatter.4.cloned.1.call-start = ((), (), s32[]{:S(2)}) async-start(), calls=%async_computation.14 | async-start | bytes 1327104
  55.1 0.6 copy-start.7
  72.5 0.5 copy-start.17
  73.7 0.6 copy-start.11
  74.8 0.6 copy-start.9
  100.3 2.3 copy-start.13
  100.3 2.9 copy-start.14
  100.3 3.6 copy-start.15
  100.3 4.3 copy-start.16
  105.3 59.7 %copy-start.4 = (bf16[160,2304]{1,0:T(8,128)(2,1)S(1)}, bf16[160,2304]{1,0:T(8,128)(2,1)}, u32[]{:S(2)}) copy-start(bf16[160,2304]{1,0:T(8,128)(2,1)} %gather_fusion) | copy-start | bytes 2211844
  171.2 25.9 %copy-start.3 = (bf16[160,2304]{1,0:T(8,128)(2,1)S(1)}, bf16[160,2304]{1,0:T(8,128)(2,1)}, u32[]{:S(2)}) copy-start(bf16[160,2304]{1,0:T(8,128)(2,1)} %gather_fusion.2) | copy-start | bytes 2211844
  200.7 67.4 %copy-start.8 = (s32[160]{0:T(256)S(1)}, s32[160]{0:T(256)}, u32[]{:S(2)}) copy-start(s32[160]{0:T(256)} %copy-done.7) | copy-start | bytes 1924
  268.0 26.0 %copy-start.2 = (bf16[160,2304]{1,0:T(8,128)(2,1)S(1)}, bf16[160,2304]{1,0:T(8,128)(2,1)}, u32[]{:S(2)}) copy-start(bf16[160,2304]{1,0:T(8,128)(2,1)} %gather_fusion.4) | copy-start | bytes 2211844
  297.6 67.4 %copy-start.12 = (s32[160]{0:T(256)S(1)}, s32[160]{0:T(256)}, u32[]{:S(2)}) copy-start(s32[160]{0:T(256)} %copy-done.11) | copy-start | bytes 1924
  365.0 26.0 %copy-start.1 = (bf16[160,2304]{1,0:T(8,128)(2,1)S(1)}, bf16[160,2304]{1,0:T(8,128)(2,1)}, u32[]{:S(2)}) copy-start(bf16[160,2304]{1,0:T(8,128)(2,1)} %gather_fusion.6) | copy-start | bytes 2211844
  394.6 67.4 %copy-start.10 = (s32[160]{0:T(256)S(1)}, s32[160]{0:T(256)}, u32[]{:S(2)}) copy-start(s32[160]{0:T(256)} %copy-done.9) | copy-start | bytes 1924
  470.2 2.6 copy-start.18
  470.2 2.8 copy-start.19
Sparse Core Ops, SparseCore 0:
  31.9 38.3 all-gather.25
  71.9 28.3 all-gather.27
  101.9 30.7 all-gather.29
  134.1 30.7 all-gather.31
  166.3 30.7 all-gather.33
  198.5 30.7 all-gather.35
  230.9 30.7 all-gather.37
  263.3 30.7 all-gather.39
  295.6 30.7 all-gather.41
  327.8 30.7 all-gather.43
  360.2 30.7 all-gather.45
  392.4 30.7 all-gather.47
  424.8 30.7 all-gather.49
  471.8 65.6 reduce-scatter.3
where the time goes:
time: 723 us; the launch traced here: 714 us
  waiting for transfers between devices  368 us (51%)
  blocking collectives  186 us (26%)
  local copies, waits for them, and re-layouts  64.4 us (9%)
  matrix products  41.8 us (6%)
  other arithmetic  38.2 us (5%)
  between operations  14.8 us (2%)
    all_gather x4, waiting for transfers between devices, body(): lax.all_gather(specialist_contract_weights[expert], 'dp', axis=1, tiled=T...  129 us
    all_gather x4, waiting for transfers between devices, body(): lax.all_gather(specialist_expand_weights[expert], 'dp', axis=0, tiled=True)  110 us
    unnamed x15, waiting for transfers between devices  70.1 us
    all_gather x1, blocking collectives, body(): lax.all_gather(end_normed[None], ('dp', 'mp'), axis=0, tiled=True)  63.8 us
    all_gather x4, waiting for transfers between devices, body(): lax.all_gather(specialist_switch_weights[expert], 'dp', axis=0, tiled=True)  59.1 us
    psum x1, blocking collectives, body(): lax.psum(jnp.sum(jnp.exp(lexicon_logit_values - largest[:, None]), axis=1...  41.3 us
    pmax x1, blocking collectives, body(): largest = lax.pmax(jnp.max(lexicon_logit_values, axis=1), ('dp', 'mp'))  39.4 us
    dot_general x4, matrix products, project(): return jnp.dot(act, piece, preferred_element_type=jnp.float32)  25.3 us
  transfers between devices with their start and end apart: 14, of which 12 were waited for; matrix products, arithmetic and copies ran while one was open for 17% of the time, Pallas kernels for 0%

commit v1 on v0

v1 whole, which is shorter than its diff:
```python
import math

import jax
import jax.numpy as jnp
from jax import lax
from jax.experimental import pallas as pl
from jax.experimental.pallas import tpu as pltpu
from jax.sharding import PartitionSpec as P

WIDTH = 2304
META = 16
branch_scale = 1.4 / math.sqrt(40.0)
epsilon = 1e-05
f32, bf16 = jnp.float32, jnp.bfloat16

VMEM = pl.BlockSpec(memory_space=pltpu.VMEM)
SMEM = pl.BlockSpec(memory_space=pltpu.SMEM)


def split3(v):
    hi = lax.reduce_precision(v, 8, 7)
    mid = lax.reduce_precision(v - hi, 8, 7)
    return hi, mid, v - hi - mid


def route_rows(core, meta):
    first, second = meta[0:1].astype(f32), meta[1:2].astype(f32)
    zero = core == 0
    return jnp.where(zero, first, second), jnp.where(zero, second, first)


def hi_lo(m):
    hi = m.astype(bf16)
    lo = (m - hi.astype(f32)).astype(bf16)
    return jnp.concatenate([hi.astype(f32), lo.astype(f32)], axis=0).astype(bf16)


def partial_kernel(scal, *refs):
    *blocks, wr, wg, wu, own, send, xs = refs
    near = blocks[0]
    n = pl.program_id(0)
    core, side = scal[0], scal[1]
    experts, tile, _ = wg.shape
    block = near.shape[0] - META
    hidden = (own.shape[0] - META) // 2

    @pl.when(n == 0)
    def _():
        for i, ref in enumerate(blocks):
            xs[pl.ds(pl.multiple_of((side ^ i) * block, 16), block)] = ref[0:block]
        router = jnp.dot(wr[...], xs[...], preferred_element_type=f32)
        sq = jnp.zeros((1, near.shape[1]), f32)
        for ref in blocks:
            for row in (4, 3, 2):
                sq = sq + ref[block + row : block + row + 1].astype(f32)
        m = jnp.concatenate([sq, router[0:7]], axis=0)
        own[2 * hidden : 2 * hidden + 8] = m
        own[2 * hidden + 8 : 2 * hidden + 16] = jnp.zeros_like(m)
        send[2 * hidden :] = hi_lo(m)

    mine, other = route_rows(core, near[block:])
    x = xs[...]
    for which, w in ((0, wg), (1, wu)):
        a = b = None
        for e in range(experts):
            d = jnp.dot(w[e], x, preferred_element_type=f32)
            a = d if a is None else jnp.where(mine == e, d, a)
            b = d if b is None else jnp.where(other == e, d, b)
        at = pl.ds(pl.multiple_of(which * hidden + n * tile, 16), tile)
        own[at] = a
        send[at] = b.astype(bf16)


def half_kernel(scal, own, recv, keep, send):
    y = scal[0]
    rows = own.shape[0] - META
    half = keep.shape[1]

    def halves(v):
        lo, hi = v[:, :half], v[:, half:]
        return jnp.where(y == 0, lo, hi), jnp.where(y == 0, hi, lo)

    step = rows // 10
    for at in range(0, rows, step):
        a, b = halves(own[at : at + step] + recv[at : at + step].astype(f32))
        keep[at : at + step] = a
        send[at : at + step] = b.astype(bf16)
    r = recv[rows:].astype(f32)
    a, b = halves(own[rows : rows + 8] + r[0:8] + r[8:16])
    keep[rows : rows + 8] = a
    keep[rows + 8 :] = jnp.zeros_like(a)
    send[rows:] = hi_lo(b)


def act_kernel(scal, keep, recv, meta, act):
    core, y = scal[0], scal[1]
    hidden, half = act.shape
    experts = 4
    mine, other = route_rows(core, meta[...])
    pick = lambda v: jnp.where(y == 0, v[:, :half], v[:, half:])
    mine, other = pick(mine), pick(other)
    r = recv[2 * hidden :].astype(f32)
    m = keep[2 * hidden : 2 * hidden + 8] + r[0:8] + r[8:16]
    scale = lax.rsqrt(m[0:1] / WIDTH + epsilon)
    la = lb = jnp.zeros_like(scale)
    for e in range(experts):
        logit = m[1 + e : 2 + e] * scale
        la = jnp.where(mine == e, logit, la)
        lb = jnp.where(other == e, logit, lb)
    mix = 1.0 / (1.0 + jnp.exp(lb - la))
    step = hidden // 5
    for at in range(0, hidden, step):
        g = (keep[at : at + step] + recv[at : at + step].astype(f32)) * scale
        up = hidden + at
        u = (keep[up : up + step] + recv[up : up + step].astype(f32)) * (scale * mix)
        act[at : at + step] = (g / (1.0 + jnp.exp(-g)) * u).astype(bf16)


def down_kernel(scal, a_near, a_far, b_near, b_far, meta, wd, out, ends, acc):
    e = pl.program_id(0)
    core, y, group = scal[0], scal[1], scal[2]
    mine, other = route_rows(core, meta[...])

    def whole(near, far):
        return jnp.concatenate(
            [jnp.where(y == 0, near[...], far[...]), jnp.where(y == 0, far[...], near[...])], axis=1
        )

    ef = e.astype(f32)
    ma = jnp.where(mine == ef, 1.0, 0.0).astype(bf16)
    mb = jnp.where(other == ef, 1.0, 0.0).astype(bf16)
    a = whole(a_near, a_far) * ma + whole(b_near, b_far) * mb
    d = jnp.dot(wd[0], a, preferred_element_type=f32)

    @pl.when(e == 0)
    def _():
        acc[...] = d

    @pl.when(e > 0)
    def _():
        acc[...] += d

    @pl.when(e == pl.num_programs(0) - 1)
    def _():
        o = acc[...].astype(bf16)
        out[...] = o
        rows = ends.shape[0]
        mark = meta[5:6].astype(f32)
        at = lax.broadcasted_iota(jnp.int32, (rows, mark.shape[1]), 0)
        want = (at - group * 4 + 1).astype(f32)
        sel = jnp.where((mark == want) & (want > 0.5) & (want < 4.5), 1.0, 0.0).astype(bf16)
        ends[...] = lax.dot_general(
            sel, o, (((1,), (1,)), ((), ())), preferred_element_type=f32
        ).astype(bf16)


def params(mib=24):
    return pltpu.CompilerParams(vmem_limit_bytes=mib * 2**20)


def partial_call(scal, blocks, wr, wg, wu):
    experts, hidden, depth = wg.shape
    rows, tokens = blocks[0].shape
    tile = hidden // 5
    full = lambda *shape: pl.BlockSpec(shape, lambda n: (0,) * len(shape))
    out_rows = 2 * hidden + META
    return pl.pallas_call(
        partial_kernel,
        grid=(hidden // tile,),
        in_specs=[
            SMEM,
            *[full(rows, tokens)] * len(blocks),
            full(*wr.shape),
            pl.BlockSpec((experts, tile, depth), lambda n: (0, n, 0)),
            pl.BlockSpec((experts, tile, depth), lambda n: (0, n, 0)),
        ],
        out_specs=[full(out_rows, tokens), full(out_rows, tokens)],
        out_shape=[
            jax.ShapeDtypeStruct((out_rows, tokens), f32),
            jax.ShapeDtypeStruct((out_rows, tokens), bf16),
        ],
        scratch_shapes=[pltpu.VMEM((depth, tokens), bf16)],
        compiler_params=params(),
        cost_estimate=pl.CostEstimate(
            flops=4 * experts * hidden * depth * tokens,
            bytes_accessed=4 * experts * hidden * depth + 6 * out_rows * tokens,
            transcendentals=0,
        ),
        name="gate_up_partial",
    )(scal, *blocks, wr, wg, wu)


def half_call(scal, own, recv):
    rows, tokens = own.shape
    shape = (rows, tokens // 2)
    return pl.pallas_call(
        half_kernel,
        in_specs=[SMEM, VMEM, VMEM],
        out_specs=[VMEM, VMEM],
        out_shape=[jax.ShapeDtypeStruct(shape, f32), jax.ShapeDtypeStruct(shape, bf16)],
        compiler_params=params(),
        cost_estimate=pl.CostEstimate(
            flops=rows * tokens, bytes_accessed=9 * rows * tokens, transcendentals=0
        ),
        name="core_sum",
    )(scal, own, recv)


def act_call(scal, keep, recv, near):
    rows, half = keep.shape
    hidden = (rows - META) // 2
    at = (near.shape[0] - META) // META
    return pl.pallas_call(
        act_kernel,
        grid=(1,),
        in_specs=[
            SMEM,
            pl.BlockSpec(keep.shape, lambda n: (0, 0)),
            pl.BlockSpec(recv.shape, lambda n: (0, 0)),
            pl.BlockSpec((META, near.shape[1]), lambda n: (at, 0)),
        ],
        out_specs=pl.BlockSpec((hidden, half), lambda n: (0, 0)),
        out_shape=jax.ShapeDtypeStruct((hidden, half), bf16),
        compiler_params=params(),
        cost_estimate=pl.CostEstimate(
            flops=8 * hidden * half, bytes_accessed=7 * rows * half, transcendentals=hidden * half
        ),
        name="act",
    )(scal, keep, recv, near)


def down_call(scal, pieces, near, wd, rows):
    experts, width, hidden = wd.shape
    tokens = near.shape[1]
    at = (near.shape[0] - META) // META
    piece = pl.BlockSpec(pieces[0].shape, lambda n: (0, 0))
    return pl.pallas_call(
        down_kernel,
        grid=(experts,),
        in_specs=[
            SMEM,
            piece,
            piece,
            piece,
            piece,
            pl.BlockSpec((META, tokens), lambda n: (at, 0)),
            pl.BlockSpec((1, width, hidden), lambda n: (n, 0, 0)),
        ],
        out_specs=[
            pl.BlockSpec((width, tokens), lambda n: (0, 0)),
            pl.BlockSpec((rows, width), lambda n: (0, 0)),
        ],
        out_shape=[
            jax.ShapeDtypeStruct((width, tokens), bf16),
            jax.ShapeDtypeStruct((rows, width), bf16),
        ],
        scratch_shapes=[pltpu.VMEM((width, tokens), f32)],
        compiler_params=params(),
        cost_estimate=pl.CostEstimate(
            flops=2 * experts * width * hidden * tokens,
            bytes_accessed=2 * experts * width * hidden + 2 * width * tokens,
            transcendentals=0,
        ),
        name="down",
    )(scal, *pieces, near, wd)


def body(
    skip_stream_arriving,
    chosen_specialists,
    sequence_piece_tallies,
    premix_rmsnorm_gain,
    dispatcher_weights,
    specialist_switch_weights,
    specialist_expand_weights,
    specialist_contract_weights,
    terminal_rmsnorm_gain,
    lexicon_projector_weights,
    softness_per_sequence,
):
    tokens, block = skip_stream_arriving.shape
    dp, mp = lax.axis_size("dp"), lax.axis_size("mp")
    parts = 4
    spread, sides = dp // parts, mp // parts
    assert dp == parts * spread and mp == parts * sides and sides & (sides - 1) == 0
    me_dp, me_mp = lax.axis_index("dp"), lax.axis_index("mp")
    part, lane = me_dp // spread, me_dp % spread
    y, core = part // 2, part % 2
    z, x = me_mp // sides, me_mp % sides

    def send(value, to):
        pairs = []
        for q in range(parts):
            for r in range(spread):
                for zz in range(parts):
                    for xx in range(sides):
                        q2, z2, x2 = to(q, zz, xx)
                        source = (q * spread + r) * mp + zz * sides + xx
                        pairs.append((source, (q2 * spread + r) * mp + z2 * sides + x2))
        return lax.ppermute(value, ("dp", "mp"), pairs)

    other_core = lambda q, zz, xx: (q ^ 1, zz, xx)
    other_y = lambda q, zz, xx: (q ^ 2, zz, xx)
    home = lambda q, zz, xx: (zz, q, xx)

    xt = (skip_stream_arriving * premix_rmsnorm_gain).T.astype(bf16)
    squares = split3(jnp.sum(skip_stream_arriving * skip_stream_arriving, axis=1))
    ends_index = jnp.cumsum(sequence_piece_tallies[0], dtype=jnp.int32) - 1
    reqs = ends_index.shape[0]
    here = jnp.arange(tokens, dtype=jnp.int32)
    mark = jnp.sum(
        jnp.where(here[None, :] == ends_index[:, None], jnp.arange(1, reqs + 1, dtype=jnp.int32)[:, None], 0),
        axis=0,
    )
    rows = [chosen_specialists[:, 0], chosen_specialists[:, 1], *squares, mark]
    meta = jnp.stack([row.astype(bf16) for row in rows])
    sent = jnp.concatenate([xt, meta, jnp.zeros((META - len(rows), tokens), bf16)], axis=0)
    feeds = [[send(sent, lambda q, zz, xx, i=i: (zz, q, xx ^ i)) for i in range(sides)]]
    for s in range(1, parts):
        shift = lambda q, zz, xx, s=s: (q, (zz - s) % parts, xx)
        feeds.append([send(v, shift) for v in feeds[0]])

    wg, wu, wd = specialist_switch_weights, specialist_expand_weights, specialist_contract_weights
    if spread > 1:
        runs = [[q * spread + r for r in range(spread)] for q in range(parts)]
        wg = lax.all_gather(wg, "dp", axis=1, tiled=True, axis_index_groups=runs)
        wu = lax.all_gather(wu, "dp", axis=1, tiled=True, axis_index_groups=runs)
        wd = lax.all_gather(wd, "dp", axis=2, tiled=True, axis_index_groups=runs)
    depth = wg.shape[1]
    short = -wg.shape[2] % 80
    wg, wu, wd = (jnp.swapaxes(w, 1, 2) for w in (wg, wu, wd))
    if short:
        wg, wu = (jnp.pad(w, ((0, 0), (0, short), (0, 0))) for w in (wg, wu))
        wd = jnp.pad(wd, ((0, 0), (0, 0), (0, short)))
    wr = lax.dynamic_slice_in_dim(dispatcher_weights, part * depth, depth).T
    wr = jnp.pad(wr, ((0, 16 - wr.shape[0]), (0, 0)))

    ints = lambda *v: jnp.stack([jnp.asarray(i, jnp.int32) for i in v])
    outs, ends = [], []
    for s in range(parts):
        own, give = partial_call(ints(core, x), feeds[s], wr, wg, wu)
        keep, give = half_call(ints(y), own, send(give, other_core))
        act = act_call(ints(core, y), keep, send(give, other_y), feeds[s][0])
        act_y = send(act, other_y)
        pieces = (act, act_y, send(act, other_core), send(act_y, other_core))
        group = (z + s) % parts
        out, end = down_call(ints(core, y, group), pieces, feeds[s][0], wd, parts * reqs)
        outs.append(out)
        ends.append(end)

    end_rows = ends[0] + ends[1] + ends[2] + ends[3]
    skip_ends = jnp.concatenate(split3(skip_stream_arriving[ends_index]), axis=0).astype(bf16)
    skip_ends = jnp.pad(skip_ends, ((0, 0), (0, depth - block)))
    message = jnp.concatenate([end_rows, skip_ends], axis=0)
    count = dp * mp
    everyone = lambda v: lax.all_to_all(
        jnp.broadcast_to(v[None], (count,) + v.shape), ("dp", "mp"), 0, 0, tiled=True
    )
    got = everyone(message).reshape(parts, spread, mp, -1, depth).astype(f32)
    all_ends = jnp.sum(got[:, :, :, : parts * reqs], axis=2).reshape(parts, spread, parts, reqs, depth)
    all_ends = all_ends.transpose(2, 1, 3, 0, 4).reshape(dp * reqs, WIDTH)
    stream = got[:, :, :, parts * reqs :, :block].reshape(parts, spread, mp, 3, reqs, block)
    stream = jnp.sum(stream, axis=3).transpose(0, 1, 3, 2, 4).reshape(dp * reqs, WIDTH)
    all_ends = stream + branch_scale * all_ends
    mean = jnp.mean(all_ends * all_ends, axis=1, keepdims=True)
    feed = (all_ends * lax.rsqrt(mean + epsilon) * terminal_rmsnorm_gain).astype(bf16)
    logits = jnp.dot(feed, lexicon_projector_weights, preferred_element_type=f32) / (
        WIDTH / 256.0 * softness_per_sequence[:, None]
    )
    top = jnp.max(logits, axis=1)
    total = jnp.sum(jnp.exp(logits - top[:, None]), axis=1)
    pairs = everyone(jnp.stack([top, total]))
    largest = jnp.max(pairs[:, 0], axis=0)
    total = jnp.sum(pairs[:, 1] * jnp.exp(pairs[:, 0] - largest), axis=0)
    logprobs = logits - largest[:, None] - jnp.log(total)[:, None]

    branch = None
    for s in range(parts):
        blocks = outs[s].reshape(sides, block, tokens)
        part_of = lambda i: lax.dynamic_index_in_dim(blocks, x ^ i, 0, keepdims=False)
        share = part_of(0).astype(f32)
        for i in range(1, sides):
            share += send(part_of(i), lambda q, zz, xx, i=i: (q, zz, xx ^ i)).astype(f32)
        if s:
            back = lambda q, zz, xx, s=s: (q, (zz + s) % parts, xx)
            share = send(share.astype(bf16), back).astype(f32)
        branch = share if branch is None else branch + share
    new_hidden = skip_stream_arriving + branch_scale * send(branch, home).T
    return (new_hidden, logprobs)


def solution(mesh):
    return jax.shard_map(
        body,
        mesh=mesh,
        in_specs=(
            P("dp", "mp"),
            P("dp", None),
            P("dp", None),
            P("mp"),
            P(),
            P(None, "dp", "mp"),
            P(None, "dp", "mp"),
            P(None, "mp", "dp"),
            P(),
            P(None, ("dp", "mp")),
            P(),
        ),
        out_specs=(P("dp", "mp"), P(None, ("dp", "mp"))),
        check_vma=False,
    )
```

time: 723 us -> 218 us (0.30)
  waiting for transfers between devices: 368 us -> 60.6 us
  blocking collectives: 186 us -> 0 us
  starting transfers between devices: 0.55 us -> 55.9 us
  Pallas kernels: 0 us -> 45.4 us
  matrix products: 41.8 us -> 1.48 us
  other arithmetic: 38.2 us -> 11 us
  local copies, waits for them, and re-layouts: 64.4 us -> 39.4 us
  between operations: 14.8 us -> 1.08 us
    all_gather x13 -> x0, waiting for transfers between devices: 298 us -> none  [the longest x4 129 us: body(): lax.all_gather(specialist_contract_weights[expert], 'dp', axis=1, tiled=T...]
    psum x3 -> x0, blocking collectives: 82.3 us -> none  [the longest x1 41.3 us: body(): lax.psum(jnp.sum(jnp.exp(lexicon_logit_values - largest[:, None]), axis=1...]
    unnamed x15 -> x0, waiting for transfers between devices: 70.1 us -> none
    all_gather x1 -> x0, blocking collectives: 63.8 us -> none  [body(): lax.all_gather(end_normed[None], ('dp', 'mp'), axis=0, tiled=True)]
    ppermute x0 -> x36, waiting for transfers between devices: none -> 58.2 us  [send(): return lax.ppermute(value, ('dp', 'mp'), pairs)]
    pallas_call x0 -> x16, Pallas kernels: none -> 45.4 us  [the longest x4 21.6 us: partial_call(): pl.pallas_call(partial_kernel, grid=(hidden // tile,), in_specs=[SMEM, *[...]
    dot_general x10 -> x1, matrix products: 41.8 us -> 1.48 us  [body(): jnp.dot(feed, lexicon_projector_weights, preferred_element_type=f32)]
    ppermute x0 -> x36, starting transfers between devices: none -> 39.5 us  [send(): return lax.ppermute(value, ('dp', 'mp'), pairs)]
  transfers between devices with their start and end apart: 14 -> 38, of which waited for: 12 -> 13; matrix products, arithmetic and copies ran while one was open for 17% -> 13% of each run, Pallas kernels for 0% -> 20%
where the time goes in v1:
time: 218 us; the launch traced here: 215 us
  waiting for transfers between devices  60.6 us (28%)
  starting transfers between devices  55.9 us (26%)
  Pallas kernels  45.4 us (21%)
  local copies, waits for them, and re-layouts  39.4 us (18%)
  other arithmetic  11 us (5%)
    ppermute x36, waiting for transfers between devices, send(): return lax.ppermute(value, ('dp', 'mp'), pairs)  58.2 us
    ppermute x36, starting transfers between devices, send(): return lax.ppermute(value, ('dp', 'mp'), pairs)  39.5 us
    unnamed x61, local copies, waits for them, and re-layouts  32.2 us
    pallas_call x4, Pallas kernels, partial_call(): pl.pallas_call(partial_kernel, grid=(hidden // tile,), in_specs=[SMEM, *[...  21.6 us
    all_to_all x2, starting transfers between devices, body(): lax.all_to_all(jnp.broadcast_to(v[None], (count,) + v.shape), ('dp', 'mp'...  16.4 us
    pallas_call x4, Pallas kernels, down_call(): pl.pallas_call(down_kernel, grid=(experts,), in_specs=[SMEM, piece, piece...  11.3 us
    pallas_call x4, Pallas kernels, half_call(): pl.pallas_call(half_kernel, in_specs=[SMEM, VMEM, VMEM], out_specs=[VMEM,...  8.24 us
  transfers between devices with their start and end apart: 38, of which 13 were waited for; matrix products, arithmetic and copies ran while one was open for 13% of the time, Pallas kernels for 20%

profile of v1, /device:TPU:4, one launch (start us, length us, event | category | flops | bytes accessed | tf_op | source)
XLA Modules:
  0.0 214.8 jit_solution(8134882046371987567)
XLA Ops:
  3.8 4.4 %collective-permute-start = (bf16[304,256]{1,0:T(8,128)(2,1)S(1)}, bf16[304,256]{1,0:T(8,128)(2,1)S(1)}, u32[]{:S(2)}, u32[]{:S(2)}) collective-permute-start(bf16[304,256]{1,0:T(8,128)(2,1)S(1)} %concatenate.10), channel_id=1, source_target_pairs={{0,0},{1,1},{2,8},{3,9},{4,16},{5,17},{6,24},{7,25},{8,2},{9,3},{1... | collective-permute-start | bytes 466952 | tf_op jit(solution)/shard_map/ppermute | solution.py:300
  8.2 2.3 %collective-permute-start.1 = (bf16[304,256]{1,0:T(8,128)(2,1)S(1)}, bf16[304,256]{1,0:T(8,128)(2,1)S(1)}, u32[]{:S(2)}, u32[]{:S(2)}) collective-permute-start(bf16[304,256]{1,0:T(8,128)(2,1)S(1)} %concatenate.10), channel_id=1, source_target_pairs={{0,1},{1,0},{2,9},{3,8},{4,17},{5,16},{6,25},{7,24},{8,3},{9,2},{1... | collective-permute-start | bytes 466952 | tf_op jit(solution)/shard_map/ppermute | solution.py:300
  11.3 6.0 %copy.37 = bf16[4,576,720]{1,2,0:T(8,128)(2,1)} copy(bf16[4,576,720]{2,1,0:T(8,128)(2,1)} %param.16) | data formatting | bytes 6635520 | tf_op args[5]
  17.2 5.9 %copy.38 = bf16[4,576,720]{1,2,0:T(8,128)(2,1)} copy(bf16[4,576,720]{2,1,0:T(8,128)(2,1)} %param.17) | data formatting | bytes 6635520 | tf_op args[6]
  25.0 2.0 copy-done.1
  27.1 2.0 copy-done.3
  29.1 5.4 %gate_up_partial.4 = (f32[1456,256]{1,0:T(8,128)S(1)}, bf16[1456,256]{1,0:T(8,128)(2,1)}) custom-call(s32[2]{0:T(128)S(1)} %pad_add_fusion.3.scal, bf16[304,256]{1,0:T(8,128)(2,1)S(1)} %collective-permute-done.refs_0_.meta, bf16[304,256]{1,0:T(8,128)(2,1)S(1)} %collective-permute-done.1.refs_1_, bf16[16,576]{1,0:T(8,128)(2,1)S(1)} %pad.8.refs_2_, ...), custom_call_target="tpu_custom_call" | custom-call | flops 1698693120 | bytes 8871936 | tf_op jit(solution)/shard_map/gate_up_partial/pallas_call | solution.py:167
  35.7 2.5 %collective-permute-start.17 = (bf16[304,256]{1,0:T(8,128)(2,1)S(1)}, bf16[304,256]{1,0:T(8,128)(2,1)S(1)}, u32[]{:S(2)}, u32[]{:S(2)}) collective-permute-start(bf16[304,256]{1,0:T(8,128)(2,1)S(1)} %collective-permute-done.refs_0_.meta), channel_id=1, source_target_pairs={{0,4},{1,5},{2,6},{3,7},{4,0},{5,1},{6,2},{7,3},{8,12},{9,13},{10,... | collective-permute-start | bytes 466952 | tf_op jit(solution)/shard_map/ppermute | solution.py:300
  38.7 3.6 %collective-permute-start.8 = (bf16[304,256]{1,0:T(8,128)(2,1)S(1)}, bf16[304,256]{1,0:T(8,128)(2,1)S(1)}, u32[]{:S(2)}, u32[]{:S(2)}) collective-permute-start(bf16[304,256]{1,0:T(8,128)(2,1)S(1)} %collective-permute-done.refs_0_.meta), channel_id=1, source_target_pairs={{0,6},{1,7},{2,0},{3,1},{4,2},{5,3},{6,4},{7,5},{8,14},{9,15},{10,... | collective-permute-start | bytes 466952 | tf_op jit(solution)/shard_map/ppermute | solution.py:300
  42.7 5.4 %gate_up_partial.7 = (f32[1456,256]{1,0:T(8,128)S(1)}, bf16[1456,256]{1,0:T(8,128)(2,1)}) custom-call(s32[2]{0:T(128)S(1)} %pad_add_fusion.3.scal, bf16[304,256]{1,0:T(8,128)(2,1)S(1)} %collective-permute-done.26.refs_0_.meta, bf16[304,256]{1,0:T(8,128)(2,1)S(1)} %collective-permute-done.27.refs_1_, bf16[16,576]{1,0:T(8,128)(2,1)S(1)} %pad.8.refs_2_, ...), custom_call_target="tpu_custom_call" | custom-call | flops 1698693120 | bytes 8871936 | tf_op jit(solution)/shard_map/gate_up_partial/pallas_call | solution.py:167
  50.2 3.3 %collective-permute-done.18.refs_1_ = bf16[304,256]{1,0:T(8,128)(2,1)S(1)} collective-permute-done((bf16[304,256]{1,0:T(8,128)(2,1)S(1)}, bf16[304,256]{1,0:T(8,128)(2,1)S(1)}, u32[]{:S(2)}, u32[]{:S(2)}) %collective-permute-start.18) | collective-permute-done | bytes 155680 | tf_op jit(solution)/shard_map/ppermute | solution.py:300
  53.5 5.4 %gate_up_partial.6 = (f32[1456,256]{1,0:T(8,128)S(1)}, bf16[1456,256]{1,0:T(8,128)(2,1)}) custom-call(s32[2]{0:T(128)S(1)} %pad_add_fusion.3.scal, bf16[304,256]{1,0:T(8,128)(2,1)S(1)} %collective-permute-done.17.refs_0_.meta, bf16[304,256]{1,0:T(8,128)(2,1)S(1)} %collective-permute-done.18.refs_1_, bf16[16,576]{1,0:T(8,128)(2,1)S(1)} %pad.8.refs_2_, ...), custom_call_target="tpu_custom_call" | custom-call | flops 1698693120 | bytes 8871936 | tf_op jit(solution)/shard_map/gate_up_partial/pallas_call | solution.py:167
  60.0 5.4 %gate_up_partial.5 = (f32[1456,256]{1,0:T(8,128)S(1)}, bf16[1456,256]{1,0:T(8,128)(2,1)}) custom-call(s32[2]{0:T(128)S(1)} %pad_add_fusion.3.scal, bf16[304,256]{1,0:T(8,128)(2,1)S(1)} %collective-permute-done.8.refs_0_.meta, bf16[304,256]{1,0:T(8,128)(2,1)S(1)} %collective-permute-done.9.refs_1_, bf16[16,576]{1,0:T(8,128)(2,1)S(1)} %pad.8.refs_2_, ...), custom_call_target="tpu_custom_call" | custom-call | flops 1698693120 | bytes 8871936 | tf_op jit(solution)/shard_map/gate_up_partial/pallas_call | solution.py:167
  67.1 1.4 copy-done.6
  68.5 2.2 %core_sum.4 = (f32[1456,128]{1,0:T(8,128)S(1)}, bf16[1456,128]{1,0:T(8,128)(2,1)}) custom-call(s32[1]{0:T(128)} %bitcast.1.scal, f32[1456,256]{1,0:T(8,128)S(1)} %copy-done.6, bf16[1456,256]{1,0:T(8,128)(2,1)} %collective-permute-done.2.recv), custom_call_target="tpu_custom_call" | custom-call | flops 372736 | bytes 3354624 | tf_op jit(solution)/shard_map/core_sum/pallas_call | solution.py:196
  71.6 1.8 collective-permute-start.3
  73.4 2.0 core_sum.7
  76.7 2.0 core_sum.6
  79.5 1.7 collective-permute-start.20
  81.3 2.0 core_sum.5
  84.6 1.9 copy.39
  86.4 1.6 gather_fusion
  90.5 1.8 collective-permute-start.4
  95.6 3.7 %collective-permute-done.20.recv = bf16[1456,128]{1,0:T(8,128)(2,1)S(1)} collective-permute-done((bf16[1456,128]{1,0:T(8,128)(2,1)}, bf16[1456,128]{1,0:T(8,128)(2,1)S(1)}, u32[]{:S(2)}, u32[]{:S(2)}) %collective-permute-start.20) | collective-permute-done | bytes 372768 | tf_op jit(solution)/shard_map/ppermute | solution.py:300
  100.0 7.4 %collective-permute-done.11.recv = bf16[1456,128]{1,0:T(8,128)(2,1)} collective-permute-done((bf16[1456,128]{1,0:T(8,128)(2,1)}, bf16[1456,128]{1,0:T(8,128)(2,1)}, u32[]{:S(2)}, u32[]{:S(2)}) %collective-permute-start.11) | collective-permute-done | bytes 372768 | tf_op jit(solution)/shard_map/ppermute | solution.py:300
  107.4 1.8 collective-permute-start.21
  111.5 1.5 collective-permute-start.12
  113.2 2.0 collective-permute-done.30.a_far
  115.7 3.4 %collective-permute-done.21.a_far = bf16[720,128]{1,0:T(8,128)(2,1)S(1)} collective-permute-done((bf16[720,128]{1,0:T(8,128)(2,1)S(1)}, bf16[720,128]{1,0:T(8,128)(2,1)S(1)}, u32[]{:S(2)}, u32[]{:S(2)}) %collective-permute-start.21) | collective-permute-done | bytes 184352 | tf_op jit(solution)/shard_map/ppermute | solution.py:300
  119.2 3.1 %collective-permute-done.12.a_far = bf16[720,128]{1,0:T(8,128)(2,1)S(1)} collective-permute-done((bf16[720,128]{1,0:T(8,128)(2,1)S(1)}, bf16[720,128]{1,0:T(8,128)(2,1)S(1)}, u32[]{:S(2)}, u32[]{:S(2)}) %collective-permute-start.12) | collective-permute-done | bytes 184352 | tf_op jit(solution)/shard_map/ppermute | solution.py:300
  122.8 2.8 %down.4 = (bf16[576,256]{1,0:T(8,128)(2,1)S(1)}, bf16[16,576]{1,0:T(8,128)(2,1)S(1)}) custom-call(s32[3]{0:T(128)S(1)} %get-tuple-element.50.scal, bf16[720,128]{1,0:T(8,128)(2,1)S(1)} %act.4.a_near, bf16[720,128]{1,0:T(8,128)(2,1)S(1)} %collective-permute-done.4.a_far, bf16[720,128]{1,0:T(8,128)(2,1)S(1)} %collective-permute-done.5.b_near, ...), custom_call_target="tpu_custom_call" | custom-call | flops 849346560 | bytes 3612672 | tf_op jit(solution)/shard_map/down/pallas_call | solution.py:237
  125.6 2.8 %down.7 = (bf16[576,256]{1,0:T(8,128)(2,1)S(1)}, bf16[16,576]{1,0:T(8,128)(2,1)S(1)}) custom-call(s32[3]{0:T(128)S(1)} %get-tuple-element.68.scal, bf16[720,128]{1,0:T(8,128)(2,1)S(1)} %act.7.a_near, bf16[720,128]{1,0:T(8,128)(2,1)S(1)} %collective-permute-done.30.a_far, bf16[720,128]{1,0:T(8,128)(2,1)S(1)} %collective-permute-done.31.b_near, ...), custom_call_target="tpu_custom_call" | custom-call | flops 849346560 | bytes 3612672 | tf_op jit(solution)/shard_map/down/pallas_call | solution.py:237
  128.4 2.8 %down.6 = (bf16[576,256]{1,0:T(8,128)(2,1)S(1)}, bf16[16,576]{1,0:T(8,128)(2,1)S(1)}) custom-call(s32[3]{0:T(128)S(1)} %get-tuple-element.67.scal, bf16[720,128]{1,0:T(8,128)(2,1)S(1)} %act.6.a_near, bf16[720,128]{1,0:T(8,128)(2,1)S(1)} %collective-permute-done.21.a_far, bf16[720,128]{1,0:T(8,128)(2,1)S(1)} %collective-permute-done.22.b_near, ...), custom_call_target="tpu_custom_call" | custom-call | flops 849346560 | bytes 3612672 | tf_op jit(solution)/shard_map/down/pallas_call | solution.py:237
  132.0 2.8 %down.5 = (bf16[576,256]{1,0:T(8,128)(2,1)S(1)}, bf16[16,576]{1,0:T(8,128)(2,1)S(1)}) custom-call(s32[3]{0:T(128)S(1)} %get-tuple-element.66.scal, bf16[720,128]{1,0:T(8,128)(2,1)S(1)} %act.5.a_near, bf16[720,128]{1,0:T(8,128)(2,1)S(1)} %collective-permute-done.12.a_far, bf16[720,128]{1,0:T(8,128)(2,1)S(1)} %collective-permute-done.13.b_near, ...), custom_call_target="tpu_custom_call" | custom-call | flops 849346560 | bytes 3612672 | tf_op jit(solution)/shard_map/down/pallas_call | solution.py:237
  136.8 11.3 %all-to-all-start = ((bf16[32,28,576]{2,1,0:T(8,128)(2,1)}), bf16[32,28,576]{2,1,0:T(8,128)(2,1)}, u32[]{:S(2)}, u32[]{:S(2)}) async-start(bf16[32,28,576]{2,1,0:T(8,128)(2,1)} %broadcast_in_dim.21), calls=%async_computation | async-start | bytes 2621440 | tf_op jit(solution)/shard_map/all_to_all | solution.py:356
  148.1 1.5 collective-permute-start.7
  150.3 1.5 collective-permute-start.24
  153.4 17.2 %collective-permute-done.33 = bf16[288,256]{1,0:T(8,128)(2,1)S(1)} collective-permute-done((bf16[288,256]{1,0:T(8,128)(2,1)S(1)}, bf16[288,256]{1,0:T(8,128)(2,1)S(1)}, u32[]{:S(2)}, u32[]{:S(2)}) %collective-permute-start.33) | collective-permute-done | bytes 147488 | tf_op jit(solution)/shard_map/ppermute | solution.py:300
  170.6 2.7 %collective-permute-start.34 = (bf16[288,256]{1,0:T(8,128)(2,1)S(1)}, bf16[288,256]{1,0:T(8,128)(2,1)S(1)}, u32[]{:S(2)}, u32[]{:S(2)}) collective-permute-start(bf16[288,256]{1,0:T(8,128)(2,1)S(1)} %fusion), channel_id=1, source_target_pairs={{0,6},{1,7},{2,0},{3,1},{4,2},{5,3},{6,4},{7,5},{8,14},{9,15},{10,... | collective-permute-start | bytes 442376 | tf_op jit(solution)/shard_map/ppermute | solution.py:300
  173.8 3.3 %collective-permute-start.25 = (bf16[288,256]{1,0:T(8,128)(2,1)S(1)}, bf16[288,256]{1,0:T(8,128)(2,1)S(1)}, u32[]{:S(2)}, u32[]{:S(2)}) collective-permute-start(bf16[288,256]{1,0:T(8,128)(2,1)S(1)} %fusion.1), channel_id=1, source_target_pairs={{0,4},{1,5},{2,6},{3,7},{4,0},{5,1},{6,2},{7,3},{8,12},{9,13},{10,... | collective-permute-start | bytes 442376 | tf_op jit(solution)/shard_map/ppermute | solution.py:300
  178.7 13.5 %collective-permute-done.25 = bf16[288,256]{1,0:T(8,128)(2,1)S(1)} collective-permute-done((bf16[288,256]{1,0:T(8,128)(2,1)S(1)}, bf16[288,256]{1,0:T(8,128)(2,1)S(1)}, u32[]{:S(2)}, u32[]{:S(2)}) %collective-permute-start.25) | collective-permute-done | bytes 147488 | tf_op jit(solution)/shard_map/ppermute | solution.py:300
  193.0 2.3 %collective-permute-start.35 = (f32[288,256]{1,0:T(8,128)}, f32[288,256]{1,0:T(8,128)}, u32[]{:S(2)}, u32[]{:S(2)}) collective-permute-start(f32[288,256]{1,0:T(8,128)} %fusion.5), channel_id=1, source_target_pairs={{0,0},{1,1},{2,8},{3,9},{4,16},{5,17},{6,24},{7,25},{8,2},{9,3},{1... | collective-permute-start | bytes 884744 | tf_op jit(solution)/shard_map/ppermute | solution.py:300
  195.3 1.7 bitcast_convert_fusion
  200.5 1.5 fusion.18
  202.8 5.2 %all-to-all-start.1 = ((f32[32,2,16]{2,1,0:T(2,128)}), f32[32,2,16]{2,1,0:T(2,128)S(1)}, u32[]{:S(2)}, u32[]{:S(2)}) async-start(f32[32,2,16]{2,1,0:T(2,128)} %broadcast_in_dim.22), calls=%async_computation.1 | async-start | bytes 65536 | tf_op jit(solution)/shard_map/all_to_all | solution.py:356
  208.0 1.9 collective-permute-done.35
  209.9 1.7 bitcast_add_fusion
  211.6 2.4 %all-to-all-done.1 = f32[32,2,16]{2,1,0:T(2,128)S(1)} async-done(((f32[32,2,16]{2,1,0:T(2,128)}), f32[32,2,16]{2,1,0:T(2,128)S(1)}, u32[]{:S(2)}, u32[]{:S(2)}) %all-to-all-start.1) | async-done | bytes 4128 | tf_op jit(solution)/shard_map/all_to_all | solution.py:356
  (161 shorter events, 39.7 us)
Async XLA Ops:
  0.6 199.8 %copy-start = (bf16[2304,512]{1,0:T(8,128)(2,1)S(1)}, bf16[2304,512]{1,0:T(8,128)(2,1)}, u32[]{:S(2)}) copy-start(bf16[2304,512]{1,0:T(8,128)(2,1)} %param.20) | copy-start | bytes 7077892
  3.8 19.4 %collective-permute-start = (bf16[304,256]{1,0:T(8,128)(2,1)S(1)}, bf16[304,256]{1,0:T(8,128)(2,1)S(1)}, u32[]{:S(2)}, u32[]{:S(2)}) collective-permute-start(bf16[304,256]{1,0:T(8,128)(2,1)S(1)} %concatenate.10), channel_id=1, source_target_pairs={{0,0},{1,1},{2,8},{3,9},{4,16},{5,17},{6,24},{7,25},{8,2},{9,3},{1... | collective-permute-start | bytes 466952 | tf_op jit(solution)/shard_map/ppermute | solution.py:300
  8.2 16.6 %collective-permute-start.1 = (bf16[304,256]{1,0:T(8,128)(2,1)S(1)}, bf16[304,256]{1,0:T(8,128)(2,1)S(1)}, u32[]{:S(2)}, u32[]{:S(2)}) collective-permute-start(bf16[304,256]{1,0:T(8,128)(2,1)S(1)} %concatenate.10), channel_id=1, source_target_pairs={{0,1},{1,0},{2,9},{3,8},{4,17},{5,16},{6,25},{7,24},{8,3},{9,2},{1... | collective-permute-start | bytes 466952 | tf_op jit(solution)/shard_map/ppermute | solution.py:300
  23.2 15.4 %collective-permute-start.26 = (bf16[304,256]{1,0:T(8,128)(2,1)S(1)}, bf16[304,256]{1,0:T(8,128)(2,1)S(1)}, u32[]{:S(2)}, u32[]{:S(2)}) collective-permute-start(bf16[304,256]{1,0:T(8,128)(2,1)S(1)} %collective-permute-done.refs_0_.meta), channel_id=1, source_target_pairs={{0,2},{1,3},{2,4},{3,5},{4,6},{5,7},{6,0},{7,1},{8,10},{9,11},{10,... | collective-permute-start | bytes 466952 | tf_op jit(solution)/shard_map/ppermute | solution.py:300
  24.8 17.4 %collective-permute-start.27 = (bf16[304,256]{1,0:T(8,128)(2,1)S(1)}, bf16[304,256]{1,0:T(8,128)(2,1)S(1)}, u32[]{:S(2)}, u32[]{:S(2)}) collective-permute-start(bf16[304,256]{1,0:T(8,128)(2,1)S(1)} %collective-permute-done.1.refs_1_), channel_id=1, source_target_pairs={{0,2},{1,3},{2,4},{3,5},{4,6},{5,7},{6,0},{7,1},{8,10},{9,11},{10,... | collective-permute-start | bytes 466952 | tf_op jit(solution)/shard_map/ppermute | solution.py:300
  29.1 13.5 %copy-start.2 = (bf16[4,576,720]{1,2,0:T(8,128)(2,1)S(1)}, bf16[4,576,720]{1,2,0:T(8,128)(2,1)}, u32[]{:S(2)}) copy-start(bf16[4,576,720]{1,2,0:T(8,128)(2,1)} %copy.37) | copy-start | bytes 9953284
  35.7 31.4 %collective-permute-start.2 = (bf16[1456,256]{1,0:T(8,128)(2,1)}, bf16[1456,256]{1,0:T(8,128)(2,1)}, u32[]{:S(2)}, u32[]{:S(2)}) collective-permute-start(bf16[1456,256]{1,0:T(8,128)(2,1)} %get-tuple-element.27), channel_id=1, source_target_pairs={{0,8},{1,9},{2,10},{3,11},{4,12},{5,13},{6,14},{7,15},{8,0},{9,1},... | collective-permute-start | bytes 2236424 | tf_op jit(solution)/shard_map/ppermute | solution.py:300
  35.7 14.5 %collective-permute-start.17 = (bf16[304,256]{1,0:T(8,128)(2,1)S(1)}, bf16[304,256]{1,0:T(8,128)(2,1)S(1)}, u32[]{:S(2)}, u32[]{:S(2)}) collective-permute-start(bf16[304,256]{1,0:T(8,128)(2,1)S(1)} %collective-permute-done.refs_0_.meta), channel_id=1, source_target_pairs={{0,4},{1,5},{2,6},{3,7},{4,0},{5,1},{6,2},{7,3},{8,12},{9,13},{10,... | collective-permute-start | bytes 466952 | tf_op jit(solution)/shard_map/ppermute | solution.py:300
  38.3 15.2 %collective-permute-start.18 = (bf16[304,256]{1,0:T(8,128)(2,1)S(1)}, bf16[304,256]{1,0:T(8,128)(2,1)S(1)}, u32[]{:S(2)}, u32[]{:S(2)}) collective-permute-start(bf16[304,256]{1,0:T(8,128)(2,1)S(1)} %collective-permute-done.1.refs_1_), channel_id=1, source_target_pairs={{0,4},{1,5},{2,6},{3,7},{4,0},{5,1},{6,2},{7,3},{8,12},{9,13},{10,... | collective-permute-start | bytes 466952 | tf_op jit(solution)/shard_map/ppermute | solution.py:300
  38.7 21.4 %collective-permute-start.8 = (bf16[304,256]{1,0:T(8,128)(2,1)S(1)}, bf16[304,256]{1,0:T(8,128)(2,1)S(1)}, u32[]{:S(2)}, u32[]{:S(2)}) collective-permute-start(bf16[304,256]{1,0:T(8,128)(2,1)S(1)} %collective-permute-done.refs_0_.meta), channel_id=1, source_target_pairs={{0,6},{1,7},{2,0},{3,1},{4,2},{5,3},{6,4},{7,5},{8,14},{9,15},{10,... | collective-permute-start | bytes 466952 | tf_op jit(solution)/shard_map/ppermute | solution.py:300
  42.3 17.8 %collective-permute-start.9 = (bf16[304,256]{1,0:T(8,128)(2,1)S(1)}, bf16[304,256]{1,0:T(8,128)(2,1)S(1)}, u32[]{:S(2)}, u32[]{:S(2)}) collective-permute-start(bf16[304,256]{1,0:T(8,128)(2,1)S(1)} %collective-permute-done.1.refs_1_), channel_id=1, source_target_pairs={{0,6},{1,7},{2,0},{3,1},{4,2},{5,3},{6,4},{7,5},{8,14},{9,15},{10,... | collective-permute-start | bytes 466952 | tf_op jit(solution)/shard_map/ppermute | solution.py:300
  50.2 23.2 %collective-permute-start.28 = (bf16[1456,256]{1,0:T(8,128)(2,1)}, bf16[1456,256]{1,0:T(8,128)(2,1)}, u32[]{:S(2)}, u32[]{:S(2)}) collective-permute-start(bf16[1456,256]{1,0:T(8,128)(2,1)} %get-tuple-element.42), channel_id=1, source_target_pairs={{0,8},{1,9},{2,10},{3,11},{4,12},{5,13},{6,14},{7,15},{8,0},{9,1},... | collective-permute-start | bytes 2236424 | tf_op jit(solution)/shard_map/ppermute | solution.py:300
  60.0 16.6 %collective-permute-start.19 = (bf16[1456,256]{1,0:T(8,128)(2,1)}, bf16[1456,256]{1,0:T(8,128)(2,1)}, u32[]{:S(2)}, u32[]{:S(2)}) collective-permute-start(bf16[1456,256]{1,0:T(8,128)(2,1)} %get-tuple-element.37), channel_id=1, source_target_pairs={{0,8},{1,9},{2,10},{3,11},{4,12},{5,13},{6,14},{7,15},{8,0},{9,1},... | collective-permute-start | bytes 2236424 | tf_op jit(solution)/shard_map/ppermute | solution.py:300
  66.6 14.6 %collective-permute-start.10 = (bf16[1456,256]{1,0:T(8,128)(2,1)}, bf16[1456,256]{1,0:T(8,128)(2,1)}, u32[]{:S(2)}, u32[]{:S(2)}) collective-permute-start(bf16[1456,256]{1,0:T(8,128)(2,1)} %get-tuple-element.32), channel_id=1, source_target_pairs={{0,8},{1,9},{2,10},{3,11},{4,12},{5,13},{6,14},{7,15},{8,0},{9,1},... | collective-permute-start | bytes 2236424 | tf_op jit(solution)/shard_map/ppermute | solution.py:300
  68.5 8.2 %copy-start.10 = (f32[1456,256]{1,0:T(8,128)S(1)}, f32[1456,256]{1,0:T(8,128)}, u32[]{:S(2)}) copy-start(f32[1456,256]{1,0:T(8,128)} %copy-done.9) | copy-start | bytes 4472836
  71.6 9.7 %copy-start.12 = (f32[1456,256]{1,0:T(8,128)S(1)}, f32[1456,256]{1,0:T(8,128)}, u32[]{:S(2)}) copy-start(f32[1456,256]{1,0:T(8,128)} %copy-done.11) | copy-start | bytes 4472836
  71.6 16.5 %collective-permute-start.3 = (bf16[1456,128]{1,0:T(8,128)(2,1)}, bf16[1456,128]{1,0:T(8,128)(2,1)}, u32[]{:S(2)}, u32[]{:S(2)}) collective-permute-start(bf16[1456,128]{1,0:T(8,128)(2,1)} %get-tuple-element.29), channel_id=1, source_target_pairs={{0,16},{1,17},{2,18},{3,19},{4,20},{5,21},{6,22},{7,23},{8,24},{9,... | collective-permute-start | bytes 1118216 | tf_op jit(solution)/shard_map/ppermute | solution.py:300
  76.3 15.9 %collective-permute-start.29 = (bf16[1456,128]{1,0:T(8,128)(2,1)}, bf16[1456,128]{1,0:T(8,128)(2,1)}, u32[]{:S(2)}, u32[]{:S(2)}) collective-permute-start(bf16[1456,128]{1,0:T(8,128)(2,1)} %get-tuple-element.44), channel_id=1, source_target_pairs={{0,16},{1,17},{2,18},{3,19},{4,20},{5,21},{6,22},{7,23},{8,24},{9,... | collective-permute-start | bytes 1118216 | tf_op jit(solution)/shard_map/ppermute | solution.py:300
  79.5 19.8 %collective-permute-start.20 = (bf16[1456,128]{1,0:T(8,128)(2,1)}, bf16[1456,128]{1,0:T(8,128)(2,1)S(1)}, u32[]{:S(2)}, u32[]{:S(2)}) collective-permute-start(bf16[1456,128]{1,0:T(8,128)(2,1)} %get-tuple-element.39), channel_id=1, source_target_pairs={{0,16},{1,17},{2,18},{3,19},{4,20},{5,21},{6,22},{7,23},{8,24},{9,... | collective-permute-start | bytes 1118216 | tf_op jit(solution)/shard_map/ppermute | solution.py:300
  84.2 23.2 %collective-permute-start.11 = (bf16[1456,128]{1,0:T(8,128)(2,1)}, bf16[1456,128]{1,0:T(8,128)(2,1)}, u32[]{:S(2)}, u32[]{:S(2)}) collective-permute-start(bf16[1456,128]{1,0:T(8,128)(2,1)} %get-tuple-element.34), channel_id=1, source_target_pairs={{0,16},{1,17},{2,18},{3,19},{4,20},{5,21},{6,22},{7,23},{8,24},{9,... | collective-permute-start | bytes 1118216 | tf_op jit(solution)/shard_map/ppermute | solution.py:300
  88.0 11.3 %copy-start.14 = (f32[1456,128]{1,0:T(8,128)S(1)}, f32[1456,128]{1,0:T(8,128)}, u32[]{:S(2)}) copy-start(f32[1456,128]{1,0:T(8,128)} %copy-done.13) | copy-start | bytes 2236420
  90.4 32.3 %copy-start.4 = (bf16[4,720,576]{1,2,0:T(8,128)(2,1)S(1)}, bf16[4,720,576]{1,2,0:T(8,128)(2,1)}, u32[]{:S(2)}) copy-start(bf16[4,720,576]{1,2,0:T(8,128)(2,1)} %param.18) | copy-start | bytes 9953284
  90.5 21.1 %collective-permute-start.4 = (bf16[720,128]{1,0:T(8,128)(2,1)S(1)}, bf16[720,128]{1,0:T(8,128)(2,1)S(1)}, u32[]{:S(2)}, u32[]{:S(2)}) collective-permute-start(bf16[720,128]{1,0:T(8,128)(2,1)S(1)} %act.4.a_near), channel_id=1, source_target_pairs={{0,16},{1,17},{2,18},{3,19},{4,20},{5,21},{6,22},{7,23},{8,24},{9,... | collective-permute-start | bytes 552968 | tf_op jit(solution)/shard_map/ppermute | solution.py:300
  92.2 20.9 %collective-permute-start.5 = (bf16[720,128]{1,0:T(8,128)(2,1)S(1)}, bf16[720,128]{1,0:T(8,128)(2,1)S(1)}, u32[]{:S(2)}, u32[]{:S(2)}) collective-permute-start(bf16[720,128]{1,0:T(8,128)(2,1)S(1)} %act.4.a_near), channel_id=1, source_target_pairs={{0,8},{1,9},{2,10},{3,11},{4,12},{5,13},{6,14},{7,15},{8,0},{9,1},... | collective-permute-start | bytes 552968 | tf_op jit(solution)/shard_map/ppermute | solution.py:300
  94.5 20.6 %collective-permute-start.30 = (bf16[720,128]{1,0:T(8,128)(2,1)S(1)}, bf16[720,128]{1,0:T(8,128)(2,1)S(1)}, u32[]{:S(2)}, u32[]{:S(2)}) collective-permute-start(bf16[720,128]{1,0:T(8,128)(2,1)S(1)} %act.7.a_near), channel_id=1, source_target_pairs={{0,16},{1,17},{2,18},{3,19},{4,20},{5,21},{6,22},{7,23},{8,24},{9,... | collective-permute-start | bytes 552968 | tf_op jit(solution)/shard_map/ppermute | solution.py:300
  99.3 15.9 %collective-permute-start.31 = (bf16[720,128]{1,0:T(8,128)(2,1)S(1)}, bf16[720,128]{1,0:T(8,128)(2,1)S(1)}, u32[]{:S(2)}, u32[]{:S(2)}) collective-permute-start(bf16[720,128]{1,0:T(8,128)(2,1)S(1)} %act.7.a_near), channel_id=1, source_target_pairs={{0,8},{1,9},{2,10},{3,11},{4,12},{5,13},{6,14},{7,15},{8,0},{9,1},... | collective-permute-start | bytes 552968 | tf_op jit(solution)/shard_map/ppermute | solution.py:300
  107.4 11.7 %collective-permute-start.21 = (bf16[720,128]{1,0:T(8,128)(2,1)S(1)}, bf16[720,128]{1,0:T(8,128)(2,1)S(1)}, u32[]{:S(2)}, u32[]{:S(2)}) collective-permute-start(bf16[720,128]{1,0:T(8,128)(2,1)S(1)} %act.6.a_near), channel_id=1, source_target_pairs={{0,16},{1,17},{2,18},{3,19},{4,20},{5,21},{6,22},{7,23},{8,24},{9,... | collective-permute-start | bytes 552968 | tf_op jit(solution)/shard_map/ppermute | solution.py:300
  111.5 10.7 %collective-permute-start.12 = (bf16[720,128]{1,0:T(8,128)(2,1)S(1)}, bf16[720,128]{1,0:T(8,128)(2,1)S(1)}, u32[]{:S(2)}, u32[]{:S(2)}) collective-permute-start(bf16[720,128]{1,0:T(8,128)(2,1)S(1)} %act.5.a_near), channel_id=1, source_target_pairs={{0,16},{1,17},{2,18},{3,19},{4,20},{5,21},{6,22},{7,23},{8,24},{9,... | collective-permute-start | bytes 552968 | tf_op jit(solution)/shard_map/ppermute | solution.py:300
  113.1 9.2 %collective-permute-start.6 = (bf16[720,128]{1,0:T(8,128)(2,1)S(1)}, bf16[720,128]{1,0:T(8,128)(2,1)S(1)}, u32[]{:S(2)}, u32[]{:S(2)}) collective-permute-start(bf16[720,128]{1,0:T(8,128)(2,1)S(1)} %collective-permute-done.4.a_far), channel_id=1, source_target_pairs={{0,8},{1,9},{2,10},{3,11},{4,12},{5,13},{6,14},{7,15},{8,0},{9,1},... | collective-permute-start | bytes 552968 | tf_op jit(solution)/shard_map/ppermute | solution.py:300
  115.2 13.2 %collective-permute-start.22 = (bf16[720,128]{1,0:T(8,128)(2,1)S(1)}, bf16[720,128]{1,0:T(8,128)(2,1)S(1)}, u32[]{:S(2)}, u32[]{:S(2)}) collective-permute-start(bf16[720,128]{1,0:T(8,128)(2,1)S(1)} %act.6.a_near), channel_id=1, source_target_pairs={{0,8},{1,9},{2,10},{3,11},{4,12},{5,13},{6,14},{7,15},{8,0},{9,1},... | collective-permute-start | bytes 552968 | tf_op jit(solution)/shard_map/ppermute | solution.py:300
  115.2 10.4 %collective-permute-start.32 = (bf16[720,128]{1,0:T(8,128)(2,1)S(1)}, bf16[720,128]{1,0:T(8,128)(2,1)S(1)}, u32[]{:S(2)}, u32[]{:S(2)}) collective-permute-start(bf16[720,128]{1,0:T(8,128)(2,1)S(1)} %collective-permute-done.30.a_far), channel_id=1, source_target_pairs={{0,8},{1,9},{2,10},{3,11},{4,12},{5,13},{6,14},{7,15},{8,0},{9,1},... | collective-permute-start | bytes 552968 | tf_op jit(solution)/shard_map/ppermute | solution.py:300
  119.1 9.3 %collective-permute-start.23 = (bf16[720,128]{1,0:T(8,128)(2,1)S(1)}, bf16[720,128]{1,0:T(8,128)(2,1)S(1)}, u32[]{:S(2)}, u32[]{:S(2)}) collective-permute-start(bf16[720,128]{1,0:T(8,128)(2,1)S(1)} %collective-permute-done.21.a_far), channel_id=1, source_target_pairs={{0,8},{1,9},{2,10},{3,11},{4,12},{5,13},{6,14},{7,15},{8,0},{9,1},... | collective-permute-start | bytes 552968 | tf_op jit(solution)/shard_map/ppermute | solution.py:300
  122.2 9.8 %collective-permute-start.13 = (bf16[720,128]{1,0:T(8,128)(2,1)S(1)}, bf16[720,128]{1,0:T(8,128)(2,1)S(1)}, u32[]{:S(2)}, u32[]{:S(2)}) collective-permute-start(bf16[720,128]{1,0:T(8,128)(2,1)S(1)} %act.5.a_near), channel_id=1, source_target_pairs={{0,8},{1,9},{2,10},{3,11},{4,12},{5,13},{6,14},{7,15},{8,0},{9,1},... | collective-permute-start | bytes 552968 | tf_op jit(solution)/shard_map/ppermute | solution.py:300
  122.2 9.8 %collective-permute-start.14 = (bf16[720,128]{1,0:T(8,128)(2,1)S(1)}, bf16[720,128]{1,0:T(8,128)(2,1)S(1)}, u32[]{:S(2)}, u32[]{:S(2)}) collective-permute-start(bf16[720,128]{1,0:T(8,128)(2,1)S(1)} %collective-permute-done.12.a_far), channel_id=1, source_target_pairs={{0,8},{1,9},{2,10},{3,11},{4,12},{5,13},{6,14},{7,15},{8,0},{9,1},... | collective-permute-start | bytes 552968 | tf_op jit(solution)/shard_map/ppermute | solution.py:300
  134.9 14.8 %copy-start.22 = (bf16[576,256]{1,0:T(8,128)(2,1)S(1)}, bf16[576,256]{1,0:T(8,128)(2,1)}, u32[]{:S(2)}) copy-start(bf16[576,256]{1,0:T(8,128)(2,1)} %copy-done.21) | copy-start | bytes 884740
  135.6 14.7 %copy-start.24 = (bf16[576,256]{1,0:T(8,128)(2,1)S(1)}, bf16[576,256]{1,0:T(8,128)(2,1)}, u32[]{:S(2)}) copy-start(bf16[576,256]{1,0:T(8,128)(2,1)} %copy-done.23) | copy-start | bytes 884740
  136.8 41.9 %copy-start.28 = (f32[16]{0:T(128)S(1)}, f32[16]{0:T(128)}, u32[]{:S(2)}) copy-start(f32[16]{0:T(128)} %param.21) | copy-start | bytes 196
  136.8 58.5 %all-to-all-start = ((bf16[32,28,576]{2,1,0:T(8,128)(2,1)}), bf16[32,28,576]{2,1,0:T(8,128)(2,1)}, u32[]{:S(2)}, u32[]{:S(2)}) async-start(bf16[32,28,576]{2,1,0:T(8,128)(2,1)} %broadcast_in_dim.21), calls=%async_computation | async-start | bytes 2621440 | tf_op jit(solution)/shard_map/all_to_all | solution.py:356
  148.1 30.6 %collective-permute-start.7 = (bf16[288,256]{1,0:T(8,128)(2,1)S(1)}, bf16[288,256]{1,0:T(8,128)(2,1)S(1)}, u32[]{:S(2)}, u32[]{:S(2)}) collective-permute-start(bf16[288,256]{1,0:T(8,128)(2,1)S(1)} %dynamic-slice_bitcast_fusion.3), channel_id=1, source_target_pairs={{0,1},{1,0},{2,3},{3,2},{4,5},{5,4},{6,7},{7,6},{8,9},{9,8},{10,11... | collective-permute-start | bytes 442376 | tf_op jit(solution)/shard_map/ppermute | solution.py:300
  149.6 20.9 %collective-permute-start.33 = (bf16[288,256]{1,0:T(8,128)(2,1)S(1)}, bf16[288,256]{1,0:T(8,128)(2,1)S(1)}, u32[]{:S(2)}, u32[]{:S(2)}) collective-permute-start(bf16[288,256]{1,0:T(8,128)(2,1)S(1)} %dynamic-slice_bitcast_fusion), channel_id=1, source_target_pairs={{0,1},{1,0},{2,3},{3,2},{4,5},{5,4},{6,7},{7,6},{8,9},{9,8},{10,11... | collective-permute-start | bytes 442376 | tf_op jit(solution)/shard_map/ppermute | solution.py:300
  150.3 23.4 %collective-permute-start.24 = (bf16[288,256]{1,0:T(8,128)(2,1)S(1)}, bf16[288,256]{1,0:T(8,128)(2,1)S(1)}, u32[]{:S(2)}, u32[]{:S(2)}) collective-permute-start(bf16[288,256]{1,0:T(8,128)(2,1)S(1)} %dynamic-slice_bitcast_fusion.1), channel_id=1, source_target_pairs={{0,1},{1,0},{2,3},{3,2},{4,5},{5,4},{6,7},{7,6},{8,9},{9,8},{10,11... | collective-permute-start | bytes 442376 | tf_op jit(solution)/shard_map/ppermute | solution.py:300
  152.7 24.3 %collective-permute-start.15 = (bf16[288,256]{1,0:T(8,128)(2,1)S(1)}, bf16[288,256]{1,0:T(8,128)(2,1)S(1)}, u32[]{:S(2)}, u32[]{:S(2)}) collective-permute-start(bf16[288,256]{1,0:T(8,128)(2,1)S(1)} %dynamic-slice_bitcast_fusion.2), channel_id=1, source_target_pairs={{0,1},{1,0},{2,3},{3,2},{4,5},{5,4},{6,7},{7,6},{8,9},{9,8},{10,11... | collective-permute-start | bytes 442376 | tf_op jit(solution)/shard_map/ppermute | solution.py:300
  170.6 8.1 %collective-permute-start.34 = (bf16[288,256]{1,0:T(8,128)(2,1)S(1)}, bf16[288,256]{1,0:T(8,128)(2,1)S(1)}, u32[]{:S(2)}, u32[]{:S(2)}) collective-permute-start(bf16[288,256]{1,0:T(8,128)(2,1)S(1)} %fusion), channel_id=1, source_target_pairs={{0,6},{1,7},{2,0},{3,1},{4,2},{5,3},{6,4},{7,5},{8,14},{9,15},{10,... | collective-permute-start | bytes 442376 | tf_op jit(solution)/shard_map/ppermute | solution.py:300
  173.8 18.5 %collective-permute-start.25 = (bf16[288,256]{1,0:T(8,128)(2,1)S(1)}, bf16[288,256]{1,0:T(8,128)(2,1)S(1)}, u32[]{:S(2)}, u32[]{:S(2)}) collective-permute-start(bf16[288,256]{1,0:T(8,128)(2,1)S(1)} %fusion.1), channel_id=1, source_target_pairs={{0,4},{1,5},{2,6},{3,7},{4,0},{5,1},{6,2},{7,3},{8,12},{9,13},{10,... | collective-permute-start | bytes 442376 | tf_op jit(solution)/shard_map/ppermute | solution.py:300
  178.0 14.2 %collective-permute-start.16 = (bf16[288,256]{1,0:T(8,128)(2,1)S(1)}, bf16[288,256]{1,0:T(8,128)(2,1)S(1)}, u32[]{:S(2)}, u32[]{:S(2)}) collective-permute-start(bf16[288,256]{1,0:T(8,128)(2,1)S(1)} %fusion.2), channel_id=1, source_target_pairs={{0,2},{1,3},{2,4},{3,5},{4,6},{5,7},{6,0},{7,1},{8,10},{9,11},{10,... | collective-permute-start | bytes 442376 | tf_op jit(solution)/shard_map/ppermute | solution.py:300
  193.0 16.9 %collective-permute-start.35 = (f32[288,256]{1,0:T(8,128)}, f32[288,256]{1,0:T(8,128)}, u32[]{:S(2)}, u32[]{:S(2)}) collective-permute-start(f32[288,256]{1,0:T(8,128)} %fusion.5), channel_id=1, source_target_pairs={{0,0},{1,1},{2,8},{3,9},{4,16},{5,17},{6,24},{7,25},{8,2},{9,3},{1... | collective-permute-start | bytes 884744 | tf_op jit(solution)/shard_map/ppermute | solution.py:300
  199.1 10.8 %copy-start.26 = (f32[256,288]{0,1:T(8,128)S(1)}, f32[256,288]{0,1:T(8,128)}, u32[]{:S(2)}) copy-start(f32[256,288]{0,1:T(8,128)} %param.11) | copy-start | bytes 884740
  202.8 11.2 %all-to-all-start.1 = ((f32[32,2,16]{2,1,0:T(2,128)}), f32[32,2,16]{2,1,0:T(2,128)S(1)}, u32[]{:S(2)}, u32[]{:S(2)}) async-start(f32[32,2,16]{2,1,0:T(2,128)} %broadcast_in_dim.22), calls=%async_computation.1 | async-start | bytes 65536 | tf_op jit(solution)/shard_map/all_to_all | solution.py:356
  (19 other events, 33.2 us)

commit v2 on v0

v2 whole, which is shorter than its diff:
```python
import math

import jax
import jax.numpy as jnp
from jax import lax
from jax.experimental import pallas as pl
from jax.experimental.pallas import tpu as pltpu
from jax.sharding import PartitionSpec as P

WIDTH = 2304
META = 16
LANES = 128
branch_scale = 1.4 / math.sqrt(40.0)
epsilon = 1e-05
f32, bf16 = jnp.float32, jnp.bfloat16

VMEM = pl.BlockSpec(memory_space=pltpu.VMEM)
SMEM = pl.BlockSpec(memory_space=pltpu.SMEM)
ANY = pl.BlockSpec(memory_space=pl.ANY)


def up_to(n, step=LANES):
    return -(-n // step) * step


def params(mib=32):
    return pltpu.CompilerParams(vmem_limit_bytes=mib * 2**20)


def cost(flops, bytes_accessed):
    return pl.CostEstimate(flops=flops, bytes_accessed=bytes_accessed, transcendentals=0)


def shape(dims, dtype):
    return jax.ShapeDtypeStruct(dims, dtype)


def prep_kernel(tallies, x, gain, routes, out, ends, wide):
    tokens, block = x.shape
    lanes = wide.shape[1]
    v = x[...]
    squares = jnp.sum(v * v, axis=1, keepdims=True)
    r = routes[...].astype(f32)
    wide[:, 0:block] = v * gain[...]
    at = lax.broadcasted_iota(jnp.int32, (tokens, lanes - block), 1)
    wide[:, block:] = jnp.where(
        at == 0, r[:, 0:1], jnp.where(at == 1, r[:, 1:2], jnp.where(at == 2, squares, 0.0))
    )
    turned = wide[...].T
    out[0:block] = turned[0:block].astype(bf16)
    sq = turned[block + 2 : block + 3]
    hi = sq.astype(bf16).astype(f32)
    mid = (sq - hi).astype(bf16).astype(f32)
    here = lax.broadcasted_iota(jnp.int32, (1, tokens), 1)
    mark, end = jnp.zeros((1, tokens), f32), jnp.int32(-1)
    for q in range(ends.shape[0]):
        end = end + tallies[0, q]
        mark = jnp.where(here == end, q + 1.0, mark)
        ends[q : q + 1] = x[pl.ds(end, 1)]
    rows = [turned[block : block + 2], hi, mid, sq - hi - mid, mark]
    rows.append(jnp.zeros((META - 6, tokens), f32))
    out[block:] = jnp.concatenate(rows, axis=0).astype(bf16)


def prep_call(x, gain, routes, tallies):
    tokens, block = x.shape
    reqs = tallies.shape[1]
    return pl.pallas_call(
        prep_kernel,
        in_specs=[SMEM, VMEM, VMEM, VMEM],
        out_specs=[VMEM, VMEM],
        out_shape=[shape((block + META, tokens), bf16), shape((reqs, block), f32)],
        scratch_shapes=[pltpu.VMEM((tokens, up_to(block + META)), f32)],
        compiler_params=params(),
        cost_estimate=cost(4 * tokens * block, 6 * tokens * block),
        name="prep",
    )(tallies, x, gain[None], routes)


def partial_kernel(sides, held, scal, *refs):
    feeds, refs = refs[:held], refs[held:]
    wr0, wr1, wg, wu, rg, ru = refs[:6]
    own, give, meta, cols, xs, xt, acc = refs[-7:]
    e = pl.program_id(0)
    core, side, y = scal[0], scal[1], scal[2]
    depth, half = rg.shape[1], rg.shape[2]
    deep = up_to(depth)
    tokens = xt.shape[0]
    block = depth // sides

    @pl.when(e == 0)
    def _():
        xs[...] = jnp.zeros_like(xs)
        sq = jnp.zeros((1, tokens), f32)
        each = 2 * sides // held
        for n in range(2 * sides):
            ref, at = feeds[n // each], (n % each) * (block + META)
            which, i = n // sides, n % sides
            row = which * deep + (side ^ i) * block
            xs[pl.ds(pl.multiple_of(row, 16), block)] = ref[at : at + block]
            row = 2 * deep + META * n
            xs[row : row + META] = ref[at + block : at + block + META]
            for term in (4, 3, 2):
                sq = sq + ref[at + block + term : at + block + term + 1].astype(f32)
        router = jnp.dot(wr0[...], xs[0:depth], preferred_element_type=f32)
        router += jnp.dot(wr1[...], xs[deep : deep + depth], preferred_element_type=f32)
        meta[...] = jnp.concatenate([sq, router[0:7]], axis=0)
        xt[...] = xs[...].T
        cols[...] = xt[:, 2 * deep :]

    routes = xt[:, 2 * deep :].astype(f32)
    ef = e.astype(f32)
    for which, (w, r) in enumerate(((wg, rg), (wu, ru))):
        d = jnp.dot(xt[:, 0:depth], w[0], preferred_element_type=f32)
        d += jnp.dot(xt[:, deep : deep + depth], r[0], preferred_element_type=f32)
        at = which * half
        for k in range(2):
            take = (routes[:, k : k + 1] == ef) | (e == 0)
            acc[k, :, at : at + half] = jnp.where(take, d, acc[k, :, at : at + half])

    @pl.when(e == pl.num_programs(0) - 1)
    def _():
        th = tokens // 2
        for k in range(2):
            own[k] = acc[k, pl.ds(pl.multiple_of(y * th, th), th)]
            give[k] = acc[k, pl.ds(pl.multiple_of((1 - y) * th, th), th)].astype(bf16)


def partial_call(scal, sides, feeds, wr, weights, swapped, deps):
    experts, depth, half = swapped[0].shape
    rows, tokens = feeds[0].shape
    deep = up_to(depth)
    full = lambda v: pl.BlockSpec(v.shape, lambda n, s: (0,) * len(v.shape))
    mine = pl.BlockSpec((1, depth, half), lambda n, s: (n, 0, s[0]))
    theirs = pl.BlockSpec((1, depth, half), lambda n, s: (n, 0, 0))
    outs = [
        shape((2, tokens // 2, 2 * half), f32),
        shape((2, tokens // 2, 2 * half), bf16),
        shape((8, tokens), f32),
        shape((tokens, LANES), bf16),
    ]
    call = pl.pallas_call(
        lambda *refs: partial_kernel(sides, len(feeds), *refs),
        grid_spec=pltpu.PrefetchScalarGridSpec(
            num_scalar_prefetch=1,
            grid=(experts,),
            in_specs=[full(v) for v in feeds]
            + [full(v) for v in wr]
            + [mine, mine, theirs, theirs]
            + [ANY] * len(deps),
            out_specs=[full(v) for v in outs],
            scratch_shapes=[
                pltpu.VMEM((2 * deep + LANES, tokens), bf16),
                pltpu.VMEM((tokens, 2 * deep + LANES), bf16),
                pltpu.VMEM((2, tokens, 2 * half), f32),
            ],
        ),
        out_shape=outs,
        compiler_params=params(),
        cost_estimate=cost(
            8 * experts * depth * half * tokens, 8 * experts * depth * half + 12 * tokens * half
        ),
        name="gate_up_partial",
    )
    return call(scal, *feeds, *wr, *weights, *swapped, *deps)


def act_kernel(scal, own, recv, meta, meta_recv, cols, *refs):
    act, turned = refs[-2:]
    y = scal[0]
    _, th, half = act.shape
    m = meta[...] + meta_recv[...]
    turned[...] = jnp.concatenate([m, jnp.zeros((LANES - 8, m.shape[1]), f32)], axis=0).T
    here = pl.ds(pl.multiple_of(y * th, th), th)
    m = turned[here]
    routes = cols[here].astype(f32)
    scale = lax.rsqrt(m[:, 0:1] / WIDTH + epsilon)
    logits = []
    for k in range(2):
        logit = jnp.zeros_like(scale)
        for e in range(4):
            logit = jnp.where(routes[:, k : k + 1] == e, m[:, 1 + e : 2 + e], logit)
        logits.append(logit * scale)
    for k in range(2):
        mix = scale / (1.0 + jnp.exp(logits[1 - k] - logits[k]))
        g = (own[k, :, 0:half] + recv[k, :, 0:half].astype(f32)) * scale
        u = (own[k, :, half:] + recv[k, :, half:].astype(f32)) * mix
        act[k] = (g / (1.0 + jnp.exp(-g)) * u).astype(bf16)


def act_call(scal, own, recv, meta, meta_recv, cols, deps):
    _, th, wide = own.shape
    return pl.pallas_call(
        act_kernel,
        in_specs=[SMEM] + [VMEM] * 5 + [ANY] * len(deps),
        out_specs=VMEM,
        out_shape=shape((2, th, wide // 2), bf16),
        scratch_shapes=[pltpu.VMEM((meta.shape[1], LANES), f32)],
        compiler_params=params(),
        cost_estimate=cost(12 * th * wide, 14 * th * wide),
        name="act",
    )(scal, own, recv, meta, meta_recv, cols, *deps)


def down_kernel(sides, scal, a, a_y, b, b_y, cols, wd, *refs):
    outs = refs[-sides - 3 : -3]
    whole, acc, turned = refs[-3:]
    e = pl.program_id(0)
    core, side, y = scal[0], scal[1], scal[2]
    _, th, half = a.shape
    hidden, width = wd.shape[1:]
    block = width // sides

    @pl.when(e == 0)
    def _():
        for mine, other, first in ((a, b, y), (a_y, b_y, 1 - y)):
            rows = pl.ds(pl.multiple_of(first * th, th), th)
            for k in range(2):
                whole[k, rows, 0:half] = jnp.where(core == 0, mine[k], other[k])
                whole[k, rows, half:] = jnp.where(core == 0, other[k], mine[k])

    ef = e.astype(f32)
    routes = cols[...].astype(f32)
    masks = [jnp.where(routes[:, k : k + 1] == ef, 1.0, 0.0).astype(bf16) for k in range(2)]
    rows = whole[0, :, 0:hidden] * masks[0] + whole[1, :, 0:hidden] * masks[1]
    d = jnp.dot(rows, wd[0], preferred_element_type=f32)

    @pl.when(e == 0)
    def _():
        acc[...] = jnp.zeros_like(acc)
        acc[:, 0:width] = d

    @pl.when(e > 0)
    def _():
        acc[:, 0:width] += d

    @pl.when(e == pl.num_programs(0) - 1)
    def _():
        turned[...] = acc[...].T
        for i in range(sides):
            rows = pl.ds(pl.multiple_of((side ^ i) * block, 16), block)
            outs[i][...] = turned[rows].astype(bf16)


def down_call(scal, sides, pieces, cols, wd, deps):
    experts, hidden, width = wd.shape
    tokens = cols.shape[0]
    half = pieces[0].shape[2]
    full = lambda v: pl.BlockSpec(v.shape, lambda n: (0,) * len(v.shape))
    outs = [shape((width // sides, tokens), bf16)] * sides
    return pl.pallas_call(
        lambda *refs: down_kernel(sides, *refs),
        grid=(experts,),
        in_specs=[SMEM]
        + [full(v) for v in pieces]
        + [full(cols), pl.BlockSpec((1, hidden, width), lambda n: (n, 0, 0))]
        + [ANY] * len(deps),
        out_specs=[full(v) for v in outs],
        out_shape=outs,
        scratch_shapes=[
            pltpu.VMEM((2, tokens, 2 * half), bf16),
            pltpu.VMEM((tokens, up_to(width)), f32),
            pltpu.VMEM((up_to(width), tokens), f32),
        ],
        compiler_params=params(),
        cost_estimate=cost(
            2 * experts * width * hidden * tokens, 2 * experts * width * hidden + 2 * width * tokens
        ),
        name="down",
    )(scal, *pieces, cols, wd, *deps)


def total_kernel(meta, stream, *refs):
    parts, (total, message) = refs[:-2], refs[-2:]
    v = parts[0][...].astype(f32)
    for ref in parts[1:]:
        v = v + ref[...].astype(f32)
    total[...] = v
    reqs = stream.shape[0]
    mark = meta[5:6].astype(f32)
    row = lax.broadcasted_iota(jnp.int32, (8, mark.shape[1]), 0)
    pick = jnp.where(mark == (row + 1).astype(f32), 1.0, 0.0)
    ends = lax.dot_general(
        pick, v, (((1,), (1,)), ((), ())), precision=lax.Precision.HIGHEST, preferred_element_type=f32
    )
    ends = stream[...] + branch_scale * ends[0:reqs]
    message[...] = jnp.broadcast_to(ends[None], message.shape)


def total_call(feed, stream, parts, block, count):
    tokens = feed.shape[1]
    full = lambda v: pl.BlockSpec(v.shape, lambda n: (0,) * len(v.shape))
    outs = [shape((block, tokens), f32), shape((count, *stream.shape), f32)]
    return pl.pallas_call(
        total_kernel,
        grid=(1,),
        in_specs=[pl.BlockSpec((META, tokens), lambda n: (block // META, 0)), full(stream)]
        + [full(v) for v in parts],
        out_specs=[full(v) for v in outs],
        out_shape=outs,
        compiler_params=params(),
        cost_estimate=cost(16 * block * tokens, 14 * block * tokens),
        name="branch_total",
    )(feed, stream, *parts)


def head_kernel(order, got, gain, words, softness, logits, message, wide):
    blocks, block = gain.shape
    rows, columns = logits.shape
    ends, squares = [], 0.0
    for b in range(blocks):
        v = jnp.concatenate([got[i] for i in order[b]], axis=0)
        squares = squares + jnp.sum(v * v, axis=1, keepdims=True)
        ends.append(v)
    scale = lax.rsqrt(squares / WIDTH + epsilon)
    total = jnp.zeros((rows, columns), f32)
    for b in range(blocks):
        feed = (ends[b] * scale * gain[b : b + 1]).astype(bf16)
        total += jnp.dot(feed, words[b * block : (b + 1) * block], preferred_element_type=f32)
    total = total / (WIDTH / 256.0 * softness[...])
    logits[...] = total
    top = jnp.max(total, axis=1, keepdims=True)
    mass = jnp.sum(jnp.exp(total - top), axis=1, keepdims=True)
    wide[...] = jnp.zeros_like(wide)
    lane = lax.broadcasted_iota(jnp.int32, (rows, LANES), 1)
    wide[0:rows] = jnp.where(lane == 0, top, jnp.where(lane == 1, mass, 0.0))
    turned = wide[...].T
    message[...] = jnp.broadcast_to(turned[None, 0:2, 0:rows], message.shape)


def head_call(order, got, gain, words, softness):
    rows, columns = softness.shape[0], words.shape[1]
    return pl.pallas_call(
        lambda *refs: head_kernel(order, *refs),
        in_specs=[VMEM] * 4,
        out_specs=[VMEM, VMEM],
        out_shape=[shape((rows, columns), f32), shape((got.shape[0], 2, rows), f32)],
        scratch_shapes=[pltpu.VMEM((LANES, LANES), f32)],
        compiler_params=params(),
        cost_estimate=cost(2 * rows * WIDTH * columns, 2 * WIDTH * columns),
        name="head",
    )(got, gain, words, softness)


def body(
    skip_stream_arriving,
    chosen_specialists,
    sequence_piece_tallies,
    premix_rmsnorm_gain,
    dispatcher_weights,
    specialist_switch_weights,
    specialist_expand_weights,
    specialist_contract_weights,
    terminal_rmsnorm_gain,
    lexicon_projector_weights,
    softness_per_sequence,
):
    tokens, block = skip_stream_arriving.shape
    dp, mp = lax.axis_size("dp"), lax.axis_size("mp")
    count = dp * mp
    parts = 4
    spread, sides = dp // parts, mp // parts
    assert dp == parts * spread and mp == parts * sides and sides & (sides - 1) == 0
    part = lax.axis_index("dp") // spread
    y, core = part // 2, part % 2
    side = lax.axis_index("mp") % sides

    def send(value, to):
        pairs = []
        for q in range(parts):
            for r in range(spread):
                for z in range(parts):
                    for x in range(sides):
                        q2, z2, x2 = to(q, z, x)
                        source = (q * spread + r) * mp + z * sides + x
                        pairs.append((source, (q2 * spread + r) * mp + z2 * sides + x2))
        return lax.ppermute(value, ("dp", "mp"), pairs)

    other_core = lambda q, z, x: (q ^ 1, z, x)
    other_y = lambda q, z, x: (q ^ 2, z, x)
    home = lambda q, z, x: (z, q, x)

    sent, stream = prep_call(
        skip_stream_arriving, premix_rmsnorm_gain, chosen_specialists, sequence_piece_tallies
    )
    first = [
        send(sent, lambda q, z, x, c=c, i=i: (z ^ c, (q - 1) % parts, x ^ i))
        for c in range(2)
        for i in range(sides)
    ]
    wg, wu, wd = specialist_switch_weights, specialist_expand_weights, specialist_contract_weights
    if spread > 1:
        runs = [[q * spread + r for r in range(spread)] for q in range(parts)]
        wg = lax.all_gather(wg, "dp", axis=1, tiled=True, axis_index_groups=runs)
        wu = lax.all_gather(wu, "dp", axis=1, tiled=True, axis_index_groups=runs)
        wd = lax.all_gather(wd, "dp", axis=2, tiled=True, axis_index_groups=runs)
    depth, hidden = wg.shape[1], wg.shape[2]
    half = up_to(-(-hidden // 2))
    swap = lambda w: jnp.where(
        core == 0, jnp.pad(w[:, :, half:], ((0, 0), (0, 0), (0, 2 * half - hidden))), w[:, :, :half]
    )
    swapped = [send(swap(w), other_core) for w in (wg, wu)]
    wr = []
    for p in (part, part ^ 1):
        w = lax.dynamic_slice_in_dim(dispatcher_weights, p * depth, depth).T
        wr.append(jnp.pad(w, ((0, 16 - w.shape[0]), (0, 0))))

    feeds = [first]
    own = jnp.concatenate(first[:sides], axis=0)
    for s in range(1, parts):
        mine = send(own, lambda q, z, x, s=s: (q, (z - s) % parts, x))
        feeds.append([mine, send(mine, other_core)])
    stream = send(stream, home)

    scal = jnp.stack([core, side, y]).astype(jnp.int32)
    y_only = scal[2:3]
    partial, act, pieces, shares, back = {}, {}, {}, {}, {}

    def do_partial(s, *deps):
        own, give, meta, cols = partial_call(scal, sides, feeds[s], wr, (wg, wu), swapped, deps)
        partial[s] = (own, send(give, other_y), meta, send(meta, other_y), cols)
        return own

    def do_act(s, *deps):
        a = act_call(y_only, *partial[s], deps)
        a_y = send(a, other_y)
        pieces[s] = (a, a_y, send(a, other_core), send(a_y, other_core))
        return a

    def do_down(s, *deps):
        outs = down_call(scal, sides, pieces[s], partial[s][4], wd, deps)
        shares[s] = [outs[0]] + [
            send(outs[i], lambda q, z, x, i=i: (q, z, x ^ i)) for i in range(1, sides)
        ]
        if s < parts - 1:
            share = sum(v.astype(f32) for v in shares[s]).astype(bf16)
            shares[s] = share
            back[s] = send(share, lambda q, z, x, s=s: (q, (z + s + 1) % parts, x))
        return outs[0]

    p0 = do_partial(0)
    p1 = do_partial(1, p0)
    a0 = do_act(0, p1)
    p2 = do_partial(2, a0)
    a1 = do_act(1, p2)
    d0 = do_down(0, a1)
    p3 = do_partial(3, d0)
    a2 = do_act(2, p3)
    d1 = do_down(1, a2, shares[0])
    a3 = do_act(3, d1)
    d2 = do_down(2, a3, shares[1], back[0])
    do_down(3, d2, back[1])
    total, message = total_call(
        feeds[3][0], stream, [*shares[3], back[0], back[1], back[2]], block, count
    )

    everyone = lambda v: lax.all_to_all(v, ("dp", "mp"), 0, 0, tiled=True)
    got = everyone(message)
    branch = send(total, home)
    order = [
        [
            (q * spread + r) * mp + z * sides + x
            for z in range(parts)
            for r in range(spread)
        ]
        for q in range(parts)
        for x in range(sides)
    ]
    logits, pairs = head_call(
        order,
        got,
        terminal_rmsnorm_gain.reshape(mp, block),
        lexicon_projector_weights,
        softness_per_sequence[:, None],
    )
    pairs = everyone(pairs)
    new_hidden = skip_stream_arriving + branch_scale * branch.T
    largest = jnp.max(pairs[:, 0], axis=0)
    mass = jnp.sum(pairs[:, 1] * jnp.exp(pairs[:, 0] - largest), axis=0)
    logprobs = logits - largest[:, None] - jnp.log(mass)[:, None]
    return (new_hidden, logprobs)


def solution(mesh):
    return jax.shard_map(
        body,
        mesh=mesh,
        in_specs=(
            P("dp", "mp"),
            P("dp", None),
            P("dp", None),
            P("mp"),
            P(),
            P(None, "dp", "mp"),
            P(None, "dp", "mp"),
            P(None, "mp", "dp"),
            P(),
            P(None, ("dp", "mp")),
            P(),
        ),
        out_specs=(P("dp", "mp"), P(None, ("dp", "mp"))),
        check_vma=False,
    )
```

time: 723 us -> 210 us (0.29); the launches traced: 714 us -> 208 us
  waiting for transfers between devices: 368 us -> 64.2 us
  blocking collectives: 186 us -> 0 us
  starting transfers between devices: 0.55 us -> 56.6 us
  Pallas kernels: 0 us -> 52.1 us
  matrix products: 41.8 us -> 0 us
  local copies, waits for them, and re-layouts: 64.4 us -> 27.7 us
  other arithmetic: 38.2 us -> 6.73 us
  between operations: 14.8 us -> 1.08 us
    all_gather x13 -> x0, waiting for transfers between devices: 298 us -> none  [the longest x4 129 us: body(): lax.all_gather(specialist_contract_weights[expert], 'dp', axis=1, tiled=T...]
    psum x3 -> x0, blocking collectives: 82.3 us -> none  [the longest x1 41.3 us: body(): lax.psum(jnp.sum(jnp.exp(lexicon_logit_values - largest[:, None]), axis=1...]
    unnamed x15 -> x0, waiting for transfers between devices: 70.1 us -> none
    all_gather x1 -> x0, blocking collectives: 63.8 us -> none  [body(): lax.all_gather(end_normed[None], ('dp', 'mp'), axis=0, tiled=True)]
    ppermute x0 -> x41, waiting for transfers between devices: none -> 54.9 us  [send(): return lax.ppermute(value, ('dp', 'mp'), pairs)]
    pallas_call x0 -> x15, Pallas kernels: none -> 52.1 us  [the longest x4 27.7 us: partial_call(): return call(scal, *feeds, *wr, *weights, *swapped, *deps)]
    ppermute x0 -> x41, starting transfers between devices: none -> 49.1 us  [send(): return lax.ppermute(value, ('dp', 'mp'), pairs)]
    dot_general x10 -> x0, matrix products: 41.8 us -> none  [the longest x4 25.3 us: project(): return jnp.dot(act, piece, preferred_element_type=jnp.float32)]
  transfers between devices with their start and end apart: 14 -> 43, of which waited for: 12 -> 12; matrix products, arithmetic and copies ran while one was open for 17% -> 7% of each run, Pallas kernels for 0% -> 23%
where the time goes in v2:
time: 210 us; the launch traced here: 208 us
  waiting for transfers between devices  64.2 us (31%)
  starting transfers between devices  56.6 us (27%)
  Pallas kernels  52.1 us (25%)
  local copies, waits for them, and re-layouts  27.7 us (13%)
  other arithmetic  6.73 us (3%)
    ppermute x41, waiting for transfers between devices, send(): return lax.ppermute(value, ('dp', 'mp'), pairs)  54.9 us
    ppermute x41, starting transfers between devices, send(): return lax.ppermute(value, ('dp', 'mp'), pairs)  49.1 us
    pallas_call x4, Pallas kernels, partial_call(): return call(scal, *feeds, *wr, *weights, *swapped, *deps)  27.7 us
    unnamed x72, local copies, waits for them, and re-layouts  21.8 us
    pallas_call x4, Pallas kernels, down_call(): pl.pallas_call(lambda *refs: down_kernel(sides, *refs), grid=(experts,),...  14.9 us
    all_to_all x2, waiting for transfers between devices, body(): everyone = lambda v: lax.all_to_all(v, ('dp', 'mp'), 0, 0, tiled=True)  9.27 us
    all_to_all x2, starting transfers between devices, body(): everyone = lambda v: lax.all_to_all(v, ('dp', 'mp'), 0, 0, tiled=True)  7.56 us
    select_n x2, other arithmetic, body(): jnp.where(core == 0, jnp.pad(w[:, :, half:], ((0, 0), (0, 0), (0, 2 * hal...  5.04 us
  transfers between devices with their start and end apart: 43, of which 12 were waited for; matrix products, arithmetic and copies ran while one was open for 7% of the time, Pallas kernels for 23%

profile of v2, /device:TPU:4, one launch (start us, length us, event | category | flops | bytes accessed | tf_op | source)
XLA Modules:
  0.0 208.5 jit_solution(13300847434822759534)
XLA Ops:
  0.7 1.5 slice-done
  2.1 3.3 %slice_select_fusion.1 = bf16[4,576,384]{2,1,0:T(8,128)(2,1)} fusion(bf16[4,576,720]{2,1,0:T(8,128)(2,1)} %refs_5_.5, bf16[4,576,336]{2,1,0:T(8,128)(2,1)S(1)} %slice-done, pred[]{:T(512)S(6)} %eq.7), kind=kLoop, calls=%fused_computation.1 | loop fusion | flops 884736 | bytes 5087233 | tf_op jit(solution)/shard_map/jit(_where)/select_n | solution.py:399
  5.4 1.5 slice-done.1
  6.9 1.7 slice_select_fusion
  8.7 1.9 copy.13.x
  13.3 1.6 prep.1
  14.9 1.5 collective-permute-start
  16.4 3.6 %collective-permute-start.1 = (bf16[304,256]{1,0:T(8,128)(2,1)}, bf16[304,256]{1,0:T(8,128)(2,1)S(1)}, u32[]{:S(2)}, u32[]{:S(2)}) collective-permute-start(bf16[304,256]{1,0:T(8,128)(2,1)} %get-tuple-element.32), channel_id=1, source_target_pairs={{0,7},{1,6},{2,15},{3,14},{4,23},{5,22},{6,31},{7,30},{8,1},{9,0},... | collective-permute-start | bytes 466952 | tf_op jit(solution)/shard_map/ppermute | solution.py:377
  20.0 3.3 %collective-permute-done.refs_1_ = bf16[304,256]{1,0:T(8,128)(2,1)S(1)} collective-permute-done((bf16[304,256]{1,0:T(8,128)(2,1)}, bf16[304,256]{1,0:T(8,128)(2,1)S(1)}, u32[]{:S(2)}, u32[]{:S(2)}) %collective-permute-start) | collective-permute-done | bytes 155680 | tf_op jit(solution)/shard_map/ppermute | solution.py:377
  24.7 2.9 %collective-permute-done.1.refs_2_ = bf16[304,256]{1,0:T(8,128)(2,1)S(1)} collective-permute-done((bf16[304,256]{1,0:T(8,128)(2,1)}, bf16[304,256]{1,0:T(8,128)(2,1)S(1)}, u32[]{:S(2)}, u32[]{:S(2)}) %collective-permute-start.1) | collective-permute-done | bytes 155680 | tf_op jit(solution)/shard_map/ppermute | solution.py:377
  29.0 6.5 %collective-permute-start.11 = (bf16[608,256]{1,0:T(8,128)(2,1)}, bf16[608,256]{1,0:T(8,128)(2,1)}, u32[]{:S(2)}, u32[]{:S(2)}) collective-permute-start(bf16[608,256]{1,0:T(8,128)(2,1)} %constant_dynamic-update-slice_fusion), channel_id=1, source_target_pairs={{0,6},{1,7},{2,0},{3,1},{4,2},{5,3},{6,4},{7,5},{8,14},{9,15},{10,... | collective-permute-start | bytes 933896 | tf_op jit(solution)/shard_map/ppermute | solution.py:377
  35.5 1.9 collective-permute-start.7
  37.5 7.7 %collective-permute-done.7.refs_3_ = bf16[304,256]{1,0:T(8,128)(2,1)} collective-permute-done((bf16[304,256]{1,0:T(8,128)(2,1)}, bf16[304,256]{1,0:T(8,128)(2,1)}, u32[]{:S(2)}, u32[]{:S(2)}) %collective-permute-start.7) | collective-permute-done | bytes 155680 | tf_op jit(solution)/shard_map/ppermute | solution.py:377
  47.4 2.0 copy-done.4
  52.7 6.5 %gate_up_partial.4 = (f32[2,128,768]{2,1,0:T(8,128)S(1)}, bf16[2,128,768]{2,1,0:T(8,128)(2,1)S(1)}, f32[8,256]{1,0:T(8,128)S(1)}, bf16[256,128]{1,0:T(8,128)(2,1)S(1)}) custom-call(s32[3]{0:T(128)S(1)} %pad_add_fusion.refs_0_, bf16[304,256]{1,0:T(8,128)(2,1)S(1)} %copy-done.12, bf16[304,256]{1,0:T(8,128)(2,1)S(1)} %copy-done.14, ...), custom_call_target="tpu_custom_call" | custom-call | flops 1811939328 | bytes 8257536 | tf_op jit(solution)/shard_map/gate_up_partial/pallas_call | solution.py:165
  59.2 6.0 %collective-permute-start.9 = (bf16[2,128,768]{2,1,0:T(8,128)(2,1)S(1)}, bf16[2,128,768]{2,1,0:T(8,128)(2,1)S(1)}, u32[]{:S(2)}, u32[]{:S(2)}) collective-permute-start(bf16[2,128,768]{2,1,0:T(8,128)(2,1)S(1)} %get-tuple-element.35), channel_id=1, source_target_pairs={{0,16},{1,17},{2,18},{3,19},{4,20},{5,21},{6,22},{7,23},{8,24},{9,... | collective-permute-start | bytes 1179656 | tf_op jit(solution)/shard_map/ppermute | solution.py:377
  65.8 7.0 %gate_up_partial.5 = (f32[2,128,768]{2,1,0:T(8,128)S(1)}, bf16[2,128,768]{2,1,0:T(8,128)(2,1)S(1)}, f32[8,256]{1,0:T(8,128)S(1)}, bf16[256,128]{1,0:T(8,128)(2,1)S(1)}) custom-call(s32[3]{0:T(128)S(1)} %pad_add_fusion.refs_0_, bf16[608,256]{1,0:T(8,128)(2,1)} %collective-permute-done.11.refs_1_, bf16[608,256]{1,0:T(8,128)(2,1)} %collective-permute-done.12.refs_2_, ...), custom_call_target="tpu_custom_call" | custom-call | flops 1811939328 | bytes 8257536 | tf_op jit(solution)/shard_map/gate_up_partial/pallas_call | solution.py:165
  73.3 1.6 collective-permute-start.10
  74.9 9.6 %collective-permute-done.10.meta_recv = f32[8,256]{1,0:T(8,128)S(1)} collective-permute-done((f32[8,256]{1,0:T(8,128)S(1)}, f32[8,256]{1,0:T(8,128)S(1)}, u32[]{:S(2)}, u32[]{:S(2)}) %collective-permute-start.10) | collective-permute-done | bytes 8224 | tf_op jit(solution)/shard_map/ppermute | solution.py:377
  84.5 1.3 act.4.refs_9_.refs_1_
  88.0 7.2 %gate_up_partial.6 = (f32[2,128,768]{2,1,0:T(8,128)S(1)}, bf16[2,128,768]{2,1,0:T(8,128)(2,1)}, f32[8,256]{1,0:T(8,128)S(1)}, bf16[256,128]{1,0:T(8,128)(2,1)S(1)}) custom-call(s32[3]{0:T(128)S(1)} %pad_add_fusion.refs_0_, bf16[608,256]{1,0:T(8,128)(2,1)} %collective-permute-done.18.refs_1_, bf16[608,256]{1,0:T(8,128)(2,1)S(1)} %collective-permute-done.19.refs_2_, ...), custom_call_target="tpu_custom_call" | custom-call | flops 1811939328 | bytes 8257536 | tf_op jit(solution)/shard_map/gate_up_partial/pallas_call | solution.py:165
  95.3 1.3 act.5.refs_7_.refs_1_
  99.6 5.9 %copy.15.refs_6_ = bf16[4,720,576]{2,1,0:T(8,128)(2,1)} copy(bf16[4,720,576]{1,2,0:T(8,128)(2,1)} %param.18) | data formatting | bytes 6635520 | tf_op args[7]
  106.6 2.0 copy-done
  109.5 4.2 %down.4 = (bf16[288,256]{1,0:T(8,128)(2,1)S(1)}, bf16[288,256]{1,0:T(8,128)(2,1)S(1)}) custom-call(s32[3]{0:T(128)S(1)} %pad_add_fusion.refs_0_, bf16[2,128,384]{2,1,0:T(8,128)(2,1)} %act.4.refs_9_.refs_1_, bf16[2,128,384]{2,1,0:T(8,128)(2,1)} %collective-permute-done.13.refs_2_, bf16[2,128,384]{2,1,0:T(8,128)(2,1)} %collective-permute-done.14.refs_3_, ...), custom_call_target="tpu_custom_call" | custom-call | flops 849346560 | bytes 3612672 | tf_op jit(solution)/shard_map/down/pallas_call | solution.py:251
  114.8 7.0 %gate_up_partial.7 = (f32[2,128,768]{2,1,0:T(8,128)S(1)}, bf16[2,128,768]{2,1,0:T(8,128)(2,1)S(1)}, f32[8,256]{1,0:T(8,128)S(1)}, bf16[256,128]{1,0:T(8,128)(2,1)S(1)}) custom-call(s32[3]{0:T(128)S(1)} %pad_add_fusion.refs_0_, bf16[608,256]{1,0:T(8,128)(2,1)} %collective-permute-done.2.refs_1_.meta, bf16[608,256]{1,0:T(8,128)(2,1)} %collective-permute-done.4.refs_2_, ...), custom_call_target="tpu_custom_call" | custom-call | flops 1811939328 | bytes 8257536 | tf_op jit(solution)/shard_map/gate_up_partial/pallas_call | solution.py:165
  121.8 1.7 collective-permute-start.20
  123.5 1.6 act.6.refs_7_.refs_1_
  125.6 3.9 %down.5 = (bf16[288,256]{1,0:T(8,128)(2,1)S(1)}, bf16[288,256]{1,0:T(8,128)(2,1)S(1)}) custom-call(s32[3]{0:T(128)S(1)} %pad_add_fusion.refs_0_, bf16[2,128,384]{2,1,0:T(8,128)(2,1)} %act.5.refs_7_.refs_1_, bf16[2,128,384]{2,1,0:T(8,128)(2,1)} %collective-permute-done.22.refs_2_, bf16[2,128,384]{2,1,0:T(8,128)(2,1)S(1)} %collective-permute-done.23.refs_3_, ...), custom_call_target="tpu_custom_call" | custom-call | flops 849346560 | bytes 3612672 | tf_op jit(solution)/shard_map/down/pallas_call | solution.py:251
  130.7 1.2 collective-permute-start.21
  131.9 5.5 %collective-permute-done.31.refs_2_ = bf16[2,128,384]{2,1,0:T(8,128)(2,1)S(1)} collective-permute-done((bf16[2,128,384]{2,1,0:T(8,128)(2,1)S(1)}, bf16[2,128,384]{2,1,0:T(8,128)(2,1)S(1)}, u32[]{:S(2)}, u32[]{:S(2)}) %collective-permute-start.31) | collective-permute-done | bytes 196640 | tf_op jit(solution)/shard_map/ppermute | solution.py:377
  137.4 2.6 %collective-permute-start.35 = (bf16[288,256]{1,0:T(8,128)(2,1)S(1)}, bf16[288,256]{1,0:T(8,128)(2,1)S(1)}, u32[]{:S(2)}, u32[]{:S(2)}) collective-permute-start(bf16[288,256]{1,0:T(8,128)(2,1)S(1)} %add_convert_fusion.2.refs_8_), channel_id=1, source_target_pairs={{0,2},{1,3},{2,4},{3,5},{4,6},{5,7},{6,0},{7,1},{8,10},{9,11},{10,... | collective-permute-start | bytes 442376 | tf_op jit(solution)/shard_map/ppermute | solution.py:377
  140.7 1.8 collective-permute-start.28
  142.5 1.9 collective-permute-done.35.refs_9_.refs_2_
  144.4 3.4 %down.6 = (bf16[288,256]{1,0:T(8,128)(2,1)S(1)}, bf16[288,256]{1,0:T(8,128)(2,1)S(1)}) custom-call(s32[3]{0:T(128)S(1)} %pad_add_fusion.refs_0_, bf16[2,128,384]{2,1,0:T(8,128)(2,1)S(1)} %act.6.refs_7_.refs_1_, bf16[2,128,384]{2,1,0:T(8,128)(2,1)S(1)} %collective-permute-done.31.refs_2_, bf16[2,128,384]{2,1,0:T(8,128)(2,1)S(1)} %collective-permute-done.32.refs_3_, ...), custom_call_target="tpu_custom_call" | custom-call | flops 849346560 | bytes 3612672 | tf_op jit(solution)/shard_map/down/pallas_call | solution.py:251
  150.5 2.4 %collective-permute-done.38 = bf16[288,256]{1,0:T(8,128)(2,1)S(1)} collective-permute-done((bf16[288,256]{1,0:T(8,128)(2,1)S(1)}, bf16[288,256]{1,0:T(8,128)(2,1)S(1)}, u32[]{:S(2)}, u32[]{:S(2)}) %collective-permute-start.38) | collective-permute-done | bytes 147488 | tf_op jit(solution)/shard_map/ppermute | solution.py:377
  154.0 4.1 %collective-permute-done.36.refs_8_.refs_3_ = bf16[288,256]{1,0:T(8,128)(2,1)S(1)} collective-permute-done((bf16[288,256]{1,0:T(8,128)(2,1)S(1)}, bf16[288,256]{1,0:T(8,128)(2,1)S(1)}, u32[]{:S(2)}, u32[]{:S(2)}) %collective-permute-start.36) | collective-permute-done | bytes 147488 | tf_op jit(solution)/shard_map/ppermute | solution.py:377
  158.2 3.4 %down.7 = (bf16[288,256]{1,0:T(8,128)(2,1)S(1)}, bf16[288,256]{1,0:T(8,128)(2,1)S(1)}) custom-call(s32[3]{0:T(128)S(1)} %pad_add_fusion.refs_0_, bf16[2,128,384]{2,1,0:T(8,128)(2,1)S(1)} %act.7.refs_7_.refs_1_, bf16[2,128,384]{2,1,0:T(8,128)(2,1)S(1)} %collective-permute-done.28.refs_2_, bf16[2,128,384]{2,1,0:T(8,128)(2,1)S(1)} %collective-permute-done.29.refs_3_, ...), custom_call_target="tpu_custom_call" | custom-call | flops 849346560 | bytes 3612672 | tf_op jit(solution)/shard_map/down/pallas_call | solution.py:251
  162.6 2.5 %collective-permute-start.3 = (f32[4,288]{1,0:T(4,128)S(1)}, f32[4,288]{1,0:T(4,128)S(1)}, u32[]{:S(2)}, u32[]{:S(2)}) collective-permute-start(f32[4,288]{1,0:T(4,128)S(1)} %copy-done.28), channel_id=1, source_target_pairs={{0,0},{1,1},{2,8},{3,9},{4,16},{5,17},{6,24},{7,25},{8,2},{9,3},{1... | collective-permute-start | bytes 13832 | tf_op jit(solution)/shard_map/ppermute | solution.py:377
  165.1 4.8 %collective-permute-done.3.stream = f32[4,288]{1,0:T(4,128)S(1)} collective-permute-done((f32[4,288]{1,0:T(4,128)S(1)}, f32[4,288]{1,0:T(4,128)S(1)}, u32[]{:S(2)}, u32[]{:S(2)}) %collective-permute-start.3) | collective-permute-done | bytes 4640 | tf_op jit(solution)/shard_map/ppermute | solution.py:377
  169.9 1.8 branch_total.1
  171.7 3.6 %all-to-all-start = ((f32[32,4,288]{2,1,0:T(4,128)}), f32[32,4,288]{2,1,0:T(4,128)S(1)}, u32[]{:S(2)}, u32[]{:S(2)}) async-start(f32[32,4,288]{2,1,0:T(4,128)} %get-tuple-element.59), calls=%async_computation | async-start | bytes 393216 | tf_op jit(solution)/shard_map/all_to_all | solution.py:457
  175.5 7.5 %all-to-all-done.refs_0_ = f32[32,4,288]{2,1,0:T(4,128)S(1)} async-done(((f32[32,4,288]{2,1,0:T(4,128)}), f32[32,4,288]{2,1,0:T(4,128)S(1)}, u32[]{:S(2)}, u32[]{:S(2)}) %all-to-all-start) | async-done | bytes 147488 | tf_op jit(solution)/shard_map/all_to_all | solution.py:457
  183.0 1.4 head.1
  184.4 3.9 %all-to-all-start.1 = ((f32[32,2,16]{2,1,0:T(2,128)}), f32[32,2,16]{2,1,0:T(2,128)S(1)}, u32[]{:S(2)}, u32[]{:S(2)}) async-start(f32[32,2,16]{2,1,0:T(2,128)} %get-tuple-element.61), calls=%async_computation.1 | async-start | bytes 65536 | tf_op jit(solution)/shard_map/all_to_all | solution.py:457
  188.4 4.3 %collective-permute-start.40 = (f32[288,256]{1,0:T(8,128)S(1)}, f32[288,256]{1,0:T(8,128)S(1)}, u32[]{:S(2)}, u32[]{:S(2)}) collective-permute-start(f32[288,256]{1,0:T(8,128)S(1)} %get-tuple-element.58), channel_id=1, source_target_pairs={{0,0},{1,1},{2,8},{3,9},{4,16},{5,17},{6,24},{7,25},{8,2},{9,3},{1... | collective-permute-start | bytes 884744 | tf_op jit(solution)/shard_map/ppermute | solution.py:377
  192.6 1.8 all-to-all-done.1
  195.2 12.5 %collective-permute-done.40 = f32[288,256]{1,0:T(8,128)S(1)} collective-permute-done((f32[288,256]{1,0:T(8,128)S(1)}, f32[288,256]{1,0:T(8,128)S(1)}, u32[]{:S(2)}, u32[]{:S(2)}) %collective-permute-start.40) | collective-permute-done | bytes 294944 | tf_op jit(solution)/shard_map/ppermute | solution.py:377
  (148 shorter events, 29.1 us)
Async XLA Ops:
  5.4 41.9 %collective-permute-start.5 = (bf16[4,576,384]{2,1,0:T(8,128)(2,1)}, bf16[4,576,384]{2,1,0:T(8,128)(2,1)}, u32[]{:S(2)}, u32[]{:S(2)}) collective-permute-start(bf16[4,576,384]{2,1,0:T(8,128)(2,1)} %slice_select_fusion.1), channel_id=1, source_target_pairs={{0,8},{1,9},{2,10},{3,11},{4,12},{5,13},{6,14},{7,15},{8,0},{9,1},... | collective-permute-start | bytes 5308424 | tf_op jit(solution)/shard_map/ppermute | solution.py:377
  6.9 40.4 %copy-start.2 = (bf16[4,576,720]{2,1,0:T(8,128)(2,1)S(1)}, bf16[4,576,720]{2,1,0:T(8,128)(2,1)}, u32[]{:S(2)}) copy-start(bf16[4,576,720]{2,1,0:T(8,128)(2,1)} %refs_5_.5) | copy-start | bytes 9953284
  8.7 38.7 %collective-permute-start.6 = (bf16[4,576,384]{2,1,0:T(8,128)(2,1)}, bf16[4,576,384]{2,1,0:T(8,128)(2,1)}, u32[]{:S(2)}, u32[]{:S(2)}) collective-permute-start(bf16[4,576,384]{2,1,0:T(8,128)(2,1)} %slice_select_fusion), channel_id=1, source_target_pairs={{0,8},{1,9},{2,10},{3,11},{4,12},{5,13},{6,14},{7,15},{8,0},{9,1},... | collective-permute-start | bytes 5308424 | tf_op jit(solution)/shard_map/ppermute | solution.py:377
  14.9 8.4 %collective-permute-start = (bf16[304,256]{1,0:T(8,128)(2,1)}, bf16[304,256]{1,0:T(8,128)(2,1)S(1)}, u32[]{:S(2)}, u32[]{:S(2)}) collective-permute-start(bf16[304,256]{1,0:T(8,128)(2,1)} %get-tuple-element.32), channel_id=1, source_target_pairs={{0,6},{1,7},{2,14},{3,15},{4,22},{5,23},{6,30},{7,31},{8,0},{9,1},... | collective-permute-start | bytes 466952 | tf_op jit(solution)/shard_map/ppermute | solution.py:377
  16.4 11.2 %collective-permute-start.1 = (bf16[304,256]{1,0:T(8,128)(2,1)}, bf16[304,256]{1,0:T(8,128)(2,1)S(1)}, u32[]{:S(2)}, u32[]{:S(2)}) collective-permute-start(bf16[304,256]{1,0:T(8,128)(2,1)} %get-tuple-element.32), channel_id=1, source_target_pairs={{0,7},{1,6},{2,15},{3,14},{4,23},{5,22},{6,31},{7,30},{8,1},{9,0},... | collective-permute-start | bytes 466952 | tf_op jit(solution)/shard_map/ppermute | solution.py:377
  29.0 16.2 %collective-permute-start.11 = (bf16[608,256]{1,0:T(8,128)(2,1)}, bf16[608,256]{1,0:T(8,128)(2,1)}, u32[]{:S(2)}, u32[]{:S(2)}) collective-permute-start(bf16[608,256]{1,0:T(8,128)(2,1)} %constant_dynamic-update-slice_fusion), channel_id=1, source_target_pairs={{0,6},{1,7},{2,0},{3,1},{4,2},{5,3},{6,4},{7,5},{8,14},{9,15},{10,... | collective-permute-start | bytes 933896 | tf_op jit(solution)/shard_map/ppermute | solution.py:377
  35.5 9.7 %collective-permute-start.7 = (bf16[304,256]{1,0:T(8,128)(2,1)}, bf16[304,256]{1,0:T(8,128)(2,1)}, u32[]{:S(2)}, u32[]{:S(2)}) collective-permute-start(bf16[304,256]{1,0:T(8,128)(2,1)} %get-tuple-element.32), channel_id=1, source_target_pairs={{0,14},{1,15},{2,6},{3,7},{4,30},{5,31},{6,22},{7,23},{8,8},{9,9},... | collective-permute-start | bytes 466952 | tf_op jit(solution)/shard_map/ppermute | solution.py:377
  37.4 10.0 %collective-permute-start.8 = (bf16[304,256]{1,0:T(8,128)(2,1)}, bf16[304,256]{1,0:T(8,128)(2,1)}, u32[]{:S(2)}, u32[]{:S(2)}) collective-permute-start(bf16[304,256]{1,0:T(8,128)(2,1)} %get-tuple-element.32), channel_id=1, source_target_pairs={{0,15},{1,14},{2,7},{3,6},{4,31},{5,30},{6,23},{7,22},{8,9},{9,8},... | collective-permute-start | bytes 466952 | tf_op jit(solution)/shard_map/ppermute | solution.py:377
  45.2 20.6 %collective-permute-start.18 = (bf16[608,256]{1,0:T(8,128)(2,1)}, bf16[608,256]{1,0:T(8,128)(2,1)}, u32[]{:S(2)}, u32[]{:S(2)}) collective-permute-start(bf16[608,256]{1,0:T(8,128)(2,1)} %constant_dynamic-update-slice_fusion), channel_id=1, source_target_pairs={{0,4},{1,5},{2,6},{3,7},{4,0},{5,1},{6,2},{7,3},{8,12},{9,13},{10,... | collective-permute-start | bytes 933896 | tf_op jit(solution)/shard_map/ppermute | solution.py:377
  45.2 20.6 %collective-permute-start.12 = (bf16[608,256]{1,0:T(8,128)(2,1)}, bf16[608,256]{1,0:T(8,128)(2,1)}, u32[]{:S(2)}, u32[]{:S(2)}) collective-permute-start(bf16[608,256]{1,0:T(8,128)(2,1)} %collective-permute-done.11.refs_1_), channel_id=1, source_target_pairs={{0,8},{1,9},{2,10},{3,11},{4,12},{5,13},{6,14},{7,15},{8,0},{9,1},... | collective-permute-start | bytes 933896 | tf_op jit(solution)/shard_map/ppermute | solution.py:377
  59.2 25.3 %copy-start.22 = (bf16[256,128]{1,0:T(8,128)(2,1)}, bf16[256,128]{1,0:T(8,128)(2,1)S(1)}, u32[]{:S(2)}) copy-start(bf16[256,128]{1,0:T(8,128)(2,1)S(1)} %get-tuple-element.37.cols.refs_5_) | copy-start | bytes 196612
  59.2 25.3 %collective-permute-start.9 = (bf16[2,128,768]{2,1,0:T(8,128)(2,1)S(1)}, bf16[2,128,768]{2,1,0:T(8,128)(2,1)S(1)}, u32[]{:S(2)}, u32[]{:S(2)}) collective-permute-start(bf16[2,128,768]{2,1,0:T(8,128)(2,1)S(1)} %get-tuple-element.35), channel_id=1, source_target_pairs={{0,16},{1,17},{2,18},{3,19},{4,20},{5,21},{6,22},{7,23},{8,24},{9,... | collective-permute-start | bytes 1179656 | tf_op jit(solution)/shard_map/ppermute | solution.py:377
  65.2 21.4 %collective-permute-start.2 = (bf16[608,256]{1,0:T(8,128)(2,1)}, bf16[608,256]{1,0:T(8,128)(2,1)}, u32[]{:S(2)}, u32[]{:S(2)}) collective-permute-start(bf16[608,256]{1,0:T(8,128)(2,1)} %constant_dynamic-update-slice_fusion), channel_id=1, source_target_pairs={{0,2},{1,3},{2,4},{3,5},{4,6},{5,7},{6,0},{7,1},{8,10},{9,11},{10,... | collective-permute-start | bytes 933896 | tf_op jit(solution)/shard_map/ppermute | solution.py:377
  65.8 22.1 %collective-permute-start.19 = (bf16[608,256]{1,0:T(8,128)(2,1)}, bf16[608,256]{1,0:T(8,128)(2,1)S(1)}, u32[]{:S(2)}, u32[]{:S(2)}) collective-permute-start(bf16[608,256]{1,0:T(8,128)(2,1)} %collective-permute-done.18.refs_1_), channel_id=1, source_target_pairs={{0,8},{1,9},{2,10},{3,11},{4,12},{5,13},{6,14},{7,15},{8,0},{9,1},... | collective-permute-start | bytes 933896 | tf_op jit(solution)/shard_map/ppermute | solution.py:377
  72.8 22.5 %copy-start.20 = (bf16[256,128]{1,0:T(8,128)(2,1)}, bf16[256,128]{1,0:T(8,128)(2,1)S(1)}, u32[]{:S(2)}) copy-start(bf16[256,128]{1,0:T(8,128)(2,1)S(1)} %get-tuple-element.41.cols.refs_5_) | copy-start | bytes 196612
  72.8 22.5 %collective-permute-start.16 = (bf16[2,128,768]{2,1,0:T(8,128)(2,1)S(1)}, bf16[2,128,768]{2,1,0:T(8,128)(2,1)S(1)}, u32[]{:S(2)}, u32[]{:S(2)}) collective-permute-start(bf16[2,128,768]{2,1,0:T(8,128)(2,1)S(1)} %get-tuple-element.39), channel_id=1, source_target_pairs={{0,16},{1,17},{2,18},{3,19},{4,20},{5,21},{6,22},{7,23},{8,24},{9,... | collective-permute-start | bytes 1179656 | tf_op jit(solution)/shard_map/ppermute | solution.py:377
  73.3 11.2 %collective-permute-start.10 = (f32[8,256]{1,0:T(8,128)S(1)}, f32[8,256]{1,0:T(8,128)S(1)}, u32[]{:S(2)}, u32[]{:S(2)}) collective-permute-start(f32[8,256]{1,0:T(8,128)S(1)} %get-tuple-element.36.meta), channel_id=1, source_target_pairs={{0,16},{1,17},{2,18},{3,19},{4,20},{5,21},{6,22},{7,23},{8,24},{9,... | collective-permute-start | bytes 24584 | tf_op jit(solution)/shard_map/ppermute | solution.py:377
  85.8 12.6 %collective-permute-start.13 = (bf16[2,128,384]{2,1,0:T(8,128)(2,1)}, bf16[2,128,384]{2,1,0:T(8,128)(2,1)}, u32[]{:S(2)}, u32[]{:S(2)}) collective-permute-start(bf16[2,128,384]{2,1,0:T(8,128)(2,1)} %act.4.refs_9_.refs_1_), channel_id=1, source_target_pairs={{0,16},{1,17},{2,18},{3,19},{4,20},{5,21},{6,22},{7,23},{8,24},{9,... | collective-permute-start | bytes 589832 | tf_op jit(solution)/shard_map/ppermute | solution.py:377
  86.6 27.1 %collective-permute-start.4 = (bf16[608,256]{1,0:T(8,128)(2,1)}, bf16[608,256]{1,0:T(8,128)(2,1)}, u32[]{:S(2)}, u32[]{:S(2)}) collective-permute-start(bf16[608,256]{1,0:T(8,128)(2,1)} %collective-permute-done.2.refs_1_.meta), channel_id=1, source_target_pairs={{0,8},{1,9},{2,10},{3,11},{4,12},{5,13},{6,14},{7,15},{8,0},{9,1},... | collective-permute-start | bytes 933896 | tf_op jit(solution)/shard_map/ppermute | solution.py:377
  86.6 8.7 %collective-permute-start.17 = (f32[8,256]{1,0:T(8,128)S(1)}, f32[8,256]{1,0:T(8,128)S(1)}, u32[]{:S(2)}, u32[]{:S(2)}) collective-permute-start(f32[8,256]{1,0:T(8,128)S(1)} %get-tuple-element.40.meta), channel_id=1, source_target_pairs={{0,16},{1,17},{2,18},{3,19},{4,20},{5,21},{6,22},{7,23},{8,24},{9,... | collective-permute-start | bytes 24584 | tf_op jit(solution)/shard_map/ppermute | solution.py:377
  87.8 17.7 %collective-permute-start.14 = (bf16[2,128,384]{2,1,0:T(8,128)(2,1)}, bf16[2,128,384]{2,1,0:T(8,128)(2,1)}, u32[]{:S(2)}, u32[]{:S(2)}) collective-permute-start(bf16[2,128,384]{2,1,0:T(8,128)(2,1)} %act.4.refs_9_.refs_1_), channel_id=1, source_target_pairs={{0,8},{1,9},{2,10},{3,11},{4,12},{5,13},{6,14},{7,15},{8,0},{9,1},... | collective-permute-start | bytes 589832 | tf_op jit(solution)/shard_map/ppermute | solution.py:377
  97.5 8.2 %collective-permute-start.22 = (bf16[2,128,384]{2,1,0:T(8,128)(2,1)}, bf16[2,128,384]{2,1,0:T(8,128)(2,1)}, u32[]{:S(2)}, u32[]{:S(2)}) collective-permute-start(bf16[2,128,384]{2,1,0:T(8,128)(2,1)} %act.5.refs_7_.refs_1_), channel_id=1, source_target_pairs={{0,16},{1,17},{2,18},{3,19},{4,20},{5,21},{6,22},{7,23},{8,24},{9,... | collective-permute-start | bytes 589832 | tf_op jit(solution)/shard_map/ppermute | solution.py:377
  98.4 8.2 %collective-permute-start.15 = (bf16[2,128,384]{2,1,0:T(8,128)(2,1)}, bf16[2,128,384]{2,1,0:T(8,128)(2,1)}, u32[]{:S(2)}, u32[]{:S(2)}) collective-permute-start(bf16[2,128,384]{2,1,0:T(8,128)(2,1)} %collective-permute-done.13.refs_2_), channel_id=1, source_target_pairs={{0,8},{1,9},{2,10},{3,11},{4,12},{5,13},{6,14},{7,15},{8,0},{9,1},... | collective-permute-start | bytes 589832 | tf_op jit(solution)/shard_map/ppermute | solution.py:377
  98.4 25.1 %collective-permute-start.25 = (bf16[2,128,768]{2,1,0:T(8,128)(2,1)}, bf16[2,128,768]{2,1,0:T(8,128)(2,1)}, u32[]{:S(2)}, u32[]{:S(2)}) collective-permute-start(bf16[2,128,768]{2,1,0:T(8,128)(2,1)} %get-tuple-element.48), channel_id=1, source_target_pairs={{0,16},{1,17},{2,18},{3,19},{4,20},{5,21},{6,22},{7,23},{8,24},{9,... | collective-permute-start | bytes 1179656 | tf_op jit(solution)/shard_map/ppermute | solution.py:377
  105.5 20.1 %collective-permute-start.23 = (bf16[2,128,384]{2,1,0:T(8,128)(2,1)}, bf16[2,128,384]{2,1,0:T(8,128)(2,1)S(1)}, u32[]{:S(2)}, u32[]{:S(2)}) collective-permute-start(bf16[2,128,384]{2,1,0:T(8,128)(2,1)} %act.5.refs_7_.refs_1_), channel_id=1, source_target_pairs={{0,8},{1,9},{2,10},{3,11},{4,12},{5,13},{6,14},{7,15},{8,0},{9,1},... | collective-permute-start | bytes 589832 | tf_op jit(solution)/shard_map/ppermute | solution.py:377
  105.7 16.0 %collective-permute-start.26 = (f32[8,256]{1,0:T(8,128)S(1)}, f32[8,256]{1,0:T(8,128)S(1)}, u32[]{:S(2)}, u32[]{:S(2)}) collective-permute-start(f32[8,256]{1,0:T(8,128)S(1)} %get-tuple-element.49.meta), channel_id=1, source_target_pairs={{0,16},{1,17},{2,18},{3,19},{4,20},{5,21},{6,22},{7,23},{8,24},{9,... | collective-permute-start | bytes 24584 | tf_op jit(solution)/shard_map/ppermute | solution.py:377
  106.6 19.0 %collective-permute-start.24 = (bf16[2,128,384]{2,1,0:T(8,128)(2,1)}, bf16[2,128,384]{2,1,0:T(8,128)(2,1)S(1)}, u32[]{:S(2)}, u32[]{:S(2)}) collective-permute-start(bf16[2,128,384]{2,1,0:T(8,128)(2,1)} %collective-permute-done.22.refs_2_), channel_id=1, source_target_pairs={{0,8},{1,9},{2,10},{3,11},{4,12},{5,13},{6,14},{7,15},{8,0},{9,1},... | collective-permute-start | bytes 589832 | tf_op jit(solution)/shard_map/ppermute | solution.py:377
  113.7 11.8 %collective-permute-start.27 = (bf16[288,256]{1,0:T(8,128)(2,1)S(1)}, bf16[288,256]{1,0:T(8,128)(2,1)S(1)}, u32[]{:S(2)}, u32[]{:S(2)}) collective-permute-start(bf16[288,256]{1,0:T(8,128)(2,1)S(1)} %get-tuple-element.51), channel_id=1, source_target_pairs={{0,1},{1,0},{2,3},{3,2},{4,5},{5,4},{6,7},{7,6},{8,9},{9,8},{10,11... | collective-permute-start | bytes 442376 | tf_op jit(solution)/shard_map/ppermute | solution.py:377
  121.8 18.3 %collective-permute-start.20 = (bf16[2,128,768]{2,1,0:T(8,128)(2,1)S(1)}, bf16[2,128,768]{2,1,0:T(8,128)(2,1)S(1)}, u32[]{:S(2)}, u32[]{:S(2)}) collective-permute-start(bf16[2,128,768]{2,1,0:T(8,128)(2,1)S(1)} %get-tuple-element.45), channel_id=1, source_target_pairs={{0,16},{1,17},{2,18},{3,19},{4,20},{5,21},{6,22},{7,23},{8,24},{9,... | collective-permute-start | bytes 1179656 | tf_op jit(solution)/shard_map/ppermute | solution.py:377
  125.0 12.4 %collective-permute-start.31 = (bf16[2,128,384]{2,1,0:T(8,128)(2,1)S(1)}, bf16[2,128,384]{2,1,0:T(8,128)(2,1)S(1)}, u32[]{:S(2)}, u32[]{:S(2)}) collective-permute-start(bf16[2,128,384]{2,1,0:T(8,128)(2,1)S(1)} %act.6.refs_7_.refs_1_), channel_id=1, source_target_pairs={{0,16},{1,17},{2,18},{3,19},{4,20},{5,21},{6,22},{7,23},{8,24},{9,... | collective-permute-start | bytes 589832 | tf_op jit(solution)/shard_map/ppermute | solution.py:377
  129.6 10.5 %collective-permute-start.34 = (bf16[288,256]{1,0:T(8,128)(2,1)S(1)}, bf16[288,256]{1,0:T(8,128)(2,1)S(1)}, u32[]{:S(2)}, u32[]{:S(2)}) collective-permute-start(bf16[288,256]{1,0:T(8,128)(2,1)S(1)} %get-tuple-element.53), channel_id=1, source_target_pairs={{0,1},{1,0},{2,3},{3,2},{4,5},{5,4},{6,7},{7,6},{8,9},{9,8},{10,11... | collective-permute-start | bytes 442376 | tf_op jit(solution)/shard_map/ppermute | solution.py:377
  130.7 11.8 %collective-permute-start.32 = (bf16[2,128,384]{2,1,0:T(8,128)(2,1)S(1)}, bf16[2,128,384]{2,1,0:T(8,128)(2,1)S(1)}, u32[]{:S(2)}, u32[]{:S(2)}) collective-permute-start(bf16[2,128,384]{2,1,0:T(8,128)(2,1)S(1)} %act.6.refs_7_.refs_1_), channel_id=1, source_target_pairs={{0,8},{1,9},{2,10},{3,11},{4,12},{5,13},{6,14},{7,15},{8,0},{9,1},... | collective-permute-start | bytes 589832 | tf_op jit(solution)/shard_map/ppermute | solution.py:377
  130.7 9.4 %collective-permute-start.21 = (f32[8,256]{1,0:T(8,128)S(1)}, f32[8,256]{1,0:T(8,128)S(1)}, u32[]{:S(2)}, u32[]{:S(2)}) collective-permute-start(f32[8,256]{1,0:T(8,128)S(1)} %get-tuple-element.46.meta), channel_id=1, source_target_pairs={{0,16},{1,17},{2,18},{3,19},{4,20},{5,21},{6,22},{7,23},{8,24},{9,... | collective-permute-start | bytes 24584 | tf_op jit(solution)/shard_map/ppermute | solution.py:377
  137.4 6.9 %collective-permute-start.35 = (bf16[288,256]{1,0:T(8,128)(2,1)S(1)}, bf16[288,256]{1,0:T(8,128)(2,1)S(1)}, u32[]{:S(2)}, u32[]{:S(2)}) collective-permute-start(bf16[288,256]{1,0:T(8,128)(2,1)S(1)} %add_convert_fusion.2.refs_8_), channel_id=1, source_target_pairs={{0,2},{1,3},{2,4},{3,5},{4,6},{5,7},{6,0},{7,1},{8,10},{9,11},{10,... | collective-permute-start | bytes 442376 | tf_op jit(solution)/shard_map/ppermute | solution.py:377
  140.0 4.3 %collective-permute-start.33 = (bf16[2,128,384]{2,1,0:T(8,128)(2,1)S(1)}, bf16[2,128,384]{2,1,0:T(8,128)(2,1)S(1)}, u32[]{:S(2)}, u32[]{:S(2)}) collective-permute-start(bf16[2,128,384]{2,1,0:T(8,128)(2,1)S(1)} %collective-permute-done.31.refs_2_), channel_id=1, source_target_pairs={{0,8},{1,9},{2,10},{3,11},{4,12},{5,13},{6,14},{7,15},{8,0},{9,1},... | collective-permute-start | bytes 589832 | tf_op jit(solution)/shard_map/ppermute | solution.py:377
  140.7 9.4 %collective-permute-start.28 = (bf16[2,128,384]{2,1,0:T(8,128)(2,1)S(1)}, bf16[2,128,384]{2,1,0:T(8,128)(2,1)S(1)}, u32[]{:S(2)}, u32[]{:S(2)}) collective-permute-start(bf16[2,128,384]{2,1,0:T(8,128)(2,1)S(1)} %act.7.refs_7_.refs_1_), channel_id=1, source_target_pairs={{0,16},{1,17},{2,18},{3,19},{4,20},{5,21},{6,22},{7,23},{8,24},{9,... | collective-permute-start | bytes 589832 | tf_op jit(solution)/shard_map/ppermute | solution.py:377
  147.7 5.2 %collective-permute-start.38 = (bf16[288,256]{1,0:T(8,128)(2,1)S(1)}, bf16[288,256]{1,0:T(8,128)(2,1)S(1)}, u32[]{:S(2)}, u32[]{:S(2)}) collective-permute-start(bf16[288,256]{1,0:T(8,128)(2,1)S(1)} %get-tuple-element.57), channel_id=1, source_target_pairs={{0,1},{1,0},{2,3},{3,2},{4,5},{5,4},{6,7},{7,6},{8,9},{9,8},{10,11... | collective-permute-start | bytes 442376 | tf_op jit(solution)/shard_map/ppermute | solution.py:377
  148.9 9.3 %collective-permute-start.36 = (bf16[288,256]{1,0:T(8,128)(2,1)S(1)}, bf16[288,256]{1,0:T(8,128)(2,1)S(1)}, u32[]{:S(2)}, u32[]{:S(2)}) collective-permute-start(bf16[288,256]{1,0:T(8,128)(2,1)S(1)} %add_convert_fusion.1.refs_8_), channel_id=1, source_target_pairs={{0,4},{1,5},{2,6},{3,7},{4,0},{5,1},{6,2},{7,3},{8,12},{9,13},{10,... | collective-permute-start | bytes 442376 | tf_op jit(solution)/shard_map/ppermute | solution.py:377
  150.0 8.1 %collective-permute-start.29 = (bf16[2,128,384]{2,1,0:T(8,128)(2,1)S(1)}, bf16[2,128,384]{2,1,0:T(8,128)(2,1)S(1)}, u32[]{:S(2)}, u32[]{:S(2)}) collective-permute-start(bf16[2,128,384]{2,1,0:T(8,128)(2,1)S(1)} %act.7.refs_7_.refs_1_), channel_id=1, source_target_pairs={{0,8},{1,9},{2,10},{3,11},{4,12},{5,13},{6,14},{7,15},{8,0},{9,1},... | collective-permute-start | bytes 589832 | tf_op jit(solution)/shard_map/ppermute | solution.py:377
  150.0 8.1 %collective-permute-start.30 = (bf16[2,128,384]{2,1,0:T(8,128)(2,1)S(1)}, bf16[2,128,384]{2,1,0:T(8,128)(2,1)S(1)}, u32[]{:S(2)}, u32[]{:S(2)}) collective-permute-start(bf16[2,128,384]{2,1,0:T(8,128)(2,1)S(1)} %collective-permute-done.28.refs_2_), channel_id=1, source_target_pairs={{0,8},{1,9},{2,10},{3,11},{4,12},{5,13},{6,14},{7,15},{8,0},{9,1},... | collective-permute-start | bytes 589832 | tf_op jit(solution)/shard_map/ppermute | solution.py:377
  153.0 16.9 %collective-permute-start.39 = (bf16[288,256]{1,0:T(8,128)(2,1)S(1)}, bf16[288,256]{1,0:T(8,128)(2,1)S(1)}, u32[]{:S(2)}, u32[]{:S(2)}) collective-permute-start(bf16[288,256]{1,0:T(8,128)(2,1)S(1)} %add_convert_fusion), channel_id=1, source_target_pairs={{0,6},{1,7},{2,0},{3,1},{4,2},{5,3},{6,4},{7,5},{8,14},{9,15},{10,... | collective-permute-start | bytes 442376 | tf_op jit(solution)/shard_map/ppermute | solution.py:377
  158.1 24.8 %copy-start.9 = (bf16[2304,512]{1,0:T(8,128)(2,1)S(1)}, bf16[2304,512]{1,0:T(8,128)(2,1)}, u32[]{:S(2)}) copy-start(bf16[2304,512]{1,0:T(8,128)(2,1)} %refs_2_.1) | copy-start | bytes 7077892
  161.6 8.3 %collective-permute-start.37 = (bf16[288,256]{1,0:T(8,128)(2,1)S(1)}, bf16[288,256]{1,0:T(8,128)(2,1)S(1)}, u32[]{:S(2)}, u32[]{:S(2)}) collective-permute-start(bf16[288,256]{1,0:T(8,128)(2,1)S(1)} %get-tuple-element.56), channel_id=1, source_target_pairs={{0,1},{1,0},{2,3},{3,2},{4,5},{5,4},{6,7},{7,6},{8,9},{9,8},{10,11... | collective-permute-start | bytes 442376 | tf_op jit(solution)/shard_map/ppermute | solution.py:377
  162.6 7.3 %collective-permute-start.3 = (f32[4,288]{1,0:T(4,128)S(1)}, f32[4,288]{1,0:T(4,128)S(1)}, u32[]{:S(2)}, u32[]{:S(2)}) collective-permute-start(f32[4,288]{1,0:T(4,128)S(1)} %copy-done.28), channel_id=1, source_target_pairs={{0,0},{1,1},{2,8},{3,9},{4,16},{5,17},{6,24},{7,25},{8,2},{9,3},{1... | collective-permute-start | bytes 13832 | tf_op jit(solution)/shard_map/ppermute | solution.py:377
  171.7 36.0 %copy-start.29 = (f32[256,288]{0,1:T(8,128)S(1)}, f32[256,288]{0,1:T(8,128)}, u32[]{:S(2)}) copy-start(f32[256,288]{0,1:T(8,128)} %param.11) | copy-start | bytes 884740
  171.7 11.3 %all-to-all-start = ((f32[32,4,288]{2,1,0:T(4,128)}), f32[32,4,288]{2,1,0:T(4,128)S(1)}, u32[]{:S(2)}, u32[]{:S(2)}) async-start(f32[32,4,288]{2,1,0:T(4,128)} %get-tuple-element.59), calls=%async_computation | async-start | bytes 393216 | tf_op jit(solution)/shard_map/all_to_all | solution.py:457
  184.4 10.0 %all-to-all-start.1 = ((f32[32,2,16]{2,1,0:T(2,128)}), f32[32,2,16]{2,1,0:T(2,128)S(1)}, u32[]{:S(2)}, u32[]{:S(2)}) async-start(f32[32,2,16]{2,1,0:T(2,128)} %get-tuple-element.61), calls=%async_computation.1 | async-start | bytes 65536 | tf_op jit(solution)/shard_map/all_to_all | solution.py:457
  188.4 19.3 %collective-permute-start.40 = (f32[288,256]{1,0:T(8,128)S(1)}, f32[288,256]{1,0:T(8,128)S(1)}, u32[]{:S(2)}, u32[]{:S(2)}) collective-permute-start(f32[288,256]{1,0:T(8,128)S(1)} %get-tuple-element.58), channel_id=1, source_target_pairs={{0,0},{1,1},{2,8},{3,9},{4,16},{5,17},{6,24},{7,25},{8,2},{9,3},{1... | collective-permute-start | bytes 884744 | tf_op jit(solution)/shard_map/ppermute | solution.py:377
  (31 other events, 170.5 us)

commit v3 on v2

--- a/solution.py
+++ b/solution.py
@@ -35,20 +35,11 @@
     return jax.ShapeDtypeStruct(dims, dtype)
 
 
-def prep_kernel(tallies, x, gain, routes, out, ends, wide):
-    tokens, block = x.shape
-    lanes = wide.shape[1]
+def prep_kernel(tallies, x, gain, routes, out, ends):
+    block, tokens = x.shape
     v = x[...]
-    squares = jnp.sum(v * v, axis=1, keepdims=True)
-    r = routes[...].astype(f32)
-    wide[:, 0:block] = v * gain[...]
-    at = lax.broadcasted_iota(jnp.int32, (tokens, lanes - block), 1)
-    wide[:, block:] = jnp.where(
-        at == 0, r[:, 0:1], jnp.where(at == 1, r[:, 1:2], jnp.where(at == 2, squares, 0.0))
-    )
-    turned = wide[...].T
-    out[0:block] = turned[0:block].astype(bf16)
-    sq = turned[block + 2 : block + 3]
+    out[0:block] = (v * gain[...]).astype(bf16)
+    sq = jnp.sum(v * v, axis=0, keepdims=True)
     hi = sq.astype(bf16).astype(f32)
     mid = (sq - hi).astype(bf16).astype(f32)
     here = lax.broadcasted_iota(jnp.int32, (1, tokens), 1)
@@ -56,103 +47,162 @@
     for q in range(ends.shape[0]):
         end = end + tallies[0, q]
         mark = jnp.where(here == end, q + 1.0, mark)
-        ends[q : q + 1] = x[pl.ds(end, 1)]
-    rows = [turned[block : block + 2], hi, mid, sq - hi - mid, mark]
+    rows = [routes[...].astype(f32), hi, mid, sq - hi - mid, mark]
     rows.append(jnp.zeros((META - 6, tokens), f32))
     out[block:] = jnp.concatenate(rows, axis=0).astype(bf16)
+    ends[...] = columns_at(mark, v)[0 : ends.shape[0]]
+
+
+def columns_at(mark, v):
+    row = lax.broadcasted_iota(jnp.int32, (8, mark.shape[1]), 0)
+    pick = jnp.where(mark == (row + 1).astype(f32), 1.0, 0.0)
+    return lax.dot_general(
+        pick, v, (((1,), (1,)), ((), ())), precision=lax.Precision.HIGHEST, preferred_element_type=f32
+    )
 
 
 def prep_call(x, gain, routes, tallies):
-    tokens, block = x.shape
+    block, tokens = x.shape
     reqs = tallies.shape[1]
     return pl.pallas_call(
         prep_kernel,
         in_specs=[SMEM, VMEM, VMEM, VMEM],
         out_specs=[VMEM, VMEM],
         out_shape=[shape((block + META, tokens), bf16), shape((reqs, block), f32)],
-        scratch_shapes=[pltpu.VMEM((tokens, up_to(block + META)), f32)],
         compiler_params=params(),
         cost_estimate=cost(4 * tokens * block, 6 * tokens * block),
         name="prep",
-    )(tallies, x, gain[None], routes)
-
-
-def partial_kernel(sides, held, scal, *refs):
-    feeds, refs = refs[:held], refs[held:]
-    wr0, wr1, wg, wu, rg, ru = refs[:6]
+    )(tallies, x, gain, routes)
+
+
+def swap_kernel(scal, wg, wu, dep, out):
+    half = wg.shape[2]
+    out[:, :, 0:half] = wg[...]
+    out[:, :, half:] = wu[...]
+
+
+def swap_call(scal, wg, wu, half, dep):
+    experts, depth, _ = wg.shape
+    theirs = pl.BlockSpec((1, depth, half), lambda n, s: (n, 0, 1 - s[0]))
+    return pl.pallas_call(
+        swap_kernel,
+        grid_spec=pltpu.PrefetchScalarGridSpec(
+            num_scalar_prefetch=1,
+            grid=(experts,),
+            in_specs=[theirs, theirs, ANY],
+            out_specs=pl.BlockSpec((1, depth, 2 * half), lambda n, s: (n, 0, 0)),
+        ),
+        out_shape=shape((experts, depth, 2 * half), bf16),
+        compiler_params=params(),
+        cost_estimate=cost(0, 8 * experts * depth * half),
+        name="swap_halves",
+    )(scal, wg, wu, dep)
+
+
+def join_call(blocks):
+    rows, tokens = blocks[0].shape
+
+    def join_kernel(*refs):
+        for i, ref in enumerate(refs[:-1]):
+            refs[-1][i * rows : (i + 1) * rows] = ref[...]
+
+    return pl.pallas_call(
+        join_kernel,
+        in_specs=[VMEM] * len(blocks),
+        out_specs=VMEM,
+        out_shape=shape((len(blocks) * rows, tokens), bf16),
+        compiler_params=params(),
+        cost_estimate=cost(0, 4 * len(blocks) * rows * tokens),
+        name="join",
+    )(*blocks)
+
+
+def partial_kernel(sides, scal, *refs):
+    feeds, refs = refs[:2], refs[2:]
+    wr0, wr1, wg, wu, theirs = refs[:5]
     own, give, meta, cols, xs, xt, acc = refs[-7:]
     e = pl.program_id(0)
     core, side, y = scal[0], scal[1], scal[2]
-    depth, half = rg.shape[1], rg.shape[2]
+    depth, half = wg.shape[1], wg.shape[2]
     deep = up_to(depth)
     tokens = xt.shape[0]
     block = depth // sides
+    th = tokens // 2
 
     @pl.when(e == 0)
     def _():
-        xs[...] = jnp.zeros_like(xs)
+        xs[depth:deep] = jnp.zeros((deep - depth, tokens), bf16)
+        xs[deep + depth : 2 * deep] = jnp.zeros((deep - depth, tokens), bf16)
+        xs[2 * deep :] = jnp.zeros((LANES, tokens), bf16)
         sq = jnp.zeros((1, tokens), f32)
-        each = 2 * sides // held
-        for n in range(2 * sides):
-            ref, at = feeds[n // each], (n % each) * (block + META)
-            which, i = n // sides, n % sides
-            row = which * deep + (side ^ i) * block
-            xs[pl.ds(pl.multiple_of(row, 16), block)] = ref[at : at + block]
-            row = 2 * deep + META * n
-            xs[row : row + META] = ref[at + block : at + block + META]
-            for term in (4, 3, 2):
-                sq = sq + ref[at + block + term : at + block + term + 1].astype(f32)
+        for which in range(2):
+            ref = feeds[which]
+            for i in range(sides):
+                at = i * (block + META)
+                row = which * deep + (side ^ i) * block
+                xs[pl.ds(pl.multiple_of(row, 16), block)] = ref[at : at + block]
+                for term in (4, 3, 2):
+                    sq = sq + ref[at + block + term : at + block + term + 1].astype(f32)
+        xs[2 * deep : 2 * deep + META] = feeds[0][block : block + META]
         router = jnp.dot(wr0[...], xs[0:depth], preferred_element_type=f32)
         router += jnp.dot(wr1[...], xs[deep : deep + depth], preferred_element_type=f32)
-        meta[...] = jnp.concatenate([sq, router[0:7]], axis=0)
+        m = jnp.concatenate([sq, router[0:7]], axis=0)
+        near = jnp.where(y == 0, m[:, 0:th], m[:, th:])
+        far = jnp.where(y == 0, m[:, th:], m[:, 0:th])
+        meta[...] = near
+        hi = far.astype(bf16).astype(f32)
+        give[2 * th :] = jnp.zeros((META, 2 * half), bf16)
+        give[2 * th :, 0:th] = jnp.concatenate([hi, far - hi], axis=0).astype(bf16)
         xt[...] = xs[...].T
         cols[...] = xt[:, 2 * deep :]
 
     routes = xt[:, 2 * deep :].astype(f32)
     ef = e.astype(f32)
-    for which, (w, r) in enumerate(((wg, rg), (wu, ru))):
+    for which, w in enumerate((wg, wu)):
+        at = which * half
         d = jnp.dot(xt[:, 0:depth], w[0], preferred_element_type=f32)
-        d += jnp.dot(xt[:, deep : deep + depth], r[0], preferred_element_type=f32)
-        at = which * half
+        d += jnp.dot(
+            xt[:, deep : deep + depth], theirs[0, :, at : at + half], preferred_element_type=f32
+        )
         for k in range(2):
             take = (routes[:, k : k + 1] == ef) | (e == 0)
             acc[k, :, at : at + half] = jnp.where(take, d, acc[k, :, at : at + half])
 
     @pl.when(e == pl.num_programs(0) - 1)
     def _():
-        th = tokens // 2
         for k in range(2):
             own[k] = acc[k, pl.ds(pl.multiple_of(y * th, th), th)]
-            give[k] = acc[k, pl.ds(pl.multiple_of((1 - y) * th, th), th)].astype(bf16)
+            give[k * th : (k + 1) * th] = acc[k, pl.ds(pl.multiple_of((1 - y) * th, th), th)].astype(bf16)
 
 
 def partial_call(scal, sides, feeds, wr, weights, swapped, deps):
-    experts, depth, half = swapped[0].shape
-    rows, tokens = feeds[0].shape
+    experts, depth, wide = swapped.shape
+    half = wide // 2
+    tokens = feeds[0].shape[1]
     deep = up_to(depth)
     full = lambda v: pl.BlockSpec(v.shape, lambda n, s: (0,) * len(v.shape))
     mine = pl.BlockSpec((1, depth, half), lambda n, s: (n, 0, s[0]))
-    theirs = pl.BlockSpec((1, depth, half), lambda n, s: (n, 0, 0))
+    theirs = pl.BlockSpec((1, depth, wide), lambda n, s: (n, 0, 0))
     outs = [
-        shape((2, tokens // 2, 2 * half), f32),
-        shape((2, tokens // 2, 2 * half), bf16),
-        shape((8, tokens), f32),
+        shape((2, tokens // 2, wide), f32),
+        shape((tokens + META, wide), bf16),
+        shape((8, tokens // 2), f32),
         shape((tokens, LANES), bf16),
     ]
     call = pl.pallas_call(
-        lambda *refs: partial_kernel(sides, len(feeds), *refs),
+        lambda *refs: partial_kernel(sides, *refs),
         grid_spec=pltpu.PrefetchScalarGridSpec(
             num_scalar_prefetch=1,
             grid=(experts,),
             in_specs=[full(v) for v in feeds]
             + [full(v) for v in wr]
-            + [mine, mine, theirs, theirs]
+            + [mine, mine, theirs]
             + [ANY] * len(deps),
             out_specs=[full(v) for v in outs],
             scratch_shapes=[
                 pltpu.VMEM((2 * deep + LANES, tokens), bf16),
                 pltpu.VMEM((tokens, 2 * deep + LANES), bf16),
-                pltpu.VMEM((2, tokens, 2 * half), f32),
+                pltpu.VMEM((2, tokens, wide), f32),
             ],
         ),
         out_shape=outs,
@@ -162,18 +212,18 @@
         ),
         name="gate_up_partial",
     )
-    return call(scal, *feeds, *wr, *weights, *swapped, *deps)
-
-
-def act_kernel(scal, own, recv, meta, meta_recv, cols, *refs):
+    return call(scal, *feeds, *wr, *weights, swapped, *deps)
+
+
+def act_kernel(scal, own, recv, meta, cols, *refs):
     act, turned = refs[-2:]
     y = scal[0]
     _, th, half = act.shape
-    m = meta[...] + meta_recv[...]
-    turned[...] = jnp.concatenate([m, jnp.zeros((LANES - 8, m.shape[1]), f32)], axis=0).T
-    here = pl.ds(pl.multiple_of(y * th, th), th)
-    m = turned[here]
-    routes = cols[here].astype(f32)
+    got = recv[2 * th :, 0:th].astype(f32)
+    m = meta[...] + got[0:8] + got[8:16]
+    turned[...] = jnp.concatenate([m, jnp.zeros((LANES - 8, th), f32)], axis=0).T
+    m = turned[...]
+    routes = cols[pl.ds(pl.multiple_of(y * th, th), th)].astype(f32)
     scale = lax.rsqrt(m[:, 0:1] / WIDTH + epsilon)
     logits = []
     for k in range(2):
@@ -183,32 +233,33 @@
         logits.append(logit * scale)
     for k in range(2):
         mix = scale / (1.0 + jnp.exp(logits[1 - k] - logits[k]))
-        g = (own[k, :, 0:half] + recv[k, :, 0:half].astype(f32)) * scale
-        u = (own[k, :, half:] + recv[k, :, half:].astype(f32)) * mix
+        at = slice(k * th, (k + 1) * th)
+        g = (own[k, :, 0:half] + recv[at, 0:half].astype(f32)) * scale
+        u = (own[k, :, half:] + recv[at, half:].astype(f32)) * mix
         act[k] = (g / (1.0 + jnp.exp(-g)) * u).astype(bf16)
 
 
-def act_call(scal, own, recv, meta, meta_recv, cols, deps):
+def act_call(scal, own, recv, meta, cols, deps):
     _, th, wide = own.shape
     return pl.pallas_call(
         act_kernel,
-        in_specs=[SMEM] + [VMEM] * 5 + [ANY] * len(deps),
+        in_specs=[SMEM] + [VMEM] * 4 + [ANY] * len(deps),
         out_specs=VMEM,
         out_shape=shape((2, th, wide // 2), bf16),
-        scratch_shapes=[pltpu.VMEM((meta.shape[1], LANES), f32)],
+        scratch_shapes=[pltpu.VMEM((th, LANES), f32)],
         compiler_params=params(),
         cost_estimate=cost(12 * th * wide, 14 * th * wide),
         name="act",
-    )(scal, own, recv, meta, meta_recv, cols, *deps)
+    )(scal, own, recv, meta, cols, *deps)
 
 
 def down_kernel(sides, scal, a, a_y, b, b_y, cols, wd, *refs):
-    outs = refs[-sides - 3 : -3]
-    whole, acc, turned = refs[-3:]
+    outs = refs[-sides - 2 : -2]
+    whole, acc = refs[-2:]
     e = pl.program_id(0)
     core, side, y = scal[0], scal[1], scal[2]
     _, th, half = a.shape
-    hidden, width = wd.shape[1:]
+    width, hidden = wd.shape[1:]
     block = width // sides
 
     @pl.when(e == 0)
@@ -223,27 +274,25 @@
     routes = cols[...].astype(f32)
     masks = [jnp.where(routes[:, k : k + 1] == ef, 1.0, 0.0).astype(bf16) for k in range(2)]
     rows = whole[0, :, 0:hidden] * masks[0] + whole[1, :, 0:hidden] * masks[1]
-    d = jnp.dot(rows, wd[0], preferred_element_type=f32)
+    d = lax.dot_general(wd[0], rows, (((1,), (1,)), ((), ())), preferred_element_type=f32)
 
     @pl.when(e == 0)
     def _():
-        acc[...] = jnp.zeros_like(acc)
-        acc[:, 0:width] = d
+        acc[...] = d
 
     @pl.when(e > 0)
     def _():
-        acc[:, 0:width] += d
+        acc[...] += d
 
     @pl.when(e == pl.num_programs(0) - 1)
     def _():
-        turned[...] = acc[...].T
         for i in range(sides):
             rows = pl.ds(pl.multiple_of((side ^ i) * block, 16), block)
-            outs[i][...] = turned[rows].astype(bf16)
+            outs[i][...] = acc[rows].astype(bf16)
 
 
 def down_call(scal, sides, pieces, cols, wd, deps):
-    experts, hidden, width = wd.shape
+    experts, width, hidden = wd.shape
     tokens = cols.shape[0]
     half = pieces[0].shape[2]
     full = lambda v: pl.BlockSpec(v.shape, lambda n: (0,) * len(v.shape))
@@ -253,14 +302,13 @@
         grid=(experts,),
         in_specs=[SMEM]
         + [full(v) for v in pieces]
-        + [full(cols), pl.BlockSpec((1, hidden, width), lambda n: (n, 0, 0))]
+        + [full(cols), pl.BlockSpec((1, width, hidden), lambda n: (n, 0, 0))]
         + [ANY] * len(deps),
         out_specs=[full(v) for v in outs],
         out_shape=outs,
         scratch_shapes=[
             pltpu.VMEM((2, tokens, 2 * half), bf16),
-            pltpu.VMEM((tokens, up_to(width)), f32),
-            pltpu.VMEM((up_to(width), tokens), f32),
+            pltpu.VMEM((width, tokens), f32),
         ],
         compiler_params=params(),
         cost_estimate=cost(
@@ -277,12 +325,7 @@
         v = v + ref[...].astype(f32)
     total[...] = v
     reqs = stream.shape[0]
-    mark = meta[5:6].astype(f32)
-    row = lax.broadcasted_iota(jnp.int32, (8, mark.shape[1]), 0)
-    pick = jnp.where(mark == (row + 1).astype(f32), 1.0, 0.0)
-    ends = lax.dot_general(
-        pick, v, (((1,), (1,)), ((), ())), precision=lax.Precision.HIGHEST, preferred_element_type=f32
-    )
+    ends = columns_at(meta[5:6].astype(f32), v)
     ends = stream[...] + branch_scale * ends[0:reqs]
     message[...] = jnp.broadcast_to(ends[None], message.shape)
 
@@ -380,45 +423,39 @@
     other_y = lambda q, z, x: (q ^ 2, z, x)
     home = lambda q, z, x: (z, q, x)
 
+    scal = jnp.stack([core, side, y]).astype(jnp.int32)
     sent, stream = prep_call(
-        skip_stream_arriving, premix_rmsnorm_gain, chosen_specialists, sequence_piece_tallies
+        skip_stream_arriving.T, premix_rmsnorm_gain[:, None], chosen_specialists.T, sequence_piece_tallies
     )
-    first = [
-        send(sent, lambda q, z, x, c=c, i=i: (z ^ c, (q - 1) % parts, x ^ i))
-        for c in range(2)
-        for i in range(sides)
-    ]
+    first = [send(sent, lambda q, z, x, i=i: (z, (q - 1) % parts, x ^ i)) for i in range(sides)]
     wg, wu, wd = specialist_switch_weights, specialist_expand_weights, specialist_contract_weights
     if spread > 1:
         runs = [[q * spread + r for r in range(spread)] for q in range(parts)]
         wg = lax.all_gather(wg, "dp", axis=1, tiled=True, axis_index_groups=runs)
         wu = lax.all_gather(wu, "dp", axis=1, tiled=True, axis_index_groups=runs)
         wd = lax.all_gather(wd, "dp", axis=2, tiled=True, axis_index_groups=runs)
+    wd = jnp.swapaxes(wd, 1, 2)
     depth, hidden = wg.shape[1], wg.shape[2]
     half = up_to(-(-hidden // 2))
-    swap = lambda w: jnp.where(
-        core == 0, jnp.pad(w[:, :, half:], ((0, 0), (0, 0), (0, 2 * half - hidden))), w[:, :, :half]
-    )
-    swapped = [send(swap(w), other_core) for w in (wg, wu)]
+    swapped = send(swap_call(scal, wg, wu, half, sent), other_core)
     wr = []
+    padded = jnp.pad(dispatcher_weights.T, ((0, 16 - dispatcher_weights.shape[1]), (0, 0)))
     for p in (part, part ^ 1):
-        w = lax.dynamic_slice_in_dim(dispatcher_weights, p * depth, depth).T
-        wr.append(jnp.pad(w, ((0, 16 - w.shape[0]), (0, 0))))
-
-    feeds = [first]
-    own = jnp.concatenate(first[:sides], axis=0)
+        wr.append(lax.dynamic_slice_in_dim(padded, p * depth, depth, axis=1))
+
+    pair = join_call(first)
+    feeds = [[pair, send(pair, other_core)]]
     for s in range(1, parts):
-        mine = send(own, lambda q, z, x, s=s: (q, (z - s) % parts, x))
+        mine = send(pair, lambda q, z, x, s=s: (q, (z - s) % parts, x))
         feeds.append([mine, send(mine, other_core)])
     stream = send(stream, home)
 
-    scal = jnp.stack([core, side, y]).astype(jnp.int32)
     y_only = scal[2:3]
     partial, act, pieces, shares, back = {}, {}, {}, {}, {}
 
     def do_partial(s, *deps):
         own, give, meta, cols = partial_call(scal, sides, feeds[s], wr, (wg, wu), swapped, deps)
-        partial[s] = (own, send(give, other_y), meta, send(meta, other_y), cols)
+        partial[s] = (own, send(give, other_y), meta, cols)
         return own
 
     def do_act(s, *deps):
@@ -428,7 +465,7 @@
         return a
 
     def do_down(s, *deps):
-        outs = down_call(scal, sides, pieces[s], partial[s][4], wd, deps)
+        outs = down_call(scal, sides, pieces[s], partial[s][3], wd, deps)
         shares[s] = [outs[0]] + [
             send(outs[i], lambda q, z, x, i=i: (q, z, x ^ i)) for i in range(1, sides)
         ]

time: 210 us -> 177 us (0.84)
  local copies, waits for them, and re-layouts: 27.7 us -> 10.1 us
  starting transfers between devices: 56.6 us -> 43.8 us
  waiting for transfers between devices: 64.2 us -> 71.3 us
  other arithmetic: 6.73 us -> 1.69 us
  Pallas kernels: 52.1 us -> 48.2 us
    ppermute x41 -> x35, starting transfers between devices: 49.1 us -> 35.1 us  [send(): return lax.ppermute(value, ('dp', 'mp'), pairs)]
    unnamed x72 -> x26, local copies, waits for them, and re-layouts: 21.8 us -> 8.34 us
    ppermute x41 -> x35, waiting for transfers between devices: 54.9 us -> 62.1 us  [send(): return lax.ppermute(value, ('dp', 'mp'), pairs)]
    select_n x2 -> x0, other arithmetic: 5.04 us -> none  [body(): jnp.where(core == 0, jnp.pad(w[:, :, half:], ((0, 0), (0, 0), (0, 2 * hal...]
    slice x4 -> x0, local copies, waits for them, and re-layouts: 2.94 us -> none  [body(): w[:, :, half:]]
    pallas_call x4, Pallas kernels: 14.9 us -> 12.1 us  [down_call(): pl.pallas_call(lambda *refs: down_kernel(sides, *refs), grid=(experts,),...]
    pallas_call x8 -> x10, Pallas kernels: 32.4 us -> 32.7 us  [the longest x4 26.8 us: partial_call(): return call(scal, *feeds, *wr, *weights, swapped, *deps)]
  transfers between devices with their start and end apart: 43 -> 37, of which waited for: 12 -> 15; matrix products, arithmetic and copies ran while one was open for 7% -> 1% of each run, Pallas kernels for 23% -> 24%
where the time goes in v3:
time: 177 us; the launch traced here: 176 us
  waiting for transfers between devices  71.3 us (40%)
  Pallas kernels  48.2 us (27%)
  starting transfers between devices  43.8 us (25%)
  local copies, waits for them, and re-layouts  10.1 us (6%)
    ppermute x35, waiting for transfers between devices, send(): return lax.ppermute(value, ('dp', 'mp'), pairs)  62.1 us
    ppermute x35, starting transfers between devices, send(): return lax.ppermute(value, ('dp', 'mp'), pairs)  35.1 us
    pallas_call x4, Pallas kernels, partial_call(): return call(scal, *feeds, *wr, *weights, swapped, *deps)  26.8 us
    pallas_call x4, Pallas kernels, down_call(): pl.pallas_call(lambda *refs: down_kernel(sides, *refs), grid=(experts,),...  12.1 us
    all_to_all x2, waiting for transfers between devices, body(): everyone = lambda v: lax.all_to_all(v, ('dp', 'mp'), 0, 0, tiled=True)  9.27 us
    all_to_all x2, starting transfers between devices, body(): everyone = lambda v: lax.all_to_all(v, ('dp', 'mp'), 0, 0, tiled=True)  8.64 us
    unnamed x26, local copies, waits for them, and re-layouts  8.34 us
  transfers between devices with their start and end apart: 37, of which 15 were waited for; matrix products, arithmetic and copies ran while one was open for 1% of the time, Pallas kernels for 24%

profile of v3, /device:TPU:4, one launch (start us, length us, event | category | flops | bytes accessed | tf_op | source)
XLA Modules:
  0.0 176.1 jit_solution(8847767140059702474)
XLA Ops:
  0.7 0.8 broadcast_in_dim.11.gain
  1.5 1.0 copy-done.7
  2.5 0.7 copy-done.9
  3.8 0.9 prep.1
  4.7 2.0 %copy-done = bf16[4,576,720]{2,1,0:T(8,128)(2,1)S(1)} copy-done((bf16[4,576,720]{2,1,0:T(8,128)(2,1)S(1)}, bf16[4,576,720]{2,1,0:T(8,128)(2,1)}, u32[]{:S(2)}) %copy-start) | copy-done | bytes 3317784
  6.7 2.0 %copy-done.2 = bf16[4,576,720]{2,1,0:T(8,128)(2,1)S(1)} copy-done((bf16[4,576,720]{2,1,0:T(8,128)(2,1)S(1)}, bf16[4,576,720]{2,1,0:T(8,128)(2,1)}, u32[]{:S(2)}) %copy-start.2) | copy-done | bytes 3317784
  8.7 3.2 %swap_halves.1 = bf16[4,576,768]{2,1,0:T(8,128)(2,1)} custom-call(s32[3]{0:T(128)S(1)} %pad_add_fusion.scal.refs_0_, bf16[4,576,720]{2,1,0:T(8,128)(2,1)S(1)} %copy-done, bf16[4,576,720]{2,1,0:T(8,128)(2,1)S(1)} %copy-done.2, bf16[304,256]{1,0:T(8,128)(2,1)S(1)} %get-tuple-element.32.dep), custom_call_target="tpu_custom_call" | custom-call | bytes 7077888 | tf_op jit(solution)/shard_map/swap_halves/pallas_call | solution.py:87
  11.9 1.5 collective-permute-start
  13.4 3.6 %collective-permute-start.1 = (bf16[304,256]{1,0:T(8,128)(2,1)S(1)}, bf16[304,256]{1,0:T(8,128)(2,1)S(1)}, u32[]{:S(2)}, u32[]{:S(2)}) collective-permute-start(bf16[304,256]{1,0:T(8,128)(2,1)S(1)} %get-tuple-element.32.dep), channel_id=1, source_target_pairs={{0,7},{1,6},{2,15},{3,14},{4,23},{5,22},{6,31},{7,30},{8,1},{9,0},... | collective-permute-start | bytes 466952 | tf_op jit(solution)/shard_map/ppermute | solution.py:420
  17.0 3.1 %collective-permute-done.refs_0_ = bf16[304,256]{1,0:T(8,128)(2,1)S(1)} collective-permute-done((bf16[304,256]{1,0:T(8,128)(2,1)S(1)}, bf16[304,256]{1,0:T(8,128)(2,1)S(1)}, u32[]{:S(2)}, u32[]{:S(2)}) %collective-permute-start) | collective-permute-done | bytes 155680 | tf_op jit(solution)/shard_map/ppermute | solution.py:420
  20.1 4.3 %collective-permute-done.1.refs_1_ = bf16[304,256]{1,0:T(8,128)(2,1)S(1)} collective-permute-done((bf16[304,256]{1,0:T(8,128)(2,1)S(1)}, bf16[304,256]{1,0:T(8,128)(2,1)S(1)}, u32[]{:S(2)}, u32[]{:S(2)}) %collective-permute-start.1) | collective-permute-done | bytes 155680 | tf_op jit(solution)/shard_map/ppermute | solution.py:420
  24.4 0.8 join.1.refs_1_
  25.1 6.5 %collective-permute-start.8 = (bf16[608,256]{1,0:T(8,128)(2,1)}, bf16[608,256]{1,0:T(8,128)(2,1)}, u32[]{:S(2)}, u32[]{:S(2)}) collective-permute-start(bf16[608,256]{1,0:T(8,128)(2,1)} %join.1.refs_1_), channel_id=1, source_target_pairs={{0,6},{1,7},{2,0},{3,1},{4,2},{5,3},{6,4},{7,5},{8,14},{9,15},{10,... | collective-permute-start | bytes 933896 | tf_op jit(solution)/shard_map/ppermute | solution.py:420
  31.6 7.9 %collective-permute-done.8.refs_1_ = bf16[608,256]{1,0:T(8,128)(2,1)} collective-permute-done((bf16[608,256]{1,0:T(8,128)(2,1)}, bf16[608,256]{1,0:T(8,128)(2,1)}, u32[]{:S(2)}, u32[]{:S(2)}) %collective-permute-start.8) | collective-permute-done | bytes 311328 | tf_op jit(solution)/shard_map/ppermute | solution.py:420
  39.6 0.8 pad_dynamic-slice_fusion
  40.5 2.0 %copy-done.3 = bf16[4,576,720]{2,1,0:T(8,128)(2,1)S(1)} copy-done((bf16[4,576,720]{2,1,0:T(8,128)(2,1)S(1)}, bf16[4,576,720]{2,1,0:T(8,128)(2,1)}, u32[]{:S(2)}) %copy-start.3) | copy-done | bytes 3317784
  42.5 6.6 %gate_up_partial.4 = (f32[2,128,768]{2,1,0:T(8,128)S(1)}, bf16[272,768]{1,0:T(8,128)(2,1)S(1)}, f32[8,128]{1,0:T(8,128)S(1)}, bf16[256,128]{1,0:T(8,128)(2,1)S(1)}) custom-call(s32[3]{0:T(128)S(1)} %pad_add_fusion.scal.refs_0_, bf16[608,256]{1,0:T(8,128)(2,1)} %join.1.refs_1_, bf16[608,256]{1,0:T(8,128)(2,1)} %collective-permute-done.6.refs_2_, ...), custom_call_target="tpu_custom_call" | custom-call | flops 1811939328 | bytes 8257536 | tf_op jit(solution)/shard_map/gate_up_partial/pallas_call | solution.py:215
  49.1 5.6 %collective-permute-start.2 = (bf16[608,256]{1,0:T(8,128)(2,1)}, bf16[608,256]{1,0:T(8,128)(2,1)S(1)}, u32[]{:S(2)}, u32[]{:S(2)}) collective-permute-start(bf16[608,256]{1,0:T(8,128)(2,1)} %join.1.refs_1_), channel_id=1, source_target_pairs={{0,2},{1,3},{2,4},{3,5},{4,6},{5,7},{6,0},{7,1},{8,10},{9,11},{10,... | collective-permute-start | bytes 933896 | tf_op jit(solution)/shard_map/ppermute | solution.py:420
  54.8 6.9 %gate_up_partial.5 = (f32[2,128,768]{2,1,0:T(8,128)S(1)}, bf16[272,768]{1,0:T(8,128)(2,1)S(1)}, f32[8,128]{1,0:T(8,128)S(1)}, bf16[256,128]{1,0:T(8,128)(2,1)S(1)}) custom-call(s32[3]{0:T(128)S(1)} %pad_add_fusion.scal.refs_0_, bf16[608,256]{1,0:T(8,128)(2,1)} %collective-permute-done.8.refs_1_, bf16[608,256]{1,0:T(8,128)(2,1)} %collective-permute-done.9.refs_2_, ...), custom_call_target="tpu_custom_call" | custom-call | flops 1811939328 | bytes 8257536 | tf_op jit(solution)/shard_map/gate_up_partial/pallas_call | solution.py:215
  62.5 1.8 %collective-permute-start.10 = (bf16[2,128,384]{2,1,0:T(8,128)(2,1)S(1)}, bf16[2,128,384]{2,1,0:T(8,128)(2,1)S(1)}, u32[]{:S(2)}, u32[]{:S(2)}) collective-permute-start(bf16[2,128,384]{2,1,0:T(8,128)(2,1)S(1)} %act.4.refs_8_.refs_1_), channel_id=1, source_target_pairs={{0,16},{1,17},{2,18},{3,19},{4,20},{5,21},{6,22},{7,23},{8,24},{9,... | collective-permute-start | bytes 589832 | tf_op jit(solution)/shard_map/ppermute | solution.py:420
  64.9 6.8 %gate_up_partial.6 = (f32[2,128,768]{2,1,0:T(8,128)S(1)}, bf16[272,768]{1,0:T(8,128)(2,1)S(1)}, f32[8,128]{1,0:T(8,128)S(1)}, bf16[256,128]{1,0:T(8,128)(2,1)S(1)}) custom-call(s32[3]{0:T(128)S(1)} %pad_add_fusion.scal.refs_0_, bf16[608,256]{1,0:T(8,128)(2,1)} %collective-permute-done.14.refs_1_, bf16[608,256]{1,0:T(8,128)(2,1)S(1)} %collective-permute-done.15.refs_2_, ...), custom_call_target="tpu_custom_call" | custom-call | flops 1811939328 | bytes 8257536 | tf_op jit(solution)/shard_map/gate_up_partial/pallas_call | solution.py:215
  71.7 2.5 %collective-permute-done.13.recv = bf16[272,768]{1,0:T(8,128)(2,1)S(1)} collective-permute-done((bf16[272,768]{1,0:T(8,128)(2,1)S(1)}, bf16[272,768]{1,0:T(8,128)(2,1)S(1)}, u32[]{:S(2)}, u32[]{:S(2)}) %collective-permute-start.13) | collective-permute-done | bytes 417824 | tf_op jit(solution)/shard_map/ppermute | solution.py:420
  75.1 3.4 %collective-permute-done.10.refs_2_ = bf16[2,128,384]{2,1,0:T(8,128)(2,1)S(1)} collective-permute-done((bf16[2,128,384]{2,1,0:T(8,128)(2,1)S(1)}, bf16[2,128,384]{2,1,0:T(8,128)(2,1)S(1)}, u32[]{:S(2)}, u32[]{:S(2)}) %collective-permute-start.10) | collective-permute-done | bytes 196640 | tf_op jit(solution)/shard_map/ppermute | solution.py:420
  78.9 3.7 %collective-permute-done.17.refs_2_ = bf16[2,128,384]{2,1,0:T(8,128)(2,1)S(1)} collective-permute-done((bf16[2,128,384]{2,1,0:T(8,128)(2,1)S(1)}, bf16[2,128,384]{2,1,0:T(8,128)(2,1)S(1)}, u32[]{:S(2)}, u32[]{:S(2)}) %collective-permute-start.17) | collective-permute-done | bytes 196640 | tf_op jit(solution)/shard_map/ppermute | solution.py:420
  82.6 3.0 %down.4 = (bf16[288,256]{1,0:T(8,128)(2,1)S(1)}, bf16[288,256]{1,0:T(8,128)(2,1)S(1)}) custom-call(s32[3]{0:T(128)S(1)} %pad_add_fusion.scal.refs_0_, bf16[2,128,384]{2,1,0:T(8,128)(2,1)S(1)} %act.4.refs_8_.refs_1_, bf16[2,128,384]{2,1,0:T(8,128)(2,1)S(1)} %collective-permute-done.10.refs_2_, bf16[2,128,384]{2,1,0:T(8,128)(2,1)S(1)} %collective-permute-done.11.refs_3_, ...), custom_call_target="tpu_custom_call" | custom-call | flops 849346560 | bytes 3612672 | tf_op jit(solution)/shard_map/down/pallas_call | solution.py:300
  85.7 1.6 collective-permute-start.21
  87.2 6.4 %gate_up_partial.7 = (f32[2,128,768]{2,1,0:T(8,128)S(1)}, bf16[272,768]{1,0:T(8,128)(2,1)S(1)}, f32[8,128]{1,0:T(8,128)S(1)}, bf16[256,128]{1,0:T(8,128)(2,1)S(1)}) custom-call(s32[3]{0:T(128)S(1)} %pad_add_fusion.scal.refs_0_, bf16[608,256]{1,0:T(8,128)(2,1)S(1)} %collective-permute-done.2.refs_1_.meta, ...), custom_call_target="tpu_custom_call" | custom-call | flops 1811939328 | bytes 8257536 | tf_op jit(solution)/shard_map/gate_up_partial/pallas_call | solution.py:215
  94.5 1.8 %collective-permute-start.25 = (bf16[2,128,384]{2,1,0:T(8,128)(2,1)S(1)}, bf16[2,128,384]{2,1,0:T(8,128)(2,1)S(1)}, u32[]{:S(2)}, u32[]{:S(2)}) collective-permute-start(bf16[2,128,384]{2,1,0:T(8,128)(2,1)S(1)} %act.6.refs_7_.refs_1_), channel_id=1, source_target_pairs={{0,16},{1,17},{2,18},{3,19},{4,20},{5,21},{6,22},{7,23},{8,24},{9,... | collective-permute-start | bytes 589832 | tf_op jit(solution)/shard_map/ppermute | solution.py:420
  96.4 3.0 %down.5 = (bf16[288,256]{1,0:T(8,128)(2,1)S(1)}, bf16[288,256]{1,0:T(8,128)(2,1)S(1)}) custom-call(s32[3]{0:T(128)S(1)} %pad_add_fusion.scal.refs_0_, bf16[2,128,384]{2,1,0:T(8,128)(2,1)S(1)} %act.5.refs_7_.refs_1_, bf16[2,128,384]{2,1,0:T(8,128)(2,1)S(1)} %collective-permute-done.17.refs_2_, bf16[2,128,384]{2,1,0:T(8,128)(2,1)S(1)} %collective-permute-done.18.refs_3_, ...), custom_call_target="tpu_custom_call" | custom-call | flops 849346560 | bytes 3612672 | tf_op jit(solution)/shard_map/down/pallas_call | solution.py:300
  100.7 9.0 %collective-permute-done.25.refs_2_ = bf16[2,128,384]{2,1,0:T(8,128)(2,1)S(1)} collective-permute-done((bf16[2,128,384]{2,1,0:T(8,128)(2,1)S(1)}, bf16[2,128,384]{2,1,0:T(8,128)(2,1)S(1)}, u32[]{:S(2)}, u32[]{:S(2)}) %collective-permute-start.25) | collective-permute-done | bytes 196640 | tf_op jit(solution)/shard_map/ppermute | solution.py:420
  111.2 3.0 %down.6 = (bf16[288,256]{1,0:T(8,128)(2,1)S(1)}, bf16[288,256]{1,0:T(8,128)(2,1)S(1)}) custom-call(s32[3]{0:T(128)S(1)} %pad_add_fusion.scal.refs_0_, bf16[2,128,384]{2,1,0:T(8,128)(2,1)S(1)} %act.6.refs_7_.refs_1_, bf16[2,128,384]{2,1,0:T(8,128)(2,1)S(1)} %collective-permute-done.25.refs_2_, bf16[2,128,384]{2,1,0:T(8,128)(2,1)S(1)} %collective-permute-done.26.refs_3_, ...), custom_call_target="tpu_custom_call" | custom-call | flops 849346560 | bytes 3612672 | tf_op jit(solution)/shard_map/down/pallas_call | solution.py:300
  115.4 2.3 %collective-permute-done.22.refs_2_ = bf16[2,128,384]{2,1,0:T(8,128)(2,1)S(1)} collective-permute-done((bf16[2,128,384]{2,1,0:T(8,128)(2,1)S(1)}, bf16[2,128,384]{2,1,0:T(8,128)(2,1)S(1)}, u32[]{:S(2)}, u32[]{:S(2)}) %collective-permute-start.22) | collective-permute-done | bytes 196640 | tf_op jit(solution)/shard_map/ppermute | solution.py:420
  117.7 2.5 %collective-permute-done.32 = bf16[288,256]{1,0:T(8,128)(2,1)S(1)} collective-permute-done((bf16[288,256]{1,0:T(8,128)(2,1)S(1)}, bf16[288,256]{1,0:T(8,128)(2,1)S(1)}, u32[]{:S(2)}, u32[]{:S(2)}) %collective-permute-start.32) | collective-permute-done | bytes 147488 | tf_op jit(solution)/shard_map/ppermute | solution.py:420
  120.3 5.0 %collective-permute-done.30.refs_8_.refs_3_ = bf16[288,256]{1,0:T(8,128)(2,1)S(1)} collective-permute-done((bf16[288,256]{1,0:T(8,128)(2,1)S(1)}, bf16[288,256]{1,0:T(8,128)(2,1)S(1)}, u32[]{:S(2)}, u32[]{:S(2)}) %collective-permute-start.30) | collective-permute-done | bytes 147488 | tf_op jit(solution)/shard_map/ppermute | solution.py:420
  125.3 3.0 %down.7 = (bf16[288,256]{1,0:T(8,128)(2,1)S(1)}, bf16[288,256]{1,0:T(8,128)(2,1)S(1)}) custom-call(s32[3]{0:T(128)S(1)} %pad_add_fusion.scal.refs_0_, bf16[2,128,384]{2,1,0:T(8,128)(2,1)S(1)} %act.7.refs_7_.refs_1_, bf16[2,128,384]{2,1,0:T(8,128)(2,1)S(1)} %collective-permute-done.22.refs_2_, bf16[2,128,384]{2,1,0:T(8,128)(2,1)S(1)} %collective-permute-done.23.refs_3_, ...), custom_call_target="tpu_custom_call" | custom-call | flops 849346560 | bytes 3612672 | tf_op jit(solution)/shard_map/down/pallas_call | solution.py:300
  128.3 1.6 collective-permute-start.31
  129.9 1.9 %collective-permute-start.3 = (f32[4,288]{1,0:T(4,128)S(1)}, f32[4,288]{1,0:T(4,128)S(1)}, u32[]{:S(2)}, u32[]{:S(2)}) collective-permute-start(f32[4,288]{1,0:T(4,128)S(1)} %get-tuple-element.33), channel_id=1, source_target_pairs={{0,0},{1,1},{2,8},{3,9},{4,16},{5,17},{6,24},{7,25},{8,2},{9,3},{1... | collective-permute-start | bytes 13832 | tf_op jit(solution)/shard_map/ppermute | solution.py:420
  131.8 5.4 %collective-permute-done.3.stream = f32[4,288]{1,0:T(4,128)S(1)} collective-permute-done((f32[4,288]{1,0:T(4,128)S(1)}, f32[4,288]{1,0:T(4,128)S(1)}, u32[]{:S(2)}, u32[]{:S(2)}) %collective-permute-start.3) | collective-permute-done | bytes 4640 | tf_op jit(solution)/shard_map/ppermute | solution.py:420
  137.2 1.1 branch_total.1
  138.3 4.7 %all-to-all-start = ((f32[32,4,288]{2,1,0:T(4,128)}), f32[32,4,288]{2,1,0:T(4,128)S(1)}, u32[]{:S(2)}, u32[]{:S(2)}) async-start(f32[32,4,288]{2,1,0:T(4,128)} %get-tuple-element.59), calls=%async_computation | async-start | bytes 393216 | tf_op jit(solution)/shard_map/all_to_all | solution.py:494
  143.2 7.5 %all-to-all-done.refs_0_ = f32[32,4,288]{2,1,0:T(4,128)S(1)} async-done(((f32[32,4,288]{2,1,0:T(4,128)}), f32[32,4,288]{2,1,0:T(4,128)S(1)}, u32[]{:S(2)}, u32[]{:S(2)}) %all-to-all-start) | async-done | bytes 147488 | tf_op jit(solution)/shard_map/all_to_all | solution.py:494
  150.7 1.4 head.1
  152.1 3.9 %all-to-all-start.1 = ((f32[32,2,16]{2,1,0:T(2,128)}), f32[32,2,16]{2,1,0:T(2,128)S(1)}, u32[]{:S(2)}, u32[]{:S(2)}) async-start(f32[32,2,16]{2,1,0:T(2,128)} %get-tuple-element.61), calls=%async_computation.1 | async-start | bytes 65536 | tf_op jit(solution)/shard_map/all_to_all | solution.py:494
  156.0 4.3 %collective-permute-start.34 = (f32[288,256]{1,0:T(8,128)S(1)}, f32[288,256]{1,0:T(8,128)S(1)}, u32[]{:S(2)}, u32[]{:S(2)}) collective-permute-start(f32[288,256]{1,0:T(8,128)S(1)} %get-tuple-element.58), channel_id=1, source_target_pairs={{0,0},{1,1},{2,8},{3,9},{4,16},{5,17},{6,24},{7,25},{8,2},{9,3},{1... | collective-permute-start | bytes 884744 | tf_op jit(solution)/shard_map/ppermute | solution.py:420
  160.3 1.8 all-to-all-done.1
  162.2 0.7 subtract_subtract_fusion
  162.9 12.5 %collective-permute-done.34 = f32[288,256]{1,0:T(8,128)S(1)} collective-permute-done((f32[288,256]{1,0:T(8,128)S(1)}, f32[288,256]{1,0:T(8,128)S(1)}, u32[]{:S(2)}, u32[]{:S(2)}) %collective-permute-start.34) | collective-permute-done | bytes 294944 | tf_op jit(solution)/shard_map/ppermute | solution.py:420
  175.4 0.8 bitcast_add_fusion
  (83 shorter events, 8.6 us)
Async XLA Ops:
  1.5 1.0 copy-start.7
  4.7 2.0 %copy-start = (bf16[4,576,720]{2,1,0:T(8,128)(2,1)S(1)}, bf16[4,576,720]{2,1,0:T(8,128)(2,1)}, u32[]{:S(2)}) copy-start(bf16[4,576,720]{2,1,0:T(8,128)(2,1)} %refs_5_.7) | copy-start | bytes 9953284
  6.7 2.0 %copy-start.2 = (bf16[4,576,720]{2,1,0:T(8,128)(2,1)S(1)}, bf16[4,576,720]{2,1,0:T(8,128)(2,1)}, u32[]{:S(2)}) copy-start(bf16[4,576,720]{2,1,0:T(8,128)(2,1)} %refs_6_.7) | copy-start | bytes 9953284
  8.7 31.7 %copy-start.1 = (bf16[4,576,720]{2,1,0:T(8,128)(2,1)S(1)}, bf16[4,576,720]{2,1,0:T(8,128)(2,1)}, u32[]{:S(2)}) copy-start(bf16[4,576,720]{2,1,0:T(8,128)(2,1)} %refs_5_.7) | copy-start | bytes 9953284
  11.9 28.6 %collective-permute-start.5 = (bf16[4,576,768]{2,1,0:T(8,128)(2,1)}, bf16[4,576,768]{2,1,0:T(8,128)(2,1)}, u32[]{:S(2)}, u32[]{:S(2)}) collective-permute-start(bf16[4,576,768]{2,1,0:T(8,128)(2,1)} %swap_halves.1), channel_id=1, source_target_pairs={{0,8},{1,9},{2,10},{3,11},{4,12},{5,13},{6,14},{7,15},{8,0},{9,1},... | collective-permute-start | bytes 10616840 | tf_op jit(solution)/shard_map/ppermute | solution.py:420
  11.9 8.2 %collective-permute-start = (bf16[304,256]{1,0:T(8,128)(2,1)S(1)}, bf16[304,256]{1,0:T(8,128)(2,1)S(1)}, u32[]{:S(2)}, u32[]{:S(2)}) collective-permute-start(bf16[304,256]{1,0:T(8,128)(2,1)S(1)} %get-tuple-element.32.dep), channel_id=1, source_target_pairs={{0,6},{1,7},{2,14},{3,15},{4,22},{5,23},{6,30},{7,31},{8,0},{9,1},... | collective-permute-start | bytes 466952 | tf_op jit(solution)/shard_map/ppermute | solution.py:420
  13.4 11.0 %collective-permute-start.1 = (bf16[304,256]{1,0:T(8,128)(2,1)S(1)}, bf16[304,256]{1,0:T(8,128)(2,1)S(1)}, u32[]{:S(2)}, u32[]{:S(2)}) collective-permute-start(bf16[304,256]{1,0:T(8,128)(2,1)S(1)} %get-tuple-element.32.dep), channel_id=1, source_target_pairs={{0,7},{1,6},{2,15},{3,14},{4,23},{5,22},{6,31},{7,30},{8,1},{9,0},... | collective-permute-start | bytes 466952 | tf_op jit(solution)/shard_map/ppermute | solution.py:420
  25.1 14.4 %collective-permute-start.8 = (bf16[608,256]{1,0:T(8,128)(2,1)}, bf16[608,256]{1,0:T(8,128)(2,1)}, u32[]{:S(2)}, u32[]{:S(2)}) collective-permute-start(bf16[608,256]{1,0:T(8,128)(2,1)} %join.1.refs_1_), channel_id=1, source_target_pairs={{0,6},{1,7},{2,0},{3,1},{4,2},{5,3},{6,4},{7,5},{8,14},{9,15},{10,... | collective-permute-start | bytes 933896 | tf_op jit(solution)/shard_map/ppermute | solution.py:420
  31.6 8.8 %collective-permute-start.6 = (bf16[608,256]{1,0:T(8,128)(2,1)}, bf16[608,256]{1,0:T(8,128)(2,1)}, u32[]{:S(2)}, u32[]{:S(2)}) collective-permute-start(bf16[608,256]{1,0:T(8,128)(2,1)} %join.1.refs_1_), channel_id=1, source_target_pairs={{0,8},{1,9},{2,10},{3,11},{4,12},{5,13},{6,14},{7,15},{8,0},{9,1},... | collective-permute-start | bytes 933896 | tf_op jit(solution)/shard_map/ppermute | solution.py:420
  31.6 23.1 %collective-permute-start.14 = (bf16[608,256]{1,0:T(8,128)(2,1)}, bf16[608,256]{1,0:T(8,128)(2,1)}, u32[]{:S(2)}, u32[]{:S(2)}) collective-permute-start(bf16[608,256]{1,0:T(8,128)(2,1)} %join.1.refs_1_), channel_id=1, source_target_pairs={{0,4},{1,5},{2,6},{3,7},{4,0},{5,1},{6,2},{7,3},{8,12},{9,13},{10,... | collective-permute-start | bytes 933896 | tf_op jit(solution)/shard_map/ppermute | solution.py:420
  39.6 15.2 %collective-permute-start.9 = (bf16[608,256]{1,0:T(8,128)(2,1)}, bf16[608,256]{1,0:T(8,128)(2,1)}, u32[]{:S(2)}, u32[]{:S(2)}) collective-permute-start(bf16[608,256]{1,0:T(8,128)(2,1)} %collective-permute-done.8.refs_1_), channel_id=1, source_target_pairs={{0,8},{1,9},{2,10},{3,11},{4,12},{5,13},{6,14},{7,15},{8,0},{9,1},... | collective-permute-start | bytes 933896 | tf_op jit(solution)/shard_map/ppermute | solution.py:420
  40.5 2.0 %copy-start.3 = (bf16[4,576,720]{2,1,0:T(8,128)(2,1)S(1)}, bf16[4,576,720]{2,1,0:T(8,128)(2,1)}, u32[]{:S(2)}) copy-start(bf16[4,576,720]{2,1,0:T(8,128)(2,1)} %refs_6_.7) | copy-start | bytes 9953284
  49.1 13.0 %collective-permute-start.7 = (bf16[272,768]{1,0:T(8,128)(2,1)S(1)}, bf16[272,768]{1,0:T(8,128)(2,1)S(1)}, u32[]{:S(2)}, u32[]{:S(2)}) collective-permute-start(bf16[272,768]{1,0:T(8,128)(2,1)S(1)} %get-tuple-element.35), channel_id=1, source_target_pairs={{0,16},{1,17},{2,18},{3,19},{4,20},{5,21},{6,22},{7,23},{8,24},{9,... | collective-permute-start | bytes 1253384 | tf_op jit(solution)/shard_map/ppermute | solution.py:420
  49.1 15.2 %collective-permute-start.2 = (bf16[608,256]{1,0:T(8,128)(2,1)}, bf16[608,256]{1,0:T(8,128)(2,1)S(1)}, u32[]{:S(2)}, u32[]{:S(2)}) collective-permute-start(bf16[608,256]{1,0:T(8,128)(2,1)} %join.1.refs_1_), channel_id=1, source_target_pairs={{0,2},{1,3},{2,4},{3,5},{4,6},{5,7},{6,0},{7,1},{8,10},{9,11},{10,... | collective-permute-start | bytes 933896 | tf_op jit(solution)/shard_map/ppermute | solution.py:420
  54.7 10.1 %collective-permute-start.15 = (bf16[608,256]{1,0:T(8,128)(2,1)}, bf16[608,256]{1,0:T(8,128)(2,1)S(1)}, u32[]{:S(2)}, u32[]{:S(2)}) collective-permute-start(bf16[608,256]{1,0:T(8,128)(2,1)} %collective-permute-done.14.refs_1_), channel_id=1, source_target_pairs={{0,8},{1,9},{2,10},{3,11},{4,12},{5,13},{6,14},{7,15},{8,0},{9,1},... | collective-permute-start | bytes 933896 | tf_op jit(solution)/shard_map/ppermute | solution.py:420
  54.8 10.1 %copy-start.4 = (bf16[4,576,720]{2,1,0:T(8,128)(2,1)S(1)}, bf16[4,576,720]{2,1,0:T(8,128)(2,1)}, u32[]{:S(2)}) copy-start(bf16[4,576,720]{2,1,0:T(8,128)(2,1)} %refs_6_.7) | copy-start | bytes 9953284
  61.7 12.5 %collective-permute-start.13 = (bf16[272,768]{1,0:T(8,128)(2,1)S(1)}, bf16[272,768]{1,0:T(8,128)(2,1)S(1)}, u32[]{:S(2)}, u32[]{:S(2)}) collective-permute-start(bf16[272,768]{1,0:T(8,128)(2,1)S(1)} %get-tuple-element.39), channel_id=1, source_target_pairs={{0,16},{1,17},{2,18},{3,19},{4,20},{5,21},{6,22},{7,23},{8,24},{9,... | collective-permute-start | bytes 1253384 | tf_op jit(solution)/shard_map/ppermute | solution.py:420
  62.5 15.9 %collective-permute-start.10 = (bf16[2,128,384]{2,1,0:T(8,128)(2,1)S(1)}, bf16[2,128,384]{2,1,0:T(8,128)(2,1)S(1)}, u32[]{:S(2)}, u32[]{:S(2)}) collective-permute-start(bf16[2,128,384]{2,1,0:T(8,128)(2,1)S(1)} %act.4.refs_8_.refs_1_), channel_id=1, source_target_pairs={{0,16},{1,17},{2,18},{3,19},{4,20},{5,21},{6,22},{7,23},{8,24},{9,... | collective-permute-start | bytes 589832 | tf_op jit(solution)/shard_map/ppermute | solution.py:420
  64.4 22.9 %collective-permute-start.4 = (bf16[608,256]{1,0:T(8,128)(2,1)S(1)}, bf16[608,256]{1,0:T(8,128)(2,1)S(1)}, u32[]{:S(2)}, u32[]{:S(2)}) collective-permute-start(bf16[608,256]{1,0:T(8,128)(2,1)S(1)} %collective-permute-done.2.refs_1_.meta), channel_id=1, source_target_pairs={{0,8},{1,9},{2,10},{3,11},{4,12},{5,13},{6,14},{7,15},{8,0},{9,1},... | collective-permute-start | bytes 933896 | tf_op jit(solution)/shard_map/ppermute | solution.py:420
  64.4 14.3 %collective-permute-start.11 = (bf16[2,128,384]{2,1,0:T(8,128)(2,1)S(1)}, bf16[2,128,384]{2,1,0:T(8,128)(2,1)S(1)}, u32[]{:S(2)}, u32[]{:S(2)}) collective-permute-start(bf16[2,128,384]{2,1,0:T(8,128)(2,1)S(1)} %act.4.refs_8_.refs_1_), channel_id=1, source_target_pairs={{0,8},{1,9},{2,10},{3,11},{4,12},{5,13},{6,14},{7,15},{8,0},{9,1},... | collective-permute-start | bytes 589832 | tf_op jit(solution)/shard_map/ppermute | solution.py:420
  64.9 17.8 %copy-start.5 = (bf16[4,720,576]{1,2,0:T(8,128)(2,1)S(1)}, bf16[4,720,576]{1,2,0:T(8,128)(2,1)}, u32[]{:S(2)}) copy-start(bf16[4,720,576]{1,2,0:T(8,128)(2,1)} %param.18) | copy-start | bytes 9953284
  74.7 7.9 %collective-permute-start.17 = (bf16[2,128,384]{2,1,0:T(8,128)(2,1)S(1)}, bf16[2,128,384]{2,1,0:T(8,128)(2,1)S(1)}, u32[]{:S(2)}, u32[]{:S(2)}) collective-permute-start(bf16[2,128,384]{2,1,0:T(8,128)(2,1)S(1)} %act.5.refs_7_.refs_1_), channel_id=1, source_target_pairs={{0,16},{1,17},{2,18},{3,19},{4,20},{5,21},{6,22},{7,23},{8,24},{9,... | collective-permute-start | bytes 589832 | tf_op jit(solution)/shard_map/ppermute | solution.py:420
  78.4 4.2 %collective-permute-start.12 = (bf16[2,128,384]{2,1,0:T(8,128)(2,1)S(1)}, bf16[2,128,384]{2,1,0:T(8,128)(2,1)S(1)}, u32[]{:S(2)}, u32[]{:S(2)}) collective-permute-start(bf16[2,128,384]{2,1,0:T(8,128)(2,1)S(1)} %collective-permute-done.10.refs_2_), channel_id=1, source_target_pairs={{0,8},{1,9},{2,10},{3,11},{4,12},{5,13},{6,14},{7,15},{8,0},{9,1},... | collective-permute-start | bytes 589832 | tf_op jit(solution)/shard_map/ppermute | solution.py:420
  78.4 15.6 %collective-permute-start.20 = (bf16[272,768]{1,0:T(8,128)(2,1)S(1)}, bf16[272,768]{1,0:T(8,128)(2,1)S(1)}, u32[]{:S(2)}, u32[]{:S(2)}) collective-permute-start(bf16[272,768]{1,0:T(8,128)(2,1)S(1)} %get-tuple-element.48), channel_id=1, source_target_pairs={{0,16},{1,17},{2,18},{3,19},{4,20},{5,21},{6,22},{7,23},{8,24},{9,... | collective-permute-start | bytes 1253384 | tf_op jit(solution)/shard_map/ppermute | solution.py:420
  78.7 17.7 %collective-permute-start.18 = (bf16[2,128,384]{2,1,0:T(8,128)(2,1)S(1)}, bf16[2,128,384]{2,1,0:T(8,128)(2,1)S(1)}, u32[]{:S(2)}, u32[]{:S(2)}) collective-permute-start(bf16[2,128,384]{2,1,0:T(8,128)(2,1)S(1)} %act.5.refs_7_.refs_1_), channel_id=1, source_target_pairs={{0,8},{1,9},{2,10},{3,11},{4,12},{5,13},{6,14},{7,15},{8,0},{9,1},... | collective-permute-start | bytes 589832 | tf_op jit(solution)/shard_map/ppermute | solution.py:420
  82.6 13.8 %collective-permute-start.19 = (bf16[2,128,384]{2,1,0:T(8,128)(2,1)S(1)}, bf16[2,128,384]{2,1,0:T(8,128)(2,1)S(1)}, u32[]{:S(2)}, u32[]{:S(2)}) collective-permute-start(bf16[2,128,384]{2,1,0:T(8,128)(2,1)S(1)} %collective-permute-done.17.refs_2_), channel_id=1, source_target_pairs={{0,8},{1,9},{2,10},{3,11},{4,12},{5,13},{6,14},{7,15},{8,0},{9,1},... | collective-permute-start | bytes 589832 | tf_op jit(solution)/shard_map/ppermute | solution.py:420
  85.7 10.7 %collective-permute-start.21 = (bf16[288,256]{1,0:T(8,128)(2,1)S(1)}, bf16[288,256]{1,0:T(8,128)(2,1)S(1)}, u32[]{:S(2)}, u32[]{:S(2)}) collective-permute-start(bf16[288,256]{1,0:T(8,128)(2,1)S(1)} %get-tuple-element.51), channel_id=1, source_target_pairs={{0,1},{1,0},{2,3},{3,2},{4,5},{5,4},{6,7},{7,6},{8,9},{9,8},{10,11... | collective-permute-start | bytes 442376 | tf_op jit(solution)/shard_map/ppermute | solution.py:420
  93.7 16.1 %collective-permute-start.16 = (bf16[272,768]{1,0:T(8,128)(2,1)S(1)}, bf16[272,768]{1,0:T(8,128)(2,1)S(1)}, u32[]{:S(2)}, u32[]{:S(2)}) collective-permute-start(bf16[272,768]{1,0:T(8,128)(2,1)S(1)} %get-tuple-element.45), channel_id=1, source_target_pairs={{0,16},{1,17},{2,18},{3,19},{4,20},{5,21},{6,22},{7,23},{8,24},{9,... | collective-permute-start | bytes 1253384 | tf_op jit(solution)/shard_map/ppermute | solution.py:420
  94.5 15.2 %collective-permute-start.25 = (bf16[2,128,384]{2,1,0:T(8,128)(2,1)S(1)}, bf16[2,128,384]{2,1,0:T(8,128)(2,1)S(1)}, u32[]{:S(2)}, u32[]{:S(2)}) collective-permute-start(bf16[2,128,384]{2,1,0:T(8,128)(2,1)S(1)} %act.6.refs_7_.refs_1_), channel_id=1, source_target_pairs={{0,16},{1,17},{2,18},{3,19},{4,20},{5,21},{6,22},{7,23},{8,24},{9,... | collective-permute-start | bytes 589832 | tf_op jit(solution)/shard_map/ppermute | solution.py:420
  99.5 10.3 %collective-permute-start.28 = (bf16[288,256]{1,0:T(8,128)(2,1)S(1)}, bf16[288,256]{1,0:T(8,128)(2,1)S(1)}, u32[]{:S(2)}, u32[]{:S(2)}) collective-permute-start(bf16[288,256]{1,0:T(8,128)(2,1)S(1)} %get-tuple-element.53), channel_id=1, source_target_pairs={{0,1},{1,0},{2,3},{3,2},{4,5},{5,4},{6,7},{7,6},{8,9},{9,8},{10,11... | collective-permute-start | bytes 442376 | tf_op jit(solution)/shard_map/ppermute | solution.py:420
  100.0 10.6 %collective-permute-start.26 = (bf16[2,128,384]{2,1,0:T(8,128)(2,1)S(1)}, bf16[2,128,384]{2,1,0:T(8,128)(2,1)S(1)}, u32[]{:S(2)}, u32[]{:S(2)}) collective-permute-start(bf16[2,128,384]{2,1,0:T(8,128)(2,1)S(1)} %act.6.refs_7_.refs_1_), channel_id=1, source_target_pairs={{0,8},{1,9},{2,10},{3,11},{4,12},{5,13},{6,14},{7,15},{8,0},{9,1},... | collective-permute-start | bytes 589832 | tf_op jit(solution)/shard_map/ppermute | solution.py:420
  100.1 10.6 %collective-permute-start.29 = (bf16[288,256]{1,0:T(8,128)(2,1)S(1)}, bf16[288,256]{1,0:T(8,128)(2,1)S(1)}, u32[]{:S(2)}, u32[]{:S(2)}) collective-permute-start(bf16[288,256]{1,0:T(8,128)(2,1)S(1)} %add_convert_fusion.2.refs_8_), channel_id=1, source_target_pairs={{0,2},{1,3},{2,4},{3,5},{4,6},{5,7},{6,0},{7,1},{8,10},{9,11},{10,... | collective-permute-start | bytes 442376 | tf_op jit(solution)/shard_map/ppermute | solution.py:420
  109.7 1.4 collective-permute-start.27
  110.3 7.4 %collective-permute-start.22 = (bf16[2,128,384]{2,1,0:T(8,128)(2,1)S(1)}, bf16[2,128,384]{2,1,0:T(8,128)(2,1)S(1)}, u32[]{:S(2)}, u32[]{:S(2)}) collective-permute-start(bf16[2,128,384]{2,1,0:T(8,128)(2,1)S(1)} %act.7.refs_7_.refs_1_), channel_id=1, source_target_pairs={{0,16},{1,17},{2,18},{3,19},{4,20},{5,21},{6,22},{7,23},{8,24},{9,... | collective-permute-start | bytes 589832 | tf_op jit(solution)/shard_map/ppermute | solution.py:420
  114.2 28.8 %copy-start.11 = (f32[2304]{0:T(1024)S(1)}, f32[2304]{0:T(1024)}, u32[]{:S(2)}) copy-start(f32[2304]{0:T(1024)} %param.19) | copy-start | bytes 27652
  114.2 28.9 %copy-start.12 = (f32[16]{0:T(128)S(1)}, f32[16]{0:T(128)}, u32[]{:S(2)}) copy-start(f32[16]{0:T(128)} %param.21) | copy-start | bytes 196
  114.2 36.5 %copy-start.6 = (bf16[2304,512]{1,0:T(8,128)(2,1)S(1)}, bf16[2304,512]{1,0:T(8,128)(2,1)}, u32[]{:S(2)}) copy-start(bf16[2304,512]{1,0:T(8,128)(2,1)} %refs_2_.1) | copy-start | bytes 7077892
  114.2 6.0 %collective-permute-start.32 = (bf16[288,256]{1,0:T(8,128)(2,1)S(1)}, bf16[288,256]{1,0:T(8,128)(2,1)S(1)}, u32[]{:S(2)}, u32[]{:S(2)}) collective-permute-start(bf16[288,256]{1,0:T(8,128)(2,1)S(1)} %get-tuple-element.57), channel_id=1, source_target_pairs={{0,1},{1,0},{2,3},{3,2},{4,5},{5,4},{6,7},{7,6},{8,9},{9,8},{10,11... | collective-permute-start | bytes 442376 | tf_op jit(solution)/shard_map/ppermute | solution.py:420
  114.8 10.5 %collective-permute-start.30 = (bf16[288,256]{1,0:T(8,128)(2,1)S(1)}, bf16[288,256]{1,0:T(8,128)(2,1)S(1)}, u32[]{:S(2)}, u32[]{:S(2)}) collective-permute-start(bf16[288,256]{1,0:T(8,128)(2,1)S(1)} %add_convert_fusion.1.refs_8_), channel_id=1, source_target_pairs={{0,4},{1,5},{2,6},{3,7},{4,0},{5,1},{6,2},{7,3},{8,12},{9,13},{10,... | collective-permute-start | bytes 442376 | tf_op jit(solution)/shard_map/ppermute | solution.py:420
  115.3 9.9 %collective-permute-start.23 = (bf16[2,128,384]{2,1,0:T(8,128)(2,1)S(1)}, bf16[2,128,384]{2,1,0:T(8,128)(2,1)S(1)}, u32[]{:S(2)}, u32[]{:S(2)}) collective-permute-start(bf16[2,128,384]{2,1,0:T(8,128)(2,1)S(1)} %act.7.refs_7_.refs_1_), channel_id=1, source_target_pairs={{0,8},{1,9},{2,10},{3,11},{4,12},{5,13},{6,14},{7,15},{8,0},{9,1},... | collective-permute-start | bytes 589832 | tf_op jit(solution)/shard_map/ppermute | solution.py:420
  117.7 7.6 %collective-permute-start.24 = (bf16[2,128,384]{2,1,0:T(8,128)(2,1)S(1)}, bf16[2,128,384]{2,1,0:T(8,128)(2,1)S(1)}, u32[]{:S(2)}, u32[]{:S(2)}) collective-permute-start(bf16[2,128,384]{2,1,0:T(8,128)(2,1)S(1)} %collective-permute-done.22.refs_2_), channel_id=1, source_target_pairs={{0,8},{1,9},{2,10},{3,11},{4,12},{5,13},{6,14},{7,15},{8,0},{9,1},... | collective-permute-start | bytes 589832 | tf_op jit(solution)/shard_map/ppermute | solution.py:420
  120.2 55.2 %copy-start.8 = (f32[256,288]{0,1:T(8,128)S(1)}, f32[256,288]{0,1:T(8,128)}, u32[]{:S(2)}) copy-start(f32[256,288]{0,1:T(8,128)} %param.11) | copy-start | bytes 884740
  120.2 17.0 %collective-permute-start.33 = (bf16[288,256]{1,0:T(8,128)(2,1)S(1)}, bf16[288,256]{1,0:T(8,128)(2,1)S(1)}, u32[]{:S(2)}, u32[]{:S(2)}) collective-permute-start(bf16[288,256]{1,0:T(8,128)(2,1)S(1)} %add_convert_fusion), channel_id=1, source_target_pairs={{0,6},{1,7},{2,0},{3,1},{4,2},{5,3},{6,4},{7,5},{8,14},{9,15},{10,... | collective-permute-start | bytes 442376 | tf_op jit(solution)/shard_map/ppermute | solution.py:420
  128.3 8.9 %collective-permute-start.31 = (bf16[288,256]{1,0:T(8,128)(2,1)S(1)}, bf16[288,256]{1,0:T(8,128)(2,1)S(1)}, u32[]{:S(2)}, u32[]{:S(2)}) collective-permute-start(bf16[288,256]{1,0:T(8,128)(2,1)S(1)} %get-tuple-element.56), channel_id=1, source_target_pairs={{0,1},{1,0},{2,3},{3,2},{4,5},{5,4},{6,7},{7,6},{8,9},{9,8},{10,11... | collective-permute-start | bytes 442376 | tf_op jit(solution)/shard_map/ppermute | solution.py:420
  129.9 7.3 %collective-permute-start.3 = (f32[4,288]{1,0:T(4,128)S(1)}, f32[4,288]{1,0:T(4,128)S(1)}, u32[]{:S(2)}, u32[]{:S(2)}) collective-permute-start(f32[4,288]{1,0:T(4,128)S(1)} %get-tuple-element.33), channel_id=1, source_target_pairs={{0,0},{1,1},{2,8},{3,9},{4,16},{5,17},{6,24},{7,25},{8,2},{9,3},{1... | collective-permute-start | bytes 13832 | tf_op jit(solution)/shard_map/ppermute | solution.py:420
  138.3 12.4 %all-to-all-start = ((f32[32,4,288]{2,1,0:T(4,128)}), f32[32,4,288]{2,1,0:T(4,128)S(1)}, u32[]{:S(2)}, u32[]{:S(2)}) async-start(f32[32,4,288]{2,1,0:T(4,128)} %get-tuple-element.59), calls=%async_computation | async-start | bytes 393216 | tf_op jit(solution)/shard_map/all_to_all | solution.py:494
  152.1 10.0 %all-to-all-start.1 = ((f32[32,2,16]{2,1,0:T(2,128)}), f32[32,2,16]{2,1,0:T(2,128)S(1)}, u32[]{:S(2)}, u32[]{:S(2)}) async-start(f32[32,2,16]{2,1,0:T(2,128)} %get-tuple-element.61), calls=%async_computation.1 | async-start | bytes 65536 | tf_op jit(solution)/shard_map/all_to_all | solution.py:494
  156.0 19.3 %collective-permute-start.34 = (f32[288,256]{1,0:T(8,128)S(1)}, f32[288,256]{1,0:T(8,128)S(1)}, u32[]{:S(2)}, u32[]{:S(2)}) collective-permute-start(f32[288,256]{1,0:T(8,128)S(1)} %get-tuple-element.58), channel_id=1, source_target_pairs={{0,0},{1,1},{2,8},{3,9},{4,16},{5,17},{6,24},{7,25},{8,2},{9,3},{1... | collective-permute-start | bytes 884744 | tf_op jit(solution)/shard_map/ppermute | solution.py:420
  (2 other events, 1.3 us)

commit v4 on v3

--- a/solution.py
+++ b/solution.py
@@ -23,7 +23,7 @@
     return -(-n // step) * step
 
 
-def params(mib=32):
+def params(mib=60):
     return pltpu.CompilerParams(vmem_limit_bytes=mib * 2**20)
 
 
@@ -35,7 +35,7 @@
     return jax.ShapeDtypeStruct(dims, dtype)
 
 
-def prep_kernel(tallies, x, gain, routes, out, ends):
+def prep_kernel(tallies, x, gain, routes, dep, out, ends):
     block, tokens = x.shape
     v = x[...]
     out[0:block] = (v * gain[...]).astype(bf16)
@@ -61,42 +61,43 @@
     )
 
 
-def prep_call(x, gain, routes, tallies):
+def prep_call(x, gain, routes, tallies, dep):
     block, tokens = x.shape
     reqs = tallies.shape[1]
     return pl.pallas_call(
         prep_kernel,
-        in_specs=[SMEM, VMEM, VMEM, VMEM],
+        in_specs=[SMEM, VMEM, VMEM, VMEM, ANY],
         out_specs=[VMEM, VMEM],
         out_shape=[shape((block + META, tokens), bf16), shape((reqs, block), f32)],
         compiler_params=params(),
         cost_estimate=cost(4 * tokens * block, 6 * tokens * block),
         name="prep",
-    )(tallies, x, gain, routes)
-
-
-def swap_kernel(scal, wg, wu, dep, out):
+    )(tallies, x, gain, routes, dep)
+
+
+def pack_kernel(scal, wg, wu, *refs):
+    out = refs[-1]
     half = wg.shape[2]
     out[:, :, 0:half] = wg[...]
     out[:, :, half:] = wu[...]
 
 
-def swap_call(scal, wg, wu, half, dep):
+def pack_call(scal, wg, wu, half, mine, deps):
     experts, depth, _ = wg.shape
-    theirs = pl.BlockSpec((1, depth, half), lambda n, s: (n, 0, 1 - s[0]))
-    return pl.pallas_call(
-        swap_kernel,
+    part = pl.BlockSpec((1, depth, half), lambda n, s: (n, 0, s[0] if mine else 1 - s[0]))
+    return pl.pallas_call(
+        pack_kernel,
         grid_spec=pltpu.PrefetchScalarGridSpec(
             num_scalar_prefetch=1,
             grid=(experts,),
-            in_specs=[theirs, theirs, ANY],
+            in_specs=[part, part] + [ANY] * len(deps),
             out_specs=pl.BlockSpec((1, depth, 2 * half), lambda n, s: (n, 0, 0)),
         ),
         out_shape=shape((experts, depth, 2 * half), bf16),
         compiler_params=params(),
         cost_estimate=cost(0, 8 * experts * depth * half),
-        name="swap_halves",
-    )(scal, wg, wu, dep)
+        name="pack_mine" if mine else "pack_other",
+    )(scal, wg, wu, *deps)
 
 
 def join_call(blocks):
@@ -119,11 +120,11 @@
 
 def partial_kernel(sides, scal, *refs):
     feeds, refs = refs[:2], refs[2:]
-    wr0, wr1, wg, wu, theirs = refs[:5]
+    wr0, wr1, mine, theirs = refs[:4]
     own, give, meta, cols, xs, xt, acc = refs[-7:]
     e = pl.program_id(0)
     core, side, y = scal[0], scal[1], scal[2]
-    depth, half = wg.shape[1], wg.shape[2]
+    depth, wide = mine.shape[1:]
     deep = up_to(depth)
     tokens = xt.shape[0]
     block = depth // sides
@@ -151,22 +152,21 @@
         far = jnp.where(y == 0, m[:, th:], m[:, 0:th])
         meta[...] = near
         hi = far.astype(bf16).astype(f32)
-        give[2 * th :] = jnp.zeros((META, 2 * half), bf16)
+        give[2 * th :] = jnp.zeros((META, wide), bf16)
         give[2 * th :, 0:th] = jnp.concatenate([hi, far - hi], axis=0).astype(bf16)
         xt[...] = xs[...].T
         cols[...] = xt[:, 2 * deep :]
 
     routes = xt[:, 2 * deep :].astype(f32)
     ef = e.astype(f32)
-    for which, w in enumerate((wg, wu)):
-        at = which * half
-        d = jnp.dot(xt[:, 0:depth], w[0], preferred_element_type=f32)
-        d += jnp.dot(
-            xt[:, deep : deep + depth], theirs[0, :, at : at + half], preferred_element_type=f32
-        )
+    step = 256
+    for at in range(0, wide, step):
+        to = slice(at, at + step)
+        d = jnp.dot(xt[:, 0:depth], mine[0, :, to], preferred_element_type=f32)
+        d += jnp.dot(xt[:, deep : deep + depth], theirs[0, :, to], preferred_element_type=f32)
         for k in range(2):
             take = (routes[:, k : k + 1] == ef) | (e == 0)
-            acc[k, :, at : at + half] = jnp.where(take, d, acc[k, :, at : at + half])
+            acc[k, :, to] = jnp.where(take, d, acc[k, :, to])
 
     @pl.when(e == pl.num_programs(0) - 1)
     def _():
@@ -175,14 +175,13 @@
             give[k * th : (k + 1) * th] = acc[k, pl.ds(pl.multiple_of((1 - y) * th, th), th)].astype(bf16)
 
 
-def partial_call(scal, sides, feeds, wr, weights, swapped, deps):
-    experts, depth, wide = swapped.shape
+def partial_call(scal, sides, feeds, wr, weights, deps):
+    experts, depth, wide = weights[0].shape
     half = wide // 2
     tokens = feeds[0].shape[1]
     deep = up_to(depth)
     full = lambda v: pl.BlockSpec(v.shape, lambda n, s: (0,) * len(v.shape))
-    mine = pl.BlockSpec((1, depth, half), lambda n, s: (n, 0, s[0]))
-    theirs = pl.BlockSpec((1, depth, wide), lambda n, s: (n, 0, 0))
+    part = pl.BlockSpec((1, depth, wide), lambda n, s: (n, 0, 0))
     outs = [
         shape((2, tokens // 2, wide), f32),
         shape((tokens + META, wide), bf16),
@@ -196,7 +195,7 @@
             grid=(experts,),
             in_specs=[full(v) for v in feeds]
             + [full(v) for v in wr]
-            + [mine, mine, theirs]
+            + [part, part]
             + [ANY] * len(deps),
             out_specs=[full(v) for v in outs],
             scratch_shapes=[
@@ -212,7 +211,7 @@
         ),
         name="gate_up_partial",
     )
-    return call(scal, *feeds, *wr, *weights, swapped, *deps)
+    return call(scal, *feeds, *wr, *weights, *deps)
 
 
 def act_kernel(scal, own, recv, meta, cols, *refs):
@@ -424,10 +423,6 @@
     home = lambda q, z, x: (z, q, x)
 
     scal = jnp.stack([core, side, y]).astype(jnp.int32)
-    sent, stream = prep_call(
-        skip_stream_arriving.T, premix_rmsnorm_gain[:, None], chosen_specialists.T, sequence_piece_tallies
-    )
-    first = [send(sent, lambda q, z, x, i=i: (z, (q - 1) % parts, x ^ i)) for i in range(sides)]
     wg, wu, wd = specialist_switch_weights, specialist_expand_weights, specialist_contract_weights
     if spread > 1:
         runs = [[q * spread + r for r in range(spread)] for q in range(parts)]
@@ -437,7 +432,16 @@
     wd = jnp.swapaxes(wd, 1, 2)
     depth, hidden = wg.shape[1], wg.shape[2]
     half = up_to(-(-hidden // 2))
-    swapped = send(swap_call(scal, wg, wu, half, sent), other_core)
+    given = pack_call(scal, wg, wu, half, False, ())
+    sent, stream = prep_call(
+        skip_stream_arriving.T,
+        premix_rmsnorm_gain[:, None],
+        chosen_specialists.T,
+        sequence_piece_tallies,
+        given,
+    )
+    first = [send(sent, lambda q, z, x, i=i: (z, (q - 1) % parts, x ^ i)) for i in range(sides)]
+    weights = (pack_call(scal, wg, wu, half, True, (sent,)), send(given, other_core))
     wr = []
     padded = jnp.pad(dispatcher_weights.T, ((0, 16 - dispatcher_weights.shape[1]), (0, 0)))
     for p in (part, part ^ 1):
@@ -454,7 +458,7 @@
     partial, act, pieces, shares, back = {}, {}, {}, {}, {}
 
     def do_partial(s, *deps):
-        own, give, meta, cols = partial_call(scal, sides, feeds[s], wr, (wg, wu), swapped, deps)
+        own, give, meta, cols = partial_call(scal, sides, feeds[s], wr, weights, deps)
         partial[s] = (own, send(give, other_y), meta, cols)
         return own
 
@@ -480,13 +484,13 @@
     a0 = do_act(0, p1)
     p2 = do_partial(2, a0)
     a1 = do_act(1, p2)
-    d0 = do_down(0, a1)
-    p3 = do_partial(3, d0)
+    p3 = do_partial(3, a1)
     a2 = do_act(2, p3)
-    d1 = do_down(1, a2, shares[0])
-    a3 = do_act(3, d1)
-    d2 = do_down(2, a3, shares[1], back[0])
-    do_down(3, d2, back[1])
+    d0 = do_down(0, a2)
+    a3 = do_act(3, d0)
+    d1 = do_down(1, a3)
+    d2 = do_down(2, d1, shares[0])
+    do_down(3, d2, shares[1])
     total, message = total_call(
         feeds[3][0], stream, [*shares[3], back[0], back[1], back[2]], block, count
     )

time: 177 us -> 205 us (1.16)
  Pallas kernels: 48.2 us -> 81.3 us
  waiting for transfers between devices: 71.3 us -> 52.7 us
  starting transfers between devices: 43.8 us -> 51.1 us
  local copies, waits for them, and re-layouts: 10.1 us -> 14.3 us
    ppermute x35, waiting for transfers between devices: 62.1 us -> 44.6 us  [send(): return lax.ppermute(value, ('dp', 'mp'), pairs)]
    pallas_call x6 -> x7, Pallas kernels: 30.8 us -> 43.5 us  [the longest x4 31.2 us: partial_call(): return call(scal, *feeds, *wr, *weights, *deps)]
    pallas_call x4, Pallas kernels: 12.1 us -> 20.8 us  [down_call(): pl.pallas_call(lambda *refs: down_kernel(sides, *refs), grid=(experts,),...]
    pallas_call x4, Pallas kernels: 2.01 us -> 9.69 us  [act_call(): pl.pallas_call(act_kernel, in_specs=[SMEM] + [VMEM] * 4 + [ANY] * len(dep...]
    ppermute x35, starting transfers between devices: 35.1 us -> 42.8 us  [send(): return lax.ppermute(value, ('dp', 'mp'), pairs)]
    unnamed x26 -> x80, local copies, waits for them, and re-layouts: 8.34 us -> 10.6 us
  transfers between devices with their start and end apart: 37 -> 37, of which waited for: 15 -> 10; matrix products, arithmetic and copies ran while one was open for 1% -> 3% of each run, Pallas kernels for 24% -> 35%
where the time goes in v4:
time: 205 us; the launch traced here: 203 us
  Pallas kernels  81.3 us (40%)
  waiting for transfers between devices  52.7 us (26%)
  starting transfers between devices  51.1 us (25%)
  local copies, waits for them, and re-layouts  14.3 us (7%)
  other arithmetic  3.03 us (1%)
    ppermute x35, waiting for transfers between devices, send(): return lax.ppermute(value, ('dp', 'mp'), pairs)  44.6 us
    ppermute x35, starting transfers between devices, send(): return lax.ppermute(value, ('dp', 'mp'), pairs)  42.8 us
    pallas_call x4, Pallas kernels, partial_call(): return call(scal, *feeds, *wr, *weights, *deps)  31.2 us
    pallas_call x4, Pallas kernels, down_call(): pl.pallas_call(lambda *refs: down_kernel(sides, *refs), grid=(experts,),...  20.8 us
    unnamed x80, local copies, waits for them, and re-layouts  10.6 us
    pallas_call x2, Pallas kernels, pack_call(): pl.pallas_call(pack_kernel, grid_spec=pltpu.PrefetchScalarGridSpec(num_sc...  10.3 us
    pallas_call x4, Pallas kernels, act_call(): pl.pallas_call(act_kernel, in_specs=[SMEM] + [VMEM] * 4 + [ANY] * len(dep...  9.69 us
    all_to_all x2, starting transfers between devices, body(): everyone = lambda v: lax.all_to_all(v, ('dp', 'mp'), 0, 0, tiled=True)  8.35 us
  transfers between devices with their start and end apart: 37, of which 10 were waited for; matrix products, arithmetic and copies ran while one was open for 3% of the time, Pallas kernels for 35%

profile of v4, /device:TPU:4, one launch (start us, length us, event | category | flops | bytes accessed | tf_op | source)
XLA Modules:
  0.0 203.4 jit_solution(3280290336643979024)
XLA Ops:
  1.3 5.2 %pack_other.1.dep = bf16[4,576,768]{2,1,0:T(8,128)(2,1)} custom-call(s32[3]{0:T(128)} %pad_add_fusion.scal.refs_0_, bf16[4,576,720]{2,1,0:T(8,128)(2,1)} %wg.3, bf16[4,576,720]{2,1,0:T(8,128)(2,1)} %wu.3), custom_call_target="tpu_custom_call" | custom-call | bytes 7077888 | tf_op jit(solution)/shard_map/pack_other/pallas_call | solution.py:88
  6.6 0.8 broadcast_in_dim.11.gain
  7.3 2.0 prep.1
  9.3 1.5 collective-permute-start
  10.8 3.6 %collective-permute-start.1 = (bf16[304,256]{1,0:T(8,128)(2,1)}, bf16[304,256]{1,0:T(8,128)(2,1)S(1)}, u32[]{:S(2)}, u32[]{:S(2)}) collective-permute-start(bf16[304,256]{1,0:T(8,128)(2,1)} %get-tuple-element.32.refs_0_), channel_id=1, source_target_pairs={{0,7},{1,6},{2,15},{3,14},{4,23},{5,22},{6,31},{7,30},{8,1},{9,0},... | collective-permute-start | bytes 466952 | tf_op jit(solution)/shard_map/ppermute | solution.py:419
  14.4 3.3 %collective-permute-done.refs_0_ = bf16[304,256]{1,0:T(8,128)(2,1)S(1)} collective-permute-done((bf16[304,256]{1,0:T(8,128)(2,1)}, bf16[304,256]{1,0:T(8,128)(2,1)S(1)}, u32[]{:S(2)}, u32[]{:S(2)}) %collective-permute-start) | collective-permute-done | bytes 155680 | tf_op jit(solution)/shard_map/ppermute | solution.py:419
  17.7 4.3 %collective-permute-done.1.refs_1_ = bf16[304,256]{1,0:T(8,128)(2,1)S(1)} collective-permute-done((bf16[304,256]{1,0:T(8,128)(2,1)}, bf16[304,256]{1,0:T(8,128)(2,1)S(1)}, u32[]{:S(2)}, u32[]{:S(2)}) %collective-permute-start.1) | collective-permute-done | bytes 155680 | tf_op jit(solution)/shard_map/ppermute | solution.py:419
  22.7 1.7 join.1.refs_1_
  24.4 6.5 %collective-permute-start.6 = (bf16[608,256]{1,0:T(8,128)(2,1)}, bf16[608,256]{1,0:T(8,128)(2,1)}, u32[]{:S(2)}, u32[]{:S(2)}) collective-permute-start(bf16[608,256]{1,0:T(8,128)(2,1)} %join.1.refs_1_), channel_id=1, source_target_pairs={{0,6},{1,7},{2,0},{3,1},{4,2},{5,3},{6,4},{7,5},{8,14},{9,15},{10,... | collective-permute-start | bytes 933896 | tf_op jit(solution)/shard_map/ppermute | solution.py:419
  30.9 7.9 %collective-permute-done.6.refs_1_ = bf16[608,256]{1,0:T(8,128)(2,1)} collective-permute-done((bf16[608,256]{1,0:T(8,128)(2,1)}, bf16[608,256]{1,0:T(8,128)(2,1)}, u32[]{:S(2)}, u32[]{:S(2)}) %collective-permute-start.6) | collective-permute-done | bytes 311328 | tf_op jit(solution)/shard_map/ppermute | solution.py:419
  38.8 5.0 %pack_mine.1.refs_5_ = bf16[4,576,768]{2,1,0:T(8,128)(2,1)} custom-call(s32[3]{0:T(128)} %pad_add_fusion.scal.refs_0_, bf16[4,576,720]{2,1,0:T(8,128)(2,1)} %wg.3, bf16[4,576,720]{2,1,0:T(8,128)(2,1)} %wu.3, bf16[304,256]{1,0:T(8,128)(2,1)} %get-tuple-element.32.refs_0_), custom_call_target="tpu_custom_call" | custom-call | bytes 7077888 | tf_op jit(solution)/shard_map/pack_mine/pallas_call | solution.py:88
  43.9 1.5 pad_dynamic-slice_fusion
  45.4 1.8 copy-done
  47.1 7.8 %gate_up_partial.4 = (f32[2,128,768]{2,1,0:T(8,128)}, bf16[272,768]{1,0:T(8,128)(2,1)}, f32[8,128]{1,0:T(8,128)}, bf16[256,128]{1,0:T(8,128)(2,1)}) custom-call(s32[3]{0:T(128)} %pad_add_fusion.scal.refs_0_, bf16[608,256]{1,0:T(8,128)(2,1)} %join.1.refs_1_, bf16[608,256]{1,0:T(8,128)(2,1)} %collective-permute-done.8.refs_2_, ...), custom_call_target="tpu_custom_call" | custom-call | flops 1811939328 | bytes 8257536 | tf_op jit(solution)/shard_map/gate_up_partial/pallas_call | solution.py:214
  54.9 5.7 %collective-permute-start.12 = (bf16[272,768]{1,0:T(8,128)(2,1)}, bf16[272,768]{1,0:T(8,128)(2,1)S(1)}, u32[]{:S(2)}, u32[]{:S(2)}) collective-permute-start(bf16[272,768]{1,0:T(8,128)(2,1)} %get-tuple-element.39), channel_id=1, source_target_pairs={{0,16},{1,17},{2,18},{3,19},{4,20},{5,21},{6,22},{7,23},{8,24},{9,... | collective-permute-start | bytes 1253384 | tf_op jit(solution)/shard_map/ppermute | solution.py:419
  60.7 7.8 %gate_up_partial.5 = (f32[2,128,768]{2,1,0:T(8,128)}, bf16[272,768]{1,0:T(8,128)(2,1)}, f32[8,128]{1,0:T(8,128)}, bf16[256,128]{1,0:T(8,128)(2,1)}) custom-call(s32[3]{0:T(128)} %pad_add_fusion.scal.refs_0_, bf16[608,256]{1,0:T(8,128)(2,1)} %collective-permute-done.6.refs_1_, bf16[608,256]{1,0:T(8,128)(2,1)} %collective-permute-done.7.refs_2_, ...), custom_call_target="tpu_custom_call" | custom-call | flops 1811939328 | bytes 8257536 | tf_op jit(solution)/shard_map/gate_up_partial/pallas_call | solution.py:214
  69.1 1.8 collective-permute-done.12.recv
  70.9 0.8 copy-done.13
  71.7 2.4 %act.4.refs_7_.refs_1_ = bf16[2,128,384]{2,1,0:T(8,128)(2,1)} custom-call(s32[1]{0:T(128)} %bitcast.4.scal, f32[2,128,768]{2,1,0:T(8,128)} %get-tuple-element.34.refs_7_.own, bf16[272,768]{1,0:T(8,128)(2,1)} %copy-done.13, f32[8,128]{1,0:T(8,128)} %get-tuple-element.40.meta, bf16[256,128]{1,0:T(8,128)(2,1)} %get-tuple-element.41.cols.refs_5_, ...), custom_call_target="tpu_custom_call" | custom-call | flops 1179648 | bytes 1376256 | tf_op jit(solution)/shard_map/act/pallas_call | solution.py:243
  74.8 7.8 %gate_up_partial.6 = (f32[2,128,768]{2,1,0:T(8,128)}, bf16[272,768]{1,0:T(8,128)(2,1)}, f32[8,128]{1,0:T(8,128)}, bf16[256,128]{1,0:T(8,128)(2,1)}) custom-call(s32[3]{0:T(128)} %pad_add_fusion.scal.refs_0_, bf16[608,256]{1,0:T(8,128)(2,1)} %collective-permute-done.10.refs_1_, bf16[608,256]{1,0:T(8,128)(2,1)} %copy-done.16, ...), custom_call_target="tpu_custom_call" | custom-call | flops 1811939328 | bytes 8257536 | tf_op jit(solution)/shard_map/gate_up_partial/pallas_call | solution.py:214
  82.6 2.2 %collective-permute-start.17 = (bf16[272,768]{1,0:T(8,128)(2,1)}, bf16[272,768]{1,0:T(8,128)(2,1)S(1)}, u32[]{:S(2)}, u32[]{:S(2)}) collective-permute-start(bf16[272,768]{1,0:T(8,128)(2,1)} %get-tuple-element.47), channel_id=1, source_target_pairs={{0,16},{1,17},{2,18},{3,19},{4,20},{5,21},{6,22},{7,23},{8,24},{9,... | collective-permute-start | bytes 1253384 | tf_op jit(solution)/shard_map/ppermute | solution.py:419
  85.0 0.8 copy-done.12
  85.7 2.4 %act.5.refs_7_.refs_1_ = bf16[2,128,384]{2,1,0:T(8,128)(2,1)} custom-call(s32[1]{0:T(128)} %bitcast.4.scal, f32[2,128,768]{2,1,0:T(8,128)} %get-tuple-element.35.refs_0_.own, bf16[272,768]{1,0:T(8,128)(2,1)} %copy-done.12, f32[8,128]{1,0:T(8,128)} %get-tuple-element.37.meta, bf16[256,128]{1,0:T(8,128)(2,1)} %get-tuple-element.38.cols.refs_5_, ...), custom_call_target="tpu_custom_call" | custom-call | flops 1179648 | bytes 1376256 | tf_op jit(solution)/shard_map/act/pallas_call | solution.py:243
  88.9 7.8 %gate_up_partial.7 = (f32[2,128,768]{2,1,0:T(8,128)}, bf16[272,768]{1,0:T(8,128)(2,1)}, f32[8,128]{1,0:T(8,128)}, bf16[256,128]{1,0:T(8,128)(2,1)}) custom-call(s32[3]{0:T(128)} %pad_add_fusion.scal.refs_0_, bf16[608,256]{1,0:T(8,128)(2,1)} %collective-permute-done.2.refs_1_.meta, bf16[608,256]{1,0:T(8,128)(2,1)} %copy-done.15, ...), custom_call_target="tpu_custom_call" | custom-call | flops 1811939328 | bytes 8257536 | tf_op jit(solution)/shard_map/gate_up_partial/pallas_call | solution.py:214
  96.7 1.9 collective-permute-start.13
  99.3 12.3 %collective-permute-done.24.refs_2_ = bf16[2,128,384]{2,1,0:T(8,128)(2,1)S(1)} collective-permute-done((bf16[2,128,384]{2,1,0:T(8,128)(2,1)S(1)}, bf16[2,128,384]{2,1,0:T(8,128)(2,1)S(1)}, u32[]{:S(2)}, u32[]{:S(2)}) %collective-permute-start.24) | collective-permute-done | bytes 196640 | tf_op jit(solution)/shard_map/ppermute | solution.py:419
  112.4 2.4 %act.6.refs_7_.refs_1_ = bf16[2,128,384]{2,1,0:T(8,128)(2,1)} custom-call(s32[1]{0:T(128)} %bitcast.4.scal, f32[2,128,768]{2,1,0:T(8,128)} %get-tuple-element.42.refs_0_.own, bf16[272,768]{1,0:T(8,128)(2,1)} %copy-done.11, f32[8,128]{1,0:T(8,128)} %get-tuple-element.48.meta, bf16[256,128]{1,0:T(8,128)(2,1)} %get-tuple-element.49.cols.refs_5_, ...), custom_call_target="tpu_custom_call" | custom-call | flops 1179648 | bytes 1376256 | tf_op jit(solution)/shard_map/act/pallas_call | solution.py:243
  114.9 1.5 collective-permute-start.21
  117.0 5.2 %down.4 = (bf16[288,256]{1,0:T(8,128)(2,1)}, bf16[288,256]{1,0:T(8,128)(2,1)}) custom-call(s32[3]{0:T(128)} %pad_add_fusion.scal.refs_0_, bf16[2,128,384]{2,1,0:T(8,128)(2,1)} %act.4.refs_7_.refs_1_, bf16[2,128,384]{2,1,0:T(8,128)(2,1)} %copy-done.21, bf16[2,128,384]{2,1,0:T(8,128)(2,1)} %copy-done.25, bf16[2,128,384]{2,1,0:T(8,128)(2,1)} %copy-done.27, ...), custom_call_target="tpu_custom_call" | custom-call | flops 849346560 | bytes 3612672 | tf_op jit(solution)/shard_map/down/pallas_call | solution.py:299
  122.3 1.5 collective-permute-start.27
  124.5 2.4 %act.7.refs_7_.refs_1_ = bf16[2,128,384]{2,1,0:T(8,128)(2,1)} custom-call(s32[1]{0:T(128)} %bitcast.4.scal, f32[2,128,768]{2,1,0:T(8,128)} %get-tuple-element.43.refs_0_.own, bf16[272,768]{1,0:T(8,128)(2,1)} %copy-done.14, f32[8,128]{1,0:T(8,128)} %get-tuple-element.45.meta, bf16[256,128]{1,0:T(8,128)(2,1)} %get-tuple-element.46.cols.refs_5_, ...), custom_call_target="tpu_custom_call" | custom-call | flops 1179648 | bytes 1376256 | tf_op jit(solution)/shard_map/act/pallas_call | solution.py:243
  128.3 5.2 %down.5 = (bf16[288,256]{1,0:T(8,128)(2,1)}, bf16[288,256]{1,0:T(8,128)(2,1)}) custom-call(s32[3]{0:T(128)} %pad_add_fusion.scal.refs_0_, bf16[2,128,384]{2,1,0:T(8,128)(2,1)} %act.5.refs_7_.refs_1_, bf16[2,128,384]{2,1,0:T(8,128)(2,1)} %copy-done.18, bf16[2,128,384]{2,1,0:T(8,128)(2,1)} %copy-done.23, bf16[2,128,384]{2,1,0:T(8,128)(2,1)} %copy-done.24, ...), custom_call_target="tpu_custom_call" | custom-call | flops 849346560 | bytes 3612672 | tf_op jit(solution)/shard_map/down/pallas_call | solution.py:299
  136.2 5.2 %down.6 = (bf16[288,256]{1,0:T(8,128)(2,1)}, bf16[288,256]{1,0:T(8,128)(2,1)}) custom-call(s32[3]{0:T(128)} %pad_add_fusion.scal.refs_0_, bf16[2,128,384]{2,1,0:T(8,128)(2,1)} %act.6.refs_7_.refs_1_, bf16[2,128,384]{2,1,0:T(8,128)(2,1)} %copy-done.17, bf16[2,128,384]{2,1,0:T(8,128)(2,1)} %copy-done.22, bf16[2,128,384]{2,1,0:T(8,128)(2,1)} %copy-done.28, ...), custom_call_target="tpu_custom_call" | custom-call | flops 849346560 | bytes 3612672 | tf_op jit(solution)/shard_map/down/pallas_call | solution.py:299
  141.4 1.6 collective-permute-start.32
  143.9 5.2 %down.7 = (bf16[288,256]{1,0:T(8,128)(2,1)}, bf16[288,256]{1,0:T(8,128)(2,1)}) custom-call(s32[3]{0:T(128)} %pad_add_fusion.scal.refs_0_, bf16[2,128,384]{2,1,0:T(8,128)(2,1)} %act.7.refs_7_.refs_1_, bf16[2,128,384]{2,1,0:T(8,128)(2,1)} %copy-done.19, bf16[2,128,384]{2,1,0:T(8,128)(2,1)} %copy-done.20, bf16[2,128,384]{2,1,0:T(8,128)(2,1)} %copy-done.26, ...), custom_call_target="tpu_custom_call" | custom-call | flops 849346560 | bytes 3612672 | tf_op jit(solution)/shard_map/down/pallas_call | solution.py:299
  149.1 1.1 collective-permute-start.29
  150.3 2.4 %collective-permute-start.33 = (bf16[288,256]{1,0:T(8,128)(2,1)S(1)}, bf16[288,256]{1,0:T(8,128)(2,1)S(1)}, u32[]{:S(2)}, u32[]{:S(2)}) collective-permute-start(bf16[288,256]{1,0:T(8,128)(2,1)S(1)} %add_convert_fusion), channel_id=1, source_target_pairs={{0,6},{1,7},{2,0},{3,1},{4,2},{5,3},{6,4},{7,5},{8,14},{9,15},{10,... | collective-permute-start | bytes 442376 | tf_op jit(solution)/shard_map/ppermute | solution.py:419
  152.7 4.8 %collective-permute-start.3 = (f32[4,288]{1,0:T(4,128)S(1)}, f32[4,288]{1,0:T(4,128)S(1)}, u32[]{:S(2)}, u32[]{:S(2)}) collective-permute-start(f32[4,288]{1,0:T(4,128)S(1)} %copy-done.39), channel_id=1, source_target_pairs={{0,0},{1,1},{2,8},{3,9},{4,16},{5,17},{6,24},{7,25},{8,2},{9,3},{1... | collective-permute-start | bytes 13832 | tf_op jit(solution)/shard_map/ppermute | solution.py:419
  157.4 2.6 %collective-permute-done.3.stream = f32[4,288]{1,0:T(4,128)S(1)} collective-permute-done((f32[4,288]{1,0:T(4,128)S(1)}, f32[4,288]{1,0:T(4,128)S(1)}, u32[]{:S(2)}, u32[]{:S(2)}) %collective-permute-start.3) | collective-permute-done | bytes 4640 | tf_op jit(solution)/shard_map/ppermute | solution.py:419
  160.8 2.3 %branch_total.1 = (f32[288,256]{1,0:T(8,128)}, f32[32,4,288]{2,1,0:T(4,128)}) custom-call(bf16[608,256]{1,0:T(8,128)(2,1)} %collective-permute-done.2.refs_1_.meta, f32[4,288]{1,0:T(4,128)} %copy-done.36, bf16[288,256]{1,0:T(8,128)(2,1)} %get-tuple-element.55.refs_0_, bf16[288,256]{1,0:T(8,128)(2,1)} %copy-done.33, bf16[288,256]{1,0:T(8,128)(2,1)} %copy-done.31, ...), custom_call_target="tpu_custom_call" | custom-call | flops 1179648 | bytes 1032192 | tf_op jit(solution)/shard_map/branch_total/pallas_call | solution.py:336
  163.1 4.4 %all-to-all-start = ((f32[32,4,288]{2,1,0:T(4,128)}), f32[32,4,288]{2,1,0:T(4,128)S(1)}, u32[]{:S(2)}, u32[]{:S(2)}) async-start(f32[32,4,288]{2,1,0:T(4,128)} %get-tuple-element.59), calls=%async_computation | async-start | bytes 393216 | tf_op jit(solution)/shard_map/all_to_all | solution.py:498
  168.9 6.3 %all-to-all-done.refs_0_ = f32[32,4,288]{2,1,0:T(4,128)S(1)} async-done(((f32[32,4,288]{2,1,0:T(4,128)}), f32[32,4,288]{2,1,0:T(4,128)S(1)}, u32[]{:S(2)}, u32[]{:S(2)}) %all-to-all-start) | async-done | bytes 147488 | tf_op jit(solution)/shard_map/all_to_all | solution.py:498
  175.9 3.2 %head.1 = (f32[16,512]{1,0:T(8,128)}, f32[32,2,16]{2,1,0:T(2,128)}) custom-call(f32[32,4,288]{2,1,0:T(4,128)} %copy-done.5, f32[8,288]{1,0:T(8,128)} %reshape.12.refs_1_, bf16[2304,512]{1,0:T(8,128)(2,1)} %refs_2_.1, f32[16,1]{1,0:T(8,128)} %copy.16.refs_3_), custom_call_target="tpu_custom_call" | custom-call | flops 37748736 | bytes 2359296 | tf_op jit(solution)/shard_map/head/pallas_call | solution.py:375
  179.2 3.9 %all-to-all-start.1 = ((f32[32,2,16]{2,1,0:T(2,128)}), f32[32,2,16]{2,1,0:T(2,128)S(1)}, u32[]{:S(2)}, u32[]{:S(2)}) async-start(f32[32,2,16]{2,1,0:T(2,128)} %get-tuple-element.61), calls=%async_computation.1 | async-start | bytes 65536 | tf_op jit(solution)/shard_map/all_to_all | solution.py:498
  183.1 4.3 %collective-permute-start.34 = (f32[288,256]{1,0:T(8,128)}, f32[288,256]{1,0:T(8,128)S(1)}, u32[]{:S(2)}, u32[]{:S(2)}) collective-permute-start(f32[288,256]{1,0:T(8,128)} %get-tuple-element.58), channel_id=1, source_target_pairs={{0,0},{1,1},{2,8},{3,9},{4,16},{5,17},{6,24},{7,25},{8,2},{9,3},{1... | collective-permute-start | bytes 884744 | tf_op jit(solution)/shard_map/ppermute | solution.py:419
  187.4 1.8 all-to-all-done.1
  189.2 1.5 subtract_subtract_fusion
  190.7 11.9 %collective-permute-done.34 = f32[288,256]{1,0:T(8,128)S(1)} collective-permute-done((f32[288,256]{1,0:T(8,128)}, f32[288,256]{1,0:T(8,128)S(1)}, u32[]{:S(2)}, u32[]{:S(2)}) %collective-permute-start.34) | collective-permute-done | bytes 294944 | tf_op jit(solution)/shard_map/ppermute | solution.py:419
  (138 shorter events, 14.9 us)
Async XLA Ops:
  6.5 38.8 %collective-permute-start.5 = (bf16[4,576,768]{2,1,0:T(8,128)(2,1)}, bf16[4,576,768]{2,1,0:T(8,128)(2,1)S(1)}, u32[]{:S(2)}, u32[]{:S(2)}) collective-permute-start(bf16[4,576,768]{2,1,0:T(8,128)(2,1)} %pack_other.1.dep), channel_id=1, source_target_pairs={{0,8},{1,9},{2,10},{3,11},{4,12},{5,13},{6,14},{7,15},{8,0},{9,1},... | collective-permute-start | bytes 10616840 | tf_op jit(solution)/shard_map/ppermute | solution.py:419
  9.3 8.4 %collective-permute-start = (bf16[304,256]{1,0:T(8,128)(2,1)}, bf16[304,256]{1,0:T(8,128)(2,1)S(1)}, u32[]{:S(2)}, u32[]{:S(2)}) collective-permute-start(bf16[304,256]{1,0:T(8,128)(2,1)} %get-tuple-element.32.refs_0_), channel_id=1, source_target_pairs={{0,6},{1,7},{2,14},{3,15},{4,22},{5,23},{6,30},{7,31},{8,0},{9,1},... | collective-permute-start | bytes 466952 | tf_op jit(solution)/shard_map/ppermute | solution.py:419
  10.8 11.2 %collective-permute-start.1 = (bf16[304,256]{1,0:T(8,128)(2,1)}, bf16[304,256]{1,0:T(8,128)(2,1)S(1)}, u32[]{:S(2)}, u32[]{:S(2)}) collective-permute-start(bf16[304,256]{1,0:T(8,128)(2,1)} %get-tuple-element.32.refs_0_), channel_id=1, source_target_pairs={{0,7},{1,6},{2,15},{3,14},{4,23},{5,22},{6,31},{7,30},{8,1},{9,0},... | collective-permute-start | bytes 466952 | tf_op jit(solution)/shard_map/ppermute | solution.py:419
  24.4 14.4 %collective-permute-start.6 = (bf16[608,256]{1,0:T(8,128)(2,1)}, bf16[608,256]{1,0:T(8,128)(2,1)}, u32[]{:S(2)}, u32[]{:S(2)}) collective-permute-start(bf16[608,256]{1,0:T(8,128)(2,1)} %join.1.refs_1_), channel_id=1, source_target_pairs={{0,6},{1,7},{2,0},{3,1},{4,2},{5,3},{6,4},{7,5},{8,14},{9,15},{10,... | collective-permute-start | bytes 933896 | tf_op jit(solution)/shard_map/ppermute | solution.py:419
  30.9 14.4 %collective-permute-start.8 = (bf16[608,256]{1,0:T(8,128)(2,1)}, bf16[608,256]{1,0:T(8,128)(2,1)}, u32[]{:S(2)}, u32[]{:S(2)}) collective-permute-start(bf16[608,256]{1,0:T(8,128)(2,1)} %join.1.refs_1_), channel_id=1, source_target_pairs={{0,8},{1,9},{2,10},{3,11},{4,12},{5,13},{6,14},{7,15},{8,0},{9,1},... | collective-permute-start | bytes 933896 | tf_op jit(solution)/shard_map/ppermute | solution.py:419
  30.9 29.8 %collective-permute-start.10 = (bf16[608,256]{1,0:T(8,128)(2,1)}, bf16[608,256]{1,0:T(8,128)(2,1)}, u32[]{:S(2)}, u32[]{:S(2)}) collective-permute-start(bf16[608,256]{1,0:T(8,128)(2,1)} %join.1.refs_1_), channel_id=1, source_target_pairs={{0,4},{1,5},{2,6},{3,7},{4,0},{5,1},{6,2},{7,3},{8,12},{9,13},{10,... | collective-permute-start | bytes 933896 | tf_op jit(solution)/shard_map/ppermute | solution.py:419
  38.8 21.8 %collective-permute-start.7 = (bf16[608,256]{1,0:T(8,128)(2,1)}, bf16[608,256]{1,0:T(8,128)(2,1)}, u32[]{:S(2)}, u32[]{:S(2)}) collective-permute-start(bf16[608,256]{1,0:T(8,128)(2,1)} %collective-permute-done.6.refs_1_), channel_id=1, source_target_pairs={{0,8},{1,9},{2,10},{3,11},{4,12},{5,13},{6,14},{7,15},{8,0},{9,1},... | collective-permute-start | bytes 933896 | tf_op jit(solution)/shard_map/ppermute | solution.py:419
  45.3 23.5 %collective-permute-start.2 = (bf16[608,256]{1,0:T(8,128)(2,1)}, bf16[608,256]{1,0:T(8,128)(2,1)}, u32[]{:S(2)}, u32[]{:S(2)}) collective-permute-start(bf16[608,256]{1,0:T(8,128)(2,1)} %join.1.refs_1_), channel_id=1, source_target_pairs={{0,2},{1,3},{2,4},{3,5},{4,6},{5,7},{6,0},{7,1},{8,10},{9,11},{10,... | collective-permute-start | bytes 933896 | tf_op jit(solution)/shard_map/ppermute | solution.py:419
  54.9 16.0 %collective-permute-start.12 = (bf16[272,768]{1,0:T(8,128)(2,1)}, bf16[272,768]{1,0:T(8,128)(2,1)S(1)}, u32[]{:S(2)}, u32[]{:S(2)}) collective-permute-start(bf16[272,768]{1,0:T(8,128)(2,1)} %get-tuple-element.39), channel_id=1, source_target_pairs={{0,16},{1,17},{2,18},{3,19},{4,20},{5,21},{6,22},{7,23},{8,24},{9,... | collective-permute-start | bytes 1253384 | tf_op jit(solution)/shard_map/ppermute | solution.py:419
  60.7 13.5 %collective-permute-start.11 = (bf16[608,256]{1,0:T(8,128)(2,1)}, bf16[608,256]{1,0:T(8,128)(2,1)S(1)}, u32[]{:S(2)}, u32[]{:S(2)}) collective-permute-start(bf16[608,256]{1,0:T(8,128)(2,1)} %collective-permute-done.10.refs_1_), channel_id=1, source_target_pairs={{0,8},{1,9},{2,10},{3,11},{4,12},{5,13},{6,14},{7,15},{8,0},{9,1},... | collective-permute-start | bytes 933896 | tf_op jit(solution)/shard_map/ppermute | solution.py:419
  68.5 16.5 %collective-permute-start.9 = (bf16[272,768]{1,0:T(8,128)(2,1)}, bf16[272,768]{1,0:T(8,128)(2,1)S(1)}, u32[]{:S(2)}, u32[]{:S(2)}) collective-permute-start(bf16[272,768]{1,0:T(8,128)(2,1)} %get-tuple-element.36), channel_id=1, source_target_pairs={{0,16},{1,17},{2,18},{3,19},{4,20},{5,21},{6,22},{7,23},{8,24},{9,... | collective-permute-start | bytes 1253384 | tf_op jit(solution)/shard_map/ppermute | solution.py:419
  68.8 19.3 %collective-permute-start.4 = (bf16[608,256]{1,0:T(8,128)(2,1)}, bf16[608,256]{1,0:T(8,128)(2,1)S(1)}, u32[]{:S(2)}, u32[]{:S(2)}) collective-permute-start(bf16[608,256]{1,0:T(8,128)(2,1)} %collective-permute-done.2.refs_1_.meta), channel_id=1, source_target_pairs={{0,8},{1,9},{2,10},{3,11},{4,12},{5,13},{6,14},{7,15},{8,0},{9,1},... | collective-permute-start | bytes 933896 | tf_op jit(solution)/shard_map/ppermute | solution.py:419
  74.1 10.7 %copy-start.3 = (bf16[2,128,384]{2,1,0:T(8,128)(2,1)S(1)}, bf16[2,128,384]{2,1,0:T(8,128)(2,1)}, u32[]{:S(2)}) copy-start(bf16[2,128,384]{2,1,0:T(8,128)(2,1)} %act.4.refs_7_.refs_1_) | copy-start | bytes 589828
  82.6 29.0 %collective-permute-start.17 = (bf16[272,768]{1,0:T(8,128)(2,1)}, bf16[272,768]{1,0:T(8,128)(2,1)S(1)}, u32[]{:S(2)}, u32[]{:S(2)}) collective-permute-start(bf16[272,768]{1,0:T(8,128)(2,1)} %get-tuple-element.47), channel_id=1, source_target_pairs={{0,16},{1,17},{2,18},{3,19},{4,20},{5,21},{6,22},{7,23},{8,24},{9,... | collective-permute-start | bytes 1253384 | tf_op jit(solution)/shard_map/ppermute | solution.py:419
  84.9 13.9 %collective-permute-start.14 = (bf16[2,128,384]{2,1,0:T(8,128)(2,1)S(1)}, bf16[2,128,384]{2,1,0:T(8,128)(2,1)S(1)}, u32[]{:S(2)}, u32[]{:S(2)}) collective-permute-start(bf16[2,128,384]{2,1,0:T(8,128)(2,1)S(1)} %copy-done.3), channel_id=1, source_target_pairs={{0,16},{1,17},{2,18},{3,19},{4,20},{5,21},{6,22},{7,23},{8,24},{9,... | collective-permute-start | bytes 589832 | tf_op jit(solution)/shard_map/ppermute | solution.py:419
  88.1 10.5 %copy-start.2 = (bf16[2,128,384]{2,1,0:T(8,128)(2,1)S(1)}, bf16[2,128,384]{2,1,0:T(8,128)(2,1)}, u32[]{:S(2)}) copy-start(bf16[2,128,384]{2,1,0:T(8,128)(2,1)} %act.5.refs_7_.refs_1_) | copy-start | bytes 589828
  96.7 27.0 %collective-permute-start.13 = (bf16[272,768]{1,0:T(8,128)(2,1)}, bf16[272,768]{1,0:T(8,128)(2,1)S(1)}, u32[]{:S(2)}, u32[]{:S(2)}) collective-permute-start(bf16[272,768]{1,0:T(8,128)(2,1)} %get-tuple-element.44), channel_id=1, source_target_pairs={{0,16},{1,17},{2,18},{3,19},{4,20},{5,21},{6,22},{7,23},{8,24},{9,... | collective-permute-start | bytes 1253384 | tf_op jit(solution)/shard_map/ppermute | solution.py:419
  98.7 12.9 %collective-permute-start.24 = (bf16[2,128,384]{2,1,0:T(8,128)(2,1)S(1)}, bf16[2,128,384]{2,1,0:T(8,128)(2,1)S(1)}, u32[]{:S(2)}, u32[]{:S(2)}) collective-permute-start(bf16[2,128,384]{2,1,0:T(8,128)(2,1)S(1)} %copy-done.2), channel_id=1, source_target_pairs={{0,16},{1,17},{2,18},{3,19},{4,20},{5,21},{6,22},{7,23},{8,24},{9,... | collective-permute-start | bytes 589832 | tf_op jit(solution)/shard_map/ppermute | solution.py:419
  98.8 16.1 %collective-permute-start.15 = (bf16[2,128,384]{2,1,0:T(8,128)(2,1)S(1)}, bf16[2,128,384]{2,1,0:T(8,128)(2,1)S(1)}, u32[]{:S(2)}, u32[]{:S(2)}) collective-permute-start(bf16[2,128,384]{2,1,0:T(8,128)(2,1)S(1)} %copy-done.3), channel_id=1, source_target_pairs={{0,8},{1,9},{2,10},{3,11},{4,12},{5,13},{6,14},{7,15},{8,0},{9,1},... | collective-permute-start | bytes 589832 | tf_op jit(solution)/shard_map/ppermute | solution.py:419
  98.8 17.6 %copy-start.21 = (bf16[2,128,384]{2,1,0:T(8,128)(2,1)}, bf16[2,128,384]{2,1,0:T(8,128)(2,1)S(1)}, u32[]{:S(2)}) copy-start(bf16[2,128,384]{2,1,0:T(8,128)(2,1)S(1)} %collective-permute-done.14.refs_2_) | copy-start | bytes 589828
  98.8 17.6 %collective-permute-start.16 = (bf16[2,128,384]{2,1,0:T(8,128)(2,1)S(1)}, bf16[2,128,384]{2,1,0:T(8,128)(2,1)S(1)}, u32[]{:S(2)}, u32[]{:S(2)}) collective-permute-start(bf16[2,128,384]{2,1,0:T(8,128)(2,1)S(1)} %collective-permute-done.14.refs_2_), channel_id=1, source_target_pairs={{0,8},{1,9},{2,10},{3,11},{4,12},{5,13},{6,14},{7,15},{8,0},{9,1},... | collective-permute-start | bytes 589832 | tf_op jit(solution)/shard_map/ppermute | solution.py:419
  111.6 16.0 %copy-start.18 = (bf16[2,128,384]{2,1,0:T(8,128)(2,1)}, bf16[2,128,384]{2,1,0:T(8,128)(2,1)S(1)}, u32[]{:S(2)}) copy-start(bf16[2,128,384]{2,1,0:T(8,128)(2,1)S(1)} %collective-permute-done.24.refs_2_) | copy-start | bytes 589828
  111.6 15.3 %collective-permute-start.25 = (bf16[2,128,384]{2,1,0:T(8,128)(2,1)S(1)}, bf16[2,128,384]{2,1,0:T(8,128)(2,1)S(1)}, u32[]{:S(2)}, u32[]{:S(2)}) collective-permute-start(bf16[2,128,384]{2,1,0:T(8,128)(2,1)S(1)} %copy-done.2), channel_id=1, source_target_pairs={{0,8},{1,9},{2,10},{3,11},{4,12},{5,13},{6,14},{7,15},{8,0},{9,1},... | collective-permute-start | bytes 589832 | tf_op jit(solution)/shard_map/ppermute | solution.py:419
  111.6 15.9 %collective-permute-start.26 = (bf16[2,128,384]{2,1,0:T(8,128)(2,1)S(1)}, bf16[2,128,384]{2,1,0:T(8,128)(2,1)S(1)}, u32[]{:S(2)}, u32[]{:S(2)}) collective-permute-start(bf16[2,128,384]{2,1,0:T(8,128)(2,1)S(1)} %collective-permute-done.24.refs_2_), channel_id=1, source_target_pairs={{0,8},{1,9},{2,10},{3,11},{4,12},{5,13},{6,14},{7,15},{8,0},{9,1},... | collective-permute-start | bytes 589832 | tf_op jit(solution)/shard_map/ppermute | solution.py:419
  114.9 8.9 %copy-start.1 = (bf16[2,128,384]{2,1,0:T(8,128)(2,1)S(1)}, bf16[2,128,384]{2,1,0:T(8,128)(2,1)}, u32[]{:S(2)}) copy-start(bf16[2,128,384]{2,1,0:T(8,128)(2,1)} %act.6.refs_7_.refs_1_) | copy-start | bytes 589828
  114.9 19.2 %collective-permute-start.21 = (bf16[2,128,384]{2,1,0:T(8,128)(2,1)}, bf16[2,128,384]{2,1,0:T(8,128)(2,1)S(1)}, u32[]{:S(2)}, u32[]{:S(2)}) collective-permute-start(bf16[2,128,384]{2,1,0:T(8,128)(2,1)} %act.6.refs_7_.refs_1_), channel_id=1, source_target_pairs={{0,16},{1,17},{2,18},{3,19},{4,20},{5,21},{6,22},{7,23},{8,24},{9,... | collective-permute-start | bytes 589832 | tf_op jit(solution)/shard_map/ppermute | solution.py:419
  122.3 11.8 %copy-start.7 = (bf16[288,256]{1,0:T(8,128)(2,1)S(1)}, bf16[288,256]{1,0:T(8,128)(2,1)}, u32[]{:S(2)}) copy-start(bf16[288,256]{1,0:T(8,128)(2,1)} %get-tuple-element.50.refs_0_) | copy-start | bytes 442372
  122.3 11.2 %collective-permute-start.27 = (bf16[288,256]{1,0:T(8,128)(2,1)}, bf16[288,256]{1,0:T(8,128)(2,1)S(1)}, u32[]{:S(2)}, u32[]{:S(2)}) collective-permute-start(bf16[288,256]{1,0:T(8,128)(2,1)} %get-tuple-element.52), channel_id=1, source_target_pairs={{0,1},{1,0},{2,3},{3,2},{4,5},{5,4},{6,7},{7,6},{8,9},{9,8},{10,11... | collective-permute-start | bytes 442376 | tf_op jit(solution)/shard_map/ppermute | solution.py:419
  123.8 10.4 %collective-permute-start.22 = (bf16[2,128,384]{2,1,0:T(8,128)(2,1)S(1)}, bf16[2,128,384]{2,1,0:T(8,128)(2,1)S(1)}, u32[]{:S(2)}, u32[]{:S(2)}) collective-permute-start(bf16[2,128,384]{2,1,0:T(8,128)(2,1)S(1)} %copy-done.1), channel_id=1, source_target_pairs={{0,8},{1,9},{2,10},{3,11},{4,12},{5,13},{6,14},{7,15},{8,0},{9,1},... | collective-permute-start | bytes 589832 | tf_op jit(solution)/shard_map/ppermute | solution.py:419
  127.0 7.9 %collective-permute-start.18 = (bf16[2,128,384]{2,1,0:T(8,128)(2,1)}, bf16[2,128,384]{2,1,0:T(8,128)(2,1)S(1)}, u32[]{:S(2)}, u32[]{:S(2)}) collective-permute-start(bf16[2,128,384]{2,1,0:T(8,128)(2,1)} %act.7.refs_7_.refs_1_), channel_id=1, source_target_pairs={{0,16},{1,17},{2,18},{3,19},{4,20},{5,21},{6,22},{7,23},{8,24},{9,... | collective-permute-start | bytes 589832 | tf_op jit(solution)/shard_map/ppermute | solution.py:419
  127.6 15.6 %collective-permute-start.19 = (bf16[2,128,384]{2,1,0:T(8,128)(2,1)}, bf16[2,128,384]{2,1,0:T(8,128)(2,1)S(1)}, u32[]{:S(2)}, u32[]{:S(2)}) collective-permute-start(bf16[2,128,384]{2,1,0:T(8,128)(2,1)} %act.7.refs_7_.refs_1_), channel_id=1, source_target_pairs={{0,8},{1,9},{2,10},{3,11},{4,12},{5,13},{6,14},{7,15},{8,0},{9,1},... | collective-permute-start | bytes 589832 | tf_op jit(solution)/shard_map/ppermute | solution.py:419
  133.5 9.5 %copy-start.8 = (bf16[288,256]{1,0:T(8,128)(2,1)S(1)}, bf16[288,256]{1,0:T(8,128)(2,1)}, u32[]{:S(2)}) copy-start(bf16[288,256]{1,0:T(8,128)(2,1)} %get-tuple-element.51.refs_7_) | copy-start | bytes 442372
  133.5 9.5 %collective-permute-start.28 = (bf16[288,256]{1,0:T(8,128)(2,1)}, bf16[288,256]{1,0:T(8,128)(2,1)S(1)}, u32[]{:S(2)}, u32[]{:S(2)}) collective-permute-start(bf16[288,256]{1,0:T(8,128)(2,1)} %get-tuple-element.54), channel_id=1, source_target_pairs={{0,1},{1,0},{2,3},{3,2},{4,5},{5,4},{6,7},{7,6},{8,9},{9,8},{10,11... | collective-permute-start | bytes 442376 | tf_op jit(solution)/shard_map/ppermute | solution.py:419
  134.1 1.4 collective-permute-start.23
  134.2 25.9 %collective-permute-start.30 = (bf16[288,256]{1,0:T(8,128)(2,1)S(1)}, bf16[288,256]{1,0:T(8,128)(2,1)S(1)}, u32[]{:S(2)}, u32[]{:S(2)}) collective-permute-start(bf16[288,256]{1,0:T(8,128)(2,1)S(1)} %add_convert_fusion.2.refs_8_), channel_id=1, source_target_pairs={{0,2},{1,3},{2,4},{3,5},{4,6},{5,7},{6,0},{7,1},{8,10},{9,11},{10,... | collective-permute-start | bytes 442376 | tf_op jit(solution)/shard_map/ppermute | solution.py:419
  134.9 8.3 %collective-permute-start.20 = (bf16[2,128,384]{2,1,0:T(8,128)(2,1)S(1)}, bf16[2,128,384]{2,1,0:T(8,128)(2,1)S(1)}, u32[]{:S(2)}, u32[]{:S(2)}) collective-permute-start(bf16[2,128,384]{2,1,0:T(8,128)(2,1)S(1)} %collective-permute-done.18.refs_2_), channel_id=1, source_target_pairs={{0,8},{1,9},{2,10},{3,11},{4,12},{5,13},{6,14},{7,15},{8,0},{9,1},... | collective-permute-start | bytes 589832 | tf_op jit(solution)/shard_map/ppermute | solution.py:419
  141.4 11.3 %copy-start.39 = (f32[4,288]{1,0:T(4,128)S(1)}, f32[4,288]{1,0:T(4,128)}, u32[]{:S(2)}) copy-start(f32[4,288]{1,0:T(4,128)} %get-tuple-element.33) | copy-start | bytes 13828
  141.4 26.2 %copy-start.35 = (f32[2304]{0:T(1024)S(1)}, f32[2304]{0:T(1024)}, u32[]{:S(2)}) copy-start(f32[2304]{0:T(1024)} %param.19) | copy-start | bytes 27652
  141.4 26.8 %copy-start.38 = (f32[16]{0:T(128)S(1)}, f32[16]{0:T(128)}, u32[]{:S(2)}) copy-start(f32[16]{0:T(128)} %param.21) | copy-start | bytes 196
  141.4 8.8 %collective-permute-start.32 = (bf16[288,256]{1,0:T(8,128)(2,1)}, bf16[288,256]{1,0:T(8,128)(2,1)S(1)}, u32[]{:S(2)}, u32[]{:S(2)}) collective-permute-start(bf16[288,256]{1,0:T(8,128)(2,1)} %get-tuple-element.57), channel_id=1, source_target_pairs={{0,1},{1,0},{2,3},{3,2},{4,5},{5,4},{6,7},{7,6},{8,9},{9,8},{10,11... | collective-permute-start | bytes 442376 | tf_op jit(solution)/shard_map/ppermute | solution.py:419
  143.0 17.0 %collective-permute-start.31 = (bf16[288,256]{1,0:T(8,128)(2,1)S(1)}, bf16[288,256]{1,0:T(8,128)(2,1)S(1)}, u32[]{:S(2)}, u32[]{:S(2)}) collective-permute-start(bf16[288,256]{1,0:T(8,128)(2,1)S(1)} %add_convert_fusion.1.refs_8_), channel_id=1, source_target_pairs={{0,4},{1,5},{2,6},{3,7},{4,0},{5,1},{6,2},{7,3},{8,12},{9,13},{10,... | collective-permute-start | bytes 442376 | tf_op jit(solution)/shard_map/ppermute | solution.py:419
  149.1 53.5 %copy-start.4 = (f32[256,288]{0,1:T(8,128)S(1)}, f32[256,288]{0,1:T(8,128)}, u32[]{:S(2)}) copy-start(f32[256,288]{0,1:T(8,128)} %param.11) | copy-start | bytes 884740
  149.1 10.9 %collective-permute-start.29 = (bf16[288,256]{1,0:T(8,128)(2,1)}, bf16[288,256]{1,0:T(8,128)(2,1)S(1)}, u32[]{:S(2)}, u32[]{:S(2)}) collective-permute-start(bf16[288,256]{1,0:T(8,128)(2,1)} %get-tuple-element.56), channel_id=1, source_target_pairs={{0,1},{1,0},{2,3},{3,2},{4,5},{5,4},{6,7},{7,6},{8,9},{9,8},{10,11... | collective-permute-start | bytes 442376 | tf_op jit(solution)/shard_map/ppermute | solution.py:419
  150.3 9.8 %collective-permute-start.33 = (bf16[288,256]{1,0:T(8,128)(2,1)S(1)}, bf16[288,256]{1,0:T(8,128)(2,1)S(1)}, u32[]{:S(2)}, u32[]{:S(2)}) collective-permute-start(bf16[288,256]{1,0:T(8,128)(2,1)S(1)} %add_convert_fusion), channel_id=1, source_target_pairs={{0,6},{1,7},{2,0},{3,1},{4,2},{5,3},{6,4},{7,5},{8,14},{9,15},{10,... | collective-permute-start | bytes 442376 | tf_op jit(solution)/shard_map/ppermute | solution.py:419
  152.7 7.3 %collective-permute-start.3 = (f32[4,288]{1,0:T(4,128)S(1)}, f32[4,288]{1,0:T(4,128)S(1)}, u32[]{:S(2)}, u32[]{:S(2)}) collective-permute-start(f32[4,288]{1,0:T(4,128)S(1)} %copy-done.39), channel_id=1, source_target_pairs={{0,0},{1,1},{2,8},{3,9},{4,16},{5,17},{6,24},{7,25},{8,2},{9,3},{1... | collective-permute-start | bytes 13832 | tf_op jit(solution)/shard_map/ppermute | solution.py:419
  163.1 12.1 %all-to-all-start = ((f32[32,4,288]{2,1,0:T(4,128)}), f32[32,4,288]{2,1,0:T(4,128)S(1)}, u32[]{:S(2)}, u32[]{:S(2)}) async-start(f32[32,4,288]{2,1,0:T(4,128)} %get-tuple-element.59), calls=%async_computation | async-start | bytes 393216 | tf_op jit(solution)/shard_map/all_to_all | solution.py:498
  179.2 10.0 %all-to-all-start.1 = ((f32[32,2,16]{2,1,0:T(2,128)}), f32[32,2,16]{2,1,0:T(2,128)S(1)}, u32[]{:S(2)}, u32[]{:S(2)}) async-start(f32[32,2,16]{2,1,0:T(2,128)} %get-tuple-element.61), calls=%async_computation.1 | async-start | bytes 65536 | tf_op jit(solution)/shard_map/all_to_all | solution.py:498
  183.1 19.5 %collective-permute-start.34 = (f32[288,256]{1,0:T(8,128)}, f32[288,256]{1,0:T(8,128)S(1)}, u32[]{:S(2)}, u32[]{:S(2)}) collective-permute-start(f32[288,256]{1,0:T(8,128)} %get-tuple-element.58), channel_id=1, source_target_pairs={{0,0},{1,1},{2,8},{3,9},{4,16},{5,17},{6,24},{7,25},{8,2},{9,3},{1... | collective-permute-start | bytes 884744 | tf_op jit(solution)/shard_map/ppermute | solution.py:419
  (29 other events, 48.3 us)

commit v5 on v3

v5 whole, which is shorter than its diff:
```python
import math

import jax
import jax.numpy as jnp
from jax import lax
from jax.experimental import pallas as pl
from jax.experimental.pallas import tpu as pltpu
from jax.sharding import PartitionSpec as P

WIDTH = 2304
META = 16
LANES = 128
branch_scale = 1.4 / math.sqrt(40.0)
epsilon = 1e-05
f32, bf16 = jnp.float32, jnp.bfloat16

VMEM = pl.BlockSpec(memory_space=pltpu.VMEM)
SMEM = pl.BlockSpec(memory_space=pltpu.SMEM)
ANY = pl.BlockSpec(memory_space=pl.ANY)


def up_to(n, step=LANES):
    return -(-n // step) * step


def params(mib=16):
    return pltpu.CompilerParams(vmem_limit_bytes=mib * 2**20)


def cost(flops, bytes_accessed):
    return pl.CostEstimate(flops=flops, bytes_accessed=bytes_accessed, transcendentals=0)


def shape(dims, dtype):
    return jax.ShapeDtypeStruct(dims, dtype)


def prep_kernel(tallies, x, gain, routes, out, ends):
    block, tokens = x.shape
    v = x[...]
    wide = up_to(block)
    g = jnp.concatenate([gain[...], jnp.zeros((1, wide - block), f32)], axis=1)
    g = jnp.broadcast_to(g, (LANES, wide)).T[0:block, 0:1]
    out[0:block] = (v * g).astype(bf16)
    sq = jnp.sum(v * v, axis=0, keepdims=True)
    hi = sq.astype(bf16).astype(f32)
    mid = (sq - hi).astype(bf16).astype(f32)
    here = lax.broadcasted_iota(jnp.int32, (1, tokens), 1)
    mark, end = jnp.zeros((1, tokens), f32), jnp.int32(-1)
    for q in range(ends.shape[0]):
        end = end + tallies[0, q]
        mark = jnp.where(here == end, q + 1.0, mark)
    rows = [routes[...].astype(f32), hi, mid, sq - hi - mid, mark]
    rows.append(jnp.zeros((META - 6, tokens), f32))
    out[block:] = jnp.concatenate(rows, axis=0).astype(bf16)
    ends[...] = columns_at(mark, v)[0 : ends.shape[0]]


def columns_at(mark, v):
    row = lax.broadcasted_iota(jnp.int32, (8, mark.shape[1]), 0)
    pick = jnp.where(mark == (row + 1).astype(f32), 1.0, 0.0)
    return lax.dot_general(
        pick, v, (((1,), (1,)), ((), ())), precision=lax.Precision.HIGHEST, preferred_element_type=f32
    )


def whole_spec(v):
    return pl.BlockSpec(v.shape, lambda *_: (0,) * len(v.shape))


def prep_call(x, gain, routes, tallies):
    block, tokens = x.shape
    reqs = tallies.shape[1]
    outs = [shape((block + META, tokens), bf16), shape((reqs, block), f32)]
    return pl.pallas_call(
        prep_kernel,
        grid=(1,),
        in_specs=[SMEM] + [whole_spec(v) for v in (x, gain, routes)],
        out_specs=[whole_spec(v) for v in outs],
        out_shape=outs,
        compiler_params=params(),
        cost_estimate=cost(4 * tokens * block, 6 * tokens * block),
        name="prep",
    )(tallies, x, gain, routes)


def join_call(blocks):
    rows, tokens = blocks[0].shape

    def join_kernel(*refs):
        for i, ref in enumerate(refs[:-1]):
            refs[-1][i * rows : (i + 1) * rows] = ref[...]

    return pl.pallas_call(
        join_kernel,
        in_specs=[VMEM] * len(blocks),
        out_specs=VMEM,
        out_shape=shape((len(blocks) * rows, tokens), bf16),
        compiler_params=params(),
        cost_estimate=cost(0, 4 * len(blocks) * rows * tokens),
        name="join",
    )(*blocks)


EXTRA = 5


def spread_lanes(v, base):
    lane = lax.broadcasted_iota(jnp.int32, v.shape, 1)
    hi = v.astype(bf16).astype(f32)
    return jnp.where(lane < base, v, jnp.where(lane < base + EXTRA, hi, v - hi)).astype(bf16)


def joined_lanes(v, base):
    lane = lax.broadcasted_iota(jnp.int32, v.shape, 1)
    left, right = pltpu.roll(v, LANES - EXTRA, 1), pltpu.roll(v, EXTRA, 1)
    return v + jnp.where(lane < base, 0.0, jnp.where(lane < base + EXTRA, left, right))


def slot_columns(core, cols):
    first, second = cols[:, 0:1].astype(f32), cols[:, 1:2].astype(f32)
    zero = core == 0
    return jnp.where(zero, first, second), jnp.where(zero, second, first)


def partial_kernel(sides, held, scal, *refs):
    feeds, (wr, wg, wu), (own, give, cols, xs, xt, acc, extra) = refs[:held], refs[held : held + 3], refs[-7:]
    e = pl.program_id(0)
    core, side = scal[0], scal[1]
    depth, hidden = wg.shape[1:]
    deep, half = up_to(depth), up_to(hidden)
    base = hidden % LANES
    tokens = feeds[0].shape[1]
    block = depth // sides
    last = slice(2 * half - LANES, 2 * half)

    @pl.when(e == 0)
    def _():
        xs[depth:] = jnp.zeros((deep + LANES - depth, xs.shape[1]), bf16)
        for n, ref in enumerate(feeds):
            to = slice(n * tokens, (n + 1) * tokens)
            for i in range(sides):
                at = i * (block + META)
                xs[pl.ds(pl.multiple_of((side ^ i) * block, 16), block), to] = ref[at : at + block]
                xs[deep + i * META : deep + (i + 1) * META, to] = ref[at + block : at + block + META]
        xt[...] = xs[...].T
        more = xt[:, deep:]
        cols[...] = more
        more = more.astype(f32)
        sq = jnp.zeros((more.shape[0], 1), f32)
        for i in range(sides):
            for term in (4, 3, 2):
                sq = sq + more[:, i * META + term : i * META + term + 1]
        router = lax.dot_general(
            xt[:, 0:depth], wr[...], (((1,), (1,)), ((), ())), preferred_element_type=f32
        )
        lane = lax.broadcasted_iota(jnp.int32, router.shape, 1)
        extra[...] = router + jnp.where((lane == base) | (lane == base + EXTRA), sq, 0.0)
        for ref in (own, acc):
            ref[:, half - LANES : half] = jnp.zeros((xt.shape[0], LANES), f32)
            ref[:, last] = jnp.zeros((xt.shape[0], LANES), f32)

    mine, other = slot_columns(core, xt[:, deep : deep + LANES])
    ef = e.astype(f32)
    take = [(v == ef) | (e == 0) for v in (mine, other)]
    for which, w in enumerate((wg, wu)):
        for at in range(0, hidden, 256):
            end = min(hidden, at + 256)
            d = jnp.dot(xt[:, 0:depth], w[0, :, at:end], preferred_element_type=f32)
            to = slice(which * half + at, which * half + end)
            for ref, pick in ((own, take[0]), (acc, take[1])):
                ref[:, to] = jnp.where(pick, d, ref[:, to])

    @pl.when(e == pl.num_programs(0) - 1)
    def _():
        lane = lax.broadcasted_iota(jnp.int32, extra.shape, 1)
        more = extra[...]
        own[:, last] = jnp.where(lane < base, own[:, last], more)
        give[:, 0 : last.start] = acc[:, 0 : last.start].astype(bf16)
        give[:, last] = spread_lanes(jnp.where(lane < base, acc[:, last], more), base)


def partial_call(scal, sides, feeds, wr, wg, wu, deps):
    experts, depth, hidden = wg.shape
    tokens = feeds[0].shape[1] * len(feeds)
    deep, wide = up_to(depth), 2 * up_to(hidden)
    part = pl.BlockSpec((1, depth, hidden), lambda n: (n, 0, 0))
    outs = [shape((tokens, wide), f32), shape((tokens, wide), bf16), shape((tokens, LANES), bf16)]
    return pl.pallas_call(
        lambda *refs: partial_kernel(sides, len(feeds), *refs),
        grid=(experts,),
        in_specs=[SMEM] + [whole_spec(v) for v in feeds] + [whole_spec(wr), part, part] + [ANY] * len(deps),
        out_specs=[whole_spec(v) for v in outs],
        out_shape=outs,
        scratch_shapes=[
            pltpu.VMEM((deep + LANES, tokens), bf16),
            pltpu.VMEM((tokens, deep + LANES), bf16),
            pltpu.VMEM((tokens, wide), f32),
            pltpu.VMEM((tokens, LANES), f32),
        ],
        compiler_params=params(32),
        cost_estimate=cost(
            4 * experts * depth * hidden * tokens, 4 * experts * depth * hidden + 6 * tokens * wide
        ),
        name="gate_up_partial",
    )(scal, *feeds, wr, wg, wu, *deps)


def sum_kernel(base, scal, own, recv, *refs):
    keep, send = refs[-2:]
    y = scal[2]
    th, wide = keep.shape
    main = wide - LANES
    for to, first in ((keep, y), (send, 1 - y)):
        rows = pl.ds(pl.multiple_of(first * th, th), th)
        to[:, 0:main] = (own[rows, 0:main] + recv[rows, 0:main].astype(f32)).astype(to.dtype)
        v = own[rows, main:] + joined_lanes(recv[rows, main:].astype(f32), base)
        to[:, main:] = v if to is keep else spread_lanes(v, base)


def sum_call(scal, base, own, recv, deps):
    tokens, wide = own.shape
    return pl.pallas_call(
        lambda *refs: sum_kernel(base, *refs),
        in_specs=[SMEM, VMEM, VMEM] + [ANY] * len(deps),
        out_specs=[VMEM, VMEM],
        out_shape=[shape((tokens // 2, wide), f32), shape((tokens // 2, wide), bf16)],
        compiler_params=params(),
        cost_estimate=cost(tokens * wide, 9 * tokens * wide),
        name="core_sum",
    )(scal, own, recv, *deps)


def act_kernel(base, scal, keep, recv, cols, *refs):
    act = refs[-1]
    core, y = scal[0], scal[2]
    th, half = act.shape
    main = 2 * half - LANES
    m = keep[:, main:] + joined_lanes(recv[:, main:].astype(f32), base)
    mine, other = slot_columns(core, cols[pl.ds(pl.multiple_of(y * th, th), th)])
    scale = lax.rsqrt(m[:, base : base + 1] / WIDTH + epsilon)
    la = lb = jnp.zeros_like(scale)
    for e in range(4):
        logit = m[:, base + 1 + e : base + 2 + e] * scale
        la = jnp.where(mine == e, logit, la)
        lb = jnp.where(other == e, logit, lb)
    mix = scale / (1.0 + jnp.exp(lb - la))
    g = (keep[:, 0:half] + recv[:, 0:half].astype(f32)) * scale
    u = (keep[:, half:] + recv[:, half:].astype(f32)) * mix
    act[...] = (g / (1.0 + jnp.exp(-g)) * u).astype(bf16)


def act_call(scal, base, keep, recv, cols, deps):
    th, wide = keep.shape
    return pl.pallas_call(
        lambda *refs: act_kernel(base, *refs),
        in_specs=[SMEM] + [VMEM] * 3 + [ANY] * len(deps),
        out_specs=VMEM,
        out_shape=shape((th, wide // 2), bf16),
        compiler_params=params(),
        cost_estimate=cost(6 * th * wide, 7 * th * wide),
        name="act",
    )(scal, keep, recv, cols, *deps)


def down_kernel(sides, scal, a, a_y, b, b_y, cols, wd, *refs):
    outs = refs[-sides - 2 : -2]
    whole, acc = refs[-2:]
    e = pl.program_id(0)
    core, side, y = scal[0], scal[1], scal[2]
    th = a.shape[0]
    width, hidden = wd.shape[1:]
    block = width // sides

    @pl.when(e == 0)
    def _():
        for k, near, far in ((0, a, a_y), (1, b, b_y)):
            whole[k, pl.ds(pl.multiple_of(y * th, th), th)] = near[...]
            whole[k, pl.ds(pl.multiple_of((1 - y) * th, th), th)] = far[...]

    ef = e.astype(f32)
    masks = [jnp.where(v == ef, 1.0, 0.0).astype(bf16) for v in slot_columns(core, cols[...])]
    rows = whole[0, :, 0:hidden] * masks[0] + whole[1, :, 0:hidden] * masks[1]
    d = lax.dot_general(wd[0], rows, (((1,), (1,)), ((), ())), preferred_element_type=f32)

    @pl.when(e == 0)
    def _():
        acc[...] = d

    @pl.when(e > 0)
    def _():
        acc[...] += d

    @pl.when(e == pl.num_programs(0) - 1)
    def _():
        for i in range(sides):
            rows = pl.ds(pl.multiple_of((side ^ i) * block, 16), block)
            outs[i][...] = acc[rows].astype(bf16)


def down_call(scal, sides, pieces, cols, wd, deps):
    experts, width, hidden = wd.shape
    tokens = cols.shape[0]
    outs = [shape((width // sides, tokens), bf16)] * sides
    return pl.pallas_call(
        lambda *refs: down_kernel(sides, *refs),
        grid=(experts,),
        in_specs=[SMEM]
        + [whole_spec(v) for v in pieces]
        + [whole_spec(cols), pl.BlockSpec((1, width, hidden), lambda n: (n, 0, 0))]
        + [ANY] * len(deps),
        out_specs=[whole_spec(v) for v in outs],
        out_shape=outs,
        scratch_shapes=[
            pltpu.VMEM((2, tokens, pieces[0].shape[1]), bf16),
            pltpu.VMEM((width, tokens), f32),
        ],
        compiler_params=params(20),
        cost_estimate=cost(
            2 * experts * width * hidden * tokens, 2 * experts * width * hidden + 2 * width * tokens
        ),
        name="down",
    )(scal, *pieces, cols, wd, *deps)


def total_kernel(meta, stream, *refs):
    parts, (total, message) = refs[:-2], refs[-2:]
    v = parts[0][...].astype(f32)
    for ref in parts[1:]:
        v = v + ref[...].astype(f32)
    total[...] = v
    reqs = stream.shape[0]
    ends = columns_at(meta[5:6].astype(f32), v)
    ends = stream[...] + branch_scale * ends[0:reqs]
    message[...] = jnp.broadcast_to(ends[None], message.shape)


def total_call(feed, stream, parts, block, count):
    tokens = feed.shape[1]
    full = lambda v: pl.BlockSpec(v.shape, lambda n: (0,) * len(v.shape))
    outs = [shape((block, tokens), f32), shape((count, *stream.shape), f32)]
    return pl.pallas_call(
        total_kernel,
        grid=(1,),
        in_specs=[pl.BlockSpec((META, tokens), lambda n: (block // META, 0)), full(stream)]
        + [full(v) for v in parts],
        out_specs=[full(v) for v in outs],
        out_shape=outs,
        compiler_params=params(),
        cost_estimate=cost(16 * block * tokens, 14 * block * tokens),
        name="branch_total",
    )(feed, stream, *parts)


def head_kernel(order, got, gain, words, softness, logits, message, wide):
    blocks, block = gain.shape
    rows, columns = logits.shape
    ends, squares = [], 0.0
    for b in range(blocks):
        v = jnp.concatenate([got[i] for i in order[b]], axis=0)
        squares = squares + jnp.sum(v * v, axis=1, keepdims=True)
        ends.append(v)
    scale = lax.rsqrt(squares / WIDTH + epsilon)
    total = jnp.zeros((rows, columns), f32)
    for b in range(blocks):
        feed = (ends[b] * scale * gain[b : b + 1]).astype(bf16)
        total += jnp.dot(feed, words[b * block : (b + 1) * block], preferred_element_type=f32)
    total = total / (WIDTH / 256.0 * softness[...])
    logits[...] = total
    top = jnp.max(total, axis=1, keepdims=True)
    mass = jnp.sum(jnp.exp(total - top), axis=1, keepdims=True)
    wide[...] = jnp.zeros_like(wide)
    lane = lax.broadcasted_iota(jnp.int32, (rows, LANES), 1)
    wide[0:rows] = jnp.where(lane == 0, top, jnp.where(lane == 1, mass, 0.0))
    turned = wide[...].T
    message[...] = jnp.broadcast_to(turned[None, 0:2, 0:rows], message.shape)


def head_call(order, got, gain, words, softness):
    rows, columns = softness.shape[0], words.shape[1]
    return pl.pallas_call(
        lambda *refs: head_kernel(order, *refs),
        in_specs=[VMEM] * 4,
        out_specs=[VMEM, VMEM],
        out_shape=[shape((rows, columns), f32), shape((got.shape[0], 2, rows), f32)],
        scratch_shapes=[pltpu.VMEM((LANES, LANES), f32)],
        compiler_params=params(),
        cost_estimate=cost(2 * rows * WIDTH * columns, 2 * WIDTH * columns),
        name="head",
    )(got, gain, words, softness)


def body(
    skip_stream_arriving,
    chosen_specialists,
    sequence_piece_tallies,
    premix_rmsnorm_gain,
    dispatcher_weights,
    specialist_switch_weights,
    specialist_expand_weights,
    specialist_contract_weights,
    terminal_rmsnorm_gain,
    lexicon_projector_weights,
    softness_per_sequence,
):
    tokens, block = skip_stream_arriving.shape
    dp, mp = lax.axis_size("dp"), lax.axis_size("mp")
    count = dp * mp
    parts = 4
    spread, sides = dp // parts, mp // parts
    assert dp == parts * spread and mp == parts * sides and sides & (sides - 1) == 0
    part = lax.axis_index("dp") // spread
    y, core = part // 2, part % 2
    side = lax.axis_index("mp") % sides

    def send(value, to):
        pairs = []
        for q in range(parts):
            for r in range(spread):
                for z in range(parts):
                    for x in range(sides):
                        q2, z2, x2 = to(q, z, x)
                        source = (q * spread + r) * mp + z * sides + x
                        pairs.append((source, (q2 * spread + r) * mp + z2 * sides + x2))
        return lax.ppermute(value, ("dp", "mp"), pairs)

    other_core = lambda q, z, x: (q ^ 1, z, x)
    other_y = lambda q, z, x: (q ^ 2, z, x)
    home = lambda q, z, x: (z, q, x)

    scal = jnp.stack([core, side, y]).astype(jnp.int32)
    sent, stream = prep_call(
        skip_stream_arriving.T, premix_rmsnorm_gain[None], chosen_specialists.T, sequence_piece_tallies
    )
    wg, wu, wd = specialist_switch_weights, specialist_expand_weights, specialist_contract_weights
    if spread > 1:
        runs = [[q * spread + r for r in range(spread)] for q in range(parts)]
        wg = lax.all_gather(wg, "dp", axis=1, tiled=True, axis_index_groups=runs)
        wu = lax.all_gather(wu, "dp", axis=1, tiled=True, axis_index_groups=runs)
        wd = lax.all_gather(wd, "dp", axis=2, tiled=True, axis_index_groups=runs)
    wd = jnp.swapaxes(wd, 1, 2)
    depth, hidden = wg.shape[1:]
    base = hidden % LANES
    wr = lax.dynamic_slice_in_dim(dispatcher_weights.T, part * depth, depth, axis=1)
    room = lambda at: jnp.pad(wr, ((at, LANES - at - wr.shape[0]), (0, 0)))
    wr = room(base + 1) + room(base + 1 + EXTRA)

    chunks = ((1,), (2, 3), (0,))
    first = [send(sent, lambda q, z, x, i=i: (z, (q - 1) % parts, x ^ i)) for i in range(sides)]
    pair = join_call(first)
    feeds = {1: pair}
    for group in (2, 3, 0):
        feeds[group] = send(pair, lambda q, z, x, group=group: (q, (z - group + 1) % parts, x))
    stream = send(stream, home)
    partial, kept, pieces, shares = {}, {}, {}, {}

    def do_partial(s, *deps):
        own, give, cols = partial_call(scal, sides, [feeds[g] for g in chunks[s]], wr, wg, wu, deps)
        partial[s] = (own, send(give, other_core), cols)
        return own

    def do_sum(s, *deps):
        own, recv, _ = partial[s]
        keep, give = sum_call(scal, base, own, recv, deps)
        kept[s] = (keep, send(give, other_y))
        return keep

    def do_act(s, *deps):
        a = act_call(scal, base, *kept[s], partial[s][2], deps)
        a_y = send(a, other_y)
        pieces[s] = (a, a_y, send(a, other_core), send(a_y, other_core))
        return a

    def do_down(s, *deps):
        outs = down_call(scal, sides, pieces[s], partial[s][2], wd, deps)
        got = [outs[0]] + [send(outs[i], lambda q, z, x, i=i: (q, z, x ^ i)) for i in range(1, sides)]
        for n, group in enumerate(chunks[s]):
            to = slice(n * tokens, (n + 1) * tokens)
            if group == 0:
                shares[0] = [v[:, to] for v in got]
            else:
                share = sum(v[:, to].astype(f32) for v in got).astype(bf16)
                back = lambda q, z, x, group=group: (q, (z + group) % parts, x)
                shares[group] = [send(share, back)]
        return outs[0]

    p0 = do_partial(0)
    s0 = do_sum(0)
    p1 = do_partial(1, s0)
    s1 = do_sum(1)
    a0 = do_act(0, s1)
    p2 = do_partial(2, a0)
    s2 = do_sum(2)
    d0 = do_down(0, s2)
    a1 = do_act(1, d0)
    a2 = do_act(2, a1)
    d1 = do_down(1, a2)
    do_down(2, d1)
    mine = [v for group in range(parts) for v in shares[group]]
    total, message = total_call(feeds[0], stream, mine, block, count)

    everyone = lambda v: lax.all_to_all(v, ("dp", "mp"), 0, 0, tiled=True)
    got = everyone(message)
    branch = send(total, home)
    order = [
        [
            (q * spread + r) * mp + z * sides + x
            for z in range(parts)
            for r in range(spread)
        ]
        for q in range(parts)
        for x in range(sides)
    ]
    logits, pairs = head_call(
        order,
        got,
        terminal_rmsnorm_gain.reshape(mp, block),
        lexicon_projector_weights,
        softness_per_sequence[:, None],
    )
    pairs = everyone(pairs)
    new_hidden = skip_stream_arriving + branch_scale * branch.T
    largest = jnp.max(pairs[:, 0], axis=0)
    mass = jnp.sum(pairs[:, 1] * jnp.exp(pairs[:, 0] - largest), axis=0)
    logprobs = logits - largest[:, None] - jnp.log(mass)[:, None]
    return (new_hidden, logprobs)


def solution(mesh):
    return jax.shard_map(
        body,
        mesh=mesh,
        in_specs=(
            P("dp", "mp"),
            P("dp", None),
            P("dp", None),
            P("mp"),
            P(),
            P(None, "dp", "mp"),
            P(None, "dp", "mp"),
            P(None, "mp", "dp"),
            P(),
            P(None, ("dp", "mp")),
            P(),
        ),
        out_specs=(P("dp", "mp"), P(None, ("dp", "mp"))),
        check_vma=False,
    )
```

time: 177 us -> 201 us (1.14)
  waiting for transfers between devices: 71.3 us -> 107 us
  Pallas kernels: 48.2 us -> 40.2 us
  local copies, waits for them, and re-layouts: 10.1 us -> 7.29 us
    ppermute x35 -> x28, waiting for transfers between devices: 62.1 us -> 97.3 us  [send(): return lax.ppermute(value, ('dp', 'mp'), pairs)]
    pallas_call x10, Pallas kernels: 32.8 us -> 26 us  [the longest x3 18.1 us: partial_call(): pl.pallas_call(lambda *refs: partial_kernel(sides, len(feeds), *refs), gr...]
    ppermute x35 -> x28, starting transfers between devices: 35.1 us -> 37.3 us  [send(): return lax.ppermute(value, ('dp', 'mp'), pairs)]
    pallas_call x4 -> x3, Pallas kernels: 12.1 us -> 11.7 us  [down_call(): pl.pallas_call(lambda *refs: down_kernel(sides, *refs), grid=(experts,),...]
  transfers between devices with their start and end apart: 37 -> 30, of which waited for: 15 -> 17; matrix products, arithmetic and copies ran while one was open for 1% -> 1% of each run, Pallas kernels for 24% -> 8%
where the time goes in v5:
time: 201 us
  waiting for transfers between devices  107 us (53%)
  starting transfers between devices  44 us (22%)
  Pallas kernels  40.2 us (20%)
  local copies, waits for them, and re-layouts  7.29 us (4%)
    ppermute x28, waiting for transfers between devices, send(): return lax.ppermute(value, ('dp', 'mp'), pairs)  97.3 us
    ppermute x28, starting transfers between devices, send(): return lax.ppermute(value, ('dp', 'mp'), pairs)  37.3 us
    pallas_call x3, Pallas kernels, partial_call(): pl.pallas_call(lambda *refs: partial_kernel(sides, len(feeds), *refs), gr...  18.1 us
    pallas_call x3, Pallas kernels, down_call(): pl.pallas_call(lambda *refs: down_kernel(sides, *refs), grid=(experts,),...  11.7 us
    all_to_all x2, waiting for transfers between devices, body(): everyone = lambda v: lax.all_to_all(v, ('dp', 'mp'), 0, 0, tiled=True)  9.27 us
    all_to_all x2, starting transfers between devices, body(): everyone = lambda v: lax.all_to_all(v, ('dp', 'mp'), 0, 0, tiled=True)  6.69 us
    unnamed x26, local copies, waits for them, and re-layouts  6.34 us
    pallas_call x3, Pallas kernels, act_call(): pl.pallas_call(lambda *refs: act_kernel(base, *refs), in_specs=[SMEM] + [...  4.2 us
  transfers between devices with their start and end apart: 30, of which 17 were waited for; matrix products, arithmetic and copies ran while one was open for 1% of the time, Pallas kernels for 8%

profile of v5, /device:TPU:4, one launch (start us, length us, event | category | flops | bytes accessed | tf_op | source)
XLA Modules:
  0.0 200.8 jit_solution(5456191210721205056)
XLA Ops:
  1.3 1.0 copy-done.7
  3.6 0.9 prep.1
  4.5 1.5 collective-permute-start
  6.0 3.0 %collective-permute-start.1 = (bf16[304,256]{1,0:T(8,128)(2,1)S(1)}, bf16[304,256]{1,0:T(8,128)(2,1)S(1)}, u32[]{:S(2)}, u32[]{:S(2)}) collective-permute-start(bf16[304,256]{1,0:T(8,128)(2,1)S(1)} %get-tuple-element.29), channel_id=1, source_target_pairs={{0,7},{1,6},{2,15},{3,14},{4,23},{5,22},{6,31},{7,30},{8,1},{9,0},... | collective-permute-start | bytes 466952 | tf_op jit(solution)/shard_map/ppermute | solution.py:425
  9.2 3.6 %collective-permute-done.refs_0_ = bf16[304,256]{1,0:T(8,128)(2,1)S(1)} collective-permute-done((bf16[304,256]{1,0:T(8,128)(2,1)S(1)}, bf16[304,256]{1,0:T(8,128)(2,1)S(1)}, u32[]{:S(2)}, u32[]{:S(2)}) %collective-permute-start) | collective-permute-done | bytes 155680 | tf_op jit(solution)/shard_map/ppermute | solution.py:425
  12.7 4.3 %collective-permute-done.1.refs_1_ = bf16[304,256]{1,0:T(8,128)(2,1)S(1)} collective-permute-done((bf16[304,256]{1,0:T(8,128)(2,1)S(1)}, bf16[304,256]{1,0:T(8,128)(2,1)S(1)}, u32[]{:S(2)}, u32[]{:S(2)}) %collective-permute-start.1) | collective-permute-done | bytes 155680 | tf_op jit(solution)/shard_map/ppermute | solution.py:425
  17.0 2.0 copy-done.2
  19.0 2.0 copy-done.4
  21.0 4.8 %gate_up_partial.3 = (f32[256,1536]{1,0:T(8,128)S(1)}, bf16[256,1536]{1,0:T(8,128)(2,1)S(1)}, bf16[256,128]{1,0:T(8,128)(2,1)S(1)}) custom-call(s32[3]{0:T(128)S(1)} %pad_add_fusion.1.refs_0_, bf16[608,256]{1,0:T(8,128)(2,1)S(1)} %join.1.refs_1_, bf16[128,576]{1,0:T(8,128)(2,1)S(1)} %pad_add_fusion.refs_2_.refs_3_, bf16[4,576,720]{2,1,0:T(8,128)(2,1)S(1)} %copy-done.2, ...), custom_call_target="tpu_custom_call" | custom-call | flops 1698693120 | bytes 8994816 | tf_op jit(solution)/shard_map/gate_up_partial/pallas_call | solution.py:189
  26.0 5.9 %collective-permute-start.6 = (bf16[608,256]{1,0:T(8,128)(2,1)S(1)}, bf16[608,256]{1,0:T(8,128)(2,1)S(1)}, u32[]{:S(2)}, u32[]{:S(2)}) collective-permute-start(bf16[608,256]{1,0:T(8,128)(2,1)S(1)} %join.1.refs_1_), channel_id=1, source_target_pairs={{0,6},{1,7},{2,0},{3,1},{4,2},{5,3},{6,4},{7,5},{8,14},{9,15},{10,... | collective-permute-start | bytes 933896 | tf_op jit(solution)/shard_map/ppermute | solution.py:425
  32.8 6.9 %collective-permute-done.6.refs_1_ = bf16[608,256]{1,0:T(8,128)(2,1)S(1)} collective-permute-done((bf16[608,256]{1,0:T(8,128)(2,1)S(1)}, bf16[608,256]{1,0:T(8,128)(2,1)S(1)}, u32[]{:S(2)}, u32[]{:S(2)}) %collective-permute-start.6) | collective-permute-done | bytes 311328 | tf_op jit(solution)/shard_map/ppermute | solution.py:425
  39.6 10.3 %collective-permute-done.7.refs_2_ = bf16[608,256]{1,0:T(8,128)(2,1)S(1)} collective-permute-done((bf16[608,256]{1,0:T(8,128)(2,1)S(1)}, bf16[608,256]{1,0:T(8,128)(2,1)S(1)}, u32[]{:S(2)}, u32[]{:S(2)}) %collective-permute-start.7) | collective-permute-done | bytes 311328 | tf_op jit(solution)/shard_map/ppermute | solution.py:425
  50.0 8.4 %gate_up_partial.4 = (f32[512,1536]{1,0:T(8,128)S(1)}, bf16[512,1536]{1,0:T(8,128)(2,1)S(1)}, bf16[512,128]{1,0:T(8,128)(2,1)S(1)}) custom-call(s32[3]{0:T(128)S(1)} %pad_add_fusion.1.refs_0_, bf16[608,256]{1,0:T(8,128)(2,1)S(1)} %collective-permute-done.6.refs_1_, bf16[608,256]{1,0:T(8,128)(2,1)S(1)} %collective-permute-done.7.refs_2_, ...), custom_call_target="tpu_custom_call" | custom-call | flops 3397386240 | bytes 11354112 | tf_op jit(solution)/shard_map/gate_up_partial/pallas_call | solution.py:189
  58.4 1.1 collective-permute-start.5
  59.5 2.2 %collective-permute-start.2 = (bf16[608,256]{1,0:T(8,128)(2,1)S(1)}, bf16[608,256]{1,0:T(8,128)(2,1)S(1)}, u32[]{:S(2)}, u32[]{:S(2)}) collective-permute-start(bf16[608,256]{1,0:T(8,128)(2,1)S(1)} %join.1.refs_1_), channel_id=1, source_target_pairs={{0,2},{1,3},{2,4},{3,5},{4,6},{5,7},{6,0},{7,1},{8,10},{9,11},{10,... | collective-permute-start | bytes 933896 | tf_op jit(solution)/shard_map/ppermute | solution.py:425
  61.8 1.2 core_sum.4
  63.0 7.0 %collective-permute-done.5.refs_2_ = bf16[128,1536]{1,0:T(8,128)(2,1)S(1)} collective-permute-done((bf16[128,1536]{1,0:T(8,128)(2,1)S(1)}, bf16[128,1536]{1,0:T(8,128)(2,1)S(1)}, u32[]{:S(2)}, u32[]{:S(2)}) %collective-permute-start.5) | collective-permute-done | bytes 393248 | tf_op jit(solution)/shard_map/ppermute | solution.py:425
  70.0 1.2 act.3.refs_5_.refs_1_
  71.2 1.2 collective-permute-done.2.refs_1_.meta
  72.4 4.8 %gate_up_partial.5 = (f32[256,1536]{1,0:T(8,128)S(1)}, bf16[256,1536]{1,0:T(8,128)(2,1)S(1)}, bf16[256,128]{1,0:T(8,128)(2,1)S(1)}) custom-call(s32[3]{0:T(128)S(1)} %pad_add_fusion.1.refs_0_, bf16[608,256]{1,0:T(8,128)(2,1)S(1)} %collective-permute-done.2.refs_1_.meta, bf16[128,576]{1,0:T(8,128)(2,1)S(1)} %pad_add_fusion.refs_2_.refs_3_, ...), custom_call_target="tpu_custom_call" | custom-call | flops 1698693120 | bytes 8994816 | tf_op jit(solution)/shard_map/gate_up_partial/pallas_call | solution.py:189
  77.3 1.8 collective-permute-start.11
  79.4 22.1 %collective-permute-done.12.refs_2_ = bf16[128,768]{1,0:T(8,128)(2,1)S(1)} collective-permute-done((bf16[128,768]{1,0:T(8,128)(2,1)S(1)}, bf16[128,768]{1,0:T(8,128)(2,1)S(1)}, u32[]{:S(2)}, u32[]{:S(2)}) %collective-permute-start.12) | collective-permute-done | bytes 196640 | tf_op jit(solution)/shard_map/ppermute | solution.py:425
  101.5 0.9 core_sum.5
  102.9 3.5 %down.3 = (bf16[288,256]{1,0:T(8,128)(2,1)S(1)}, bf16[288,256]{1,0:T(8,128)(2,1)S(1)}) custom-call(s32[3]{0:T(128)S(1)} %pad_add_fusion.1.refs_0_, bf16[128,768]{1,0:T(8,128)(2,1)S(1)} %act.3.refs_5_.refs_1_, bf16[128,768]{1,0:T(8,128)(2,1)S(1)} %collective-permute-done.12.refs_2_, bf16[128,768]{1,0:T(8,128)(2,1)S(1)} %collective-permute-done.13.refs_3_, ...), custom_call_target="tpu_custom_call" | custom-call | flops 849346560 | bytes 3612672 | tf_op jit(solution)/shard_map/down/pallas_call | solution.py:305
  106.4 1.7 act.4.refs_4_.refs_1_
  108.1 1.8 collective-permute-start.18
  110.2 9.9 %collective-permute-done.18.refs_2_ = bf16[256,768]{1,0:T(8,128)(2,1)S(1)} collective-permute-done((bf16[256,768]{1,0:T(8,128)(2,1)S(1)}, bf16[256,768]{1,0:T(8,128)(2,1)S(1)}, u32[]{:S(2)}, u32[]{:S(2)}) %collective-permute-start.18) | collective-permute-done | bytes 393248 | tf_op jit(solution)/shard_map/ppermute | solution.py:425
  120.1 7.6 %collective-permute-done.10.refs_2_ = bf16[128,1536]{1,0:T(8,128)(2,1)S(1)} collective-permute-done((bf16[128,1536]{1,0:T(8,128)(2,1)S(1)}, bf16[128,1536]{1,0:T(8,128)(2,1)S(1)}, u32[]{:S(2)}, u32[]{:S(2)}) %collective-permute-start.10) | collective-permute-done | bytes 393248 | tf_op jit(solution)/shard_map/ppermute | solution.py:425
  127.8 1.2 act.5.refs_7_.refs_1_
  129.0 1.8 collective-permute-start.15
  131.4 3.8 %collective-permute-done.15.refs_2_ = bf16[128,768]{1,0:T(8,128)(2,1)S(1)} collective-permute-done((bf16[128,768]{1,0:T(8,128)(2,1)S(1)}, bf16[128,768]{1,0:T(8,128)(2,1)S(1)}, u32[]{:S(2)}, u32[]{:S(2)}) %collective-permute-start.15) | collective-permute-done | bytes 196640 | tf_op jit(solution)/shard_map/ppermute | solution.py:425
  135.2 4.8 %down.4 = (bf16[288,512]{1,0:T(8,128)(2,1)S(1)}, bf16[288,512]{1,0:T(8,128)(2,1)S(1)}) custom-call(s32[3]{0:T(128)S(1)} %pad_add_fusion.1.refs_0_, bf16[256,768]{1,0:T(8,128)(2,1)S(1)} %act.4.refs_4_.refs_1_, bf16[256,768]{1,0:T(8,128)(2,1)S(1)} %collective-permute-done.18.refs_2_, bf16[256,768]{1,0:T(8,128)(2,1)S(1)} %collective-permute-done.19.refs_3_, ...), custom_call_target="tpu_custom_call" | custom-call | flops 1698693120 | bytes 3907584 | tf_op jit(solution)/shard_map/down/pallas_call | solution.py:305
  140.7 2.0 collective-permute-start.23
  142.7 3.5 %down.5 = (bf16[288,256]{1,0:T(8,128)(2,1)S(1)}, bf16[288,256]{1,0:T(8,128)(2,1)S(1)}) custom-call(s32[3]{0:T(128)S(1)} %pad_add_fusion.1.refs_0_, bf16[128,768]{1,0:T(8,128)(2,1)S(1)} %act.5.refs_7_.refs_1_, bf16[128,768]{1,0:T(8,128)(2,1)S(1)} %collective-permute-done.15.refs_2_, bf16[128,768]{1,0:T(8,128)(2,1)S(1)} %collective-permute-done.16.refs_3_, ...), custom_call_target="tpu_custom_call" | custom-call | flops 849346560 | bytes 3612672 | tf_op jit(solution)/shard_map/down/pallas_call | solution.py:305
  146.2 1.5 collective-permute-start.21
  147.7 2.2 %collective-permute-done.24 = bf16[288,512]{1,0:T(8,128)(2,1)S(1)} collective-permute-done((bf16[288,512]{1,0:T(8,128)(2,1)S(1)}, bf16[288,512]{1,0:T(8,128)(2,1)S(1)}, u32[]{:S(2)}, u32[]{:S(2)}) %collective-permute-start.24) | collective-permute-done | bytes 294944 | tf_op jit(solution)/shard_map/ppermute | solution.py:425
  150.0 1.3 collective-permute-start.25
  151.3 3.6 %collective-permute-start.26 = (bf16[288,256]{1,0:T(8,128)(2,1)S(1)}, bf16[288,256]{1,0:T(8,128)(2,1)S(1)}, u32[]{:S(2)}, u32[]{:S(2)}) collective-permute-start(bf16[288,256]{1,0:T(8,128)(2,1)S(1)} %get-tuple-element.56), channel_id=1, source_target_pairs={{0,6},{1,7},{2,0},{3,1},{4,2},{5,3},{6,4},{7,5},{8,14},{9,15},{10,... | collective-permute-start | bytes 442376 | tf_op jit(solution)/shard_map/ppermute | solution.py:425
  154.9 3.6 %collective-permute-start.3 = (f32[4,288]{1,0:T(4,128)S(1)}, f32[4,288]{1,0:T(4,128)S(1)}, u32[]{:S(2)}, u32[]{:S(2)}) collective-permute-start(f32[4,288]{1,0:T(4,128)S(1)} %get-tuple-element.30), channel_id=1, source_target_pairs={{0,0},{1,1},{2,8},{3,9},{4,16},{5,17},{6,24},{7,25},{8,2},{9,3},{1... | collective-permute-start | bytes 13832 | tf_op jit(solution)/shard_map/ppermute | solution.py:425
  158.5 5.3 %collective-permute-done.3.stream = f32[4,288]{1,0:T(4,128)S(1)} collective-permute-done((f32[4,288]{1,0:T(4,128)S(1)}, f32[4,288]{1,0:T(4,128)S(1)}, u32[]{:S(2)}, u32[]{:S(2)}) %collective-permute-start.3) | collective-permute-done | bytes 4640 | tf_op jit(solution)/shard_map/ppermute | solution.py:425
  163.8 1.1 branch_total.1
  164.9 2.8 %all-to-all-start = ((f32[32,4,288]{2,1,0:T(4,128)}), f32[32,4,288]{2,1,0:T(4,128)S(1)}, u32[]{:S(2)}, u32[]{:S(2)}) async-start(f32[32,4,288]{2,1,0:T(4,128)} %get-tuple-element.53), calls=%async_computation | async-start | bytes 393216 | tf_op jit(solution)/shard_map/all_to_all | solution.py:502
  167.8 7.5 %all-to-all-done.refs_0_ = f32[32,4,288]{2,1,0:T(4,128)S(1)} async-done(((f32[32,4,288]{2,1,0:T(4,128)}), f32[32,4,288]{2,1,0:T(4,128)S(1)}, u32[]{:S(2)}, u32[]{:S(2)}) %all-to-all-start) | async-done | bytes 147488 | tf_op jit(solution)/shard_map/all_to_all | solution.py:502
  175.3 1.4 head.1
  176.8 3.9 %all-to-all-start.1 = ((f32[32,2,16]{2,1,0:T(2,128)}), f32[32,2,16]{2,1,0:T(2,128)S(1)}, u32[]{:S(2)}, u32[]{:S(2)}) async-start(f32[32,2,16]{2,1,0:T(2,128)} %get-tuple-element.55), calls=%async_computation.1 | async-start | bytes 65536 | tf_op jit(solution)/shard_map/all_to_all | solution.py:502
  180.7 4.3 %collective-permute-start.27 = (f32[288,256]{1,0:T(8,128)S(1)}, f32[288,256]{1,0:T(8,128)S(1)}, u32[]{:S(2)}, u32[]{:S(2)}) collective-permute-start(f32[288,256]{1,0:T(8,128)S(1)} %get-tuple-element.52), channel_id=1, source_target_pairs={{0,0},{1,1},{2,8},{3,9},{4,16},{5,17},{6,24},{7,25},{8,2},{9,3},{1... | collective-permute-start | bytes 884744 | tf_op jit(solution)/shard_map/ppermute | solution.py:425
  185.0 1.8 all-to-all-done.1
  187.5 12.5 %collective-permute-done.27 = f32[288,256]{1,0:T(8,128)S(1)} collective-permute-done((f32[288,256]{1,0:T(8,128)S(1)}, f32[288,256]{1,0:T(8,128)S(1)}, u32[]{:S(2)}, u32[]{:S(2)}) %collective-permute-start.27) | collective-permute-done | bytes 294944 | tf_op jit(solution)/shard_map/ppermute | solution.py:425
  (68 shorter events, 7.6 us)
Async XLA Ops:
  0.6 8.4 %copy-start = (bf16[2304,4]{0,1:T(4,128)(2,1)S(1)}, bf16[2304,4]{0,1:T(4,128)(2,1)}, u32[]{:S(2)}) copy-start(bf16[2304,4]{0,1:T(4,128)(2,1)} %param.15) | copy-start | bytes 55300
  1.3 1.0 copy-start.7
  2.3 0.7 copy-start.9
  3.0 0.7 copy-start.10
  4.5 8.2 %collective-permute-start = (bf16[304,256]{1,0:T(8,128)(2,1)S(1)}, bf16[304,256]{1,0:T(8,128)(2,1)S(1)}, u32[]{:S(2)}, u32[]{:S(2)}) collective-permute-start(bf16[304,256]{1,0:T(8,128)(2,1)S(1)} %get-tuple-element.29), channel_id=1, source_target_pairs={{0,6},{1,7},{2,14},{3,15},{4,22},{5,23},{6,30},{7,31},{8,0},{9,1},... | collective-permute-start | bytes 466952 | tf_op jit(solution)/shard_map/ppermute | solution.py:425
  6.0 11.0 %collective-permute-start.1 = (bf16[304,256]{1,0:T(8,128)(2,1)S(1)}, bf16[304,256]{1,0:T(8,128)(2,1)S(1)}, u32[]{:S(2)}, u32[]{:S(2)}) collective-permute-start(bf16[304,256]{1,0:T(8,128)(2,1)S(1)} %get-tuple-element.29), channel_id=1, source_target_pairs={{0,7},{1,6},{2,15},{3,14},{4,23},{5,22},{6,31},{7,30},{8,1},{9,0},... | collective-permute-start | bytes 466952 | tf_op jit(solution)/shard_map/ppermute | solution.py:425
  17.0 2.0 copy-start.2
  19.0 2.0 copy-start.4
  21.0 28.9 %copy-start.3 = (bf16[4,576,720]{2,1,0:T(8,128)(2,1)S(1)}, bf16[4,576,720]{2,1,0:T(8,128)(2,1)}, u32[]{:S(2)}) copy-start(bf16[4,576,720]{2,1,0:T(8,128)(2,1)} %refs_3_.3) | copy-start | bytes 9953284
  21.0 28.9 %copy-start.5 = (bf16[4,576,720]{2,1,0:T(8,128)(2,1)S(1)}, bf16[4,576,720]{2,1,0:T(8,128)(2,1)}, u32[]{:S(2)}) copy-start(bf16[4,576,720]{2,1,0:T(8,128)(2,1)} %refs_4_.5) | copy-start | bytes 9953284
  25.9 6.0 %collective-permute-start.4 = (bf16[256,1536]{1,0:T(8,128)(2,1)S(1)}, bf16[256,1536]{1,0:T(8,128)(2,1)S(1)}, u32[]{:S(2)}, u32[]{:S(2)}) collective-permute-start(bf16[256,1536]{1,0:T(8,128)(2,1)S(1)} %get-tuple-element.32), channel_id=1, source_target_pairs={{0,8},{1,9},{2,10},{3,11},{4,12},{5,13},{6,14},{7,15},{8,0},{9,1},... | collective-permute-start | bytes 2359304 | tf_op jit(solution)/shard_map/ppermute | solution.py:425
  26.0 13.7 %collective-permute-start.6 = (bf16[608,256]{1,0:T(8,128)(2,1)S(1)}, bf16[608,256]{1,0:T(8,128)(2,1)S(1)}, u32[]{:S(2)}, u32[]{:S(2)}) collective-permute-start(bf16[608,256]{1,0:T(8,128)(2,1)S(1)} %join.1.refs_1_), channel_id=1, source_target_pairs={{0,6},{1,7},{2,0},{3,1},{4,2},{5,3},{6,4},{7,5},{8,14},{9,15},{10,... | collective-permute-start | bytes 933896 | tf_op jit(solution)/shard_map/ppermute | solution.py:425
  31.9 18.0 %collective-permute-start.7 = (bf16[608,256]{1,0:T(8,128)(2,1)S(1)}, bf16[608,256]{1,0:T(8,128)(2,1)S(1)}, u32[]{:S(2)}, u32[]{:S(2)}) collective-permute-start(bf16[608,256]{1,0:T(8,128)(2,1)S(1)} %join.1.refs_1_), channel_id=1, source_target_pairs={{0,4},{1,5},{2,6},{3,7},{4,0},{5,1},{6,2},{7,3},{8,12},{9,13},{10,... | collective-permute-start | bytes 933896 | tf_op jit(solution)/shard_map/ppermute | solution.py:425
  58.4 3.5 %collective-permute-start.8 = (bf16[512,1536]{1,0:T(8,128)(2,1)S(1)}, bf16[512,1536]{1,0:T(8,128)(2,1)S(1)}, u32[]{:S(2)}, u32[]{:S(2)}) collective-permute-start(bf16[512,1536]{1,0:T(8,128)(2,1)S(1)} %get-tuple-element.37), channel_id=1, source_target_pairs={{0,8},{1,9},{2,10},{3,11},{4,12},{5,13},{6,14},{7,15},{8,0},{9,1},... | collective-permute-start | bytes 4718600 | tf_op jit(solution)/shard_map/ppermute | solution.py:425
  58.4 11.5 %collective-permute-start.5 = (bf16[128,1536]{1,0:T(8,128)(2,1)S(1)}, bf16[128,1536]{1,0:T(8,128)(2,1)S(1)}, u32[]{:S(2)}, u32[]{:S(2)}) collective-permute-start(bf16[128,1536]{1,0:T(8,128)(2,1)S(1)} %get-tuple-element.34), channel_id=1, source_target_pairs={{0,16},{1,17},{2,18},{3,19},{4,20},{5,21},{6,22},{7,23},{8,24},{9,... | collective-permute-start | bytes 1179656 | tf_op jit(solution)/shard_map/ppermute | solution.py:425
  59.5 12.9 %collective-permute-start.2 = (bf16[608,256]{1,0:T(8,128)(2,1)S(1)}, bf16[608,256]{1,0:T(8,128)(2,1)S(1)}, u32[]{:S(2)}, u32[]{:S(2)}) collective-permute-start(bf16[608,256]{1,0:T(8,128)(2,1)S(1)} %join.1.refs_1_), channel_id=1, source_target_pairs={{0,2},{1,3},{2,4},{3,5},{4,6},{5,7},{6,0},{7,1},{8,10},{9,11},{10,... | collective-permute-start | bytes 933896 | tf_op jit(solution)/shard_map/ppermute | solution.py:425
  72.4 30.5 %copy-start.1 = (bf16[4,720,576]{1,2,0:T(8,128)(2,1)S(1)}, bf16[4,720,576]{1,2,0:T(8,128)(2,1)}, u32[]{:S(2)}) copy-start(bf16[4,720,576]{1,2,0:T(8,128)(2,1)} %param.18) | copy-start | bytes 9953284
  77.2 24.3 %collective-permute-start.9 = (bf16[256,1536]{1,0:T(8,128)(2,1)S(1)}, bf16[256,1536]{1,0:T(8,128)(2,1)S(1)}, u32[]{:S(2)}, u32[]{:S(2)}) collective-permute-start(bf16[256,1536]{1,0:T(8,128)(2,1)S(1)} %get-tuple-element.40), channel_id=1, source_target_pairs={{0,8},{1,9},{2,10},{3,11},{4,12},{5,13},{6,14},{7,15},{8,0},{9,1},... | collective-permute-start | bytes 2359304 | tf_op jit(solution)/shard_map/ppermute | solution.py:425
  77.3 29.1 %collective-permute-start.11 = (bf16[256,1536]{1,0:T(8,128)(2,1)S(1)}, bf16[256,1536]{1,0:T(8,128)(2,1)S(1)}, u32[]{:S(2)}, u32[]{:S(2)}) collective-permute-start(bf16[256,1536]{1,0:T(8,128)(2,1)S(1)} %get-tuple-element.44), channel_id=1, source_target_pairs={{0,16},{1,17},{2,18},{3,19},{4,20},{5,21},{6,22},{7,23},{8,24},{9,... | collective-permute-start | bytes 2359304 | tf_op jit(solution)/shard_map/ppermute | solution.py:425
  79.1 22.3 %collective-permute-start.12 = (bf16[128,768]{1,0:T(8,128)(2,1)S(1)}, bf16[128,768]{1,0:T(8,128)(2,1)S(1)}, u32[]{:S(2)}, u32[]{:S(2)}) collective-permute-start(bf16[128,768]{1,0:T(8,128)(2,1)S(1)} %act.3.refs_5_.refs_1_), channel_id=1, source_target_pairs={{0,16},{1,17},{2,18},{3,19},{4,20},{5,21},{6,22},{7,23},{8,24},{9,... | collective-permute-start | bytes 589832 | tf_op jit(solution)/shard_map/ppermute | solution.py:425
  79.4 23.0 %collective-permute-start.13 = (bf16[128,768]{1,0:T(8,128)(2,1)S(1)}, bf16[128,768]{1,0:T(8,128)(2,1)S(1)}, u32[]{:S(2)}, u32[]{:S(2)}) collective-permute-start(bf16[128,768]{1,0:T(8,128)(2,1)S(1)} %act.3.refs_5_.refs_1_), channel_id=1, source_target_pairs={{0,8},{1,9},{2,10},{3,11},{4,12},{5,13},{6,14},{7,15},{8,0},{9,1},... | collective-permute-start | bytes 589832 | tf_op jit(solution)/shard_map/ppermute | solution.py:425
  101.5 1.4 collective-permute-start.14
  108.1 12.0 %collective-permute-start.18 = (bf16[256,768]{1,0:T(8,128)(2,1)S(1)}, bf16[256,768]{1,0:T(8,128)(2,1)S(1)}, u32[]{:S(2)}, u32[]{:S(2)}) collective-permute-start(bf16[256,768]{1,0:T(8,128)(2,1)S(1)} %act.4.refs_4_.refs_1_), channel_id=1, source_target_pairs={{0,16},{1,17},{2,18},{3,19},{4,20},{5,21},{6,22},{7,23},{8,24},{9,... | collective-permute-start | bytes 1179656 | tf_op jit(solution)/shard_map/ppermute | solution.py:425
  109.9 17.8 %collective-permute-start.10 = (bf16[128,1536]{1,0:T(8,128)(2,1)S(1)}, bf16[128,1536]{1,0:T(8,128)(2,1)S(1)}, u32[]{:S(2)}, u32[]{:S(2)}) collective-permute-start(bf16[128,1536]{1,0:T(8,128)(2,1)S(1)} %get-tuple-element.42), channel_id=1, source_target_pairs={{0,16},{1,17},{2,18},{3,19},{4,20},{5,21},{6,22},{7,23},{8,24},{9,... | collective-permute-start | bytes 1179656 | tf_op jit(solution)/shard_map/ppermute | solution.py:425
  110.2 25.0 %collective-permute-start.19 = (bf16[256,768]{1,0:T(8,128)(2,1)S(1)}, bf16[256,768]{1,0:T(8,128)(2,1)S(1)}, u32[]{:S(2)}, u32[]{:S(2)}) collective-permute-start(bf16[256,768]{1,0:T(8,128)(2,1)S(1)} %act.4.refs_4_.refs_1_), channel_id=1, source_target_pairs={{0,8},{1,9},{2,10},{3,11},{4,12},{5,13},{6,14},{7,15},{8,0},{9,1},... | collective-permute-start | bytes 1179656 | tf_op jit(solution)/shard_map/ppermute | solution.py:425
  120.1 15.1 %collective-permute-start.20 = (bf16[256,768]{1,0:T(8,128)(2,1)S(1)}, bf16[256,768]{1,0:T(8,128)(2,1)S(1)}, u32[]{:S(2)}, u32[]{:S(2)}) collective-permute-start(bf16[256,768]{1,0:T(8,128)(2,1)S(1)} %collective-permute-done.18.refs_2_), channel_id=1, source_target_pairs={{0,8},{1,9},{2,10},{3,11},{4,12},{5,13},{6,14},{7,15},{8,0},{9,1},... | collective-permute-start | bytes 1179656 | tf_op jit(solution)/shard_map/ppermute | solution.py:425
  129.0 6.2 %collective-permute-start.15 = (bf16[128,768]{1,0:T(8,128)(2,1)S(1)}, bf16[128,768]{1,0:T(8,128)(2,1)S(1)}, u32[]{:S(2)}, u32[]{:S(2)}) collective-permute-start(bf16[128,768]{1,0:T(8,128)(2,1)S(1)} %act.5.refs_7_.refs_1_), channel_id=1, source_target_pairs={{0,16},{1,17},{2,18},{3,19},{4,20},{5,21},{6,22},{7,23},{8,24},{9,... | collective-permute-start | bytes 589832 | tf_op jit(solution)/shard_map/ppermute | solution.py:425
  130.8 9.8 %collective-permute-start.22 = (bf16[288,256]{1,0:T(8,128)(2,1)S(1)}, bf16[288,256]{1,0:T(8,128)(2,1)S(1)}, u32[]{:S(2)}, u32[]{:S(2)}) collective-permute-start(bf16[288,256]{1,0:T(8,128)(2,1)S(1)} %get-tuple-element.50), channel_id=1, source_target_pairs={{0,1},{1,0},{2,3},{3,2},{4,5},{5,4},{6,7},{7,6},{8,9},{9,8},{10,11... | collective-permute-start | bytes 442376 | tf_op jit(solution)/shard_map/ppermute | solution.py:425
  131.4 11.3 %collective-permute-start.16 = (bf16[128,768]{1,0:T(8,128)(2,1)S(1)}, bf16[128,768]{1,0:T(8,128)(2,1)S(1)}, u32[]{:S(2)}, u32[]{:S(2)}) collective-permute-start(bf16[128,768]{1,0:T(8,128)(2,1)S(1)} %act.5.refs_7_.refs_1_), channel_id=1, source_target_pairs={{0,8},{1,9},{2,10},{3,11},{4,12},{5,13},{6,14},{7,15},{8,0},{9,1},... | collective-permute-start | bytes 589832 | tf_op jit(solution)/shard_map/ppermute | solution.py:425
  135.2 7.5 %collective-permute-start.17 = (bf16[128,768]{1,0:T(8,128)(2,1)S(1)}, bf16[128,768]{1,0:T(8,128)(2,1)S(1)}, u32[]{:S(2)}, u32[]{:S(2)}) collective-permute-start(bf16[128,768]{1,0:T(8,128)(2,1)S(1)} %collective-permute-done.15.refs_2_), channel_id=1, source_target_pairs={{0,8},{1,9},{2,10},{3,11},{4,12},{5,13},{6,14},{7,15},{8,0},{9,1},... | collective-permute-start | bytes 589832 | tf_op jit(solution)/shard_map/ppermute | solution.py:425
  140.0 9.9 %collective-permute-start.24 = (bf16[288,512]{1,0:T(8,128)(2,1)S(1)}, bf16[288,512]{1,0:T(8,128)(2,1)S(1)}, u32[]{:S(2)}, u32[]{:S(2)}) collective-permute-start(bf16[288,512]{1,0:T(8,128)(2,1)S(1)} %get-tuple-element.51), channel_id=1, source_target_pairs={{0,1},{1,0},{2,3},{3,2},{4,5},{5,4},{6,7},{7,6},{8,9},{9,8},{10,11... | collective-permute-start | bytes 884744 | tf_op jit(solution)/shard_map/ppermute | solution.py:425
  140.7 23.1 %collective-permute-start.23 = (bf16[288,256]{1,0:T(8,128)(2,1)S(1)}, bf16[288,256]{1,0:T(8,128)(2,1)S(1)}, u32[]{:S(2)}, u32[]{:S(2)}) collective-permute-start(bf16[288,256]{1,0:T(8,128)(2,1)S(1)} %add_convert_fusion.2), channel_id=1, source_target_pairs={{0,2},{1,3},{2,4},{3,5},{4,6},{5,7},{6,0},{7,1},{8,10},{9,11},{10,... | collective-permute-start | bytes 442376 | tf_op jit(solution)/shard_map/ppermute | solution.py:425
  142.7 25.0 %copy-start.11 = (f32[2304]{0:T(1024)S(1)}, f32[2304]{0:T(1024)}, u32[]{:S(2)}) copy-start(f32[2304]{0:T(1024)} %param.19) | copy-start | bytes 27652
  142.7 25.0 %copy-start.12 = (f32[16]{0:T(128)S(1)}, f32[16]{0:T(128)}, u32[]{:S(2)}) copy-start(f32[16]{0:T(128)} %param.21) | copy-start | bytes 196
  146.2 29.1 %copy-start.6 = (bf16[2304,512]{1,0:T(8,128)(2,1)S(1)}, bf16[2304,512]{1,0:T(8,128)(2,1)}, u32[]{:S(2)}) copy-start(bf16[2304,512]{1,0:T(8,128)(2,1)} %refs_2_.1) | copy-start | bytes 7077892
  146.2 17.6 %collective-permute-start.21 = (bf16[288,256]{1,0:T(8,128)(2,1)S(1)}, bf16[288,256]{1,0:T(8,128)(2,1)S(1)}, u32[]{:S(2)}, u32[]{:S(2)}) collective-permute-start(bf16[288,256]{1,0:T(8,128)(2,1)S(1)} %get-tuple-element.49), channel_id=1, source_target_pairs={{0,1},{1,0},{2,3},{3,2},{4,5},{5,4},{6,7},{7,6},{8,9},{9,8},{10,11... | collective-permute-start | bytes 442376 | tf_op jit(solution)/shard_map/ppermute | solution.py:425
  150.0 50.0 %copy-start.8 = (f32[256,288]{0,1:T(8,128)S(1)}, f32[256,288]{0,1:T(8,128)}, u32[]{:S(2)}) copy-start(f32[256,288]{0,1:T(8,128)} %param.11) | copy-start | bytes 884740
  150.0 13.8 %collective-permute-start.25 = (bf16[288,256]{1,0:T(8,128)(2,1)S(1)}, bf16[288,256]{1,0:T(8,128)(2,1)S(1)}, u32[]{:S(2)}, u32[]{:S(2)}) collective-permute-start(bf16[288,256]{1,0:T(8,128)(2,1)S(1)} %get-tuple-element.57), channel_id=1, source_target_pairs={{0,4},{1,5},{2,6},{3,7},{4,0},{5,1},{6,2},{7,3},{8,12},{9,13},{10,... | collective-permute-start | bytes 442376 | tf_op jit(solution)/shard_map/ppermute | solution.py:425
  151.3 12.5 %collective-permute-start.26 = (bf16[288,256]{1,0:T(8,128)(2,1)S(1)}, bf16[288,256]{1,0:T(8,128)(2,1)S(1)}, u32[]{:S(2)}, u32[]{:S(2)}) collective-permute-start(bf16[288,256]{1,0:T(8,128)(2,1)S(1)} %get-tuple-element.56), channel_id=1, source_target_pairs={{0,6},{1,7},{2,0},{3,1},{4,2},{5,3},{6,4},{7,5},{8,14},{9,15},{10,... | collective-permute-start | bytes 442376 | tf_op jit(solution)/shard_map/ppermute | solution.py:425
  154.9 8.9 %collective-permute-start.3 = (f32[4,288]{1,0:T(4,128)S(1)}, f32[4,288]{1,0:T(4,128)S(1)}, u32[]{:S(2)}, u32[]{:S(2)}) collective-permute-start(f32[4,288]{1,0:T(4,128)S(1)} %get-tuple-element.30), channel_id=1, source_target_pairs={{0,0},{1,1},{2,8},{3,9},{4,16},{5,17},{6,24},{7,25},{8,2},{9,3},{1... | collective-permute-start | bytes 13832 | tf_op jit(solution)/shard_map/ppermute | solution.py:425
  164.9 10.5 %all-to-all-start = ((f32[32,4,288]{2,1,0:T(4,128)}), f32[32,4,288]{2,1,0:T(4,128)S(1)}, u32[]{:S(2)}, u32[]{:S(2)}) async-start(f32[32,4,288]{2,1,0:T(4,128)} %get-tuple-element.53), calls=%async_computation | async-start | bytes 393216 | tf_op jit(solution)/shard_map/all_to_all | solution.py:502
  176.8 10.0 %all-to-all-start.1 = ((f32[32,2,16]{2,1,0:T(2,128)}), f32[32,2,16]{2,1,0:T(2,128)S(1)}, u32[]{:S(2)}, u32[]{:S(2)}) async-start(f32[32,2,16]{2,1,0:T(2,128)} %get-tuple-element.55), calls=%async_computation.1 | async-start | bytes 65536 | tf_op jit(solution)/shard_map/all_to_all | solution.py:502
  180.7 19.3 %collective-permute-start.27 = (f32[288,256]{1,0:T(8,128)S(1)}, f32[288,256]{1,0:T(8,128)S(1)}, u32[]{:S(2)}, u32[]{:S(2)}) collective-permute-start(f32[288,256]{1,0:T(8,128)S(1)} %get-tuple-element.52), channel_id=1, source_target_pairs={{0,0},{1,1},{2,8},{3,9},{4,16},{5,17},{6,24},{7,25},{8,2},{9,3},{1... | collective-permute-start | bytes 884744 | tf_op jit(solution)/shard_map/ppermute | solution.py:425

commit v6 on v5

--- a/solution.py
+++ b/solution.py
@@ -17,6 +17,7 @@
 VMEM = pl.BlockSpec(memory_space=pltpu.VMEM)
 SMEM = pl.BlockSpec(memory_space=pltpu.SMEM)
 ANY = pl.BlockSpec(memory_space=pl.ANY)
+HBM = pl.BlockSpec(memory_space=pltpu.HBM)
 
 
 def up_to(n, step=LANES):
@@ -27,8 +28,7 @@
     return pltpu.CompilerParams(vmem_limit_bytes=mib * 2**20)
 
 
-def cost(flops, bytes_accessed):
-    return pl.CostEstimate(flops=flops, bytes_accessed=bytes_accessed, transcendentals=0)
+HINT = pl.CostEstimate(flops=1, bytes_accessed=1024, transcendentals=0)
 
 
 def shape(dims, dtype):
@@ -79,7 +79,7 @@
         out_specs=[whole_spec(v) for v in outs],
         out_shape=outs,
         compiler_params=params(),
-        cost_estimate=cost(4 * tokens * block, 6 * tokens * block),
+        cost_estimate=HINT,
         name="prep",
     )(tallies, x, gain, routes)
 
@@ -97,7 +97,7 @@
         out_specs=VMEM,
         out_shape=shape((len(blocks) * rows, tokens), bf16),
         compiler_params=params(),
-        cost_estimate=cost(0, 4 * len(blocks) * rows * tokens),
+        cost_estimate=HINT,
         name="join",
     )(*blocks)
 
@@ -124,8 +124,20 @@
 
 
 def partial_kernel(sides, held, scal, *refs):
-    feeds, (wr, wg, wu), (own, give, cols, xs, xt, acc, extra) = refs[:held], refs[held : held + 3], refs[-7:]
+    feeds, (wr, wg, wu) = refs[:held], refs[held : held + 3]
+    own, give, cols, xs, xt, acc, extra, ring, sems = refs[-9:]
     e = pl.program_id(0)
+    experts = wg.shape[0]
+
+    def fetch(n, slot, which):
+        return pltpu.make_async_copy((wg, wu)[which].at[n], ring.at[slot, which], sems.at[slot, which])
+
+    @pl.when(e == 0)
+    def _():
+        for n in range(min(2, experts)):
+            for which in range(2):
+                fetch(n, n, which).start()
+
     core, side = scal[0], scal[1]
     depth, hidden = wg.shape[1:]
     deep, half = up_to(depth), up_to(hidden)
@@ -163,15 +175,22 @@
     mine, other = slot_columns(core, xt[:, deep : deep + LANES])
     ef = e.astype(f32)
     take = [(v == ef) | (e == 0) for v in (mine, other)]
-    for which, w in enumerate((wg, wu)):
+    slot = e % 2
+    for which in range(2):
+        fetch(e, slot, which).wait()
         for at in range(0, hidden, 256):
             end = min(hidden, at + 256)
-            d = jnp.dot(xt[:, 0:depth], w[0, :, at:end], preferred_element_type=f32)
+            d = jnp.dot(xt[:, 0:depth], ring[slot, which, :, at:end], preferred_element_type=f32)
             to = slice(which * half + at, which * half + end)
             for ref, pick in ((own, take[0]), (acc, take[1])):
                 ref[:, to] = jnp.where(pick, d, ref[:, to])
 
-    @pl.when(e == pl.num_programs(0) - 1)
+    @pl.when(e + 2 < experts)
+    def _():
+        for which in range(2):
+            fetch(e + 2, slot, which).start()
+
+    @pl.when(e == experts - 1)
     def _():
         lane = lax.broadcasted_iota(jnp.int32, extra.shape, 1)
         more = extra[...]
@@ -184,12 +203,11 @@
     experts, depth, hidden = wg.shape
     tokens = feeds[0].shape[1] * len(feeds)
     deep, wide = up_to(depth), 2 * up_to(hidden)
-    part = pl.BlockSpec((1, depth, hidden), lambda n: (n, 0, 0))
     outs = [shape((tokens, wide), f32), shape((tokens, wide), bf16), shape((tokens, LANES), bf16)]
     return pl.pallas_call(
         lambda *refs: partial_kernel(sides, len(feeds), *refs),
         grid=(experts,),
-        in_specs=[SMEM] + [whole_spec(v) for v in feeds] + [whole_spec(wr), part, part] + [ANY] * len(deps),
+        in_specs=[SMEM] + [whole_spec(v) for v in feeds] + [whole_spec(wr), HBM, HBM] + [ANY] * len(deps),
         out_specs=[whole_spec(v) for v in outs],
         out_shape=outs,
         scratch_shapes=[
@@ -197,11 +215,11 @@
             pltpu.VMEM((tokens, deep + LANES), bf16),
             pltpu.VMEM((tokens, wide), f32),
             pltpu.VMEM((tokens, LANES), f32),
+            pltpu.VMEM((2, 2, depth, hidden), bf16),
+            pltpu.SemaphoreType.DMA((2, 2)),
         ],
-        compiler_params=params(32),
-        cost_estimate=cost(
-            4 * experts * depth * hidden * tokens, 4 * experts * depth * hidden + 6 * tokens * wide
-        ),
+        compiler_params=params(20),
+        cost_estimate=HINT,
         name="gate_up_partial",
     )(scal, *feeds, wr, wg, wu, *deps)
 
@@ -226,7 +244,7 @@
         out_specs=[VMEM, VMEM],
         out_shape=[shape((tokens // 2, wide), f32), shape((tokens // 2, wide), bf16)],
         compiler_params=params(),
-        cost_estimate=cost(tokens * wide, 9 * tokens * wide),
+        cost_estimate=HINT,
         name="core_sum",
     )(scal, own, recv, *deps)
 
@@ -258,7 +276,7 @@
         out_specs=VMEM,
         out_shape=shape((th, wide // 2), bf16),
         compiler_params=params(),
-        cost_estimate=cost(6 * th * wide, 7 * th * wide),
+        cost_estimate=HINT,
         name="act",
     )(scal, keep, recv, cols, *deps)
 
@@ -316,9 +334,7 @@
             pltpu.VMEM((width, tokens), f32),
         ],
         compiler_params=params(20),
-        cost_estimate=cost(
-            2 * experts * width * hidden * tokens, 2 * experts * width * hidden + 2 * width * tokens
-        ),
+        cost_estimate=HINT,
         name="down",
     )(scal, *pieces, cols, wd, *deps)
 
@@ -347,7 +363,7 @@
         out_specs=[full(v) for v in outs],
         out_shape=outs,
         compiler_params=params(),
-        cost_estimate=cost(16 * block * tokens, 14 * block * tokens),
+        cost_estimate=HINT,
         name="branch_total",
     )(feed, stream, *parts)
 
@@ -385,7 +401,7 @@
         out_shape=[shape((rows, columns), f32), shape((got.shape[0], 2, rows), f32)],
         scratch_shapes=[pltpu.VMEM((LANES, LANES), f32)],
         compiler_params=params(),
-        cost_estimate=cost(2 * rows * WIDTH * columns, 2 * WIDTH * columns),
+        cost_estimate=HINT,
         name="head",
     )(got, gain, words, softness)
 
@@ -445,12 +461,12 @@
     room = lambda at: jnp.pad(wr, ((at, LANES - at - wr.shape[0]), (0, 0)))
     wr = room(base + 1) + room(base + 1 + EXTRA)
 
-    chunks = ((1,), (2, 3), (0,))
+    chunks = ((1,), (2,), (3,), (0,))
     first = [send(sent, lambda q, z, x, i=i: (z, (q - 1) % parts, x ^ i)) for i in range(sides)]
     pair = join_call(first)
     feeds = {1: pair}
     for group in (2, 3, 0):
-        feeds[group] = send(pair, lambda q, z, x, group=group: (q, (z - group + 1) % parts, x))
+        feeds[group] = send(feeds[(group - 1) % parts], lambda q, z, x: (q, (z - 1) % parts, x))
     stream = send(stream, home)
     partial, kept, pieces, shares = {}, {}, {}, {}
 
@@ -485,17 +501,21 @@
         return outs[0]
 
     p0 = do_partial(0)
-    s0 = do_sum(0)
-    p1 = do_partial(1, s0)
-    s1 = do_sum(1)
-    a0 = do_act(0, s1)
-    p2 = do_partial(2, a0)
-    s2 = do_sum(2)
-    d0 = do_down(0, s2)
-    a1 = do_act(1, d0)
-    a2 = do_act(2, a1)
+    p1 = do_partial(1, p0)
+    s0 = do_sum(0, p1)
+    p2 = do_partial(2, s0)
+    s1 = do_sum(1, p2)
+    p3 = do_partial(3, s1)
+    s2 = do_sum(2, p3)
+    a0 = do_act(0, s2)
+    s3 = do_sum(3, a0)
+    a1 = do_act(1, s3)
+    d0 = do_down(0, a1)
+    a2 = do_act(2, d0)
     d1 = do_down(1, a2)
-    do_down(2, d1)
+    a3 = do_act(3, d1)
+    d2 = do_down(2, a3)
+    do_down(3, d2)
     mine = [v for group in range(parts) for v in shares[group]]
     total, message = total_call(feeds[0], stream, mine, block, count)
 

time: 201 us -> 184 us (0.915)
  waiting for transfers between devices: 107 us -> 78.3 us
  Pallas kernels: 40.2 us -> 57.3 us
  starting transfers between devices: 44 us -> 37.8 us
    ppermute x28 -> x34, waiting for transfers between devices: 97.3 us -> 69.1 us  [send(): return lax.ppermute(value, ('dp', 'mp'), pairs)]
    pallas_call x3 -> x4, Pallas kernels: 18.1 us -> 31.7 us  [partial_call(): pl.pallas_call(lambda *refs: partial_kernel(sides, len(feeds), *refs), gr...]
    ppermute x28 -> x34, starting transfers between devices: 37.3 us -> 30.6 us  [send(): return lax.ppermute(value, ('dp', 'mp'), pairs)]
    pallas_call x3 -> x4, Pallas kernels: 11.7 us -> 13.9 us  [down_call(): pl.pallas_call(lambda *refs: down_kernel(sides, *refs), grid=(experts,),...]
    pallas_call x3 -> x4, Pallas kernels: 4.2 us -> 4.95 us  [act_call(): pl.pallas_call(lambda *refs: act_kernel(base, *refs), in_specs=[SMEM] + [...]
  transfers between devices with their start and end apart: 30 -> 36, of which waited for: 17 -> 15; matrix products, arithmetic and copies ran while one was open for 1% -> 1% of each run, Pallas kernels for 8% -> 29%
where the time goes in v6:
time: 184 us; the launch traced here: 183 us
  waiting for transfers between devices  78.3 us (43%)
  Pallas kernels  57.3 us (31%)
  starting transfers between devices  37.8 us (21%)
  local copies, waits for them, and re-layouts  7.3 us (4%)
    ppermute x34, waiting for transfers between devices, send(): return lax.ppermute(value, ('dp', 'mp'), pairs)  69.1 us
    pallas_call x4, Pallas kernels, partial_call(): pl.pallas_call(lambda *refs: partial_kernel(sides, len(feeds), *refs), gr...  31.7 us
    ppermute x34, starting transfers between devices, send(): return lax.ppermute(value, ('dp', 'mp'), pairs)  30.6 us
    pallas_call x4, Pallas kernels, down_call(): pl.pallas_call(lambda *refs: down_kernel(sides, *refs), grid=(experts,),...  13.9 us
    all_to_all x2, waiting for transfers between devices, body(): everyone = lambda v: lax.all_to_all(v, ('dp', 'mp'), 0, 0, tiled=True)  9.27 us
    all_to_all x2, starting transfers between devices, body(): everyone = lambda v: lax.all_to_all(v, ('dp', 'mp'), 0, 0, tiled=True)  7.25 us
    unnamed x26, local copies, waits for them, and re-layouts  6.34 us
    pallas_call x4, Pallas kernels, act_call(): pl.pallas_call(lambda *refs: act_kernel(base, *refs), in_specs=[SMEM] + [...  4.95 us
  transfers between devices with their start and end apart: 36, of which 15 were waited for; matrix products, arithmetic and copies ran while one was open for 1% of the time, Pallas kernels for 29%

profile of v6, /device:TPU:4, one launch (start us, length us, event | category | flops | bytes accessed | tf_op | source)
XLA Modules:
  0.0 183.5 jit_solution(12109758156587697294)
XLA Ops:
  1.3 1.0 copy-done.7
  3.6 0.9 prep.1
  4.5 1.5 collective-permute-start
  6.0 3.0 %collective-permute-start.1 = (bf16[304,256]{1,0:T(8,128)(2,1)S(1)}, bf16[304,256]{1,0:T(8,128)(2,1)S(1)}, u32[]{:S(2)}, u32[]{:S(2)}) collective-permute-start(bf16[304,256]{1,0:T(8,128)(2,1)S(1)} %get-tuple-element.36), channel_id=1, source_target_pairs={{0,7},{1,6},{2,15},{3,14},{4,23},{5,22},{6,31},{7,30},{8,1},{9,0},... | collective-permute-start | bytes 466952 | tf_op jit(solution)/shard_map/ppermute | solution.py:441
  9.2 3.6 %collective-permute-done.refs_0_ = bf16[304,256]{1,0:T(8,128)(2,1)S(1)} collective-permute-done((bf16[304,256]{1,0:T(8,128)(2,1)S(1)}, bf16[304,256]{1,0:T(8,128)(2,1)S(1)}, u32[]{:S(2)}, u32[]{:S(2)}) %collective-permute-start) | collective-permute-done | bytes 155680 | tf_op jit(solution)/shard_map/ppermute | solution.py:441
  12.7 4.3 %collective-permute-done.1.refs_1_ = bf16[304,256]{1,0:T(8,128)(2,1)S(1)} collective-permute-done((bf16[304,256]{1,0:T(8,128)(2,1)S(1)}, bf16[304,256]{1,0:T(8,128)(2,1)S(1)}, u32[]{:S(2)}, u32[]{:S(2)}) %collective-permute-start.1) | collective-permute-done | bytes 155680 | tf_op jit(solution)/shard_map/ppermute | solution.py:441
  17.0 5.9 %collective-permute-start.2 = (bf16[608,256]{1,0:T(8,128)(2,1)S(1)}, bf16[608,256]{1,0:T(8,128)(2,1)S(1)}, u32[]{:S(2)}, u32[]{:S(2)}) collective-permute-start(bf16[608,256]{1,0:T(8,128)(2,1)S(1)} %join.1.refs_1_), channel_id=1, source_target_pairs={{0,6},{1,7},{2,0},{3,1},{4,2},{5,3},{6,4},{7,5},{8,14},{9,15},{10,... | collective-permute-start | bytes 933896 | tf_op jit(solution)/shard_map/ppermute | solution.py:441
  23.0 2.0 %copy-done.2 = bf16[4,576,720]{2,1,0:T(8,128)(2,1)S(1)} copy-done((bf16[4,576,720]{2,1,0:T(8,128)(2,1)S(1)}, bf16[4,576,720]{2,1,0:T(8,128)(2,1)}, u32[]{:S(2)}) %copy-start.2) | copy-done | bytes 3317784
  25.0 2.0 %copy-done.4 = bf16[4,576,720]{2,1,0:T(8,128)(2,1)S(1)} copy-done((bf16[4,576,720]{2,1,0:T(8,128)(2,1)S(1)}, bf16[4,576,720]{2,1,0:T(8,128)(2,1)}, u32[]{:S(2)}) %copy-start.4) | copy-done | bytes 3317784
  27.0 7.9 %gate_up_partial.4 = (f32[256,1536]{1,0:T(8,128)S(1)}, bf16[256,1536]{1,0:T(8,128)(2,1)S(1)}, bf16[256,128]{1,0:T(8,128)(2,1)S(1)}) custom-call(s32[3]{0:T(128)S(1)} %pad_add_fusion.1.refs_0_, bf16[608,256]{1,0:T(8,128)(2,1)S(1)} %join.1.refs_1_, bf16[128,576]{1,0:T(8,128)(2,1)S(1)} %pad_add_fusion.refs_2_, bf16[4,576,720]{2,1,0:T(8,128)(2,1)S(1)} %copy-done.2, ...), custom_call_target="tpu_custom_call" | custom-call | flops 1 | bytes 1024 | tf_op jit(solution)/shard_map/gate_up_partial/pallas_call | solution.py:207
  35.0 7.9 %gate_up_partial.5 = (f32[256,1536]{1,0:T(8,128)S(1)}, bf16[256,1536]{1,0:T(8,128)(2,1)S(1)}, bf16[256,128]{1,0:T(8,128)(2,1)S(1)}) custom-call(s32[3]{0:T(128)S(1)} %pad_add_fusion.1.refs_0_, bf16[608,256]{1,0:T(8,128)(2,1)S(1)} %collective-permute-done.2.refs_1_, bf16[128,576]{1,0:T(8,128)(2,1)S(1)} %pad_add_fusion.refs_2_, ...), custom_call_target="tpu_custom_call" | custom-call | flops 1 | bytes 1024 | tf_op jit(solution)/shard_map/gate_up_partial/pallas_call | solution.py:207
  43.5 9.3 %collective-permute-done.3.refs_1_ = bf16[608,256]{1,0:T(8,128)(2,1)S(1)} collective-permute-done((bf16[608,256]{1,0:T(8,128)(2,1)S(1)}, bf16[608,256]{1,0:T(8,128)(2,1)S(1)}, u32[]{:S(2)}, u32[]{:S(2)}) %collective-permute-start.3) | collective-permute-done | bytes 311328 | tf_op jit(solution)/shard_map/ppermute | solution.py:441
  52.8 2.1 %collective-permute-start.4 = (bf16[608,256]{1,0:T(8,128)(2,1)S(1)}, bf16[608,256]{1,0:T(8,128)(2,1)S(1)}, u32[]{:S(2)}, u32[]{:S(2)}) collective-permute-start(bf16[608,256]{1,0:T(8,128)(2,1)S(1)} %collective-permute-done.3.refs_1_), channel_id=1, source_target_pairs={{0,6},{1,7},{2,0},{3,1},{4,2},{5,3},{6,4},{7,5},{8,14},{9,15},{10,... | collective-permute-start | bytes 933896 | tf_op jit(solution)/shard_map/ppermute | solution.py:441
  54.9 0.9 core_sum.4
  55.8 7.9 %gate_up_partial.6 = (f32[256,1536]{1,0:T(8,128)S(1)}, bf16[256,1536]{1,0:T(8,128)(2,1)S(1)}, bf16[256,128]{1,0:T(8,128)(2,1)S(1)}) custom-call(s32[3]{0:T(128)S(1)} %pad_add_fusion.1.refs_0_, bf16[608,256]{1,0:T(8,128)(2,1)S(1)} %collective-permute-done.3.refs_1_, bf16[128,576]{1,0:T(8,128)(2,1)S(1)} %pad_add_fusion.refs_2_, ...), custom_call_target="tpu_custom_call" | custom-call | flops 1 | bytes 1024 | tf_op jit(solution)/shard_map/gate_up_partial/pallas_call | solution.py:207
  63.8 0.9 core_sum.5
  64.7 7.9 %gate_up_partial.7 = (f32[256,1536]{1,0:T(8,128)S(1)}, bf16[256,1536]{1,0:T(8,128)(2,1)S(1)}, bf16[256,128]{1,0:T(8,128)(2,1)S(1)}) custom-call(s32[3]{0:T(128)S(1)} %pad_add_fusion.1.refs_0_, bf16[608,256]{1,0:T(8,128)(2,1)S(1)} %collective-permute-done.4.refs_1_.meta, bf16[128,576]{1,0:T(8,128)(2,1)S(1)} %pad_add_fusion.refs_2_, ...), custom_call_target="tpu_custom_call" | custom-call | flops 1 | bytes 1024 | tf_op jit(solution)/shard_map/gate_up_partial/pallas_call | solution.py:207
  73.1 2.0 %collective-permute-start.12 = (bf16[128,1536]{1,0:T(8,128)(2,1)S(1)}, bf16[128,1536]{1,0:T(8,128)(2,1)S(1)}, u32[]{:S(2)}, u32[]{:S(2)}) collective-permute-start(bf16[128,1536]{1,0:T(8,128)(2,1)S(1)} %get-tuple-element.54), channel_id=1, source_target_pairs={{0,16},{1,17},{2,18},{3,19},{4,20},{5,21},{6,22},{7,23},{8,24},{9,... | collective-permute-start | bytes 1179656 | tf_op jit(solution)/shard_map/ppermute | solution.py:441
  75.2 0.9 core_sum.6
  76.0 9.1 %collective-permute-done.9.refs_2_ = bf16[128,1536]{1,0:T(8,128)(2,1)S(1)} collective-permute-done((bf16[128,1536]{1,0:T(8,128)(2,1)S(1)}, bf16[128,1536]{1,0:T(8,128)(2,1)S(1)}, u32[]{:S(2)}, u32[]{:S(2)}) %collective-permute-start.9) | collective-permute-done | bytes 393248 | tf_op jit(solution)/shard_map/ppermute | solution.py:441
  85.1 1.2 act.4.refs_3_.refs_1_
  86.5 2.0 %collective-permute-start.16 = (bf16[128,1536]{1,0:T(8,128)(2,1)S(1)}, bf16[128,1536]{1,0:T(8,128)(2,1)S(1)}, u32[]{:S(2)}, u32[]{:S(2)}) collective-permute-start(bf16[128,1536]{1,0:T(8,128)(2,1)S(1)} %get-tuple-element.56), channel_id=1, source_target_pairs={{0,16},{1,17},{2,18},{3,19},{4,20},{5,21},{6,22},{7,23},{8,24},{9,... | collective-permute-start | bytes 1179656 | tf_op jit(solution)/shard_map/ppermute | solution.py:441
  88.5 9.3 %collective-permute-done.17.refs_2_ = bf16[128,768]{1,0:T(8,128)(2,1)S(1)} collective-permute-done((bf16[128,768]{1,0:T(8,128)(2,1)S(1)}, bf16[128,768]{1,0:T(8,128)(2,1)S(1)}, u32[]{:S(2)}, u32[]{:S(2)}) %collective-permute-start.17) | collective-permute-done | bytes 196640 | tf_op jit(solution)/shard_map/ppermute | solution.py:441
  97.8 0.9 core_sum.7
  98.6 1.2 act.5.refs_7_.refs_1_
  100.5 3.5 %down.4 = (bf16[288,256]{1,0:T(8,128)(2,1)S(1)}, bf16[288,256]{1,0:T(8,128)(2,1)S(1)}) custom-call(s32[3]{0:T(128)S(1)} %pad_add_fusion.1.refs_0_, bf16[128,768]{1,0:T(8,128)(2,1)S(1)} %act.4.refs_3_.refs_1_, bf16[128,768]{1,0:T(8,128)(2,1)S(1)} %collective-permute-done.17.refs_2_, bf16[128,768]{1,0:T(8,128)(2,1)S(1)} %collective-permute-done.18.refs_3_, ...), custom_call_target="tpu_custom_call" | custom-call | flops 1 | bytes 1024 | tf_op jit(solution)/shard_map/down/pallas_call | solution.py:323
  104.0 2.2 %collective-permute-done.16.refs_2_ = bf16[128,1536]{1,0:T(8,128)(2,1)S(1)} collective-permute-done((bf16[128,1536]{1,0:T(8,128)(2,1)S(1)}, bf16[128,1536]{1,0:T(8,128)(2,1)S(1)}, u32[]{:S(2)}, u32[]{:S(2)}) %collective-permute-start.16) | collective-permute-done | bytes 393248 | tf_op jit(solution)/shard_map/ppermute | solution.py:441
  106.2 1.2 act.6.refs_7_.refs_1_
  107.5 2.9 %collective-permute-done.13.refs_2_ = bf16[128,768]{1,0:T(8,128)(2,1)S(1)} collective-permute-done((bf16[128,768]{1,0:T(8,128)(2,1)S(1)}, bf16[128,768]{1,0:T(8,128)(2,1)S(1)}, u32[]{:S(2)}, u32[]{:S(2)}) %collective-permute-start.13) | collective-permute-done | bytes 196640 | tf_op jit(solution)/shard_map/ppermute | solution.py:441
  111.2 2.7 %collective-permute-done.23.refs_2_ = bf16[128,768]{1,0:T(8,128)(2,1)S(1)} collective-permute-done((bf16[128,768]{1,0:T(8,128)(2,1)S(1)}, bf16[128,768]{1,0:T(8,128)(2,1)S(1)}, u32[]{:S(2)}, u32[]{:S(2)}) %collective-permute-start.23) | collective-permute-done | bytes 196640 | tf_op jit(solution)/shard_map/ppermute | solution.py:441
  113.9 3.5 %down.5 = (bf16[288,256]{1,0:T(8,128)(2,1)S(1)}, bf16[288,256]{1,0:T(8,128)(2,1)S(1)}) custom-call(s32[3]{0:T(128)S(1)} %pad_add_fusion.1.refs_0_, bf16[128,768]{1,0:T(8,128)(2,1)S(1)} %act.5.refs_7_.refs_1_, bf16[128,768]{1,0:T(8,128)(2,1)S(1)} %collective-permute-done.13.refs_2_, bf16[128,768]{1,0:T(8,128)(2,1)S(1)} %collective-permute-done.14.refs_3_, ...), custom_call_target="tpu_custom_call" | custom-call | flops 1 | bytes 1024 | tf_op jit(solution)/shard_map/down/pallas_call | solution.py:323
  118.1 4.0 %collective-permute-done.11.refs_2_ = bf16[128,1536]{1,0:T(8,128)(2,1)S(1)} collective-permute-done((bf16[128,1536]{1,0:T(8,128)(2,1)S(1)}, bf16[128,1536]{1,0:T(8,128)(2,1)S(1)}, u32[]{:S(2)}, u32[]{:S(2)}) %collective-permute-start.11) | collective-permute-done | bytes 393248 | tf_op jit(solution)/shard_map/ppermute | solution.py:441
  122.2 1.2 act.7.refs_7_.refs_1_
  123.8 3.5 %down.6 = (bf16[288,256]{1,0:T(8,128)(2,1)S(1)}, bf16[288,256]{1,0:T(8,128)(2,1)S(1)}) custom-call(s32[3]{0:T(128)S(1)} %pad_add_fusion.1.refs_0_, bf16[128,768]{1,0:T(8,128)(2,1)S(1)} %act.6.refs_7_.refs_1_, bf16[128,768]{1,0:T(8,128)(2,1)S(1)} %collective-permute-done.23.refs_2_, bf16[128,768]{1,0:T(8,128)(2,1)S(1)} %collective-permute-done.24.refs_3_, ...), custom_call_target="tpu_custom_call" | custom-call | flops 1 | bytes 1024 | tf_op jit(solution)/shard_map/down/pallas_call | solution.py:323
  128.1 2.1 %collective-permute-done.20.refs_2_ = bf16[128,768]{1,0:T(8,128)(2,1)S(1)} collective-permute-done((bf16[128,768]{1,0:T(8,128)(2,1)S(1)}, bf16[128,768]{1,0:T(8,128)(2,1)S(1)}, u32[]{:S(2)}, u32[]{:S(2)}) %collective-permute-start.20) | collective-permute-done | bytes 196640 | tf_op jit(solution)/shard_map/ppermute | solution.py:441
  130.2 3.5 %collective-permute-done.31 = bf16[288,256]{1,0:T(8,128)(2,1)S(1)} collective-permute-done((bf16[288,256]{1,0:T(8,128)(2,1)S(1)}, bf16[288,256]{1,0:T(8,128)(2,1)S(1)}, u32[]{:S(2)}, u32[]{:S(2)}) %collective-permute-start.31) | collective-permute-done | bytes 147488 | tf_op jit(solution)/shard_map/ppermute | solution.py:441
  134.5 3.5 %down.7 = (bf16[288,256]{1,0:T(8,128)(2,1)S(1)}, bf16[288,256]{1,0:T(8,128)(2,1)S(1)}) custom-call(s32[3]{0:T(128)S(1)} %pad_add_fusion.1.refs_0_, bf16[128,768]{1,0:T(8,128)(2,1)S(1)} %act.7.refs_7_.refs_1_, bf16[128,768]{1,0:T(8,128)(2,1)S(1)} %collective-permute-done.20.refs_2_, bf16[128,768]{1,0:T(8,128)(2,1)S(1)} %collective-permute-done.21.refs_3_, ...), custom_call_target="tpu_custom_call" | custom-call | flops 1 | bytes 1024 | tf_op jit(solution)/shard_map/down/pallas_call | solution.py:323
  138.6 3.7 %collective-permute-start.5 = (f32[4,288]{1,0:T(4,128)S(1)}, f32[4,288]{1,0:T(4,128)S(1)}, u32[]{:S(2)}, u32[]{:S(2)}) collective-permute-start(f32[4,288]{1,0:T(4,128)S(1)} %get-tuple-element.37), channel_id=1, source_target_pairs={{0,0},{1,1},{2,8},{3,9},{4,16},{5,17},{6,24},{7,25},{8,2},{9,3},{1... | collective-permute-start | bytes 13832 | tf_op jit(solution)/shard_map/ppermute | solution.py:441
  142.3 3.6 %collective-permute-done.5.stream = f32[4,288]{1,0:T(4,128)S(1)} collective-permute-done((f32[4,288]{1,0:T(4,128)S(1)}, f32[4,288]{1,0:T(4,128)S(1)}, u32[]{:S(2)}, u32[]{:S(2)}) %collective-permute-start.5) | collective-permute-done | bytes 4640 | tf_op jit(solution)/shard_map/ppermute | solution.py:441
  145.9 1.1 branch_total.1
  147.0 3.3 %all-to-all-start = ((f32[32,4,288]{2,1,0:T(4,128)}), f32[32,4,288]{2,1,0:T(4,128)S(1)}, u32[]{:S(2)}, u32[]{:S(2)}) async-start(f32[32,4,288]{2,1,0:T(4,128)} %get-tuple-element.67), calls=%async_computation | async-start | bytes 393216 | tf_op jit(solution)/shard_map/all_to_all | solution.py:522
  150.5 7.5 %all-to-all-done.refs_0_ = f32[32,4,288]{2,1,0:T(4,128)S(1)} async-done(((f32[32,4,288]{2,1,0:T(4,128)}), f32[32,4,288]{2,1,0:T(4,128)S(1)}, u32[]{:S(2)}, u32[]{:S(2)}) %all-to-all-start) | async-done | bytes 147488 | tf_op jit(solution)/shard_map/all_to_all | solution.py:522
  158.0 1.4 head.1
  159.5 3.9 %all-to-all-start.1 = ((f32[32,2,16]{2,1,0:T(2,128)}), f32[32,2,16]{2,1,0:T(2,128)S(1)}, u32[]{:S(2)}, u32[]{:S(2)}) async-start(f32[32,2,16]{2,1,0:T(2,128)} %get-tuple-element.69), calls=%async_computation.1 | async-start | bytes 65536 | tf_op jit(solution)/shard_map/all_to_all | solution.py:522
  163.4 4.3 %collective-permute-start.33 = (f32[288,256]{1,0:T(8,128)S(1)}, f32[288,256]{1,0:T(8,128)S(1)}, u32[]{:S(2)}, u32[]{:S(2)}) collective-permute-start(f32[288,256]{1,0:T(8,128)S(1)} %get-tuple-element.66), channel_id=1, source_target_pairs={{0,0},{1,1},{2,8},{3,9},{4,16},{5,17},{6,24},{7,25},{8,2},{9,3},{1... | collective-permute-start | bytes 884744 | tf_op jit(solution)/shard_map/ppermute | solution.py:441
  167.7 1.8 all-to-all-done.1
  170.2 12.5 %collective-permute-done.33 = f32[288,256]{1,0:T(8,128)S(1)} collective-permute-done((f32[288,256]{1,0:T(8,128)S(1)}, f32[288,256]{1,0:T(8,128)S(1)}, u32[]{:S(2)}, u32[]{:S(2)}) %collective-permute-start.33) | collective-permute-done | bytes 294944 | tf_op jit(solution)/shard_map/ppermute | solution.py:441
  182.7 0.8 bitcast_add_fusion
  (85 shorter events, 9.5 us)
Async XLA Ops:
  0.6 8.4 %copy-start = (bf16[2304,4]{0,1:T(4,128)(2,1)S(1)}, bf16[2304,4]{0,1:T(4,128)(2,1)}, u32[]{:S(2)}) copy-start(bf16[2304,4]{0,1:T(4,128)(2,1)} %param.15) | copy-start | bytes 55300
  1.3 1.0 copy-start.7
  2.3 0.7 copy-start.9
  4.5 8.2 %collective-permute-start = (bf16[304,256]{1,0:T(8,128)(2,1)S(1)}, bf16[304,256]{1,0:T(8,128)(2,1)S(1)}, u32[]{:S(2)}, u32[]{:S(2)}) collective-permute-start(bf16[304,256]{1,0:T(8,128)(2,1)S(1)} %get-tuple-element.36), channel_id=1, source_target_pairs={{0,6},{1,7},{2,14},{3,15},{4,22},{5,23},{6,30},{7,31},{8,0},{9,1},... | collective-permute-start | bytes 466952 | tf_op jit(solution)/shard_map/ppermute | solution.py:441
  6.0 11.0 %collective-permute-start.1 = (bf16[304,256]{1,0:T(8,128)(2,1)S(1)}, bf16[304,256]{1,0:T(8,128)(2,1)S(1)}, u32[]{:S(2)}, u32[]{:S(2)}) collective-permute-start(bf16[304,256]{1,0:T(8,128)(2,1)S(1)} %get-tuple-element.36), channel_id=1, source_target_pairs={{0,7},{1,6},{2,15},{3,14},{4,23},{5,22},{6,31},{7,30},{8,1},{9,0},... | collective-permute-start | bytes 466952 | tf_op jit(solution)/shard_map/ppermute | solution.py:441
  17.0 18.0 %collective-permute-start.2 = (bf16[608,256]{1,0:T(8,128)(2,1)S(1)}, bf16[608,256]{1,0:T(8,128)(2,1)S(1)}, u32[]{:S(2)}, u32[]{:S(2)}) collective-permute-start(bf16[608,256]{1,0:T(8,128)(2,1)S(1)} %join.1.refs_1_), channel_id=1, source_target_pairs={{0,6},{1,7},{2,0},{3,1},{4,2},{5,3},{6,4},{7,5},{8,14},{9,15},{10,... | collective-permute-start | bytes 933896 | tf_op jit(solution)/shard_map/ppermute | solution.py:441
  23.0 2.0 %copy-start.2 = (bf16[4,576,720]{2,1,0:T(8,128)(2,1)S(1)}, bf16[4,576,720]{2,1,0:T(8,128)(2,1)}, u32[]{:S(2)}) copy-start(bf16[4,576,720]{2,1,0:T(8,128)(2,1)} %refs_3_.7) | copy-start | bytes 9953284
  25.0 2.0 %copy-start.4 = (bf16[4,576,720]{2,1,0:T(8,128)(2,1)S(1)}, bf16[4,576,720]{2,1,0:T(8,128)(2,1)}, u32[]{:S(2)}) copy-start(bf16[4,576,720]{2,1,0:T(8,128)(2,1)} %refs_4_.7) | copy-start | bytes 9953284
  27.0 8.0 %copy-start.3 = (bf16[4,576,720]{2,1,0:T(8,128)(2,1)S(1)}, bf16[4,576,720]{2,1,0:T(8,128)(2,1)}, u32[]{:S(2)}) copy-start(bf16[4,576,720]{2,1,0:T(8,128)(2,1)} %refs_3_.7) | copy-start | bytes 9953284
  27.0 8.0 %copy-start.5 = (bf16[4,576,720]{2,1,0:T(8,128)(2,1)S(1)}, bf16[4,576,720]{2,1,0:T(8,128)(2,1)}, u32[]{:S(2)}) copy-start(bf16[4,576,720]{2,1,0:T(8,128)(2,1)} %refs_4_.7) | copy-start | bytes 9953284
  34.9 20.0 %collective-permute-start.7 = (bf16[256,1536]{1,0:T(8,128)(2,1)S(1)}, bf16[256,1536]{1,0:T(8,128)(2,1)S(1)}, u32[]{:S(2)}, u32[]{:S(2)}) collective-permute-start(bf16[256,1536]{1,0:T(8,128)(2,1)S(1)} %get-tuple-element.41), channel_id=1, source_target_pairs={{0,8},{1,9},{2,10},{3,11},{4,12},{5,13},{6,14},{7,15},{8,0},{9,1},... | collective-permute-start | bytes 2359304 | tf_op jit(solution)/shard_map/ppermute | solution.py:441
  43.0 20.8 %collective-permute-start.6 = (bf16[256,1536]{1,0:T(8,128)(2,1)S(1)}, bf16[256,1536]{1,0:T(8,128)(2,1)S(1)}, u32[]{:S(2)}, u32[]{:S(2)}) collective-permute-start(bf16[256,1536]{1,0:T(8,128)(2,1)S(1)} %get-tuple-element.40), channel_id=1, source_target_pairs={{0,8},{1,9},{2,10},{3,11},{4,12},{5,13},{6,14},{7,15},{8,0},{9,1},... | collective-permute-start | bytes 2359304 | tf_op jit(solution)/shard_map/ppermute | solution.py:441
  43.5 9.3 %collective-permute-start.3 = (bf16[608,256]{1,0:T(8,128)(2,1)S(1)}, bf16[608,256]{1,0:T(8,128)(2,1)S(1)}, u32[]{:S(2)}, u32[]{:S(2)}) collective-permute-start(bf16[608,256]{1,0:T(8,128)(2,1)S(1)} %collective-permute-done.2.refs_1_), channel_id=1, source_target_pairs={{0,6},{1,7},{2,0},{3,1},{4,2},{5,3},{6,4},{7,5},{8,14},{9,15},{10,... | collective-permute-start | bytes 933896 | tf_op jit(solution)/shard_map/ppermute | solution.py:441
  52.8 11.8 %collective-permute-start.4 = (bf16[608,256]{1,0:T(8,128)(2,1)S(1)}, bf16[608,256]{1,0:T(8,128)(2,1)S(1)}, u32[]{:S(2)}, u32[]{:S(2)}) collective-permute-start(bf16[608,256]{1,0:T(8,128)(2,1)S(1)} %collective-permute-done.3.refs_1_), channel_id=1, source_target_pairs={{0,6},{1,7},{2,0},{3,1},{4,2},{5,3},{6,4},{7,5},{8,14},{9,15},{10,... | collective-permute-start | bytes 933896 | tf_op jit(solution)/shard_map/ppermute | solution.py:441
  63.7 11.5 %collective-permute-start.10 = (bf16[256,1536]{1,0:T(8,128)(2,1)S(1)}, bf16[256,1536]{1,0:T(8,128)(2,1)S(1)}, u32[]{:S(2)}, u32[]{:S(2)}) collective-permute-start(bf16[256,1536]{1,0:T(8,128)(2,1)S(1)} %get-tuple-element.49), channel_id=1, source_target_pairs={{0,8},{1,9},{2,10},{3,11},{4,12},{5,13},{6,14},{7,15},{8,0},{9,1},... | collective-permute-start | bytes 2359304 | tf_op jit(solution)/shard_map/ppermute | solution.py:441
  72.6 25.2 %collective-permute-start.8 = (bf16[256,1536]{1,0:T(8,128)(2,1)S(1)}, bf16[256,1536]{1,0:T(8,128)(2,1)S(1)}, u32[]{:S(2)}, u32[]{:S(2)}) collective-permute-start(bf16[256,1536]{1,0:T(8,128)(2,1)S(1)} %get-tuple-element.46), channel_id=1, source_target_pairs={{0,8},{1,9},{2,10},{3,11},{4,12},{5,13},{6,14},{7,15},{8,0},{9,1},... | collective-permute-start | bytes 2359304 | tf_op jit(solution)/shard_map/ppermute | solution.py:441
  73.1 12.0 %collective-permute-start.9 = (bf16[128,1536]{1,0:T(8,128)(2,1)S(1)}, bf16[128,1536]{1,0:T(8,128)(2,1)S(1)}, u32[]{:S(2)}, u32[]{:S(2)}) collective-permute-start(bf16[128,1536]{1,0:T(8,128)(2,1)S(1)} %get-tuple-element.47), channel_id=1, source_target_pairs={{0,16},{1,17},{2,18},{3,19},{4,20},{5,21},{6,22},{7,23},{8,24},{9,... | collective-permute-start | bytes 1179656 | tf_op jit(solution)/shard_map/ppermute | solution.py:441
  73.1 25.5 %collective-permute-start.12 = (bf16[128,1536]{1,0:T(8,128)(2,1)S(1)}, bf16[128,1536]{1,0:T(8,128)(2,1)S(1)}, u32[]{:S(2)}, u32[]{:S(2)}) collective-permute-start(bf16[128,1536]{1,0:T(8,128)(2,1)S(1)} %get-tuple-element.54), channel_id=1, source_target_pairs={{0,16},{1,17},{2,18},{3,19},{4,20},{5,21},{6,22},{7,23},{8,24},{9,... | collective-permute-start | bytes 1179656 | tf_op jit(solution)/shard_map/ppermute | solution.py:441
  86.4 11.4 %collective-permute-start.17 = (bf16[128,768]{1,0:T(8,128)(2,1)S(1)}, bf16[128,768]{1,0:T(8,128)(2,1)S(1)}, u32[]{:S(2)}, u32[]{:S(2)}) collective-permute-start(bf16[128,768]{1,0:T(8,128)(2,1)S(1)} %act.4.refs_3_.refs_1_), channel_id=1, source_target_pairs={{0,16},{1,17},{2,18},{3,19},{4,20},{5,21},{6,22},{7,23},{8,24},{9,... | collective-permute-start | bytes 589832 | tf_op jit(solution)/shard_map/ppermute | solution.py:441
  86.4 14.1 %copy-start.1 = (bf16[4,720,576]{1,2,0:T(8,128)(2,1)S(1)}, bf16[4,720,576]{1,2,0:T(8,128)(2,1)}, u32[]{:S(2)}) copy-start(bf16[4,720,576]{1,2,0:T(8,128)(2,1)} %param.18) | copy-start | bytes 9953284
  86.5 19.7 %collective-permute-start.16 = (bf16[128,1536]{1,0:T(8,128)(2,1)S(1)}, bf16[128,1536]{1,0:T(8,128)(2,1)S(1)}, u32[]{:S(2)}, u32[]{:S(2)}) collective-permute-start(bf16[128,1536]{1,0:T(8,128)(2,1)S(1)} %get-tuple-element.56), channel_id=1, source_target_pairs={{0,16},{1,17},{2,18},{3,19},{4,20},{5,21},{6,22},{7,23},{8,24},{9,... | collective-permute-start | bytes 1179656 | tf_op jit(solution)/shard_map/ppermute | solution.py:441
  88.5 12.1 %collective-permute-start.18 = (bf16[128,768]{1,0:T(8,128)(2,1)S(1)}, bf16[128,768]{1,0:T(8,128)(2,1)S(1)}, u32[]{:S(2)}, u32[]{:S(2)}) collective-permute-start(bf16[128,768]{1,0:T(8,128)(2,1)S(1)} %act.4.refs_3_.refs_1_), channel_id=1, source_target_pairs={{0,8},{1,9},{2,10},{3,11},{4,12},{5,13},{6,14},{7,15},{8,0},{9,1},... | collective-permute-start | bytes 589832 | tf_op jit(solution)/shard_map/ppermute | solution.py:441
  97.8 2.8 %collective-permute-start.19 = (bf16[128,768]{1,0:T(8,128)(2,1)S(1)}, bf16[128,768]{1,0:T(8,128)(2,1)S(1)}, u32[]{:S(2)}, u32[]{:S(2)}) collective-permute-start(bf16[128,768]{1,0:T(8,128)(2,1)S(1)} %collective-permute-done.17.refs_2_), channel_id=1, source_target_pairs={{0,8},{1,9},{2,10},{3,11},{4,12},{5,13},{6,14},{7,15},{8,0},{9,1},... | collective-permute-start | bytes 589832 | tf_op jit(solution)/shard_map/ppermute | solution.py:441
  99.9 10.5 %collective-permute-start.13 = (bf16[128,768]{1,0:T(8,128)(2,1)S(1)}, bf16[128,768]{1,0:T(8,128)(2,1)S(1)}, u32[]{:S(2)}, u32[]{:S(2)}) collective-permute-start(bf16[128,768]{1,0:T(8,128)(2,1)S(1)} %act.5.refs_7_.refs_1_), channel_id=1, source_target_pairs={{0,16},{1,17},{2,18},{3,19},{4,20},{5,21},{6,22},{7,23},{8,24},{9,... | collective-permute-start | bytes 589832 | tf_op jit(solution)/shard_map/ppermute | solution.py:441
  100.0 11.0 %collective-permute-start.14 = (bf16[128,768]{1,0:T(8,128)(2,1)S(1)}, bf16[128,768]{1,0:T(8,128)(2,1)S(1)}, u32[]{:S(2)}, u32[]{:S(2)}) collective-permute-start(bf16[128,768]{1,0:T(8,128)(2,1)S(1)} %act.5.refs_7_.refs_1_), channel_id=1, source_target_pairs={{0,8},{1,9},{2,10},{3,11},{4,12},{5,13},{6,14},{7,15},{8,0},{9,1},... | collective-permute-start | bytes 589832 | tf_op jit(solution)/shard_map/ppermute | solution.py:441
  107.4 6.5 %collective-permute-start.23 = (bf16[128,768]{1,0:T(8,128)(2,1)S(1)}, bf16[128,768]{1,0:T(8,128)(2,1)S(1)}, u32[]{:S(2)}, u32[]{:S(2)}) collective-permute-start(bf16[128,768]{1,0:T(8,128)(2,1)S(1)} %act.6.refs_7_.refs_1_), channel_id=1, source_target_pairs={{0,16},{1,17},{2,18},{3,19},{4,20},{5,21},{6,22},{7,23},{8,24},{9,... | collective-permute-start | bytes 589832 | tf_op jit(solution)/shard_map/ppermute | solution.py:441
  110.4 3.5 %collective-permute-start.15 = (bf16[128,768]{1,0:T(8,128)(2,1)S(1)}, bf16[128,768]{1,0:T(8,128)(2,1)S(1)}, u32[]{:S(2)}, u32[]{:S(2)}) collective-permute-start(bf16[128,768]{1,0:T(8,128)(2,1)S(1)} %collective-permute-done.13.refs_2_), channel_id=1, source_target_pairs={{0,8},{1,9},{2,10},{3,11},{4,12},{5,13},{6,14},{7,15},{8,0},{9,1},... | collective-permute-start | bytes 589832 | tf_op jit(solution)/shard_map/ppermute | solution.py:441
  110.4 11.8 %collective-permute-start.11 = (bf16[128,1536]{1,0:T(8,128)(2,1)S(1)}, bf16[128,1536]{1,0:T(8,128)(2,1)S(1)}, u32[]{:S(2)}, u32[]{:S(2)}) collective-permute-start(bf16[128,1536]{1,0:T(8,128)(2,1)S(1)} %get-tuple-element.52), channel_id=1, source_target_pairs={{0,16},{1,17},{2,18},{3,19},{4,20},{5,21},{6,22},{7,23},{8,24},{9,... | collective-permute-start | bytes 1179656 | tf_op jit(solution)/shard_map/ppermute | solution.py:441
  110.4 7.6 %collective-permute-start.27 = (bf16[288,256]{1,0:T(8,128)(2,1)S(1)}, bf16[288,256]{1,0:T(8,128)(2,1)S(1)}, u32[]{:S(2)}, u32[]{:S(2)}) collective-permute-start(bf16[288,256]{1,0:T(8,128)(2,1)S(1)} %get-tuple-element.63), channel_id=1, source_target_pairs={{0,1},{1,0},{2,3},{3,2},{4,5},{5,4},{6,7},{7,6},{8,9},{9,8},{10,11... | collective-permute-start | bytes 442376 | tf_op jit(solution)/shard_map/ppermute | solution.py:441
  111.0 12.9 %collective-permute-start.24 = (bf16[128,768]{1,0:T(8,128)(2,1)S(1)}, bf16[128,768]{1,0:T(8,128)(2,1)S(1)}, u32[]{:S(2)}, u32[]{:S(2)}) collective-permute-start(bf16[128,768]{1,0:T(8,128)(2,1)S(1)} %act.6.refs_7_.refs_1_), channel_id=1, source_target_pairs={{0,8},{1,9},{2,10},{3,11},{4,12},{5,13},{6,14},{7,15},{8,0},{9,1},... | collective-permute-start | bytes 589832 | tf_op jit(solution)/shard_map/ppermute | solution.py:441
  113.9 9.9 %collective-permute-start.25 = (bf16[128,768]{1,0:T(8,128)(2,1)S(1)}, bf16[128,768]{1,0:T(8,128)(2,1)S(1)}, u32[]{:S(2)}, u32[]{:S(2)}) collective-permute-start(bf16[128,768]{1,0:T(8,128)(2,1)S(1)} %collective-permute-done.23.refs_2_), channel_id=1, source_target_pairs={{0,8},{1,9},{2,10},{3,11},{4,12},{5,13},{6,14},{7,15},{8,0},{9,1},... | collective-permute-start | bytes 589832 | tf_op jit(solution)/shard_map/ppermute | solution.py:441
  117.4 10.6 %collective-permute-start.29 = (bf16[288,256]{1,0:T(8,128)(2,1)S(1)}, bf16[288,256]{1,0:T(8,128)(2,1)S(1)}, u32[]{:S(2)}, u32[]{:S(2)}) collective-permute-start(bf16[288,256]{1,0:T(8,128)(2,1)S(1)} %get-tuple-element.64), channel_id=1, source_target_pairs={{0,1},{1,0},{2,3},{3,2},{4,5},{5,4},{6,7},{7,6},{8,9},{9,8},{10,11... | collective-permute-start | bytes 442376 | tf_op jit(solution)/shard_map/ppermute | solution.py:441
  118.0 27.9 %collective-permute-start.28 = (bf16[288,256]{1,0:T(8,128)(2,1)S(1)}, bf16[288,256]{1,0:T(8,128)(2,1)S(1)}, u32[]{:S(2)}, u32[]{:S(2)}) collective-permute-start(bf16[288,256]{1,0:T(8,128)(2,1)S(1)} %add_convert_fusion.2), channel_id=1, source_target_pairs={{0,2},{1,3},{2,4},{3,5},{4,6},{5,7},{6,0},{7,1},{8,10},{9,11},{10,... | collective-permute-start | bytes 442376 | tf_op jit(solution)/shard_map/ppermute | solution.py:441
  123.4 6.8 %collective-permute-start.20 = (bf16[128,768]{1,0:T(8,128)(2,1)S(1)}, bf16[128,768]{1,0:T(8,128)(2,1)S(1)}, u32[]{:S(2)}, u32[]{:S(2)}) collective-permute-start(bf16[128,768]{1,0:T(8,128)(2,1)S(1)} %act.7.refs_7_.refs_1_), channel_id=1, source_target_pairs={{0,16},{1,17},{2,18},{3,19},{4,20},{5,21},{6,22},{7,23},{8,24},{9,... | collective-permute-start | bytes 589832 | tf_op jit(solution)/shard_map/ppermute | solution.py:441
  123.8 10.6 %collective-permute-start.21 = (bf16[128,768]{1,0:T(8,128)(2,1)S(1)}, bf16[128,768]{1,0:T(8,128)(2,1)S(1)}, u32[]{:S(2)}, u32[]{:S(2)}) collective-permute-start(bf16[128,768]{1,0:T(8,128)(2,1)S(1)} %act.7.refs_7_.refs_1_), channel_id=1, source_target_pairs={{0,8},{1,9},{2,10},{3,11},{4,12},{5,13},{6,14},{7,15},{8,0},{9,1},... | collective-permute-start | bytes 589832 | tf_op jit(solution)/shard_map/ppermute | solution.py:441
  127.3 6.3 %collective-permute-start.31 = (bf16[288,256]{1,0:T(8,128)(2,1)S(1)}, bf16[288,256]{1,0:T(8,128)(2,1)S(1)}, u32[]{:S(2)}, u32[]{:S(2)}) collective-permute-start(bf16[288,256]{1,0:T(8,128)(2,1)S(1)} %get-tuple-element.65), channel_id=1, source_target_pairs={{0,1},{1,0},{2,3},{3,2},{4,5},{5,4},{6,7},{7,6},{8,9},{9,8},{10,11... | collective-permute-start | bytes 442376 | tf_op jit(solution)/shard_map/ppermute | solution.py:441
  128.0 17.9 %collective-permute-start.30 = (bf16[288,256]{1,0:T(8,128)(2,1)S(1)}, bf16[288,256]{1,0:T(8,128)(2,1)S(1)}, u32[]{:S(2)}, u32[]{:S(2)}) collective-permute-start(bf16[288,256]{1,0:T(8,128)(2,1)S(1)} %add_convert_fusion.1), channel_id=1, source_target_pairs={{0,4},{1,5},{2,6},{3,7},{4,0},{5,1},{6,2},{7,3},{8,12},{9,13},{10,... | collective-permute-start | bytes 442376 | tf_op jit(solution)/shard_map/ppermute | solution.py:441
  130.2 4.3 %collective-permute-start.22 = (bf16[128,768]{1,0:T(8,128)(2,1)S(1)}, bf16[128,768]{1,0:T(8,128)(2,1)S(1)}, u32[]{:S(2)}, u32[]{:S(2)}) collective-permute-start(bf16[128,768]{1,0:T(8,128)(2,1)S(1)} %collective-permute-done.20.refs_2_), channel_id=1, source_target_pairs={{0,8},{1,9},{2,10},{3,11},{4,12},{5,13},{6,14},{7,15},{8,0},{9,1},... | collective-permute-start | bytes 589832 | tf_op jit(solution)/shard_map/ppermute | solution.py:441
  133.7 16.7 %copy-start.11 = (f32[2304]{0:T(1024)S(1)}, f32[2304]{0:T(1024)}, u32[]{:S(2)}) copy-start(f32[2304]{0:T(1024)} %param.19) | copy-start | bytes 27652
  133.7 16.8 %copy-start.12 = (f32[16]{0:T(128)S(1)}, f32[16]{0:T(128)}, u32[]{:S(2)}) copy-start(f32[16]{0:T(128)} %param.21) | copy-start | bytes 196
  133.7 24.3 %copy-start.6 = (bf16[2304,512]{1,0:T(8,128)(2,1)S(1)}, bf16[2304,512]{1,0:T(8,128)(2,1)}, u32[]{:S(2)}) copy-start(bf16[2304,512]{1,0:T(8,128)(2,1)} %refs_2_.1) | copy-start | bytes 7077892
  133.7 12.2 %collective-permute-start.32 = (bf16[288,256]{1,0:T(8,128)(2,1)S(1)}, bf16[288,256]{1,0:T(8,128)(2,1)S(1)}, u32[]{:S(2)}, u32[]{:S(2)}) collective-permute-start(bf16[288,256]{1,0:T(8,128)(2,1)S(1)} %add_convert_fusion), channel_id=1, source_target_pairs={{0,6},{1,7},{2,0},{3,1},{4,2},{5,3},{6,4},{7,5},{8,14},{9,15},{10,... | collective-permute-start | bytes 442376 | tf_op jit(solution)/shard_map/ppermute | solution.py:441
  137.9 44.8 %copy-start.8 = (f32[256,288]{0,1:T(8,128)S(1)}, f32[256,288]{0,1:T(8,128)}, u32[]{:S(2)}) copy-start(f32[256,288]{0,1:T(8,128)} %param.11) | copy-start | bytes 884740
  137.9 8.0 %collective-permute-start.26 = (bf16[288,256]{1,0:T(8,128)(2,1)S(1)}, bf16[288,256]{1,0:T(8,128)(2,1)S(1)}, u32[]{:S(2)}, u32[]{:S(2)}) collective-permute-start(bf16[288,256]{1,0:T(8,128)(2,1)S(1)} %get-tuple-element.62), channel_id=1, source_target_pairs={{0,1},{1,0},{2,3},{3,2},{4,5},{5,4},{6,7},{7,6},{8,9},{9,8},{10,11... | collective-permute-start | bytes 442376 | tf_op jit(solution)/shard_map/ppermute | solution.py:441
  138.6 7.3 %collective-permute-start.5 = (f32[4,288]{1,0:T(4,128)S(1)}, f32[4,288]{1,0:T(4,128)S(1)}, u32[]{:S(2)}, u32[]{:S(2)}) collective-permute-start(f32[4,288]{1,0:T(4,128)S(1)} %get-tuple-element.37), channel_id=1, source_target_pairs={{0,0},{1,1},{2,8},{3,9},{4,16},{5,17},{6,24},{7,25},{8,2},{9,3},{1... | collective-permute-start | bytes 13832 | tf_op jit(solution)/shard_map/ppermute | solution.py:441
  147.0 11.0 %all-to-all-start = ((f32[32,4,288]{2,1,0:T(4,128)}), f32[32,4,288]{2,1,0:T(4,128)S(1)}, u32[]{:S(2)}, u32[]{:S(2)}) async-start(f32[32,4,288]{2,1,0:T(4,128)} %get-tuple-element.67), calls=%async_computation | async-start | bytes 393216 | tf_op jit(solution)/shard_map/all_to_all | solution.py:522
  159.5 10.0 %all-to-all-start.1 = ((f32[32,2,16]{2,1,0:T(2,128)}), f32[32,2,16]{2,1,0:T(2,128)S(1)}, u32[]{:S(2)}, u32[]{:S(2)}) async-start(f32[32,2,16]{2,1,0:T(2,128)} %get-tuple-element.69), calls=%async_computation.1 | async-start | bytes 65536 | tf_op jit(solution)/shard_map/all_to_all | solution.py:522
  163.4 19.3 %collective-permute-start.33 = (f32[288,256]{1,0:T(8,128)S(1)}, f32[288,256]{1,0:T(8,128)S(1)}, u32[]{:S(2)}, u32[]{:S(2)}) collective-permute-start(f32[288,256]{1,0:T(8,128)S(1)} %get-tuple-element.66), channel_id=1, source_target_pairs={{0,0},{1,1},{2,8},{3,9},{4,16},{5,17},{6,24},{7,25},{8,2},{9,3},{1... | collective-permute-start | bytes 884744 | tf_op jit(solution)/shard_map/ppermute | solution.py:441
  (1 other events, 0.7 us)

commit v7 on v6

--- a/solution.py
+++ b/solution.py
@@ -17,7 +17,6 @@
 VMEM = pl.BlockSpec(memory_space=pltpu.VMEM)
 SMEM = pl.BlockSpec(memory_space=pltpu.SMEM)
 ANY = pl.BlockSpec(memory_space=pl.ANY)
-HBM = pl.BlockSpec(memory_space=pltpu.HBM)
 
 
 def up_to(n, step=LANES):
@@ -125,19 +124,8 @@
 
 def partial_kernel(sides, held, scal, *refs):
     feeds, (wr, wg, wu) = refs[:held], refs[held : held + 3]
-    own, give, cols, xs, xt, acc, extra, ring, sems = refs[-9:]
+    own, give, cols, xs, xt, acc, extra = refs[-7:]
     e = pl.program_id(0)
-    experts = wg.shape[0]
-
-    def fetch(n, slot, which):
-        return pltpu.make_async_copy((wg, wu)[which].at[n], ring.at[slot, which], sems.at[slot, which])
-
-    @pl.when(e == 0)
-    def _():
-        for n in range(min(2, experts)):
-            for which in range(2):
-                fetch(n, n, which).start()
-
     core, side = scal[0], scal[1]
     depth, hidden = wg.shape[1:]
     deep, half = up_to(depth), up_to(hidden)
@@ -175,22 +163,15 @@
     mine, other = slot_columns(core, xt[:, deep : deep + LANES])
     ef = e.astype(f32)
     take = [(v == ef) | (e == 0) for v in (mine, other)]
-    slot = e % 2
-    for which in range(2):
-        fetch(e, slot, which).wait()
+    for which, w in enumerate((wg, wu)):
         for at in range(0, hidden, 256):
             end = min(hidden, at + 256)
-            d = jnp.dot(xt[:, 0:depth], ring[slot, which, :, at:end], preferred_element_type=f32)
+            d = jnp.dot(xt[:, 0:depth], w[0, :, at:end], preferred_element_type=f32)
             to = slice(which * half + at, which * half + end)
             for ref, pick in ((own, take[0]), (acc, take[1])):
                 ref[:, to] = jnp.where(pick, d, ref[:, to])
 
-    @pl.when(e + 2 < experts)
-    def _():
-        for which in range(2):
-            fetch(e + 2, slot, which).start()
-
-    @pl.when(e == experts - 1)
+    @pl.when(e == pl.num_programs(0) - 1)
     def _():
         lane = lax.broadcasted_iota(jnp.int32, extra.shape, 1)
         more = extra[...]
@@ -201,27 +182,35 @@
 
 def partial_call(scal, sides, feeds, wr, wg, wu, deps):
     experts, depth, hidden = wg.shape
-    tokens = feeds[0].shape[1] * len(feeds)
+    tokens = feeds[0][0].shape[-1] * len(feeds)
     deep, wide = up_to(depth), 2 * up_to(hidden)
+    part = pl.BlockSpec((1, depth, hidden), lambda n, s: (n, 0, 0))
     outs = [shape((tokens, wide), f32), shape((tokens, wide), bf16), shape((tokens, LANES), bf16)]
+    feed_specs = []
+    for v, place in feeds:
+        if place is None:
+            feed_specs.append(whole_spec(v))
+        else:
+            feed_specs.append(pl.BlockSpec((None, *v.shape[1:]), lambda n, s, place=place: (s[place], 0, 0)))
     return pl.pallas_call(
         lambda *refs: partial_kernel(sides, len(feeds), *refs),
-        grid=(experts,),
-        in_specs=[SMEM] + [whole_spec(v) for v in feeds] + [whole_spec(wr), HBM, HBM] + [ANY] * len(deps),
-        out_specs=[whole_spec(v) for v in outs],
+        grid_spec=pltpu.PrefetchScalarGridSpec(
+            num_scalar_prefetch=1,
+            grid=(experts,),
+            in_specs=feed_specs + [whole_spec(wr), part, part] + [ANY] * len(deps),
+            out_specs=[whole_spec(v) for v in outs],
+            scratch_shapes=[
+                pltpu.VMEM((deep + LANES, tokens), bf16),
+                pltpu.VMEM((tokens, deep + LANES), bf16),
+                pltpu.VMEM((tokens, wide), f32),
+                pltpu.VMEM((tokens, LANES), f32),
+            ],
+        ),
         out_shape=outs,
-        scratch_shapes=[
-            pltpu.VMEM((deep + LANES, tokens), bf16),
-            pltpu.VMEM((tokens, deep + LANES), bf16),
-            pltpu.VMEM((tokens, wide), f32),
-            pltpu.VMEM((tokens, LANES), f32),
-            pltpu.VMEM((2, 2, depth, hidden), bf16),
-            pltpu.SemaphoreType.DMA((2, 2)),
-        ],
         compiler_params=params(20),
         cost_estimate=HINT,
         name="gate_up_partial",
-    )(scal, *feeds, wr, wg, wu, *deps)
+    )(scal, *[v for v, _ in feeds], wr, wg, wu, *deps)
 
 
 def sum_kernel(base, scal, own, recv, *refs):
@@ -254,6 +243,7 @@
     core, y = scal[0], scal[2]
     th, half = act.shape
     main = 2 * half - LANES
+    recv = recv.at[1 - y]
     m = keep[:, main:] + joined_lanes(recv[:, main:].astype(f32), base)
     mine, other = slot_columns(core, cols[pl.ds(pl.multiple_of(y * th, th), th)])
     scale = lax.rsqrt(m[:, base : base + 1] / WIDTH + epsilon)
@@ -281,24 +271,15 @@
     )(scal, keep, recv, cols, *deps)
 
 
-def down_kernel(sides, scal, a, a_y, b, b_y, cols, wd, *refs):
-    outs = refs[-sides - 2 : -2]
-    whole, acc = refs[-2:]
+def down_kernel(sides, scal, mine, other, cols, wd, *refs):
+    outs, acc = refs[-sides - 1 : -1], refs[-1]
     e = pl.program_id(0)
-    core, side, y = scal[0], scal[1], scal[2]
-    th = a.shape[0]
+    core, side = scal[0], scal[1]
     width, hidden = wd.shape[1:]
     block = width // sides
-
-    @pl.when(e == 0)
-    def _():
-        for k, near, far in ((0, a, a_y), (1, b, b_y)):
-            whole[k, pl.ds(pl.multiple_of(y * th, th), th)] = near[...]
-            whole[k, pl.ds(pl.multiple_of((1 - y) * th, th), th)] = far[...]
-
     ef = e.astype(f32)
     masks = [jnp.where(v == ef, 1.0, 0.0).astype(bf16) for v in slot_columns(core, cols[...])]
-    rows = whole[0, :, 0:hidden] * masks[0] + whole[1, :, 0:hidden] * masks[1]
+    rows = mine[:, 0:hidden] * masks[0] + other[:, 0:hidden] * masks[1]
     d = lax.dot_general(wd[0], rows, (((1,), (1,)), ((), ())), preferred_element_type=f32)
 
     @pl.when(e == 0)
@@ -329,43 +310,37 @@
         + [ANY] * len(deps),
         out_specs=[whole_spec(v) for v in outs],
         out_shape=outs,
-        scratch_shapes=[
-            pltpu.VMEM((2, tokens, pieces[0].shape[1]), bf16),
-            pltpu.VMEM((width, tokens), f32),
-        ],
-        compiler_params=params(20),
+        scratch_shapes=[pltpu.VMEM((width, tokens), f32)],
+        compiler_params=params(16),
         cost_estimate=HINT,
         name="down",
     )(scal, *pieces, cols, wd, *deps)
 
 
-def total_kernel(meta, stream, *refs):
+def total_kernel(cols, stream, *refs):
     parts, (total, message) = refs[:-2], refs[-2:]
     v = parts[0][...].astype(f32)
     for ref in parts[1:]:
         v = v + ref[...].astype(f32)
     total[...] = v
     reqs = stream.shape[0]
-    ends = columns_at(meta[5:6].astype(f32), v)
+    ends = columns_at(cols[...].astype(f32).T[5:6], v)
     ends = stream[...] + branch_scale * ends[0:reqs]
     message[...] = jnp.broadcast_to(ends[None], message.shape)
 
 
-def total_call(feed, stream, parts, block, count):
-    tokens = feed.shape[1]
-    full = lambda v: pl.BlockSpec(v.shape, lambda n: (0,) * len(v.shape))
-    outs = [shape((block, tokens), f32), shape((count, *stream.shape), f32)]
+def total_call(cols, stream, parts, block, count):
+    outs = [shape((block, cols.shape[0]), f32), shape((count, *stream.shape), f32)]
     return pl.pallas_call(
         total_kernel,
         grid=(1,),
-        in_specs=[pl.BlockSpec((META, tokens), lambda n: (block // META, 0)), full(stream)]
-        + [full(v) for v in parts],
-        out_specs=[full(v) for v in outs],
+        in_specs=[whole_spec(v) for v in (cols, stream, *parts)],
+        out_specs=[whole_spec(v) for v in outs],
         out_shape=outs,
         compiler_params=params(),
         cost_estimate=HINT,
         name="branch_total",
-    )(feed, stream, *parts)
+    )(cols, stream, *parts)
 
 
 def head_kernel(order, got, gain, words, softness, logits, message, wide):
@@ -427,7 +402,7 @@
     assert dp == parts * spread and mp == parts * sides and sides & (sides - 1) == 0
     part = lax.axis_index("dp") // spread
     y, core = part // 2, part % 2
-    side = lax.axis_index("mp") % sides
+    side, z = lax.axis_index("mp") % sides, lax.axis_index("mp") // sides
 
     def send(value, to):
         pairs = []
@@ -441,10 +416,9 @@
         return lax.ppermute(value, ("dp", "mp"), pairs)
 
     other_core = lambda q, z, x: (q ^ 1, z, x)
-    other_y = lambda q, z, x: (q ^ 2, z, x)
     home = lambda q, z, x: (z, q, x)
 
-    scal = jnp.stack([core, side, y]).astype(jnp.int32)
+    scal = jnp.stack([core, side, y] + [(z + s) % parts for s in range(parts)]).astype(jnp.int32)
     sent, stream = prep_call(
         skip_stream_arriving.T, premix_rmsnorm_gain[None], chosen_specialists.T, sequence_piece_tallies
     )
@@ -464,9 +438,11 @@
     chunks = ((1,), (2,), (3,), (0,))
     first = [send(sent, lambda q, z, x, i=i: (z, (q - 1) % parts, x ^ i)) for i in range(sides)]
     pair = join_call(first)
-    feeds = {1: pair}
-    for group in (2, 3, 0):
-        feeds[group] = send(feeds[(group - 1) % parts], lambda q, z, x: (q, (z - 1) % parts, x))
+    along_z = [[n * sides + x for n in range(parts)] for x in range(sides)]
+    along_y = [[(q + n) * spread + r for n in (0, 2)] for q in range(2) for r in range(spread)]
+    pairs = lax.all_gather(pair, "mp", axis_index_groups=along_z)
+    feeds = {1: (pair, None), 2: (send(pair, lambda q, z, x: (q, (z - 1) % parts, x)), None)}
+    feeds |= {3: (pairs, 3 + 2), 0: (pairs, 3 + 3)}
     stream = send(stream, home)
     partial, kept, pieces, shares = {}, {}, {}, {}
 
@@ -478,13 +454,13 @@
     def do_sum(s, *deps):
         own, recv, _ = partial[s]
         keep, give = sum_call(scal, base, own, recv, deps)
-        kept[s] = (keep, send(give, other_y))
+        kept[s] = (keep, lax.all_gather(give, "dp", axis_index_groups=along_y))
         return keep
 
     def do_act(s, *deps):
         a = act_call(scal, base, *kept[s], partial[s][2], deps)
-        a_y = send(a, other_y)
-        pieces[s] = (a, a_y, send(a, other_core), send(a_y, other_core))
+        both = lax.all_gather(a, "dp", axis_index_groups=along_y, tiled=True)
+        pieces[s] = (both, send(both, other_core))
         return a
 
     def do_down(s, *deps):
@@ -503,21 +479,21 @@
     p0 = do_partial(0)
     p1 = do_partial(1, p0)
     s0 = do_sum(0, p1)
-    p2 = do_partial(2, s0)
-    s1 = do_sum(1, p2)
-    p3 = do_partial(3, s1)
+    s1 = do_sum(1, s0)
+    p2 = do_partial(2, s1)
+    a0 = do_act(0, p2)
+    p3 = do_partial(3, a0)
     s2 = do_sum(2, p3)
-    a0 = do_act(0, s2)
-    s3 = do_sum(3, a0)
-    a1 = do_act(1, s3)
-    d0 = do_down(0, a1)
+    a1 = do_act(1, s2)
+    s3 = do_sum(3, a1)
+    d0 = do_down(0, s3)
     a2 = do_act(2, d0)
     d1 = do_down(1, a2)
     a3 = do_act(3, d1)
     d2 = do_down(2, a3)
     do_down(3, d2)
     mine = [v for group in range(parts) for v in shares[group]]
-    total, message = total_call(feeds[0], stream, mine, block, count)
+    total, message = total_call(partial[parts - 1][2], stream, mine, block, count)
 
     everyone = lambda v: lax.all_to_all(v, ("dp", "mp"), 0, 0, tiled=True)
     got = everyone(message)

time: 184 us -> 233 us (1.27)
  blocking collectives: 0 us -> 77.2 us
  waiting for transfers between devices: 78.3 us -> 43 us
  between operations: 1.02 us -> 14.4 us
  Pallas kernels: 57.3 us -> 46.8 us
  local copies, waits for them, and re-layouts: 7.3 us -> 12.8 us
    all_gather x0 -> x8, blocking collectives: none -> 77.2 us  [the longest x4 48.7 us: do_sum(): kept[s] = (keep, lax.all_gather(give, 'dp', axis_index_groups=along_y))]
    ppermute x34 -> x20, waiting for transfers between devices: 69.1 us -> 24.1 us  [send(): return lax.ppermute(value, ('dp', 'mp'), pairs)]
    pallas_call x4, Pallas kernels: 31.7 us -> 20.6 us  [partial_call(): pl.pallas_call(lambda *refs: partial_kernel(sides, len(feeds), *refs), gr...]
    all_gather x0 -> x1, waiting for transfers between devices: none -> 9.62 us  [body(): pairs = lax.all_gather(pair, 'mp', axis_index_groups=along_z)]
    unnamed x26 -> x34, local copies, waits for them, and re-layouts: 6.34 us -> 11.8 us
    ppermute x34 -> x20, starting transfers between devices: 30.6 us -> 28.4 us  [send(): return lax.ppermute(value, ('dp', 'mp'), pairs)]
  transfers between devices with their start and end apart: 36 -> 23, of which waited for: 15 -> 8; matrix products, arithmetic and copies ran while one was open for 1% -> 1% of each run, Pallas kernels for 29% -> 16%
where the time goes in v7:
time: 233 us
  blocking collectives  77.2 us (33%)
  Pallas kernels  46.8 us (20%)
  waiting for transfers between devices  43 us (18%)
  starting transfers between devices  36.8 us (16%)
  between operations  14.4 us (6%)
  local copies, waits for them, and re-layouts  12.8 us (5%)
    all_gather x4, blocking collectives, do_sum(): kept[s] = (keep, lax.all_gather(give, 'dp', axis_index_groups=along_y))  48.7 us
    all_gather x4, blocking collectives, do_act(): both = lax.all_gather(a, 'dp', axis_index_groups=along_y, tiled=True)  28.6 us
    ppermute x20, starting transfers between devices, send(): return lax.ppermute(value, ('dp', 'mp'), pairs)  28.4 us
    ppermute x20, waiting for transfers between devices, send(): return lax.ppermute(value, ('dp', 'mp'), pairs)  24.1 us
    pallas_call x4, Pallas kernels, partial_call(): pl.pallas_call(lambda *refs: partial_kernel(sides, len(feeds), *refs), gr...  20.6 us
    pallas_call x4, Pallas kernels, down_call(): pl.pallas_call(lambda *refs: down_kernel(sides, *refs), grid=(experts,),...  13.6 us
    unnamed x34, local copies, waits for them, and re-layouts  11.8 us
    all_gather x1, waiting for transfers between devices, body(): pairs = lax.all_gather(pair, 'mp', axis_index_groups=along_z)  9.62 us
  transfers between devices with their start and end apart: 23, of which 8 were waited for; matrix products, arithmetic and copies ran while one was open for 1% of the time, Pallas kernels for 16%

profile of v7, /device:TPU:4, one launch (start us, length us, event | category | flops | bytes accessed | tf_op | source)
XLA Modules:
  0.0 232.6 jit_solution(5816769178257925138)
XLA Ops:
  7.9 1.0 copy-done.11
  10.2 0.9 prep.1
  11.1 1.5 collective-permute-start
  12.6 3.0 %collective-permute-start.1 = (bf16[304,256]{1,0:T(8,128)(2,1)S(1)}, bf16[304,256]{1,0:T(8,128)(2,1)S(1)}, u32[]{:S(2)}, u32[]{:S(2)}) collective-permute-start(bf16[304,256]{1,0:T(8,128)(2,1)S(1)} %get-tuple-element.36), channel_id=1, source_target_pairs={{0,7},{1,6},{2,15},{3,14},{4,23},{5,22},{6,31},{7,30},{8,1},{9,0},... | collective-permute-start | bytes 466952 | tf_op jit(solution)/shard_map/ppermute | solution.py:416
  15.6 3.8 %collective-permute-done.refs_0_ = bf16[304,256]{1,0:T(8,128)(2,1)S(1)} collective-permute-done((bf16[304,256]{1,0:T(8,128)(2,1)S(1)}, bf16[304,256]{1,0:T(8,128)(2,1)S(1)}, u32[]{:S(2)}, u32[]{:S(2)}) %collective-permute-start) | collective-permute-done | bytes 155680 | tf_op jit(solution)/shard_map/ppermute | solution.py:416
  19.3 4.3 %collective-permute-done.1.refs_1_ = bf16[304,256]{1,0:T(8,128)(2,1)S(1)} collective-permute-done((bf16[304,256]{1,0:T(8,128)(2,1)S(1)}, bf16[304,256]{1,0:T(8,128)(2,1)S(1)}, u32[]{:S(2)}, u32[]{:S(2)}) %collective-permute-start.1) | collective-permute-done | bytes 155680 | tf_op jit(solution)/shard_map/ppermute | solution.py:416
  24.4 5.9 %collective-permute-start.3 = (bf16[608,256]{1,0:T(8,128)(2,1)}, bf16[608,256]{1,0:T(8,128)(2,1)S(1)}, u32[]{:S(2)}, u32[]{:S(2)}) collective-permute-start(bf16[608,256]{1,0:T(8,128)(2,1)} %join.1.refs_1_), channel_id=1, source_target_pairs={{0,6},{1,7},{2,0},{3,1},{4,2},{5,3},{6,4},{7,5},{8,14},{9,15},{10,... | collective-permute-start | bytes 933896 | tf_op jit(solution)/shard_map/ppermute | solution.py:416
  30.5 2.0 copy-done.1
  32.5 2.1 copy-done.4
  34.6 6.2 %gate_up_partial.4 = (f32[256,1536]{1,0:T(8,128)S(1)}, bf16[256,1536]{1,0:T(8,128)(2,1)S(1)}, bf16[256,128]{1,0:T(8,128)(2,1)S(1)}) custom-call(s32[7]{0:T(128)S(1)} %stack.31.refs_0_, bf16[608,256]{1,0:T(8,128)(2,1)} %join.1.refs_1_, bf16[128,576]{1,0:T(8,128)(2,1)S(1)} %pad_add_fusion.refs_2_, bf16[4,576,720]{2,1,0:T(8,128)(2,1)S(1)} %copy-done.1, ...), custom_call_target="tpu_custom_call" | custom-call | flops 1 | bytes 1024 | tf_op jit(solution)/shard_map/gate_up_partial/pallas_call | solution.py:195
  40.9 4.8 %gate_up_partial.5 = (f32[256,1536]{1,0:T(8,128)S(1)}, bf16[256,1536]{1,0:T(8,128)(2,1)S(1)}, bf16[256,128]{1,0:T(8,128)(2,1)S(1)}) custom-call(s32[7]{0:T(128)S(1)} %stack.31.refs_0_, bf16[608,256]{1,0:T(8,128)(2,1)S(1)} %collective-permute-done.3.refs_1_, bf16[128,576]{1,0:T(8,128)(2,1)S(1)} %pad_add_fusion.refs_2_, bf16[4,576,720]{2,1,0:T(8,128)(2,1)S(1)} %copy-done.2, ...), custom_call_target="tpu_custom_call" | custom-call | flops 1 | bytes 1024 | tf_op jit(solution)/shard_map/gate_up_partial/pallas_call | solution.py:195
  47.1 1.0 collective-permute-done.4.refs_2_
  49.0 9.6 %all-gather.7.cloned.1.call-done = bf16[2432,256]{1,0:T(8,128)(2,1)} async-done(((bf16[608,256]{1,0:T(8,128)(2,1)}), bf16[2432,256]{1,0:T(8,128)(2,1)}) %all-gather.7.cloned.1.call-update) | async-done | bytes 1245200 | tf_op jit(solution)/shard_map/all_gather | solution.py:443
  58.7 2.0 copy-done.3
  60.7 2.0 copy-done.6
  62.7 1.3 copy-done.8
  64.0 4.8 %gate_up_partial.6 = (f32[256,1536]{1,0:T(8,128)S(1)}, bf16[256,1536]{1,0:T(8,128)(2,1)S(1)}, bf16[256,128]{1,0:T(8,128)(2,1)S(1)}) custom-call(s32[7]{0:T(128)S(1)} %stack.31.refs_0_, bf16[4,608,256]{2,1,0:T(8,128)(2,1)S(1)} %bitcast.28, bf16[128,576]{1,0:T(8,128)(2,1)S(1)} %pad_add_fusion.refs_2_, bf16[4,576,720]{2,1,0:T(8,128)(2,1)S(1)} %copy-done.3, ...), custom_call_target="tpu_custom_call" | custom-call | flops 1 | bytes 1024 | tf_op jit(solution)/shard_map/gate_up_partial/pallas_call | solution.py:195
  68.9 12.2 %all-gather.1 = bf16[256,1536]{1,0:T(8,128)(2,1)S(1)} all-gather(bf16[128,1536]{1,0:T(8,128)(2,1)S(1)} %get-tuple-element.41), channel_id=3, replica_groups={{0,16},{8,24},{1,17},{9,25},{2,18},{10,26},{3,19},{11,27},{4,20},{12,28..., dimensions={0}, use_global_device_ids=true | all-gather | bytes 1179648 | tf_op jit(solution)/shard_map/all_gather | solution.py:457
  81.1 1.2 act.4.refs_5_
  82.3 4.8 %gate_up_partial.7 = (f32[256,1536]{1,0:T(8,128)S(1)}, bf16[256,1536]{1,0:T(8,128)(2,1)S(1)}, bf16[256,128]{1,0:T(8,128)(2,1)S(1)}) custom-call(s32[7]{0:T(128)S(1)} %stack.31.refs_0_, bf16[4,608,256]{2,1,0:T(8,128)(2,1)S(1)} %bitcast.29, bf16[128,576]{1,0:T(8,128)(2,1)S(1)} %pad_add_fusion.refs_2_, bf16[4,576,720]{2,1,0:T(8,128)(2,1)S(1)} %copy-done.3, ...), custom_call_target="tpu_custom_call" | custom-call | flops 1 | bytes 1024 | tf_op jit(solution)/shard_map/gate_up_partial/pallas_call | solution.py:195
  87.3 8.0 %all_gather.53.refs_1_ = bf16[256,768]{1,0:T(8,128)(2,1)S(1)} all-gather(bf16[128,768]{1,0:T(8,128)(2,1)S(1)} %act.4.refs_5_), channel_id=1, replica_groups={{0,16},{8,24},{1,17},{9,25},{2,18},{10,26},{3,19},{11,27},{4,20},{12,28..., dimensions={0}, use_global_device_ids=true | all-gather | bytes 589824 | tf_op jit(solution)/shard_map/all_gather | solution.py:462
  95.2 12.2 %all-gather.2 = bf16[256,1536]{1,0:T(8,128)(2,1)S(1)} all-gather(bf16[128,1536]{1,0:T(8,128)(2,1)S(1)} %get-tuple-element.50), channel_id=4, replica_groups={{0,16},{8,24},{1,17},{9,25},{2,18},{10,26},{3,19},{11,27},{4,20},{12,28..., dimensions={0}, use_global_device_ids=true | all-gather | bytes 1179648 | tf_op jit(solution)/shard_map/all_gather | solution.py:457
  108.3 1.2 act.5.refs_3_
  109.5 7.2 %all_gather.50.refs_1_ = bf16[256,768]{1,0:T(8,128)(2,1)S(1)} all-gather(bf16[128,768]{1,0:T(8,128)(2,1)S(1)} %act.5.refs_3_), channel_id=1, replica_groups={{0,16},{8,24},{1,17},{9,25},{2,18},{10,26},{3,19},{11,27},{4,20},{12,28..., dimensions={0}, use_global_device_ids=true | all-gather | bytes 589824 | tf_op jit(solution)/shard_map/all_gather | solution.py:462
  117.6 12.2 %all-gather.4 = bf16[256,1536]{1,0:T(8,128)(2,1)S(1)} all-gather(bf16[128,1536]{1,0:T(8,128)(2,1)S(1)} %get-tuple-element.56), channel_id=6, replica_groups={{0,16},{8,24},{1,17},{9,25},{2,18},{10,26},{3,19},{11,27},{4,20},{12,28..., dimensions={0}, use_global_device_ids=true | all-gather | bytes 1179648 | tf_op jit(solution)/shard_map/all_gather | solution.py:457
  129.8 3.4 %down.4 = (bf16[288,256]{1,0:T(8,128)(2,1)S(1)}, bf16[288,256]{1,0:T(8,128)(2,1)S(1)}) custom-call(s32[7]{0:T(128)S(1)} %stack.31.refs_0_, bf16[256,768]{1,0:T(8,128)(2,1)S(1)} %all_gather.53.refs_1_, bf16[256,768]{1,0:T(8,128)(2,1)S(1)} %collective-permute-done.9.refs_2_, bf16[256,128]{1,0:T(8,128)(2,1)S(1)} %get-tuple-element.42.refs_3_, ...), custom_call_target="tpu_custom_call" | custom-call | flops 1 | bytes 1024 | tf_op jit(solution)/shard_map/down/pallas_call | solution.py:304
  133.2 1.2 act.6.refs_5_
  134.5 7.0 %all_gather.55.refs_1_ = bf16[256,768]{1,0:T(8,128)(2,1)S(1)} all-gather(bf16[128,768]{1,0:T(8,128)(2,1)S(1)} %act.6.refs_5_), channel_id=1, replica_groups={{0,16},{8,24},{1,17},{9,25},{2,18},{10,26},{3,19},{11,27},{4,20},{12,28..., dimensions={0}, use_global_device_ids=true | all-gather | bytes 589824 | tf_op jit(solution)/shard_map/all_gather | solution.py:462
  141.5 1.5 collective-permute-start.13
  143.0 12.1 %all-gather.3 = bf16[256,1536]{1,0:T(8,128)(2,1)S(1)} all-gather(bf16[128,1536]{1,0:T(8,128)(2,1)S(1)} %get-tuple-element.55), channel_id=5, replica_groups={{0,16},{8,24},{1,17},{9,25},{2,18},{10,26},{3,19},{11,27},{4,20},{12,28..., dimensions={0}, use_global_device_ids=true | all-gather | bytes 1179648 | tf_op jit(solution)/shard_map/all_gather | solution.py:457
  155.1 3.4 %down.5 = (bf16[288,256]{1,0:T(8,128)(2,1)S(1)}, bf16[288,256]{1,0:T(8,128)(2,1)S(1)}) custom-call(s32[7]{0:T(128)S(1)} %stack.31.refs_0_, bf16[256,768]{1,0:T(8,128)(2,1)S(1)} %all_gather.50.refs_1_, bf16[256,768]{1,0:T(8,128)(2,1)S(1)} %collective-permute-done.8.refs_2_, bf16[256,128]{1,0:T(8,128)(2,1)S(1)} %get-tuple-element.51.refs_3_, ...), custom_call_target="tpu_custom_call" | custom-call | flops 1 | bytes 1024 | tf_op jit(solution)/shard_map/down/pallas_call | solution.py:304
  158.5 1.2 act.7.refs_5_
  159.7 3.4 %down.6 = (bf16[288,256]{1,0:T(8,128)(2,1)S(1)}, bf16[288,256]{1,0:T(8,128)(2,1)S(1)}) custom-call(s32[7]{0:T(128)S(1)} %stack.31.refs_0_, bf16[256,768]{1,0:T(8,128)(2,1)S(1)} %all_gather.55.refs_1_, bf16[256,768]{1,0:T(8,128)(2,1)S(1)} %collective-permute-done.11.refs_2_, bf16[256,128]{1,0:T(8,128)(2,1)S(1)} %get-tuple-element.57.refs_3_, ...), custom_call_target="tpu_custom_call" | custom-call | flops 1 | bytes 1024 | tf_op jit(solution)/shard_map/down/pallas_call | solution.py:304
  163.8 0.9 collective-permute-start.14
  164.7 1.5 collective-permute-start.15
  166.2 6.3 %all_gather.54.refs_1_ = bf16[256,768]{1,0:T(8,128)(2,1)S(1)} all-gather(bf16[128,768]{1,0:T(8,128)(2,1)S(1)} %act.7.refs_5_), channel_id=1, replica_groups={{0,16},{8,24},{1,17},{9,25},{2,18},{10,26},{3,19},{11,27},{4,20},{12,28..., dimensions={0}, use_global_device_ids=true | all-gather | bytes 589824 | tf_op jit(solution)/shard_map/all_gather | solution.py:462
  172.6 3.0 %collective-permute-start.18 = (bf16[288,256]{1,0:T(8,128)(2,1)S(1)}, bf16[288,256]{1,0:T(8,128)(2,1)S(1)}, u32[]{:S(2)}, u32[]{:S(2)}) collective-permute-start(bf16[288,256]{1,0:T(8,128)(2,1)S(1)} %add_convert_fusion), channel_id=1, source_target_pairs={{0,6},{1,7},{2,0},{3,1},{4,2},{5,3},{6,4},{7,5},{8,14},{9,15},{10,... | collective-permute-start | bytes 442376 | tf_op jit(solution)/shard_map/ppermute | solution.py:416
  175.8 3.4 %down.7 = (bf16[288,256]{1,0:T(8,128)(2,1)S(1)}, bf16[288,256]{1,0:T(8,128)(2,1)S(1)}) custom-call(s32[7]{0:T(128)S(1)} %stack.31.refs_0_, bf16[256,768]{1,0:T(8,128)(2,1)S(1)} %all_gather.54.refs_1_, bf16[256,768]{1,0:T(8,128)(2,1)S(1)} %collective-permute-done.10.refs_2_, bf16[256,128]{1,0:T(8,128)(2,1)S(1)} %get-tuple-element.46.refs_3_.cols, ...), custom_call_target="tpu_custom_call" | custom-call | flops 1 | bytes 1024 | tf_op jit(solution)/shard_map/down/pallas_call | solution.py:304
  179.8 4.8 %collective-permute-start.5 = (f32[4,288]{1,0:T(4,128)S(1)}, f32[4,288]{1,0:T(4,128)S(1)}, u32[]{:S(2)}, u32[]{:S(2)}) collective-permute-start(f32[4,288]{1,0:T(4,128)S(1)} %get-tuple-element.47), channel_id=1, source_target_pairs={{0,0},{1,1},{2,8},{3,9},{4,16},{5,17},{6,24},{7,25},{8,2},{9,3},{1... | collective-permute-start | bytes 13832 | tf_op jit(solution)/shard_map/ppermute | solution.py:416
  184.5 2.5 %collective-permute-done.5.stream = f32[4,288]{1,0:T(4,128)S(1)} collective-permute-done((f32[4,288]{1,0:T(4,128)S(1)}, f32[4,288]{1,0:T(4,128)S(1)}, u32[]{:S(2)}, u32[]{:S(2)}) %collective-permute-start.5) | collective-permute-done | bytes 4640 | tf_op jit(solution)/shard_map/ppermute | solution.py:416
  187.1 1.1 branch_total.1
  188.2 4.4 %all-to-all-start = ((f32[32,4,288]{2,1,0:T(4,128)}), f32[32,4,288]{2,1,0:T(4,128)S(1)}, u32[]{:S(2)}, u32[]{:S(2)}) async-start(f32[32,4,288]{2,1,0:T(4,128)} %get-tuple-element.67), calls=%async_computation | async-start | bytes 393216 | tf_op jit(solution)/shard_map/all_to_all | solution.py:498
  192.8 7.5 %all-to-all-done.refs_0_ = f32[32,4,288]{2,1,0:T(4,128)S(1)} async-done(((f32[32,4,288]{2,1,0:T(4,128)}), f32[32,4,288]{2,1,0:T(4,128)S(1)}, u32[]{:S(2)}, u32[]{:S(2)}) %all-to-all-start) | async-done | bytes 147488 | tf_op jit(solution)/shard_map/all_to_all | solution.py:498
  200.3 1.4 head.1
  201.8 3.9 %all-to-all-start.1 = ((f32[32,2,16]{2,1,0:T(2,128)}), f32[32,2,16]{2,1,0:T(2,128)S(1)}, u32[]{:S(2)}, u32[]{:S(2)}) async-start(f32[32,2,16]{2,1,0:T(2,128)} %get-tuple-element.69), calls=%async_computation.1 | async-start | bytes 65536 | tf_op jit(solution)/shard_map/all_to_all | solution.py:498
  205.7 4.3 %collective-permute-start.19 = (f32[288,256]{1,0:T(8,128)S(1)}, f32[288,256]{1,0:T(8,128)S(1)}, u32[]{:S(2)}, u32[]{:S(2)}) collective-permute-start(f32[288,256]{1,0:T(8,128)S(1)} %get-tuple-element.66), channel_id=1, source_target_pairs={{0,0},{1,1},{2,8},{3,9},{4,16},{5,17},{6,24},{7,25},{8,2},{9,3},{1... | collective-permute-start | bytes 884744 | tf_op jit(solution)/shard_map/ppermute | solution.py:416
  210.0 1.8 all-to-all-done.1
  212.5 12.5 %collective-permute-done.19 = f32[288,256]{1,0:T(8,128)S(1)} collective-permute-done((f32[288,256]{1,0:T(8,128)S(1)}, f32[288,256]{1,0:T(8,128)S(1)}, u32[]{:S(2)}, u32[]{:S(2)}) %collective-permute-start.19) | collective-permute-done | bytes 294944 | tf_op jit(solution)/shard_map/ppermute | solution.py:416
  (76 shorter events, 10.4 us)
Async XLA Ops:
  7.2 23.2 %copy-start = (bf16[2304,4]{0,1:T(4,128)(2,1)S(1)}, bf16[2304,4]{0,1:T(4,128)(2,1)}, u32[]{:S(2)}) copy-start(bf16[2304,4]{0,1:T(4,128)(2,1)} %param.15) | copy-start | bytes 55300
  7.2 51.5 %all-gather.7.cloned.1.call-start = ((), (), s32[]{:S(2)}) async-start(), calls=%async_computation.2 | async-start | bytes 1556480 | tf_op jit(solution)/shard_map/all_gather | solution.py:443
  7.9 1.0 copy-start.11
  8.9 0.7 copy-start.13
  9.6 0.7 copy-start.14
  11.1 8.2 %collective-permute-start = (bf16[304,256]{1,0:T(8,128)(2,1)S(1)}, bf16[304,256]{1,0:T(8,128)(2,1)S(1)}, u32[]{:S(2)}, u32[]{:S(2)}) collective-permute-start(bf16[304,256]{1,0:T(8,128)(2,1)S(1)} %get-tuple-element.36), channel_id=1, source_target_pairs={{0,6},{1,7},{2,14},{3,15},{4,22},{5,23},{6,30},{7,31},{8,0},{9,1},... | collective-permute-start | bytes 466952 | tf_op jit(solution)/shard_map/ppermute | solution.py:416
  12.6 11.0 %collective-permute-start.1 = (bf16[304,256]{1,0:T(8,128)(2,1)S(1)}, bf16[304,256]{1,0:T(8,128)(2,1)S(1)}, u32[]{:S(2)}, u32[]{:S(2)}) collective-permute-start(bf16[304,256]{1,0:T(8,128)(2,1)S(1)} %get-tuple-element.36), channel_id=1, source_target_pairs={{0,7},{1,6},{2,15},{3,14},{4,23},{5,22},{6,31},{7,30},{8,1},{9,0},... | collective-permute-start | bytes 466952 | tf_op jit(solution)/shard_map/ppermute | solution.py:416
  24.4 16.5 %collective-permute-start.3 = (bf16[608,256]{1,0:T(8,128)(2,1)}, bf16[608,256]{1,0:T(8,128)(2,1)S(1)}, u32[]{:S(2)}, u32[]{:S(2)}) collective-permute-start(bf16[608,256]{1,0:T(8,128)(2,1)} %join.1.refs_1_), channel_id=1, source_target_pairs={{0,6},{1,7},{2,0},{3,1},{4,2},{5,3},{6,4},{7,5},{8,14},{9,15},{10,... | collective-permute-start | bytes 933896 | tf_op jit(solution)/shard_map/ppermute | solution.py:416
  30.5 2.0 copy-start.1
  32.5 2.1 copy-start.4
  34.6 6.3 %copy-start.2 = (bf16[4,576,720]{2,1,0:T(8,128)(2,1)S(1)}, bf16[4,576,720]{2,1,0:T(8,128)(2,1)}, u32[]{:S(2)}) copy-start(bf16[4,576,720]{2,1,0:T(8,128)(2,1)} %refs_3_.7) | copy-start | bytes 9953284
  34.6 6.3 %copy-start.5 = (bf16[4,576,720]{2,1,0:T(8,128)(2,1)S(1)}, bf16[4,576,720]{2,1,0:T(8,128)(2,1)}, u32[]{:S(2)}) copy-start(bf16[4,576,720]{2,1,0:T(8,128)(2,1)} %refs_4_.7) | copy-start | bytes 9953284
  40.8 5.5 %collective-permute-start.2 = (bf16[256,1536]{1,0:T(8,128)(2,1)S(1)}, bf16[256,1536]{1,0:T(8,128)(2,1)S(1)}, u32[]{:S(2)}, u32[]{:S(2)}) collective-permute-start(bf16[256,1536]{1,0:T(8,128)(2,1)S(1)} %get-tuple-element.38), channel_id=1, source_target_pairs={{0,8},{1,9},{2,10},{3,11},{4,12},{5,13},{6,14},{7,15},{8,0},{9,1},... | collective-permute-start | bytes 2359304 | tf_op jit(solution)/shard_map/ppermute | solution.py:416
  45.7 2.5 %collective-permute-start.4 = (bf16[256,1536]{1,0:T(8,128)(2,1)S(1)}, bf16[256,1536]{1,0:T(8,128)(2,1)S(1)}, u32[]{:S(2)}, u32[]{:S(2)}) collective-permute-start(bf16[256,1536]{1,0:T(8,128)(2,1)S(1)} %get-tuple-element.43), channel_id=1, source_target_pairs={{0,8},{1,9},{2,10},{3,11},{4,12},{5,13},{6,14},{7,15},{8,0},{9,1},... | collective-permute-start | bytes 2359304 | tf_op jit(solution)/shard_map/ppermute | solution.py:416
  58.7 2.0 copy-start.3
  60.7 2.0 copy-start.6
  62.7 1.3 copy-start.8
  68.8 38.6 %collective-permute-start.7 = (bf16[256,1536]{1,0:T(8,128)(2,1)S(1)}, bf16[256,1536]{1,0:T(8,128)(2,1)S(1)}, u32[]{:S(2)}, u32[]{:S(2)}) collective-permute-start(bf16[256,1536]{1,0:T(8,128)(2,1)S(1)} %get-tuple-element.52), channel_id=1, source_target_pairs={{0,8},{1,9},{2,10},{3,11},{4,12},{5,13},{6,14},{7,15},{8,0},{9,1},... | collective-permute-start | bytes 2359304 | tf_op jit(solution)/shard_map/ppermute | solution.py:416
  81.1 1.3 copy-start.9
  87.2 29.6 %collective-permute-start.6 = (bf16[256,1536]{1,0:T(8,128)(2,1)S(1)}, bf16[256,1536]{1,0:T(8,128)(2,1)S(1)}, u32[]{:S(2)}, u32[]{:S(2)}) collective-permute-start(bf16[256,1536]{1,0:T(8,128)(2,1)S(1)} %get-tuple-element.49), channel_id=1, source_target_pairs={{0,8},{1,9},{2,10},{3,11},{4,12},{5,13},{6,14},{7,15},{8,0},{9,1},... | collective-permute-start | bytes 2359304 | tf_op jit(solution)/shard_map/ppermute | solution.py:416
  95.2 34.6 %collective-permute-start.9 = (bf16[256,768]{1,0:T(8,128)(2,1)S(1)}, bf16[256,768]{1,0:T(8,128)(2,1)S(1)}, u32[]{:S(2)}, u32[]{:S(2)}) collective-permute-start(bf16[256,768]{1,0:T(8,128)(2,1)S(1)} %all_gather.53.refs_1_), channel_id=1, source_target_pairs={{0,8},{1,9},{2,10},{3,11},{4,12},{5,13},{6,14},{7,15},{8,0},{9,1},... | collective-permute-start | bytes 1179656 | tf_op jit(solution)/shard_map/ppermute | solution.py:416
  116.7 13.1 %copy-start.7 = (bf16[4,720,576]{1,2,0:T(8,128)(2,1)S(1)}, bf16[4,720,576]{1,2,0:T(8,128)(2,1)}, u32[]{:S(2)}) copy-start(bf16[4,720,576]{1,2,0:T(8,128)(2,1)} %param.18) | copy-start | bytes 9953284
  116.7 38.4 %collective-permute-start.8 = (bf16[256,768]{1,0:T(8,128)(2,1)S(1)}, bf16[256,768]{1,0:T(8,128)(2,1)S(1)}, u32[]{:S(2)}, u32[]{:S(2)}) collective-permute-start(bf16[256,768]{1,0:T(8,128)(2,1)S(1)} %all_gather.50.refs_1_), channel_id=1, source_target_pairs={{0,8},{1,9},{2,10},{3,11},{4,12},{5,13},{6,14},{7,15},{8,0},{9,1},... | collective-permute-start | bytes 1179656 | tf_op jit(solution)/shard_map/ppermute | solution.py:416
  141.5 18.2 %collective-permute-start.11 = (bf16[256,768]{1,0:T(8,128)(2,1)S(1)}, bf16[256,768]{1,0:T(8,128)(2,1)S(1)}, u32[]{:S(2)}, u32[]{:S(2)}) collective-permute-start(bf16[256,768]{1,0:T(8,128)(2,1)S(1)} %all_gather.55.refs_1_), channel_id=1, source_target_pairs={{0,8},{1,9},{2,10},{3,11},{4,12},{5,13},{6,14},{7,15},{8,0},{9,1},... | collective-permute-start | bytes 1179656 | tf_op jit(solution)/shard_map/ppermute | solution.py:416
  141.5 22.2 %collective-permute-start.13 = (bf16[288,256]{1,0:T(8,128)(2,1)S(1)}, bf16[288,256]{1,0:T(8,128)(2,1)S(1)}, u32[]{:S(2)}, u32[]{:S(2)}) collective-permute-start(bf16[288,256]{1,0:T(8,128)(2,1)S(1)} %get-tuple-element.63), channel_id=1, source_target_pairs={{0,1},{1,0},{2,3},{3,2},{4,5},{5,4},{6,7},{7,6},{8,9},{9,8},{10,11... | collective-permute-start | bytes 442376 | tf_op jit(solution)/shard_map/ppermute | solution.py:416
  163.2 9.4 %collective-permute-start.17 = (bf16[288,256]{1,0:T(8,128)(2,1)S(1)}, bf16[288,256]{1,0:T(8,128)(2,1)S(1)}, u32[]{:S(2)}, u32[]{:S(2)}) collective-permute-start(bf16[288,256]{1,0:T(8,128)(2,1)S(1)} %get-tuple-element.65), channel_id=1, source_target_pairs={{0,1},{1,0},{2,3},{3,2},{4,5},{5,4},{6,7},{7,6},{8,9},{9,8},{10,11... | collective-permute-start | bytes 442376 | tf_op jit(solution)/shard_map/ppermute | solution.py:416
  163.8 23.3 %collective-permute-start.14 = (bf16[288,256]{1,0:T(8,128)(2,1)S(1)}, bf16[288,256]{1,0:T(8,128)(2,1)S(1)}, u32[]{:S(2)}, u32[]{:S(2)}) collective-permute-start(bf16[288,256]{1,0:T(8,128)(2,1)S(1)} %add_convert_fusion.2), channel_id=1, source_target_pairs={{0,2},{1,3},{2,4},{3,5},{4,6},{5,7},{6,0},{7,1},{8,10},{9,11},{10,... | collective-permute-start | bytes 442376 | tf_op jit(solution)/shard_map/ppermute | solution.py:416
  164.7 10.9 %collective-permute-start.15 = (bf16[288,256]{1,0:T(8,128)(2,1)S(1)}, bf16[288,256]{1,0:T(8,128)(2,1)S(1)}, u32[]{:S(2)}, u32[]{:S(2)}) collective-permute-start(bf16[288,256]{1,0:T(8,128)(2,1)S(1)} %get-tuple-element.64), channel_id=1, source_target_pairs={{0,1},{1,0},{2,3},{3,2},{4,5},{5,4},{6,7},{7,6},{8,9},{9,8},{10,11... | collective-permute-start | bytes 442376 | tf_op jit(solution)/shard_map/ppermute | solution.py:416
  172.5 3.2 %collective-permute-start.10 = (bf16[256,768]{1,0:T(8,128)(2,1)S(1)}, bf16[256,768]{1,0:T(8,128)(2,1)S(1)}, u32[]{:S(2)}, u32[]{:S(2)}) collective-permute-start(bf16[256,768]{1,0:T(8,128)(2,1)S(1)} %all_gather.54.refs_1_), channel_id=1, source_target_pairs={{0,8},{1,9},{2,10},{3,11},{4,12},{5,13},{6,14},{7,15},{8,0},{9,1},... | collective-permute-start | bytes 1179656 | tf_op jit(solution)/shard_map/ppermute | solution.py:416
  172.6 14.5 %collective-permute-start.18 = (bf16[288,256]{1,0:T(8,128)(2,1)S(1)}, bf16[288,256]{1,0:T(8,128)(2,1)S(1)}, u32[]{:S(2)}, u32[]{:S(2)}) collective-permute-start(bf16[288,256]{1,0:T(8,128)(2,1)S(1)} %add_convert_fusion), channel_id=1, source_target_pairs={{0,6},{1,7},{2,0},{3,1},{4,2},{5,3},{6,4},{7,5},{8,14},{9,15},{10,... | collective-permute-start | bytes 442376 | tf_op jit(solution)/shard_map/ppermute | solution.py:416
  175.6 17.0 %copy-start.15 = (f32[2304]{0:T(1024)S(1)}, f32[2304]{0:T(1024)}, u32[]{:S(2)}) copy-start(f32[2304]{0:T(1024)} %param.19) | copy-start | bytes 27652
  175.7 17.1 %copy-start.16 = (f32[16]{0:T(128)S(1)}, f32[16]{0:T(128)}, u32[]{:S(2)}) copy-start(f32[16]{0:T(128)} %param.21) | copy-start | bytes 196
  175.7 11.4 %collective-permute-start.16 = (bf16[288,256]{1,0:T(8,128)(2,1)S(1)}, bf16[288,256]{1,0:T(8,128)(2,1)S(1)}, u32[]{:S(2)}, u32[]{:S(2)}) collective-permute-start(bf16[288,256]{1,0:T(8,128)(2,1)S(1)} %add_convert_fusion.1), channel_id=1, source_target_pairs={{0,4},{1,5},{2,6},{3,7},{4,0},{5,1},{6,2},{7,3},{8,12},{9,13},{10,... | collective-permute-start | bytes 442376 | tf_op jit(solution)/shard_map/ppermute | solution.py:416
  175.8 24.6 %copy-start.10 = (bf16[2304,512]{1,0:T(8,128)(2,1)S(1)}, bf16[2304,512]{1,0:T(8,128)(2,1)}, u32[]{:S(2)}) copy-start(bf16[2304,512]{1,0:T(8,128)(2,1)} %refs_2_.1) | copy-start | bytes 7077892
  179.2 7.9 %collective-permute-start.12 = (bf16[288,256]{1,0:T(8,128)(2,1)S(1)}, bf16[288,256]{1,0:T(8,128)(2,1)S(1)}, u32[]{:S(2)}, u32[]{:S(2)}) collective-permute-start(bf16[288,256]{1,0:T(8,128)(2,1)S(1)} %get-tuple-element.62), channel_id=1, source_target_pairs={{0,1},{1,0},{2,3},{3,2},{4,5},{5,4},{6,7},{7,6},{8,9},{9,8},{10,11... | collective-permute-start | bytes 442376 | tf_op jit(solution)/shard_map/ppermute | solution.py:416
  179.8 7.3 %collective-permute-start.5 = (f32[4,288]{1,0:T(4,128)S(1)}, f32[4,288]{1,0:T(4,128)S(1)}, u32[]{:S(2)}, u32[]{:S(2)}) collective-permute-start(f32[4,288]{1,0:T(4,128)S(1)} %get-tuple-element.47), channel_id=1, source_target_pairs={{0,0},{1,1},{2,8},{3,9},{4,16},{5,17},{6,24},{7,25},{8,2},{9,3},{1... | collective-permute-start | bytes 13832 | tf_op jit(solution)/shard_map/ppermute | solution.py:416
  188.2 36.8 %copy-start.12 = (f32[256,288]{0,1:T(8,128)S(1)}, f32[256,288]{0,1:T(8,128)}, u32[]{:S(2)}) copy-start(f32[256,288]{0,1:T(8,128)} %param.11) | copy-start | bytes 884740
  188.2 12.1 %all-to-all-start = ((f32[32,4,288]{2,1,0:T(4,128)}), f32[32,4,288]{2,1,0:T(4,128)S(1)}, u32[]{:S(2)}, u32[]{:S(2)}) async-start(f32[32,4,288]{2,1,0:T(4,128)} %get-tuple-element.67), calls=%async_computation | async-start | bytes 393216 | tf_op jit(solution)/shard_map/all_to_all | solution.py:498
  201.8 10.0 %all-to-all-start.1 = ((f32[32,2,16]{2,1,0:T(2,128)}), f32[32,2,16]{2,1,0:T(2,128)S(1)}, u32[]{:S(2)}, u32[]{:S(2)}) async-start(f32[32,2,16]{2,1,0:T(2,128)} %get-tuple-element.69), calls=%async_computation.1 | async-start | bytes 65536 | tf_op jit(solution)/shard_map/all_to_all | solution.py:498
  205.7 19.3 %collective-permute-start.19 = (f32[288,256]{1,0:T(8,128)S(1)}, f32[288,256]{1,0:T(8,128)S(1)}, u32[]{:S(2)}, u32[]{:S(2)}) collective-permute-start(f32[288,256]{1,0:T(8,128)S(1)} %get-tuple-element.66), channel_id=1, source_target_pairs={{0,0},{1,1},{2,8},{3,9},{4,16},{5,17},{6,24},{7,25},{8,2},{9,3},{1... | collective-permute-start | bytes 884744 | tf_op jit(solution)/shard_map/ppermute | solution.py:416
Sparse Core Ops, SparseCore 0:
  24.5 34.1 all-gather.6

commit v8 on v6

--- a/solution.py
+++ b/solution.py
@@ -17,7 +17,6 @@
 VMEM = pl.BlockSpec(memory_space=pltpu.VMEM)
 SMEM = pl.BlockSpec(memory_space=pltpu.SMEM)
 ANY = pl.BlockSpec(memory_space=pl.ANY)
-HBM = pl.BlockSpec(memory_space=pltpu.HBM)
 
 
 def up_to(n, step=LANES):
@@ -125,19 +124,8 @@
 
 def partial_kernel(sides, held, scal, *refs):
     feeds, (wr, wg, wu) = refs[:held], refs[held : held + 3]
-    own, give, cols, xs, xt, acc, extra, ring, sems = refs[-9:]
+    own, give, cols, xs, xt, acc, extra = refs[-7:]
     e = pl.program_id(0)
-    experts = wg.shape[0]
-
-    def fetch(n, slot, which):
-        return pltpu.make_async_copy((wg, wu)[which].at[n], ring.at[slot, which], sems.at[slot, which])
-
-    @pl.when(e == 0)
-    def _():
-        for n in range(min(2, experts)):
-            for which in range(2):
-                fetch(n, n, which).start()
-
     core, side = scal[0], scal[1]
     depth, hidden = wg.shape[1:]
     deep, half = up_to(depth), up_to(hidden)
@@ -175,22 +163,15 @@
     mine, other = slot_columns(core, xt[:, deep : deep + LANES])
     ef = e.astype(f32)
     take = [(v == ef) | (e == 0) for v in (mine, other)]
-    slot = e % 2
-    for which in range(2):
-        fetch(e, slot, which).wait()
+    for which, w in enumerate((wg, wu)):
         for at in range(0, hidden, 256):
             end = min(hidden, at + 256)
-            d = jnp.dot(xt[:, 0:depth], ring[slot, which, :, at:end], preferred_element_type=f32)
+            d = jnp.dot(xt[:, 0:depth], w[0, :, at:end], preferred_element_type=f32)
             to = slice(which * half + at, which * half + end)
             for ref, pick in ((own, take[0]), (acc, take[1])):
                 ref[:, to] = jnp.where(pick, d, ref[:, to])
 
-    @pl.when(e + 2 < experts)
-    def _():
-        for which in range(2):
-            fetch(e + 2, slot, which).start()
-
-    @pl.when(e == experts - 1)
+    @pl.when(e == pl.num_programs(0) - 1)
     def _():
         lane = lax.broadcasted_iota(jnp.int32, extra.shape, 1)
         more = extra[...]
@@ -203,11 +184,12 @@
     experts, depth, hidden = wg.shape
     tokens = feeds[0].shape[1] * len(feeds)
     deep, wide = up_to(depth), 2 * up_to(hidden)
+    part = pl.BlockSpec((1, depth, hidden), lambda n: (n, 0, 0))
     outs = [shape((tokens, wide), f32), shape((tokens, wide), bf16), shape((tokens, LANES), bf16)]
     return pl.pallas_call(
         lambda *refs: partial_kernel(sides, len(feeds), *refs),
         grid=(experts,),
-        in_specs=[SMEM] + [whole_spec(v) for v in feeds] + [whole_spec(wr), HBM, HBM] + [ANY] * len(deps),
+        in_specs=[SMEM] + [whole_spec(v) for v in feeds] + [whole_spec(wr), part, part] + [ANY] * len(deps),
         out_specs=[whole_spec(v) for v in outs],
         out_shape=outs,
         scratch_shapes=[
@@ -215,8 +197,6 @@
             pltpu.VMEM((tokens, deep + LANES), bf16),
             pltpu.VMEM((tokens, wide), f32),
             pltpu.VMEM((tokens, LANES), f32),
-            pltpu.VMEM((2, 2, depth, hidden), bf16),
-            pltpu.SemaphoreType.DMA((2, 2)),
         ],
         compiler_params=params(20),
         cost_estimate=HINT,
@@ -466,7 +446,7 @@
     pair = join_call(first)
     feeds = {1: pair}
     for group in (2, 3, 0):
-        feeds[group] = send(feeds[(group - 1) % parts], lambda q, z, x: (q, (z - 1) % parts, x))
+        feeds[group] = send(pair, lambda q, z, x, group=group: (q, (z - group + 1) % parts, x))
     stream = send(stream, home)
     partial, kept, pieces, shares = {}, {}, {}, {}
 
@@ -503,14 +483,14 @@
     p0 = do_partial(0)
     p1 = do_partial(1, p0)
     s0 = do_sum(0, p1)
-    p2 = do_partial(2, s0)
-    s1 = do_sum(1, p2)
-    p3 = do_partial(3, s1)
-    s2 = do_sum(2, p3)
-    a0 = do_act(0, s2)
-    s3 = do_sum(3, a0)
-    a1 = do_act(1, s3)
-    d0 = do_down(0, a1)
+    s1 = do_sum(1, s0)
+    p2 = do_partial(2, s1)
+    a0 = do_act(0, p2)
+    p3 = do_partial(3, a0)
+    a1 = do_act(1, p3)
+    s2 = do_sum(2, a1)
+    s3 = do_sum(3, s2)
+    d0 = do_down(0, s3)
     a2 = do_act(2, d0)
     d1 = do_down(1, a2)
     a3 = do_act(3, d1)

time: 184 us -> 177 us (0.962)
  Pallas kernels: 57.3 us -> 45 us
  starting transfers between devices: 37.8 us -> 44.1 us
    pallas_call x4, Pallas kernels: 31.7 us -> 19.4 us  [partial_call(): pl.pallas_call(lambda *refs: partial_kernel(sides, len(feeds), *refs), gr...]
    ppermute x34, starting transfers between devices: 30.6 us -> 34.3 us  [send(): return lax.ppermute(value, ('dp', 'mp'), pairs)]
    all_to_all x2, starting transfers between devices: 7.25 us -> 9.84 us  [body(): everyone = lambda v: lax.all_to_all(v, ('dp', 'mp'), 0, 0, tiled=True)]
  transfers between devices with their start and end apart: 36 -> 36, of which waited for: 15 -> 12; matrix products, arithmetic and copies ran while one was open for 1% -> 1% of each run, Pallas kernels for 29% -> 24%
where the time goes in v8:
time: 177 us
  waiting for transfers between devices  77.6 us (44%)
  Pallas kernels  45 us (25%)
  starting transfers between devices  44.1 us (25%)
  local copies, waits for them, and re-layouts  7.3 us (4%)
    ppermute x34, waiting for transfers between devices, send(): return lax.ppermute(value, ('dp', 'mp'), pairs)  68.4 us
    ppermute x34, starting transfers between devices, send(): return lax.ppermute(value, ('dp', 'mp'), pairs)  34.3 us
    pallas_call x4, Pallas kernels, partial_call(): pl.pallas_call(lambda *refs: partial_kernel(sides, len(feeds), *refs), gr...  19.4 us
    pallas_call x4, Pallas kernels, down_call(): pl.pallas_call(lambda *refs: down_kernel(sides, *refs), grid=(experts,),...  13.8 us
    all_to_all x2, starting transfers between devices, body(): everyone = lambda v: lax.all_to_all(v, ('dp', 'mp'), 0, 0, tiled=True)  9.84 us
    all_to_all x2, waiting for transfers between devices, body(): everyone = lambda v: lax.all_to_all(v, ('dp', 'mp'), 0, 0, tiled=True)  9.27 us
    unnamed x26, local copies, waits for them, and re-layouts  6.34 us
    pallas_call x4, Pallas kernels, act_call(): pl.pallas_call(lambda *refs: act_kernel(base, *refs), in_specs=[SMEM] + [...  4.95 us
  transfers between devices with their start and end apart: 36, of which 12 were waited for; matrix products, arithmetic and copies ran while one was open for 1% of the time, Pallas kernels for 24%

profile of v8, /device:TPU:4, one launch (start us, length us, event | category | flops | bytes accessed | tf_op | source)
XLA Modules:
  0.0 176.8 jit_solution(466271573634254745)
XLA Ops:
  0.6 0.7 broadcast_in_dim.4.gain
  1.3 1.0 copy-done.7
  2.3 0.7 copy-done.9
  3.6 0.9 prep.1
  4.5 1.5 collective-permute-start
  6.0 3.0 %collective-permute-start.1 = (bf16[304,256]{1,0:T(8,128)(2,1)S(1)}, bf16[304,256]{1,0:T(8,128)(2,1)S(1)}, u32[]{:S(2)}, u32[]{:S(2)}) collective-permute-start(bf16[304,256]{1,0:T(8,128)(2,1)S(1)} %get-tuple-element.36), channel_id=1, source_target_pairs={{0,7},{1,6},{2,15},{3,14},{4,23},{5,22},{6,31},{7,30},{8,1},{9,0},... | collective-permute-start | bytes 466952 | tf_op jit(solution)/shard_map/ppermute | solution.py:421
  9.2 3.6 %collective-permute-done.refs_0_ = bf16[304,256]{1,0:T(8,128)(2,1)S(1)} collective-permute-done((bf16[304,256]{1,0:T(8,128)(2,1)S(1)}, bf16[304,256]{1,0:T(8,128)(2,1)S(1)}, u32[]{:S(2)}, u32[]{:S(2)}) %collective-permute-start) | collective-permute-done | bytes 155680 | tf_op jit(solution)/shard_map/ppermute | solution.py:421
  12.7 4.3 %collective-permute-done.1.refs_1_ = bf16[304,256]{1,0:T(8,128)(2,1)S(1)} collective-permute-done((bf16[304,256]{1,0:T(8,128)(2,1)S(1)}, bf16[304,256]{1,0:T(8,128)(2,1)S(1)}, u32[]{:S(2)}, u32[]{:S(2)}) %collective-permute-start.1) | collective-permute-done | bytes 155680 | tf_op jit(solution)/shard_map/ppermute | solution.py:421
  17.0 5.9 %collective-permute-start.5 = (bf16[608,256]{1,0:T(8,128)(2,1)S(1)}, bf16[608,256]{1,0:T(8,128)(2,1)S(1)}, u32[]{:S(2)}, u32[]{:S(2)}) collective-permute-start(bf16[608,256]{1,0:T(8,128)(2,1)S(1)} %join.1.refs_1_), channel_id=1, source_target_pairs={{0,6},{1,7},{2,0},{3,1},{4,2},{5,3},{6,4},{7,5},{8,14},{9,15},{10,... | collective-permute-start | bytes 933896 | tf_op jit(solution)/shard_map/ppermute | solution.py:421
  23.0 2.0 %copy-done.2 = bf16[4,576,720]{2,1,0:T(8,128)(2,1)S(1)} copy-done((bf16[4,576,720]{2,1,0:T(8,128)(2,1)S(1)}, bf16[4,576,720]{2,1,0:T(8,128)(2,1)}, u32[]{:S(2)}) %copy-start.2) | copy-done | bytes 3317784
  25.0 2.0 %copy-done.4 = bf16[4,576,720]{2,1,0:T(8,128)(2,1)S(1)} copy-done((bf16[4,576,720]{2,1,0:T(8,128)(2,1)S(1)}, bf16[4,576,720]{2,1,0:T(8,128)(2,1)}, u32[]{:S(2)}) %copy-start.4) | copy-done | bytes 3317784
  27.0 4.8 %gate_up_partial.4 = (f32[256,1536]{1,0:T(8,128)S(1)}, bf16[256,1536]{1,0:T(8,128)(2,1)S(1)}, bf16[256,128]{1,0:T(8,128)(2,1)S(1)}) custom-call(s32[3]{0:T(128)S(1)} %pad_add_fusion.1.refs_0_, bf16[608,256]{1,0:T(8,128)(2,1)S(1)} %join.1.refs_1_, bf16[128,576]{1,0:T(8,128)(2,1)S(1)} %pad_add_fusion.refs_2_, bf16[4,576,720]{2,1,0:T(8,128)(2,1)S(1)} %copy-done.2, ...), custom_call_target="tpu_custom_call" | custom-call | flops 1 | bytes 1024 | tf_op jit(solution)/shard_map/gate_up_partial/pallas_call | solution.py:189
  32.0 4.9 %gate_up_partial.5 = (f32[256,1536]{1,0:T(8,128)S(1)}, bf16[256,1536]{1,0:T(8,128)(2,1)S(1)}, bf16[256,128]{1,0:T(8,128)(2,1)S(1)}) custom-call(s32[3]{0:T(128)S(1)} %pad_add_fusion.1.refs_0_, bf16[608,256]{1,0:T(8,128)(2,1)S(1)} %collective-permute-done.5.refs_1_, bf16[128,576]{1,0:T(8,128)(2,1)S(1)} %pad_add_fusion.refs_2_, ...), custom_call_target="tpu_custom_call" | custom-call | flops 1 | bytes 1024 | tf_op jit(solution)/shard_map/gate_up_partial/pallas_call | solution.py:189
  37.4 0.9 core_sum.4
  39.3 0.9 core_sum.5
  40.1 18.2 %collective-permute-done.7.refs_1_ = bf16[608,256]{1,0:T(8,128)(2,1)S(1)} collective-permute-done((bf16[608,256]{1,0:T(8,128)(2,1)S(1)}, bf16[608,256]{1,0:T(8,128)(2,1)S(1)}, u32[]{:S(2)}, u32[]{:S(2)}) %collective-permute-start.7) | collective-permute-done | bytes 311328 | tf_op jit(solution)/shard_map/ppermute | solution.py:421
  58.3 4.8 %gate_up_partial.6 = (f32[256,1536]{1,0:T(8,128)S(1)}, bf16[256,1536]{1,0:T(8,128)(2,1)S(1)}, bf16[256,128]{1,0:T(8,128)(2,1)S(1)}) custom-call(s32[3]{0:T(128)S(1)} %pad_add_fusion.1.refs_0_, bf16[608,256]{1,0:T(8,128)(2,1)S(1)} %collective-permute-done.7.refs_1_, bf16[128,576]{1,0:T(8,128)(2,1)S(1)} %pad_add_fusion.refs_2_, ...), custom_call_target="tpu_custom_call" | custom-call | flops 1 | bytes 1024 | tf_op jit(solution)/shard_map/gate_up_partial/pallas_call | solution.py:189
  63.3 1.2 act.4.refs_5_.refs_1_
  64.5 4.9 %gate_up_partial.7 = (f32[256,1536]{1,0:T(8,128)S(1)}, bf16[256,1536]{1,0:T(8,128)(2,1)S(1)}, bf16[256,128]{1,0:T(8,128)(2,1)S(1)}) custom-call(s32[3]{0:T(128)S(1)} %pad_add_fusion.1.refs_0_, bf16[608,256]{1,0:T(8,128)(2,1)S(1)} %collective-permute-done.2.refs_1_.meta, bf16[128,576]{1,0:T(8,128)(2,1)S(1)} %pad_add_fusion.refs_2_, ...), custom_call_target="tpu_custom_call" | custom-call | flops 1 | bytes 1024 | tf_op jit(solution)/shard_map/gate_up_partial/pallas_call | solution.py:189
  69.9 2.0 %collective-permute-start.17 = (bf16[128,768]{1,0:T(8,128)(2,1)S(1)}, bf16[128,768]{1,0:T(8,128)(2,1)S(1)}, u32[]{:S(2)}, u32[]{:S(2)}) collective-permute-start(bf16[128,768]{1,0:T(8,128)(2,1)S(1)} %act.4.refs_5_.refs_1_), channel_id=1, source_target_pairs={{0,16},{1,17},{2,18},{3,19},{4,20},{5,21},{6,22},{7,23},{8,24},{9,... | collective-permute-start | bytes 589832 | tf_op jit(solution)/shard_map/ppermute | solution.py:421
  72.0 9.9 %collective-permute-done.11.refs_2_ = bf16[128,1536]{1,0:T(8,128)(2,1)S(1)} collective-permute-done((bf16[128,1536]{1,0:T(8,128)(2,1)S(1)}, bf16[128,1536]{1,0:T(8,128)(2,1)S(1)}, u32[]{:S(2)}, u32[]{:S(2)}) %collective-permute-start.11) | collective-permute-done | bytes 393248 | tf_op jit(solution)/shard_map/ppermute | solution.py:421
  81.9 1.2 act.5.refs_3_.refs_1_
  83.2 0.9 core_sum.6
  84.2 1.9 %collective-permute-start.13 = (bf16[128,768]{1,0:T(8,128)(2,1)S(1)}, bf16[128,768]{1,0:T(8,128)(2,1)S(1)}, u32[]{:S(2)}, u32[]{:S(2)}) collective-permute-start(bf16[128,768]{1,0:T(8,128)(2,1)S(1)} %act.5.refs_3_.refs_1_), channel_id=1, source_target_pairs={{0,16},{1,17},{2,18},{3,19},{4,20},{5,21},{6,22},{7,23},{8,24},{9,... | collective-permute-start | bytes 589832 | tf_op jit(solution)/shard_map/ppermute | solution.py:421
  86.4 0.9 core_sum.7
  87.7 12.7 %collective-permute-done.13.refs_2_ = bf16[128,768]{1,0:T(8,128)(2,1)S(1)} collective-permute-done((bf16[128,768]{1,0:T(8,128)(2,1)S(1)}, bf16[128,768]{1,0:T(8,128)(2,1)S(1)}, u32[]{:S(2)}, u32[]{:S(2)}) %collective-permute-start.13) | collective-permute-done | bytes 196640 | tf_op jit(solution)/shard_map/ppermute | solution.py:421
  100.4 3.5 %down.4 = (bf16[288,256]{1,0:T(8,128)(2,1)S(1)}, bf16[288,256]{1,0:T(8,128)(2,1)S(1)}) custom-call(s32[3]{0:T(128)S(1)} %pad_add_fusion.1.refs_0_, bf16[128,768]{1,0:T(8,128)(2,1)S(1)} %act.4.refs_5_.refs_1_, bf16[128,768]{1,0:T(8,128)(2,1)S(1)} %collective-permute-done.17.refs_2_, bf16[128,768]{1,0:T(8,128)(2,1)S(1)} %collective-permute-done.18.refs_3_, ...), custom_call_target="tpu_custom_call" | custom-call | flops 1 | bytes 1024 | tf_op jit(solution)/shard_map/down/pallas_call | solution.py:303
  103.9 1.2 act.6.refs_7_.refs_1_
  106.0 3.5 %down.5 = (bf16[288,256]{1,0:T(8,128)(2,1)S(1)}, bf16[288,256]{1,0:T(8,128)(2,1)S(1)}) custom-call(s32[3]{0:T(128)S(1)} %pad_add_fusion.1.refs_0_, bf16[128,768]{1,0:T(8,128)(2,1)S(1)} %act.5.refs_3_.refs_1_, bf16[128,768]{1,0:T(8,128)(2,1)S(1)} %collective-permute-done.13.refs_2_, bf16[128,768]{1,0:T(8,128)(2,1)S(1)} %collective-permute-done.14.refs_3_, ...), custom_call_target="tpu_custom_call" | custom-call | flops 1 | bytes 1024 | tf_op jit(solution)/shard_map/down/pallas_call | solution.py:303
  109.5 1.5 collective-permute-start.29
  111.0 1.2 act.7.refs_7_.refs_1_
  112.3 1.8 %collective-permute-start.20 = (bf16[128,768]{1,0:T(8,128)(2,1)S(1)}, bf16[128,768]{1,0:T(8,128)(2,1)S(1)}, u32[]{:S(2)}, u32[]{:S(2)}) collective-permute-start(bf16[128,768]{1,0:T(8,128)(2,1)S(1)} %act.7.refs_7_.refs_1_), channel_id=1, source_target_pairs={{0,16},{1,17},{2,18},{3,19},{4,20},{5,21},{6,22},{7,23},{8,24},{9,... | collective-permute-start | bytes 589832 | tf_op jit(solution)/shard_map/ppermute | solution.py:421
  115.0 4.4 %collective-permute-done.20.refs_2_ = bf16[128,768]{1,0:T(8,128)(2,1)S(1)} collective-permute-done((bf16[128,768]{1,0:T(8,128)(2,1)S(1)}, bf16[128,768]{1,0:T(8,128)(2,1)S(1)}, u32[]{:S(2)}, u32[]{:S(2)}) %collective-permute-start.20) | collective-permute-done | bytes 196640 | tf_op jit(solution)/shard_map/ppermute | solution.py:421
  119.4 3.5 %down.6 = (bf16[288,256]{1,0:T(8,128)(2,1)S(1)}, bf16[288,256]{1,0:T(8,128)(2,1)S(1)}) custom-call(s32[3]{0:T(128)S(1)} %pad_add_fusion.1.refs_0_, bf16[128,768]{1,0:T(8,128)(2,1)S(1)} %act.6.refs_7_.refs_1_, bf16[128,768]{1,0:T(8,128)(2,1)S(1)} %collective-permute-done.23.refs_2_, bf16[128,768]{1,0:T(8,128)(2,1)S(1)} %collective-permute-done.24.refs_3_, ...), custom_call_target="tpu_custom_call" | custom-call | flops 1 | bytes 1024 | tf_op jit(solution)/shard_map/down/pallas_call | solution.py:303
  123.7 3.5 %down.7 = (bf16[288,256]{1,0:T(8,128)(2,1)S(1)}, bf16[288,256]{1,0:T(8,128)(2,1)S(1)}) custom-call(s32[3]{0:T(128)S(1)} %pad_add_fusion.1.refs_0_, bf16[128,768]{1,0:T(8,128)(2,1)S(1)} %act.7.refs_7_.refs_1_, bf16[128,768]{1,0:T(8,128)(2,1)S(1)} %collective-permute-done.20.refs_2_, bf16[128,768]{1,0:T(8,128)(2,1)S(1)} %collective-permute-done.21.refs_3_, ...), custom_call_target="tpu_custom_call" | custom-call | flops 1 | bytes 1024 | tf_op jit(solution)/shard_map/down/pallas_call | solution.py:303
  127.1 1.5 collective-permute-start.26
  129.3 5.5 %collective-permute-start.3 = (f32[4,288]{1,0:T(4,128)S(1)}, f32[4,288]{1,0:T(4,128)S(1)}, u32[]{:S(2)}, u32[]{:S(2)}) collective-permute-start(f32[4,288]{1,0:T(4,128)S(1)} %get-tuple-element.37), channel_id=1, source_target_pairs={{0,0},{1,1},{2,8},{3,9},{4,16},{5,17},{6,24},{7,25},{8,2},{9,3},{1... | collective-permute-start | bytes 13832 | tf_op jit(solution)/shard_map/ppermute | solution.py:421
  134.8 1.9 %collective-permute-done.3.stream = f32[4,288]{1,0:T(4,128)S(1)} collective-permute-done((f32[4,288]{1,0:T(4,128)S(1)}, f32[4,288]{1,0:T(4,128)S(1)}, u32[]{:S(2)}, u32[]{:S(2)}) %collective-permute-start.3) | collective-permute-done | bytes 4640 | tf_op jit(solution)/shard_map/ppermute | solution.py:421
  136.7 1.1 branch_total.1
  137.8 5.9 %all-to-all-start = ((f32[32,4,288]{2,1,0:T(4,128)}), f32[32,4,288]{2,1,0:T(4,128)S(1)}, u32[]{:S(2)}, u32[]{:S(2)}) async-start(f32[32,4,288]{2,1,0:T(4,128)} %get-tuple-element.67), calls=%async_computation | async-start | bytes 393216 | tf_op jit(solution)/shard_map/all_to_all | solution.py:502
  143.9 7.5 %all-to-all-done.refs_0_ = f32[32,4,288]{2,1,0:T(4,128)S(1)} async-done(((f32[32,4,288]{2,1,0:T(4,128)}), f32[32,4,288]{2,1,0:T(4,128)S(1)}, u32[]{:S(2)}, u32[]{:S(2)}) %all-to-all-start) | async-done | bytes 147488 | tf_op jit(solution)/shard_map/all_to_all | solution.py:502
  151.4 1.4 head.1
  152.8 3.9 %all-to-all-start.1 = ((f32[32,2,16]{2,1,0:T(2,128)}), f32[32,2,16]{2,1,0:T(2,128)S(1)}, u32[]{:S(2)}, u32[]{:S(2)}) async-start(f32[32,2,16]{2,1,0:T(2,128)} %get-tuple-element.69), calls=%async_computation.1 | async-start | bytes 65536 | tf_op jit(solution)/shard_map/all_to_all | solution.py:502
  156.8 4.3 %collective-permute-start.33 = (f32[288,256]{1,0:T(8,128)S(1)}, f32[288,256]{1,0:T(8,128)S(1)}, u32[]{:S(2)}, u32[]{:S(2)}) collective-permute-start(f32[288,256]{1,0:T(8,128)S(1)} %get-tuple-element.66), channel_id=1, source_target_pairs={{0,0},{1,1},{2,8},{3,9},{4,16},{5,17},{6,24},{7,25},{8,2},{9,3},{1... | collective-permute-start | bytes 884744 | tf_op jit(solution)/shard_map/ppermute | solution.py:421
  161.1 1.8 all-to-all-done.1
  162.9 0.7 subtract_subtract_fusion
  163.6 12.5 %collective-permute-done.33 = f32[288,256]{1,0:T(8,128)S(1)} collective-permute-done((f32[288,256]{1,0:T(8,128)S(1)}, f32[288,256]{1,0:T(8,128)S(1)}, u32[]{:S(2)}, u32[]{:S(2)}) %collective-permute-start.33) | collective-permute-done | bytes 294944 | tf_op jit(solution)/shard_map/ppermute | solution.py:421
  176.1 0.8 bitcast_add_fusion
  (85 shorter events, 7.4 us)
Async XLA Ops:
  0.6 8.4 %copy-start = (bf16[2304,4]{0,1:T(4,128)(2,1)S(1)}, bf16[2304,4]{0,1:T(4,128)(2,1)}, u32[]{:S(2)}) copy-start(bf16[2304,4]{0,1:T(4,128)(2,1)} %param.15) | copy-start | bytes 55300
  1.3 1.0 copy-start.7
  2.3 0.7 copy-start.9
  4.5 8.2 %collective-permute-start = (bf16[304,256]{1,0:T(8,128)(2,1)S(1)}, bf16[304,256]{1,0:T(8,128)(2,1)S(1)}, u32[]{:S(2)}, u32[]{:S(2)}) collective-permute-start(bf16[304,256]{1,0:T(8,128)(2,1)S(1)} %get-tuple-element.36), channel_id=1, source_target_pairs={{0,6},{1,7},{2,14},{3,15},{4,22},{5,23},{6,30},{7,31},{8,0},{9,1},... | collective-permute-start | bytes 466952 | tf_op jit(solution)/shard_map/ppermute | solution.py:421
  6.0 11.0 %collective-permute-start.1 = (bf16[304,256]{1,0:T(8,128)(2,1)S(1)}, bf16[304,256]{1,0:T(8,128)(2,1)S(1)}, u32[]{:S(2)}, u32[]{:S(2)}) collective-permute-start(bf16[304,256]{1,0:T(8,128)(2,1)S(1)} %get-tuple-element.36), channel_id=1, source_target_pairs={{0,7},{1,6},{2,15},{3,14},{4,23},{5,22},{6,31},{7,30},{8,1},{9,0},... | collective-permute-start | bytes 466952 | tf_op jit(solution)/shard_map/ppermute | solution.py:421
  17.0 14.9 %collective-permute-start.5 = (bf16[608,256]{1,0:T(8,128)(2,1)S(1)}, bf16[608,256]{1,0:T(8,128)(2,1)S(1)}, u32[]{:S(2)}, u32[]{:S(2)}) collective-permute-start(bf16[608,256]{1,0:T(8,128)(2,1)S(1)} %join.1.refs_1_), channel_id=1, source_target_pairs={{0,6},{1,7},{2,0},{3,1},{4,2},{5,3},{6,4},{7,5},{8,14},{9,15},{10,... | collective-permute-start | bytes 933896 | tf_op jit(solution)/shard_map/ppermute | solution.py:421
  23.0 2.0 %copy-start.2 = (bf16[4,576,720]{2,1,0:T(8,128)(2,1)S(1)}, bf16[4,576,720]{2,1,0:T(8,128)(2,1)}, u32[]{:S(2)}) copy-start(bf16[4,576,720]{2,1,0:T(8,128)(2,1)} %refs_3_.7) | copy-start | bytes 9953284
  25.0 2.0 %copy-start.4 = (bf16[4,576,720]{2,1,0:T(8,128)(2,1)S(1)}, bf16[4,576,720]{2,1,0:T(8,128)(2,1)}, u32[]{:S(2)}) copy-start(bf16[4,576,720]{2,1,0:T(8,128)(2,1)} %refs_4_.7) | copy-start | bytes 9953284
  27.0 4.9 %copy-start.3 = (bf16[4,576,720]{2,1,0:T(8,128)(2,1)S(1)}, bf16[4,576,720]{2,1,0:T(8,128)(2,1)}, u32[]{:S(2)}) copy-start(bf16[4,576,720]{2,1,0:T(8,128)(2,1)} %refs_3_.7) | copy-start | bytes 9953284
  27.0 4.9 %copy-start.5 = (bf16[4,576,720]{2,1,0:T(8,128)(2,1)S(1)}, bf16[4,576,720]{2,1,0:T(8,128)(2,1)}, u32[]{:S(2)}) copy-start(bf16[4,576,720]{2,1,0:T(8,128)(2,1)} %refs_4_.7) | copy-start | bytes 9953284
  31.8 5.5 %collective-permute-start.4 = (bf16[256,1536]{1,0:T(8,128)(2,1)S(1)}, bf16[256,1536]{1,0:T(8,128)(2,1)S(1)}, u32[]{:S(2)}, u32[]{:S(2)}) collective-permute-start(bf16[256,1536]{1,0:T(8,128)(2,1)S(1)} %get-tuple-element.39), channel_id=1, source_target_pairs={{0,8},{1,9},{2,10},{3,11},{4,12},{5,13},{6,14},{7,15},{8,0},{9,1},... | collective-permute-start | bytes 2359304 | tf_op jit(solution)/shard_map/ppermute | solution.py:421
  36.8 2.5 %collective-permute-start.8 = (bf16[256,1536]{1,0:T(8,128)(2,1)S(1)}, bf16[256,1536]{1,0:T(8,128)(2,1)S(1)}, u32[]{:S(2)}, u32[]{:S(2)}) collective-permute-start(bf16[256,1536]{1,0:T(8,128)(2,1)S(1)} %get-tuple-element.44), channel_id=1, source_target_pairs={{0,8},{1,9},{2,10},{3,11},{4,12},{5,13},{6,14},{7,15},{8,0},{9,1},... | collective-permute-start | bytes 2359304 | tf_op jit(solution)/shard_map/ppermute | solution.py:421
  37.4 21.0 %collective-permute-start.7 = (bf16[608,256]{1,0:T(8,128)(2,1)S(1)}, bf16[608,256]{1,0:T(8,128)(2,1)S(1)}, u32[]{:S(2)}, u32[]{:S(2)}) collective-permute-start(bf16[608,256]{1,0:T(8,128)(2,1)S(1)} %join.1.refs_1_), channel_id=1, source_target_pairs={{0,4},{1,5},{2,6},{3,7},{4,0},{5,1},{6,2},{7,3},{8,12},{9,13},{10,... | collective-permute-start | bytes 933896 | tf_op jit(solution)/shard_map/ppermute | solution.py:421
  38.2 25.0 %collective-permute-start.6 = (bf16[128,1536]{1,0:T(8,128)(2,1)S(1)}, bf16[128,1536]{1,0:T(8,128)(2,1)S(1)}, u32[]{:S(2)}, u32[]{:S(2)}) collective-permute-start(bf16[128,1536]{1,0:T(8,128)(2,1)S(1)} %get-tuple-element.42), channel_id=1, source_target_pairs={{0,16},{1,17},{2,18},{3,19},{4,20},{5,21},{6,22},{7,23},{8,24},{9,... | collective-permute-start | bytes 1179656 | tf_op jit(solution)/shard_map/ppermute | solution.py:421
  38.3 26.2 %collective-permute-start.2 = (bf16[608,256]{1,0:T(8,128)(2,1)S(1)}, bf16[608,256]{1,0:T(8,128)(2,1)S(1)}, u32[]{:S(2)}, u32[]{:S(2)}) collective-permute-start(bf16[608,256]{1,0:T(8,128)(2,1)S(1)} %join.1.refs_1_), channel_id=1, source_target_pairs={{0,2},{1,3},{2,4},{3,5},{4,6},{5,7},{6,0},{7,1},{8,10},{9,11},{10,... | collective-permute-start | bytes 933896 | tf_op jit(solution)/shard_map/ppermute | solution.py:421
  63.2 20.0 %collective-permute-start.10 = (bf16[256,1536]{1,0:T(8,128)(2,1)S(1)}, bf16[256,1536]{1,0:T(8,128)(2,1)S(1)}, u32[]{:S(2)}, u32[]{:S(2)}) collective-permute-start(bf16[256,1536]{1,0:T(8,128)(2,1)S(1)} %get-tuple-element.49), channel_id=1, source_target_pairs={{0,8},{1,9},{2,10},{3,11},{4,12},{5,13},{6,14},{7,15},{8,0},{9,1},... | collective-permute-start | bytes 2359304 | tf_op jit(solution)/shard_map/ppermute | solution.py:421
  69.4 17.0 %collective-permute-start.9 = (bf16[256,1536]{1,0:T(8,128)(2,1)S(1)}, bf16[256,1536]{1,0:T(8,128)(2,1)S(1)}, u32[]{:S(2)}, u32[]{:S(2)}) collective-permute-start(bf16[256,1536]{1,0:T(8,128)(2,1)S(1)} %get-tuple-element.48), channel_id=1, source_target_pairs={{0,8},{1,9},{2,10},{3,11},{4,12},{5,13},{6,14},{7,15},{8,0},{9,1},... | collective-permute-start | bytes 2359304 | tf_op jit(solution)/shard_map/ppermute | solution.py:421
  69.9 12.0 %collective-permute-start.11 = (bf16[128,1536]{1,0:T(8,128)(2,1)S(1)}, bf16[128,1536]{1,0:T(8,128)(2,1)S(1)}, u32[]{:S(2)}, u32[]{:S(2)}) collective-permute-start(bf16[128,1536]{1,0:T(8,128)(2,1)S(1)} %get-tuple-element.50), channel_id=1, source_target_pairs={{0,16},{1,17},{2,18},{3,19},{4,20},{5,21},{6,22},{7,23},{8,24},{9,... | collective-permute-start | bytes 1179656 | tf_op jit(solution)/shard_map/ppermute | solution.py:421
  69.9 16.2 %collective-permute-start.17 = (bf16[128,768]{1,0:T(8,128)(2,1)S(1)}, bf16[128,768]{1,0:T(8,128)(2,1)S(1)}, u32[]{:S(2)}, u32[]{:S(2)}) collective-permute-start(bf16[128,768]{1,0:T(8,128)(2,1)S(1)} %act.4.refs_5_.refs_1_), channel_id=1, source_target_pairs={{0,16},{1,17},{2,18},{3,19},{4,20},{5,21},{6,22},{7,23},{8,24},{9,... | collective-permute-start | bytes 589832 | tf_op jit(solution)/shard_map/ppermute | solution.py:421
  83.1 17.2 %copy-start.1 = (bf16[4,720,576]{1,2,0:T(8,128)(2,1)S(1)}, bf16[4,720,576]{1,2,0:T(8,128)(2,1)}, u32[]{:S(2)}) copy-start(bf16[4,720,576]{1,2,0:T(8,128)(2,1)} %param.18) | copy-start | bytes 9953284
  84.0 19.8 %collective-permute-start.16 = (bf16[128,1536]{1,0:T(8,128)(2,1)S(1)}, bf16[128,1536]{1,0:T(8,128)(2,1)S(1)}, u32[]{:S(2)}, u32[]{:S(2)}) collective-permute-start(bf16[128,1536]{1,0:T(8,128)(2,1)S(1)} %get-tuple-element.56), channel_id=1, source_target_pairs={{0,16},{1,17},{2,18},{3,19},{4,20},{5,21},{6,22},{7,23},{8,24},{9,... | collective-permute-start | bytes 1179656 | tf_op jit(solution)/shard_map/ppermute | solution.py:421
  84.1 3.5 %collective-permute-start.18 = (bf16[128,768]{1,0:T(8,128)(2,1)S(1)}, bf16[128,768]{1,0:T(8,128)(2,1)S(1)}, u32[]{:S(2)}, u32[]{:S(2)}) collective-permute-start(bf16[128,768]{1,0:T(8,128)(2,1)S(1)} %act.4.refs_5_.refs_1_), channel_id=1, source_target_pairs={{0,8},{1,9},{2,10},{3,11},{4,12},{5,13},{6,14},{7,15},{8,0},{9,1},... | collective-permute-start | bytes 589832 | tf_op jit(solution)/shard_map/ppermute | solution.py:421
  84.2 16.2 %collective-permute-start.13 = (bf16[128,768]{1,0:T(8,128)(2,1)S(1)}, bf16[128,768]{1,0:T(8,128)(2,1)S(1)}, u32[]{:S(2)}, u32[]{:S(2)}) collective-permute-start(bf16[128,768]{1,0:T(8,128)(2,1)S(1)} %act.5.refs_3_.refs_1_), channel_id=1, source_target_pairs={{0,16},{1,17},{2,18},{3,19},{4,20},{5,21},{6,22},{7,23},{8,24},{9,... | collective-permute-start | bytes 589832 | tf_op jit(solution)/shard_map/ppermute | solution.py:421
  86.1 14.2 %collective-permute-start.19 = (bf16[128,768]{1,0:T(8,128)(2,1)S(1)}, bf16[128,768]{1,0:T(8,128)(2,1)S(1)}, u32[]{:S(2)}, u32[]{:S(2)}) collective-permute-start(bf16[128,768]{1,0:T(8,128)(2,1)S(1)} %collective-permute-done.17.refs_2_), channel_id=1, source_target_pairs={{0,8},{1,9},{2,10},{3,11},{4,12},{5,13},{6,14},{7,15},{8,0},{9,1},... | collective-permute-start | bytes 589832 | tf_op jit(solution)/shard_map/ppermute | solution.py:421
  87.2 23.8 %collective-permute-start.12 = (bf16[128,1536]{1,0:T(8,128)(2,1)S(1)}, bf16[128,1536]{1,0:T(8,128)(2,1)S(1)}, u32[]{:S(2)}, u32[]{:S(2)}) collective-permute-start(bf16[128,1536]{1,0:T(8,128)(2,1)S(1)} %get-tuple-element.54), channel_id=1, source_target_pairs={{0,16},{1,17},{2,18},{3,19},{4,20},{5,21},{6,22},{7,23},{8,24},{9,... | collective-permute-start | bytes 1179656 | tf_op jit(solution)/shard_map/ppermute | solution.py:421
  87.6 18.2 %collective-permute-start.14 = (bf16[128,768]{1,0:T(8,128)(2,1)S(1)}, bf16[128,768]{1,0:T(8,128)(2,1)S(1)}, u32[]{:S(2)}, u32[]{:S(2)}) collective-permute-start(bf16[128,768]{1,0:T(8,128)(2,1)S(1)} %act.5.refs_3_.refs_1_), channel_id=1, source_target_pairs={{0,8},{1,9},{2,10},{3,11},{4,12},{5,13},{6,14},{7,15},{8,0},{9,1},... | collective-permute-start | bytes 589832 | tf_op jit(solution)/shard_map/ppermute | solution.py:421
  100.4 5.7 %collective-permute-start.15 = (bf16[128,768]{1,0:T(8,128)(2,1)S(1)}, bf16[128,768]{1,0:T(8,128)(2,1)S(1)}, u32[]{:S(2)}, u32[]{:S(2)}) collective-permute-start(bf16[128,768]{1,0:T(8,128)(2,1)S(1)} %collective-permute-done.13.refs_2_), channel_id=1, source_target_pairs={{0,8},{1,9},{2,10},{3,11},{4,12},{5,13},{6,14},{7,15},{8,0},{9,1},... | collective-permute-start | bytes 589832 | tf_op jit(solution)/shard_map/ppermute | solution.py:421
  105.1 9.0 %collective-permute-start.23 = (bf16[128,768]{1,0:T(8,128)(2,1)S(1)}, bf16[128,768]{1,0:T(8,128)(2,1)S(1)}, u32[]{:S(2)}, u32[]{:S(2)}) collective-permute-start(bf16[128,768]{1,0:T(8,128)(2,1)S(1)} %act.6.refs_7_.refs_1_), channel_id=1, source_target_pairs={{0,16},{1,17},{2,18},{3,19},{4,20},{5,21},{6,22},{7,23},{8,24},{9,... | collective-permute-start | bytes 589832 | tf_op jit(solution)/shard_map/ppermute | solution.py:421
  105.2 8.9 %collective-permute-start.27 = (bf16[288,256]{1,0:T(8,128)(2,1)S(1)}, bf16[288,256]{1,0:T(8,128)(2,1)S(1)}, u32[]{:S(2)}, u32[]{:S(2)}) collective-permute-start(bf16[288,256]{1,0:T(8,128)(2,1)S(1)} %get-tuple-element.63), channel_id=1, source_target_pairs={{0,1},{1,0},{2,3},{3,2},{4,5},{5,4},{6,7},{7,6},{8,9},{9,8},{10,11... | collective-permute-start | bytes 442376 | tf_op jit(solution)/shard_map/ppermute | solution.py:421
  105.8 8.6 %collective-permute-start.24 = (bf16[128,768]{1,0:T(8,128)(2,1)S(1)}, bf16[128,768]{1,0:T(8,128)(2,1)S(1)}, u32[]{:S(2)}, u32[]{:S(2)}) collective-permute-start(bf16[128,768]{1,0:T(8,128)(2,1)S(1)} %act.6.refs_7_.refs_1_), channel_id=1, source_target_pairs={{0,8},{1,9},{2,10},{3,11},{4,12},{5,13},{6,14},{7,15},{8,0},{9,1},... | collective-permute-start | bytes 589832 | tf_op jit(solution)/shard_map/ppermute | solution.py:421
  109.5 14.0 %collective-permute-start.29 = (bf16[288,256]{1,0:T(8,128)(2,1)S(1)}, bf16[288,256]{1,0:T(8,128)(2,1)S(1)}, u32[]{:S(2)}, u32[]{:S(2)}) collective-permute-start(bf16[288,256]{1,0:T(8,128)(2,1)S(1)} %get-tuple-element.64), channel_id=1, source_target_pairs={{0,1},{1,0},{2,3},{3,2},{4,5},{5,4},{6,7},{7,6},{8,9},{9,8},{10,11... | collective-permute-start | bytes 442376 | tf_op jit(solution)/shard_map/ppermute | solution.py:421
  112.3 7.1 %collective-permute-start.20 = (bf16[128,768]{1,0:T(8,128)(2,1)S(1)}, bf16[128,768]{1,0:T(8,128)(2,1)S(1)}, u32[]{:S(2)}, u32[]{:S(2)}) collective-permute-start(bf16[128,768]{1,0:T(8,128)(2,1)S(1)} %act.7.refs_7_.refs_1_), channel_id=1, source_target_pairs={{0,16},{1,17},{2,18},{3,19},{4,20},{5,21},{6,22},{7,23},{8,24},{9,... | collective-permute-start | bytes 589832 | tf_op jit(solution)/shard_map/ppermute | solution.py:421
  114.1 5.3 %collective-permute-start.25 = (bf16[128,768]{1,0:T(8,128)(2,1)S(1)}, bf16[128,768]{1,0:T(8,128)(2,1)S(1)}, u32[]{:S(2)}, u32[]{:S(2)}) collective-permute-start(bf16[128,768]{1,0:T(8,128)(2,1)S(1)} %collective-permute-done.23.refs_2_), channel_id=1, source_target_pairs={{0,8},{1,9},{2,10},{3,11},{4,12},{5,13},{6,14},{7,15},{8,0},{9,1},... | collective-permute-start | bytes 589832 | tf_op jit(solution)/shard_map/ppermute | solution.py:421
  114.2 22.5 %collective-permute-start.28 = (bf16[288,256]{1,0:T(8,128)(2,1)S(1)}, bf16[288,256]{1,0:T(8,128)(2,1)S(1)}, u32[]{:S(2)}, u32[]{:S(2)}) collective-permute-start(bf16[288,256]{1,0:T(8,128)(2,1)S(1)} %add_convert_fusion.2), channel_id=1, source_target_pairs={{0,2},{1,3},{2,4},{3,5},{4,6},{5,7},{6,0},{7,1},{8,10},{9,11},{10,... | collective-permute-start | bytes 442376 | tf_op jit(solution)/shard_map/ppermute | solution.py:421
  114.4 9.2 %collective-permute-start.21 = (bf16[128,768]{1,0:T(8,128)(2,1)S(1)}, bf16[128,768]{1,0:T(8,128)(2,1)S(1)}, u32[]{:S(2)}, u32[]{:S(2)}) collective-permute-start(bf16[128,768]{1,0:T(8,128)(2,1)S(1)} %act.7.refs_7_.refs_1_), channel_id=1, source_target_pairs={{0,8},{1,9},{2,10},{3,11},{4,12},{5,13},{6,14},{7,15},{8,0},{9,1},... | collective-permute-start | bytes 589832 | tf_op jit(solution)/shard_map/ppermute | solution.py:421
  119.4 4.2 %collective-permute-start.22 = (bf16[128,768]{1,0:T(8,128)(2,1)S(1)}, bf16[128,768]{1,0:T(8,128)(2,1)S(1)}, u32[]{:S(2)}, u32[]{:S(2)}) collective-permute-start(bf16[128,768]{1,0:T(8,128)(2,1)S(1)} %collective-permute-done.20.refs_2_), channel_id=1, source_target_pairs={{0,8},{1,9},{2,10},{3,11},{4,12},{5,13},{6,14},{7,15},{8,0},{9,1},... | collective-permute-start | bytes 589832 | tf_op jit(solution)/shard_map/ppermute | solution.py:421
  122.8 6.3 %collective-permute-start.31 = (bf16[288,256]{1,0:T(8,128)(2,1)S(1)}, bf16[288,256]{1,0:T(8,128)(2,1)S(1)}, u32[]{:S(2)}, u32[]{:S(2)}) collective-permute-start(bf16[288,256]{1,0:T(8,128)(2,1)S(1)} %get-tuple-element.65), channel_id=1, source_target_pairs={{0,1},{1,0},{2,3},{3,2},{4,5},{5,4},{6,7},{7,6},{8,9},{9,8},{10,11... | collective-permute-start | bytes 442376 | tf_op jit(solution)/shard_map/ppermute | solution.py:421
  123.5 13.2 %collective-permute-start.30 = (bf16[288,256]{1,0:T(8,128)(2,1)S(1)}, bf16[288,256]{1,0:T(8,128)(2,1)S(1)}, u32[]{:S(2)}, u32[]{:S(2)}) collective-permute-start(bf16[288,256]{1,0:T(8,128)(2,1)S(1)} %add_convert_fusion.1), channel_id=1, source_target_pairs={{0,4},{1,5},{2,6},{3,7},{4,0},{5,1},{6,2},{7,3},{8,12},{9,13},{10,... | collective-permute-start | bytes 442376 | tf_op jit(solution)/shard_map/ppermute | solution.py:421
  123.6 20.1 %copy-start.11 = (f32[2304]{0:T(1024)S(1)}, f32[2304]{0:T(1024)}, u32[]{:S(2)}) copy-start(f32[2304]{0:T(1024)} %param.19) | copy-start | bytes 27652
  123.6 20.2 %copy-start.12 = (f32[16]{0:T(128)S(1)}, f32[16]{0:T(128)}, u32[]{:S(2)}) copy-start(f32[16]{0:T(128)} %param.21) | copy-start | bytes 196
  123.6 27.8 %copy-start.6 = (bf16[2304,512]{1,0:T(8,128)(2,1)S(1)}, bf16[2304,512]{1,0:T(8,128)(2,1)}, u32[]{:S(2)}) copy-start(bf16[2304,512]{1,0:T(8,128)(2,1)} %refs_2_.1) | copy-start | bytes 7077892
  127.1 49.0 %copy-start.8 = (f32[256,288]{0,1:T(8,128)S(1)}, f32[256,288]{0,1:T(8,128)}, u32[]{:S(2)}) copy-start(f32[256,288]{0,1:T(8,128)} %param.11) | copy-start | bytes 884740
  127.1 9.6 %collective-permute-start.26 = (bf16[288,256]{1,0:T(8,128)(2,1)S(1)}, bf16[288,256]{1,0:T(8,128)(2,1)S(1)}, u32[]{:S(2)}, u32[]{:S(2)}) collective-permute-start(bf16[288,256]{1,0:T(8,128)(2,1)S(1)} %get-tuple-element.62), channel_id=1, source_target_pairs={{0,1},{1,0},{2,3},{3,2},{4,5},{5,4},{6,7},{7,6},{8,9},{9,8},{10,11... | collective-permute-start | bytes 442376 | tf_op jit(solution)/shard_map/ppermute | solution.py:421
  129.2 7.5 %collective-permute-start.32 = (bf16[288,256]{1,0:T(8,128)(2,1)S(1)}, bf16[288,256]{1,0:T(8,128)(2,1)S(1)}, u32[]{:S(2)}, u32[]{:S(2)}) collective-permute-start(bf16[288,256]{1,0:T(8,128)(2,1)S(1)} %add_convert_fusion), channel_id=1, source_target_pairs={{0,6},{1,7},{2,0},{3,1},{4,2},{5,3},{6,4},{7,5},{8,14},{9,15},{10,... | collective-permute-start | bytes 442376 | tf_op jit(solution)/shard_map/ppermute | solution.py:421
  129.3 7.4 %collective-permute-start.3 = (f32[4,288]{1,0:T(4,128)S(1)}, f32[4,288]{1,0:T(4,128)S(1)}, u32[]{:S(2)}, u32[]{:S(2)}) collective-permute-start(f32[4,288]{1,0:T(4,128)S(1)} %get-tuple-element.37), channel_id=1, source_target_pairs={{0,0},{1,1},{2,8},{3,9},{4,16},{5,17},{6,24},{7,25},{8,2},{9,3},{1... | collective-permute-start | bytes 13832 | tf_op jit(solution)/shard_map/ppermute | solution.py:421
  137.8 13.6 %all-to-all-start = ((f32[32,4,288]{2,1,0:T(4,128)}), f32[32,4,288]{2,1,0:T(4,128)S(1)}, u32[]{:S(2)}, u32[]{:S(2)}) async-start(f32[32,4,288]{2,1,0:T(4,128)} %get-tuple-element.67), calls=%async_computation | async-start | bytes 393216 | tf_op jit(solution)/shard_map/all_to_all | solution.py:502
  152.8 10.0 %all-to-all-start.1 = ((f32[32,2,16]{2,1,0:T(2,128)}), f32[32,2,16]{2,1,0:T(2,128)S(1)}, u32[]{:S(2)}, u32[]{:S(2)}) async-start(f32[32,2,16]{2,1,0:T(2,128)} %get-tuple-element.69), calls=%async_computation.1 | async-start | bytes 65536 | tf_op jit(solution)/shard_map/all_to_all | solution.py:502
  156.8 19.3 %collective-permute-start.33 = (f32[288,256]{1,0:T(8,128)S(1)}, f32[288,256]{1,0:T(8,128)S(1)}, u32[]{:S(2)}, u32[]{:S(2)}) collective-permute-start(f32[288,256]{1,0:T(8,128)S(1)} %get-tuple-element.66), channel_id=1, source_target_pairs={{0,0},{1,1},{2,8},{3,9},{4,16},{5,17},{6,24},{7,25},{8,2},{9,3},{1... | collective-permute-start | bytes 884744 | tf_op jit(solution)/shard_map/ppermute | solution.py:421
  (1 other events, 0.7 us)

commit v9 on v8

--- a/solution.py
+++ b/solution.py
@@ -27,7 +27,8 @@
     return pltpu.CompilerParams(vmem_limit_bytes=mib * 2**20)
 
 
-HINT = pl.CostEstimate(flops=1, bytes_accessed=1024, transcendentals=0)
+def hint(flops, bytes_accessed, scale=0.3):
+    return pl.CostEstimate(flops=int(flops * scale), bytes_accessed=int(bytes_accessed * scale), transcendentals=0)
 
 
 def shape(dims, dtype):
@@ -78,7 +79,7 @@
         out_specs=[whole_spec(v) for v in outs],
         out_shape=outs,
         compiler_params=params(),
-        cost_estimate=HINT,
+        cost_estimate=hint(4 * tokens * block, 6 * tokens * block),
         name="prep",
     )(tallies, x, gain, routes)
 
@@ -96,7 +97,7 @@
         out_specs=VMEM,
         out_shape=shape((len(blocks) * rows, tokens), bf16),
         compiler_params=params(),
-        cost_estimate=HINT,
+        cost_estimate=hint(1, 4 * len(blocks) * rows * tokens),
         name="join",
     )(*blocks)
 
@@ -199,7 +200,9 @@
             pltpu.VMEM((tokens, LANES), f32),
         ],
         compiler_params=params(20),
-        cost_estimate=HINT,
+        cost_estimate=hint(
+            4 * experts * depth * hidden * tokens, 4 * experts * depth * hidden + 6 * tokens * wide, 4.0
+        ),
         name="gate_up_partial",
     )(scal, *feeds, wr, wg, wu, *deps)
 
@@ -224,7 +227,7 @@
         out_specs=[VMEM, VMEM],
         out_shape=[shape((tokens // 2, wide), f32), shape((tokens // 2, wide), bf16)],
         compiler_params=params(),
-        cost_estimate=HINT,
+        cost_estimate=hint(tokens * wide, 9 * tokens * wide),
         name="core_sum",
     )(scal, own, recv, *deps)
 
@@ -256,7 +259,7 @@
         out_specs=VMEM,
         out_shape=shape((th, wide // 2), bf16),
         compiler_params=params(),
-        cost_estimate=HINT,
+        cost_estimate=hint(6 * th * wide, 7 * th * wide),
         name="act",
     )(scal, keep, recv, cols, *deps)
 
@@ -314,7 +317,9 @@
             pltpu.VMEM((width, tokens), f32),
         ],
         compiler_params=params(20),
-        cost_estimate=HINT,
+        cost_estimate=hint(
+            2 * experts * width * hidden * tokens, 2 * experts * width * hidden + 2 * width * tokens, 4.0
+        ),
         name="down",
     )(scal, *pieces, cols, wd, *deps)
 
@@ -343,7 +348,7 @@
         out_specs=[full(v) for v in outs],
         out_shape=outs,
         compiler_params=params(),
-        cost_estimate=HINT,
+        cost_estimate=hint(16 * block * tokens, 14 * block * tokens),
         name="branch_total",
     )(feed, stream, *parts)
 
@@ -381,7 +386,7 @@
         out_shape=[shape((rows, columns), f32), shape((got.shape[0], 2, rows), f32)],
         scratch_shapes=[pltpu.VMEM((LANES, LANES), f32)],
         compiler_params=params(),
-        cost_estimate=HINT,
+        cost_estimate=hint(2 * rows * WIDTH * columns, 2 * WIDTH * columns),
         name="head",
     )(got, gain, words, softness)
 
@@ -446,7 +451,7 @@
     pair = join_call(first)
     feeds = {1: pair}
     for group in (2, 3, 0):
-        feeds[group] = send(pair, lambda q, z, x, group=group: (q, (z - group + 1) % parts, x))
+        feeds[group] = send(feeds[(group - 1) % parts], lambda q, z, x: (q, (z - 1) % parts, x))
     stream = send(stream, home)
     partial, kept, pieces, shares = {}, {}, {}, {}
 
@@ -483,19 +488,19 @@
     p0 = do_partial(0)
     p1 = do_partial(1, p0)
     s0 = do_sum(0, p1)
-    s1 = do_sum(1, s0)
-    p2 = do_partial(2, s1)
-    a0 = do_act(0, p2)
+    p2 = do_partial(2, s0)
+    s1 = do_sum(1, p2)
+    a0 = do_act(0, s1)
     p3 = do_partial(3, a0)
-    a1 = do_act(1, p3)
-    s2 = do_sum(2, a1)
-    s3 = do_sum(3, s2)
-    d0 = do_down(0, s3)
-    a2 = do_act(2, d0)
+    s2 = do_sum(2, p3)
+    a1 = do_act(1, s2)
+    d0 = do_down(0, a1)
+    s3 = do_sum(3, d0)
+    a2 = do_act(2, s3)
     d1 = do_down(1, a2)
     a3 = do_act(3, d1)
     d2 = do_down(2, a3)
-    do_down(3, d2)
+    d3 = do_down(3, d2)
     mine = [v for group in range(parts) for v in shares[group]]
     total, message = total_call(feeds[0], stream, mine, block, count)
 

time: 177 us -> 166 us (0.938)
  waiting for transfers between devices: 77.6 us -> 70.2 us
  starting transfers between devices: 44.1 us -> 40.7 us
    ppermute x34, waiting for transfers between devices: 68.4 us -> 60.9 us  [send(): return lax.ppermute(value, ('dp', 'mp'), pairs)]
    all_to_all x2, starting transfers between devices: 9.84 us -> 6.66 us  [body(): everyone = lambda v: lax.all_to_all(v, ('dp', 'mp'), 0, 0, tiled=True)]
  transfers between devices with their start and end apart: 36 -> 36, of which waited for: 12 -> 13; matrix products, arithmetic and copies ran while one was open for 1% -> 1% of each run, Pallas kernels for 24% -> 25%
where the time goes in v9:
time: 166 us
  waiting for transfers between devices  70.2 us (42%)
  Pallas kernels  45.1 us (27%)
  starting transfers between devices  40.7 us (25%)
  local copies, waits for them, and re-layouts  7.3 us (4%)
  other arithmetic  1.71 us (1%)
    ppermute x34, waiting for transfers between devices, send(): return lax.ppermute(value, ('dp', 'mp'), pairs)  60.9 us
    ppermute x34, starting transfers between devices, send(): return lax.ppermute(value, ('dp', 'mp'), pairs)  34 us
    pallas_call x4, Pallas kernels, partial_call(): pl.pallas_call(lambda *refs: partial_kernel(sides, len(feeds), *refs), gr...  19.5 us
    pallas_call x4, Pallas kernels, down_call(): pl.pallas_call(lambda *refs: down_kernel(sides, *refs), grid=(experts,),...  13.8 us
    all_to_all x2, waiting for transfers between devices, body(): everyone = lambda v: lax.all_to_all(v, ('dp', 'mp'), 0, 0, tiled=True)  9.27 us
    all_to_all x2, starting transfers between devices, body(): everyone = lambda v: lax.all_to_all(v, ('dp', 'mp'), 0, 0, tiled=True)  6.66 us
    unnamed x26, local copies, waits for them, and re-layouts  6.34 us
    pallas_call x4, Pallas kernels, act_call(): pl.pallas_call(lambda *refs: act_kernel(base, *refs), in_specs=[SMEM] + [...  4.94 us
  transfers between devices with their start and end apart: 36, of which 13 were waited for; matrix products, arithmetic and copies ran while one was open for 1% of the time, Pallas kernels for 25%

profile of v9, /device:TPU:4, one launch (start us, length us, event | category | flops | bytes accessed | tf_op | source)
XLA Modules:
  0.0 166.0 jit_solution(9381200875503012008)
XLA Ops:
  1.3 1.0 copy-done.2
  3.6 0.9 prep.1
  4.5 1.5 collective-permute-start
  6.0 3.0 %collective-permute-start.1 = (bf16[304,256]{1,0:T(8,128)(2,1)S(1)}, bf16[304,256]{1,0:T(8,128)(2,1)S(1)}, u32[]{:S(2)}, u32[]{:S(2)}) collective-permute-start(bf16[304,256]{1,0:T(8,128)(2,1)S(1)} %get-tuple-element.36), channel_id=1, source_target_pairs={{0,7},{1,6},{2,15},{3,14},{4,23},{5,22},{6,31},{7,30},{8,1},{9,0},... | collective-permute-start | bytes 466952 | tf_op jit(solution)/shard_map/ppermute | solution.py:426
  9.2 3.6 %collective-permute-done.refs_0_ = bf16[304,256]{1,0:T(8,128)(2,1)S(1)} collective-permute-done((bf16[304,256]{1,0:T(8,128)(2,1)S(1)}, bf16[304,256]{1,0:T(8,128)(2,1)S(1)}, u32[]{:S(2)}, u32[]{:S(2)}) %collective-permute-start) | collective-permute-done | bytes 155680 | tf_op jit(solution)/shard_map/ppermute | solution.py:426
  12.7 4.3 %collective-permute-done.1.refs_1_ = bf16[304,256]{1,0:T(8,128)(2,1)S(1)} collective-permute-done((bf16[304,256]{1,0:T(8,128)(2,1)S(1)}, bf16[304,256]{1,0:T(8,128)(2,1)S(1)}, u32[]{:S(2)}, u32[]{:S(2)}) %collective-permute-start.1) | collective-permute-done | bytes 155680 | tf_op jit(solution)/shard_map/ppermute | solution.py:426
  17.0 5.9 %collective-permute-start.2 = (bf16[608,256]{1,0:T(8,128)(2,1)S(1)}, bf16[608,256]{1,0:T(8,128)(2,1)S(1)}, u32[]{:S(2)}, u32[]{:S(2)}) collective-permute-start(bf16[608,256]{1,0:T(8,128)(2,1)S(1)} %join.1.refs_1_), channel_id=1, source_target_pairs={{0,6},{1,7},{2,0},{3,1},{4,2},{5,3},{6,4},{7,5},{8,14},{9,15},{10,... | collective-permute-start | bytes 933896 | tf_op jit(solution)/shard_map/ppermute | solution.py:426
  23.0 2.0 %copy-done.6 = bf16[4,576,720]{2,1,0:T(8,128)(2,1)S(1)} copy-done((bf16[4,576,720]{2,1,0:T(8,128)(2,1)S(1)}, bf16[4,576,720]{2,1,0:T(8,128)(2,1)}, u32[]{:S(2)}) %copy-start.6) | copy-done | bytes 3317784
  25.0 2.0 %copy-done.8 = bf16[4,576,720]{2,1,0:T(8,128)(2,1)S(1)} copy-done((bf16[4,576,720]{2,1,0:T(8,128)(2,1)S(1)}, bf16[4,576,720]{2,1,0:T(8,128)(2,1)}, u32[]{:S(2)}) %copy-start.8) | copy-done | bytes 3317784
  27.0 4.9 %gate_up_partial.4 = (f32[256,1536]{1,0:T(8,128)S(1)}, bf16[256,1536]{1,0:T(8,128)(2,1)S(1)}, bf16[256,128]{1,0:T(8,128)(2,1)S(1)}) custom-call(s32[3]{0:T(128)S(1)} %pad_add_fusion.1.refs_0_, bf16[608,256]{1,0:T(8,128)(2,1)S(1)} %join.1.refs_1_, bf16[128,576]{1,0:T(8,128)(2,1)S(1)} %pad_add_fusion.refs_2_, bf16[4,576,720]{2,1,0:T(8,128)(2,1)S(1)} %copy-done.6, ...), custom_call_target="tpu_custom_call" | custom-call | flops 6794772480 | bytes 35979264 | tf_op jit(solution)/shard_map/gate_up_partial/pallas_call | solution.py:190
  32.1 4.9 %gate_up_partial.5 = (f32[256,1536]{1,0:T(8,128)S(1)}, bf16[256,1536]{1,0:T(8,128)(2,1)S(1)}, bf16[256,128]{1,0:T(8,128)(2,1)S(1)}) custom-call(s32[3]{0:T(128)S(1)} %pad_add_fusion.1.refs_0_, bf16[608,256]{1,0:T(8,128)(2,1)S(1)} %collective-permute-done.2.refs_1_, bf16[128,576]{1,0:T(8,128)(2,1)S(1)} %pad_add_fusion.refs_2_, ...), custom_call_target="tpu_custom_call" | custom-call | flops 6794772480 | bytes 35979264 | tf_op jit(solution)/shard_map/gate_up_partial/pallas_call | solution.py:190
  37.4 4.3 %collective-permute-done.3.refs_1_ = bf16[608,256]{1,0:T(8,128)(2,1)S(1)} collective-permute-done((bf16[608,256]{1,0:T(8,128)(2,1)S(1)}, bf16[608,256]{1,0:T(8,128)(2,1)S(1)}, u32[]{:S(2)}, u32[]{:S(2)}) %collective-permute-start.3) | collective-permute-done | bytes 311328 | tf_op jit(solution)/shard_map/ppermute | solution.py:426
  41.7 2.1 %collective-permute-start.4 = (bf16[608,256]{1,0:T(8,128)(2,1)S(1)}, bf16[608,256]{1,0:T(8,128)(2,1)S(1)}, u32[]{:S(2)}, u32[]{:S(2)}) collective-permute-start(bf16[608,256]{1,0:T(8,128)(2,1)S(1)} %collective-permute-done.3.refs_1_), channel_id=1, source_target_pairs={{0,6},{1,7},{2,0},{3,1},{4,2},{5,3},{6,4},{7,5},{8,14},{9,15},{10,... | collective-permute-start | bytes 933896 | tf_op jit(solution)/shard_map/ppermute | solution.py:426
  43.8 0.9 core_sum.4
  44.8 4.8 %gate_up_partial.6 = (f32[256,1536]{1,0:T(8,128)S(1)}, bf16[256,1536]{1,0:T(8,128)(2,1)S(1)}, bf16[256,128]{1,0:T(8,128)(2,1)S(1)}) custom-call(s32[3]{0:T(128)S(1)} %pad_add_fusion.1.refs_0_, bf16[608,256]{1,0:T(8,128)(2,1)S(1)} %collective-permute-done.3.refs_1_, bf16[128,576]{1,0:T(8,128)(2,1)S(1)} %pad_add_fusion.refs_2_, ...), custom_call_target="tpu_custom_call" | custom-call | flops 6794772480 | bytes 35979264 | tf_op jit(solution)/shard_map/gate_up_partial/pallas_call | solution.py:190
  49.7 0.9 core_sum.5
  50.6 2.1 %collective-permute-start.13 = (bf16[128,1536]{1,0:T(8,128)(2,1)S(1)}, bf16[128,1536]{1,0:T(8,128)(2,1)S(1)}, u32[]{:S(2)}, u32[]{:S(2)}) collective-permute-start(bf16[128,1536]{1,0:T(8,128)(2,1)S(1)} %get-tuple-element.49), channel_id=1, source_target_pairs={{0,16},{1,17},{2,18},{3,19},{4,20},{5,21},{6,22},{7,23},{8,24},{9,... | collective-permute-start | bytes 1179656 | tf_op jit(solution)/shard_map/ppermute | solution.py:426
  52.6 4.0 %collective-permute-done.7.refs_2_ = bf16[128,1536]{1,0:T(8,128)(2,1)S(1)} collective-permute-done((bf16[128,1536]{1,0:T(8,128)(2,1)S(1)}, bf16[128,1536]{1,0:T(8,128)(2,1)S(1)}, u32[]{:S(2)}, u32[]{:S(2)}) %collective-permute-start.7) | collective-permute-done | bytes 393248 | tf_op jit(solution)/shard_map/ppermute | solution.py:426
  56.6 1.2 act.4.refs_5_.refs_1_
  58.0 4.8 %gate_up_partial.7 = (f32[256,1536]{1,0:T(8,128)S(1)}, bf16[256,1536]{1,0:T(8,128)(2,1)S(1)}, bf16[256,128]{1,0:T(8,128)(2,1)S(1)}) custom-call(s32[3]{0:T(128)S(1)} %pad_add_fusion.1.refs_0_, bf16[608,256]{1,0:T(8,128)(2,1)S(1)} %collective-permute-done.4.refs_1_.meta, bf16[128,576]{1,0:T(8,128)(2,1)S(1)} %pad_add_fusion.refs_2_, ...), custom_call_target="tpu_custom_call" | custom-call | flops 6794772480 | bytes 35979264 | tf_op jit(solution)/shard_map/gate_up_partial/pallas_call | solution.py:190
  63.4 4.6 %collective-permute-done.10.refs_2_ = bf16[128,768]{1,0:T(8,128)(2,1)S(1)} collective-permute-done((bf16[128,768]{1,0:T(8,128)(2,1)S(1)}, bf16[128,768]{1,0:T(8,128)(2,1)S(1)}, u32[]{:S(2)}, u32[]{:S(2)}) %collective-permute-start.10) | collective-permute-done | bytes 196640 | tf_op jit(solution)/shard_map/ppermute | solution.py:426
  68.0 0.9 core_sum.6
  69.3 1.2 act.5.refs_7_.refs_1_
  70.6 1.7 %collective-permute-start.16 = (bf16[128,768]{1,0:T(8,128)(2,1)S(1)}, bf16[128,768]{1,0:T(8,128)(2,1)S(1)}, u32[]{:S(2)}, u32[]{:S(2)}) collective-permute-start(bf16[128,768]{1,0:T(8,128)(2,1)S(1)} %act.5.refs_7_.refs_1_), channel_id=1, source_target_pairs={{0,16},{1,17},{2,18},{3,19},{4,20},{5,21},{6,22},{7,23},{8,24},{9,... | collective-permute-start | bytes 589832 | tf_op jit(solution)/shard_map/ppermute | solution.py:426
  72.3 3.5 %down.4 = (bf16[288,256]{1,0:T(8,128)(2,1)S(1)}, bf16[288,256]{1,0:T(8,128)(2,1)S(1)}) custom-call(s32[3]{0:T(128)S(1)} %pad_add_fusion.1.refs_0_, bf16[128,768]{1,0:T(8,128)(2,1)S(1)} %act.4.refs_5_.refs_1_, bf16[128,768]{1,0:T(8,128)(2,1)S(1)} %collective-permute-done.10.refs_2_, bf16[128,768]{1,0:T(8,128)(2,1)S(1)} %collective-permute-done.11.refs_3_, ...), custom_call_target="tpu_custom_call" | custom-call | flops 3397386240 | bytes 14450688 | tf_op jit(solution)/shard_map/down/pallas_call | solution.py:306
  76.4 8.3 %collective-permute-done.16.refs_2_ = bf16[128,768]{1,0:T(8,128)(2,1)S(1)} collective-permute-done((bf16[128,768]{1,0:T(8,128)(2,1)S(1)}, bf16[128,768]{1,0:T(8,128)(2,1)S(1)}, u32[]{:S(2)}, u32[]{:S(2)}) %collective-permute-start.16) | collective-permute-done | bytes 196640 | tf_op jit(solution)/shard_map/ppermute | solution.py:426
  84.7 0.9 core_sum.7
  86.0 1.2 act.6.refs_7_.refs_1_
  87.2 1.7 %collective-permute-start.23 = (bf16[128,768]{1,0:T(8,128)(2,1)S(1)}, bf16[128,768]{1,0:T(8,128)(2,1)S(1)}, u32[]{:S(2)}, u32[]{:S(2)}) collective-permute-start(bf16[128,768]{1,0:T(8,128)(2,1)S(1)} %act.6.refs_7_.refs_1_), channel_id=1, source_target_pairs={{0,16},{1,17},{2,18},{3,19},{4,20},{5,21},{6,22},{7,23},{8,24},{9,... | collective-permute-start | bytes 589832 | tf_op jit(solution)/shard_map/ppermute | solution.py:426
  89.3 12.0 %collective-permute-done.23.refs_2_ = bf16[128,768]{1,0:T(8,128)(2,1)S(1)} collective-permute-done((bf16[128,768]{1,0:T(8,128)(2,1)S(1)}, bf16[128,768]{1,0:T(8,128)(2,1)S(1)}, u32[]{:S(2)}, u32[]{:S(2)}) %collective-permute-start.23) | collective-permute-done | bytes 196640 | tf_op jit(solution)/shard_map/ppermute | solution.py:426
  101.3 3.5 %down.5 = (bf16[288,256]{1,0:T(8,128)(2,1)S(1)}, bf16[288,256]{1,0:T(8,128)(2,1)S(1)}) custom-call(s32[3]{0:T(128)S(1)} %pad_add_fusion.1.refs_0_, bf16[128,768]{1,0:T(8,128)(2,1)S(1)} %act.5.refs_7_.refs_1_, bf16[128,768]{1,0:T(8,128)(2,1)S(1)} %collective-permute-done.16.refs_2_, bf16[128,768]{1,0:T(8,128)(2,1)S(1)} %collective-permute-done.17.refs_3_, ...), custom_call_target="tpu_custom_call" | custom-call | flops 3397386240 | bytes 14450688 | tf_op jit(solution)/shard_map/down/pallas_call | solution.py:306
  105.5 1.2 act.7.refs_7_.refs_1_
  107.1 3.4 %down.6 = (bf16[288,256]{1,0:T(8,128)(2,1)S(1)}, bf16[288,256]{1,0:T(8,128)(2,1)S(1)}) custom-call(s32[3]{0:T(128)S(1)} %pad_add_fusion.1.refs_0_, bf16[128,768]{1,0:T(8,128)(2,1)S(1)} %act.6.refs_7_.refs_1_, bf16[128,768]{1,0:T(8,128)(2,1)S(1)} %collective-permute-done.23.refs_2_, bf16[128,768]{1,0:T(8,128)(2,1)S(1)} %collective-permute-done.24.refs_3_, ...), custom_call_target="tpu_custom_call" | custom-call | flops 3397386240 | bytes 14450688 | tf_op jit(solution)/shard_map/down/pallas_call | solution.py:306
  110.6 1.5 collective-permute-start.31
  112.3 1.5 collective-permute-done.20.refs_2_
  113.8 2.6 %collective-permute-done.31 = bf16[288,256]{1,0:T(8,128)(2,1)S(1)} collective-permute-done((bf16[288,256]{1,0:T(8,128)(2,1)S(1)}, bf16[288,256]{1,0:T(8,128)(2,1)S(1)}, u32[]{:S(2)}, u32[]{:S(2)}) %collective-permute-start.31) | collective-permute-done | bytes 147488 | tf_op jit(solution)/shard_map/ppermute | solution.py:426
  116.7 3.5 %down.7 = (bf16[288,256]{1,0:T(8,128)(2,1)S(1)}, bf16[288,256]{1,0:T(8,128)(2,1)S(1)}) custom-call(s32[3]{0:T(128)S(1)} %pad_add_fusion.1.refs_0_, bf16[128,768]{1,0:T(8,128)(2,1)S(1)} %act.7.refs_7_.refs_1_, bf16[128,768]{1,0:T(8,128)(2,1)S(1)} %collective-permute-done.20.refs_2_, bf16[128,768]{1,0:T(8,128)(2,1)S(1)} %collective-permute-done.21.refs_3_, ...), custom_call_target="tpu_custom_call" | custom-call | flops 3397386240 | bytes 14450688 | tf_op jit(solution)/shard_map/down/pallas_call | solution.py:306
  120.2 1.5 collective-permute-start.26
  121.7 4.0 %collective-permute-start.5 = (f32[4,288]{1,0:T(4,128)S(1)}, f32[4,288]{1,0:T(4,128)S(1)}, u32[]{:S(2)}, u32[]{:S(2)}) collective-permute-start(f32[4,288]{1,0:T(4,128)S(1)} %get-tuple-element.37), channel_id=1, source_target_pairs={{0,0},{1,1},{2,8},{3,9},{4,16},{5,17},{6,24},{7,25},{8,2},{9,3},{1... | collective-permute-start | bytes 13832 | tf_op jit(solution)/shard_map/ppermute | solution.py:426
  125.7 3.3 %collective-permute-done.5.stream = f32[4,288]{1,0:T(4,128)S(1)} collective-permute-done((f32[4,288]{1,0:T(4,128)S(1)}, f32[4,288]{1,0:T(4,128)S(1)}, u32[]{:S(2)}, u32[]{:S(2)}) %collective-permute-start.5) | collective-permute-done | bytes 4640 | tf_op jit(solution)/shard_map/ppermute | solution.py:426
  129.1 1.1 branch_total.1
  130.1 2.7 %all-to-all-start = ((f32[32,4,288]{2,1,0:T(4,128)}), f32[32,4,288]{2,1,0:T(4,128)S(1)}, u32[]{:S(2)}, u32[]{:S(2)}) async-start(f32[32,4,288]{2,1,0:T(4,128)} %get-tuple-element.67), calls=%async_computation | async-start | bytes 393216 | tf_op jit(solution)/shard_map/all_to_all | solution.py:507
  133.1 7.5 %all-to-all-done.refs_0_ = f32[32,4,288]{2,1,0:T(4,128)S(1)} async-done(((f32[32,4,288]{2,1,0:T(4,128)}), f32[32,4,288]{2,1,0:T(4,128)S(1)}, u32[]{:S(2)}, u32[]{:S(2)}) %all-to-all-start) | async-done | bytes 147488 | tf_op jit(solution)/shard_map/all_to_all | solution.py:507
  140.6 1.4 head.1
  142.0 3.9 %all-to-all-start.1 = ((f32[32,2,16]{2,1,0:T(2,128)}), f32[32,2,16]{2,1,0:T(2,128)S(1)}, u32[]{:S(2)}, u32[]{:S(2)}) async-start(f32[32,2,16]{2,1,0:T(2,128)} %get-tuple-element.69), calls=%async_computation.1 | async-start | bytes 65536 | tf_op jit(solution)/shard_map/all_to_all | solution.py:507
  145.9 4.3 %collective-permute-start.33 = (f32[288,256]{1,0:T(8,128)S(1)}, f32[288,256]{1,0:T(8,128)S(1)}, u32[]{:S(2)}, u32[]{:S(2)}) collective-permute-start(f32[288,256]{1,0:T(8,128)S(1)} %get-tuple-element.66), channel_id=1, source_target_pairs={{0,0},{1,1},{2,8},{3,9},{4,16},{5,17},{6,24},{7,25},{8,2},{9,3},{1... | collective-permute-start | bytes 884744 | tf_op jit(solution)/shard_map/ppermute | solution.py:426
  150.2 1.8 %all-to-all-done.1 = f32[32,2,16]{2,1,0:T(2,128)S(1)} async-done(((f32[32,2,16]{2,1,0:T(2,128)}), f32[32,2,16]{2,1,0:T(2,128)S(1)}, u32[]{:S(2)}, u32[]{:S(2)}) %all-to-all-start.1) | async-done | bytes 4128 | tf_op jit(solution)/shard_map/all_to_all | solution.py:507
  152.8 12.5 %collective-permute-done.33 = f32[288,256]{1,0:T(8,128)S(1)} collective-permute-done((f32[288,256]{1,0:T(8,128)S(1)}, f32[288,256]{1,0:T(8,128)S(1)}, u32[]{:S(2)}, u32[]{:S(2)}) %collective-permute-start.33) | collective-permute-done | bytes 294944 | tf_op jit(solution)/shard_map/ppermute | solution.py:426
  (85 shorter events, 8.9 us)
Async XLA Ops:
  0.6 8.4 %copy-start = (bf16[2304,4]{0,1:T(4,128)(2,1)S(1)}, bf16[2304,4]{0,1:T(4,128)(2,1)}, u32[]{:S(2)}) copy-start(bf16[2304,4]{0,1:T(4,128)(2,1)} %param.15) | copy-start | bytes 55300
  1.3 1.0 copy-start.2
  2.3 0.7 copy-start.4
  4.5 8.2 %collective-permute-start = (bf16[304,256]{1,0:T(8,128)(2,1)S(1)}, bf16[304,256]{1,0:T(8,128)(2,1)S(1)}, u32[]{:S(2)}, u32[]{:S(2)}) collective-permute-start(bf16[304,256]{1,0:T(8,128)(2,1)S(1)} %get-tuple-element.36), channel_id=1, source_target_pairs={{0,6},{1,7},{2,14},{3,15},{4,22},{5,23},{6,30},{7,31},{8,0},{9,1},... | collective-permute-start | bytes 466952 | tf_op jit(solution)/shard_map/ppermute | solution.py:426
  6.0 11.0 %collective-permute-start.1 = (bf16[304,256]{1,0:T(8,128)(2,1)S(1)}, bf16[304,256]{1,0:T(8,128)(2,1)S(1)}, u32[]{:S(2)}, u32[]{:S(2)}) collective-permute-start(bf16[304,256]{1,0:T(8,128)(2,1)S(1)} %get-tuple-element.36), channel_id=1, source_target_pairs={{0,7},{1,6},{2,15},{3,14},{4,23},{5,22},{6,31},{7,30},{8,1},{9,0},... | collective-permute-start | bytes 466952 | tf_op jit(solution)/shard_map/ppermute | solution.py:426
  17.0 14.9 %collective-permute-start.2 = (bf16[608,256]{1,0:T(8,128)(2,1)S(1)}, bf16[608,256]{1,0:T(8,128)(2,1)S(1)}, u32[]{:S(2)}, u32[]{:S(2)}) collective-permute-start(bf16[608,256]{1,0:T(8,128)(2,1)S(1)} %join.1.refs_1_), channel_id=1, source_target_pairs={{0,6},{1,7},{2,0},{3,1},{4,2},{5,3},{6,4},{7,5},{8,14},{9,15},{10,... | collective-permute-start | bytes 933896 | tf_op jit(solution)/shard_map/ppermute | solution.py:426
  23.0 2.0 %copy-start.6 = (bf16[4,576,720]{2,1,0:T(8,128)(2,1)S(1)}, bf16[4,576,720]{2,1,0:T(8,128)(2,1)}, u32[]{:S(2)}) copy-start(bf16[4,576,720]{2,1,0:T(8,128)(2,1)} %refs_3_.7) | copy-start | bytes 9953284
  25.0 2.0 %copy-start.8 = (bf16[4,576,720]{2,1,0:T(8,128)(2,1)S(1)}, bf16[4,576,720]{2,1,0:T(8,128)(2,1)}, u32[]{:S(2)}) copy-start(bf16[4,576,720]{2,1,0:T(8,128)(2,1)} %refs_4_.7) | copy-start | bytes 9953284
  27.0 5.1 %copy-start.7 = (bf16[4,576,720]{2,1,0:T(8,128)(2,1)S(1)}, bf16[4,576,720]{2,1,0:T(8,128)(2,1)}, u32[]{:S(2)}) copy-start(bf16[4,576,720]{2,1,0:T(8,128)(2,1)} %refs_3_.7) | copy-start | bytes 9953284
  27.0 5.1 %copy-start.9 = (bf16[4,576,720]{2,1,0:T(8,128)(2,1)S(1)}, bf16[4,576,720]{2,1,0:T(8,128)(2,1)}, u32[]{:S(2)}) copy-start(bf16[4,576,720]{2,1,0:T(8,128)(2,1)} %refs_4_.7) | copy-start | bytes 9953284
  31.9 11.9 %collective-permute-start.6 = (bf16[256,1536]{1,0:T(8,128)(2,1)S(1)}, bf16[256,1536]{1,0:T(8,128)(2,1)S(1)}, u32[]{:S(2)}, u32[]{:S(2)}) collective-permute-start(bf16[256,1536]{1,0:T(8,128)(2,1)S(1)} %get-tuple-element.39), channel_id=1, source_target_pairs={{0,8},{1,9},{2,10},{3,11},{4,12},{5,13},{6,14},{7,15},{8,0},{9,1},... | collective-permute-start | bytes 2359304 | tf_op jit(solution)/shard_map/ppermute | solution.py:426
  32.0 9.8 %collective-permute-start.3 = (bf16[608,256]{1,0:T(8,128)(2,1)S(1)}, bf16[608,256]{1,0:T(8,128)(2,1)S(1)}, u32[]{:S(2)}, u32[]{:S(2)}) collective-permute-start(bf16[608,256]{1,0:T(8,128)(2,1)S(1)} %collective-permute-done.2.refs_1_), channel_id=1, source_target_pairs={{0,6},{1,7},{2,0},{3,1},{4,2},{5,3},{6,4},{7,5},{8,14},{9,15},{10,... | collective-permute-start | bytes 933896 | tf_op jit(solution)/shard_map/ppermute | solution.py:426
  36.9 12.8 %collective-permute-start.8 = (bf16[256,1536]{1,0:T(8,128)(2,1)S(1)}, bf16[256,1536]{1,0:T(8,128)(2,1)S(1)}, u32[]{:S(2)}, u32[]{:S(2)}) collective-permute-start(bf16[256,1536]{1,0:T(8,128)(2,1)S(1)} %get-tuple-element.44), channel_id=1, source_target_pairs={{0,8},{1,9},{2,10},{3,11},{4,12},{5,13},{6,14},{7,15},{8,0},{9,1},... | collective-permute-start | bytes 2359304 | tf_op jit(solution)/shard_map/ppermute | solution.py:426
  41.7 16.2 %collective-permute-start.4 = (bf16[608,256]{1,0:T(8,128)(2,1)S(1)}, bf16[608,256]{1,0:T(8,128)(2,1)S(1)}, u32[]{:S(2)}, u32[]{:S(2)}) collective-permute-start(bf16[608,256]{1,0:T(8,128)(2,1)S(1)} %collective-permute-done.3.refs_1_), channel_id=1, source_target_pairs={{0,6},{1,7},{2,0},{3,1},{4,2},{5,3},{6,4},{7,5},{8,14},{9,15},{10,... | collective-permute-start | bytes 933896 | tf_op jit(solution)/shard_map/ppermute | solution.py:426
  44.7 11.9 %collective-permute-start.7 = (bf16[128,1536]{1,0:T(8,128)(2,1)S(1)}, bf16[128,1536]{1,0:T(8,128)(2,1)S(1)}, u32[]{:S(2)}, u32[]{:S(2)}) collective-permute-start(bf16[128,1536]{1,0:T(8,128)(2,1)S(1)} %get-tuple-element.42), channel_id=1, source_target_pairs={{0,16},{1,17},{2,18},{3,19},{4,20},{5,21},{6,22},{7,23},{8,24},{9,... | collective-permute-start | bytes 1179656 | tf_op jit(solution)/shard_map/ppermute | solution.py:426
  49.6 18.4 %collective-permute-start.14 = (bf16[256,1536]{1,0:T(8,128)(2,1)S(1)}, bf16[256,1536]{1,0:T(8,128)(2,1)S(1)}, u32[]{:S(2)}, u32[]{:S(2)}) collective-permute-start(bf16[256,1536]{1,0:T(8,128)(2,1)S(1)} %get-tuple-element.51), channel_id=1, source_target_pairs={{0,8},{1,9},{2,10},{3,11},{4,12},{5,13},{6,14},{7,15},{8,0},{9,1},... | collective-permute-start | bytes 2359304 | tf_op jit(solution)/shard_map/ppermute | solution.py:426
  50.6 18.7 %collective-permute-start.13 = (bf16[128,1536]{1,0:T(8,128)(2,1)S(1)}, bf16[128,1536]{1,0:T(8,128)(2,1)S(1)}, u32[]{:S(2)}, u32[]{:S(2)}) collective-permute-start(bf16[128,1536]{1,0:T(8,128)(2,1)S(1)} %get-tuple-element.49), channel_id=1, source_target_pairs={{0,16},{1,17},{2,18},{3,19},{4,20},{5,21},{6,22},{7,23},{8,24},{9,... | collective-permute-start | bytes 1179656 | tf_op jit(solution)/shard_map/ppermute | solution.py:426
  57.9 10.1 %collective-permute-start.10 = (bf16[128,768]{1,0:T(8,128)(2,1)S(1)}, bf16[128,768]{1,0:T(8,128)(2,1)S(1)}, u32[]{:S(2)}, u32[]{:S(2)}) collective-permute-start(bf16[128,768]{1,0:T(8,128)(2,1)S(1)} %act.4.refs_5_.refs_1_), channel_id=1, source_target_pairs={{0,16},{1,17},{2,18},{3,19},{4,20},{5,21},{6,22},{7,23},{8,24},{9,... | collective-permute-start | bytes 589832 | tf_op jit(solution)/shard_map/ppermute | solution.py:426
  62.8 21.8 %collective-permute-start.9 = (bf16[256,1536]{1,0:T(8,128)(2,1)S(1)}, bf16[256,1536]{1,0:T(8,128)(2,1)S(1)}, u32[]{:S(2)}, u32[]{:S(2)}) collective-permute-start(bf16[256,1536]{1,0:T(8,128)(2,1)S(1)} %get-tuple-element.48), channel_id=1, source_target_pairs={{0,8},{1,9},{2,10},{3,11},{4,12},{5,13},{6,14},{7,15},{8,0},{9,1},... | collective-permute-start | bytes 2359304 | tf_op jit(solution)/shard_map/ppermute | solution.py:426
  62.9 9.4 %collective-permute-start.11 = (bf16[128,768]{1,0:T(8,128)(2,1)S(1)}, bf16[128,768]{1,0:T(8,128)(2,1)S(1)}, u32[]{:S(2)}, u32[]{:S(2)}) collective-permute-start(bf16[128,768]{1,0:T(8,128)(2,1)S(1)} %act.4.refs_5_.refs_1_), channel_id=1, source_target_pairs={{0,8},{1,9},{2,10},{3,11},{4,12},{5,13},{6,14},{7,15},{8,0},{9,1},... | collective-permute-start | bytes 589832 | tf_op jit(solution)/shard_map/ppermute | solution.py:426
  68.0 4.3 %collective-permute-start.12 = (bf16[128,768]{1,0:T(8,128)(2,1)S(1)}, bf16[128,768]{1,0:T(8,128)(2,1)S(1)}, u32[]{:S(2)}, u32[]{:S(2)}) collective-permute-start(bf16[128,768]{1,0:T(8,128)(2,1)S(1)} %collective-permute-done.10.refs_2_), channel_id=1, source_target_pairs={{0,8},{1,9},{2,10},{3,11},{4,12},{5,13},{6,14},{7,15},{8,0},{9,1},... | collective-permute-start | bytes 589832 | tf_op jit(solution)/shard_map/ppermute | solution.py:426
  68.0 4.3 %copy-start.10 = (bf16[4,720,576]{1,2,0:T(8,128)(2,1)S(1)}, bf16[4,720,576]{1,2,0:T(8,128)(2,1)}, u32[]{:S(2)}) copy-start(bf16[4,720,576]{1,2,0:T(8,128)(2,1)} %param.18) | copy-start | bytes 9953284
  68.9 17.1 %collective-permute-start.19 = (bf16[128,1536]{1,0:T(8,128)(2,1)S(1)}, bf16[128,1536]{1,0:T(8,128)(2,1)S(1)}, u32[]{:S(2)}, u32[]{:S(2)}) collective-permute-start(bf16[128,1536]{1,0:T(8,128)(2,1)S(1)} %get-tuple-element.57), channel_id=1, source_target_pairs={{0,16},{1,17},{2,18},{3,19},{4,20},{5,21},{6,22},{7,23},{8,24},{9,... | collective-permute-start | bytes 1179656 | tf_op jit(solution)/shard_map/ppermute | solution.py:426
  70.6 14.1 %collective-permute-start.16 = (bf16[128,768]{1,0:T(8,128)(2,1)S(1)}, bf16[128,768]{1,0:T(8,128)(2,1)S(1)}, u32[]{:S(2)}, u32[]{:S(2)}) collective-permute-start(bf16[128,768]{1,0:T(8,128)(2,1)S(1)} %act.5.refs_7_.refs_1_), channel_id=1, source_target_pairs={{0,16},{1,17},{2,18},{3,19},{4,20},{5,21},{6,22},{7,23},{8,24},{9,... | collective-permute-start | bytes 589832 | tf_op jit(solution)/shard_map/ppermute | solution.py:426
  75.8 13.2 %collective-permute-start.27 = (bf16[288,256]{1,0:T(8,128)(2,1)S(1)}, bf16[288,256]{1,0:T(8,128)(2,1)S(1)}, u32[]{:S(2)}, u32[]{:S(2)}) collective-permute-start(bf16[288,256]{1,0:T(8,128)(2,1)S(1)} %get-tuple-element.63), channel_id=1, source_target_pairs={{0,1},{1,0},{2,3},{3,2},{4,5},{5,4},{6,7},{7,6},{8,9},{9,8},{10,11... | collective-permute-start | bytes 442376 | tf_op jit(solution)/shard_map/ppermute | solution.py:426
  76.4 12.8 %collective-permute-start.17 = (bf16[128,768]{1,0:T(8,128)(2,1)S(1)}, bf16[128,768]{1,0:T(8,128)(2,1)S(1)}, u32[]{:S(2)}, u32[]{:S(2)}) collective-permute-start(bf16[128,768]{1,0:T(8,128)(2,1)S(1)} %act.5.refs_7_.refs_1_), channel_id=1, source_target_pairs={{0,8},{1,9},{2,10},{3,11},{4,12},{5,13},{6,14},{7,15},{8,0},{9,1},... | collective-permute-start | bytes 589832 | tf_op jit(solution)/shard_map/ppermute | solution.py:426
  84.7 16.7 %collective-permute-start.18 = (bf16[128,768]{1,0:T(8,128)(2,1)S(1)}, bf16[128,768]{1,0:T(8,128)(2,1)S(1)}, u32[]{:S(2)}, u32[]{:S(2)}) collective-permute-start(bf16[128,768]{1,0:T(8,128)(2,1)S(1)} %collective-permute-done.16.refs_2_), channel_id=1, source_target_pairs={{0,8},{1,9},{2,10},{3,11},{4,12},{5,13},{6,14},{7,15},{8,0},{9,1},... | collective-permute-start | bytes 589832 | tf_op jit(solution)/shard_map/ppermute | solution.py:426
  85.5 19.9 %collective-permute-start.15 = (bf16[128,1536]{1,0:T(8,128)(2,1)S(1)}, bf16[128,1536]{1,0:T(8,128)(2,1)S(1)}, u32[]{:S(2)}, u32[]{:S(2)}) collective-permute-start(bf16[128,1536]{1,0:T(8,128)(2,1)S(1)} %get-tuple-element.55), channel_id=1, source_target_pairs={{0,16},{1,17},{2,18},{3,19},{4,20},{5,21},{6,22},{7,23},{8,24},{9,... | collective-permute-start | bytes 1179656 | tf_op jit(solution)/shard_map/ppermute | solution.py:426
  87.2 14.1 %collective-permute-start.23 = (bf16[128,768]{1,0:T(8,128)(2,1)S(1)}, bf16[128,768]{1,0:T(8,128)(2,1)S(1)}, u32[]{:S(2)}, u32[]{:S(2)}) collective-permute-start(bf16[128,768]{1,0:T(8,128)(2,1)S(1)} %act.6.refs_7_.refs_1_), channel_id=1, source_target_pairs={{0,16},{1,17},{2,18},{3,19},{4,20},{5,21},{6,22},{7,23},{8,24},{9,... | collective-permute-start | bytes 589832 | tf_op jit(solution)/shard_map/ppermute | solution.py:426
  89.0 40.1 %collective-permute-start.28 = (bf16[288,256]{1,0:T(8,128)(2,1)S(1)}, bf16[288,256]{1,0:T(8,128)(2,1)S(1)}, u32[]{:S(2)}, u32[]{:S(2)}) collective-permute-start(bf16[288,256]{1,0:T(8,128)(2,1)S(1)} %add_convert_fusion.2), channel_id=1, source_target_pairs={{0,2},{1,3},{2,4},{3,5},{4,6},{5,7},{6,0},{7,1},{8,10},{9,11},{10,... | collective-permute-start | bytes 442376 | tf_op jit(solution)/shard_map/ppermute | solution.py:426
  89.2 17.9 %collective-permute-start.24 = (bf16[128,768]{1,0:T(8,128)(2,1)S(1)}, bf16[128,768]{1,0:T(8,128)(2,1)S(1)}, u32[]{:S(2)}, u32[]{:S(2)}) collective-permute-start(bf16[128,768]{1,0:T(8,128)(2,1)S(1)} %act.6.refs_7_.refs_1_), channel_id=1, source_target_pairs={{0,8},{1,9},{2,10},{3,11},{4,12},{5,13},{6,14},{7,15},{8,0},{9,1},... | collective-permute-start | bytes 589832 | tf_op jit(solution)/shard_map/ppermute | solution.py:426
  101.3 5.8 %collective-permute-start.25 = (bf16[128,768]{1,0:T(8,128)(2,1)S(1)}, bf16[128,768]{1,0:T(8,128)(2,1)S(1)}, u32[]{:S(2)}, u32[]{:S(2)}) collective-permute-start(bf16[128,768]{1,0:T(8,128)(2,1)S(1)} %collective-permute-done.23.refs_2_), channel_id=1, source_target_pairs={{0,8},{1,9},{2,10},{3,11},{4,12},{5,13},{6,14},{7,15},{8,0},{9,1},... | collective-permute-start | bytes 589832 | tf_op jit(solution)/shard_map/ppermute | solution.py:426
  104.8 7.3 %collective-permute-start.29 = (bf16[288,256]{1,0:T(8,128)(2,1)S(1)}, bf16[288,256]{1,0:T(8,128)(2,1)S(1)}, u32[]{:S(2)}, u32[]{:S(2)}) collective-permute-start(bf16[288,256]{1,0:T(8,128)(2,1)S(1)} %get-tuple-element.64), channel_id=1, source_target_pairs={{0,1},{1,0},{2,3},{3,2},{4,5},{5,4},{6,7},{7,6},{8,9},{9,8},{10,11... | collective-permute-start | bytes 442376 | tf_op jit(solution)/shard_map/ppermute | solution.py:426
  106.7 7.1 %collective-permute-start.20 = (bf16[128,768]{1,0:T(8,128)(2,1)S(1)}, bf16[128,768]{1,0:T(8,128)(2,1)S(1)}, u32[]{:S(2)}, u32[]{:S(2)}) collective-permute-start(bf16[128,768]{1,0:T(8,128)(2,1)S(1)} %act.7.refs_7_.refs_1_), channel_id=1, source_target_pairs={{0,16},{1,17},{2,18},{3,19},{4,20},{5,21},{6,22},{7,23},{8,24},{9,... | collective-permute-start | bytes 589832 | tf_op jit(solution)/shard_map/ppermute | solution.py:426
  110.6 5.8 %collective-permute-start.31 = (bf16[288,256]{1,0:T(8,128)(2,1)S(1)}, bf16[288,256]{1,0:T(8,128)(2,1)S(1)}, u32[]{:S(2)}, u32[]{:S(2)}) collective-permute-start(bf16[288,256]{1,0:T(8,128)(2,1)S(1)} %get-tuple-element.65), channel_id=1, source_target_pairs={{0,1},{1,0},{2,3},{3,2},{4,5},{5,4},{6,7},{7,6},{8,9},{9,8},{10,11... | collective-permute-start | bytes 442376 | tf_op jit(solution)/shard_map/ppermute | solution.py:426
  112.2 16.9 %collective-permute-start.30 = (bf16[288,256]{1,0:T(8,128)(2,1)S(1)}, bf16[288,256]{1,0:T(8,128)(2,1)S(1)}, u32[]{:S(2)}, u32[]{:S(2)}) collective-permute-start(bf16[288,256]{1,0:T(8,128)(2,1)S(1)} %add_convert_fusion.1), channel_id=1, source_target_pairs={{0,4},{1,5},{2,6},{3,7},{4,0},{5,1},{6,2},{7,3},{8,12},{9,13},{10,... | collective-permute-start | bytes 442376 | tf_op jit(solution)/shard_map/ppermute | solution.py:426
  112.2 4.5 %collective-permute-start.21 = (bf16[128,768]{1,0:T(8,128)(2,1)S(1)}, bf16[128,768]{1,0:T(8,128)(2,1)S(1)}, u32[]{:S(2)}, u32[]{:S(2)}) collective-permute-start(bf16[128,768]{1,0:T(8,128)(2,1)S(1)} %act.7.refs_7_.refs_1_), channel_id=1, source_target_pairs={{0,8},{1,9},{2,10},{3,11},{4,12},{5,13},{6,14},{7,15},{8,0},{9,1},... | collective-permute-start | bytes 589832 | tf_op jit(solution)/shard_map/ppermute | solution.py:426
  113.8 2.9 %collective-permute-start.22 = (bf16[128,768]{1,0:T(8,128)(2,1)S(1)}, bf16[128,768]{1,0:T(8,128)(2,1)S(1)}, u32[]{:S(2)}, u32[]{:S(2)}) collective-permute-start(bf16[128,768]{1,0:T(8,128)(2,1)S(1)} %collective-permute-done.20.refs_2_), channel_id=1, source_target_pairs={{0,8},{1,9},{2,10},{3,11},{4,12},{5,13},{6,14},{7,15},{8,0},{9,1},... | collective-permute-start | bytes 589832 | tf_op jit(solution)/shard_map/ppermute | solution.py:426
  116.4 16.5 %copy-start.11 = (f32[2304]{0:T(1024)S(1)}, f32[2304]{0:T(1024)}, u32[]{:S(2)}) copy-start(f32[2304]{0:T(1024)} %param.19) | copy-start | bytes 27652
  116.4 16.5 %copy-start.12 = (f32[16]{0:T(128)S(1)}, f32[16]{0:T(128)}, u32[]{:S(2)}) copy-start(f32[16]{0:T(128)} %param.21) | copy-start | bytes 196
  116.4 12.6 %collective-permute-start.32 = (bf16[288,256]{1,0:T(8,128)(2,1)S(1)}, bf16[288,256]{1,0:T(8,128)(2,1)S(1)}, u32[]{:S(2)}, u32[]{:S(2)}) collective-permute-start(bf16[288,256]{1,0:T(8,128)(2,1)S(1)} %add_convert_fusion), channel_id=1, source_target_pairs={{0,6},{1,7},{2,0},{3,1},{4,2},{5,3},{6,4},{7,5},{8,14},{9,15},{10,... | collective-permute-start | bytes 442376 | tf_op jit(solution)/shard_map/ppermute | solution.py:426
  116.7 23.8 %copy-start.1 = (bf16[2304,512]{1,0:T(8,128)(2,1)S(1)}, bf16[2304,512]{1,0:T(8,128)(2,1)}, u32[]{:S(2)}) copy-start(bf16[2304,512]{1,0:T(8,128)(2,1)} %refs_2_.1) | copy-start | bytes 7077892
  120.2 45.1 %copy-start.3 = (f32[256,288]{0,1:T(8,128)S(1)}, f32[256,288]{0,1:T(8,128)}, u32[]{:S(2)}) copy-start(f32[256,288]{0,1:T(8,128)} %param.11) | copy-start | bytes 884740
  120.2 8.8 %collective-permute-start.26 = (bf16[288,256]{1,0:T(8,128)(2,1)S(1)}, bf16[288,256]{1,0:T(8,128)(2,1)S(1)}, u32[]{:S(2)}, u32[]{:S(2)}) collective-permute-start(bf16[288,256]{1,0:T(8,128)(2,1)S(1)} %get-tuple-element.62), channel_id=1, source_target_pairs={{0,1},{1,0},{2,3},{3,2},{4,5},{5,4},{6,7},{7,6},{8,9},{9,8},{10,11... | collective-permute-start | bytes 442376 | tf_op jit(solution)/shard_map/ppermute | solution.py:426
  121.7 7.3 %collective-permute-start.5 = (f32[4,288]{1,0:T(4,128)S(1)}, f32[4,288]{1,0:T(4,128)S(1)}, u32[]{:S(2)}, u32[]{:S(2)}) collective-permute-start(f32[4,288]{1,0:T(4,128)S(1)} %get-tuple-element.37), channel_id=1, source_target_pairs={{0,0},{1,1},{2,8},{3,9},{4,16},{5,17},{6,24},{7,25},{8,2},{9,3},{1... | collective-permute-start | bytes 13832 | tf_op jit(solution)/shard_map/ppermute | solution.py:426
  130.1 10.4 %all-to-all-start = ((f32[32,4,288]{2,1,0:T(4,128)}), f32[32,4,288]{2,1,0:T(4,128)S(1)}, u32[]{:S(2)}, u32[]{:S(2)}) async-start(f32[32,4,288]{2,1,0:T(4,128)} %get-tuple-element.67), calls=%async_computation | async-start | bytes 393216 | tf_op jit(solution)/shard_map/all_to_all | solution.py:507
  142.0 10.0 %all-to-all-start.1 = ((f32[32,2,16]{2,1,0:T(2,128)}), f32[32,2,16]{2,1,0:T(2,128)S(1)}, u32[]{:S(2)}, u32[]{:S(2)}) async-start(f32[32,2,16]{2,1,0:T(2,128)} %get-tuple-element.69), calls=%async_computation.1 | async-start | bytes 65536 | tf_op jit(solution)/shard_map/all_to_all | solution.py:507
  145.9 19.3 %collective-permute-start.33 = (f32[288,256]{1,0:T(8,128)S(1)}, f32[288,256]{1,0:T(8,128)S(1)}, u32[]{:S(2)}, u32[]{:S(2)}) collective-permute-start(f32[288,256]{1,0:T(8,128)S(1)} %get-tuple-element.66), channel_id=1, source_target_pairs={{0,0},{1,1},{2,8},{3,9},{4,16},{5,17},{6,24},{7,25},{8,2},{9,3},{1... | collective-permute-start | bytes 884744 | tf_op jit(solution)/shard_map/ppermute | solution.py:426
  (1 other events, 0.7 us)

commit v10 on v9

--- a/solution.py
+++ b/solution.py
@@ -28,7 +28,7 @@
 
 
 def hint(flops, bytes_accessed, scale=0.3):
-    return pl.CostEstimate(flops=int(flops * scale), bytes_accessed=int(bytes_accessed * scale), transcendentals=0)
+    return pl.CostEstimate(int(flops * scale), 0, int(bytes_accessed * scale))
 
 
 def shape(dims, dtype):
@@ -78,7 +78,7 @@
         in_specs=[SMEM] + [whole_spec(v) for v in (x, gain, routes)],
         out_specs=[whole_spec(v) for v in outs],
         out_shape=outs,
-        compiler_params=params(),
+        compiler_params=params(60),
         cost_estimate=hint(4 * tokens * block, 6 * tokens * block),
         name="prep",
     )(tallies, x, gain, routes)
@@ -181,7 +181,7 @@
         give[:, last] = spread_lanes(jnp.where(lane < base, acc[:, last], more), base)
 
 
-def partial_call(scal, sides, feeds, wr, wg, wu, deps):
+def partial_call(scal, sides, feeds, wr, wg, wu, mib, deps):
     experts, depth, hidden = wg.shape
     tokens = feeds[0].shape[1] * len(feeds)
     deep, wide = up_to(depth), 2 * up_to(hidden)
@@ -199,9 +199,9 @@
             pltpu.VMEM((tokens, wide), f32),
             pltpu.VMEM((tokens, LANES), f32),
         ],
-        compiler_params=params(20),
+        compiler_params=params(mib),
         cost_estimate=hint(
-            4 * experts * depth * hidden * tokens, 4 * experts * depth * hidden + 6 * tokens * wide, 4.0
+            4 * experts * depth * hidden * tokens, 4 * experts * depth * hidden + 6 * tokens * wide, 4
         ),
         name="gate_up_partial",
     )(scal, *feeds, wr, wg, wu, *deps)
@@ -318,47 +318,54 @@
         ],
         compiler_params=params(20),
         cost_estimate=hint(
-            2 * experts * width * hidden * tokens, 2 * experts * width * hidden + 2 * width * tokens, 4.0
+            2 * experts * width * hidden * tokens, 2 * experts * width * hidden + 2 * width * tokens, 4
         ),
         name="down",
     )(scal, *pieces, cols, wd, *deps)
 
 
-def total_kernel(meta, stream, *refs):
-    parts, (total, message) = refs[:-2], refs[-2:]
-    v = parts[0][...].astype(f32)
-    for ref in parts[1:]:
-        v = v + ref[...].astype(f32)
-    total[...] = v
+def ends_kernel(sides, cols, stream, *refs):
+    outs, backs, message = refs[:sides], refs[sides : sides + 3], refs[sides + 3]
     reqs = stream.shape[0]
-    ends = columns_at(meta[5:6].astype(f32), v)
-    ends = stream[...] + branch_scale * ends[0:reqs]
-    message[...] = jnp.broadcast_to(ends[None], message.shape)
-
-
-def total_call(feed, stream, parts, block, count):
-    tokens = feed.shape[1]
-    full = lambda v: pl.BlockSpec(v.shape, lambda n: (0,) * len(v.shape))
-    outs = [shape((block, tokens), f32), shape((count, *stream.shape), f32)]
-    return pl.pallas_call(
-        total_kernel,
+    mark = cols[...].astype(f32).T[5:6]
+    for i, ref in enumerate(outs):
+        v = ref[...].astype(f32)
+        if i == 0:
+            for back in backs:
+                v = v + back[...].astype(f32)
+        ends = branch_scale * columns_at(mark, v)[0:reqs]
+        if i == 0:
+            ends = ends + stream[...]
+        message[:, i * reqs : (i + 1) * reqs] = jnp.broadcast_to(ends[None], (message.shape[0], *ends.shape))
+
+
+def ends_call(cols, stream, outs, backs, count):
+    reqs, block = stream.shape
+    args = (cols, stream, *outs, *backs)
+    out = shape((count, len(outs) * reqs, block), f32)
+    return pl.pallas_call(
+        lambda *refs: ends_kernel(len(outs), *refs),
         grid=(1,),
-        in_specs=[pl.BlockSpec((META, tokens), lambda n: (block // META, 0)), full(stream)]
-        + [full(v) for v in parts],
-        out_specs=[full(v) for v in outs],
-        out_shape=outs,
+        in_specs=[whole_spec(v) for v in args],
+        out_specs=whole_spec(out),
+        out_shape=out,
         compiler_params=params(),
-        cost_estimate=hint(16 * block * tokens, 14 * block * tokens),
-        name="branch_total",
-    )(feed, stream, *parts)
+        cost_estimate=hint(16 * block * cols.shape[0], 14 * block * cols.shape[0]),
+        name="end_rows",
+    )(*args)
 
 
 def head_kernel(order, got, gain, words, softness, logits, message, wide):
     blocks, block = gain.shape
     rows, columns = logits.shape
     ends, squares = [], 0.0
+    reqs = rows // len(order[0])
     for b in range(blocks):
-        v = jnp.concatenate([got[i] for i in order[b]], axis=0)
+        v = []
+        for sources in order[b]:
+            terms = [got[at, i * reqs : (i + 1) * reqs] for at, i in sources]
+            v.append(sum(terms[1:], terms[0]))
+        v = jnp.concatenate(v, axis=0)
         squares = squares + jnp.sum(v * v, axis=1, keepdims=True)
         ends.append(v)
     scale = lax.rsqrt(squares / WIDTH + epsilon)
@@ -450,13 +457,14 @@
     first = [send(sent, lambda q, z, x, i=i: (z, (q - 1) % parts, x ^ i)) for i in range(sides)]
     pair = join_call(first)
     feeds = {1: pair}
-    for group in (2, 3, 0):
-        feeds[group] = send(feeds[(group - 1) % parts], lambda q, z, x: (q, (z - 1) % parts, x))
+    step = lambda v: send(v, lambda q, z, x: (q, (z - 1) % parts, x))
+    feeds[2] = step(pair)
+    feeds[3] = step(feeds[2])
     stream = send(stream, home)
-    partial, kept, pieces, shares = {}, {}, {}, {}
+    partial, kept, pieces, shares, last = {}, {}, {}, {}, []
 
     def do_partial(s, *deps):
-        own, give, cols = partial_call(scal, sides, [feeds[g] for g in chunks[s]], wr, wg, wu, deps)
+        own, give, cols = partial_call(scal, sides, [feeds[g] for g in chunks[s]], wr, wg, wu, 20 if s else 57, deps)
         partial[s] = (own, send(give, other_core), cols)
         return own
 
@@ -468,12 +476,17 @@
 
     def do_act(s, *deps):
         a = act_call(scal, base, *kept[s], partial[s][2], deps)
-        a_y = send(a, other_y)
-        pieces[s] = (a, a_y, send(a, other_core), send(a_y, other_core))
+        pieces[s] = (a, send(a, other_y))
         return a
+
+    def do_hop(s, dep):
+        a, a_y = pieces[s]
+        late = [v if dep is None else lax.optimization_barrier((v, dep))[0] for v in (a, a_y)]
+        pieces[s] = (a, a_y, *[send(v, other_core) for v in late])
 
     def do_down(s, *deps):
         outs = down_call(scal, sides, pieces[s], partial[s][2], wd, deps)
+        last[:] = outs
         got = [outs[0]] + [send(outs[i], lambda q, z, x, i=i: (q, z, x ^ i)) for i in range(1, sides)]
         for n, group in enumerate(chunks[s]):
             to = slice(n * tokens, (n + 1) * tokens)
@@ -489,27 +502,33 @@
     p1 = do_partial(1, p0)
     s0 = do_sum(0, p1)
     p2 = do_partial(2, s0)
+    feeds[0] = step(lax.optimization_barrier((feeds[3], p2))[0])
     s1 = do_sum(1, p2)
     a0 = do_act(0, s1)
     p3 = do_partial(3, a0)
     s2 = do_sum(2, p3)
+    do_hop(0, s2)
     a1 = do_act(1, s2)
     d0 = do_down(0, a1)
     s3 = do_sum(3, d0)
+    do_hop(1, s3)
     a2 = do_act(2, s3)
     d1 = do_down(1, a2)
+    do_hop(2, None)
     a3 = do_act(3, d1)
     d2 = do_down(2, a3)
+    do_hop(3, None)
     d3 = do_down(3, d2)
-    mine = [v for group in range(parts) for v in shares[group]]
-    total, message = total_call(feeds[0], stream, mine, block, count)
+    backs = [shares[group][0] for group in range(1, parts)]
+    message = ends_call(partial[parts - 1][2], stream, last, backs, count)
+    total = sum(v.astype(f32) for v in shares[0] + backs)
 
     everyone = lambda v: lax.all_to_all(v, ("dp", "mp"), 0, 0, tiled=True)
     got = everyone(message)
     branch = send(total, home)
     order = [
         [
-            (q * spread + r) * mp + z * sides + x
+            [((q * spread + r) * mp + z * sides + x2, x2 ^ x) for x2 in range(sides)]
             for z in range(parts)
             for r in range(spread)
         ]

time: 166 us -> 157 us (0.946); the launches traced: 166 us -> 154 us
  waiting for transfers between devices: 70.2 us -> 47.5 us
  Pallas kernels: 45.1 us -> 49.4 us
  starting transfers between devices: 40.7 us -> 44.2 us
  other arithmetic: 1.71 us -> 4.57 us
    ppermute x34, waiting for transfers between devices: 60.9 us -> 30.7 us  [send(): return lax.ppermute(value, ('dp', 'mp'), pairs)]
    all_to_all x2, waiting for transfers between devices: 9.27 us -> 16.7 us  [body(): everyone = lambda v: lax.all_to_all(v, ('dp', 'mp'), 0, 0, tiled=True)]
    pallas_call x4, Pallas kernels: 19.5 us -> 22.4 us  [partial_call(): pl.pallas_call(lambda *refs: partial_kernel(sides, len(feeds), *refs), gr...]
    all_to_all x2, starting transfers between devices: 6.66 us -> 8.45 us  [body(): everyone = lambda v: lax.all_to_all(v, ('dp', 'mp'), 0, 0, tiled=True)]
    ppermute x34, starting transfers between devices: 34 us -> 35.8 us  [send(): return lax.ppermute(value, ('dp', 'mp'), pairs)]
    add x0 -> x1, other arithmetic: none -> 1.72 us  [body(): total = sum((v.astype(f32) for v in shares[0] + backs))]
    unnamed x26 -> x30, local copies, waits for them, and re-layouts: 6.34 us -> 6.27 us
  transfers between devices with their start and end apart: 36 -> 36, of which waited for: 13 -> 14; matrix products, arithmetic and copies ran while one was open for 1% -> 3% of each run, Pallas kernels for 25% -> 31%
where the time goes in v10:
time: 157 us; the launch traced here: 154 us
  Pallas kernels  49.4 us (31%)
  waiting for transfers between devices  47.5 us (30%)
  starting transfers between devices  44.2 us (28%)
  local copies, waits for them, and re-layouts  7.79 us (5%)
  other arithmetic  4.57 us (3%)
    ppermute x34, starting transfers between devices, send(): return lax.ppermute(value, ('dp', 'mp'), pairs)  35.8 us
    ppermute x34, waiting for transfers between devices, send(): return lax.ppermute(value, ('dp', 'mp'), pairs)  30.7 us
    pallas_call x4, Pallas kernels, partial_call(): pl.pallas_call(lambda *refs: partial_kernel(sides, len(feeds), *refs), gr...  22.4 us
    all_to_all x2, waiting for transfers between devices, body(): everyone = lambda v: lax.all_to_all(v, ('dp', 'mp'), 0, 0, tiled=True)  16.7 us
    pallas_call x4, Pallas kernels, down_call(): pl.pallas_call(lambda *refs: down_kernel(sides, *refs), grid=(experts,),...  13.8 us
    all_to_all x2, starting transfers between devices, body(): everyone = lambda v: lax.all_to_all(v, ('dp', 'mp'), 0, 0, tiled=True)  8.45 us
    unnamed x30, local copies, waits for them, and re-layouts  6.27 us
    pallas_call x4, Pallas kernels, act_call(): pl.pallas_call(lambda *refs: act_kernel(base, *refs), in_specs=[SMEM] + [...  4.94 us
  transfers between devices with their start and end apart: 36, of which 14 were waited for; matrix products, arithmetic and copies ran while one was open for 3% of the time, Pallas kernels for 31%

profile of v10, /device:TPU:4, one launch (start us, length us, event | category | flops | bytes accessed | tf_op | source)
XLA Modules:
  0.0 154.5 jit_solution(3455952334544221695)
XLA Ops:
  0.6 1.3 broadcast_in_dim.4.gain
  1.9 1.9 %prep.1 = (bf16[304,256]{1,0:T(8,128)(2,1)}, f32[4,288]{1,0:T(4,128)}) custom-call(s32[1,4]{1,0:T(1,128)} %tallies.1, f32[288,256]{1,0:T(8,128)} %bitcast.19, f32[1,288]{1,0:T(1,128)} %broadcast_in_dim.4.gain, s32[2,256]{1,0:T(2,128)} %bitcast.23), custom_call_target="tpu_custom_call" | custom-call | flops 88473 | bytes 132710 | tf_op jit(solution)/shard_map/prep/pallas_call | solution.py:75
  3.8 1.5 collective-permute-start
  5.3 3.0 %collective-permute-start.1 = (bf16[304,256]{1,0:T(8,128)(2,1)}, bf16[304,256]{1,0:T(8,128)(2,1)S(1)}, u32[]{:S(2)}, u32[]{:S(2)}) collective-permute-start(bf16[304,256]{1,0:T(8,128)(2,1)} %get-tuple-element.39), channel_id=1, source_target_pairs={{0,7},{1,6},{2,15},{3,14},{4,23},{5,22},{6,31},{7,30},{8,1},{9,0},... | collective-permute-start | bytes 466952 | tf_op jit(solution)/shard_map/ppermute | solution.py:433
  9.6 2.6 %collective-permute-done.refs_0_ = bf16[304,256]{1,0:T(8,128)(2,1)S(1)} collective-permute-done((bf16[304,256]{1,0:T(8,128)(2,1)}, bf16[304,256]{1,0:T(8,128)(2,1)S(1)}, u32[]{:S(2)}, u32[]{:S(2)}) %collective-permute-start) | collective-permute-done | bytes 155680 | tf_op jit(solution)/shard_map/ppermute | solution.py:433
  12.3 4.3 %collective-permute-done.1.refs_1_ = bf16[304,256]{1,0:T(8,128)(2,1)S(1)} collective-permute-done((bf16[304,256]{1,0:T(8,128)(2,1)}, bf16[304,256]{1,0:T(8,128)(2,1)S(1)}, u32[]{:S(2)}, u32[]{:S(2)}) %collective-permute-start.1) | collective-permute-done | bytes 155680 | tf_op jit(solution)/shard_map/ppermute | solution.py:433
  16.6 5.9 %collective-permute-start.2 = (bf16[608,256]{1,0:T(8,128)(2,1)S(1)}, bf16[608,256]{1,0:T(8,128)(2,1)S(1)}, u32[]{:S(2)}, u32[]{:S(2)}) collective-permute-start(bf16[608,256]{1,0:T(8,128)(2,1)S(1)} %join.1.refs_1_), channel_id=1, source_target_pairs={{0,6},{1,7},{2,0},{3,1},{4,2},{5,3},{6,4},{7,5},{8,14},{9,15},{10,... | collective-permute-start | bytes 933896 | tf_op jit(solution)/shard_map/ppermute | solution.py:433
  22.5 7.9 %gate_up_partial.4 = (f32[256,1536]{1,0:T(8,128)}, bf16[256,1536]{1,0:T(8,128)(2,1)}, bf16[256,128]{1,0:T(8,128)(2,1)}) custom-call(s32[3]{0:T(128)} %pad_add_fusion.1.refs_0_, bf16[608,256]{1,0:T(8,128)(2,1)} %copy-done.3, bf16[128,576]{1,0:T(8,128)(2,1)} %pad_add_fusion.refs_2_, bf16[4,576,720]{2,1,0:T(8,128)(2,1)} %refs_3_.7, bf16[4,576,720]{2,1,0:T(8,128)(2,1)} %refs_4_.7), custom_call_target="tpu_custom_call" | custom-call | flops 6794772480 | bytes 35979264 | tf_op jit(solution)/shard_map/gate_up_partial/pallas_call | solution.py:190
  30.4 0.9 collective-permute-start.3
  31.3 1.4 copy-done.2
  32.7 2.0 %copy-done.7 = bf16[4,576,720]{2,1,0:T(8,128)(2,1)S(1)} copy-done((bf16[4,576,720]{2,1,0:T(8,128)(2,1)S(1)}, bf16[4,576,720]{2,1,0:T(8,128)(2,1)}, u32[]{:S(2)}) %copy-start.7) | copy-done | bytes 3317784
  34.7 2.0 %copy-done.9 = bf16[4,576,720]{2,1,0:T(8,128)(2,1)S(1)} copy-done((bf16[4,576,720]{2,1,0:T(8,128)(2,1)S(1)}, bf16[4,576,720]{2,1,0:T(8,128)(2,1)}, u32[]{:S(2)}) %copy-start.9) | copy-done | bytes 3317784
  36.7 4.8 %gate_up_partial.5 = (f32[256,1536]{1,0:T(8,128)S(1)}, bf16[256,1536]{1,0:T(8,128)(2,1)S(1)}, bf16[256,128]{1,0:T(8,128)(2,1)S(1)}) custom-call(s32[3]{0:T(128)S(1)} %copy-done.6, bf16[608,256]{1,0:T(8,128)(2,1)S(1)} %collective-permute-done.2.refs_1_, bf16[128,576]{1,0:T(8,128)(2,1)S(1)} %copy-done.4, bf16[4,576,720]{2,1,0:T(8,128)(2,1)S(1)} %copy-done.7, ...), custom_call_target="tpu_custom_call" | custom-call | flops 6794772480 | bytes 35979264 | tf_op jit(solution)/shard_map/gate_up_partial/pallas_call | solution.py:190
  43.6 4.8 %gate_up_partial.6 = (f32[256,1536]{1,0:T(8,128)S(1)}, bf16[256,1536]{1,0:T(8,128)(2,1)S(1)}, bf16[256,128]{1,0:T(8,128)(2,1)S(1)}) custom-call(s32[3]{0:T(128)S(1)} %copy-done.6, bf16[608,256]{1,0:T(8,128)(2,1)S(1)} %collective-permute-done.3.refs_1_, bf16[128,576]{1,0:T(8,128)(2,1)S(1)} %copy-done.4, bf16[4,576,720]{2,1,0:T(8,128)(2,1)S(1)} %copy-done.8, ...), custom_call_target="tpu_custom_call" | custom-call | flops 6794772480 | bytes 35979264 | tf_op jit(solution)/shard_map/gate_up_partial/pallas_call | solution.py:190
  49.6 1.3 collective-permute-start.13
  50.9 3.8 %collective-permute-done.6.refs_2_ = bf16[128,1536]{1,0:T(8,128)(2,1)S(1)} collective-permute-done((bf16[128,1536]{1,0:T(8,128)(2,1)S(1)}, bf16[128,1536]{1,0:T(8,128)(2,1)S(1)}, u32[]{:S(2)}, u32[]{:S(2)}) %collective-permute-start.6) | collective-permute-done | bytes 393248 | tf_op jit(solution)/shard_map/ppermute | solution.py:433
  54.7 1.2 act.4.refs_5_.refs_1_
  56.0 1.9 %collective-permute-done.5.refs_1_ = bf16[608,256]{1,0:T(8,128)(2,1)S(1)} collective-permute-done((bf16[608,256]{1,0:T(8,128)(2,1)S(1)}, bf16[608,256]{1,0:T(8,128)(2,1)S(1)}, u32[]{:S(2)}, u32[]{:S(2)}) %collective-permute-start.5) | collective-permute-done | bytes 311328 | tf_op jit(solution)/shard_map/ppermute | solution.py:433
  57.9 4.8 %gate_up_partial.7 = (f32[256,1536]{1,0:T(8,128)S(1)}, bf16[256,1536]{1,0:T(8,128)(2,1)S(1)}, bf16[256,128]{1,0:T(8,128)(2,1)S(1)}) custom-call(s32[3]{0:T(128)S(1)} %copy-done.6, bf16[608,256]{1,0:T(8,128)(2,1)S(1)} %collective-permute-done.5.refs_1_, bf16[128,576]{1,0:T(8,128)(2,1)S(1)} %copy-done.4, bf16[4,576,720]{2,1,0:T(8,128)(2,1)S(1)} %copy-done.8, ...), custom_call_target="tpu_custom_call" | custom-call | flops 6794772480 | bytes 35979264 | tf_op jit(solution)/shard_map/gate_up_partial/pallas_call | solution.py:190
  64.3 2.5 %collective-permute-done.9.refs_2_ = bf16[128,768]{1,0:T(8,128)(2,1)S(1)} collective-permute-done((bf16[128,768]{1,0:T(8,128)(2,1)S(1)}, bf16[128,768]{1,0:T(8,128)(2,1)S(1)}, u32[]{:S(2)}, u32[]{:S(2)}) %collective-permute-start.9) | collective-permute-done | bytes 196640 | tf_op jit(solution)/shard_map/ppermute | solution.py:433
  67.0 1.2 act.5.refs_7_.refs_1_
  68.3 1.8 %collective-permute-start.15 = (bf16[128,768]{1,0:T(8,128)(2,1)S(1)}, bf16[128,768]{1,0:T(8,128)(2,1)S(1)}, u32[]{:S(2)}, u32[]{:S(2)}) collective-permute-start(bf16[128,768]{1,0:T(8,128)(2,1)S(1)} %act.5.refs_7_.refs_1_), channel_id=1, source_target_pairs={{0,16},{1,17},{2,18},{3,19},{4,20},{5,21},{6,22},{7,23},{8,24},{9,... | collective-permute-start | bytes 589832 | tf_op jit(solution)/shard_map/ppermute | solution.py:433
  70.1 3.5 %down.4 = (bf16[288,256]{1,0:T(8,128)(2,1)S(1)}, bf16[288,256]{1,0:T(8,128)(2,1)S(1)}) custom-call(s32[3]{0:T(128)S(1)} %copy-done.6, bf16[128,768]{1,0:T(8,128)(2,1)S(1)} %act.4.refs_5_.refs_1_, bf16[128,768]{1,0:T(8,128)(2,1)S(1)} %collective-permute-done.9.refs_2_, bf16[128,768]{1,0:T(8,128)(2,1)S(1)} %collective-permute-done.11.refs_3_, ...), custom_call_target="tpu_custom_call" | custom-call | flops 3397386240 | bytes 14450688 | tf_op jit(solution)/shard_map/down/pallas_call | solution.py:306
  75.1 3.6 %collective-permute-done.18.refs_2_ = bf16[128,1536]{1,0:T(8,128)(2,1)S(1)} collective-permute-done((bf16[128,1536]{1,0:T(8,128)(2,1)S(1)}, bf16[128,1536]{1,0:T(8,128)(2,1)S(1)}, u32[]{:S(2)}, u32[]{:S(2)}) %collective-permute-start.18) | collective-permute-done | bytes 393248 | tf_op jit(solution)/shard_map/ppermute | solution.py:433
  78.7 1.2 act.6.refs_7_.refs_1_
  80.3 1.7 %collective-permute-start.14 = (bf16[128,1536]{1,0:T(8,128)(2,1)S(1)}, bf16[128,1536]{1,0:T(8,128)(2,1)S(1)}, u32[]{:S(2)}, u32[]{:S(2)}) collective-permute-start(bf16[128,1536]{1,0:T(8,128)(2,1)S(1)} %get-tuple-element.60), channel_id=1, source_target_pairs={{0,16},{1,17},{2,18},{3,19},{4,20},{5,21},{6,22},{7,23},{8,24},{9,... | collective-permute-start | bytes 1179656 | tf_op jit(solution)/shard_map/ppermute | solution.py:433
  82.0 0.9 collective-permute-done.15.refs_2_
  82.9 1.4 collective-permute-start.27
  84.3 3.5 %collective-permute-done.22.refs_2_ = bf16[128,768]{1,0:T(8,128)(2,1)S(1)} collective-permute-done((bf16[128,768]{1,0:T(8,128)(2,1)S(1)}, bf16[128,768]{1,0:T(8,128)(2,1)S(1)}, u32[]{:S(2)}, u32[]{:S(2)}) %collective-permute-start.22) | collective-permute-done | bytes 196640 | tf_op jit(solution)/shard_map/ppermute | solution.py:433
  88.3 3.5 %down.5 = (bf16[288,256]{1,0:T(8,128)(2,1)S(1)}, bf16[288,256]{1,0:T(8,128)(2,1)S(1)}) custom-call(s32[3]{0:T(128)S(1)} %copy-done.6, bf16[128,768]{1,0:T(8,128)(2,1)S(1)} %act.5.refs_7_.refs_1_, bf16[128,768]{1,0:T(8,128)(2,1)S(1)} %collective-permute-done.15.refs_2_, bf16[128,768]{1,0:T(8,128)(2,1)S(1)} %collective-permute-done.16.refs_3_, ...), custom_call_target="tpu_custom_call" | custom-call | flops 3397386240 | bytes 14450688 | tf_op jit(solution)/shard_map/down/pallas_call | solution.py:306
  92.4 2.7 %collective-permute-done.14.refs_2_ = bf16[128,1536]{1,0:T(8,128)(2,1)S(1)} collective-permute-done((bf16[128,1536]{1,0:T(8,128)(2,1)S(1)}, bf16[128,1536]{1,0:T(8,128)(2,1)S(1)}, u32[]{:S(2)}, u32[]{:S(2)}) %collective-permute-start.14) | collective-permute-done | bytes 393248 | tf_op jit(solution)/shard_map/ppermute | solution.py:433
  95.1 1.2 act.7.refs_7_.refs_1_
  96.7 3.5 %down.6 = (bf16[288,256]{1,0:T(8,128)(2,1)S(1)}, bf16[288,256]{1,0:T(8,128)(2,1)S(1)}) custom-call(s32[3]{0:T(128)S(1)} %copy-done.6, bf16[128,768]{1,0:T(8,128)(2,1)S(1)} %act.6.refs_7_.refs_1_, bf16[128,768]{1,0:T(8,128)(2,1)S(1)} %collective-permute-done.22.refs_2_, bf16[128,768]{1,0:T(8,128)(2,1)S(1)} %collective-permute-done.23.refs_3_, ...), custom_call_target="tpu_custom_call" | custom-call | flops 3397386240 | bytes 14450688 | tf_op jit(solution)/shard_map/down/pallas_call | solution.py:306
  100.9 2.0 %collective-permute-start.29 = (bf16[288,256]{1,0:T(8,128)(2,1)S(1)}, bf16[288,256]{1,0:T(8,128)(2,1)S(1)}, u32[]{:S(2)}, u32[]{:S(2)}) collective-permute-start(bf16[288,256]{1,0:T(8,128)(2,1)S(1)} %add_convert_fusion.1), channel_id=1, source_target_pairs={{0,4},{1,5},{2,6},{3,7},{4,0},{5,1},{6,2},{7,3},{8,12},{9,13},{10,... | collective-permute-start | bytes 442376 | tf_op jit(solution)/shard_map/ppermute | solution.py:433
  103.4 2.0 %collective-permute-done.30 = bf16[288,256]{1,0:T(8,128)(2,1)S(1)} collective-permute-done((bf16[288,256]{1,0:T(8,128)(2,1)S(1)}, bf16[288,256]{1,0:T(8,128)(2,1)S(1)}, u32[]{:S(2)}, u32[]{:S(2)}) %collective-permute-start.30) | collective-permute-done | bytes 147488 | tf_op jit(solution)/shard_map/ppermute | solution.py:433
  105.9 3.5 %down.7 = (bf16[288,256]{1,0:T(8,128)(2,1)S(1)}, bf16[288,256]{1,0:T(8,128)(2,1)S(1)}) custom-call(s32[3]{0:T(128)S(1)} %copy-done.6, bf16[128,768]{1,0:T(8,128)(2,1)S(1)} %act.7.refs_7_.refs_1_, bf16[128,768]{1,0:T(8,128)(2,1)S(1)} %collective-permute-done.19.refs_2_, bf16[128,768]{1,0:T(8,128)(2,1)S(1)} %collective-permute-done.20.refs_3_, ...), custom_call_target="tpu_custom_call" | custom-call | flops 3397386240 | bytes 14450688 | tf_op jit(solution)/shard_map/down/pallas_call | solution.py:306
  109.4 0.9 collective-permute-start.25
  110.3 5.2 %collective-permute-start.33 = (f32[4,288]{1,0:T(4,128)S(1)}, f32[4,288]{1,0:T(4,128)S(1)}, u32[]{:S(2)}, u32[]{:S(2)}) collective-permute-start(f32[4,288]{1,0:T(4,128)S(1)} %copy-done.14), channel_id=1, source_target_pairs={{0,0},{1,1},{2,8},{3,9},{4,16},{5,17},{6,24},{7,25},{8,2},{9,3},{1... | collective-permute-start | bytes 13832 | tf_op jit(solution)/shard_map/ppermute | solution.py:433
  115.5 2.1 %collective-permute-done.33.refs_1_ = f32[4,288]{1,0:T(4,128)S(1)} collective-permute-done((f32[4,288]{1,0:T(4,128)S(1)}, f32[4,288]{1,0:T(4,128)S(1)}, u32[]{:S(2)}, u32[]{:S(2)}) %collective-permute-start.33) | collective-permute-done | bytes 4640 | tf_op jit(solution)/shard_map/ppermute | solution.py:433
  117.7 1.4 end_rows.1
  119.1 4.9 %all-to-all-start = ((f32[32,8,288]{2,1,0:T(8,128)}), f32[32,8,288]{2,1,0:T(8,128)S(1)}, u32[]{:S(2)}, u32[]{:S(2)}) async-start(f32[32,8,288]{2,1,0:T(8,128)} %end_rows.1), calls=%async_computation | async-start | bytes 786432 | tf_op jit(solution)/shard_map/all_to_all | solution.py:526
  124.0 1.7 %convert_add_fusion = f32[288,256]{1,0:T(8,128)} fusion(bf16[288,256]{1,0:T(8,128)(2,1)S(1)} %collective-permute-done.31.refs_6_, bf16[288,256]{1,0:T(8,128)(2,1)S(1)} %collective-permute-done.29.refs_5_, bf16[288,256]{1,0:T(8,128)(2,1)S(1)} %collective-permute-done.27.refs_4_, bf16[288,256]{1,0:T(8,128)(2,1)} %collective-permute-done.25, ...), kind=kLoop, calls=%fused_computation.1 | loop fusion | flops 663552 | bytes 1032192 | tf_op jit(solution)/shard_map/add | solution.py:524
  125.7 4.4 %collective-permute-start.32 = (f32[288,256]{1,0:T(8,128)}, f32[288,256]{1,0:T(8,128)S(1)}, u32[]{:S(2)}, u32[]{:S(2)}) collective-permute-start(f32[288,256]{1,0:T(8,128)} %convert_add_fusion), channel_id=1, source_target_pairs={{0,0},{1,1},{2,8},{3,9},{4,16},{5,17},{6,24},{7,25},{8,2},{9,3},{1... | collective-permute-start | bytes 884744 | tf_op jit(solution)/shard_map/ppermute | solution.py:433
  130.3 12.3 %all-to-all-done.refs_0_ = f32[32,8,288]{2,1,0:T(8,128)S(1)} async-done(((f32[32,8,288]{2,1,0:T(8,128)}), f32[32,8,288]{2,1,0:T(8,128)S(1)}, u32[]{:S(2)}, u32[]{:S(2)}) %all-to-all-start) | async-done | bytes 294944 | tf_op jit(solution)/shard_map/all_to_all | solution.py:526
  142.6 1.5 head.1
  144.1 3.5 %all-to-all-start.1 = ((f32[32,2,16]{2,1,0:T(2,128)}), f32[32,2,16]{2,1,0:T(2,128)S(1)}, u32[]{:S(2)}, u32[]{:S(2)}) async-start(f32[32,2,16]{2,1,0:T(2,128)} %get-tuple-element.75), calls=%async_computation.1 | async-start | bytes 65536 | tf_op jit(solution)/shard_map/all_to_all | solution.py:526
  147.6 0.9 collective-permute-done.32
  149.3 4.4 %all-to-all-done.1 = f32[32,2,16]{2,1,0:T(2,128)S(1)} async-done(((f32[32,2,16]{2,1,0:T(2,128)}), f32[32,2,16]{2,1,0:T(2,128)S(1)}, u32[]{:S(2)}, u32[]{:S(2)}) %all-to-all-start.1) | async-done | bytes 4128 | tf_op jit(solution)/shard_map/all_to_all | solution.py:526
  (90 shorter events, 13.2 us)
Async XLA Ops:
  0.6 7.7 %copy-start = (bf16[2304,4]{0,1:T(4,128)(2,1)S(1)}, bf16[2304,4]{0,1:T(4,128)(2,1)}, u32[]{:S(2)}) copy-start(bf16[2304,4]{0,1:T(4,128)(2,1)} %param.15) | copy-start | bytes 55300
  3.8 8.4 %collective-permute-start = (bf16[304,256]{1,0:T(8,128)(2,1)}, bf16[304,256]{1,0:T(8,128)(2,1)S(1)}, u32[]{:S(2)}, u32[]{:S(2)}) collective-permute-start(bf16[304,256]{1,0:T(8,128)(2,1)} %get-tuple-element.39), channel_id=1, source_target_pairs={{0,6},{1,7},{2,14},{3,15},{4,22},{5,23},{6,30},{7,31},{8,0},{9,1},... | collective-permute-start | bytes 466952 | tf_op jit(solution)/shard_map/ppermute | solution.py:433
  5.3 11.2 %collective-permute-start.1 = (bf16[304,256]{1,0:T(8,128)(2,1)}, bf16[304,256]{1,0:T(8,128)(2,1)S(1)}, u32[]{:S(2)}, u32[]{:S(2)}) collective-permute-start(bf16[304,256]{1,0:T(8,128)(2,1)} %get-tuple-element.39), channel_id=1, source_target_pairs={{0,7},{1,6},{2,15},{3,14},{4,23},{5,22},{6,31},{7,30},{8,1},{9,0},... | collective-permute-start | bytes 466952 | tf_op jit(solution)/shard_map/ppermute | solution.py:433
  16.5 6.0 %copy-start.3 = (bf16[608,256]{1,0:T(8,128)(2,1)}, bf16[608,256]{1,0:T(8,128)(2,1)S(1)}, u32[]{:S(2)}) copy-start(bf16[608,256]{1,0:T(8,128)(2,1)S(1)} %join.1.refs_1_) | copy-start | bytes 933892
  16.6 14.8 %copy-start.4 = (bf16[128,576]{1,0:T(8,128)(2,1)S(1)}, bf16[128,576]{1,0:T(8,128)(2,1)}, u32[]{:S(2)}) copy-start(bf16[128,576]{1,0:T(8,128)(2,1)} %pad_add_fusion.refs_2_) | copy-start | bytes 442372
  16.6 14.7 %copy-start.6 = (s32[3]{0:T(128)S(1)}, s32[3]{0:T(128)}, u32[]{:S(2)}) copy-start(s32[3]{0:T(128)} %pad_add_fusion.1.refs_0_) | copy-start | bytes 40
  16.6 13.8 %collective-permute-start.2 = (bf16[608,256]{1,0:T(8,128)(2,1)S(1)}, bf16[608,256]{1,0:T(8,128)(2,1)S(1)}, u32[]{:S(2)}, u32[]{:S(2)}) collective-permute-start(bf16[608,256]{1,0:T(8,128)(2,1)S(1)} %join.1.refs_1_), channel_id=1, source_target_pairs={{0,6},{1,7},{2,0},{3,1},{4,2},{5,3},{6,4},{7,5},{8,14},{9,15},{10,... | collective-permute-start | bytes 933896 | tf_op jit(solution)/shard_map/ppermute | solution.py:433
  30.4 11.4 %collective-permute-start.4 = (bf16[256,1536]{1,0:T(8,128)(2,1)}, bf16[256,1536]{1,0:T(8,128)(2,1)S(1)}, u32[]{:S(2)}, u32[]{:S(2)}) collective-permute-start(bf16[256,1536]{1,0:T(8,128)(2,1)} %get-tuple-element.41), channel_id=1, source_target_pairs={{0,8},{1,9},{2,10},{3,11},{4,12},{5,13},{6,14},{7,15},{8,0},{9,1},... | collective-permute-start | bytes 2359304 | tf_op jit(solution)/shard_map/ppermute | solution.py:433
  30.4 12.4 %collective-permute-start.3 = (bf16[608,256]{1,0:T(8,128)(2,1)S(1)}, bf16[608,256]{1,0:T(8,128)(2,1)S(1)}, u32[]{:S(2)}, u32[]{:S(2)}) collective-permute-start(bf16[608,256]{1,0:T(8,128)(2,1)S(1)} %collective-permute-done.2.refs_1_), channel_id=1, source_target_pairs={{0,6},{1,7},{2,0},{3,1},{4,2},{5,3},{6,4},{7,5},{8,14},{9,15},{10,... | collective-permute-start | bytes 933896 | tf_op jit(solution)/shard_map/ppermute | solution.py:433
  41.6 2.0 %copy-start.8 = (bf16[4,576,720]{2,1,0:T(8,128)(2,1)S(1)}, bf16[4,576,720]{2,1,0:T(8,128)(2,1)}, u32[]{:S(2)}) copy-start(bf16[4,576,720]{2,1,0:T(8,128)(2,1)} %refs_3_.7) | copy-start | bytes 9953284
  41.6 7.2 %collective-permute-start.7 = (bf16[256,1536]{1,0:T(8,128)(2,1)S(1)}, bf16[256,1536]{1,0:T(8,128)(2,1)S(1)}, u32[]{:S(2)}, u32[]{:S(2)}) collective-permute-start(bf16[256,1536]{1,0:T(8,128)(2,1)S(1)} %get-tuple-element.48), channel_id=1, source_target_pairs={{0,8},{1,9},{2,10},{3,11},{4,12},{5,13},{6,14},{7,15},{8,0},{9,1},... | collective-permute-start | bytes 2359304 | tf_op jit(solution)/shard_map/ppermute | solution.py:433
  42.7 12.0 %collective-permute-start.6 = (bf16[128,1536]{1,0:T(8,128)(2,1)S(1)}, bf16[128,1536]{1,0:T(8,128)(2,1)S(1)}, u32[]{:S(2)}, u32[]{:S(2)}) collective-permute-start(bf16[128,1536]{1,0:T(8,128)(2,1)S(1)} %get-tuple-element.46), channel_id=1, source_target_pairs={{0,16},{1,17},{2,18},{3,19},{4,20},{5,21},{6,22},{7,23},{8,24},{9,... | collective-permute-start | bytes 1179656 | tf_op jit(solution)/shard_map/ppermute | solution.py:433
  48.4 6.3 %copy-start.5 = (bf16[256,128]{1,0:T(8,128)(2,1)S(1)}, bf16[256,128]{1,0:T(8,128)(2,1)}, u32[]{:S(2)}) copy-start(bf16[256,128]{1,0:T(8,128)(2,1)} %get-tuple-element.47.refs_3_.refs_5_) | copy-start | bytes 196612
  48.4 9.5 %collective-permute-start.5 = (bf16[608,256]{1,0:T(8,128)(2,1)S(1)}, bf16[608,256]{1,0:T(8,128)(2,1)S(1)}, u32[]{:S(2)}, u32[]{:S(2)}) collective-permute-start(bf16[608,256]{1,0:T(8,128)(2,1)S(1)} %collective-permute-done.3.refs_1_), channel_id=1, source_target_pairs={{0,6},{1,7},{2,0},{3,1},{4,2},{5,3},{6,4},{7,5},{8,14},{9,15},{10,... | collective-permute-start | bytes 933896 | tf_op jit(solution)/shard_map/ppermute | solution.py:433
  48.5 14.3 %collective-permute-start.10 = (bf16[256,1536]{1,0:T(8,128)(2,1)S(1)}, bf16[256,1536]{1,0:T(8,128)(2,1)S(1)}, u32[]{:S(2)}, u32[]{:S(2)}) collective-permute-start(bf16[256,1536]{1,0:T(8,128)(2,1)S(1)} %get-tuple-element.52), channel_id=1, source_target_pairs={{0,8},{1,9},{2,10},{3,11},{4,12},{5,13},{6,14},{7,15},{8,0},{9,1},... | collective-permute-start | bytes 2359304 | tf_op jit(solution)/shard_map/ppermute | solution.py:433
  49.6 17.4 %collective-permute-start.13 = (bf16[128,1536]{1,0:T(8,128)(2,1)S(1)}, bf16[128,1536]{1,0:T(8,128)(2,1)S(1)}, u32[]{:S(2)}, u32[]{:S(2)}) collective-permute-start(bf16[128,1536]{1,0:T(8,128)(2,1)S(1)} %get-tuple-element.56), channel_id=1, source_target_pairs={{0,16},{1,17},{2,18},{3,19},{4,20},{5,21},{6,22},{7,23},{8,24},{9,... | collective-permute-start | bytes 1179656 | tf_op jit(solution)/shard_map/ppermute | solution.py:433
  55.9 10.8 %collective-permute-start.9 = (bf16[128,768]{1,0:T(8,128)(2,1)S(1)}, bf16[128,768]{1,0:T(8,128)(2,1)S(1)}, u32[]{:S(2)}, u32[]{:S(2)}) collective-permute-start(bf16[128,768]{1,0:T(8,128)(2,1)S(1)} %act.4.refs_5_.refs_1_), channel_id=1, source_target_pairs={{0,16},{1,17},{2,18},{3,19},{4,20},{5,21},{6,22},{7,23},{8,24},{9,... | collective-permute-start | bytes 589832 | tf_op jit(solution)/shard_map/ppermute | solution.py:433
  62.8 11.5 %collective-permute-start.8 = (bf16[256,1536]{1,0:T(8,128)(2,1)S(1)}, bf16[256,1536]{1,0:T(8,128)(2,1)S(1)}, u32[]{:S(2)}, u32[]{:S(2)}) collective-permute-start(bf16[256,1536]{1,0:T(8,128)(2,1)S(1)} %get-tuple-element.51), channel_id=1, source_target_pairs={{0,8},{1,9},{2,10},{3,11},{4,12},{5,13},{6,14},{7,15},{8,0},{9,1},... | collective-permute-start | bytes 2359304 | tf_op jit(solution)/shard_map/ppermute | solution.py:433
  62.8 7.3 %copy-start.10 = (bf16[4,720,576]{1,2,0:T(8,128)(2,1)S(1)}, bf16[4,720,576]{1,2,0:T(8,128)(2,1)}, u32[]{:S(2)}) copy-start(bf16[4,720,576]{1,2,0:T(8,128)(2,1)} %param.18) | copy-start | bytes 9953284
  63.7 6.4 %collective-permute-start.11 = (bf16[128,768]{1,0:T(8,128)(2,1)S(1)}, bf16[128,768]{1,0:T(8,128)(2,1)S(1)}, u32[]{:S(2)}, u32[]{:S(2)}) collective-permute-start(bf16[128,768]{1,0:T(8,128)(2,1)S(1)} %act.4.refs_5_.refs_1_), channel_id=1, source_target_pairs={{0,8},{1,9},{2,10},{3,11},{4,12},{5,13},{6,14},{7,15},{8,0},{9,1},... | collective-permute-start | bytes 589832 | tf_op jit(solution)/shard_map/ppermute | solution.py:433
  66.7 3.3 %collective-permute-start.12 = (bf16[128,768]{1,0:T(8,128)(2,1)S(1)}, bf16[128,768]{1,0:T(8,128)(2,1)S(1)}, u32[]{:S(2)}, u32[]{:S(2)}) collective-permute-start(bf16[128,768]{1,0:T(8,128)(2,1)S(1)} %collective-permute-done.9.refs_2_), channel_id=1, source_target_pairs={{0,8},{1,9},{2,10},{3,11},{4,12},{5,13},{6,14},{7,15},{8,0},{9,1},... | collective-permute-start | bytes 589832 | tf_op jit(solution)/shard_map/ppermute | solution.py:433
  66.7 11.9 %collective-permute-start.18 = (bf16[128,1536]{1,0:T(8,128)(2,1)S(1)}, bf16[128,1536]{1,0:T(8,128)(2,1)S(1)}, u32[]{:S(2)}, u32[]{:S(2)}) collective-permute-start(bf16[128,1536]{1,0:T(8,128)(2,1)S(1)} %get-tuple-element.64), channel_id=1, source_target_pairs={{0,16},{1,17},{2,18},{3,19},{4,20},{5,21},{6,22},{7,23},{8,24},{9,... | collective-permute-start | bytes 1179656 | tf_op jit(solution)/shard_map/ppermute | solution.py:433
  68.3 14.6 %collective-permute-start.15 = (bf16[128,768]{1,0:T(8,128)(2,1)S(1)}, bf16[128,768]{1,0:T(8,128)(2,1)S(1)}, u32[]{:S(2)}, u32[]{:S(2)}) collective-permute-start(bf16[128,768]{1,0:T(8,128)(2,1)S(1)} %act.5.refs_7_.refs_1_), channel_id=1, source_target_pairs={{0,16},{1,17},{2,18},{3,19},{4,20},{5,21},{6,22},{7,23},{8,24},{9,... | collective-permute-start | bytes 589832 | tf_op jit(solution)/shard_map/ppermute | solution.py:433
  73.6 9.3 %collective-permute-start.26 = (bf16[288,256]{1,0:T(8,128)(2,1)S(1)}, bf16[288,256]{1,0:T(8,128)(2,1)S(1)}, u32[]{:S(2)}, u32[]{:S(2)}) collective-permute-start(bf16[288,256]{1,0:T(8,128)(2,1)S(1)} %get-tuple-element.70), channel_id=1, source_target_pairs={{0,1},{1,0},{2,3},{3,2},{4,5},{5,4},{6,7},{7,6},{8,9},{9,8},{10,11... | collective-permute-start | bytes 442376 | tf_op jit(solution)/shard_map/ppermute | solution.py:433
  79.9 7.9 %collective-permute-start.22 = (bf16[128,768]{1,0:T(8,128)(2,1)S(1)}, bf16[128,768]{1,0:T(8,128)(2,1)S(1)}, u32[]{:S(2)}, u32[]{:S(2)}) collective-permute-start(bf16[128,768]{1,0:T(8,128)(2,1)S(1)} %act.6.refs_7_.refs_1_), channel_id=1, source_target_pairs={{0,16},{1,17},{2,18},{3,19},{4,20},{5,21},{6,22},{7,23},{8,24},{9,... | collective-permute-start | bytes 589832 | tf_op jit(solution)/shard_map/ppermute | solution.py:433
  80.3 14.9 %collective-permute-start.14 = (bf16[128,1536]{1,0:T(8,128)(2,1)S(1)}, bf16[128,1536]{1,0:T(8,128)(2,1)S(1)}, u32[]{:S(2)}, u32[]{:S(2)}) collective-permute-start(bf16[128,1536]{1,0:T(8,128)(2,1)S(1)} %get-tuple-element.60), channel_id=1, source_target_pairs={{0,16},{1,17},{2,18},{3,19},{4,20},{5,21},{6,22},{7,23},{8,24},{9,... | collective-permute-start | bytes 1179656 | tf_op jit(solution)/shard_map/ppermute | solution.py:433
  82.0 5.8 %collective-permute-start.16 = (bf16[128,768]{1,0:T(8,128)(2,1)S(1)}, bf16[128,768]{1,0:T(8,128)(2,1)S(1)}, u32[]{:S(2)}, u32[]{:S(2)}) collective-permute-start(bf16[128,768]{1,0:T(8,128)(2,1)S(1)} %act.5.refs_7_.refs_1_), channel_id=1, source_target_pairs={{0,8},{1,9},{2,10},{3,11},{4,12},{5,13},{6,14},{7,15},{8,0},{9,1},... | collective-permute-start | bytes 589832 | tf_op jit(solution)/shard_map/ppermute | solution.py:433
  82.9 5.5 %collective-permute-start.17 = (bf16[128,768]{1,0:T(8,128)(2,1)S(1)}, bf16[128,768]{1,0:T(8,128)(2,1)S(1)}, u32[]{:S(2)}, u32[]{:S(2)}) collective-permute-start(bf16[128,768]{1,0:T(8,128)(2,1)S(1)} %collective-permute-done.15.refs_2_), channel_id=1, source_target_pairs={{0,8},{1,9},{2,10},{3,11},{4,12},{5,13},{6,14},{7,15},{8,0},{9,1},... | collective-permute-start | bytes 589832 | tf_op jit(solution)/shard_map/ppermute | solution.py:433
  82.9 34.7 %collective-permute-start.27 = (bf16[288,256]{1,0:T(8,128)(2,1)S(1)}, bf16[288,256]{1,0:T(8,128)(2,1)S(1)}, u32[]{:S(2)}, u32[]{:S(2)}) collective-permute-start(bf16[288,256]{1,0:T(8,128)(2,1)S(1)} %add_convert_fusion.2), channel_id=1, source_target_pairs={{0,2},{1,3},{2,4},{3,5},{4,6},{5,7},{6,0},{7,1},{8,10},{9,11},{10,... | collective-permute-start | bytes 442376 | tf_op jit(solution)/shard_map/ppermute | solution.py:433
  87.8 8.9 %collective-permute-start.23 = (bf16[128,768]{1,0:T(8,128)(2,1)S(1)}, bf16[128,768]{1,0:T(8,128)(2,1)S(1)}, u32[]{:S(2)}, u32[]{:S(2)}) collective-permute-start(bf16[128,768]{1,0:T(8,128)(2,1)S(1)} %act.6.refs_7_.refs_1_), channel_id=1, source_target_pairs={{0,8},{1,9},{2,10},{3,11},{4,12},{5,13},{6,14},{7,15},{8,0},{9,1},... | collective-permute-start | bytes 589832 | tf_op jit(solution)/shard_map/ppermute | solution.py:433
  87.8 8.9 %collective-permute-start.24 = (bf16[128,768]{1,0:T(8,128)(2,1)S(1)}, bf16[128,768]{1,0:T(8,128)(2,1)S(1)}, u32[]{:S(2)}, u32[]{:S(2)}) collective-permute-start(bf16[128,768]{1,0:T(8,128)(2,1)S(1)} %collective-permute-done.22.refs_2_), channel_id=1, source_target_pairs={{0,8},{1,9},{2,10},{3,11},{4,12},{5,13},{6,14},{7,15},{8,0},{9,1},... | collective-permute-start | bytes 589832 | tf_op jit(solution)/shard_map/ppermute | solution.py:433
  91.8 9.0 %collective-permute-start.28 = (bf16[288,256]{1,0:T(8,128)(2,1)S(1)}, bf16[288,256]{1,0:T(8,128)(2,1)S(1)}, u32[]{:S(2)}, u32[]{:S(2)}) collective-permute-start(bf16[288,256]{1,0:T(8,128)(2,1)S(1)} %get-tuple-element.71), channel_id=1, source_target_pairs={{0,1},{1,0},{2,3},{3,2},{4,5},{5,4},{6,7},{7,6},{8,9},{9,8},{10,11... | collective-permute-start | bytes 442376 | tf_op jit(solution)/shard_map/ppermute | solution.py:433
  96.4 6.5 %collective-permute-start.19 = (bf16[128,768]{1,0:T(8,128)(2,1)S(1)}, bf16[128,768]{1,0:T(8,128)(2,1)S(1)}, u32[]{:S(2)}, u32[]{:S(2)}) collective-permute-start(bf16[128,768]{1,0:T(8,128)(2,1)S(1)} %act.7.refs_7_.refs_1_), channel_id=1, source_target_pairs={{0,16},{1,17},{2,18},{3,19},{4,20},{5,21},{6,22},{7,23},{8,24},{9,... | collective-permute-start | bytes 589832 | tf_op jit(solution)/shard_map/ppermute | solution.py:433
  100.2 5.2 %collective-permute-start.30 = (bf16[288,256]{1,0:T(8,128)(2,1)S(1)}, bf16[288,256]{1,0:T(8,128)(2,1)S(1)}, u32[]{:S(2)}, u32[]{:S(2)}) collective-permute-start(bf16[288,256]{1,0:T(8,128)(2,1)S(1)} %get-tuple-element.72), channel_id=1, source_target_pairs={{0,1},{1,0},{2,3},{3,2},{4,5},{5,4},{6,7},{7,6},{8,9},{9,8},{10,11... | collective-permute-start | bytes 442376 | tf_op jit(solution)/shard_map/ppermute | solution.py:433
  100.9 16.8 %collective-permute-start.29 = (bf16[288,256]{1,0:T(8,128)(2,1)S(1)}, bf16[288,256]{1,0:T(8,128)(2,1)S(1)}, u32[]{:S(2)}, u32[]{:S(2)}) collective-permute-start(bf16[288,256]{1,0:T(8,128)(2,1)S(1)} %add_convert_fusion.1), channel_id=1, source_target_pairs={{0,4},{1,5},{2,6},{3,7},{4,0},{5,1},{6,2},{7,3},{8,12},{9,13},{10,... | collective-permute-start | bytes 442376 | tf_op jit(solution)/shard_map/ppermute | solution.py:433
  102.9 3.0 %collective-permute-start.20 = (bf16[128,768]{1,0:T(8,128)(2,1)S(1)}, bf16[128,768]{1,0:T(8,128)(2,1)S(1)}, u32[]{:S(2)}, u32[]{:S(2)}) collective-permute-start(bf16[128,768]{1,0:T(8,128)(2,1)S(1)} %act.7.refs_7_.refs_1_), channel_id=1, source_target_pairs={{0,8},{1,9},{2,10},{3,11},{4,12},{5,13},{6,14},{7,15},{8,0},{9,1},... | collective-permute-start | bytes 589832 | tf_op jit(solution)/shard_map/ppermute | solution.py:433
  102.9 3.0 %collective-permute-start.21 = (bf16[128,768]{1,0:T(8,128)(2,1)S(1)}, bf16[128,768]{1,0:T(8,128)(2,1)S(1)}, u32[]{:S(2)}, u32[]{:S(2)}) collective-permute-start(bf16[128,768]{1,0:T(8,128)(2,1)S(1)} %collective-permute-done.19.refs_2_), channel_id=1, source_target_pairs={{0,8},{1,9},{2,10},{3,11},{4,12},{5,13},{6,14},{7,15},{8,0},{9,1},... | collective-permute-start | bytes 589832 | tf_op jit(solution)/shard_map/ppermute | solution.py:433
  105.4 4.9 %copy-start.14 = (f32[4,288]{1,0:T(4,128)S(1)}, f32[4,288]{1,0:T(4,128)}, u32[]{:S(2)}) copy-start(f32[4,288]{1,0:T(4,128)} %get-tuple-element.73) | copy-start | bytes 13828
  105.5 12.2 %collective-permute-start.31 = (bf16[288,256]{1,0:T(8,128)(2,1)S(1)}, bf16[288,256]{1,0:T(8,128)(2,1)S(1)}, u32[]{:S(2)}, u32[]{:S(2)}) collective-permute-start(bf16[288,256]{1,0:T(8,128)(2,1)S(1)} %add_convert_fusion), channel_id=1, source_target_pairs={{0,6},{1,7},{2,0},{3,1},{4,2},{5,3},{6,4},{7,5},{8,14},{9,15},{10,... | collective-permute-start | bytes 442376 | tf_op jit(solution)/shard_map/ppermute | solution.py:433
  109.4 20.7 %copy-start.12 = (f32[2304]{0:T(1024)S(1)}, f32[2304]{0:T(1024)}, u32[]{:S(2)}) copy-start(f32[2304]{0:T(1024)} %param.19) | copy-start | bytes 27652
  109.4 20.8 %copy-start.13 = (f32[16]{0:T(128)S(1)}, f32[16]{0:T(128)}, u32[]{:S(2)}) copy-start(f32[16]{0:T(128)} %param.21) | copy-start | bytes 196
  109.4 33.2 %copy-start.1 = (bf16[2304,512]{1,0:T(8,128)(2,1)S(1)}, bf16[2304,512]{1,0:T(8,128)(2,1)}, u32[]{:S(2)}) copy-start(bf16[2304,512]{1,0:T(8,128)(2,1)} %refs_2_.1) | copy-start | bytes 7077892
  109.4 14.6 %collective-permute-start.25 = (bf16[288,256]{1,0:T(8,128)(2,1)S(1)}, bf16[288,256]{1,0:T(8,128)(2,1)}, u32[]{:S(2)}, u32[]{:S(2)}) collective-permute-start(bf16[288,256]{1,0:T(8,128)(2,1)S(1)} %get-tuple-element.69.refs_3_), channel_id=1, source_target_pairs={{0,1},{1,0},{2,3},{3,2},{4,5},{5,4},{6,7},{7,6},{8,9},{9,8},{10,11... | collective-permute-start | bytes 442376 | tf_op jit(solution)/shard_map/ppermute | solution.py:433
  110.3 7.3 %collective-permute-start.33 = (f32[4,288]{1,0:T(4,128)S(1)}, f32[4,288]{1,0:T(4,128)S(1)}, u32[]{:S(2)}, u32[]{:S(2)}) collective-permute-start(f32[4,288]{1,0:T(4,128)S(1)} %copy-done.14), channel_id=1, source_target_pairs={{0,0},{1,1},{2,8},{3,9},{4,16},{5,17},{6,24},{7,25},{8,2},{9,3},{1... | collective-permute-start | bytes 13832 | tf_op jit(solution)/shard_map/ppermute | solution.py:433
  119.1 23.5 %all-to-all-start = ((f32[32,8,288]{2,1,0:T(8,128)}), f32[32,8,288]{2,1,0:T(8,128)S(1)}, u32[]{:S(2)}, u32[]{:S(2)}) async-start(f32[32,8,288]{2,1,0:T(8,128)} %end_rows.1), calls=%async_computation | async-start | bytes 786432 | tf_op jit(solution)/shard_map/all_to_all | solution.py:526
  125.7 22.8 %copy-start.11 = (f32[256,288]{0,1:T(8,128)S(1)}, f32[256,288]{0,1:T(8,128)}, u32[]{:S(2)}) copy-start(f32[256,288]{0,1:T(8,128)} %param.11) | copy-start | bytes 884740
  125.7 22.8 %collective-permute-start.32 = (f32[288,256]{1,0:T(8,128)}, f32[288,256]{1,0:T(8,128)S(1)}, u32[]{:S(2)}, u32[]{:S(2)}) collective-permute-start(f32[288,256]{1,0:T(8,128)} %convert_add_fusion), channel_id=1, source_target_pairs={{0,0},{1,1},{2,8},{3,9},{4,16},{5,17},{6,24},{7,25},{8,2},{9,3},{1... | collective-permute-start | bytes 884744 | tf_op jit(solution)/shard_map/ppermute | solution.py:433
  144.1 9.6 %all-to-all-start.1 = ((f32[32,2,16]{2,1,0:T(2,128)}), f32[32,2,16]{2,1,0:T(2,128)S(1)}, u32[]{:S(2)}, u32[]{:S(2)}) async-start(f32[32,2,16]{2,1,0:T(2,128)} %get-tuple-element.75), calls=%async_computation.1 | async-start | bytes 65536 | tf_op jit(solution)/shard_map/all_to_all | solution.py:526
  (3 other events, 5.4 us)

commit v11 on v10

--- a/solution.py
+++ b/solution.py
@@ -181,7 +181,7 @@
         give[:, last] = spread_lanes(jnp.where(lane < base, acc[:, last], more), base)
 
 
-def partial_call(scal, sides, feeds, wr, wg, wu, mib, deps):
+def partial_call(scal, sides, feeds, wr, wg, wu, deps):
     experts, depth, hidden = wg.shape
     tokens = feeds[0].shape[1] * len(feeds)
     deep, wide = up_to(depth), 2 * up_to(hidden)
@@ -199,7 +199,7 @@
             pltpu.VMEM((tokens, wide), f32),
             pltpu.VMEM((tokens, LANES), f32),
         ],
-        compiler_params=params(mib),
+        compiler_params=params(20),
         cost_estimate=hint(
             4 * experts * depth * hidden * tokens, 4 * experts * depth * hidden + 6 * tokens * wide, 4
         ),
@@ -355,17 +355,38 @@
     )(*args)
 
 
+def gather_kernel(sides, got, message):
+    reqs = got.shape[1] // sides
+    for i in range(sides):
+        for group in range(got.shape[0] // sides):
+            v = 0.0
+            for x in range(sides):
+                at = (x ^ i) * reqs
+                v = v + got[group * sides + x, at : at + reqs]
+            at = (i * (got.shape[0] // sides) + group) * reqs
+            message[:, at : at + reqs] = jnp.broadcast_to(v[None], (message.shape[0], *v.shape))
+
+
+def gather_call(sides, got, copies):
+    out = shape((copies, got.shape[0] * got.shape[1] // sides, got.shape[2]), f32)
+    return pl.pallas_call(
+        lambda *refs: gather_kernel(sides, *refs),
+        in_specs=[VMEM],
+        out_specs=VMEM,
+        out_shape=out,
+        compiler_params=params(),
+        cost_estimate=hint(got.size, 8 * got.size),
+        name="end_rows_whole",
+    )(got)
+
+
 def head_kernel(order, got, gain, words, softness, logits, message, wide):
     blocks, block = gain.shape
     rows, columns = logits.shape
     ends, squares = [], 0.0
     reqs = rows // len(order[0])
     for b in range(blocks):
-        v = []
-        for sources in order[b]:
-            terms = [got[at, i * reqs : (i + 1) * reqs] for at, i in sources]
-            v.append(sum(terms[1:], terms[0]))
-        v = jnp.concatenate(v, axis=0)
+        v = jnp.concatenate([got[at, row : row + reqs] for at, row in order[b]], axis=0)
         squares = squares + jnp.sum(v * v, axis=1, keepdims=True)
         ends.append(v)
     scale = lax.rsqrt(squares / WIDTH + epsilon)
@@ -384,13 +405,33 @@
     message[...] = jnp.broadcast_to(turned[None, 0:2, 0:rows], message.shape)
 
 
-def head_call(order, got, gain, words, softness):
+def pairs_kernel(pairs, message):
+    top, mass = pairs[:, 0], pairs[:, 1]
+    largest = jnp.max(top, axis=0, keepdims=True)
+    total = jnp.sum(mass * jnp.exp(top - largest), axis=0, keepdims=True)
+    both = jnp.concatenate([largest, total], axis=0)
+    message[...] = jnp.broadcast_to(both[None], message.shape)
+
+
+def pairs_call(pairs, copies):
+    return pl.pallas_call(
+        pairs_kernel,
+        in_specs=[VMEM],
+        out_specs=VMEM,
+        out_shape=shape((copies, *pairs.shape[1:]), f32),
+        compiler_params=params(),
+        cost_estimate=hint(pairs.size, 8 * pairs.size),
+        name="pairs",
+    )(pairs)
+
+
+def head_call(order, got, gain, words, softness, copies):
     rows, columns = softness.shape[0], words.shape[1]
     return pl.pallas_call(
         lambda *refs: head_kernel(order, *refs),
         in_specs=[VMEM] * 4,
         out_specs=[VMEM, VMEM],
-        out_shape=[shape((rows, columns), f32), shape((got.shape[0], 2, rows), f32)],
+        out_shape=[shape((rows, columns), f32), shape((copies, 2, rows), f32)],
         scratch_shapes=[pltpu.VMEM((LANES, LANES), f32)],
         compiler_params=params(),
         cost_estimate=hint(2 * rows * WIDTH * columns, 2 * WIDTH * columns),
@@ -413,7 +454,6 @@
 ):
     tokens, block = skip_stream_arriving.shape
     dp, mp = lax.axis_size("dp"), lax.axis_size("mp")
-    count = dp * mp
     parts = 4
     spread, sides = dp // parts, mp // parts
     assert dp == parts * spread and mp == parts * sides and sides & (sides - 1) == 0
@@ -458,13 +498,15 @@
     pair = join_call(first)
     feeds = {1: pair}
     step = lambda v: send(v, lambda q, z, x: (q, (z - 1) % parts, x))
-    feeds[2] = step(pair)
-    feeds[3] = step(feeds[2])
     stream = send(stream, home)
+    reqs = sequence_piece_tallies.shape[1]
     partial, kept, pieces, shares, last = {}, {}, {}, {}, []
 
+    def after(v, dep):
+        return lax.optimization_barrier((v, dep))[0]
+
     def do_partial(s, *deps):
-        own, give, cols = partial_call(scal, sides, [feeds[g] for g in chunks[s]], wr, wg, wu, 20 if s else 57, deps)
+        own, give, cols = partial_call(scal, sides, [feeds[g] for g in chunks[s]], wr, wg, wu, deps)
         partial[s] = (own, send(give, other_core), cols)
         return own
 
@@ -481,7 +523,7 @@
 
     def do_hop(s, dep):
         a, a_y = pieces[s]
-        late = [v if dep is None else lax.optimization_barrier((v, dep))[0] for v in (a, a_y)]
+        late = [v if dep is None else after(v, dep) for v in (a, a_y)]
         pieces[s] = (a, a_y, *[send(v, other_core) for v in late])
 
     def do_down(s, *deps):
@@ -498,11 +540,13 @@
                 shares[group] = [send(share, back)]
         return outs[0]
 
+    feeds[2] = step(feeds[1])
+    feeds[3] = step(feeds[2])
     p0 = do_partial(0)
     p1 = do_partial(1, p0)
     s0 = do_sum(0, p1)
     p2 = do_partial(2, s0)
-    feeds[0] = step(lax.optimization_barrier((feeds[3], p2))[0])
+    feeds[0] = step(after(feeds[3], p2))
     s1 = do_sum(1, p2)
     a0 = do_act(0, s1)
     p3 = do_partial(3, a0)
@@ -520,18 +564,14 @@
     do_hop(3, None)
     d3 = do_down(3, d2)
     backs = [shares[group][0] for group in range(1, parts)]
-    message = ends_call(partial[parts - 1][2], stream, last, backs, count)
+    exchange = lambda v, axis: lax.all_to_all(v, axis, 0, 0, tiled=True)
+    message = ends_call(partial[parts - 1][2], stream, last, backs, mp)
+    got, shares[0] = lax.optimization_barrier((exchange(message, "mp"), shares[0]))
+    got = exchange(gather_call(sides, got, dp), "dp")
     total = sum(v.astype(f32) for v in shares[0] + backs)
-
-    everyone = lambda v: lax.all_to_all(v, ("dp", "mp"), 0, 0, tiled=True)
-    got = everyone(message)
     branch = send(total, home)
     order = [
-        [
-            [((q * spread + r) * mp + z * sides + x2, x2 ^ x) for x2 in range(sides)]
-            for z in range(parts)
-            for r in range(spread)
-        ]
+        [(q * spread + r, (x * parts + group) * reqs) for group in range(parts) for r in range(spread)]
         for q in range(parts)
         for x in range(sides)
     ]
@@ -541,8 +581,9 @@
         terminal_rmsnorm_gain.reshape(mp, block),
         lexicon_projector_weights,
         softness_per_sequence[:, None],
+        mp,
     )
-    pairs = everyone(pairs)
+    pairs = exchange(pairs_call(exchange(pairs, "mp"), dp), "dp")
     new_hidden = skip_stream_arriving + branch_scale * branch.T
     largest = jnp.max(pairs[:, 0], axis=0)
     mass = jnp.sum(pairs[:, 1] * jnp.exp(pairs[:, 0] - largest), axis=0)

time: 157 us -> 172 us (1.096); the launches traced: 154 us -> 172 us
  blocking collectives: 0 us -> 18.7 us
  waiting for transfers between devices: 47.5 us -> 56.2 us
  starting transfers between devices: 44.2 us -> 40.6 us
  Pallas kernels: 49.4 us -> 46.5 us
  other arithmetic: 4.57 us -> 2.7 us
    ppermute x34, waiting for transfers between devices: 30.7 us -> 52.7 us  [send(): return lax.ppermute(value, ('dp', 'mp'), pairs)]
    all_to_all x0 -> x2, blocking collectives: none -> 18.7 us  [body(): exchange = lambda v, axis: lax.all_to_all(v, axis, 0, 0, tiled=True)]
    all_to_all x2, waiting for transfers between devices: 16.7 us -> 3.51 us  [body(): exchange = lambda v, axis: lax.all_to_all(v, axis, 0, 0, tiled=True)]
    ppermute x34, starting transfers between devices: 35.8 us -> 30.5 us  [send(): return lax.ppermute(value, ('dp', 'mp'), pairs)]
    pallas_call x4, Pallas kernels: 22.4 us -> 19.6 us  [partial_call(): pl.pallas_call(lambda *refs: partial_kernel(sides, len(feeds), *refs), gr...]
    all_to_all x2, starting transfers between devices: 8.45 us -> 10.2 us  [body(): exchange = lambda v, axis: lax.all_to_all(v, axis, 0, 0, tiled=True)]
    unnamed x30 -> x24, local copies, waits for them, and re-layouts: 6.27 us -> 4.71 us
  transfers between devices with their start and end apart: 36 -> 36, of which waited for: 14 -> 14; matrix products, arithmetic and copies ran while one was open for 3% -> 1% of each run, Pallas kernels for 31% -> 25%
where the time goes in v11:
time: 172 us
  waiting for transfers between devices  56.2 us (33%)
  Pallas kernels  46.5 us (27%)
  starting transfers between devices  40.6 us (24%)
  blocking collectives  18.7 us (11%)
  local copies, waits for them, and re-layouts  6.22 us (4%)
  other arithmetic  2.7 us (2%)
    ppermute x34, waiting for transfers between devices, send(): return lax.ppermute(value, ('dp', 'mp'), pairs)  52.7 us
    ppermute x34, starting transfers between devices, send(): return lax.ppermute(value, ('dp', 'mp'), pairs)  30.5 us
    pallas_call x4, Pallas kernels, partial_call(): pl.pallas_call(lambda *refs: partial_kernel(sides, len(feeds), *refs), gr...  19.6 us
    all_to_all x2, blocking collectives, body(): exchange = lambda v, axis: lax.all_to_all(v, axis, 0, 0, tiled=True)  18.7 us
    pallas_call x4, Pallas kernels, down_call(): pl.pallas_call(lambda *refs: down_kernel(sides, *refs), grid=(experts,),...  13.9 us
    all_to_all x2, starting transfers between devices, body(): exchange = lambda v, axis: lax.all_to_all(v, axis, 0, 0, tiled=True)  10.2 us
    pallas_call x4, Pallas kernels, act_call(): pl.pallas_call(lambda *refs: act_kernel(base, *refs), in_specs=[SMEM] + [...  4.94 us
    unnamed x24, local copies, waits for them, and re-layouts  4.71 us
  transfers between devices with their start and end apart: 36, of which 14 were waited for; matrix products, arithmetic and copies ran while one was open for 1% of the time, Pallas kernels for 25%

profile of v11, /device:TPU:4, one launch (start us, length us, event | category | flops | bytes accessed | tf_op | source)
XLA Modules:
  0.0 171.9 jit_solution(16458710373570102271)
XLA Ops:
  0.6 1.3 broadcast_in_dim.4.gain
  1.9 1.9 %prep.1 = (bf16[304,256]{1,0:T(8,128)(2,1)}, f32[4,288]{1,0:T(4,128)}) custom-call(s32[1,4]{1,0:T(1,128)} %tallies.1, f32[288,256]{1,0:T(8,128)} %bitcast.17, f32[1,288]{1,0:T(1,128)} %broadcast_in_dim.4.gain, s32[2,256]{1,0:T(2,128)} %bitcast.20), custom_call_target="tpu_custom_call" | custom-call | flops 88473 | bytes 132710 | tf_op jit(solution)/shard_map/prep/pallas_call | solution.py:75
  3.8 1.5 collective-permute-start
  5.3 3.0 %collective-permute-start.1 = (bf16[304,256]{1,0:T(8,128)(2,1)}, bf16[304,256]{1,0:T(8,128)(2,1)S(1)}, u32[]{:S(2)}, u32[]{:S(2)}) collective-permute-start(bf16[304,256]{1,0:T(8,128)(2,1)} %get-tuple-element.42), channel_id=1, source_target_pairs={{0,7},{1,6},{2,15},{3,14},{4,23},{5,22},{6,31},{7,30},{8,1},{9,0},... | collective-permute-start | bytes 466952 | tf_op jit(solution)/shard_map/ppermute | solution.py:473
  8.5 3.8 %collective-permute-done.refs_0_ = bf16[304,256]{1,0:T(8,128)(2,1)S(1)} collective-permute-done((bf16[304,256]{1,0:T(8,128)(2,1)}, bf16[304,256]{1,0:T(8,128)(2,1)S(1)}, u32[]{:S(2)}, u32[]{:S(2)}) %collective-permute-start) | collective-permute-done | bytes 155680 | tf_op jit(solution)/shard_map/ppermute | solution.py:473
  12.3 4.3 %collective-permute-done.1.refs_1_ = bf16[304,256]{1,0:T(8,128)(2,1)S(1)} collective-permute-done((bf16[304,256]{1,0:T(8,128)(2,1)}, bf16[304,256]{1,0:T(8,128)(2,1)S(1)}, u32[]{:S(2)}, u32[]{:S(2)}) %collective-permute-start.1) | collective-permute-done | bytes 155680 | tf_op jit(solution)/shard_map/ppermute | solution.py:473
  16.5 5.9 %collective-permute-start.2 = (bf16[608,256]{1,0:T(8,128)(2,1)S(1)}, bf16[608,256]{1,0:T(8,128)(2,1)S(1)}, u32[]{:S(2)}, u32[]{:S(2)}) collective-permute-start(bf16[608,256]{1,0:T(8,128)(2,1)S(1)} %join.1.refs_1_), channel_id=1, source_target_pairs={{0,6},{1,7},{2,0},{3,1},{4,2},{5,3},{6,4},{7,5},{8,14},{9,15},{10,... | collective-permute-start | bytes 933896 | tf_op jit(solution)/shard_map/ppermute | solution.py:473
  22.5 2.0 %copy-done.2 = bf16[4,576,720]{2,1,0:T(8,128)(2,1)S(1)} copy-done((bf16[4,576,720]{2,1,0:T(8,128)(2,1)S(1)}, bf16[4,576,720]{2,1,0:T(8,128)(2,1)}, u32[]{:S(2)}) %copy-start.2) | copy-done | bytes 3317784
  24.5 2.0 %copy-done.4 = bf16[4,576,720]{2,1,0:T(8,128)(2,1)S(1)} copy-done((bf16[4,576,720]{2,1,0:T(8,128)(2,1)S(1)}, bf16[4,576,720]{2,1,0:T(8,128)(2,1)}, u32[]{:S(2)}) %copy-start.4) | copy-done | bytes 3317784
  26.5 4.9 %gate_up_partial.4 = (f32[256,1536]{1,0:T(8,128)S(1)}, bf16[256,1536]{1,0:T(8,128)(2,1)S(1)}, bf16[256,128]{1,0:T(8,128)(2,1)S(1)}) custom-call(s32[3]{0:T(128)S(1)} %pad_add_fusion.1.refs_0_, bf16[608,256]{1,0:T(8,128)(2,1)S(1)} %join.1.refs_1_, bf16[128,576]{1,0:T(8,128)(2,1)S(1)} %pad_add_fusion.refs_2_, bf16[4,576,720]{2,1,0:T(8,128)(2,1)S(1)} %copy-done.2, ...), custom_call_target="tpu_custom_call" | custom-call | flops 6794772480 | bytes 35979264 | tf_op jit(solution)/shard_map/gate_up_partial/pallas_call | solution.py:190
  31.6 4.9 %gate_up_partial.5 = (f32[256,1536]{1,0:T(8,128)S(1)}, bf16[256,1536]{1,0:T(8,128)(2,1)S(1)}, bf16[256,128]{1,0:T(8,128)(2,1)S(1)}) custom-call(s32[3]{0:T(128)S(1)} %pad_add_fusion.1.refs_0_, bf16[608,256]{1,0:T(8,128)(2,1)S(1)} %collective-permute-done.2.refs_1_, bf16[128,576]{1,0:T(8,128)(2,1)S(1)} %pad_add_fusion.refs_2_, ...), custom_call_target="tpu_custom_call" | custom-call | flops 6794772480 | bytes 35979264 | tf_op jit(solution)/shard_map/gate_up_partial/pallas_call | solution.py:190
  37.0 0.9 core_sum.4
  37.9 3.3 %collective-permute-done.3.refs_1_ = bf16[608,256]{1,0:T(8,128)(2,1)S(1)} collective-permute-done((bf16[608,256]{1,0:T(8,128)(2,1)S(1)}, bf16[608,256]{1,0:T(8,128)(2,1)S(1)}, u32[]{:S(2)}, u32[]{:S(2)}) %collective-permute-start.3) | collective-permute-done | bytes 311328 | tf_op jit(solution)/shard_map/ppermute | solution.py:473
  41.2 4.9 %gate_up_partial.6 = (f32[256,1536]{1,0:T(8,128)S(1)}, bf16[256,1536]{1,0:T(8,128)(2,1)S(1)}, bf16[256,128]{1,0:T(8,128)(2,1)S(1)}) custom-call(s32[3]{0:T(128)S(1)} %pad_add_fusion.1.refs_0_, bf16[608,256]{1,0:T(8,128)(2,1)S(1)} %collective-permute-done.3.refs_1_, bf16[128,576]{1,0:T(8,128)(2,1)S(1)} %pad_add_fusion.refs_2_, ...), custom_call_target="tpu_custom_call" | custom-call | flops 6794772480 | bytes 35979264 | tf_op jit(solution)/shard_map/gate_up_partial/pallas_call | solution.py:190
  46.1 2.1 %collective-permute-start.5 = (bf16[608,256]{1,0:T(8,128)(2,1)S(1)}, bf16[608,256]{1,0:T(8,128)(2,1)S(1)}, u32[]{:S(2)}, u32[]{:S(2)}) collective-permute-start(bf16[608,256]{1,0:T(8,128)(2,1)S(1)} %collective-permute-done.3.refs_1_), channel_id=1, source_target_pairs={{0,6},{1,7},{2,0},{3,1},{4,2},{5,3},{6,4},{7,5},{8,14},{9,15},{10,... | collective-permute-start | bytes 933896 | tf_op jit(solution)/shard_map/ppermute | solution.py:473
  48.3 0.9 core_sum.5
  49.2 1.2 act.4.refs_5_.refs_1_
  50.5 2.1 %collective-permute-start.10 = (bf16[128,768]{1,0:T(8,128)(2,1)S(1)}, bf16[128,768]{1,0:T(8,128)(2,1)S(1)}, u32[]{:S(2)}, u32[]{:S(2)}) collective-permute-start(bf16[128,768]{1,0:T(8,128)(2,1)S(1)} %act.4.refs_5_.refs_1_), channel_id=1, source_target_pairs={{0,16},{1,17},{2,18},{3,19},{4,20},{5,21},{6,22},{7,23},{8,24},{9,... | collective-permute-start | bytes 589832 | tf_op jit(solution)/shard_map/ppermute | solution.py:473
  52.5 2.6 %collective-permute-done.5.refs_1_ = bf16[608,256]{1,0:T(8,128)(2,1)S(1)} collective-permute-done((bf16[608,256]{1,0:T(8,128)(2,1)S(1)}, bf16[608,256]{1,0:T(8,128)(2,1)S(1)}, u32[]{:S(2)}, u32[]{:S(2)}) %collective-permute-start.5) | collective-permute-done | bytes 311328 | tf_op jit(solution)/shard_map/ppermute | solution.py:473
  55.1 4.9 %gate_up_partial.7 = (f32[256,1536]{1,0:T(8,128)S(1)}, bf16[256,1536]{1,0:T(8,128)(2,1)S(1)}, bf16[256,128]{1,0:T(8,128)(2,1)S(1)}) custom-call(s32[3]{0:T(128)S(1)} %pad_add_fusion.1.refs_0_, bf16[608,256]{1,0:T(8,128)(2,1)S(1)} %collective-permute-done.5.refs_1_, bf16[128,576]{1,0:T(8,128)(2,1)S(1)} %pad_add_fusion.refs_2_, ...), custom_call_target="tpu_custom_call" | custom-call | flops 6794772480 | bytes 35979264 | tf_op jit(solution)/shard_map/gate_up_partial/pallas_call | solution.py:190
  60.1 0.9 core_sum.6
  61.5 3.4 %collective-permute-done.10.refs_2_ = bf16[128,768]{1,0:T(8,128)(2,1)S(1)} collective-permute-done((bf16[128,768]{1,0:T(8,128)(2,1)S(1)}, bf16[128,768]{1,0:T(8,128)(2,1)S(1)}, u32[]{:S(2)}, u32[]{:S(2)}) %collective-permute-start.10) | collective-permute-done | bytes 196640 | tf_op jit(solution)/shard_map/ppermute | solution.py:473
  65.2 1.2 act.5.refs_7_.refs_1_
  66.5 1.8 %collective-permute-start.16 = (bf16[128,768]{1,0:T(8,128)(2,1)S(1)}, bf16[128,768]{1,0:T(8,128)(2,1)S(1)}, u32[]{:S(2)}, u32[]{:S(2)}) collective-permute-start(bf16[128,768]{1,0:T(8,128)(2,1)S(1)} %act.5.refs_7_.refs_1_), channel_id=1, source_target_pairs={{0,16},{1,17},{2,18},{3,19},{4,20},{5,21},{6,22},{7,23},{8,24},{9,... | collective-permute-start | bytes 589832 | tf_op jit(solution)/shard_map/ppermute | solution.py:473
  68.3 3.5 %down.4 = (bf16[288,256]{1,0:T(8,128)(2,1)S(1)}, bf16[288,256]{1,0:T(8,128)(2,1)S(1)}) custom-call(s32[3]{0:T(128)S(1)} %pad_add_fusion.1.refs_0_, bf16[128,768]{1,0:T(8,128)(2,1)S(1)} %act.4.refs_5_.refs_1_, bf16[128,768]{1,0:T(8,128)(2,1)S(1)} %collective-permute-done.10.refs_2_, bf16[128,768]{1,0:T(8,128)(2,1)S(1)} %collective-permute-done.12.refs_3_, ...), custom_call_target="tpu_custom_call" | custom-call | flops 3397386240 | bytes 14450688 | tf_op jit(solution)/shard_map/down/pallas_call | solution.py:306
  72.4 0.9 core_sum.7
  73.3 3.6 %collective-permute-done.19.refs_2_ = bf16[128,1536]{1,0:T(8,128)(2,1)S(1)} collective-permute-done((bf16[128,1536]{1,0:T(8,128)(2,1)S(1)}, bf16[128,1536]{1,0:T(8,128)(2,1)S(1)}, u32[]{:S(2)}, u32[]{:S(2)}) %collective-permute-start.19) | collective-permute-done | bytes 393248 | tf_op jit(solution)/shard_map/ppermute | solution.py:473
  76.9 1.2 act.6.refs_7_.refs_1_
  78.4 1.7 %collective-permute-start.15 = (bf16[128,1536]{1,0:T(8,128)(2,1)S(1)}, bf16[128,1536]{1,0:T(8,128)(2,1)S(1)}, u32[]{:S(2)}, u32[]{:S(2)}) collective-permute-start(bf16[128,1536]{1,0:T(8,128)(2,1)S(1)} %get-tuple-element.65), channel_id=1, source_target_pairs={{0,16},{1,17},{2,18},{3,19},{4,20},{5,21},{6,22},{7,23},{8,24},{9,... | collective-permute-start | bytes 1179656 | tf_op jit(solution)/shard_map/ppermute | solution.py:473
  80.2 0.9 collective-permute-done.16.refs_2_
  81.4 4.6 %collective-permute-done.23.refs_2_ = bf16[128,768]{1,0:T(8,128)(2,1)S(1)} collective-permute-done((bf16[128,768]{1,0:T(8,128)(2,1)S(1)}, bf16[128,768]{1,0:T(8,128)(2,1)S(1)}, u32[]{:S(2)}, u32[]{:S(2)}) %collective-permute-start.23) | collective-permute-done | bytes 196640 | tf_op jit(solution)/shard_map/ppermute | solution.py:473
  86.5 3.5 %down.5 = (bf16[288,256]{1,0:T(8,128)(2,1)S(1)}, bf16[288,256]{1,0:T(8,128)(2,1)S(1)}) custom-call(s32[3]{0:T(128)S(1)} %pad_add_fusion.1.refs_0_, bf16[128,768]{1,0:T(8,128)(2,1)S(1)} %act.5.refs_7_.refs_1_, bf16[128,768]{1,0:T(8,128)(2,1)S(1)} %collective-permute-done.16.refs_2_, bf16[128,768]{1,0:T(8,128)(2,1)S(1)} %collective-permute-done.17.refs_3_, ...), custom_call_target="tpu_custom_call" | custom-call | flops 3397386240 | bytes 14450688 | tf_op jit(solution)/shard_map/down/pallas_call | solution.py:306
  90.6 2.7 %collective-permute-done.15.refs_2_ = bf16[128,1536]{1,0:T(8,128)(2,1)S(1)} collective-permute-done((bf16[128,1536]{1,0:T(8,128)(2,1)S(1)}, bf16[128,1536]{1,0:T(8,128)(2,1)S(1)}, u32[]{:S(2)}, u32[]{:S(2)}) %collective-permute-start.15) | collective-permute-done | bytes 393248 | tf_op jit(solution)/shard_map/ppermute | solution.py:473
  93.3 1.2 act.7.refs_7_.refs_1_
  94.9 3.5 %down.6 = (bf16[288,256]{1,0:T(8,128)(2,1)S(1)}, bf16[288,256]{1,0:T(8,128)(2,1)S(1)}) custom-call(s32[3]{0:T(128)S(1)} %pad_add_fusion.1.refs_0_, bf16[128,768]{1,0:T(8,128)(2,1)S(1)} %act.6.refs_7_.refs_1_, bf16[128,768]{1,0:T(8,128)(2,1)S(1)} %collective-permute-done.23.refs_2_, bf16[128,768]{1,0:T(8,128)(2,1)S(1)} %collective-permute-done.24.refs_3_, ...), custom_call_target="tpu_custom_call" | custom-call | flops 3397386240 | bytes 14450688 | tf_op jit(solution)/shard_map/down/pallas_call | solution.py:306
  99.2 1.2 collective-permute-done.20.refs_2_
  100.4 3.2 %collective-permute-done.30 = bf16[288,256]{1,0:T(8,128)(2,1)S(1)} collective-permute-done((bf16[288,256]{1,0:T(8,128)(2,1)S(1)}, bf16[288,256]{1,0:T(8,128)(2,1)S(1)}, u32[]{:S(2)}, u32[]{:S(2)}) %collective-permute-start.30) | collective-permute-done | bytes 147488 | tf_op jit(solution)/shard_map/ppermute | solution.py:473
  104.4 3.5 %down.7 = (bf16[288,256]{1,0:T(8,128)(2,1)S(1)}, bf16[288,256]{1,0:T(8,128)(2,1)S(1)}) custom-call(s32[3]{0:T(128)S(1)} %pad_add_fusion.1.refs_0_, bf16[128,768]{1,0:T(8,128)(2,1)S(1)} %act.7.refs_7_.refs_1_, bf16[128,768]{1,0:T(8,128)(2,1)S(1)} %collective-permute-done.20.refs_2_, bf16[128,768]{1,0:T(8,128)(2,1)S(1)} %collective-permute-done.21.refs_3_, ...), custom_call_target="tpu_custom_call" | custom-call | flops 3397386240 | bytes 14450688 | tf_op jit(solution)/shard_map/down/pallas_call | solution.py:306
  108.5 3.8 %collective-permute-start.8 = (f32[4,288]{1,0:T(4,128)S(1)}, f32[4,288]{1,0:T(4,128)S(1)}, u32[]{:S(2)}, u32[]{:S(2)}) collective-permute-start(f32[4,288]{1,0:T(4,128)S(1)} %copy-done.11), channel_id=1, source_target_pairs={{0,0},{1,1},{2,8},{3,9},{4,16},{5,17},{6,24},{7,25},{8,2},{9,3},{1... | collective-permute-start | bytes 13832 | tf_op jit(solution)/shard_map/ppermute | solution.py:473
  112.4 3.5 %collective-permute-done.8.refs_1_ = f32[4,288]{1,0:T(4,128)S(1)} collective-permute-done((f32[4,288]{1,0:T(4,128)S(1)}, f32[4,288]{1,0:T(4,128)S(1)}, u32[]{:S(2)}, u32[]{:S(2)}) %collective-permute-start.8) | collective-permute-done | bytes 4640 | tf_op jit(solution)/shard_map/ppermute | solution.py:473
  116.5 9.8 %all_to_all.20.refs_0_ = f32[8,8,288]{2,1,0:T(8,128)S(1)} all-to-all(f32[8,8,288]{2,1,0:T(8,128)S(1)} %end_rows.1), channel_id=1, replica_groups=mesh['dp'=4,'mp'=8] {'mp'}, dimensions={0} | all-to-all | bytes 147456 | tf_op jit(solution)/shard_map/all_to_all | solution.py:567
  127.6 5.3 %all-to-all-start.1 = ((f32[4,32,288]{2,1,0:T(8,128)}), f32[4,32,288]{2,1,0:T(8,128)S(1)}, u32[]{:S(2)}, u32[]{:S(2)}) async-start(f32[4,32,288]{2,1,0:T(8,128)} %end_rows_whole.1), calls=%async_computation.1 | async-start | bytes 393216 | tf_op jit(solution)/shard_map/all_to_all | solution.py:567
  133.1 3.5 %all-to-all-done.1.refs_0_ = f32[4,32,288]{2,1,0:T(8,128)S(1)} async-done(((f32[4,32,288]{2,1,0:T(8,128)}), f32[4,32,288]{2,1,0:T(8,128)S(1)}, u32[]{:S(2)}, u32[]{:S(2)}) %all-to-all-start.1) | async-done | bytes 147488 | tf_op jit(solution)/shard_map/all_to_all | solution.py:567
  137.4 8.9 %all_to_all.21.pairs = f32[8,2,16]{2,1,0:T(2,128)S(1)} all-to-all(f32[8,2,16]{2,1,0:T(2,128)S(1)} %get-tuple-element.81), channel_id=1, replica_groups=mesh['dp'=4,'mp'=8] {'mp'}, dimensions={0} | all-to-all | bytes 2048 | tf_op jit(solution)/shard_map/all_to_all | solution.py:567
  146.9 4.9 %all-to-all-start.3 = ((f32[4,2,16]{2,1,0:T(2,128)}), f32[4,2,16]{2,1,0:T(2,128)S(1)}, u32[]{:S(2)}, u32[]{:S(2)}) async-start(f32[4,2,16]{2,1,0:T(2,128)} %pairs.1), calls=%async_computation.3 | async-start | bytes 8192 | tf_op jit(solution)/shard_map/all_to_all | solution.py:567
  151.8 1.0 convert_add_fusion
  152.8 1.9 %collective-permute-start.33 = (f32[288,256]{1,0:T(8,128)S(1)}, f32[288,256]{1,0:T(8,128)S(1)}, u32[]{:S(2)}, u32[]{:S(2)}) collective-permute-start(f32[288,256]{1,0:T(8,128)S(1)} %convert_add_fusion), channel_id=1, source_target_pairs={{0,0},{1,1},{2,8},{3,9},{4,16},{5,17},{6,24},{7,25},{8,2},{9,3},{1... | collective-permute-start | bytes 884744 | tf_op jit(solution)/shard_map/ppermute | solution.py:473
  155.5 15.7 %collective-permute-done.33 = f32[288,256]{1,0:T(8,128)S(1)} collective-permute-done((f32[288,256]{1,0:T(8,128)S(1)}, f32[288,256]{1,0:T(8,128)S(1)}, u32[]{:S(2)}, u32[]{:S(2)}) %collective-permute-start.33) | collective-permute-done | bytes 294944 | tf_op jit(solution)/shard_map/ppermute | solution.py:473
  (87 shorter events, 12.1 us)
Async XLA Ops:
  0.6 7.7 %copy-start = (bf16[2304,4]{0,1:T(4,128)(2,1)S(1)}, bf16[2304,4]{0,1:T(4,128)(2,1)}, u32[]{:S(2)}) copy-start(bf16[2304,4]{0,1:T(4,128)(2,1)} %param.15) | copy-start | bytes 55300
  3.8 8.4 %collective-permute-start = (bf16[304,256]{1,0:T(8,128)(2,1)}, bf16[304,256]{1,0:T(8,128)(2,1)S(1)}, u32[]{:S(2)}, u32[]{:S(2)}) collective-permute-start(bf16[304,256]{1,0:T(8,128)(2,1)} %get-tuple-element.42), channel_id=1, source_target_pairs={{0,6},{1,7},{2,14},{3,15},{4,22},{5,23},{6,30},{7,31},{8,0},{9,1},... | collective-permute-start | bytes 466952 | tf_op jit(solution)/shard_map/ppermute | solution.py:473
  5.3 11.2 %collective-permute-start.1 = (bf16[304,256]{1,0:T(8,128)(2,1)}, bf16[304,256]{1,0:T(8,128)(2,1)S(1)}, u32[]{:S(2)}, u32[]{:S(2)}) collective-permute-start(bf16[304,256]{1,0:T(8,128)(2,1)} %get-tuple-element.42), channel_id=1, source_target_pairs={{0,7},{1,6},{2,15},{3,14},{4,23},{5,22},{6,31},{7,30},{8,1},{9,0},... | collective-permute-start | bytes 466952 | tf_op jit(solution)/shard_map/ppermute | solution.py:473
  16.5 14.9 %collective-permute-start.2 = (bf16[608,256]{1,0:T(8,128)(2,1)S(1)}, bf16[608,256]{1,0:T(8,128)(2,1)S(1)}, u32[]{:S(2)}, u32[]{:S(2)}) collective-permute-start(bf16[608,256]{1,0:T(8,128)(2,1)S(1)} %join.1.refs_1_), channel_id=1, source_target_pairs={{0,6},{1,7},{2,0},{3,1},{4,2},{5,3},{6,4},{7,5},{8,14},{9,15},{10,... | collective-permute-start | bytes 933896 | tf_op jit(solution)/shard_map/ppermute | solution.py:473
  22.5 2.0 %copy-start.2 = (bf16[4,576,720]{2,1,0:T(8,128)(2,1)S(1)}, bf16[4,576,720]{2,1,0:T(8,128)(2,1)}, u32[]{:S(2)}) copy-start(bf16[4,576,720]{2,1,0:T(8,128)(2,1)} %refs_3_.7) | copy-start | bytes 9953284
  24.5 2.0 %copy-start.4 = (bf16[4,576,720]{2,1,0:T(8,128)(2,1)S(1)}, bf16[4,576,720]{2,1,0:T(8,128)(2,1)}, u32[]{:S(2)}) copy-start(bf16[4,576,720]{2,1,0:T(8,128)(2,1)} %refs_4_.7) | copy-start | bytes 9953284
  26.5 5.1 %copy-start.3 = (bf16[4,576,720]{2,1,0:T(8,128)(2,1)S(1)}, bf16[4,576,720]{2,1,0:T(8,128)(2,1)}, u32[]{:S(2)}) copy-start(bf16[4,576,720]{2,1,0:T(8,128)(2,1)} %refs_3_.7) | copy-start | bytes 9953284
  26.5 5.1 %copy-start.5 = (bf16[4,576,720]{2,1,0:T(8,128)(2,1)S(1)}, bf16[4,576,720]{2,1,0:T(8,128)(2,1)}, u32[]{:S(2)}) copy-start(bf16[4,576,720]{2,1,0:T(8,128)(2,1)} %refs_4_.7) | copy-start | bytes 9953284
  31.4 5.6 %collective-permute-start.4 = (bf16[256,1536]{1,0:T(8,128)(2,1)S(1)}, bf16[256,1536]{1,0:T(8,128)(2,1)S(1)}, u32[]{:S(2)}, u32[]{:S(2)}) collective-permute-start(bf16[256,1536]{1,0:T(8,128)(2,1)S(1)} %get-tuple-element.44), channel_id=1, source_target_pairs={{0,8},{1,9},{2,10},{3,11},{4,12},{5,13},{6,14},{7,15},{8,0},{9,1},... | collective-permute-start | bytes 2359304 | tf_op jit(solution)/shard_map/ppermute | solution.py:473
  31.5 9.8 %collective-permute-start.3 = (bf16[608,256]{1,0:T(8,128)(2,1)S(1)}, bf16[608,256]{1,0:T(8,128)(2,1)S(1)}, u32[]{:S(2)}, u32[]{:S(2)}) collective-permute-start(bf16[608,256]{1,0:T(8,128)(2,1)S(1)} %collective-permute-done.2.refs_1_), channel_id=1, source_target_pairs={{0,6},{1,7},{2,0},{3,1},{4,2},{5,3},{6,4},{7,5},{8,14},{9,15},{10,... | collective-permute-start | bytes 933896 | tf_op jit(solution)/shard_map/ppermute | solution.py:473
  36.5 11.8 %collective-permute-start.7 = (bf16[256,1536]{1,0:T(8,128)(2,1)S(1)}, bf16[256,1536]{1,0:T(8,128)(2,1)S(1)}, u32[]{:S(2)}, u32[]{:S(2)}) collective-permute-start(bf16[256,1536]{1,0:T(8,128)(2,1)S(1)} %get-tuple-element.51), channel_id=1, source_target_pairs={{0,8},{1,9},{2,10},{3,11},{4,12},{5,13},{6,14},{7,15},{8,0},{9,1},... | collective-permute-start | bytes 2359304 | tf_op jit(solution)/shard_map/ppermute | solution.py:473
  37.8 11.4 %collective-permute-start.6 = (bf16[128,1536]{1,0:T(8,128)(2,1)S(1)}, bf16[128,1536]{1,0:T(8,128)(2,1)S(1)}, u32[]{:S(2)}, u32[]{:S(2)}) collective-permute-start(bf16[128,1536]{1,0:T(8,128)(2,1)S(1)} %get-tuple-element.49), channel_id=1, source_target_pairs={{0,16},{1,17},{2,18},{3,19},{4,20},{5,21},{6,22},{7,23},{8,24},{9,... | collective-permute-start | bytes 1179656 | tf_op jit(solution)/shard_map/ppermute | solution.py:473
  46.1 9.0 %collective-permute-start.5 = (bf16[608,256]{1,0:T(8,128)(2,1)S(1)}, bf16[608,256]{1,0:T(8,128)(2,1)S(1)}, u32[]{:S(2)}, u32[]{:S(2)}) collective-permute-start(bf16[608,256]{1,0:T(8,128)(2,1)S(1)} %collective-permute-done.3.refs_1_), channel_id=1, source_target_pairs={{0,6},{1,7},{2,0},{3,1},{4,2},{5,3},{6,4},{7,5},{8,14},{9,15},{10,... | collective-permute-start | bytes 933896 | tf_op jit(solution)/shard_map/ppermute | solution.py:473
  48.3 11.8 %collective-permute-start.11 = (bf16[256,1536]{1,0:T(8,128)(2,1)S(1)}, bf16[256,1536]{1,0:T(8,128)(2,1)S(1)}, u32[]{:S(2)}, u32[]{:S(2)}) collective-permute-start(bf16[256,1536]{1,0:T(8,128)(2,1)S(1)} %get-tuple-element.57), channel_id=1, source_target_pairs={{0,8},{1,9},{2,10},{3,11},{4,12},{5,13},{6,14},{7,15},{8,0},{9,1},... | collective-permute-start | bytes 2359304 | tf_op jit(solution)/shard_map/ppermute | solution.py:473
  49.1 16.1 %collective-permute-start.14 = (bf16[128,1536]{1,0:T(8,128)(2,1)S(1)}, bf16[128,1536]{1,0:T(8,128)(2,1)S(1)}, u32[]{:S(2)}, u32[]{:S(2)}) collective-permute-start(bf16[128,1536]{1,0:T(8,128)(2,1)S(1)} %get-tuple-element.61), channel_id=1, source_target_pairs={{0,16},{1,17},{2,18},{3,19},{4,20},{5,21},{6,22},{7,23},{8,24},{9,... | collective-permute-start | bytes 1179656 | tf_op jit(solution)/shard_map/ppermute | solution.py:473
  50.5 14.5 %collective-permute-start.10 = (bf16[128,768]{1,0:T(8,128)(2,1)S(1)}, bf16[128,768]{1,0:T(8,128)(2,1)S(1)}, u32[]{:S(2)}, u32[]{:S(2)}) collective-permute-start(bf16[128,768]{1,0:T(8,128)(2,1)S(1)} %act.4.refs_5_.refs_1_), channel_id=1, source_target_pairs={{0,16},{1,17},{2,18},{3,19},{4,20},{5,21},{6,22},{7,23},{8,24},{9,... | collective-permute-start | bytes 589832 | tf_op jit(solution)/shard_map/ppermute | solution.py:473
  60.0 12.4 %collective-permute-start.9 = (bf16[256,1536]{1,0:T(8,128)(2,1)S(1)}, bf16[256,1536]{1,0:T(8,128)(2,1)S(1)}, u32[]{:S(2)}, u32[]{:S(2)}) collective-permute-start(bf16[256,1536]{1,0:T(8,128)(2,1)S(1)} %get-tuple-element.56), channel_id=1, source_target_pairs={{0,8},{1,9},{2,10},{3,11},{4,12},{5,13},{6,14},{7,15},{8,0},{9,1},... | collective-permute-start | bytes 2359304 | tf_op jit(solution)/shard_map/ppermute | solution.py:473
  60.1 8.2 %copy-start.6 = (bf16[4,720,576]{1,2,0:T(8,128)(2,1)S(1)}, bf16[4,720,576]{1,2,0:T(8,128)(2,1)}, u32[]{:S(2)}) copy-start(bf16[4,720,576]{1,2,0:T(8,128)(2,1)} %param.18) | copy-start | bytes 9953284
  60.9 7.3 %collective-permute-start.12 = (bf16[128,768]{1,0:T(8,128)(2,1)S(1)}, bf16[128,768]{1,0:T(8,128)(2,1)S(1)}, u32[]{:S(2)}, u32[]{:S(2)}) collective-permute-start(bf16[128,768]{1,0:T(8,128)(2,1)S(1)} %act.4.refs_5_.refs_1_), channel_id=1, source_target_pairs={{0,8},{1,9},{2,10},{3,11},{4,12},{5,13},{6,14},{7,15},{8,0},{9,1},... | collective-permute-start | bytes 589832 | tf_op jit(solution)/shard_map/ppermute | solution.py:473
  64.9 3.3 %collective-permute-start.13 = (bf16[128,768]{1,0:T(8,128)(2,1)S(1)}, bf16[128,768]{1,0:T(8,128)(2,1)S(1)}, u32[]{:S(2)}, u32[]{:S(2)}) collective-permute-start(bf16[128,768]{1,0:T(8,128)(2,1)S(1)} %collective-permute-done.10.refs_2_), channel_id=1, source_target_pairs={{0,8},{1,9},{2,10},{3,11},{4,12},{5,13},{6,14},{7,15},{8,0},{9,1},... | collective-permute-start | bytes 589832 | tf_op jit(solution)/shard_map/ppermute | solution.py:473
  64.9 11.9 %collective-permute-start.19 = (bf16[128,1536]{1,0:T(8,128)(2,1)S(1)}, bf16[128,1536]{1,0:T(8,128)(2,1)S(1)}, u32[]{:S(2)}, u32[]{:S(2)}) collective-permute-start(bf16[128,1536]{1,0:T(8,128)(2,1)S(1)} %get-tuple-element.68), channel_id=1, source_target_pairs={{0,16},{1,17},{2,18},{3,19},{4,20},{5,21},{6,22},{7,23},{8,24},{9,... | collective-permute-start | bytes 1179656 | tf_op jit(solution)/shard_map/ppermute | solution.py:473
  66.5 14.6 %collective-permute-start.16 = (bf16[128,768]{1,0:T(8,128)(2,1)S(1)}, bf16[128,768]{1,0:T(8,128)(2,1)S(1)}, u32[]{:S(2)}, u32[]{:S(2)}) collective-permute-start(bf16[128,768]{1,0:T(8,128)(2,1)S(1)} %act.5.refs_7_.refs_1_), channel_id=1, source_target_pairs={{0,16},{1,17},{2,18},{3,19},{4,20},{5,21},{6,22},{7,23},{8,24},{9,... | collective-permute-start | bytes 589832 | tf_op jit(solution)/shard_map/ppermute | solution.py:473
  71.8 9.3 %collective-permute-start.26 = (bf16[288,256]{1,0:T(8,128)(2,1)S(1)}, bf16[288,256]{1,0:T(8,128)(2,1)S(1)}, u32[]{:S(2)}, u32[]{:S(2)}) collective-permute-start(bf16[288,256]{1,0:T(8,128)(2,1)S(1)} %get-tuple-element.74), channel_id=1, source_target_pairs={{0,1},{1,0},{2,3},{3,2},{4,5},{5,4},{6,7},{7,6},{8,9},{9,8},{10,11... | collective-permute-start | bytes 442376 | tf_op jit(solution)/shard_map/ppermute | solution.py:473
  78.1 7.9 %collective-permute-start.23 = (bf16[128,768]{1,0:T(8,128)(2,1)S(1)}, bf16[128,768]{1,0:T(8,128)(2,1)S(1)}, u32[]{:S(2)}, u32[]{:S(2)}) collective-permute-start(bf16[128,768]{1,0:T(8,128)(2,1)S(1)} %act.6.refs_7_.refs_1_), channel_id=1, source_target_pairs={{0,16},{1,17},{2,18},{3,19},{4,20},{5,21},{6,22},{7,23},{8,24},{9,... | collective-permute-start | bytes 589832 | tf_op jit(solution)/shard_map/ppermute | solution.py:473
  78.4 14.9 %collective-permute-start.15 = (bf16[128,1536]{1,0:T(8,128)(2,1)S(1)}, bf16[128,1536]{1,0:T(8,128)(2,1)S(1)}, u32[]{:S(2)}, u32[]{:S(2)}) collective-permute-start(bf16[128,1536]{1,0:T(8,128)(2,1)S(1)} %get-tuple-element.65), channel_id=1, source_target_pairs={{0,16},{1,17},{2,18},{3,19},{4,20},{5,21},{6,22},{7,23},{8,24},{9,... | collective-permute-start | bytes 1179656 | tf_op jit(solution)/shard_map/ppermute | solution.py:473
  80.2 5.8 %collective-permute-start.17 = (bf16[128,768]{1,0:T(8,128)(2,1)S(1)}, bf16[128,768]{1,0:T(8,128)(2,1)S(1)}, u32[]{:S(2)}, u32[]{:S(2)}) collective-permute-start(bf16[128,768]{1,0:T(8,128)(2,1)S(1)} %act.5.refs_7_.refs_1_), channel_id=1, source_target_pairs={{0,8},{1,9},{2,10},{3,11},{4,12},{5,13},{6,14},{7,15},{8,0},{9,1},... | collective-permute-start | bytes 589832 | tf_op jit(solution)/shard_map/ppermute | solution.py:473
  81.1 5.4 %collective-permute-start.18 = (bf16[128,768]{1,0:T(8,128)(2,1)S(1)}, bf16[128,768]{1,0:T(8,128)(2,1)S(1)}, u32[]{:S(2)}, u32[]{:S(2)}) collective-permute-start(bf16[128,768]{1,0:T(8,128)(2,1)S(1)} %collective-permute-done.16.refs_2_), channel_id=1, source_target_pairs={{0,8},{1,9},{2,10},{3,11},{4,12},{5,13},{6,14},{7,15},{8,0},{9,1},... | collective-permute-start | bytes 589832 | tf_op jit(solution)/shard_map/ppermute | solution.py:473
  81.1 34.7 %collective-permute-start.27 = (bf16[288,256]{1,0:T(8,128)(2,1)S(1)}, bf16[288,256]{1,0:T(8,128)(2,1)S(1)}, u32[]{:S(2)}, u32[]{:S(2)}) collective-permute-start(bf16[288,256]{1,0:T(8,128)(2,1)S(1)} %add_convert_fusion.2), channel_id=1, source_target_pairs={{0,2},{1,3},{2,4},{3,5},{4,6},{5,7},{6,0},{7,1},{8,10},{9,11},{10,... | collective-permute-start | bytes 442376 | tf_op jit(solution)/shard_map/ppermute | solution.py:473
  86.0 8.9 %collective-permute-start.24 = (bf16[128,768]{1,0:T(8,128)(2,1)S(1)}, bf16[128,768]{1,0:T(8,128)(2,1)S(1)}, u32[]{:S(2)}, u32[]{:S(2)}) collective-permute-start(bf16[128,768]{1,0:T(8,128)(2,1)S(1)} %act.6.refs_7_.refs_1_), channel_id=1, source_target_pairs={{0,8},{1,9},{2,10},{3,11},{4,12},{5,13},{6,14},{7,15},{8,0},{9,1},... | collective-permute-start | bytes 589832 | tf_op jit(solution)/shard_map/ppermute | solution.py:473
  86.0 8.9 %collective-permute-start.25 = (bf16[128,768]{1,0:T(8,128)(2,1)S(1)}, bf16[128,768]{1,0:T(8,128)(2,1)S(1)}, u32[]{:S(2)}, u32[]{:S(2)}) collective-permute-start(bf16[128,768]{1,0:T(8,128)(2,1)S(1)} %collective-permute-done.23.refs_2_), channel_id=1, source_target_pairs={{0,8},{1,9},{2,10},{3,11},{4,12},{5,13},{6,14},{7,15},{8,0},{9,1},... | collective-permute-start | bytes 589832 | tf_op jit(solution)/shard_map/ppermute | solution.py:473
  90.0 9.0 %collective-permute-start.28 = (bf16[288,256]{1,0:T(8,128)(2,1)S(1)}, bf16[288,256]{1,0:T(8,128)(2,1)S(1)}, u32[]{:S(2)}, u32[]{:S(2)}) collective-permute-start(bf16[288,256]{1,0:T(8,128)(2,1)S(1)} %get-tuple-element.75), channel_id=1, source_target_pairs={{0,1},{1,0},{2,3},{3,2},{4,5},{5,4},{6,7},{7,6},{8,9},{9,8},{10,11... | collective-permute-start | bytes 442376 | tf_op jit(solution)/shard_map/ppermute | solution.py:473
  94.6 5.9 %collective-permute-start.20 = (bf16[128,768]{1,0:T(8,128)(2,1)S(1)}, bf16[128,768]{1,0:T(8,128)(2,1)S(1)}, u32[]{:S(2)}, u32[]{:S(2)}) collective-permute-start(bf16[128,768]{1,0:T(8,128)(2,1)S(1)} %act.7.refs_7_.refs_1_), channel_id=1, source_target_pairs={{0,16},{1,17},{2,18},{3,19},{4,20},{5,21},{6,22},{7,23},{8,24},{9,... | collective-permute-start | bytes 589832 | tf_op jit(solution)/shard_map/ppermute | solution.py:473
  98.4 5.2 %collective-permute-start.30 = (bf16[288,256]{1,0:T(8,128)(2,1)S(1)}, bf16[288,256]{1,0:T(8,128)(2,1)S(1)}, u32[]{:S(2)}, u32[]{:S(2)}) collective-permute-start(bf16[288,256]{1,0:T(8,128)(2,1)S(1)} %get-tuple-element.76), channel_id=1, source_target_pairs={{0,1},{1,0},{2,3},{3,2},{4,5},{5,4},{6,7},{7,6},{8,9},{9,8},{10,11... | collective-permute-start | bytes 442376 | tf_op jit(solution)/shard_map/ppermute | solution.py:473
  99.1 16.8 %collective-permute-start.29 = (bf16[288,256]{1,0:T(8,128)(2,1)S(1)}, bf16[288,256]{1,0:T(8,128)(2,1)S(1)}, u32[]{:S(2)}, u32[]{:S(2)}) collective-permute-start(bf16[288,256]{1,0:T(8,128)(2,1)S(1)} %add_convert_fusion.1), channel_id=1, source_target_pairs={{0,4},{1,5},{2,6},{3,7},{4,0},{5,1},{6,2},{7,3},{8,12},{9,13},{10,... | collective-permute-start | bytes 442376 | tf_op jit(solution)/shard_map/ppermute | solution.py:473
  99.1 5.2 %collective-permute-start.21 = (bf16[128,768]{1,0:T(8,128)(2,1)S(1)}, bf16[128,768]{1,0:T(8,128)(2,1)S(1)}, u32[]{:S(2)}, u32[]{:S(2)}) collective-permute-start(bf16[128,768]{1,0:T(8,128)(2,1)S(1)} %act.7.refs_7_.refs_1_), channel_id=1, source_target_pairs={{0,8},{1,9},{2,10},{3,11},{4,12},{5,13},{6,14},{7,15},{8,0},{9,1},... | collective-permute-start | bytes 589832 | tf_op jit(solution)/shard_map/ppermute | solution.py:473
  100.4 3.9 %collective-permute-start.22 = (bf16[128,768]{1,0:T(8,128)(2,1)S(1)}, bf16[128,768]{1,0:T(8,128)(2,1)S(1)}, u32[]{:S(2)}, u32[]{:S(2)}) collective-permute-start(bf16[128,768]{1,0:T(8,128)(2,1)S(1)} %collective-permute-done.20.refs_2_), channel_id=1, source_target_pairs={{0,8},{1,9},{2,10},{3,11},{4,12},{5,13},{6,14},{7,15},{8,0},{9,1},... | collective-permute-start | bytes 589832 | tf_op jit(solution)/shard_map/ppermute | solution.py:473
  103.6 4.9 %copy-start.11 = (f32[4,288]{1,0:T(4,128)S(1)}, f32[4,288]{1,0:T(4,128)}, u32[]{:S(2)}) copy-start(f32[4,288]{1,0:T(4,128)} %get-tuple-element.54) | copy-start | bytes 13828
  103.7 29.3 %copy-start.9 = (f32[2304]{0:T(1024)S(1)}, f32[2304]{0:T(1024)}, u32[]{:S(2)}) copy-start(f32[2304]{0:T(1024)} %param.19) | copy-start | bytes 27652
  103.7 29.4 %copy-start.10 = (f32[16]{0:T(128)S(1)}, f32[16]{0:T(128)}, u32[]{:S(2)}) copy-start(f32[16]{0:T(128)} %param.21) | copy-start | bytes 196
  103.7 12.1 %collective-permute-start.31 = (bf16[288,256]{1,0:T(8,128)(2,1)S(1)}, bf16[288,256]{1,0:T(8,128)(2,1)S(1)}, u32[]{:S(2)}, u32[]{:S(2)}) collective-permute-start(bf16[288,256]{1,0:T(8,128)(2,1)S(1)} %add_convert_fusion), channel_id=1, source_target_pairs={{0,6},{1,7},{2,0},{3,1},{4,2},{5,3},{6,4},{7,5},{8,14},{9,15},{10,... | collective-permute-start | bytes 442376 | tf_op jit(solution)/shard_map/ppermute | solution.py:473
  104.4 32.2 %copy-start.1 = (bf16[2304,512]{1,0:T(8,128)(2,1)S(1)}, bf16[2304,512]{1,0:T(8,128)(2,1)}, u32[]{:S(2)}) copy-start(bf16[2304,512]{1,0:T(8,128)(2,1)} %refs_2_.1) | copy-start | bytes 7077892
  107.9 18.4 %collective-permute-start.32 = (bf16[288,256]{1,0:T(8,128)(2,1)S(1)}, bf16[288,256]{1,0:T(8,128)(2,1)S(1)}, u32[]{:S(2)}, u32[]{:S(2)}) collective-permute-start(bf16[288,256]{1,0:T(8,128)(2,1)S(1)} %get-tuple-element.73.refs_3_), channel_id=1, source_target_pairs={{0,1},{1,0},{2,3},{3,2},{4,5},{5,4},{6,7},{7,6},{8,9},{9,8},{10,11... | collective-permute-start | bytes 442376 | tf_op jit(solution)/shard_map/ppermute | solution.py:473
  108.5 7.3 %collective-permute-start.8 = (f32[4,288]{1,0:T(4,128)S(1)}, f32[4,288]{1,0:T(4,128)S(1)}, u32[]{:S(2)}, u32[]{:S(2)}) collective-permute-start(f32[4,288]{1,0:T(4,128)S(1)} %copy-done.11), channel_id=1, source_target_pairs={{0,0},{1,1},{2,8},{3,9},{4,16},{5,17},{6,24},{7,25},{8,2},{9,3},{1... | collective-permute-start | bytes 13832 | tf_op jit(solution)/shard_map/ppermute | solution.py:473
  116.5 54.7 %copy-start.7 = (f32[256,288]{0,1:T(8,128)S(1)}, f32[256,288]{0,1:T(8,128)}, u32[]{:S(2)}) copy-start(f32[256,288]{0,1:T(8,128)} %param.11) | copy-start | bytes 884740
  126.3 0.7 copy-start.8
  127.6 9.0 %all-to-all-start.1 = ((f32[4,32,288]{2,1,0:T(8,128)}), f32[4,32,288]{2,1,0:T(8,128)S(1)}, u32[]{:S(2)}, u32[]{:S(2)}) async-start(f32[4,32,288]{2,1,0:T(8,128)} %end_rows_whole.1), calls=%async_computation.1 | async-start | bytes 393216 | tf_op jit(solution)/shard_map/all_to_all | solution.py:567
  146.9 7.8 %all-to-all-start.3 = ((f32[4,2,16]{2,1,0:T(2,128)}), f32[4,2,16]{2,1,0:T(2,128)S(1)}, u32[]{:S(2)}, u32[]{:S(2)}) async-start(f32[4,2,16]{2,1,0:T(2,128)} %pairs.1), calls=%async_computation.3 | async-start | bytes 8192 | tf_op jit(solution)/shard_map/all_to_all | solution.py:567
  152.8 18.4 %collective-permute-start.33 = (f32[288,256]{1,0:T(8,128)S(1)}, f32[288,256]{1,0:T(8,128)S(1)}, u32[]{:S(2)}, u32[]{:S(2)}) collective-permute-start(f32[288,256]{1,0:T(8,128)S(1)} %convert_add_fusion), channel_id=1, source_target_pairs={{0,0},{1,1},{2,8},{3,9},{4,16},{5,17},{6,24},{7,25},{8,2},{9,3},{1... | collective-permute-start | bytes 884744 | tf_op jit(solution)/shard_map/ppermute | solution.py:473

commit v12 on v9

--- a/solution.py
+++ b/solution.py
@@ -28,7 +28,7 @@
 
 
 def hint(flops, bytes_accessed, scale=0.3):
-    return pl.CostEstimate(flops=int(flops * scale), bytes_accessed=int(bytes_accessed * scale), transcendentals=0)
+    return pl.CostEstimate(int(flops * scale), 0, int(bytes_accessed * scale))
 
 
 def shape(dims, dtype):
@@ -78,7 +78,7 @@
         in_specs=[SMEM] + [whole_spec(v) for v in (x, gain, routes)],
         out_specs=[whole_spec(v) for v in outs],
         out_shape=outs,
-        compiler_params=params(),
+        compiler_params=params(60),
         cost_estimate=hint(4 * tokens * block, 6 * tokens * block),
         name="prep",
     )(tallies, x, gain, routes)
@@ -201,7 +201,7 @@
         ],
         compiler_params=params(20),
         cost_estimate=hint(
-            4 * experts * depth * hidden * tokens, 4 * experts * depth * hidden + 6 * tokens * wide, 4.0
+            4 * experts * depth * hidden * tokens, 4 * experts * depth * hidden + 6 * tokens * wide, 4
         ),
         name="gate_up_partial",
     )(scal, *feeds, wr, wg, wu, *deps)
@@ -318,39 +318,37 @@
         ],
         compiler_params=params(20),
         cost_estimate=hint(
-            2 * experts * width * hidden * tokens, 2 * experts * width * hidden + 2 * width * tokens, 4.0
+            2 * experts * width * hidden * tokens, 2 * experts * width * hidden + 2 * width * tokens, 4
         ),
         name="down",
     )(scal, *pieces, cols, wd, *deps)
 
 
-def total_kernel(meta, stream, *refs):
+def total_kernel(cols, stream, *refs):
     parts, (total, message) = refs[:-2], refs[-2:]
     v = parts[0][...].astype(f32)
     for ref in parts[1:]:
         v = v + ref[...].astype(f32)
     total[...] = v
-    reqs = stream.shape[0]
-    ends = columns_at(meta[5:6].astype(f32), v)
-    ends = stream[...] + branch_scale * ends[0:reqs]
+    ends = columns_at(cols[...].astype(f32).T[5:6], v)[0 : stream.shape[0]]
+    ends = stream[...] + branch_scale * ends
     message[...] = jnp.broadcast_to(ends[None], message.shape)
 
 
-def total_call(feed, stream, parts, block, count):
-    tokens = feed.shape[1]
-    full = lambda v: pl.BlockSpec(v.shape, lambda n: (0,) * len(v.shape))
-    outs = [shape((block, tokens), f32), shape((count, *stream.shape), f32)]
+def total_call(cols, stream, parts, count):
+    reqs, block = stream.shape
+    tokens = cols.shape[0]
+    outs = [shape((block, tokens), f32), shape((count, reqs, block), f32)]
     return pl.pallas_call(
         total_kernel,
         grid=(1,),
-        in_specs=[pl.BlockSpec((META, tokens), lambda n: (block // META, 0)), full(stream)]
-        + [full(v) for v in parts],
-        out_specs=[full(v) for v in outs],
+        in_specs=[whole_spec(v) for v in (cols, stream, *parts)],
+        out_specs=[whole_spec(v) for v in outs],
         out_shape=outs,
         compiler_params=params(),
         cost_estimate=hint(16 * block * tokens, 14 * block * tokens),
         name="branch_total",
-    )(feed, stream, *parts)
+    )(cols, stream, *parts)
 
 
 def head_kernel(order, got, gain, words, softness, logits, message, wide):
@@ -358,7 +356,7 @@
     rows, columns = logits.shape
     ends, squares = [], 0.0
     for b in range(blocks):
-        v = jnp.concatenate([got[i] for i in order[b]], axis=0)
+        v = jnp.concatenate([got[at] for at in order[b]], axis=0)
         squares = squares + jnp.sum(v * v, axis=1, keepdims=True)
         ends.append(v)
     scale = lax.rsqrt(squares / WIDTH + epsilon)
@@ -406,7 +404,6 @@
 ):
     tokens, block = skip_stream_arriving.shape
     dp, mp = lax.axis_size("dp"), lax.axis_size("mp")
-    count = dp * mp
     parts = 4
     spread, sides = dp // parts, mp // parts
     assert dp == parts * spread and mp == parts * sides and sides & (sides - 1) == 0
@@ -450,10 +447,12 @@
     first = [send(sent, lambda q, z, x, i=i: (z, (q - 1) % parts, x ^ i)) for i in range(sides)]
     pair = join_call(first)
     feeds = {1: pair}
-    for group in (2, 3, 0):
-        feeds[group] = send(feeds[(group - 1) % parts], lambda q, z, x: (q, (z - 1) % parts, x))
+    step = lambda v: send(v, lambda q, z, x: (q, (z - 1) % parts, x))
     stream = send(stream, home)
     partial, kept, pieces, shares = {}, {}, {}, {}
+
+    def after(v, dep):
+        return lax.optimization_barrier((v, dep))[0]
 
     def do_partial(s, *deps):
         own, give, cols = partial_call(scal, sides, [feeds[g] for g in chunks[s]], wr, wg, wu, deps)
@@ -468,9 +467,13 @@
 
     def do_act(s, *deps):
         a = act_call(scal, base, *kept[s], partial[s][2], deps)
-        a_y = send(a, other_y)
-        pieces[s] = (a, a_y, send(a, other_core), send(a_y, other_core))
+        pieces[s] = (a, send(a, other_y))
         return a
+
+    def do_hop(s, dep):
+        a, a_y = pieces[s]
+        late = [v if dep is None else after(v, dep) for v in (a, a_y)]
+        pieces[s] = (a, a_y, *[send(v, other_core) for v in late])
 
     def do_down(s, *deps):
         outs = down_call(scal, sides, pieces[s], partial[s][2], wd, deps)
@@ -485,34 +488,36 @@
                 shares[group] = [send(share, back)]
         return outs[0]
 
+    feeds[2] = step(feeds[1])
+    feeds[3] = step(feeds[2])
     p0 = do_partial(0)
     p1 = do_partial(1, p0)
     s0 = do_sum(0, p1)
     p2 = do_partial(2, s0)
+    feeds[0] = step(after(feeds[3], p2))
     s1 = do_sum(1, p2)
     a0 = do_act(0, s1)
     p3 = do_partial(3, a0)
     s2 = do_sum(2, p3)
+    do_hop(0, s2)
     a1 = do_act(1, s2)
     d0 = do_down(0, a1)
     s3 = do_sum(3, d0)
+    do_hop(1, s3)
     a2 = do_act(2, s3)
     d1 = do_down(1, a2)
+    do_hop(2, None)
     a3 = do_act(3, d1)
     d2 = do_down(2, a3)
+    do_hop(3, None)
     d3 = do_down(3, d2)
-    mine = [v for group in range(parts) for v in shares[group]]
-    total, message = total_call(feeds[0], stream, mine, block, count)
-
-    everyone = lambda v: lax.all_to_all(v, ("dp", "mp"), 0, 0, tiled=True)
-    got = everyone(message)
+    terms = [v for group in range(parts) for v in shares[group]]
+    total, message = total_call(partial[parts - 1][2], stream, terms, dp * mp)
+    exchange = lambda v: lax.all_to_all(v, ("dp", "mp"), 0, 0, tiled=True)
+    got = exchange(message)
     branch = send(total, home)
     order = [
-        [
-            (q * spread + r) * mp + z * sides + x
-            for z in range(parts)
-            for r in range(spread)
-        ]
+        [(q * spread + r) * mp + group * sides + x for group in range(parts) for r in range(spread)]
         for q in range(parts)
         for x in range(sides)
     ]
@@ -523,7 +528,7 @@
         lexicon_projector_weights,
         softness_per_sequence[:, None],
     )
-    pairs = everyone(pairs)
+    pairs = exchange(pairs)
     new_hidden = skip_stream_arriving + branch_scale * branch.T
     largest = jnp.max(pairs[:, 0], axis=0)
     mass = jnp.sum(pairs[:, 1] * jnp.exp(pairs[:, 0] - largest), axis=0)

time: 166 us -> 160 us (0.964)
  waiting for transfers between devices: 70.2 us -> 65.7 us
  local copies, waits for them, and re-layouts: 7.3 us -> 5.58 us
    ppermute x34, waiting for transfers between devices: 60.9 us -> 56.4 us  [send(): return lax.ppermute(value, ('dp', 'mp'), pairs)]
    unnamed x26 -> x22, local copies, waits for them, and re-layouts: 6.34 us -> 4.05 us
  transfers between devices with their start and end apart: 36 -> 36, of which waited for: 13 -> 14; matrix products, arithmetic and copies ran while one was open for 1% -> 1% of each run, Pallas kernels for 25% -> 26%
where the time goes in v12:
time: 160 us; the launch traced here: 159 us
  waiting for transfers between devices  65.7 us (41%)
  Pallas kernels  46.1 us (29%)
  starting transfers between devices  39.4 us (25%)
  local copies, waits for them, and re-layouts  5.58 us (3%)
  other arithmetic  1.71 us (1%)
    ppermute x34, waiting for transfers between devices, send(): return lax.ppermute(value, ('dp', 'mp'), pairs)  56.4 us
    ppermute x34, starting transfers between devices, send(): return lax.ppermute(value, ('dp', 'mp'), pairs)  32.9 us
    pallas_call x4, Pallas kernels, partial_call(): pl.pallas_call(lambda *refs: partial_kernel(sides, len(feeds), *refs), gr...  19.4 us
    pallas_call x4, Pallas kernels, down_call(): pl.pallas_call(lambda *refs: down_kernel(sides, *refs), grid=(experts,),...  13.8 us
    all_to_all x2, waiting for transfers between devices, body(): exchange = lambda v: lax.all_to_all(v, ('dp', 'mp'), 0, 0, tiled=True)  9.27 us
    all_to_all x2, starting transfers between devices, body(): exchange = lambda v: lax.all_to_all(v, ('dp', 'mp'), 0, 0, tiled=True)  6.53 us
    pallas_call x4, Pallas kernels, act_call(): pl.pallas_call(lambda *refs: act_kernel(base, *refs), in_specs=[SMEM] + [...  4.95 us
    unnamed x22, local copies, waits for them, and re-layouts  4.05 us
  transfers between devices with their start and end apart: 36, of which 14 were waited for; matrix products, arithmetic and copies ran while one was open for 1% of the time, Pallas kernels for 26%

profile of v12, /device:TPU:4, one launch (start us, length us, event | category | flops | bytes accessed | tf_op | source)
XLA Modules:
  0.0 159.5 jit_solution(12842991397379916183)
XLA Ops:
  0.6 1.3 broadcast_in_dim.4.gain
  1.9 1.9 %prep.1 = (bf16[304,256]{1,0:T(8,128)(2,1)}, f32[4,288]{1,0:T(4,128)}) custom-call(s32[1,4]{1,0:T(1,128)} %tallies.1, f32[288,256]{1,0:T(8,128)} %bitcast.19, f32[1,288]{1,0:T(1,128)} %broadcast_in_dim.4.gain, s32[2,256]{1,0:T(2,128)} %bitcast.23), custom_call_target="tpu_custom_call" | custom-call | flops 88473 | bytes 132710 | tf_op jit(solution)/shard_map/prep/pallas_call | solution.py:75
  3.8 1.5 collective-permute-start
  5.3 3.0 %collective-permute-start.1 = (bf16[304,256]{1,0:T(8,128)(2,1)}, bf16[304,256]{1,0:T(8,128)(2,1)S(1)}, u32[]{:S(2)}, u32[]{:S(2)}) collective-permute-start(bf16[304,256]{1,0:T(8,128)(2,1)} %get-tuple-element.41), channel_id=1, source_target_pairs={{0,7},{1,6},{2,15},{3,14},{4,23},{5,22},{6,31},{7,30},{8,1},{9,0},... | collective-permute-start | bytes 466952 | tf_op jit(solution)/shard_map/ppermute | solution.py:423
  8.5 3.8 %collective-permute-done.refs_0_ = bf16[304,256]{1,0:T(8,128)(2,1)S(1)} collective-permute-done((bf16[304,256]{1,0:T(8,128)(2,1)}, bf16[304,256]{1,0:T(8,128)(2,1)S(1)}, u32[]{:S(2)}, u32[]{:S(2)}) %collective-permute-start) | collective-permute-done | bytes 155680 | tf_op jit(solution)/shard_map/ppermute | solution.py:423
  12.3 4.3 %collective-permute-done.1.refs_1_ = bf16[304,256]{1,0:T(8,128)(2,1)S(1)} collective-permute-done((bf16[304,256]{1,0:T(8,128)(2,1)}, bf16[304,256]{1,0:T(8,128)(2,1)S(1)}, u32[]{:S(2)}, u32[]{:S(2)}) %collective-permute-start.1) | collective-permute-done | bytes 155680 | tf_op jit(solution)/shard_map/ppermute | solution.py:423
  16.5 5.9 %collective-permute-start.2 = (bf16[608,256]{1,0:T(8,128)(2,1)S(1)}, bf16[608,256]{1,0:T(8,128)(2,1)S(1)}, u32[]{:S(2)}, u32[]{:S(2)}) collective-permute-start(bf16[608,256]{1,0:T(8,128)(2,1)S(1)} %join.1.refs_1_), channel_id=1, source_target_pairs={{0,6},{1,7},{2,0},{3,1},{4,2},{5,3},{6,4},{7,5},{8,14},{9,15},{10,... | collective-permute-start | bytes 933896 | tf_op jit(solution)/shard_map/ppermute | solution.py:423
  22.5 2.0 %copy-done.2 = bf16[4,576,720]{2,1,0:T(8,128)(2,1)S(1)} copy-done((bf16[4,576,720]{2,1,0:T(8,128)(2,1)S(1)}, bf16[4,576,720]{2,1,0:T(8,128)(2,1)}, u32[]{:S(2)}) %copy-start.2) | copy-done | bytes 3317784
  24.5 2.0 %copy-done.4 = bf16[4,576,720]{2,1,0:T(8,128)(2,1)S(1)} copy-done((bf16[4,576,720]{2,1,0:T(8,128)(2,1)S(1)}, bf16[4,576,720]{2,1,0:T(8,128)(2,1)}, u32[]{:S(2)}) %copy-start.4) | copy-done | bytes 3317784
  26.5 4.9 %gate_up_partial.4 = (f32[256,1536]{1,0:T(8,128)S(1)}, bf16[256,1536]{1,0:T(8,128)(2,1)S(1)}, bf16[256,128]{1,0:T(8,128)(2,1)S(1)}) custom-call(s32[3]{0:T(128)S(1)} %pad_add_fusion.1.refs_0_, bf16[608,256]{1,0:T(8,128)(2,1)S(1)} %join.1.refs_1_, bf16[128,576]{1,0:T(8,128)(2,1)S(1)} %pad_add_fusion.refs_2_, bf16[4,576,720]{2,1,0:T(8,128)(2,1)S(1)} %copy-done.2, ...), custom_call_target="tpu_custom_call" | custom-call | flops 6794772480 | bytes 35979264 | tf_op jit(solution)/shard_map/gate_up_partial/pallas_call | solution.py:190
  31.6 4.9 %gate_up_partial.5 = (f32[256,1536]{1,0:T(8,128)S(1)}, bf16[256,1536]{1,0:T(8,128)(2,1)S(1)}, bf16[256,128]{1,0:T(8,128)(2,1)S(1)}) custom-call(s32[3]{0:T(128)S(1)} %pad_add_fusion.1.refs_0_, bf16[608,256]{1,0:T(8,128)(2,1)S(1)} %collective-permute-done.2.refs_1_, bf16[128,576]{1,0:T(8,128)(2,1)S(1)} %pad_add_fusion.refs_2_, ...), custom_call_target="tpu_custom_call" | custom-call | flops 6794772480 | bytes 35979264 | tf_op jit(solution)/shard_map/gate_up_partial/pallas_call | solution.py:190
  36.9 0.9 core_sum.4
  37.9 3.4 %collective-permute-done.3.refs_1_ = bf16[608,256]{1,0:T(8,128)(2,1)S(1)} collective-permute-done((bf16[608,256]{1,0:T(8,128)(2,1)S(1)}, bf16[608,256]{1,0:T(8,128)(2,1)S(1)}, u32[]{:S(2)}, u32[]{:S(2)}) %collective-permute-start.3) | collective-permute-done | bytes 311328 | tf_op jit(solution)/shard_map/ppermute | solution.py:423
  41.3 4.8 %gate_up_partial.6 = (f32[256,1536]{1,0:T(8,128)S(1)}, bf16[256,1536]{1,0:T(8,128)(2,1)S(1)}, bf16[256,128]{1,0:T(8,128)(2,1)S(1)}) custom-call(s32[3]{0:T(128)S(1)} %pad_add_fusion.1.refs_0_, bf16[608,256]{1,0:T(8,128)(2,1)S(1)} %collective-permute-done.3.refs_1_, bf16[128,576]{1,0:T(8,128)(2,1)S(1)} %pad_add_fusion.refs_2_, ...), custom_call_target="tpu_custom_call" | custom-call | flops 6794772480 | bytes 35979264 | tf_op jit(solution)/shard_map/gate_up_partial/pallas_call | solution.py:190
  46.1 2.1 %collective-permute-start.5 = (bf16[608,256]{1,0:T(8,128)(2,1)S(1)}, bf16[608,256]{1,0:T(8,128)(2,1)S(1)}, u32[]{:S(2)}, u32[]{:S(2)}) collective-permute-start(bf16[608,256]{1,0:T(8,128)(2,1)S(1)} %collective-permute-done.3.refs_1_), channel_id=1, source_target_pairs={{0,6},{1,7},{2,0},{3,1},{4,2},{5,3},{6,4},{7,5},{8,14},{9,15},{10,... | collective-permute-start | bytes 933896 | tf_op jit(solution)/shard_map/ppermute | solution.py:423
  48.2 0.9 core_sum.5
  49.2 1.2 act.4.refs_5_.refs_1_
  50.4 2.1 %collective-permute-start.10 = (bf16[128,768]{1,0:T(8,128)(2,1)S(1)}, bf16[128,768]{1,0:T(8,128)(2,1)S(1)}, u32[]{:S(2)}, u32[]{:S(2)}) collective-permute-start(bf16[128,768]{1,0:T(8,128)(2,1)S(1)} %act.4.refs_5_.refs_1_), channel_id=1, source_target_pairs={{0,16},{1,17},{2,18},{3,19},{4,20},{5,21},{6,22},{7,23},{8,24},{9,... | collective-permute-start | bytes 589832 | tf_op jit(solution)/shard_map/ppermute | solution.py:423
  52.5 2.6 %collective-permute-done.5.refs_1_ = bf16[608,256]{1,0:T(8,128)(2,1)S(1)} collective-permute-done((bf16[608,256]{1,0:T(8,128)(2,1)S(1)}, bf16[608,256]{1,0:T(8,128)(2,1)S(1)}, u32[]{:S(2)}, u32[]{:S(2)}) %collective-permute-start.5) | collective-permute-done | bytes 311328 | tf_op jit(solution)/shard_map/ppermute | solution.py:423
  55.1 4.8 %gate_up_partial.7 = (f32[256,1536]{1,0:T(8,128)S(1)}, bf16[256,1536]{1,0:T(8,128)(2,1)S(1)}, bf16[256,128]{1,0:T(8,128)(2,1)S(1)}) custom-call(s32[3]{0:T(128)S(1)} %pad_add_fusion.1.refs_0_, bf16[608,256]{1,0:T(8,128)(2,1)S(1)} %collective-permute-done.5.refs_1_, bf16[128,576]{1,0:T(8,128)(2,1)S(1)} %pad_add_fusion.refs_2_, ...), custom_call_target="tpu_custom_call" | custom-call | flops 6794772480 | bytes 35979264 | tf_op jit(solution)/shard_map/gate_up_partial/pallas_call | solution.py:190
  60.0 0.9 core_sum.6
  61.4 3.5 %collective-permute-done.10.refs_2_ = bf16[128,768]{1,0:T(8,128)(2,1)S(1)} collective-permute-done((bf16[128,768]{1,0:T(8,128)(2,1)S(1)}, bf16[128,768]{1,0:T(8,128)(2,1)S(1)}, u32[]{:S(2)}, u32[]{:S(2)}) %collective-permute-start.10) | collective-permute-done | bytes 196640 | tf_op jit(solution)/shard_map/ppermute | solution.py:423
  64.9 1.2 act.5.refs_7_.refs_1_
  66.5 1.7 %collective-permute-start.19 = (bf16[128,1536]{1,0:T(8,128)(2,1)S(1)}, bf16[128,1536]{1,0:T(8,128)(2,1)S(1)}, u32[]{:S(2)}, u32[]{:S(2)}) collective-permute-start(bf16[128,1536]{1,0:T(8,128)(2,1)S(1)} %get-tuple-element.67), channel_id=1, source_target_pairs={{0,16},{1,17},{2,18},{3,19},{4,20},{5,21},{6,22},{7,23},{8,24},{9,... | collective-permute-start | bytes 1179656 | tf_op jit(solution)/shard_map/ppermute | solution.py:423
  68.3 3.5 %down.4 = (bf16[288,256]{1,0:T(8,128)(2,1)S(1)}, bf16[288,256]{1,0:T(8,128)(2,1)S(1)}) custom-call(s32[3]{0:T(128)S(1)} %pad_add_fusion.1.refs_0_, bf16[128,768]{1,0:T(8,128)(2,1)S(1)} %act.4.refs_5_.refs_1_, bf16[128,768]{1,0:T(8,128)(2,1)S(1)} %collective-permute-done.10.refs_2_, bf16[128,768]{1,0:T(8,128)(2,1)S(1)} %collective-permute-done.12.refs_3_, ...), custom_call_target="tpu_custom_call" | custom-call | flops 3397386240 | bytes 14450688 | tf_op jit(solution)/shard_map/down/pallas_call | solution.py:306
  72.4 0.9 core_sum.7
  74.1 8.2 %collective-permute-done.19.refs_2_ = bf16[128,1536]{1,0:T(8,128)(2,1)S(1)} collective-permute-done((bf16[128,1536]{1,0:T(8,128)(2,1)S(1)}, bf16[128,1536]{1,0:T(8,128)(2,1)S(1)}, u32[]{:S(2)}, u32[]{:S(2)}) %collective-permute-start.19) | collective-permute-done | bytes 393248 | tf_op jit(solution)/shard_map/ppermute | solution.py:423
  82.3 1.2 act.6.refs_7_.refs_1_
  84.3 10.3 %collective-permute-done.23.refs_2_ = bf16[128,768]{1,0:T(8,128)(2,1)S(1)} collective-permute-done((bf16[128,768]{1,0:T(8,128)(2,1)S(1)}, bf16[128,768]{1,0:T(8,128)(2,1)S(1)}, u32[]{:S(2)}, u32[]{:S(2)}) %collective-permute-start.23) | collective-permute-done | bytes 196640 | tf_op jit(solution)/shard_map/ppermute | solution.py:423
  94.6 3.5 %down.5 = (bf16[288,256]{1,0:T(8,128)(2,1)S(1)}, bf16[288,256]{1,0:T(8,128)(2,1)S(1)}) custom-call(s32[3]{0:T(128)S(1)} %pad_add_fusion.1.refs_0_, bf16[128,768]{1,0:T(8,128)(2,1)S(1)} %act.5.refs_7_.refs_1_, bf16[128,768]{1,0:T(8,128)(2,1)S(1)} %collective-permute-done.16.refs_2_, bf16[128,768]{1,0:T(8,128)(2,1)S(1)} %collective-permute-done.17.refs_3_, ...), custom_call_target="tpu_custom_call" | custom-call | flops 3397386240 | bytes 14450688 | tf_op jit(solution)/shard_map/down/pallas_call | solution.py:306
  98.7 1.2 act.7.refs_7_.refs_1_
  100.3 3.5 %down.6 = (bf16[288,256]{1,0:T(8,128)(2,1)S(1)}, bf16[288,256]{1,0:T(8,128)(2,1)S(1)}) custom-call(s32[3]{0:T(128)S(1)} %pad_add_fusion.1.refs_0_, bf16[128,768]{1,0:T(8,128)(2,1)S(1)} %act.6.refs_7_.refs_1_, bf16[128,768]{1,0:T(8,128)(2,1)S(1)} %collective-permute-done.23.refs_2_, bf16[128,768]{1,0:T(8,128)(2,1)S(1)} %collective-permute-done.24.refs_3_, ...), custom_call_target="tpu_custom_call" | custom-call | flops 3397386240 | bytes 14450688 | tf_op jit(solution)/shard_map/down/pallas_call | solution.py:306
  103.8 1.5 collective-permute-start.31
  105.5 1.6 collective-permute-done.20.refs_2_
  107.0 2.5 %collective-permute-done.31 = bf16[288,256]{1,0:T(8,128)(2,1)S(1)} collective-permute-done((bf16[288,256]{1,0:T(8,128)(2,1)S(1)}, bf16[288,256]{1,0:T(8,128)(2,1)S(1)}, u32[]{:S(2)}, u32[]{:S(2)}) %collective-permute-start.31) | collective-permute-done | bytes 147488 | tf_op jit(solution)/shard_map/ppermute | solution.py:423
  110.3 3.5 %down.7 = (bf16[288,256]{1,0:T(8,128)(2,1)S(1)}, bf16[288,256]{1,0:T(8,128)(2,1)S(1)}) custom-call(s32[3]{0:T(128)S(1)} %pad_add_fusion.1.refs_0_, bf16[128,768]{1,0:T(8,128)(2,1)S(1)} %act.7.refs_7_.refs_1_, bf16[128,768]{1,0:T(8,128)(2,1)S(1)} %collective-permute-done.20.refs_2_, bf16[128,768]{1,0:T(8,128)(2,1)S(1)} %collective-permute-done.21.refs_3_, ...), custom_call_target="tpu_custom_call" | custom-call | flops 3397386240 | bytes 14450688 | tf_op jit(solution)/shard_map/down/pallas_call | solution.py:306
  113.8 1.5 collective-permute-start.26
  115.3 3.8 %collective-permute-start.8 = (f32[4,288]{1,0:T(4,128)S(1)}, f32[4,288]{1,0:T(4,128)S(1)}, u32[]{:S(2)}, u32[]{:S(2)}) collective-permute-start(f32[4,288]{1,0:T(4,128)S(1)} %copy-done.10), channel_id=1, source_target_pairs={{0,0},{1,1},{2,8},{3,9},{4,16},{5,17},{6,24},{7,25},{8,2},{9,3},{1... | collective-permute-start | bytes 13832 | tf_op jit(solution)/shard_map/ppermute | solution.py:423
  119.2 3.5 %collective-permute-done.8.stream = f32[4,288]{1,0:T(4,128)S(1)} collective-permute-done((f32[4,288]{1,0:T(4,128)S(1)}, f32[4,288]{1,0:T(4,128)S(1)}, u32[]{:S(2)}, u32[]{:S(2)}) %collective-permute-start.8) | collective-permute-done | bytes 4640 | tf_op jit(solution)/shard_map/ppermute | solution.py:423
  122.7 1.1 branch_total.1
  123.7 2.6 %all-to-all-start = ((f32[32,4,288]{2,1,0:T(4,128)}), f32[32,4,288]{2,1,0:T(4,128)S(1)}, u32[]{:S(2)}, u32[]{:S(2)}) async-start(f32[32,4,288]{2,1,0:T(4,128)} %get-tuple-element.77), calls=%async_computation | async-start | bytes 393216 | tf_op jit(solution)/shard_map/all_to_all | solution.py:516
  126.5 7.5 %all-to-all-done.refs_0_ = f32[32,4,288]{2,1,0:T(4,128)S(1)} async-done(((f32[32,4,288]{2,1,0:T(4,128)}), f32[32,4,288]{2,1,0:T(4,128)S(1)}, u32[]{:S(2)}, u32[]{:S(2)}) %all-to-all-start) | async-done | bytes 147488 | tf_op jit(solution)/shard_map/all_to_all | solution.py:516
  134.0 1.4 head.1
  135.5 3.9 %all-to-all-start.1 = ((f32[32,2,16]{2,1,0:T(2,128)}), f32[32,2,16]{2,1,0:T(2,128)S(1)}, u32[]{:S(2)}, u32[]{:S(2)}) async-start(f32[32,2,16]{2,1,0:T(2,128)} %get-tuple-element.79), calls=%async_computation.1 | async-start | bytes 65536 | tf_op jit(solution)/shard_map/all_to_all | solution.py:516
  139.4 4.3 %collective-permute-start.33 = (f32[288,256]{1,0:T(8,128)S(1)}, f32[288,256]{1,0:T(8,128)S(1)}, u32[]{:S(2)}, u32[]{:S(2)}) collective-permute-start(f32[288,256]{1,0:T(8,128)S(1)} %get-tuple-element.76), channel_id=1, source_target_pairs={{0,0},{1,1},{2,8},{3,9},{4,16},{5,17},{6,24},{7,25},{8,2},{9,3},{1... | collective-permute-start | bytes 884744 | tf_op jit(solution)/shard_map/ppermute | solution.py:423
  143.7 1.8 %all-to-all-done.1 = f32[32,2,16]{2,1,0:T(2,128)S(1)} async-done(((f32[32,2,16]{2,1,0:T(2,128)}), f32[32,2,16]{2,1,0:T(2,128)S(1)}, u32[]{:S(2)}, u32[]{:S(2)}) %all-to-all-start.1) | async-done | bytes 4128 | tf_op jit(solution)/shard_map/all_to_all | solution.py:516
  146.2 12.5 %collective-permute-done.33 = f32[288,256]{1,0:T(8,128)S(1)} collective-permute-done((f32[288,256]{1,0:T(8,128)S(1)}, f32[288,256]{1,0:T(8,128)S(1)}, u32[]{:S(2)}, u32[]{:S(2)}) %collective-permute-start.33) | collective-permute-done | bytes 294944 | tf_op jit(solution)/shard_map/ppermute | solution.py:423
  158.7 0.8 bitcast_add_fusion
  (81 shorter events, 7.0 us)
Async XLA Ops:
  0.6 7.7 %copy-start = (bf16[2304,4]{0,1:T(4,128)(2,1)S(1)}, bf16[2304,4]{0,1:T(4,128)(2,1)}, u32[]{:S(2)}) copy-start(bf16[2304,4]{0,1:T(4,128)(2,1)} %param.15) | copy-start | bytes 55300
  3.8 8.4 %collective-permute-start = (bf16[304,256]{1,0:T(8,128)(2,1)}, bf16[304,256]{1,0:T(8,128)(2,1)S(1)}, u32[]{:S(2)}, u32[]{:S(2)}) collective-permute-start(bf16[304,256]{1,0:T(8,128)(2,1)} %get-tuple-element.41), channel_id=1, source_target_pairs={{0,6},{1,7},{2,14},{3,15},{4,22},{5,23},{6,30},{7,31},{8,0},{9,1},... | collective-permute-start | bytes 466952 | tf_op jit(solution)/shard_map/ppermute | solution.py:423
  5.3 11.2 %collective-permute-start.1 = (bf16[304,256]{1,0:T(8,128)(2,1)}, bf16[304,256]{1,0:T(8,128)(2,1)S(1)}, u32[]{:S(2)}, u32[]{:S(2)}) collective-permute-start(bf16[304,256]{1,0:T(8,128)(2,1)} %get-tuple-element.41), channel_id=1, source_target_pairs={{0,7},{1,6},{2,15},{3,14},{4,23},{5,22},{6,31},{7,30},{8,1},{9,0},... | collective-permute-start | bytes 466952 | tf_op jit(solution)/shard_map/ppermute | solution.py:423
  16.5 14.9 %collective-permute-start.2 = (bf16[608,256]{1,0:T(8,128)(2,1)S(1)}, bf16[608,256]{1,0:T(8,128)(2,1)S(1)}, u32[]{:S(2)}, u32[]{:S(2)}) collective-permute-start(bf16[608,256]{1,0:T(8,128)(2,1)S(1)} %join.1.refs_1_), channel_id=1, source_target_pairs={{0,6},{1,7},{2,0},{3,1},{4,2},{5,3},{6,4},{7,5},{8,14},{9,15},{10,... | collective-permute-start | bytes 933896 | tf_op jit(solution)/shard_map/ppermute | solution.py:423
  22.5 2.0 %copy-start.2 = (bf16[4,576,720]{2,1,0:T(8,128)(2,1)S(1)}, bf16[4,576,720]{2,1,0:T(8,128)(2,1)}, u32[]{:S(2)}) copy-start(bf16[4,576,720]{2,1,0:T(8,128)(2,1)} %refs_3_.7) | copy-start | bytes 9953284
  24.5 2.0 %copy-start.4 = (bf16[4,576,720]{2,1,0:T(8,128)(2,1)S(1)}, bf16[4,576,720]{2,1,0:T(8,128)(2,1)}, u32[]{:S(2)}) copy-start(bf16[4,576,720]{2,1,0:T(8,128)(2,1)} %refs_4_.7) | copy-start | bytes 9953284
  26.5 5.1 %copy-start.3 = (bf16[4,576,720]{2,1,0:T(8,128)(2,1)S(1)}, bf16[4,576,720]{2,1,0:T(8,128)(2,1)}, u32[]{:S(2)}) copy-start(bf16[4,576,720]{2,1,0:T(8,128)(2,1)} %refs_3_.7) | copy-start | bytes 9953284
  26.5 5.1 %copy-start.5 = (bf16[4,576,720]{2,1,0:T(8,128)(2,1)S(1)}, bf16[4,576,720]{2,1,0:T(8,128)(2,1)}, u32[]{:S(2)}) copy-start(bf16[4,576,720]{2,1,0:T(8,128)(2,1)} %refs_4_.7) | copy-start | bytes 9953284
  31.4 5.5 %collective-permute-start.4 = (bf16[256,1536]{1,0:T(8,128)(2,1)S(1)}, bf16[256,1536]{1,0:T(8,128)(2,1)S(1)}, u32[]{:S(2)}, u32[]{:S(2)}) collective-permute-start(bf16[256,1536]{1,0:T(8,128)(2,1)S(1)} %get-tuple-element.43), channel_id=1, source_target_pairs={{0,8},{1,9},{2,10},{3,11},{4,12},{5,13},{6,14},{7,15},{8,0},{9,1},... | collective-permute-start | bytes 2359304 | tf_op jit(solution)/shard_map/ppermute | solution.py:423
  31.5 9.8 %collective-permute-start.3 = (bf16[608,256]{1,0:T(8,128)(2,1)S(1)}, bf16[608,256]{1,0:T(8,128)(2,1)S(1)}, u32[]{:S(2)}, u32[]{:S(2)}) collective-permute-start(bf16[608,256]{1,0:T(8,128)(2,1)S(1)} %collective-permute-done.2.refs_1_), channel_id=1, source_target_pairs={{0,6},{1,7},{2,0},{3,1},{4,2},{5,3},{6,4},{7,5},{8,14},{9,15},{10,... | collective-permute-start | bytes 933896 | tf_op jit(solution)/shard_map/ppermute | solution.py:423
  36.4 11.8 %collective-permute-start.7 = (bf16[256,1536]{1,0:T(8,128)(2,1)S(1)}, bf16[256,1536]{1,0:T(8,128)(2,1)S(1)}, u32[]{:S(2)}, u32[]{:S(2)}) collective-permute-start(bf16[256,1536]{1,0:T(8,128)(2,1)S(1)} %get-tuple-element.50), channel_id=1, source_target_pairs={{0,8},{1,9},{2,10},{3,11},{4,12},{5,13},{6,14},{7,15},{8,0},{9,1},... | collective-permute-start | bytes 2359304 | tf_op jit(solution)/shard_map/ppermute | solution.py:423
  37.8 11.4 %collective-permute-start.6 = (bf16[128,1536]{1,0:T(8,128)(2,1)S(1)}, bf16[128,1536]{1,0:T(8,128)(2,1)S(1)}, u32[]{:S(2)}, u32[]{:S(2)}) collective-permute-start(bf16[128,1536]{1,0:T(8,128)(2,1)S(1)} %get-tuple-element.48), channel_id=1, source_target_pairs={{0,16},{1,17},{2,18},{3,19},{4,20},{5,21},{6,22},{7,23},{8,24},{9,... | collective-permute-start | bytes 1179656 | tf_op jit(solution)/shard_map/ppermute | solution.py:423
  46.1 9.0 %collective-permute-start.5 = (bf16[608,256]{1,0:T(8,128)(2,1)S(1)}, bf16[608,256]{1,0:T(8,128)(2,1)S(1)}, u32[]{:S(2)}, u32[]{:S(2)}) collective-permute-start(bf16[608,256]{1,0:T(8,128)(2,1)S(1)} %collective-permute-done.3.refs_1_), channel_id=1, source_target_pairs={{0,6},{1,7},{2,0},{3,1},{4,2},{5,3},{6,4},{7,5},{8,14},{9,15},{10,... | collective-permute-start | bytes 933896 | tf_op jit(solution)/shard_map/ppermute | solution.py:423
  48.2 11.8 %collective-permute-start.11 = (bf16[256,1536]{1,0:T(8,128)(2,1)S(1)}, bf16[256,1536]{1,0:T(8,128)(2,1)S(1)}, u32[]{:S(2)}, u32[]{:S(2)}) collective-permute-start(bf16[256,1536]{1,0:T(8,128)(2,1)S(1)} %get-tuple-element.56), channel_id=1, source_target_pairs={{0,8},{1,9},{2,10},{3,11},{4,12},{5,13},{6,14},{7,15},{8,0},{9,1},... | collective-permute-start | bytes 2359304 | tf_op jit(solution)/shard_map/ppermute | solution.py:423
  49.1 15.8 %collective-permute-start.14 = (bf16[128,1536]{1,0:T(8,128)(2,1)S(1)}, bf16[128,1536]{1,0:T(8,128)(2,1)S(1)}, u32[]{:S(2)}, u32[]{:S(2)}) collective-permute-start(bf16[128,1536]{1,0:T(8,128)(2,1)S(1)} %get-tuple-element.60), channel_id=1, source_target_pairs={{0,16},{1,17},{2,18},{3,19},{4,20},{5,21},{6,22},{7,23},{8,24},{9,... | collective-permute-start | bytes 1179656 | tf_op jit(solution)/shard_map/ppermute | solution.py:423
  50.4 14.5 %collective-permute-start.10 = (bf16[128,768]{1,0:T(8,128)(2,1)S(1)}, bf16[128,768]{1,0:T(8,128)(2,1)S(1)}, u32[]{:S(2)}, u32[]{:S(2)}) collective-permute-start(bf16[128,768]{1,0:T(8,128)(2,1)S(1)} %act.4.refs_5_.refs_1_), channel_id=1, source_target_pairs={{0,16},{1,17},{2,18},{3,19},{4,20},{5,21},{6,22},{7,23},{8,24},{9,... | collective-permute-start | bytes 589832 | tf_op jit(solution)/shard_map/ppermute | solution.py:423
  59.9 12.5 %collective-permute-start.9 = (bf16[256,1536]{1,0:T(8,128)(2,1)S(1)}, bf16[256,1536]{1,0:T(8,128)(2,1)S(1)}, u32[]{:S(2)}, u32[]{:S(2)}) collective-permute-start(bf16[256,1536]{1,0:T(8,128)(2,1)S(1)} %get-tuple-element.55), channel_id=1, source_target_pairs={{0,8},{1,9},{2,10},{3,11},{4,12},{5,13},{6,14},{7,15},{8,0},{9,1},... | collective-permute-start | bytes 2359304 | tf_op jit(solution)/shard_map/ppermute | solution.py:423
  60.0 8.3 %copy-start.6 = (bf16[4,720,576]{1,2,0:T(8,128)(2,1)S(1)}, bf16[4,720,576]{1,2,0:T(8,128)(2,1)}, u32[]{:S(2)}) copy-start(bf16[4,720,576]{1,2,0:T(8,128)(2,1)} %param.18) | copy-start | bytes 9953284
  60.9 7.4 %collective-permute-start.12 = (bf16[128,768]{1,0:T(8,128)(2,1)S(1)}, bf16[128,768]{1,0:T(8,128)(2,1)S(1)}, u32[]{:S(2)}, u32[]{:S(2)}) collective-permute-start(bf16[128,768]{1,0:T(8,128)(2,1)S(1)} %act.4.refs_5_.refs_1_), channel_id=1, source_target_pairs={{0,8},{1,9},{2,10},{3,11},{4,12},{5,13},{6,14},{7,15},{8,0},{9,1},... | collective-permute-start | bytes 589832 | tf_op jit(solution)/shard_map/ppermute | solution.py:423
  64.9 3.3 %collective-permute-start.13 = (bf16[128,768]{1,0:T(8,128)(2,1)S(1)}, bf16[128,768]{1,0:T(8,128)(2,1)S(1)}, u32[]{:S(2)}, u32[]{:S(2)}) collective-permute-start(bf16[128,768]{1,0:T(8,128)(2,1)S(1)} %collective-permute-done.10.refs_2_), channel_id=1, source_target_pairs={{0,8},{1,9},{2,10},{3,11},{4,12},{5,13},{6,14},{7,15},{8,0},{9,1},... | collective-permute-start | bytes 589832 | tf_op jit(solution)/shard_map/ppermute | solution.py:423
  66.2 7.8 %collective-permute-start.16 = (bf16[128,768]{1,0:T(8,128)(2,1)S(1)}, bf16[128,768]{1,0:T(8,128)(2,1)S(1)}, u32[]{:S(2)}, u32[]{:S(2)}) collective-permute-start(bf16[128,768]{1,0:T(8,128)(2,1)S(1)} %act.5.refs_7_.refs_1_), channel_id=1, source_target_pairs={{0,16},{1,17},{2,18},{3,19},{4,20},{5,21},{6,22},{7,23},{8,24},{9,... | collective-permute-start | bytes 589832 | tf_op jit(solution)/shard_map/ppermute | solution.py:423
  66.5 15.8 %collective-permute-start.19 = (bf16[128,1536]{1,0:T(8,128)(2,1)S(1)}, bf16[128,1536]{1,0:T(8,128)(2,1)S(1)}, u32[]{:S(2)}, u32[]{:S(2)}) collective-permute-start(bf16[128,1536]{1,0:T(8,128)(2,1)S(1)} %get-tuple-element.67), channel_id=1, source_target_pairs={{0,16},{1,17},{2,18},{3,19},{4,20},{5,21},{6,22},{7,23},{8,24},{9,... | collective-permute-start | bytes 1179656 | tf_op jit(solution)/shard_map/ppermute | solution.py:423
  71.7 12.2 %collective-permute-start.27 = (bf16[288,256]{1,0:T(8,128)(2,1)S(1)}, bf16[288,256]{1,0:T(8,128)(2,1)S(1)}, u32[]{:S(2)}, u32[]{:S(2)}) collective-permute-start(bf16[288,256]{1,0:T(8,128)(2,1)S(1)} %get-tuple-element.73), channel_id=1, source_target_pairs={{0,1},{1,0},{2,3},{3,2},{4,5},{5,4},{6,7},{7,6},{8,9},{9,8},{10,11... | collective-permute-start | bytes 442376 | tf_op jit(solution)/shard_map/ppermute | solution.py:423
  73.2 25.5 %collective-permute-start.15 = (bf16[128,1536]{1,0:T(8,128)(2,1)S(1)}, bf16[128,1536]{1,0:T(8,128)(2,1)S(1)}, u32[]{:S(2)}, u32[]{:S(2)}) collective-permute-start(bf16[128,1536]{1,0:T(8,128)(2,1)S(1)} %get-tuple-element.64), channel_id=1, source_target_pairs={{0,16},{1,17},{2,18},{3,19},{4,20},{5,21},{6,22},{7,23},{8,24},{9,... | collective-permute-start | bytes 1179656 | tf_op jit(solution)/shard_map/ppermute | solution.py:423
  73.6 10.7 %collective-permute-start.17 = (bf16[128,768]{1,0:T(8,128)(2,1)S(1)}, bf16[128,768]{1,0:T(8,128)(2,1)S(1)}, u32[]{:S(2)}, u32[]{:S(2)}) collective-permute-start(bf16[128,768]{1,0:T(8,128)(2,1)S(1)} %act.5.refs_7_.refs_1_), channel_id=1, source_target_pairs={{0,8},{1,9},{2,10},{3,11},{4,12},{5,13},{6,14},{7,15},{8,0},{9,1},... | collective-permute-start | bytes 589832 | tf_op jit(solution)/shard_map/ppermute | solution.py:423
  73.9 20.7 %collective-permute-start.18 = (bf16[128,768]{1,0:T(8,128)(2,1)S(1)}, bf16[128,768]{1,0:T(8,128)(2,1)S(1)}, u32[]{:S(2)}, u32[]{:S(2)}) collective-permute-start(bf16[128,768]{1,0:T(8,128)(2,1)S(1)} %collective-permute-done.16.refs_2_), channel_id=1, source_target_pairs={{0,8},{1,9},{2,10},{3,11},{4,12},{5,13},{6,14},{7,15},{8,0},{9,1},... | collective-permute-start | bytes 589832 | tf_op jit(solution)/shard_map/ppermute | solution.py:423
  83.6 11.0 %collective-permute-start.23 = (bf16[128,768]{1,0:T(8,128)(2,1)S(1)}, bf16[128,768]{1,0:T(8,128)(2,1)S(1)}, u32[]{:S(2)}, u32[]{:S(2)}) collective-permute-start(bf16[128,768]{1,0:T(8,128)(2,1)S(1)} %act.6.refs_7_.refs_1_), channel_id=1, source_target_pairs={{0,16},{1,17},{2,18},{3,19},{4,20},{5,21},{6,22},{7,23},{8,24},{9,... | collective-permute-start | bytes 589832 | tf_op jit(solution)/shard_map/ppermute | solution.py:423
  84.0 38.7 %collective-permute-start.28 = (bf16[288,256]{1,0:T(8,128)(2,1)S(1)}, bf16[288,256]{1,0:T(8,128)(2,1)S(1)}, u32[]{:S(2)}, u32[]{:S(2)}) collective-permute-start(bf16[288,256]{1,0:T(8,128)(2,1)S(1)} %add_convert_fusion.2), channel_id=1, source_target_pairs={{0,2},{1,3},{2,4},{3,5},{4,6},{5,7},{6,0},{7,1},{8,10},{9,11},{10,... | collective-permute-start | bytes 442376 | tf_op jit(solution)/shard_map/ppermute | solution.py:423
  84.2 16.1 %collective-permute-start.24 = (bf16[128,768]{1,0:T(8,128)(2,1)S(1)}, bf16[128,768]{1,0:T(8,128)(2,1)S(1)}, u32[]{:S(2)}, u32[]{:S(2)}) collective-permute-start(bf16[128,768]{1,0:T(8,128)(2,1)S(1)} %act.6.refs_7_.refs_1_), channel_id=1, source_target_pairs={{0,8},{1,9},{2,10},{3,11},{4,12},{5,13},{6,14},{7,15},{8,0},{9,1},... | collective-permute-start | bytes 589832 | tf_op jit(solution)/shard_map/ppermute | solution.py:423
  94.6 5.7 %collective-permute-start.25 = (bf16[128,768]{1,0:T(8,128)(2,1)S(1)}, bf16[128,768]{1,0:T(8,128)(2,1)S(1)}, u32[]{:S(2)}, u32[]{:S(2)}) collective-permute-start(bf16[128,768]{1,0:T(8,128)(2,1)S(1)} %collective-permute-done.23.refs_2_), channel_id=1, source_target_pairs={{0,8},{1,9},{2,10},{3,11},{4,12},{5,13},{6,14},{7,15},{8,0},{9,1},... | collective-permute-start | bytes 589832 | tf_op jit(solution)/shard_map/ppermute | solution.py:423
  98.1 7.2 %collective-permute-start.29 = (bf16[288,256]{1,0:T(8,128)(2,1)S(1)}, bf16[288,256]{1,0:T(8,128)(2,1)S(1)}, u32[]{:S(2)}, u32[]{:S(2)}) collective-permute-start(bf16[288,256]{1,0:T(8,128)(2,1)S(1)} %get-tuple-element.74), channel_id=1, source_target_pairs={{0,1},{1,0},{2,3},{3,2},{4,5},{5,4},{6,7},{7,6},{8,9},{9,8},{10,11... | collective-permute-start | bytes 442376 | tf_op jit(solution)/shard_map/ppermute | solution.py:423
  99.9 7.1 %collective-permute-start.20 = (bf16[128,768]{1,0:T(8,128)(2,1)S(1)}, bf16[128,768]{1,0:T(8,128)(2,1)S(1)}, u32[]{:S(2)}, u32[]{:S(2)}) collective-permute-start(bf16[128,768]{1,0:T(8,128)(2,1)S(1)} %act.7.refs_7_.refs_1_), channel_id=1, source_target_pairs={{0,16},{1,17},{2,18},{3,19},{4,20},{5,21},{6,22},{7,23},{8,24},{9,... | collective-permute-start | bytes 589832 | tf_op jit(solution)/shard_map/ppermute | solution.py:423
  103.8 5.8 %collective-permute-start.31 = (bf16[288,256]{1,0:T(8,128)(2,1)S(1)}, bf16[288,256]{1,0:T(8,128)(2,1)S(1)}, u32[]{:S(2)}, u32[]{:S(2)}) collective-permute-start(bf16[288,256]{1,0:T(8,128)(2,1)S(1)} %get-tuple-element.75), channel_id=1, source_target_pairs={{0,1},{1,0},{2,3},{3,2},{4,5},{5,4},{6,7},{7,6},{8,9},{9,8},{10,11... | collective-permute-start | bytes 442376 | tf_op jit(solution)/shard_map/ppermute | solution.py:423
  105.3 17.3 %collective-permute-start.30 = (bf16[288,256]{1,0:T(8,128)(2,1)S(1)}, bf16[288,256]{1,0:T(8,128)(2,1)S(1)}, u32[]{:S(2)}, u32[]{:S(2)}) collective-permute-start(bf16[288,256]{1,0:T(8,128)(2,1)S(1)} %add_convert_fusion.1), channel_id=1, source_target_pairs={{0,4},{1,5},{2,6},{3,7},{4,0},{5,1},{6,2},{7,3},{8,12},{9,13},{10,... | collective-permute-start | bytes 442376 | tf_op jit(solution)/shard_map/ppermute | solution.py:423
  105.4 4.9 %collective-permute-start.21 = (bf16[128,768]{1,0:T(8,128)(2,1)S(1)}, bf16[128,768]{1,0:T(8,128)(2,1)S(1)}, u32[]{:S(2)}, u32[]{:S(2)}) collective-permute-start(bf16[128,768]{1,0:T(8,128)(2,1)S(1)} %act.7.refs_7_.refs_1_), channel_id=1, source_target_pairs={{0,8},{1,9},{2,10},{3,11},{4,12},{5,13},{6,14},{7,15},{8,0},{9,1},... | collective-permute-start | bytes 589832 | tf_op jit(solution)/shard_map/ppermute | solution.py:423
  107.0 3.3 %collective-permute-start.22 = (bf16[128,768]{1,0:T(8,128)(2,1)S(1)}, bf16[128,768]{1,0:T(8,128)(2,1)S(1)}, u32[]{:S(2)}, u32[]{:S(2)}) collective-permute-start(bf16[128,768]{1,0:T(8,128)(2,1)S(1)} %collective-permute-done.20.refs_2_), channel_id=1, source_target_pairs={{0,8},{1,9},{2,10},{3,11},{4,12},{5,13},{6,14},{7,15},{8,0},{9,1},... | collective-permute-start | bytes 589832 | tf_op jit(solution)/shard_map/ppermute | solution.py:423
  109.6 5.7 %copy-start.10 = (f32[4,288]{1,0:T(4,128)S(1)}, f32[4,288]{1,0:T(4,128)}, u32[]{:S(2)}) copy-start(f32[4,288]{1,0:T(4,128)} %get-tuple-element.53) | copy-start | bytes 13828
  109.6 16.7 %copy-start.8 = (f32[2304]{0:T(1024)S(1)}, f32[2304]{0:T(1024)}, u32[]{:S(2)}) copy-start(f32[2304]{0:T(1024)} %param.19) | copy-start | bytes 27652
  109.6 16.8 %copy-start.9 = (f32[16]{0:T(128)S(1)}, f32[16]{0:T(128)}, u32[]{:S(2)}) copy-start(f32[16]{0:T(128)} %param.21) | copy-start | bytes 196
  109.6 13.0 %collective-permute-start.32 = (bf16[288,256]{1,0:T(8,128)(2,1)S(1)}, bf16[288,256]{1,0:T(8,128)(2,1)S(1)}, u32[]{:S(2)}, u32[]{:S(2)}) collective-permute-start(bf16[288,256]{1,0:T(8,128)(2,1)S(1)} %add_convert_fusion), channel_id=1, source_target_pairs={{0,6},{1,7},{2,0},{3,1},{4,2},{5,3},{6,4},{7,5},{8,14},{9,15},{10,... | collective-permute-start | bytes 442376 | tf_op jit(solution)/shard_map/ppermute | solution.py:423
  110.3 23.7 %copy-start.1 = (bf16[2304,512]{1,0:T(8,128)(2,1)S(1)}, bf16[2304,512]{1,0:T(8,128)(2,1)}, u32[]{:S(2)}) copy-start(bf16[2304,512]{1,0:T(8,128)(2,1)} %refs_2_.1) | copy-start | bytes 7077892
  113.8 45.0 %copy-start.7 = (f32[256,288]{0,1:T(8,128)S(1)}, f32[256,288]{0,1:T(8,128)}, u32[]{:S(2)}) copy-start(f32[256,288]{0,1:T(8,128)} %param.11) | copy-start | bytes 884740
  113.8 8.9 %collective-permute-start.26 = (bf16[288,256]{1,0:T(8,128)(2,1)S(1)}, bf16[288,256]{1,0:T(8,128)(2,1)S(1)}, u32[]{:S(2)}, u32[]{:S(2)}) collective-permute-start(bf16[288,256]{1,0:T(8,128)(2,1)S(1)} %get-tuple-element.72), channel_id=1, source_target_pairs={{0,1},{1,0},{2,3},{3,2},{4,5},{5,4},{6,7},{7,6},{8,9},{9,8},{10,11... | collective-permute-start | bytes 442376 | tf_op jit(solution)/shard_map/ppermute | solution.py:423
  115.3 7.3 %collective-permute-start.8 = (f32[4,288]{1,0:T(4,128)S(1)}, f32[4,288]{1,0:T(4,128)S(1)}, u32[]{:S(2)}, u32[]{:S(2)}) collective-permute-start(f32[4,288]{1,0:T(4,128)S(1)} %copy-done.10), channel_id=1, source_target_pairs={{0,0},{1,1},{2,8},{3,9},{4,16},{5,17},{6,24},{7,25},{8,2},{9,3},{1... | collective-permute-start | bytes 13832 | tf_op jit(solution)/shard_map/ppermute | solution.py:423
  123.7 10.3 %all-to-all-start = ((f32[32,4,288]{2,1,0:T(4,128)}), f32[32,4,288]{2,1,0:T(4,128)S(1)}, u32[]{:S(2)}, u32[]{:S(2)}) async-start(f32[32,4,288]{2,1,0:T(4,128)} %get-tuple-element.77), calls=%async_computation | async-start | bytes 393216 | tf_op jit(solution)/shard_map/all_to_all | solution.py:516
  135.5 10.0 %all-to-all-start.1 = ((f32[32,2,16]{2,1,0:T(2,128)}), f32[32,2,16]{2,1,0:T(2,128)S(1)}, u32[]{:S(2)}, u32[]{:S(2)}) async-start(f32[32,2,16]{2,1,0:T(2,128)} %get-tuple-element.79), calls=%async_computation.1 | async-start | bytes 65536 | tf_op jit(solution)/shard_map/all_to_all | solution.py:516
  139.4 19.3 %collective-permute-start.33 = (f32[288,256]{1,0:T(8,128)S(1)}, f32[288,256]{1,0:T(8,128)S(1)}, u32[]{:S(2)}, u32[]{:S(2)}) collective-permute-start(f32[288,256]{1,0:T(8,128)S(1)} %get-tuple-element.76), channel_id=1, source_target_pairs={{0,0},{1,1},{2,8},{3,9},{4,16},{5,17},{6,24},{7,25},{8,2},{9,3},{1... | collective-permute-start | bytes 884744 | tf_op jit(solution)/shard_map/ppermute | solution.py:423

commit v13 on v12

--- a/solution.py
+++ b/solution.py
@@ -329,7 +329,7 @@
     v = parts[0][...].astype(f32)
     for ref in parts[1:]:
         v = v + ref[...].astype(f32)
-    total[...] = v
+    total[...] = v.astype(bf16)
     ends = columns_at(cols[...].astype(f32).T[5:6], v)[0 : stream.shape[0]]
     ends = stream[...] + branch_scale * ends
     message[...] = jnp.broadcast_to(ends[None], message.shape)
@@ -338,7 +338,7 @@
 def total_call(cols, stream, parts, count):
     reqs, block = stream.shape
     tokens = cols.shape[0]
-    outs = [shape((block, tokens), f32), shape((count, reqs, block), f32)]
+    outs = [shape((block, tokens), bf16), shape((count, reqs, block), f32)]
     return pl.pallas_call(
         total_kernel,
         grid=(1,),
@@ -490,6 +490,8 @@
 
     feeds[2] = step(feeds[1])
     feeds[3] = step(feeds[2])
+    feeds[2] = step(feeds[1])
+    feeds[3] = step(feeds[2])
     p0 = do_partial(0)
     p1 = do_partial(1, p0)
     s0 = do_sum(0, p1)
@@ -499,12 +501,12 @@
     a0 = do_act(0, s1)
     p3 = do_partial(3, a0)
     s2 = do_sum(2, p3)
-    do_hop(0, s2)
     a1 = do_act(1, s2)
+    do_hop(0, a1)
     d0 = do_down(0, a1)
     s3 = do_sum(3, d0)
-    do_hop(1, s3)
     a2 = do_act(2, s3)
+    do_hop(1, a2)
     d1 = do_down(1, a2)
     do_hop(2, None)
     a3 = do_act(3, d1)
@@ -514,8 +516,7 @@
     terms = [v for group in range(parts) for v in shares[group]]
     total, message = total_call(partial[parts - 1][2], stream, terms, dp * mp)
     exchange = lambda v: lax.all_to_all(v, ("dp", "mp"), 0, 0, tiled=True)
-    got = exchange(message)
-    branch = send(total, home)
+    got, branch = lax.optimization_barrier((exchange(message), send(total, home)))
     order = [
         [(q * spread + r) * mp + group * sides + x for group in range(parts) for r in range(spread)]
         for q in range(parts)
@@ -529,7 +530,7 @@
         softness_per_sequence[:, None],
     )
     pairs = exchange(pairs)
-    new_hidden = skip_stream_arriving + branch_scale * branch.T
+    new_hidden = skip_stream_arriving + branch_scale * branch.T.astype(f32)
     largest = jnp.max(pairs[:, 0], axis=0)
     mass = jnp.sum(pairs[:, 1] * jnp.exp(pairs[:, 0] - largest), axis=0)
     logprobs = logits - largest[:, None] - jnp.log(mass)[:, None]

time: 160 us -> 153 us (0.956); the launches traced: 159 us -> 150 us
  waiting for transfers between devices: 65.7 us -> 57.1 us
    ppermute x34, waiting for transfers between devices: 56.4 us -> 51.8 us  [send(): return lax.ppermute(value, ('dp', 'mp'), pairs)]
    all_to_all x2, waiting for transfers between devices: 9.27 us -> 5.29 us  [body(): exchange = lambda v: lax.all_to_all(v, ('dp', 'mp'), 0, 0, tiled=True)]
  transfers between devices with their start and end apart: 36 -> 36, of which waited for: 14 -> 15; matrix products, arithmetic and copies ran while one was open for 1% -> 1% of each run, Pallas kernels for 26% -> 28%
where the time goes in v13:
time: 153 us; the launch traced here: 150 us
  waiting for transfers between devices  57.1 us (37%)
  Pallas kernels  46.1 us (30%)
  starting transfers between devices  38.9 us (25%)
  local copies, waits for them, and re-layouts  5.58 us (4%)
  other arithmetic  1.7 us (1%)
    ppermute x34, waiting for transfers between devices, send(): return lax.ppermute(value, ('dp', 'mp'), pairs)  51.8 us
    ppermute x34, starting transfers between devices, send(): return lax.ppermute(value, ('dp', 'mp'), pairs)  32.6 us
    pallas_call x4, Pallas kernels, partial_call(): pl.pallas_call(lambda *refs: partial_kernel(sides, len(feeds), *refs), gr...  19.4 us
    pallas_call x4, Pallas kernels, down_call(): pl.pallas_call(lambda *refs: down_kernel(sides, *refs), grid=(experts,),...  13.8 us
    all_to_all x2, starting transfers between devices, body(): exchange = lambda v: lax.all_to_all(v, ('dp', 'mp'), 0, 0, tiled=True)  6.26 us
    all_to_all x2, waiting for transfers between devices, body(): exchange = lambda v: lax.all_to_all(v, ('dp', 'mp'), 0, 0, tiled=True)  5.29 us
    pallas_call x4, Pallas kernels, act_call(): pl.pallas_call(lambda *refs: act_kernel(base, *refs), in_specs=[SMEM] + [...  4.95 us
    unnamed x22, local copies, waits for them, and re-layouts  4.05 us
  transfers between devices with their start and end apart: 36, of which 15 were waited for; matrix products, arithmetic and copies ran while one was open for 1% of the time, Pallas kernels for 28%

profile of v13, /device:TPU:4, one launch (start us, length us, event | category | flops | bytes accessed | tf_op | source)
XLA Modules:
  0.0 150.4 jit_solution(4466346999485484251)
XLA Ops:
  0.6 1.3 broadcast_in_dim.4.gain
  1.9 1.9 %prep.1 = (bf16[304,256]{1,0:T(8,128)(2,1)}, f32[4,288]{1,0:T(4,128)}) custom-call(s32[1,4]{1,0:T(1,128)} %tallies.1, f32[288,256]{1,0:T(8,128)} %bitcast.19, f32[1,288]{1,0:T(1,128)} %broadcast_in_dim.4.gain, s32[2,256]{1,0:T(2,128)} %bitcast.23), custom_call_target="tpu_custom_call" | custom-call | flops 88473 | bytes 132710 | tf_op jit(solution)/shard_map/prep/pallas_call | solution.py:75
  3.8 1.5 %collective-permute-start = (bf16[304,256]{1,0:T(8,128)(2,1)}, bf16[304,256]{1,0:T(8,128)(2,1)S(1)}, u32[]{:S(2)}, u32[]{:S(2)}) collective-permute-start(bf16[304,256]{1,0:T(8,128)(2,1)} %get-tuple-element.43), channel_id=1, source_target_pairs={{0,6},{1,7},{2,14},{3,15},{4,22},{5,23},{6,30},{7,31},{8,0},{9,1},... | collective-permute-start | bytes 466952 | tf_op jit(solution)/shard_map/ppermute | solution.py:423
  5.3 3.0 %collective-permute-start.1 = (bf16[304,256]{1,0:T(8,128)(2,1)}, bf16[304,256]{1,0:T(8,128)(2,1)S(1)}, u32[]{:S(2)}, u32[]{:S(2)}) collective-permute-start(bf16[304,256]{1,0:T(8,128)(2,1)} %get-tuple-element.43), channel_id=1, source_target_pairs={{0,7},{1,6},{2,15},{3,14},{4,23},{5,22},{6,31},{7,30},{8,1},{9,0},... | collective-permute-start | bytes 466952 | tf_op jit(solution)/shard_map/ppermute | solution.py:423
  8.5 3.8 %collective-permute-done.refs_0_ = bf16[304,256]{1,0:T(8,128)(2,1)S(1)} collective-permute-done((bf16[304,256]{1,0:T(8,128)(2,1)}, bf16[304,256]{1,0:T(8,128)(2,1)S(1)}, u32[]{:S(2)}, u32[]{:S(2)}) %collective-permute-start) | collective-permute-done | bytes 155680 | tf_op jit(solution)/shard_map/ppermute | solution.py:423
  12.3 4.3 %collective-permute-done.1.refs_1_ = bf16[304,256]{1,0:T(8,128)(2,1)S(1)} collective-permute-done((bf16[304,256]{1,0:T(8,128)(2,1)}, bf16[304,256]{1,0:T(8,128)(2,1)S(1)}, u32[]{:S(2)}, u32[]{:S(2)}) %collective-permute-start.1) | collective-permute-done | bytes 155680 | tf_op jit(solution)/shard_map/ppermute | solution.py:423
  16.5 5.9 %collective-permute-start.2 = (bf16[608,256]{1,0:T(8,128)(2,1)S(1)}, bf16[608,256]{1,0:T(8,128)(2,1)S(1)}, u32[]{:S(2)}, u32[]{:S(2)}) collective-permute-start(bf16[608,256]{1,0:T(8,128)(2,1)S(1)} %join.1.refs_1_), channel_id=1, source_target_pairs={{0,6},{1,7},{2,0},{3,1},{4,2},{5,3},{6,4},{7,5},{8,14},{9,15},{10,... | collective-permute-start | bytes 933896 | tf_op jit(solution)/shard_map/ppermute | solution.py:423
  22.5 2.0 %copy-done.2 = bf16[4,576,720]{2,1,0:T(8,128)(2,1)S(1)} copy-done((bf16[4,576,720]{2,1,0:T(8,128)(2,1)S(1)}, bf16[4,576,720]{2,1,0:T(8,128)(2,1)}, u32[]{:S(2)}) %copy-start.2) | copy-done | bytes 3317784
  24.5 2.0 %copy-done.4 = bf16[4,576,720]{2,1,0:T(8,128)(2,1)S(1)} copy-done((bf16[4,576,720]{2,1,0:T(8,128)(2,1)S(1)}, bf16[4,576,720]{2,1,0:T(8,128)(2,1)}, u32[]{:S(2)}) %copy-start.4) | copy-done | bytes 3317784
  26.5 4.9 %gate_up_partial.4 = (f32[256,1536]{1,0:T(8,128)S(1)}, bf16[256,1536]{1,0:T(8,128)(2,1)S(1)}, bf16[256,128]{1,0:T(8,128)(2,1)S(1)}) custom-call(s32[3]{0:T(128)S(1)} %pad_add_fusion.1.refs_0_, bf16[608,256]{1,0:T(8,128)(2,1)S(1)} %join.1.refs_1_, bf16[128,576]{1,0:T(8,128)(2,1)S(1)} %pad_add_fusion.refs_2_, bf16[4,576,720]{2,1,0:T(8,128)(2,1)S(1)} %copy-done.2, ...), custom_call_target="tpu_custom_call" | custom-call | flops 6794772480 | bytes 35979264 | tf_op jit(solution)/shard_map/gate_up_partial/pallas_call | solution.py:190
  31.6 4.9 %gate_up_partial.5 = (f32[256,1536]{1,0:T(8,128)S(1)}, bf16[256,1536]{1,0:T(8,128)(2,1)S(1)}, bf16[256,128]{1,0:T(8,128)(2,1)S(1)}) custom-call(s32[3]{0:T(128)S(1)} %pad_add_fusion.1.refs_0_, bf16[608,256]{1,0:T(8,128)(2,1)S(1)} %collective-permute-done.2.refs_1_, bf16[128,576]{1,0:T(8,128)(2,1)S(1)} %pad_add_fusion.refs_2_, ...), custom_call_target="tpu_custom_call" | custom-call | flops 6794772480 | bytes 35979264 | tf_op jit(solution)/shard_map/gate_up_partial/pallas_call | solution.py:190
  36.9 0.9 core_sum.4
  37.9 3.4 %collective-permute-done.3.refs_1_ = bf16[608,256]{1,0:T(8,128)(2,1)S(1)} collective-permute-done((bf16[608,256]{1,0:T(8,128)(2,1)S(1)}, bf16[608,256]{1,0:T(8,128)(2,1)S(1)}, u32[]{:S(2)}, u32[]{:S(2)}) %collective-permute-start.3) | collective-permute-done | bytes 311328 | tf_op jit(solution)/shard_map/ppermute | solution.py:423
  41.3 4.8 %gate_up_partial.6 = (f32[256,1536]{1,0:T(8,128)S(1)}, bf16[256,1536]{1,0:T(8,128)(2,1)S(1)}, bf16[256,128]{1,0:T(8,128)(2,1)S(1)}) custom-call(s32[3]{0:T(128)S(1)} %pad_add_fusion.1.refs_0_, bf16[608,256]{1,0:T(8,128)(2,1)S(1)} %collective-permute-done.3.refs_1_, bf16[128,576]{1,0:T(8,128)(2,1)S(1)} %pad_add_fusion.refs_2_, ...), custom_call_target="tpu_custom_call" | custom-call | flops 6794772480 | bytes 35979264 | tf_op jit(solution)/shard_map/gate_up_partial/pallas_call | solution.py:190
  46.1 2.1 %collective-permute-start.5 = (bf16[608,256]{1,0:T(8,128)(2,1)S(1)}, bf16[608,256]{1,0:T(8,128)(2,1)S(1)}, u32[]{:S(2)}, u32[]{:S(2)}) collective-permute-start(bf16[608,256]{1,0:T(8,128)(2,1)S(1)} %collective-permute-done.3.refs_1_), channel_id=1, source_target_pairs={{0,6},{1,7},{2,0},{3,1},{4,2},{5,3},{6,4},{7,5},{8,14},{9,15},{10,... | collective-permute-start | bytes 933896 | tf_op jit(solution)/shard_map/ppermute | solution.py:423
  48.2 0.9 core_sum.5
  49.2 1.2 act.4.refs_5_.refs_1_
  50.4 2.1 %collective-permute-start.10 = (bf16[128,768]{1,0:T(8,128)(2,1)S(1)}, bf16[128,768]{1,0:T(8,128)(2,1)S(1)}, u32[]{:S(2)}, u32[]{:S(2)}) collective-permute-start(bf16[128,768]{1,0:T(8,128)(2,1)S(1)} %act.4.refs_5_.refs_1_), channel_id=1, source_target_pairs={{0,16},{1,17},{2,18},{3,19},{4,20},{5,21},{6,22},{7,23},{8,24},{9,... | collective-permute-start | bytes 589832 | tf_op jit(solution)/shard_map/ppermute | solution.py:423
  52.5 2.6 %collective-permute-done.5.refs_1_ = bf16[608,256]{1,0:T(8,128)(2,1)S(1)} collective-permute-done((bf16[608,256]{1,0:T(8,128)(2,1)S(1)}, bf16[608,256]{1,0:T(8,128)(2,1)S(1)}, u32[]{:S(2)}, u32[]{:S(2)}) %collective-permute-start.5) | collective-permute-done | bytes 311328 | tf_op jit(solution)/shard_map/ppermute | solution.py:423
  55.1 4.8 %gate_up_partial.7 = (f32[256,1536]{1,0:T(8,128)S(1)}, bf16[256,1536]{1,0:T(8,128)(2,1)S(1)}, bf16[256,128]{1,0:T(8,128)(2,1)S(1)}) custom-call(s32[3]{0:T(128)S(1)} %pad_add_fusion.1.refs_0_, bf16[608,256]{1,0:T(8,128)(2,1)S(1)} %collective-permute-done.5.refs_1_, bf16[128,576]{1,0:T(8,128)(2,1)S(1)} %pad_add_fusion.refs_2_, ...), custom_call_target="tpu_custom_call" | custom-call | flops 6794772480 | bytes 35979264 | tf_op jit(solution)/shard_map/gate_up_partial/pallas_call | solution.py:190
  60.0 0.9 core_sum.6
  61.1 1.2 act.5.refs_7_.refs_1_
  62.7 2.2 %collective-permute-done.10.refs_2_ = bf16[128,768]{1,0:T(8,128)(2,1)S(1)} collective-permute-done((bf16[128,768]{1,0:T(8,128)(2,1)S(1)}, bf16[128,768]{1,0:T(8,128)(2,1)S(1)}, u32[]{:S(2)}, u32[]{:S(2)}) %collective-permute-start.10) | collective-permute-done | bytes 196640 | tf_op jit(solution)/shard_map/ppermute | solution.py:423
  65.2 1.7 %collective-permute-start.17 = (bf16[128,1536]{1,0:T(8,128)(2,1)S(1)}, bf16[128,1536]{1,0:T(8,128)(2,1)S(1)}, u32[]{:S(2)}, u32[]{:S(2)}) collective-permute-start(bf16[128,1536]{1,0:T(8,128)(2,1)S(1)} %get-tuple-element.67), channel_id=1, source_target_pairs={{0,16},{1,17},{2,18},{3,19},{4,20},{5,21},{6,22},{7,23},{8,24},{9,... | collective-permute-start | bytes 1179656 | tf_op jit(solution)/shard_map/ppermute | solution.py:423
  66.9 3.5 %down.4 = (bf16[288,256]{1,0:T(8,128)(2,1)S(1)}, bf16[288,256]{1,0:T(8,128)(2,1)S(1)}) custom-call(s32[3]{0:T(128)S(1)} %pad_add_fusion.1.refs_0_, bf16[128,768]{1,0:T(8,128)(2,1)S(1)} %act.4.refs_5_.refs_1_, bf16[128,768]{1,0:T(8,128)(2,1)S(1)} %collective-permute-done.10.refs_2_, bf16[128,768]{1,0:T(8,128)(2,1)S(1)} %collective-permute-done.13.refs_3_, ...), custom_call_target="tpu_custom_call" | custom-call | flops 3397386240 | bytes 14450688 | tf_op jit(solution)/shard_map/down/pallas_call | solution.py:306
  71.1 0.9 core_sum.7
  71.9 8.7 %collective-permute-done.17.refs_2_ = bf16[128,1536]{1,0:T(8,128)(2,1)S(1)} collective-permute-done((bf16[128,1536]{1,0:T(8,128)(2,1)S(1)}, bf16[128,1536]{1,0:T(8,128)(2,1)S(1)}, u32[]{:S(2)}, u32[]{:S(2)}) %collective-permute-start.17) | collective-permute-done | bytes 393248 | tf_op jit(solution)/shard_map/ppermute | solution.py:423
  80.6 1.2 act.6.refs_7_.refs_1_
  82.2 1.7 %collective-permute-start.15 = (bf16[128,1536]{1,0:T(8,128)(2,1)S(1)}, bf16[128,1536]{1,0:T(8,128)(2,1)S(1)}, u32[]{:S(2)}, u32[]{:S(2)}) collective-permute-start(bf16[128,1536]{1,0:T(8,128)(2,1)S(1)} %get-tuple-element.66), channel_id=1, source_target_pairs={{0,16},{1,17},{2,18},{3,19},{4,20},{5,21},{6,22},{7,23},{8,24},{9,... | collective-permute-start | bytes 1179656 | tf_op jit(solution)/shard_map/ppermute | solution.py:423
  85.6 4.2 %collective-permute-done.23.refs_2_ = bf16[128,768]{1,0:T(8,128)(2,1)S(1)} collective-permute-done((bf16[128,768]{1,0:T(8,128)(2,1)S(1)}, bf16[128,768]{1,0:T(8,128)(2,1)S(1)}, u32[]{:S(2)}, u32[]{:S(2)}) %collective-permute-start.23) | collective-permute-done | bytes 196640 | tf_op jit(solution)/shard_map/ppermute | solution.py:423
  89.8 3.5 %down.5 = (bf16[288,256]{1,0:T(8,128)(2,1)S(1)}, bf16[288,256]{1,0:T(8,128)(2,1)S(1)}) custom-call(s32[3]{0:T(128)S(1)} %pad_add_fusion.1.refs_0_, bf16[128,768]{1,0:T(8,128)(2,1)S(1)} %act.5.refs_7_.refs_1_, bf16[128,768]{1,0:T(8,128)(2,1)S(1)} %collective-permute-done.16.refs_2_, bf16[128,768]{1,0:T(8,128)(2,1)S(1)} %collective-permute-done.18.refs_3_, ...), custom_call_target="tpu_custom_call" | custom-call | flops 3397386240 | bytes 14450688 | tf_op jit(solution)/shard_map/down/pallas_call | solution.py:306
  93.9 3.1 %collective-permute-done.15.refs_2_ = bf16[128,1536]{1,0:T(8,128)(2,1)S(1)} collective-permute-done((bf16[128,1536]{1,0:T(8,128)(2,1)S(1)}, bf16[128,1536]{1,0:T(8,128)(2,1)S(1)}, u32[]{:S(2)}, u32[]{:S(2)}) %collective-permute-start.15) | collective-permute-done | bytes 393248 | tf_op jit(solution)/shard_map/ppermute | solution.py:423
  96.9 1.2 act.7.refs_7_.refs_1_
  98.5 3.4 %down.6 = (bf16[288,256]{1,0:T(8,128)(2,1)S(1)}, bf16[288,256]{1,0:T(8,128)(2,1)S(1)}) custom-call(s32[3]{0:T(128)S(1)} %pad_add_fusion.1.refs_0_, bf16[128,768]{1,0:T(8,128)(2,1)S(1)} %act.6.refs_7_.refs_1_, bf16[128,768]{1,0:T(8,128)(2,1)S(1)} %collective-permute-done.23.refs_2_, bf16[128,768]{1,0:T(8,128)(2,1)S(1)} %collective-permute-done.24.refs_3_, ...), custom_call_target="tpu_custom_call" | custom-call | flops 3397386240 | bytes 14450688 | tf_op jit(solution)/shard_map/down/pallas_call | solution.py:306
  102.8 1.1 collective-permute-done.20.refs_2_
  103.9 3.3 %collective-permute-done.31 = bf16[288,256]{1,0:T(8,128)(2,1)S(1)} collective-permute-done((bf16[288,256]{1,0:T(8,128)(2,1)S(1)}, bf16[288,256]{1,0:T(8,128)(2,1)S(1)}, u32[]{:S(2)}, u32[]{:S(2)}) %collective-permute-start.31) | collective-permute-done | bytes 147488 | tf_op jit(solution)/shard_map/ppermute | solution.py:423
  107.3 2.0 %collective-permute-start.32 = (bf16[288,256]{1,0:T(8,128)(2,1)S(1)}, bf16[288,256]{1,0:T(8,128)(2,1)S(1)}, u32[]{:S(2)}, u32[]{:S(2)}) collective-permute-start(bf16[288,256]{1,0:T(8,128)(2,1)S(1)} %add_convert_fusion), channel_id=1, source_target_pairs={{0,6},{1,7},{2,0},{3,1},{4,2},{5,3},{6,4},{7,5},{8,14},{9,15},{10,... | collective-permute-start | bytes 442376 | tf_op jit(solution)/shard_map/ppermute | solution.py:423
  109.3 3.5 %down.7 = (bf16[288,256]{1,0:T(8,128)(2,1)S(1)}, bf16[288,256]{1,0:T(8,128)(2,1)S(1)}) custom-call(s32[3]{0:T(128)S(1)} %pad_add_fusion.1.refs_0_, bf16[128,768]{1,0:T(8,128)(2,1)S(1)} %act.7.refs_7_.refs_1_, bf16[128,768]{1,0:T(8,128)(2,1)S(1)} %collective-permute-done.20.refs_2_, bf16[128,768]{1,0:T(8,128)(2,1)S(1)} %collective-permute-done.21.refs_3_, ...), custom_call_target="tpu_custom_call" | custom-call | flops 3397386240 | bytes 14450688 | tf_op jit(solution)/shard_map/down/pallas_call | solution.py:306
  113.4 2.5 %collective-permute-start.8 = (f32[4,288]{1,0:T(4,128)S(1)}, f32[4,288]{1,0:T(4,128)S(1)}, u32[]{:S(2)}, u32[]{:S(2)}) collective-permute-start(f32[4,288]{1,0:T(4,128)S(1)} %copy-done.10), channel_id=1, source_target_pairs={{0,0},{1,1},{2,8},{3,9},{4,16},{5,17},{6,24},{7,25},{8,2},{9,3},{1... | collective-permute-start | bytes 13832 | tf_op jit(solution)/shard_map/ppermute | solution.py:423
  115.9 4.8 %collective-permute-done.8.stream = f32[4,288]{1,0:T(4,128)S(1)} collective-permute-done((f32[4,288]{1,0:T(4,128)S(1)}, f32[4,288]{1,0:T(4,128)S(1)}, u32[]{:S(2)}, u32[]{:S(2)}) %collective-permute-start.8) | collective-permute-done | bytes 4640 | tf_op jit(solution)/shard_map/ppermute | solution.py:423
  120.7 1.1 branch_total.1
  121.8 3.0 %all-to-all-start = ((f32[32,4,288]{2,1,0:T(4,128)}), f32[32,4,288]{2,1,0:T(4,128)S(1)}, u32[]{:S(2)}, u32[]{:S(2)}) async-start(f32[32,4,288]{2,1,0:T(4,128)} %get-tuple-element.78), calls=%async_computation | async-start | bytes 393216 | tf_op jit(solution)/shard_map/all_to_all | solution.py:518
  124.9 4.3 %collective-permute-start.33 = (bf16[288,256]{1,0:T(8,128)(2,1)S(1)}, bf16[288,256]{1,0:T(8,128)(2,1)S(1)}, u32[]{:S(2)}, u32[]{:S(2)}) collective-permute-start(bf16[288,256]{1,0:T(8,128)(2,1)S(1)} %get-tuple-element.79), channel_id=1, source_target_pairs={{0,0},{1,1},{2,8},{3,9},{4,16},{5,17},{6,24},{7,25},{8,2},{9,3},{1... | collective-permute-start | bytes 442376 | tf_op jit(solution)/shard_map/ppermute | solution.py:423
  129.3 9.5 %collective-permute-done.33 = bf16[288,256]{1,0:T(8,128)(2,1)S(1)} collective-permute-done((bf16[288,256]{1,0:T(8,128)(2,1)S(1)}, bf16[288,256]{1,0:T(8,128)(2,1)S(1)}, u32[]{:S(2)}, u32[]{:S(2)}) %collective-permute-start.33) | collective-permute-done | bytes 147488 | tf_op jit(solution)/shard_map/ppermute | solution.py:423
  138.9 1.4 head.1
  140.3 3.2 %all-to-all-start.1 = ((f32[32,2,16]{2,1,0:T(2,128)}), f32[32,2,16]{2,1,0:T(2,128)S(1)}, u32[]{:S(2)}, u32[]{:S(2)}) async-start(f32[32,2,16]{2,1,0:T(2,128)} %get-tuple-element.83), calls=%async_computation.1 | async-start | bytes 65536 | tf_op jit(solution)/shard_map/all_to_all | solution.py:518
  143.5 0.7 bitcast_add_fusion
  144.3 5.3 %all-to-all-done.1 = f32[32,2,16]{2,1,0:T(2,128)S(1)} async-done(((f32[32,2,16]{2,1,0:T(2,128)}), f32[32,2,16]{2,1,0:T(2,128)S(1)}, u32[]{:S(2)}, u32[]{:S(2)}) %all-to-all-start.1) | async-done | bytes 4128 | tf_op jit(solution)/shard_map/all_to_all | solution.py:518
  (81 shorter events, 7.9 us)
Async XLA Ops:
  0.6 7.7 %copy-start = (bf16[2304,4]{0,1:T(4,128)(2,1)S(1)}, bf16[2304,4]{0,1:T(4,128)(2,1)}, u32[]{:S(2)}) copy-start(bf16[2304,4]{0,1:T(4,128)(2,1)} %param.15) | copy-start | bytes 55300
  3.8 8.4 %collective-permute-start = (bf16[304,256]{1,0:T(8,128)(2,1)}, bf16[304,256]{1,0:T(8,128)(2,1)S(1)}, u32[]{:S(2)}, u32[]{:S(2)}) collective-permute-start(bf16[304,256]{1,0:T(8,128)(2,1)} %get-tuple-element.43), channel_id=1, source_target_pairs={{0,6},{1,7},{2,14},{3,15},{4,22},{5,23},{6,30},{7,31},{8,0},{9,1},... | collective-permute-start | bytes 466952 | tf_op jit(solution)/shard_map/ppermute | solution.py:423
  5.3 11.2 %collective-permute-start.1 = (bf16[304,256]{1,0:T(8,128)(2,1)}, bf16[304,256]{1,0:T(8,128)(2,1)S(1)}, u32[]{:S(2)}, u32[]{:S(2)}) collective-permute-start(bf16[304,256]{1,0:T(8,128)(2,1)} %get-tuple-element.43), channel_id=1, source_target_pairs={{0,7},{1,6},{2,15},{3,14},{4,23},{5,22},{6,31},{7,30},{8,1},{9,0},... | collective-permute-start | bytes 466952 | tf_op jit(solution)/shard_map/ppermute | solution.py:423
  16.5 14.9 %collective-permute-start.2 = (bf16[608,256]{1,0:T(8,128)(2,1)S(1)}, bf16[608,256]{1,0:T(8,128)(2,1)S(1)}, u32[]{:S(2)}, u32[]{:S(2)}) collective-permute-start(bf16[608,256]{1,0:T(8,128)(2,1)S(1)} %join.1.refs_1_), channel_id=1, source_target_pairs={{0,6},{1,7},{2,0},{3,1},{4,2},{5,3},{6,4},{7,5},{8,14},{9,15},{10,... | collective-permute-start | bytes 933896 | tf_op jit(solution)/shard_map/ppermute | solution.py:423
  22.5 2.0 %copy-start.2 = (bf16[4,576,720]{2,1,0:T(8,128)(2,1)S(1)}, bf16[4,576,720]{2,1,0:T(8,128)(2,1)}, u32[]{:S(2)}) copy-start(bf16[4,576,720]{2,1,0:T(8,128)(2,1)} %refs_3_.7) | copy-start | bytes 9953284
  24.5 2.0 %copy-start.4 = (bf16[4,576,720]{2,1,0:T(8,128)(2,1)S(1)}, bf16[4,576,720]{2,1,0:T(8,128)(2,1)}, u32[]{:S(2)}) copy-start(bf16[4,576,720]{2,1,0:T(8,128)(2,1)} %refs_4_.7) | copy-start | bytes 9953284
  26.5 5.1 %copy-start.3 = (bf16[4,576,720]{2,1,0:T(8,128)(2,1)S(1)}, bf16[4,576,720]{2,1,0:T(8,128)(2,1)}, u32[]{:S(2)}) copy-start(bf16[4,576,720]{2,1,0:T(8,128)(2,1)} %refs_3_.7) | copy-start | bytes 9953284
  26.5 5.1 %copy-start.5 = (bf16[4,576,720]{2,1,0:T(8,128)(2,1)S(1)}, bf16[4,576,720]{2,1,0:T(8,128)(2,1)}, u32[]{:S(2)}) copy-start(bf16[4,576,720]{2,1,0:T(8,128)(2,1)} %refs_4_.7) | copy-start | bytes 9953284
  31.4 5.5 %collective-permute-start.4 = (bf16[256,1536]{1,0:T(8,128)(2,1)S(1)}, bf16[256,1536]{1,0:T(8,128)(2,1)S(1)}, u32[]{:S(2)}, u32[]{:S(2)}) collective-permute-start(bf16[256,1536]{1,0:T(8,128)(2,1)S(1)} %get-tuple-element.45), channel_id=1, source_target_pairs={{0,8},{1,9},{2,10},{3,11},{4,12},{5,13},{6,14},{7,15},{8,0},{9,1},... | collective-permute-start | bytes 2359304 | tf_op jit(solution)/shard_map/ppermute | solution.py:423
  31.5 9.8 %collective-permute-start.3 = (bf16[608,256]{1,0:T(8,128)(2,1)S(1)}, bf16[608,256]{1,0:T(8,128)(2,1)S(1)}, u32[]{:S(2)}, u32[]{:S(2)}) collective-permute-start(bf16[608,256]{1,0:T(8,128)(2,1)S(1)} %collective-permute-done.2.refs_1_), channel_id=1, source_target_pairs={{0,6},{1,7},{2,0},{3,1},{4,2},{5,3},{6,4},{7,5},{8,14},{9,15},{10,... | collective-permute-start | bytes 933896 | tf_op jit(solution)/shard_map/ppermute | solution.py:423
  36.4 11.8 %collective-permute-start.7 = (bf16[256,1536]{1,0:T(8,128)(2,1)S(1)}, bf16[256,1536]{1,0:T(8,128)(2,1)S(1)}, u32[]{:S(2)}, u32[]{:S(2)}) collective-permute-start(bf16[256,1536]{1,0:T(8,128)(2,1)S(1)} %get-tuple-element.52), channel_id=1, source_target_pairs={{0,8},{1,9},{2,10},{3,11},{4,12},{5,13},{6,14},{7,15},{8,0},{9,1},... | collective-permute-start | bytes 2359304 | tf_op jit(solution)/shard_map/ppermute | solution.py:423
  37.8 11.4 %collective-permute-start.6 = (bf16[128,1536]{1,0:T(8,128)(2,1)S(1)}, bf16[128,1536]{1,0:T(8,128)(2,1)S(1)}, u32[]{:S(2)}, u32[]{:S(2)}) collective-permute-start(bf16[128,1536]{1,0:T(8,128)(2,1)S(1)} %get-tuple-element.50), channel_id=1, source_target_pairs={{0,16},{1,17},{2,18},{3,19},{4,20},{5,21},{6,22},{7,23},{8,24},{9,... | collective-permute-start | bytes 1179656 | tf_op jit(solution)/shard_map/ppermute | solution.py:423
  46.1 9.0 %collective-permute-start.5 = (bf16[608,256]{1,0:T(8,128)(2,1)S(1)}, bf16[608,256]{1,0:T(8,128)(2,1)S(1)}, u32[]{:S(2)}, u32[]{:S(2)}) collective-permute-start(bf16[608,256]{1,0:T(8,128)(2,1)S(1)} %collective-permute-done.3.refs_1_), channel_id=1, source_target_pairs={{0,6},{1,7},{2,0},{3,1},{4,2},{5,3},{6,4},{7,5},{8,14},{9,15},{10,... | collective-permute-start | bytes 933896 | tf_op jit(solution)/shard_map/ppermute | solution.py:423
  48.2 11.8 %collective-permute-start.12 = (bf16[256,1536]{1,0:T(8,128)(2,1)S(1)}, bf16[256,1536]{1,0:T(8,128)(2,1)S(1)}, u32[]{:S(2)}, u32[]{:S(2)}) collective-permute-start(bf16[256,1536]{1,0:T(8,128)(2,1)S(1)} %get-tuple-element.60), channel_id=1, source_target_pairs={{0,8},{1,9},{2,10},{3,11},{4,12},{5,13},{6,14},{7,15},{8,0},{9,1},... | collective-permute-start | bytes 2359304 | tf_op jit(solution)/shard_map/ppermute | solution.py:423
  49.1 12.0 %collective-permute-start.11 = (bf16[128,1536]{1,0:T(8,128)(2,1)S(1)}, bf16[128,1536]{1,0:T(8,128)(2,1)S(1)}, u32[]{:S(2)}, u32[]{:S(2)}) collective-permute-start(bf16[128,1536]{1,0:T(8,128)(2,1)S(1)} %get-tuple-element.58), channel_id=1, source_target_pairs={{0,16},{1,17},{2,18},{3,19},{4,20},{5,21},{6,22},{7,23},{8,24},{9,... | collective-permute-start | bytes 1179656 | tf_op jit(solution)/shard_map/ppermute | solution.py:423
  50.4 14.5 %collective-permute-start.10 = (bf16[128,768]{1,0:T(8,128)(2,1)S(1)}, bf16[128,768]{1,0:T(8,128)(2,1)S(1)}, u32[]{:S(2)}, u32[]{:S(2)}) collective-permute-start(bf16[128,768]{1,0:T(8,128)(2,1)S(1)} %act.4.refs_5_.refs_1_), channel_id=1, source_target_pairs={{0,16},{1,17},{2,18},{3,19},{4,20},{5,21},{6,22},{7,23},{8,24},{9,... | collective-permute-start | bytes 589832 | tf_op jit(solution)/shard_map/ppermute | solution.py:423
  59.9 11.2 %collective-permute-start.9 = (bf16[256,1536]{1,0:T(8,128)(2,1)S(1)}, bf16[256,1536]{1,0:T(8,128)(2,1)S(1)}, u32[]{:S(2)}, u32[]{:S(2)}) collective-permute-start(bf16[256,1536]{1,0:T(8,128)(2,1)S(1)} %get-tuple-element.57), channel_id=1, source_target_pairs={{0,8},{1,9},{2,10},{3,11},{4,12},{5,13},{6,14},{7,15},{8,0},{9,1},... | collective-permute-start | bytes 2359304 | tf_op jit(solution)/shard_map/ppermute | solution.py:423
  60.0 7.0 %copy-start.6 = (bf16[4,720,576]{1,2,0:T(8,128)(2,1)S(1)}, bf16[4,720,576]{1,2,0:T(8,128)(2,1)}, u32[]{:S(2)}) copy-start(bf16[4,720,576]{1,2,0:T(8,128)(2,1)} %param.18) | copy-start | bytes 9953284
  62.3 4.6 %collective-permute-start.13 = (bf16[128,768]{1,0:T(8,128)(2,1)S(1)}, bf16[128,768]{1,0:T(8,128)(2,1)S(1)}, u32[]{:S(2)}, u32[]{:S(2)}) collective-permute-start(bf16[128,768]{1,0:T(8,128)(2,1)S(1)} %act.4.refs_5_.refs_1_), channel_id=1, source_target_pairs={{0,8},{1,9},{2,10},{3,11},{4,12},{5,13},{6,14},{7,15},{8,0},{9,1},... | collective-permute-start | bytes 589832 | tf_op jit(solution)/shard_map/ppermute | solution.py:423
  64.9 2.0 %collective-permute-start.14 = (bf16[128,768]{1,0:T(8,128)(2,1)S(1)}, bf16[128,768]{1,0:T(8,128)(2,1)S(1)}, u32[]{:S(2)}, u32[]{:S(2)}) collective-permute-start(bf16[128,768]{1,0:T(8,128)(2,1)S(1)} %collective-permute-done.10.refs_2_), channel_id=1, source_target_pairs={{0,8},{1,9},{2,10},{3,11},{4,12},{5,13},{6,14},{7,15},{8,0},{9,1},... | collective-permute-start | bytes 589832 | tf_op jit(solution)/shard_map/ppermute | solution.py:423
  64.9 19.1 %collective-permute-start.16 = (bf16[128,768]{1,0:T(8,128)(2,1)S(1)}, bf16[128,768]{1,0:T(8,128)(2,1)S(1)}, u32[]{:S(2)}, u32[]{:S(2)}) collective-permute-start(bf16[128,768]{1,0:T(8,128)(2,1)S(1)} %act.5.refs_7_.refs_1_), channel_id=1, source_target_pairs={{0,16},{1,17},{2,18},{3,19},{4,20},{5,21},{6,22},{7,23},{8,24},{9,... | collective-permute-start | bytes 589832 | tf_op jit(solution)/shard_map/ppermute | solution.py:423
  65.2 15.5 %collective-permute-start.17 = (bf16[128,1536]{1,0:T(8,128)(2,1)S(1)}, bf16[128,1536]{1,0:T(8,128)(2,1)S(1)}, u32[]{:S(2)}, u32[]{:S(2)}) collective-permute-start(bf16[128,1536]{1,0:T(8,128)(2,1)S(1)} %get-tuple-element.67), channel_id=1, source_target_pairs={{0,16},{1,17},{2,18},{3,19},{4,20},{5,21},{6,22},{7,23},{8,24},{9,... | collective-permute-start | bytes 1179656 | tf_op jit(solution)/shard_map/ppermute | solution.py:423
  70.4 14.1 %collective-permute-start.27 = (bf16[288,256]{1,0:T(8,128)(2,1)S(1)}, bf16[288,256]{1,0:T(8,128)(2,1)S(1)}, u32[]{:S(2)}, u32[]{:S(2)}) collective-permute-start(bf16[288,256]{1,0:T(8,128)(2,1)S(1)} %get-tuple-element.75), channel_id=1, source_target_pairs={{0,1},{1,0},{2,3},{3,2},{4,5},{5,4},{6,7},{7,6},{8,9},{9,8},{10,11... | collective-permute-start | bytes 442376 | tf_op jit(solution)/shard_map/ppermute | solution.py:423
  81.9 7.9 %collective-permute-start.23 = (bf16[128,768]{1,0:T(8,128)(2,1)S(1)}, bf16[128,768]{1,0:T(8,128)(2,1)S(1)}, u32[]{:S(2)}, u32[]{:S(2)}) collective-permute-start(bf16[128,768]{1,0:T(8,128)(2,1)S(1)} %act.6.refs_7_.refs_1_), channel_id=1, source_target_pairs={{0,16},{1,17},{2,18},{3,19},{4,20},{5,21},{6,22},{7,23},{8,24},{9,... | collective-permute-start | bytes 589832 | tf_op jit(solution)/shard_map/ppermute | solution.py:423
  82.2 14.7 %collective-permute-start.15 = (bf16[128,1536]{1,0:T(8,128)(2,1)S(1)}, bf16[128,1536]{1,0:T(8,128)(2,1)S(1)}, u32[]{:S(2)}, u32[]{:S(2)}) collective-permute-start(bf16[128,1536]{1,0:T(8,128)(2,1)S(1)} %get-tuple-element.66), channel_id=1, source_target_pairs={{0,16},{1,17},{2,18},{3,19},{4,20},{5,21},{6,22},{7,23},{8,24},{9,... | collective-permute-start | bytes 1179656 | tf_op jit(solution)/shard_map/ppermute | solution.py:423
  84.0 1.4 collective-permute-start.18
  84.0 5.8 %collective-permute-start.19 = (bf16[128,768]{1,0:T(8,128)(2,1)S(1)}, bf16[128,768]{1,0:T(8,128)(2,1)S(1)}, u32[]{:S(2)}, u32[]{:S(2)}) collective-permute-start(bf16[128,768]{1,0:T(8,128)(2,1)S(1)} %collective-permute-done.16.refs_2_), channel_id=1, source_target_pairs={{0,8},{1,9},{2,10},{3,11},{4,12},{5,13},{6,14},{7,15},{8,0},{9,1},... | collective-permute-start | bytes 589832 | tf_op jit(solution)/shard_map/ppermute | solution.py:423
  84.5 36.2 %collective-permute-start.28 = (bf16[288,256]{1,0:T(8,128)(2,1)S(1)}, bf16[288,256]{1,0:T(8,128)(2,1)S(1)}, u32[]{:S(2)}, u32[]{:S(2)}) collective-permute-start(bf16[288,256]{1,0:T(8,128)(2,1)S(1)} %add_convert_fusion.2), channel_id=1, source_target_pairs={{0,2},{1,3},{2,4},{3,5},{4,6},{5,7},{6,0},{7,1},{8,10},{9,11},{10,... | collective-permute-start | bytes 442376 | tf_op jit(solution)/shard_map/ppermute | solution.py:423
  85.4 13.1 %collective-permute-start.24 = (bf16[128,768]{1,0:T(8,128)(2,1)S(1)}, bf16[128,768]{1,0:T(8,128)(2,1)S(1)}, u32[]{:S(2)}, u32[]{:S(2)}) collective-permute-start(bf16[128,768]{1,0:T(8,128)(2,1)S(1)} %act.6.refs_7_.refs_1_), channel_id=1, source_target_pairs={{0,8},{1,9},{2,10},{3,11},{4,12},{5,13},{6,14},{7,15},{8,0},{9,1},... | collective-permute-start | bytes 589832 | tf_op jit(solution)/shard_map/ppermute | solution.py:423
  89.8 8.8 %collective-permute-start.25 = (bf16[128,768]{1,0:T(8,128)(2,1)S(1)}, bf16[128,768]{1,0:T(8,128)(2,1)S(1)}, u32[]{:S(2)}, u32[]{:S(2)}) collective-permute-start(bf16[128,768]{1,0:T(8,128)(2,1)S(1)} %collective-permute-done.23.refs_2_), channel_id=1, source_target_pairs={{0,8},{1,9},{2,10},{3,11},{4,12},{5,13},{6,14},{7,15},{8,0},{9,1},... | collective-permute-start | bytes 589832 | tf_op jit(solution)/shard_map/ppermute | solution.py:423
  93.2 9.4 %collective-permute-start.29 = (bf16[288,256]{1,0:T(8,128)(2,1)S(1)}, bf16[288,256]{1,0:T(8,128)(2,1)S(1)}, u32[]{:S(2)}, u32[]{:S(2)}) collective-permute-start(bf16[288,256]{1,0:T(8,128)(2,1)S(1)} %get-tuple-element.76), channel_id=1, source_target_pairs={{0,1},{1,0},{2,3},{3,2},{4,5},{5,4},{6,7},{7,6},{8,9},{9,8},{10,11... | collective-permute-start | bytes 442376 | tf_op jit(solution)/shard_map/ppermute | solution.py:423
  98.2 5.7 %collective-permute-start.20 = (bf16[128,768]{1,0:T(8,128)(2,1)S(1)}, bf16[128,768]{1,0:T(8,128)(2,1)S(1)}, u32[]{:S(2)}, u32[]{:S(2)}) collective-permute-start(bf16[128,768]{1,0:T(8,128)(2,1)S(1)} %act.7.refs_7_.refs_1_), channel_id=1, source_target_pairs={{0,16},{1,17},{2,18},{3,19},{4,20},{5,21},{6,22},{7,23},{8,24},{9,... | collective-permute-start | bytes 589832 | tf_op jit(solution)/shard_map/ppermute | solution.py:423
  102.0 5.2 %collective-permute-start.31 = (bf16[288,256]{1,0:T(8,128)(2,1)S(1)}, bf16[288,256]{1,0:T(8,128)(2,1)S(1)}, u32[]{:S(2)}, u32[]{:S(2)}) collective-permute-start(bf16[288,256]{1,0:T(8,128)(2,1)S(1)} %get-tuple-element.77), channel_id=1, source_target_pairs={{0,1},{1,0},{2,3},{3,2},{4,5},{5,4},{6,7},{7,6},{8,9},{9,8},{10,11... | collective-permute-start | bytes 442376 | tf_op jit(solution)/shard_map/ppermute | solution.py:423
  102.6 18.1 %collective-permute-start.30 = (bf16[288,256]{1,0:T(8,128)(2,1)S(1)}, bf16[288,256]{1,0:T(8,128)(2,1)S(1)}, u32[]{:S(2)}, u32[]{:S(2)}) collective-permute-start(bf16[288,256]{1,0:T(8,128)(2,1)S(1)} %add_convert_fusion.1), channel_id=1, source_target_pairs={{0,4},{1,5},{2,6},{3,7},{4,0},{5,1},{6,2},{7,3},{8,12},{9,13},{10,... | collective-permute-start | bytes 442376 | tf_op jit(solution)/shard_map/ppermute | solution.py:423
  102.7 6.6 %collective-permute-start.21 = (bf16[128,768]{1,0:T(8,128)(2,1)S(1)}, bf16[128,768]{1,0:T(8,128)(2,1)S(1)}, u32[]{:S(2)}, u32[]{:S(2)}) collective-permute-start(bf16[128,768]{1,0:T(8,128)(2,1)S(1)} %act.7.refs_7_.refs_1_), channel_id=1, source_target_pairs={{0,8},{1,9},{2,10},{3,11},{4,12},{5,13},{6,14},{7,15},{8,0},{9,1},... | collective-permute-start | bytes 589832 | tf_op jit(solution)/shard_map/ppermute | solution.py:423
  103.9 5.4 %collective-permute-start.22 = (bf16[128,768]{1,0:T(8,128)(2,1)S(1)}, bf16[128,768]{1,0:T(8,128)(2,1)S(1)}, u32[]{:S(2)}, u32[]{:S(2)}) collective-permute-start(bf16[128,768]{1,0:T(8,128)(2,1)S(1)} %collective-permute-done.20.refs_2_), channel_id=1, source_target_pairs={{0,8},{1,9},{2,10},{3,11},{4,12},{5,13},{6,14},{7,15},{8,0},{9,1},... | collective-permute-start | bytes 589832 | tf_op jit(solution)/shard_map/ppermute | solution.py:423
  107.2 6.2 %copy-start.10 = (f32[4,288]{1,0:T(4,128)S(1)}, f32[4,288]{1,0:T(4,128)}, u32[]{:S(2)}) copy-start(f32[4,288]{1,0:T(4,128)} %get-tuple-element.55) | copy-start | bytes 13828
  107.2 21.9 %copy-start.8 = (f32[2304]{0:T(1024)S(1)}, f32[2304]{0:T(1024)}, u32[]{:S(2)}) copy-start(f32[2304]{0:T(1024)} %param.19) | copy-start | bytes 27652
  107.2 22.0 %copy-start.9 = (f32[16]{0:T(128)S(1)}, f32[16]{0:T(128)}, u32[]{:S(2)}) copy-start(f32[16]{0:T(128)} %param.21) | copy-start | bytes 196
  107.3 13.5 %collective-permute-start.32 = (bf16[288,256]{1,0:T(8,128)(2,1)S(1)}, bf16[288,256]{1,0:T(8,128)(2,1)S(1)}, u32[]{:S(2)}, u32[]{:S(2)}) collective-permute-start(bf16[288,256]{1,0:T(8,128)(2,1)S(1)} %add_convert_fusion), channel_id=1, source_target_pairs={{0,6},{1,7},{2,0},{3,1},{4,2},{5,3},{6,4},{7,5},{8,14},{9,15},{10,... | collective-permute-start | bytes 442376 | tf_op jit(solution)/shard_map/ppermute | solution.py:423
  109.3 29.6 %copy-start.1 = (bf16[2304,512]{1,0:T(8,128)(2,1)S(1)}, bf16[2304,512]{1,0:T(8,128)(2,1)}, u32[]{:S(2)}) copy-start(bf16[2304,512]{1,0:T(8,128)(2,1)} %refs_2_.1) | copy-start | bytes 7077892
  112.8 30.8 %copy-start.7 = (f32[256,288]{0,1:T(8,128)S(1)}, f32[256,288]{0,1:T(8,128)}, u32[]{:S(2)}) copy-start(f32[256,288]{0,1:T(8,128)} %param.11) | copy-start | bytes 884740
  112.8 7.9 %collective-permute-start.26 = (bf16[288,256]{1,0:T(8,128)(2,1)S(1)}, bf16[288,256]{1,0:T(8,128)(2,1)S(1)}, u32[]{:S(2)}, u32[]{:S(2)}) collective-permute-start(bf16[288,256]{1,0:T(8,128)(2,1)S(1)} %get-tuple-element.74), channel_id=1, source_target_pairs={{0,1},{1,0},{2,3},{3,2},{4,5},{5,4},{6,7},{7,6},{8,9},{9,8},{10,11... | collective-permute-start | bytes 442376 | tf_op jit(solution)/shard_map/ppermute | solution.py:423
  113.4 7.3 %collective-permute-start.8 = (f32[4,288]{1,0:T(4,128)S(1)}, f32[4,288]{1,0:T(4,128)S(1)}, u32[]{:S(2)}, u32[]{:S(2)}) collective-permute-start(f32[4,288]{1,0:T(4,128)S(1)} %copy-done.10), channel_id=1, source_target_pairs={{0,0},{1,1},{2,8},{3,9},{4,16},{5,17},{6,24},{7,25},{8,2},{9,3},{1... | collective-permute-start | bytes 13832 | tf_op jit(solution)/shard_map/ppermute | solution.py:423
  121.8 17.0 %all-to-all-start = ((f32[32,4,288]{2,1,0:T(4,128)}), f32[32,4,288]{2,1,0:T(4,128)S(1)}, u32[]{:S(2)}, u32[]{:S(2)}) async-start(f32[32,4,288]{2,1,0:T(4,128)} %get-tuple-element.78), calls=%async_computation | async-start | bytes 393216 | tf_op jit(solution)/shard_map/all_to_all | solution.py:518
  124.9 14.0 %collective-permute-start.33 = (bf16[288,256]{1,0:T(8,128)(2,1)S(1)}, bf16[288,256]{1,0:T(8,128)(2,1)S(1)}, u32[]{:S(2)}, u32[]{:S(2)}) collective-permute-start(bf16[288,256]{1,0:T(8,128)(2,1)S(1)} %get-tuple-element.79), channel_id=1, source_target_pairs={{0,0},{1,1},{2,8},{3,9},{4,16},{5,17},{6,24},{7,25},{8,2},{9,3},{1... | collective-permute-start | bytes 442376 | tf_op jit(solution)/shard_map/ppermute | solution.py:423
  140.3 9.3 %all-to-all-start.1 = ((f32[32,2,16]{2,1,0:T(2,128)}), f32[32,2,16]{2,1,0:T(2,128)S(1)}, u32[]{:S(2)}, u32[]{:S(2)}) async-start(f32[32,2,16]{2,1,0:T(2,128)} %get-tuple-element.83), calls=%async_computation.1 | async-start | bytes 65536 | tf_op jit(solution)/shard_map/all_to_all | solution.py:518

commit v14 on v13

--- a/solution.py
+++ b/solution.py
@@ -490,8 +490,6 @@
 
     feeds[2] = step(feeds[1])
     feeds[3] = step(feeds[2])
-    feeds[2] = step(feeds[1])
-    feeds[3] = step(feeds[2])
     p0 = do_partial(0)
     p1 = do_partial(1, p0)
     s0 = do_sum(0, p1)
@@ -501,18 +499,18 @@
     a0 = do_act(0, s1)
     p3 = do_partial(3, a0)
     s2 = do_sum(2, p3)
+    do_hop(0, s2)
     a1 = do_act(1, s2)
-    do_hop(0, a1)
     d0 = do_down(0, a1)
     s3 = do_sum(3, d0)
+    do_hop(1, s3)
     a2 = do_act(2, s3)
-    do_hop(1, a2)
     d1 = do_down(1, a2)
     do_hop(2, None)
-    a3 = do_act(3, d1)
-    d2 = do_down(2, a3)
+    d2 = do_down(2, d1)
+    a3 = do_act(3, d2)
     do_hop(3, None)
-    d3 = do_down(3, d2)
+    d3 = do_down(3, a3)
     terms = [v for group in range(parts) for v in shares[group]]
     total, message = total_call(partial[parts - 1][2], stream, terms, dp * mp)
     exchange = lambda v: lax.all_to_all(v, ("dp", "mp"), 0, 0, tiled=True)

time: 153 us -> 148 us (0.967)
  waiting for transfers between devices: 57.1 us -> 53.1 us
    ppermute x34, waiting for transfers between devices: 51.8 us -> 47.8 us  [send(): return lax.ppermute(value, ('dp', 'mp'), pairs)]
  transfers between devices with their start and end apart: 36 -> 36, of which waited for: 15 -> 13; matrix products, arithmetic and copies ran while one was open for 1% -> 1% of each run, Pallas kernels for 28% -> 29%
where the time goes in v14:
time: 148 us; the launch traced here: 145 us
  waiting for transfers between devices  53.1 us (36%)
  Pallas kernels  46.1 us (31%)
  starting transfers between devices  37.9 us (26%)
  local copies, waits for them, and re-layouts  5.58 us (4%)
  other arithmetic  1.7 us (1%)
    ppermute x34, waiting for transfers between devices, send(): return lax.ppermute(value, ('dp', 'mp'), pairs)  47.8 us
    ppermute x34, starting transfers between devices, send(): return lax.ppermute(value, ('dp', 'mp'), pairs)  31.6 us
    pallas_call x4, Pallas kernels, partial_call(): pl.pallas_call(lambda *refs: partial_kernel(sides, len(feeds), *refs), gr...  19.4 us
    pallas_call x4, Pallas kernels, down_call(): pl.pallas_call(lambda *refs: down_kernel(sides, *refs), grid=(experts,),...  13.9 us
    all_to_all x2, starting transfers between devices, body(): exchange = lambda v: lax.all_to_all(v, ('dp', 'mp'), 0, 0, tiled=True)  6.24 us
    all_to_all x2, waiting for transfers between devices, body(): exchange = lambda v: lax.all_to_all(v, ('dp', 'mp'), 0, 0, tiled=True)  5.29 us
    pallas_call x4, Pallas kernels, act_call(): pl.pallas_call(lambda *refs: act_kernel(base, *refs), in_specs=[SMEM] + [...  4.95 us
    unnamed x22, local copies, waits for them, and re-layouts  4.05 us
  transfers between devices with their start and end apart: 36, of which 13 were waited for; matrix products, arithmetic and copies ran while one was open for 1% of the time, Pallas kernels for 29%

profile of v14, /device:TPU:4, one launch (start us, length us, event | category | flops | bytes accessed | tf_op | source)
XLA Modules:
  0.0 145.4 jit_solution(7456441362971232120)
XLA Ops:
  0.6 1.3 broadcast_in_dim.4.gain
  1.9 1.9 %prep.1 = (bf16[304,256]{1,0:T(8,128)(2,1)}, f32[4,288]{1,0:T(4,128)}) custom-call(s32[1,4]{1,0:T(1,128)} %tallies.1, f32[288,256]{1,0:T(8,128)} %bitcast.19, f32[1,288]{1,0:T(1,128)} %broadcast_in_dim.4.gain, s32[2,256]{1,0:T(2,128)} %bitcast.23), custom_call_target="tpu_custom_call" | custom-call | flops 88473 | bytes 132710 | tf_op jit(solution)/shard_map/prep/pallas_call | solution.py:75
  3.8 1.5 %collective-permute-start = (bf16[304,256]{1,0:T(8,128)(2,1)}, bf16[304,256]{1,0:T(8,128)(2,1)S(1)}, u32[]{:S(2)}, u32[]{:S(2)}) collective-permute-start(bf16[304,256]{1,0:T(8,128)(2,1)} %get-tuple-element.43), channel_id=1, source_target_pairs={{0,6},{1,7},{2,14},{3,15},{4,22},{5,23},{6,30},{7,31},{8,0},{9,1},... | collective-permute-start | bytes 466952 | tf_op jit(solution)/shard_map/ppermute | solution.py:423
  5.3 3.0 %collective-permute-start.1 = (bf16[304,256]{1,0:T(8,128)(2,1)}, bf16[304,256]{1,0:T(8,128)(2,1)S(1)}, u32[]{:S(2)}, u32[]{:S(2)}) collective-permute-start(bf16[304,256]{1,0:T(8,128)(2,1)} %get-tuple-element.43), channel_id=1, source_target_pairs={{0,7},{1,6},{2,15},{3,14},{4,23},{5,22},{6,31},{7,30},{8,1},{9,0},... | collective-permute-start | bytes 466952 | tf_op jit(solution)/shard_map/ppermute | solution.py:423
  8.5 3.8 %collective-permute-done.refs_0_ = bf16[304,256]{1,0:T(8,128)(2,1)S(1)} collective-permute-done((bf16[304,256]{1,0:T(8,128)(2,1)}, bf16[304,256]{1,0:T(8,128)(2,1)S(1)}, u32[]{:S(2)}, u32[]{:S(2)}) %collective-permute-start) | collective-permute-done | bytes 155680 | tf_op jit(solution)/shard_map/ppermute | solution.py:423
  12.3 4.3 %collective-permute-done.1.refs_1_ = bf16[304,256]{1,0:T(8,128)(2,1)S(1)} collective-permute-done((bf16[304,256]{1,0:T(8,128)(2,1)}, bf16[304,256]{1,0:T(8,128)(2,1)S(1)}, u32[]{:S(2)}, u32[]{:S(2)}) %collective-permute-start.1) | collective-permute-done | bytes 155680 | tf_op jit(solution)/shard_map/ppermute | solution.py:423
  16.5 5.9 %collective-permute-start.2 = (bf16[608,256]{1,0:T(8,128)(2,1)S(1)}, bf16[608,256]{1,0:T(8,128)(2,1)S(1)}, u32[]{:S(2)}, u32[]{:S(2)}) collective-permute-start(bf16[608,256]{1,0:T(8,128)(2,1)S(1)} %join.1.refs_1_), channel_id=1, source_target_pairs={{0,6},{1,7},{2,0},{3,1},{4,2},{5,3},{6,4},{7,5},{8,14},{9,15},{10,... | collective-permute-start | bytes 933896 | tf_op jit(solution)/shard_map/ppermute | solution.py:423
  22.5 2.0 %copy-done.2 = bf16[4,576,720]{2,1,0:T(8,128)(2,1)S(1)} copy-done((bf16[4,576,720]{2,1,0:T(8,128)(2,1)S(1)}, bf16[4,576,720]{2,1,0:T(8,128)(2,1)}, u32[]{:S(2)}) %copy-start.2) | copy-done | bytes 3317784
  24.5 2.0 %copy-done.4 = bf16[4,576,720]{2,1,0:T(8,128)(2,1)S(1)} copy-done((bf16[4,576,720]{2,1,0:T(8,128)(2,1)S(1)}, bf16[4,576,720]{2,1,0:T(8,128)(2,1)}, u32[]{:S(2)}) %copy-start.4) | copy-done | bytes 3317784
  26.5 4.9 %gate_up_partial.4 = (f32[256,1536]{1,0:T(8,128)S(1)}, bf16[256,1536]{1,0:T(8,128)(2,1)S(1)}, bf16[256,128]{1,0:T(8,128)(2,1)S(1)}) custom-call(s32[3]{0:T(128)S(1)} %pad_add_fusion.1.refs_0_, bf16[608,256]{1,0:T(8,128)(2,1)S(1)} %join.1.refs_1_, bf16[128,576]{1,0:T(8,128)(2,1)S(1)} %pad_add_fusion.refs_2_, bf16[4,576,720]{2,1,0:T(8,128)(2,1)S(1)} %copy-done.2, ...), custom_call_target="tpu_custom_call" | custom-call | flops 6794772480 | bytes 35979264 | tf_op jit(solution)/shard_map/gate_up_partial/pallas_call | solution.py:190
  31.6 4.9 %gate_up_partial.5 = (f32[256,1536]{1,0:T(8,128)S(1)}, bf16[256,1536]{1,0:T(8,128)(2,1)S(1)}, bf16[256,128]{1,0:T(8,128)(2,1)S(1)}) custom-call(s32[3]{0:T(128)S(1)} %pad_add_fusion.1.refs_0_, bf16[608,256]{1,0:T(8,128)(2,1)S(1)} %collective-permute-done.2.refs_1_, bf16[128,576]{1,0:T(8,128)(2,1)S(1)} %pad_add_fusion.refs_2_, ...), custom_call_target="tpu_custom_call" | custom-call | flops 6794772480 | bytes 35979264 | tf_op jit(solution)/shard_map/gate_up_partial/pallas_call | solution.py:190
  36.9 0.9 core_sum.4
  37.9 3.4 %collective-permute-done.3.refs_1_ = bf16[608,256]{1,0:T(8,128)(2,1)S(1)} collective-permute-done((bf16[608,256]{1,0:T(8,128)(2,1)S(1)}, bf16[608,256]{1,0:T(8,128)(2,1)S(1)}, u32[]{:S(2)}, u32[]{:S(2)}) %collective-permute-start.3) | collective-permute-done | bytes 311328 | tf_op jit(solution)/shard_map/ppermute | solution.py:423
  41.3 4.8 %gate_up_partial.6 = (f32[256,1536]{1,0:T(8,128)S(1)}, bf16[256,1536]{1,0:T(8,128)(2,1)S(1)}, bf16[256,128]{1,0:T(8,128)(2,1)S(1)}) custom-call(s32[3]{0:T(128)S(1)} %pad_add_fusion.1.refs_0_, bf16[608,256]{1,0:T(8,128)(2,1)S(1)} %collective-permute-done.3.refs_1_, bf16[128,576]{1,0:T(8,128)(2,1)S(1)} %pad_add_fusion.refs_2_, ...), custom_call_target="tpu_custom_call" | custom-call | flops 6794772480 | bytes 35979264 | tf_op jit(solution)/shard_map/gate_up_partial/pallas_call | solution.py:190
  46.1 2.1 %collective-permute-start.5 = (bf16[608,256]{1,0:T(8,128)(2,1)S(1)}, bf16[608,256]{1,0:T(8,128)(2,1)S(1)}, u32[]{:S(2)}, u32[]{:S(2)}) collective-permute-start(bf16[608,256]{1,0:T(8,128)(2,1)S(1)} %collective-permute-done.3.refs_1_), channel_id=1, source_target_pairs={{0,6},{1,7},{2,0},{3,1},{4,2},{5,3},{6,4},{7,5},{8,14},{9,15},{10,... | collective-permute-start | bytes 933896 | tf_op jit(solution)/shard_map/ppermute | solution.py:423
  48.2 0.9 core_sum.5
  49.2 1.2 act.4.refs_5_.refs_1_
  50.4 2.1 %collective-permute-start.10 = (bf16[128,768]{1,0:T(8,128)(2,1)S(1)}, bf16[128,768]{1,0:T(8,128)(2,1)S(1)}, u32[]{:S(2)}, u32[]{:S(2)}) collective-permute-start(bf16[128,768]{1,0:T(8,128)(2,1)S(1)} %act.4.refs_5_.refs_1_), channel_id=1, source_target_pairs={{0,16},{1,17},{2,18},{3,19},{4,20},{5,21},{6,22},{7,23},{8,24},{9,... | collective-permute-start | bytes 589832 | tf_op jit(solution)/shard_map/ppermute | solution.py:423
  52.5 2.6 %collective-permute-done.5.refs_1_ = bf16[608,256]{1,0:T(8,128)(2,1)S(1)} collective-permute-done((bf16[608,256]{1,0:T(8,128)(2,1)S(1)}, bf16[608,256]{1,0:T(8,128)(2,1)S(1)}, u32[]{:S(2)}, u32[]{:S(2)}) %collective-permute-start.5) | collective-permute-done | bytes 311328 | tf_op jit(solution)/shard_map/ppermute | solution.py:423
  55.1 4.8 %gate_up_partial.7 = (f32[256,1536]{1,0:T(8,128)S(1)}, bf16[256,1536]{1,0:T(8,128)(2,1)S(1)}, bf16[256,128]{1,0:T(8,128)(2,1)S(1)}) custom-call(s32[3]{0:T(128)S(1)} %pad_add_fusion.1.refs_0_, bf16[608,256]{1,0:T(8,128)(2,1)S(1)} %collective-permute-done.5.refs_1_, bf16[128,576]{1,0:T(8,128)(2,1)S(1)} %pad_add_fusion.refs_2_, ...), custom_call_target="tpu_custom_call" | custom-call | flops 6794772480 | bytes 35979264 | tf_op jit(solution)/shard_map/gate_up_partial/pallas_call | solution.py:190
  60.0 0.9 core_sum.6
  61.4 3.5 %collective-permute-done.10.refs_2_ = bf16[128,768]{1,0:T(8,128)(2,1)S(1)} collective-permute-done((bf16[128,768]{1,0:T(8,128)(2,1)S(1)}, bf16[128,768]{1,0:T(8,128)(2,1)S(1)}, u32[]{:S(2)}, u32[]{:S(2)}) %collective-permute-start.10) | collective-permute-done | bytes 196640 | tf_op jit(solution)/shard_map/ppermute | solution.py:423
  65.2 1.2 act.5.refs_7_.refs_1_
  66.4 1.8 %collective-permute-start.20 = (bf16[128,768]{1,0:T(8,128)(2,1)S(1)}, bf16[128,768]{1,0:T(8,128)(2,1)S(1)}, u32[]{:S(2)}, u32[]{:S(2)}) collective-permute-start(bf16[128,768]{1,0:T(8,128)(2,1)S(1)} %act.5.refs_7_.refs_1_), channel_id=1, source_target_pairs={{0,16},{1,17},{2,18},{3,19},{4,20},{5,21},{6,22},{7,23},{8,24},{9,... | collective-permute-start | bytes 589832 | tf_op jit(solution)/shard_map/ppermute | solution.py:423
  68.3 3.5 %down.4 = (bf16[288,256]{1,0:T(8,128)(2,1)S(1)}, bf16[288,256]{1,0:T(8,128)(2,1)S(1)}) custom-call(s32[3]{0:T(128)S(1)} %pad_add_fusion.1.refs_0_, bf16[128,768]{1,0:T(8,128)(2,1)S(1)} %act.4.refs_5_.refs_1_, bf16[128,768]{1,0:T(8,128)(2,1)S(1)} %collective-permute-done.10.refs_2_, bf16[128,768]{1,0:T(8,128)(2,1)S(1)} %collective-permute-done.12.refs_3_, ...), custom_call_target="tpu_custom_call" | custom-call | flops 3397386240 | bytes 14450688 | tf_op jit(solution)/shard_map/down/pallas_call | solution.py:306
  72.4 0.9 core_sum.7
  73.2 3.6 %collective-permute-done.16.refs_2_ = bf16[128,1536]{1,0:T(8,128)(2,1)S(1)} collective-permute-done((bf16[128,1536]{1,0:T(8,128)(2,1)S(1)}, bf16[128,1536]{1,0:T(8,128)(2,1)S(1)}, u32[]{:S(2)}, u32[]{:S(2)}) %collective-permute-start.16) | collective-permute-done | bytes 393248 | tf_op jit(solution)/shard_map/ppermute | solution.py:423
  76.8 1.2 act.6.refs_7_.refs_1_
  78.4 2.6 %collective-permute-done.20.refs_2_ = bf16[128,768]{1,0:T(8,128)(2,1)S(1)} collective-permute-done((bf16[128,768]{1,0:T(8,128)(2,1)S(1)}, bf16[128,768]{1,0:T(8,128)(2,1)S(1)}, u32[]{:S(2)}, u32[]{:S(2)}) %collective-permute-start.20) | collective-permute-done | bytes 196640 | tf_op jit(solution)/shard_map/ppermute | solution.py:423
  81.9 3.0 %collective-permute-done.17.refs_2_ = bf16[128,768]{1,0:T(8,128)(2,1)S(1)} collective-permute-done((bf16[128,768]{1,0:T(8,128)(2,1)S(1)}, bf16[128,768]{1,0:T(8,128)(2,1)S(1)}, u32[]{:S(2)}, u32[]{:S(2)}) %collective-permute-start.17) | collective-permute-done | bytes 196640 | tf_op jit(solution)/shard_map/ppermute | solution.py:423
  85.2 3.5 %down.5 = (bf16[288,256]{1,0:T(8,128)(2,1)S(1)}, bf16[288,256]{1,0:T(8,128)(2,1)S(1)}) custom-call(s32[3]{0:T(128)S(1)} %pad_add_fusion.1.refs_0_, bf16[128,768]{1,0:T(8,128)(2,1)S(1)} %act.5.refs_7_.refs_1_, bf16[128,768]{1,0:T(8,128)(2,1)S(1)} %collective-permute-done.20.refs_2_, bf16[128,768]{1,0:T(8,128)(2,1)S(1)} %collective-permute-done.21.refs_3_, ...), custom_call_target="tpu_custom_call" | custom-call | flops 3397386240 | bytes 14450688 | tf_op jit(solution)/shard_map/down/pallas_call | solution.py:306
  89.3 3.5 %down.6 = (bf16[288,256]{1,0:T(8,128)(2,1)S(1)}, bf16[288,256]{1,0:T(8,128)(2,1)S(1)}) custom-call(s32[3]{0:T(128)S(1)} %pad_add_fusion.1.refs_0_, bf16[128,768]{1,0:T(8,128)(2,1)S(1)} %act.6.refs_7_.refs_1_, bf16[128,768]{1,0:T(8,128)(2,1)S(1)} %collective-permute-done.17.refs_2_, bf16[128,768]{1,0:T(8,128)(2,1)S(1)} %collective-permute-done.18.refs_3_, ...), custom_call_target="tpu_custom_call" | custom-call | flops 3397386240 | bytes 14450688 | tf_op jit(solution)/shard_map/down/pallas_call | solution.py:306
  92.7 2.2 %collective-permute-done.15.refs_2_ = bf16[128,1536]{1,0:T(8,128)(2,1)S(1)} collective-permute-done((bf16[128,1536]{1,0:T(8,128)(2,1)S(1)}, bf16[128,1536]{1,0:T(8,128)(2,1)S(1)}, u32[]{:S(2)}, u32[]{:S(2)}) %collective-permute-start.15) | collective-permute-done | bytes 393248 | tf_op jit(solution)/shard_map/ppermute | solution.py:423
  94.9 1.2 act.7.refs_1_.refs_7_
  96.5 0.8 collective-permute-start.31
  97.5 4.4 %collective-permute-done.23.refs_2_ = bf16[128,768]{1,0:T(8,128)(2,1)S(1)} collective-permute-done((bf16[128,768]{1,0:T(8,128)(2,1)S(1)}, bf16[128,768]{1,0:T(8,128)(2,1)S(1)}, u32[]{:S(2)}, u32[]{:S(2)}) %collective-permute-start.23) | collective-permute-done | bytes 196640 | tf_op jit(solution)/shard_map/ppermute | solution.py:423
  101.9 2.3 %collective-permute-start.32 = (bf16[288,256]{1,0:T(8,128)(2,1)S(1)}, bf16[288,256]{1,0:T(8,128)(2,1)S(1)}, u32[]{:S(2)}, u32[]{:S(2)}) collective-permute-start(bf16[288,256]{1,0:T(8,128)(2,1)S(1)} %add_convert_fusion), channel_id=1, source_target_pairs={{0,6},{1,7},{2,0},{3,1},{4,2},{5,3},{6,4},{7,5},{8,14},{9,15},{10,... | collective-permute-start | bytes 442376 | tf_op jit(solution)/shard_map/ppermute | solution.py:423
  104.3 3.5 %down.7 = (bf16[288,256]{1,0:T(8,128)(2,1)S(1)}, bf16[288,256]{1,0:T(8,128)(2,1)S(1)}) custom-call(s32[3]{0:T(128)S(1)} %pad_add_fusion.1.refs_0_, bf16[128,768]{1,0:T(8,128)(2,1)S(1)} %act.7.refs_1_.refs_7_, bf16[128,768]{1,0:T(8,128)(2,1)S(1)} %collective-permute-done.23.refs_2_, bf16[128,768]{1,0:T(8,128)(2,1)S(1)} %collective-permute-done.24.refs_3_, ...), custom_call_target="tpu_custom_call" | custom-call | flops 3397386240 | bytes 14450688 | tf_op jit(solution)/shard_map/down/pallas_call | solution.py:306
  108.4 2.3 %collective-permute-start.8 = (f32[4,288]{1,0:T(4,128)S(1)}, f32[4,288]{1,0:T(4,128)S(1)}, u32[]{:S(2)}, u32[]{:S(2)}) collective-permute-start(f32[4,288]{1,0:T(4,128)S(1)} %copy-done.10), channel_id=1, source_target_pairs={{0,0},{1,1},{2,8},{3,9},{4,16},{5,17},{6,24},{7,25},{8,2},{9,3},{1... | collective-permute-start | bytes 13832 | tf_op jit(solution)/shard_map/ppermute | solution.py:423
  110.7 5.0 %collective-permute-done.8.stream = f32[4,288]{1,0:T(4,128)S(1)} collective-permute-done((f32[4,288]{1,0:T(4,128)S(1)}, f32[4,288]{1,0:T(4,128)S(1)}, u32[]{:S(2)}, u32[]{:S(2)}) %collective-permute-start.8) | collective-permute-done | bytes 4640 | tf_op jit(solution)/shard_map/ppermute | solution.py:423
  115.8 1.1 branch_total.1
  116.8 3.0 %all-to-all-start = ((f32[32,4,288]{2,1,0:T(4,128)}), f32[32,4,288]{2,1,0:T(4,128)S(1)}, u32[]{:S(2)}, u32[]{:S(2)}) async-start(f32[32,4,288]{2,1,0:T(4,128)} %get-tuple-element.78), calls=%async_computation | async-start | bytes 393216 | tf_op jit(solution)/shard_map/all_to_all | solution.py:516
  119.9 4.3 %collective-permute-start.33 = (bf16[288,256]{1,0:T(8,128)(2,1)S(1)}, bf16[288,256]{1,0:T(8,128)(2,1)S(1)}, u32[]{:S(2)}, u32[]{:S(2)}) collective-permute-start(bf16[288,256]{1,0:T(8,128)(2,1)S(1)} %get-tuple-element.79), channel_id=1, source_target_pairs={{0,0},{1,1},{2,8},{3,9},{4,16},{5,17},{6,24},{7,25},{8,2},{9,3},{1... | collective-permute-start | bytes 442376 | tf_op jit(solution)/shard_map/ppermute | solution.py:423
  124.3 9.5 %collective-permute-done.33 = bf16[288,256]{1,0:T(8,128)(2,1)S(1)} collective-permute-done((bf16[288,256]{1,0:T(8,128)(2,1)S(1)}, bf16[288,256]{1,0:T(8,128)(2,1)S(1)}, u32[]{:S(2)}, u32[]{:S(2)}) %collective-permute-start.33) | collective-permute-done | bytes 147488 | tf_op jit(solution)/shard_map/ppermute | solution.py:423
  133.9 1.4 head.1
  135.3 3.2 %all-to-all-start.1 = ((f32[32,2,16]{2,1,0:T(2,128)}), f32[32,2,16]{2,1,0:T(2,128)S(1)}, u32[]{:S(2)}, u32[]{:S(2)}) async-start(f32[32,2,16]{2,1,0:T(2,128)} %get-tuple-element.83), calls=%async_computation.1 | async-start | bytes 65536 | tf_op jit(solution)/shard_map/all_to_all | solution.py:516
  138.6 0.7 bitcast_add_fusion
  139.3 5.3 %all-to-all-done.1 = f32[32,2,16]{2,1,0:T(2,128)S(1)} async-done(((f32[32,2,16]{2,1,0:T(2,128)}), f32[32,2,16]{2,1,0:T(2,128)S(1)}, u32[]{:S(2)}, u32[]{:S(2)}) %all-to-all-start.1) | async-done | bytes 4128 | tf_op jit(solution)/shard_map/all_to_all | solution.py:516
  (81 shorter events, 6.9 us)
Async XLA Ops:
  0.6 7.7 %copy-start = (bf16[2304,4]{0,1:T(4,128)(2,1)S(1)}, bf16[2304,4]{0,1:T(4,128)(2,1)}, u32[]{:S(2)}) copy-start(bf16[2304,4]{0,1:T(4,128)(2,1)} %param.15) | copy-start | bytes 55300
  3.8 8.4 %collective-permute-start = (bf16[304,256]{1,0:T(8,128)(2,1)}, bf16[304,256]{1,0:T(8,128)(2,1)S(1)}, u32[]{:S(2)}, u32[]{:S(2)}) collective-permute-start(bf16[304,256]{1,0:T(8,128)(2,1)} %get-tuple-element.43), channel_id=1, source_target_pairs={{0,6},{1,7},{2,14},{3,15},{4,22},{5,23},{6,30},{7,31},{8,0},{9,1},... | collective-permute-start | bytes 466952 | tf_op jit(solution)/shard_map/ppermute | solution.py:423
  5.3 11.2 %collective-permute-start.1 = (bf16[304,256]{1,0:T(8,128)(2,1)}, bf16[304,256]{1,0:T(8,128)(2,1)S(1)}, u32[]{:S(2)}, u32[]{:S(2)}) collective-permute-start(bf16[304,256]{1,0:T(8,128)(2,1)} %get-tuple-element.43), channel_id=1, source_target_pairs={{0,7},{1,6},{2,15},{3,14},{4,23},{5,22},{6,31},{7,30},{8,1},{9,0},... | collective-permute-start | bytes 466952 | tf_op jit(solution)/shard_map/ppermute | solution.py:423
  16.5 14.9 %collective-permute-start.2 = (bf16[608,256]{1,0:T(8,128)(2,1)S(1)}, bf16[608,256]{1,0:T(8,128)(2,1)S(1)}, u32[]{:S(2)}, u32[]{:S(2)}) collective-permute-start(bf16[608,256]{1,0:T(8,128)(2,1)S(1)} %join.1.refs_1_), channel_id=1, source_target_pairs={{0,6},{1,7},{2,0},{3,1},{4,2},{5,3},{6,4},{7,5},{8,14},{9,15},{10,... | collective-permute-start | bytes 933896 | tf_op jit(solution)/shard_map/ppermute | solution.py:423
  22.5 2.0 %copy-start.2 = (bf16[4,576,720]{2,1,0:T(8,128)(2,1)S(1)}, bf16[4,576,720]{2,1,0:T(8,128)(2,1)}, u32[]{:S(2)}) copy-start(bf16[4,576,720]{2,1,0:T(8,128)(2,1)} %refs_3_.7) | copy-start | bytes 9953284
  24.5 2.0 %copy-start.4 = (bf16[4,576,720]{2,1,0:T(8,128)(2,1)S(1)}, bf16[4,576,720]{2,1,0:T(8,128)(2,1)}, u32[]{:S(2)}) copy-start(bf16[4,576,720]{2,1,0:T(8,128)(2,1)} %refs_4_.7) | copy-start | bytes 9953284
  26.5 5.1 %copy-start.3 = (bf16[4,576,720]{2,1,0:T(8,128)(2,1)S(1)}, bf16[4,576,720]{2,1,0:T(8,128)(2,1)}, u32[]{:S(2)}) copy-start(bf16[4,576,720]{2,1,0:T(8,128)(2,1)} %refs_3_.7) | copy-start | bytes 9953284
  26.5 5.1 %copy-start.5 = (bf16[4,576,720]{2,1,0:T(8,128)(2,1)S(1)}, bf16[4,576,720]{2,1,0:T(8,128)(2,1)}, u32[]{:S(2)}) copy-start(bf16[4,576,720]{2,1,0:T(8,128)(2,1)} %refs_4_.7) | copy-start | bytes 9953284
  31.4 5.5 %collective-permute-start.4 = (bf16[256,1536]{1,0:T(8,128)(2,1)S(1)}, bf16[256,1536]{1,0:T(8,128)(2,1)S(1)}, u32[]{:S(2)}, u32[]{:S(2)}) collective-permute-start(bf16[256,1536]{1,0:T(8,128)(2,1)S(1)} %get-tuple-element.45), channel_id=1, source_target_pairs={{0,8},{1,9},{2,10},{3,11},{4,12},{5,13},{6,14},{7,15},{8,0},{9,1},... | collective-permute-start | bytes 2359304 | tf_op jit(solution)/shard_map/ppermute | solution.py:423
  31.5 9.8 %collective-permute-start.3 = (bf16[608,256]{1,0:T(8,128)(2,1)S(1)}, bf16[608,256]{1,0:T(8,128)(2,1)S(1)}, u32[]{:S(2)}, u32[]{:S(2)}) collective-permute-start(bf16[608,256]{1,0:T(8,128)(2,1)S(1)} %collective-permute-done.2.refs_1_), channel_id=1, source_target_pairs={{0,6},{1,7},{2,0},{3,1},{4,2},{5,3},{6,4},{7,5},{8,14},{9,15},{10,... | collective-permute-start | bytes 933896 | tf_op jit(solution)/shard_map/ppermute | solution.py:423
  36.4 11.8 %collective-permute-start.7 = (bf16[256,1536]{1,0:T(8,128)(2,1)S(1)}, bf16[256,1536]{1,0:T(8,128)(2,1)S(1)}, u32[]{:S(2)}, u32[]{:S(2)}) collective-permute-start(bf16[256,1536]{1,0:T(8,128)(2,1)S(1)} %get-tuple-element.52), channel_id=1, source_target_pairs={{0,8},{1,9},{2,10},{3,11},{4,12},{5,13},{6,14},{7,15},{8,0},{9,1},... | collective-permute-start | bytes 2359304 | tf_op jit(solution)/shard_map/ppermute | solution.py:423
  37.8 11.4 %collective-permute-start.6 = (bf16[128,1536]{1,0:T(8,128)(2,1)S(1)}, bf16[128,1536]{1,0:T(8,128)(2,1)S(1)}, u32[]{:S(2)}, u32[]{:S(2)}) collective-permute-start(bf16[128,1536]{1,0:T(8,128)(2,1)S(1)} %get-tuple-element.50), channel_id=1, source_target_pairs={{0,16},{1,17},{2,18},{3,19},{4,20},{5,21},{6,22},{7,23},{8,24},{9,... | collective-permute-start | bytes 1179656 | tf_op jit(solution)/shard_map/ppermute | solution.py:423
  46.1 9.0 %collective-permute-start.5 = (bf16[608,256]{1,0:T(8,128)(2,1)S(1)}, bf16[608,256]{1,0:T(8,128)(2,1)S(1)}, u32[]{:S(2)}, u32[]{:S(2)}) collective-permute-start(bf16[608,256]{1,0:T(8,128)(2,1)S(1)} %collective-permute-done.3.refs_1_), channel_id=1, source_target_pairs={{0,6},{1,7},{2,0},{3,1},{4,2},{5,3},{6,4},{7,5},{8,14},{9,15},{10,... | collective-permute-start | bytes 933896 | tf_op jit(solution)/shard_map/ppermute | solution.py:423
  48.2 11.8 %collective-permute-start.11 = (bf16[256,1536]{1,0:T(8,128)(2,1)S(1)}, bf16[256,1536]{1,0:T(8,128)(2,1)S(1)}, u32[]{:S(2)}, u32[]{:S(2)}) collective-permute-start(bf16[256,1536]{1,0:T(8,128)(2,1)S(1)} %get-tuple-element.58), channel_id=1, source_target_pairs={{0,8},{1,9},{2,10},{3,11},{4,12},{5,13},{6,14},{7,15},{8,0},{9,1},... | collective-permute-start | bytes 2359304 | tf_op jit(solution)/shard_map/ppermute | solution.py:423
  49.1 16.1 %collective-permute-start.14 = (bf16[128,1536]{1,0:T(8,128)(2,1)S(1)}, bf16[128,1536]{1,0:T(8,128)(2,1)S(1)}, u32[]{:S(2)}, u32[]{:S(2)}) collective-permute-start(bf16[128,1536]{1,0:T(8,128)(2,1)S(1)} %get-tuple-element.62), channel_id=1, source_target_pairs={{0,16},{1,17},{2,18},{3,19},{4,20},{5,21},{6,22},{7,23},{8,24},{9,... | collective-permute-start | bytes 1179656 | tf_op jit(solution)/shard_map/ppermute | solution.py:423
  50.4 14.5 %collective-permute-start.10 = (bf16[128,768]{1,0:T(8,128)(2,1)S(1)}, bf16[128,768]{1,0:T(8,128)(2,1)S(1)}, u32[]{:S(2)}, u32[]{:S(2)}) collective-permute-start(bf16[128,768]{1,0:T(8,128)(2,1)S(1)} %act.4.refs_5_.refs_1_), channel_id=1, source_target_pairs={{0,16},{1,17},{2,18},{3,19},{4,20},{5,21},{6,22},{7,23},{8,24},{9,... | collective-permute-start | bytes 589832 | tf_op jit(solution)/shard_map/ppermute | solution.py:423
  59.9 12.5 %collective-permute-start.9 = (bf16[256,1536]{1,0:T(8,128)(2,1)S(1)}, bf16[256,1536]{1,0:T(8,128)(2,1)S(1)}, u32[]{:S(2)}, u32[]{:S(2)}) collective-permute-start(bf16[256,1536]{1,0:T(8,128)(2,1)S(1)} %get-tuple-element.57), channel_id=1, source_target_pairs={{0,8},{1,9},{2,10},{3,11},{4,12},{5,13},{6,14},{7,15},{8,0},{9,1},... | collective-permute-start | bytes 2359304 | tf_op jit(solution)/shard_map/ppermute | solution.py:423
  60.0 8.3 %copy-start.6 = (bf16[4,720,576]{1,2,0:T(8,128)(2,1)S(1)}, bf16[4,720,576]{1,2,0:T(8,128)(2,1)}, u32[]{:S(2)}) copy-start(bf16[4,720,576]{1,2,0:T(8,128)(2,1)} %param.18) | copy-start | bytes 9953284
  60.9 7.4 %collective-permute-start.12 = (bf16[128,768]{1,0:T(8,128)(2,1)S(1)}, bf16[128,768]{1,0:T(8,128)(2,1)S(1)}, u32[]{:S(2)}, u32[]{:S(2)}) collective-permute-start(bf16[128,768]{1,0:T(8,128)(2,1)S(1)} %act.4.refs_5_.refs_1_), channel_id=1, source_target_pairs={{0,8},{1,9},{2,10},{3,11},{4,12},{5,13},{6,14},{7,15},{8,0},{9,1},... | collective-permute-start | bytes 589832 | tf_op jit(solution)/shard_map/ppermute | solution.py:423
  64.9 3.3 %collective-permute-start.13 = (bf16[128,768]{1,0:T(8,128)(2,1)S(1)}, bf16[128,768]{1,0:T(8,128)(2,1)S(1)}, u32[]{:S(2)}, u32[]{:S(2)}) collective-permute-start(bf16[128,768]{1,0:T(8,128)(2,1)S(1)} %collective-permute-done.10.refs_2_), channel_id=1, source_target_pairs={{0,8},{1,9},{2,10},{3,11},{4,12},{5,13},{6,14},{7,15},{8,0},{9,1},... | collective-permute-start | bytes 589832 | tf_op jit(solution)/shard_map/ppermute | solution.py:423
  64.9 11.9 %collective-permute-start.16 = (bf16[128,1536]{1,0:T(8,128)(2,1)S(1)}, bf16[128,1536]{1,0:T(8,128)(2,1)S(1)}, u32[]{:S(2)}, u32[]{:S(2)}) collective-permute-start(bf16[128,1536]{1,0:T(8,128)(2,1)S(1)} %get-tuple-element.67), channel_id=1, source_target_pairs={{0,16},{1,17},{2,18},{3,19},{4,20},{5,21},{6,22},{7,23},{8,24},{9,... | collective-permute-start | bytes 1179656 | tf_op jit(solution)/shard_map/ppermute | solution.py:423
  66.4 14.6 %collective-permute-start.20 = (bf16[128,768]{1,0:T(8,128)(2,1)S(1)}, bf16[128,768]{1,0:T(8,128)(2,1)S(1)}, u32[]{:S(2)}, u32[]{:S(2)}) collective-permute-start(bf16[128,768]{1,0:T(8,128)(2,1)S(1)} %act.5.refs_7_.refs_1_), channel_id=1, source_target_pairs={{0,16},{1,17},{2,18},{3,19},{4,20},{5,21},{6,22},{7,23},{8,24},{9,... | collective-permute-start | bytes 589832 | tf_op jit(solution)/shard_map/ppermute | solution.py:423
  71.7 9.3 %collective-permute-start.27 = (bf16[288,256]{1,0:T(8,128)(2,1)S(1)}, bf16[288,256]{1,0:T(8,128)(2,1)S(1)}, u32[]{:S(2)}, u32[]{:S(2)}) collective-permute-start(bf16[288,256]{1,0:T(8,128)(2,1)S(1)} %get-tuple-element.75), channel_id=1, source_target_pairs={{0,1},{1,0},{2,3},{3,2},{4,5},{5,4},{6,7},{7,6},{8,9},{9,8},{10,11... | collective-permute-start | bytes 442376 | tf_op jit(solution)/shard_map/ppermute | solution.py:423
  78.1 6.8 %collective-permute-start.17 = (bf16[128,768]{1,0:T(8,128)(2,1)S(1)}, bf16[128,768]{1,0:T(8,128)(2,1)S(1)}, u32[]{:S(2)}, u32[]{:S(2)}) collective-permute-start(bf16[128,768]{1,0:T(8,128)(2,1)S(1)} %act.6.refs_7_.refs_1_), channel_id=1, source_target_pairs={{0,16},{1,17},{2,18},{3,19},{4,20},{5,21},{6,22},{7,23},{8,24},{9,... | collective-permute-start | bytes 589832 | tf_op jit(solution)/shard_map/ppermute | solution.py:423
  78.4 6.7 %collective-permute-start.21 = (bf16[128,768]{1,0:T(8,128)(2,1)S(1)}, bf16[128,768]{1,0:T(8,128)(2,1)S(1)}, u32[]{:S(2)}, u32[]{:S(2)}) collective-permute-start(bf16[128,768]{1,0:T(8,128)(2,1)S(1)} %act.5.refs_7_.refs_1_), channel_id=1, source_target_pairs={{0,8},{1,9},{2,10},{3,11},{4,12},{5,13},{6,14},{7,15},{8,0},{9,1},... | collective-permute-start | bytes 589832 | tf_op jit(solution)/shard_map/ppermute | solution.py:423
  81.0 4.1 %collective-permute-start.22 = (bf16[128,768]{1,0:T(8,128)(2,1)S(1)}, bf16[128,768]{1,0:T(8,128)(2,1)S(1)}, u32[]{:S(2)}, u32[]{:S(2)}) collective-permute-start(bf16[128,768]{1,0:T(8,128)(2,1)S(1)} %collective-permute-done.20.refs_2_), channel_id=1, source_target_pairs={{0,8},{1,9},{2,10},{3,11},{4,12},{5,13},{6,14},{7,15},{8,0},{9,1},... | collective-permute-start | bytes 589832 | tf_op jit(solution)/shard_map/ppermute | solution.py:423
  81.1 34.7 %collective-permute-start.28 = (bf16[288,256]{1,0:T(8,128)(2,1)S(1)}, bf16[288,256]{1,0:T(8,128)(2,1)S(1)}, u32[]{:S(2)}, u32[]{:S(2)}) collective-permute-start(bf16[288,256]{1,0:T(8,128)(2,1)S(1)} %add_convert_fusion.2), channel_id=1, source_target_pairs={{0,2},{1,3},{2,4},{3,5},{4,6},{5,7},{6,0},{7,1},{8,10},{9,11},{10,... | collective-permute-start | bytes 442376 | tf_op jit(solution)/shard_map/ppermute | solution.py:423
  81.3 7.9 %collective-permute-start.18 = (bf16[128,768]{1,0:T(8,128)(2,1)S(1)}, bf16[128,768]{1,0:T(8,128)(2,1)S(1)}, u32[]{:S(2)}, u32[]{:S(2)}) collective-permute-start(bf16[128,768]{1,0:T(8,128)(2,1)S(1)} %act.6.refs_7_.refs_1_), channel_id=1, source_target_pairs={{0,8},{1,9},{2,10},{3,11},{4,12},{5,13},{6,14},{7,15},{8,0},{9,1},... | collective-permute-start | bytes 589832 | tf_op jit(solution)/shard_map/ppermute | solution.py:423
  84.9 10.0 %collective-permute-start.15 = (bf16[128,1536]{1,0:T(8,128)(2,1)S(1)}, bf16[128,1536]{1,0:T(8,128)(2,1)S(1)}, u32[]{:S(2)}, u32[]{:S(2)}) collective-permute-start(bf16[128,1536]{1,0:T(8,128)(2,1)S(1)} %get-tuple-element.66), channel_id=1, source_target_pairs={{0,16},{1,17},{2,18},{3,19},{4,20},{5,21},{6,22},{7,23},{8,24},{9,... | collective-permute-start | bytes 1179656 | tf_op jit(solution)/shard_map/ppermute | solution.py:423
  85.2 4.1 %collective-permute-start.19 = (bf16[128,768]{1,0:T(8,128)(2,1)S(1)}, bf16[128,768]{1,0:T(8,128)(2,1)S(1)}, u32[]{:S(2)}, u32[]{:S(2)}) collective-permute-start(bf16[128,768]{1,0:T(8,128)(2,1)S(1)} %collective-permute-done.17.refs_2_), channel_id=1, source_target_pairs={{0,8},{1,9},{2,10},{3,11},{4,12},{5,13},{6,14},{7,15},{8,0},{9,1},... | collective-permute-start | bytes 589832 | tf_op jit(solution)/shard_map/ppermute | solution.py:423
  88.6 8.6 %collective-permute-start.29 = (bf16[288,256]{1,0:T(8,128)(2,1)S(1)}, bf16[288,256]{1,0:T(8,128)(2,1)S(1)}, u32[]{:S(2)}, u32[]{:S(2)}) collective-permute-start(bf16[288,256]{1,0:T(8,128)(2,1)S(1)} %get-tuple-element.76), channel_id=1, source_target_pairs={{0,1},{1,0},{2,3},{3,2},{4,5},{5,4},{6,7},{7,6},{8,9},{9,8},{10,11... | collective-permute-start | bytes 442376 | tf_op jit(solution)/shard_map/ppermute | solution.py:423
  96.1 5.7 %collective-permute-start.23 = (bf16[128,768]{1,0:T(8,128)(2,1)S(1)}, bf16[128,768]{1,0:T(8,128)(2,1)S(1)}, u32[]{:S(2)}, u32[]{:S(2)}) collective-permute-start(bf16[128,768]{1,0:T(8,128)(2,1)S(1)} %act.7.refs_1_.refs_7_), channel_id=1, source_target_pairs={{0,16},{1,17},{2,18},{3,19},{4,20},{5,21},{6,22},{7,23},{8,24},{9,... | collective-permute-start | bytes 589832 | tf_op jit(solution)/shard_map/ppermute | solution.py:423
  96.5 5.4 %collective-permute-start.31 = (bf16[288,256]{1,0:T(8,128)(2,1)S(1)}, bf16[288,256]{1,0:T(8,128)(2,1)S(1)}, u32[]{:S(2)}, u32[]{:S(2)}) collective-permute-start(bf16[288,256]{1,0:T(8,128)(2,1)S(1)} %get-tuple-element.77), channel_id=1, source_target_pairs={{0,1},{1,0},{2,3},{3,2},{4,5},{5,4},{6,7},{7,6},{8,9},{9,8},{10,11... | collective-permute-start | bytes 442376 | tf_op jit(solution)/shard_map/ppermute | solution.py:423
  97.3 18.4 %collective-permute-start.30 = (bf16[288,256]{1,0:T(8,128)(2,1)S(1)}, bf16[288,256]{1,0:T(8,128)(2,1)S(1)}, u32[]{:S(2)}, u32[]{:S(2)}) collective-permute-start(bf16[288,256]{1,0:T(8,128)(2,1)S(1)} %add_convert_fusion.1), channel_id=1, source_target_pairs={{0,4},{1,5},{2,6},{3,7},{4,0},{5,1},{6,2},{7,3},{8,12},{9,13},{10,... | collective-permute-start | bytes 442376 | tf_op jit(solution)/shard_map/ppermute | solution.py:423
  97.4 6.9 %collective-permute-start.24 = (bf16[128,768]{1,0:T(8,128)(2,1)S(1)}, bf16[128,768]{1,0:T(8,128)(2,1)S(1)}, u32[]{:S(2)}, u32[]{:S(2)}) collective-permute-start(bf16[128,768]{1,0:T(8,128)(2,1)S(1)} %act.7.refs_1_.refs_7_), channel_id=1, source_target_pairs={{0,8},{1,9},{2,10},{3,11},{4,12},{5,13},{6,14},{7,15},{8,0},{9,1},... | collective-permute-start | bytes 589832 | tf_op jit(solution)/shard_map/ppermute | solution.py:423
  101.9 2.4 %collective-permute-start.25 = (bf16[128,768]{1,0:T(8,128)(2,1)S(1)}, bf16[128,768]{1,0:T(8,128)(2,1)S(1)}, u32[]{:S(2)}, u32[]{:S(2)}) collective-permute-start(bf16[128,768]{1,0:T(8,128)(2,1)S(1)} %collective-permute-done.23.refs_2_), channel_id=1, source_target_pairs={{0,8},{1,9},{2,10},{3,11},{4,12},{5,13},{6,14},{7,15},{8,0},{9,1},... | collective-permute-start | bytes 589832 | tf_op jit(solution)/shard_map/ppermute | solution.py:423
  101.9 6.5 %copy-start.10 = (f32[4,288]{1,0:T(4,128)S(1)}, f32[4,288]{1,0:T(4,128)}, u32[]{:S(2)}) copy-start(f32[4,288]{1,0:T(4,128)} %get-tuple-element.55) | copy-start | bytes 13828
  101.9 22.2 %copy-start.8 = (f32[2304]{0:T(1024)S(1)}, f32[2304]{0:T(1024)}, u32[]{:S(2)}) copy-start(f32[2304]{0:T(1024)} %param.19) | copy-start | bytes 27652
  101.9 22.3 %copy-start.9 = (f32[16]{0:T(128)S(1)}, f32[16]{0:T(128)}, u32[]{:S(2)}) copy-start(f32[16]{0:T(128)} %param.21) | copy-start | bytes 196
  101.9 13.8 %collective-permute-start.32 = (bf16[288,256]{1,0:T(8,128)(2,1)S(1)}, bf16[288,256]{1,0:T(8,128)(2,1)S(1)}, u32[]{:S(2)}, u32[]{:S(2)}) collective-permute-start(bf16[288,256]{1,0:T(8,128)(2,1)S(1)} %add_convert_fusion), channel_id=1, source_target_pairs={{0,6},{1,7},{2,0},{3,1},{4,2},{5,3},{6,4},{7,5},{8,14},{9,15},{10,... | collective-permute-start | bytes 442376 | tf_op jit(solution)/shard_map/ppermute | solution.py:423
  104.3 29.6 %copy-start.1 = (bf16[2304,512]{1,0:T(8,128)(2,1)S(1)}, bf16[2304,512]{1,0:T(8,128)(2,1)}, u32[]{:S(2)}) copy-start(bf16[2304,512]{1,0:T(8,128)(2,1)} %refs_2_.1) | copy-start | bytes 7077892
  107.8 30.8 %copy-start.7 = (f32[256,288]{0,1:T(8,128)S(1)}, f32[256,288]{0,1:T(8,128)}, u32[]{:S(2)}) copy-start(f32[256,288]{0,1:T(8,128)} %param.11) | copy-start | bytes 884740
  107.8 8.0 %collective-permute-start.26 = (bf16[288,256]{1,0:T(8,128)(2,1)S(1)}, bf16[288,256]{1,0:T(8,128)(2,1)S(1)}, u32[]{:S(2)}, u32[]{:S(2)}) collective-permute-start(bf16[288,256]{1,0:T(8,128)(2,1)S(1)} %get-tuple-element.74), channel_id=1, source_target_pairs={{0,1},{1,0},{2,3},{3,2},{4,5},{5,4},{6,7},{7,6},{8,9},{9,8},{10,11... | collective-permute-start | bytes 442376 | tf_op jit(solution)/shard_map/ppermute | solution.py:423
  108.4 7.3 %collective-permute-start.8 = (f32[4,288]{1,0:T(4,128)S(1)}, f32[4,288]{1,0:T(4,128)S(1)}, u32[]{:S(2)}, u32[]{:S(2)}) collective-permute-start(f32[4,288]{1,0:T(4,128)S(1)} %copy-done.10), channel_id=1, source_target_pairs={{0,0},{1,1},{2,8},{3,9},{4,16},{5,17},{6,24},{7,25},{8,2},{9,3},{1... | collective-permute-start | bytes 13832 | tf_op jit(solution)/shard_map/ppermute | solution.py:423
  116.8 17.0 %all-to-all-start = ((f32[32,4,288]{2,1,0:T(4,128)}), f32[32,4,288]{2,1,0:T(4,128)S(1)}, u32[]{:S(2)}, u32[]{:S(2)}) async-start(f32[32,4,288]{2,1,0:T(4,128)} %get-tuple-element.78), calls=%async_computation | async-start | bytes 393216 | tf_op jit(solution)/shard_map/all_to_all | solution.py:516
  119.9 14.0 %collective-permute-start.33 = (bf16[288,256]{1,0:T(8,128)(2,1)S(1)}, bf16[288,256]{1,0:T(8,128)(2,1)S(1)}, u32[]{:S(2)}, u32[]{:S(2)}) collective-permute-start(bf16[288,256]{1,0:T(8,128)(2,1)S(1)} %get-tuple-element.79), channel_id=1, source_target_pairs={{0,0},{1,1},{2,8},{3,9},{4,16},{5,17},{6,24},{7,25},{8,2},{9,3},{1... | collective-permute-start | bytes 442376 | tf_op jit(solution)/shard_map/ppermute | solution.py:423
  135.3 9.3 %all-to-all-start.1 = ((f32[32,2,16]{2,1,0:T(2,128)}), f32[32,2,16]{2,1,0:T(2,128)S(1)}, u32[]{:S(2)}, u32[]{:S(2)}) async-start(f32[32,2,16]{2,1,0:T(2,128)} %get-tuple-element.83), calls=%async_computation.1 | async-start | bytes 65536 | tf_op jit(solution)/shard_map/all_to_all | solution.py:516

commit v15 on v14

--- a/solution.py
+++ b/solution.py
@@ -514,7 +514,8 @@
     terms = [v for group in range(parts) for v in shares[group]]
     total, message = total_call(partial[parts - 1][2], stream, terms, dp * mp)
     exchange = lambda v: lax.all_to_all(v, ("dp", "mp"), 0, 0, tiled=True)
-    got, branch = lax.optimization_barrier((exchange(message), send(total, home)))
+    got = exchange(message)
+    branch = send(total, home)
     order = [
         [(q * spread + r) * mp + group * sides + x for group in range(parts) for r in range(spread)]
         for q in range(parts)
@@ -527,6 +528,7 @@
         lexicon_projector_weights,
         softness_per_sequence[:, None],
     )
+    pairs, branch = lax.optimization_barrier((pairs, branch))
     pairs = exchange(pairs)
     new_hidden = skip_stream_arriving + branch_scale * branch.T.astype(f32)
     largest = jnp.max(pairs[:, 0], axis=0)

time: 148 us -> 147 us (level)
  waiting for transfers between devices: 53.1 us -> 51.6 us
    ppermute x34, waiting for transfers between devices: 47.8 us -> 43.1 us  [send(): return lax.ppermute(value, ('dp', 'mp'), pairs)]
    all_to_all x2, waiting for transfers between devices: 5.29 us -> 8.51 us  [body(): exchange = lambda v: lax.all_to_all(v, ('dp', 'mp'), 0, 0, tiled=True)]
  transfers between devices with their start and end apart: 36 -> 36, of which waited for: 13 -> 14; matrix products, arithmetic and copies ran while one was open for 1% -> 1% of each run, Pallas kernels for 29% -> 30%
where the time goes in v15:
time: 147 us; the launch traced here: 144 us
  waiting for transfers between devices  51.6 us (35%)
  Pallas kernels  46.1 us (31%)
  starting transfers between devices  37.9 us (26%)
  local copies, waits for them, and re-layouts  5.58 us (4%)
  other arithmetic  1.7 us (1%)
    ppermute x34, waiting for transfers between devices, send(): return lax.ppermute(value, ('dp', 'mp'), pairs)  43.1 us
    ppermute x34, starting transfers between devices, send(): return lax.ppermute(value, ('dp', 'mp'), pairs)  31.6 us
    pallas_call x4, Pallas kernels, partial_call(): pl.pallas_call(lambda *refs: partial_kernel(sides, len(feeds), *refs), gr...  19.4 us
    pallas_call x4, Pallas kernels, down_call(): pl.pallas_call(lambda *refs: down_kernel(sides, *refs), grid=(experts,),...  13.9 us
    all_to_all x2, waiting for transfers between devices, body(): exchange = lambda v: lax.all_to_all(v, ('dp', 'mp'), 0, 0, tiled=True)  8.51 us
    all_to_all x2, starting transfers between devices, body(): exchange = lambda v: lax.all_to_all(v, ('dp', 'mp'), 0, 0, tiled=True)  6.24 us
    pallas_call x4, Pallas kernels, act_call(): pl.pallas_call(lambda *refs: act_kernel(base, *refs), in_specs=[SMEM] + [...  4.95 us
    unnamed x22, local copies, waits for them, and re-layouts  4.05 us
  transfers between devices with their start and end apart: 36, of which 14 were waited for; matrix products, arithmetic and copies ran while one was open for 1% of the time, Pallas kernels for 30%

profile of v15, /device:TPU:4, one launch (start us, length us, event | category | flops | bytes accessed | tf_op | source)
XLA Modules:
  0.0 143.9 jit_solution(6536033471028505640)
XLA Ops:
  0.6 1.3 broadcast_in_dim.4.gain
  1.9 1.9 %prep.1 = (bf16[304,256]{1,0:T(8,128)(2,1)}, f32[4,288]{1,0:T(4,128)}) custom-call(s32[1,4]{1,0:T(1,128)} %tallies.1, f32[288,256]{1,0:T(8,128)} %bitcast.19, f32[1,288]{1,0:T(1,128)} %broadcast_in_dim.4.gain, s32[2,256]{1,0:T(2,128)} %bitcast.23), custom_call_target="tpu_custom_call" | custom-call | flops 88473 | bytes 132710 | tf_op jit(solution)/shard_map/prep/pallas_call | solution.py:75
  3.8 1.5 %collective-permute-start = (bf16[304,256]{1,0:T(8,128)(2,1)}, bf16[304,256]{1,0:T(8,128)(2,1)S(1)}, u32[]{:S(2)}, u32[]{:S(2)}) collective-permute-start(bf16[304,256]{1,0:T(8,128)(2,1)} %get-tuple-element.43), channel_id=1, source_target_pairs={{0,6},{1,7},{2,14},{3,15},{4,22},{5,23},{6,30},{7,31},{8,0},{9,1},... | collective-permute-start | bytes 466952 | tf_op jit(solution)/shard_map/ppermute | solution.py:423
  5.3 3.0 %collective-permute-start.1 = (bf16[304,256]{1,0:T(8,128)(2,1)}, bf16[304,256]{1,0:T(8,128)(2,1)S(1)}, u32[]{:S(2)}, u32[]{:S(2)}) collective-permute-start(bf16[304,256]{1,0:T(8,128)(2,1)} %get-tuple-element.43), channel_id=1, source_target_pairs={{0,7},{1,6},{2,15},{3,14},{4,23},{5,22},{6,31},{7,30},{8,1},{9,0},... | collective-permute-start | bytes 466952 | tf_op jit(solution)/shard_map/ppermute | solution.py:423
  8.5 3.8 %collective-permute-done.refs_0_ = bf16[304,256]{1,0:T(8,128)(2,1)S(1)} collective-permute-done((bf16[304,256]{1,0:T(8,128)(2,1)}, bf16[304,256]{1,0:T(8,128)(2,1)S(1)}, u32[]{:S(2)}, u32[]{:S(2)}) %collective-permute-start) | collective-permute-done | bytes 155680 | tf_op jit(solution)/shard_map/ppermute | solution.py:423
  12.3 4.3 %collective-permute-done.1.refs_1_ = bf16[304,256]{1,0:T(8,128)(2,1)S(1)} collective-permute-done((bf16[304,256]{1,0:T(8,128)(2,1)}, bf16[304,256]{1,0:T(8,128)(2,1)S(1)}, u32[]{:S(2)}, u32[]{:S(2)}) %collective-permute-start.1) | collective-permute-done | bytes 155680 | tf_op jit(solution)/shard_map/ppermute | solution.py:423
  16.5 5.9 %collective-permute-start.2 = (bf16[608,256]{1,0:T(8,128)(2,1)S(1)}, bf16[608,256]{1,0:T(8,128)(2,1)S(1)}, u32[]{:S(2)}, u32[]{:S(2)}) collective-permute-start(bf16[608,256]{1,0:T(8,128)(2,1)S(1)} %join.1.refs_1_), channel_id=1, source_target_pairs={{0,6},{1,7},{2,0},{3,1},{4,2},{5,3},{6,4},{7,5},{8,14},{9,15},{10,... | collective-permute-start | bytes 933896 | tf_op jit(solution)/shard_map/ppermute | solution.py:423
  22.5 2.0 %copy-done.2 = bf16[4,576,720]{2,1,0:T(8,128)(2,1)S(1)} copy-done((bf16[4,576,720]{2,1,0:T(8,128)(2,1)S(1)}, bf16[4,576,720]{2,1,0:T(8,128)(2,1)}, u32[]{:S(2)}) %copy-start.2) | copy-done | bytes 3317784
  24.5 2.0 %copy-done.4 = bf16[4,576,720]{2,1,0:T(8,128)(2,1)S(1)} copy-done((bf16[4,576,720]{2,1,0:T(8,128)(2,1)S(1)}, bf16[4,576,720]{2,1,0:T(8,128)(2,1)}, u32[]{:S(2)}) %copy-start.4) | copy-done | bytes 3317784
  26.5 4.9 %gate_up_partial.4 = (f32[256,1536]{1,0:T(8,128)S(1)}, bf16[256,1536]{1,0:T(8,128)(2,1)S(1)}, bf16[256,128]{1,0:T(8,128)(2,1)S(1)}) custom-call(s32[3]{0:T(128)S(1)} %pad_add_fusion.1.refs_0_, bf16[608,256]{1,0:T(8,128)(2,1)S(1)} %join.1.refs_1_, bf16[128,576]{1,0:T(8,128)(2,1)S(1)} %pad_add_fusion.refs_2_, bf16[4,576,720]{2,1,0:T(8,128)(2,1)S(1)} %copy-done.2, ...), custom_call_target="tpu_custom_call" | custom-call | flops 6794772480 | bytes 35979264 | tf_op jit(solution)/shard_map/gate_up_partial/pallas_call | solution.py:190
  31.6 4.9 %gate_up_partial.5 = (f32[256,1536]{1,0:T(8,128)S(1)}, bf16[256,1536]{1,0:T(8,128)(2,1)S(1)}, bf16[256,128]{1,0:T(8,128)(2,1)S(1)}) custom-call(s32[3]{0:T(128)S(1)} %pad_add_fusion.1.refs_0_, bf16[608,256]{1,0:T(8,128)(2,1)S(1)} %collective-permute-done.2.refs_1_, bf16[128,576]{1,0:T(8,128)(2,1)S(1)} %pad_add_fusion.refs_2_, ...), custom_call_target="tpu_custom_call" | custom-call | flops 6794772480 | bytes 35979264 | tf_op jit(solution)/shard_map/gate_up_partial/pallas_call | solution.py:190
  36.9 0.9 core_sum.4
  37.9 3.4 %collective-permute-done.3.refs_1_ = bf16[608,256]{1,0:T(8,128)(2,1)S(1)} collective-permute-done((bf16[608,256]{1,0:T(8,128)(2,1)S(1)}, bf16[608,256]{1,0:T(8,128)(2,1)S(1)}, u32[]{:S(2)}, u32[]{:S(2)}) %collective-permute-start.3) | collective-permute-done | bytes 311328 | tf_op jit(solution)/shard_map/ppermute | solution.py:423
  41.3 4.8 %gate_up_partial.6 = (f32[256,1536]{1,0:T(8,128)S(1)}, bf16[256,1536]{1,0:T(8,128)(2,1)S(1)}, bf16[256,128]{1,0:T(8,128)(2,1)S(1)}) custom-call(s32[3]{0:T(128)S(1)} %pad_add_fusion.1.refs_0_, bf16[608,256]{1,0:T(8,128)(2,1)S(1)} %collective-permute-done.3.refs_1_, bf16[128,576]{1,0:T(8,128)(2,1)S(1)} %pad_add_fusion.refs_2_, ...), custom_call_target="tpu_custom_call" | custom-call | flops 6794772480 | bytes 35979264 | tf_op jit(solution)/shard_map/gate_up_partial/pallas_call | solution.py:190
  46.1 2.1 %collective-permute-start.5 = (bf16[608,256]{1,0:T(8,128)(2,1)S(1)}, bf16[608,256]{1,0:T(8,128)(2,1)S(1)}, u32[]{:S(2)}, u32[]{:S(2)}) collective-permute-start(bf16[608,256]{1,0:T(8,128)(2,1)S(1)} %collective-permute-done.3.refs_1_), channel_id=1, source_target_pairs={{0,6},{1,7},{2,0},{3,1},{4,2},{5,3},{6,4},{7,5},{8,14},{9,15},{10,... | collective-permute-start | bytes 933896 | tf_op jit(solution)/shard_map/ppermute | solution.py:423
  48.2 0.9 core_sum.5
  49.2 1.2 act.4.refs_5_.refs_1_
  50.4 2.1 %collective-permute-start.10 = (bf16[128,768]{1,0:T(8,128)(2,1)S(1)}, bf16[128,768]{1,0:T(8,128)(2,1)S(1)}, u32[]{:S(2)}, u32[]{:S(2)}) collective-permute-start(bf16[128,768]{1,0:T(8,128)(2,1)S(1)} %act.4.refs_5_.refs_1_), channel_id=1, source_target_pairs={{0,16},{1,17},{2,18},{3,19},{4,20},{5,21},{6,22},{7,23},{8,24},{9,... | collective-permute-start | bytes 589832 | tf_op jit(solution)/shard_map/ppermute | solution.py:423
  52.5 2.6 %collective-permute-done.5.refs_1_ = bf16[608,256]{1,0:T(8,128)(2,1)S(1)} collective-permute-done((bf16[608,256]{1,0:T(8,128)(2,1)S(1)}, bf16[608,256]{1,0:T(8,128)(2,1)S(1)}, u32[]{:S(2)}, u32[]{:S(2)}) %collective-permute-start.5) | collective-permute-done | bytes 311328 | tf_op jit(solution)/shard_map/ppermute | solution.py:423
  55.1 4.8 %gate_up_partial.7 = (f32[256,1536]{1,0:T(8,128)S(1)}, bf16[256,1536]{1,0:T(8,128)(2,1)S(1)}, bf16[256,128]{1,0:T(8,128)(2,1)S(1)}) custom-call(s32[3]{0:T(128)S(1)} %pad_add_fusion.1.refs_0_, bf16[608,256]{1,0:T(8,128)(2,1)S(1)} %collective-permute-done.5.refs_1_, bf16[128,576]{1,0:T(8,128)(2,1)S(1)} %pad_add_fusion.refs_2_, ...), custom_call_target="tpu_custom_call" | custom-call | flops 6794772480 | bytes 35979264 | tf_op jit(solution)/shard_map/gate_up_partial/pallas_call | solution.py:190
  60.0 0.9 core_sum.6
  61.4 3.5 %collective-permute-done.10.refs_2_ = bf16[128,768]{1,0:T(8,128)(2,1)S(1)} collective-permute-done((bf16[128,768]{1,0:T(8,128)(2,1)S(1)}, bf16[128,768]{1,0:T(8,128)(2,1)S(1)}, u32[]{:S(2)}, u32[]{:S(2)}) %collective-permute-start.10) | collective-permute-done | bytes 196640 | tf_op jit(solution)/shard_map/ppermute | solution.py:423
  65.2 1.2 act.5.refs_7_.refs_1_
  66.4 1.8 %collective-permute-start.20 = (bf16[128,768]{1,0:T(8,128)(2,1)S(1)}, bf16[128,768]{1,0:T(8,128)(2,1)S(1)}, u32[]{:S(2)}, u32[]{:S(2)}) collective-permute-start(bf16[128,768]{1,0:T(8,128)(2,1)S(1)} %act.5.refs_7_.refs_1_), channel_id=1, source_target_pairs={{0,16},{1,17},{2,18},{3,19},{4,20},{5,21},{6,22},{7,23},{8,24},{9,... | collective-permute-start | bytes 589832 | tf_op jit(solution)/shard_map/ppermute | solution.py:423
  68.3 3.5 %down.4 = (bf16[288,256]{1,0:T(8,128)(2,1)S(1)}, bf16[288,256]{1,0:T(8,128)(2,1)S(1)}) custom-call(s32[3]{0:T(128)S(1)} %pad_add_fusion.1.refs_0_, bf16[128,768]{1,0:T(8,128)(2,1)S(1)} %act.4.refs_5_.refs_1_, bf16[128,768]{1,0:T(8,128)(2,1)S(1)} %collective-permute-done.10.refs_2_, bf16[128,768]{1,0:T(8,128)(2,1)S(1)} %collective-permute-done.12.refs_3_, ...), custom_call_target="tpu_custom_call" | custom-call | flops 3397386240 | bytes 14450688 | tf_op jit(solution)/shard_map/down/pallas_call | solution.py:306
  72.4 0.9 core_sum.7
  73.2 3.6 %collective-permute-done.16.refs_2_ = bf16[128,1536]{1,0:T(8,128)(2,1)S(1)} collective-permute-done((bf16[128,1536]{1,0:T(8,128)(2,1)S(1)}, bf16[128,1536]{1,0:T(8,128)(2,1)S(1)}, u32[]{:S(2)}, u32[]{:S(2)}) %collective-permute-start.16) | collective-permute-done | bytes 393248 | tf_op jit(solution)/shard_map/ppermute | solution.py:423
  76.8 1.2 act.6.refs_7_.refs_1_
  78.4 2.6 %collective-permute-done.20.refs_2_ = bf16[128,768]{1,0:T(8,128)(2,1)S(1)} collective-permute-done((bf16[128,768]{1,0:T(8,128)(2,1)S(1)}, bf16[128,768]{1,0:T(8,128)(2,1)S(1)}, u32[]{:S(2)}, u32[]{:S(2)}) %collective-permute-start.20) | collective-permute-done | bytes 196640 | tf_op jit(solution)/shard_map/ppermute | solution.py:423
  81.9 3.0 %collective-permute-done.17.refs_2_ = bf16[128,768]{1,0:T(8,128)(2,1)S(1)} collective-permute-done((bf16[128,768]{1,0:T(8,128)(2,1)S(1)}, bf16[128,768]{1,0:T(8,128)(2,1)S(1)}, u32[]{:S(2)}, u32[]{:S(2)}) %collective-permute-start.17) | collective-permute-done | bytes 196640 | tf_op jit(solution)/shard_map/ppermute | solution.py:423
  85.2 3.5 %down.5 = (bf16[288,256]{1,0:T(8,128)(2,1)S(1)}, bf16[288,256]{1,0:T(8,128)(2,1)S(1)}) custom-call(s32[3]{0:T(128)S(1)} %pad_add_fusion.1.refs_0_, bf16[128,768]{1,0:T(8,128)(2,1)S(1)} %act.5.refs_7_.refs_1_, bf16[128,768]{1,0:T(8,128)(2,1)S(1)} %collective-permute-done.20.refs_2_, bf16[128,768]{1,0:T(8,128)(2,1)S(1)} %collective-permute-done.21.refs_3_, ...), custom_call_target="tpu_custom_call" | custom-call | flops 3397386240 | bytes 14450688 | tf_op jit(solution)/shard_map/down/pallas_call | solution.py:306
  89.3 3.5 %down.6 = (bf16[288,256]{1,0:T(8,128)(2,1)S(1)}, bf16[288,256]{1,0:T(8,128)(2,1)S(1)}) custom-call(s32[3]{0:T(128)S(1)} %pad_add_fusion.1.refs_0_, bf16[128,768]{1,0:T(8,128)(2,1)S(1)} %act.6.refs_7_.refs_1_, bf16[128,768]{1,0:T(8,128)(2,1)S(1)} %collective-permute-done.17.refs_2_, bf16[128,768]{1,0:T(8,128)(2,1)S(1)} %collective-permute-done.18.refs_3_, ...), custom_call_target="tpu_custom_call" | custom-call | flops 3397386240 | bytes 14450688 | tf_op jit(solution)/shard_map/down/pallas_call | solution.py:306
  92.7 2.2 %collective-permute-done.15.refs_2_ = bf16[128,1536]{1,0:T(8,128)(2,1)S(1)} collective-permute-done((bf16[128,1536]{1,0:T(8,128)(2,1)S(1)}, bf16[128,1536]{1,0:T(8,128)(2,1)S(1)}, u32[]{:S(2)}, u32[]{:S(2)}) %collective-permute-start.15) | collective-permute-done | bytes 393248 | tf_op jit(solution)/shard_map/ppermute | solution.py:423
  94.9 1.2 act.7.refs_1_.refs_7_
  96.5 0.8 collective-permute-start.31
  97.5 4.4 %collective-permute-done.23.refs_2_ = bf16[128,768]{1,0:T(8,128)(2,1)S(1)} collective-permute-done((bf16[128,768]{1,0:T(8,128)(2,1)S(1)}, bf16[128,768]{1,0:T(8,128)(2,1)S(1)}, u32[]{:S(2)}, u32[]{:S(2)}) %collective-permute-start.23) | collective-permute-done | bytes 196640 | tf_op jit(solution)/shard_map/ppermute | solution.py:423
  101.9 2.3 %collective-permute-start.32 = (bf16[288,256]{1,0:T(8,128)(2,1)S(1)}, bf16[288,256]{1,0:T(8,128)(2,1)S(1)}, u32[]{:S(2)}, u32[]{:S(2)}) collective-permute-start(bf16[288,256]{1,0:T(8,128)(2,1)S(1)} %add_convert_fusion), channel_id=1, source_target_pairs={{0,6},{1,7},{2,0},{3,1},{4,2},{5,3},{6,4},{7,5},{8,14},{9,15},{10,... | collective-permute-start | bytes 442376 | tf_op jit(solution)/shard_map/ppermute | solution.py:423
  104.3 3.5 %down.7 = (bf16[288,256]{1,0:T(8,128)(2,1)S(1)}, bf16[288,256]{1,0:T(8,128)(2,1)S(1)}) custom-call(s32[3]{0:T(128)S(1)} %pad_add_fusion.1.refs_0_, bf16[128,768]{1,0:T(8,128)(2,1)S(1)} %act.7.refs_1_.refs_7_, bf16[128,768]{1,0:T(8,128)(2,1)S(1)} %collective-permute-done.23.refs_2_, bf16[128,768]{1,0:T(8,128)(2,1)S(1)} %collective-permute-done.24.refs_3_, ...), custom_call_target="tpu_custom_call" | custom-call | flops 3397386240 | bytes 14450688 | tf_op jit(solution)/shard_map/down/pallas_call | solution.py:306
  108.4 2.3 %collective-permute-start.8 = (f32[4,288]{1,0:T(4,128)S(1)}, f32[4,288]{1,0:T(4,128)S(1)}, u32[]{:S(2)}, u32[]{:S(2)}) collective-permute-start(f32[4,288]{1,0:T(4,128)S(1)} %copy-done.10), channel_id=1, source_target_pairs={{0,0},{1,1},{2,8},{3,9},{4,16},{5,17},{6,24},{7,25},{8,2},{9,3},{1... | collective-permute-start | bytes 13832 | tf_op jit(solution)/shard_map/ppermute | solution.py:423
  110.7 5.0 %collective-permute-done.8.stream = f32[4,288]{1,0:T(4,128)S(1)} collective-permute-done((f32[4,288]{1,0:T(4,128)S(1)}, f32[4,288]{1,0:T(4,128)S(1)}, u32[]{:S(2)}, u32[]{:S(2)}) %collective-permute-start.8) | collective-permute-done | bytes 4640 | tf_op jit(solution)/shard_map/ppermute | solution.py:423
  115.8 1.1 branch_total.1
  116.8 3.0 %all-to-all-start = ((f32[32,4,288]{2,1,0:T(4,128)}), f32[32,4,288]{2,1,0:T(4,128)S(1)}, u32[]{:S(2)}, u32[]{:S(2)}) async-start(f32[32,4,288]{2,1,0:T(4,128)} %get-tuple-element.78), calls=%async_computation | async-start | bytes 393216 | tf_op jit(solution)/shard_map/all_to_all | solution.py:516
  119.9 4.3 %collective-permute-start.33 = (bf16[288,256]{1,0:T(8,128)(2,1)S(1)}, bf16[288,256]{1,0:T(8,128)(2,1)S(1)}, u32[]{:S(2)}, u32[]{:S(2)}) collective-permute-start(bf16[288,256]{1,0:T(8,128)(2,1)S(1)} %get-tuple-element.80), channel_id=1, source_target_pairs={{0,0},{1,1},{2,8},{3,9},{4,16},{5,17},{6,24},{7,25},{8,2},{9,3},{1... | collective-permute-start | bytes 442376 | tf_op jit(solution)/shard_map/ppermute | solution.py:423
  124.3 3.2 %all-to-all-done.refs_0_ = f32[32,4,288]{2,1,0:T(4,128)S(1)} async-done(((f32[32,4,288]{2,1,0:T(4,128)}), f32[32,4,288]{2,1,0:T(4,128)S(1)}, u32[]{:S(2)}, u32[]{:S(2)}) %all-to-all-start) | async-done | bytes 147488 | tf_op jit(solution)/shard_map/all_to_all | solution.py:516
  127.6 1.4 head.1
  129.0 4.9 %collective-permute-done.33 = bf16[288,256]{1,0:T(8,128)(2,1)S(1)} collective-permute-done((bf16[288,256]{1,0:T(8,128)(2,1)S(1)}, bf16[288,256]{1,0:T(8,128)(2,1)S(1)}, u32[]{:S(2)}, u32[]{:S(2)}) %collective-permute-start.33) | collective-permute-done | bytes 147488 | tf_op jit(solution)/shard_map/ppermute | solution.py:423
  133.9 3.2 %all-to-all-start.1 = ((f32[32,2,16]{2,1,0:T(2,128)}), f32[32,2,16]{2,1,0:T(2,128)S(1)}, u32[]{:S(2)}, u32[]{:S(2)}) async-start(f32[32,2,16]{2,1,0:T(2,128)} %get-tuple-element.83), calls=%async_computation.1 | async-start | bytes 65536 | tf_op jit(solution)/shard_map/all_to_all | solution.py:516
  137.9 5.3 %all-to-all-done.1 = f32[32,2,16]{2,1,0:T(2,128)S(1)} async-done(((f32[32,2,16]{2,1,0:T(2,128)}), f32[32,2,16]{2,1,0:T(2,128)S(1)}, u32[]{:S(2)}, u32[]{:S(2)}) %all-to-all-start.1) | async-done | bytes 4128 | tf_op jit(solution)/shard_map/all_to_all | solution.py:516
  (81 shorter events, 7.6 us)
Async XLA Ops:
  0.6 7.7 %copy-start = (bf16[2304,4]{0,1:T(4,128)(2,1)S(1)}, bf16[2304,4]{0,1:T(4,128)(2,1)}, u32[]{:S(2)}) copy-start(bf16[2304,4]{0,1:T(4,128)(2,1)} %param.15) | copy-start | bytes 55300
  3.8 8.4 %collective-permute-start = (bf16[304,256]{1,0:T(8,128)(2,1)}, bf16[304,256]{1,0:T(8,128)(2,1)S(1)}, u32[]{:S(2)}, u32[]{:S(2)}) collective-permute-start(bf16[304,256]{1,0:T(8,128)(2,1)} %get-tuple-element.43), channel_id=1, source_target_pairs={{0,6},{1,7},{2,14},{3,15},{4,22},{5,23},{6,30},{7,31},{8,0},{9,1},... | collective-permute-start | bytes 466952 | tf_op jit(solution)/shard_map/ppermute | solution.py:423
  5.3 11.2 %collective-permute-start.1 = (bf16[304,256]{1,0:T(8,128)(2,1)}, bf16[304,256]{1,0:T(8,128)(2,1)S(1)}, u32[]{:S(2)}, u32[]{:S(2)}) collective-permute-start(bf16[304,256]{1,0:T(8,128)(2,1)} %get-tuple-element.43), channel_id=1, source_target_pairs={{0,7},{1,6},{2,15},{3,14},{4,23},{5,22},{6,31},{7,30},{8,1},{9,0},... | collective-permute-start | bytes 466952 | tf_op jit(solution)/shard_map/ppermute | solution.py:423
  16.5 14.9 %collective-permute-start.2 = (bf16[608,256]{1,0:T(8,128)(2,1)S(1)}, bf16[608,256]{1,0:T(8,128)(2,1)S(1)}, u32[]{:S(2)}, u32[]{:S(2)}) collective-permute-start(bf16[608,256]{1,0:T(8,128)(2,1)S(1)} %join.1.refs_1_), channel_id=1, source_target_pairs={{0,6},{1,7},{2,0},{3,1},{4,2},{5,3},{6,4},{7,5},{8,14},{9,15},{10,... | collective-permute-start | bytes 933896 | tf_op jit(solution)/shard_map/ppermute | solution.py:423
  22.5 2.0 %copy-start.2 = (bf16[4,576,720]{2,1,0:T(8,128)(2,1)S(1)}, bf16[4,576,720]{2,1,0:T(8,128)(2,1)}, u32[]{:S(2)}) copy-start(bf16[4,576,720]{2,1,0:T(8,128)(2,1)} %refs_3_.7) | copy-start | bytes 9953284
  24.5 2.0 %copy-start.4 = (bf16[4,576,720]{2,1,0:T(8,128)(2,1)S(1)}, bf16[4,576,720]{2,1,0:T(8,128)(2,1)}, u32[]{:S(2)}) copy-start(bf16[4,576,720]{2,1,0:T(8,128)(2,1)} %refs_4_.7) | copy-start | bytes 9953284
  26.5 5.1 %copy-start.3 = (bf16[4,576,720]{2,1,0:T(8,128)(2,1)S(1)}, bf16[4,576,720]{2,1,0:T(8,128)(2,1)}, u32[]{:S(2)}) copy-start(bf16[4,576,720]{2,1,0:T(8,128)(2,1)} %refs_3_.7) | copy-start | bytes 9953284
  26.5 5.1 %copy-start.5 = (bf16[4,576,720]{2,1,0:T(8,128)(2,1)S(1)}, bf16[4,576,720]{2,1,0:T(8,128)(2,1)}, u32[]{:S(2)}) copy-start(bf16[4,576,720]{2,1,0:T(8,128)(2,1)} %refs_4_.7) | copy-start | bytes 9953284
  31.4 5.5 %collective-permute-start.4 = (bf16[256,1536]{1,0:T(8,128)(2,1)S(1)}, bf16[256,1536]{1,0:T(8,128)(2,1)S(1)}, u32[]{:S(2)}, u32[]{:S(2)}) collective-permute-start(bf16[256,1536]{1,0:T(8,128)(2,1)S(1)} %get-tuple-element.45), channel_id=1, source_target_pairs={{0,8},{1,9},{2,10},{3,11},{4,12},{5,13},{6,14},{7,15},{8,0},{9,1},... | collective-permute-start | bytes 2359304 | tf_op jit(solution)/shard_map/ppermute | solution.py:423
  31.5 9.8 %collective-permute-start.3 = (bf16[608,256]{1,0:T(8,128)(2,1)S(1)}, bf16[608,256]{1,0:T(8,128)(2,1)S(1)}, u32[]{:S(2)}, u32[]{:S(2)}) collective-permute-start(bf16[608,256]{1,0:T(8,128)(2,1)S(1)} %collective-permute-done.2.refs_1_), channel_id=1, source_target_pairs={{0,6},{1,7},{2,0},{3,1},{4,2},{5,3},{6,4},{7,5},{8,14},{9,15},{10,... | collective-permute-start | bytes 933896 | tf_op jit(solution)/shard_map/ppermute | solution.py:423
  36.4 11.8 %collective-permute-start.7 = (bf16[256,1536]{1,0:T(8,128)(2,1)S(1)}, bf16[256,1536]{1,0:T(8,128)(2,1)S(1)}, u32[]{:S(2)}, u32[]{:S(2)}) collective-permute-start(bf16[256,1536]{1,0:T(8,128)(2,1)S(1)} %get-tuple-element.52), channel_id=1, source_target_pairs={{0,8},{1,9},{2,10},{3,11},{4,12},{5,13},{6,14},{7,15},{8,0},{9,1},... | collective-permute-start | bytes 2359304 | tf_op jit(solution)/shard_map/ppermute | solution.py:423
  37.8 11.4 %collective-permute-start.6 = (bf16[128,1536]{1,0:T(8,128)(2,1)S(1)}, bf16[128,1536]{1,0:T(8,128)(2,1)S(1)}, u32[]{:S(2)}, u32[]{:S(2)}) collective-permute-start(bf16[128,1536]{1,0:T(8,128)(2,1)S(1)} %get-tuple-element.50), channel_id=1, source_target_pairs={{0,16},{1,17},{2,18},{3,19},{4,20},{5,21},{6,22},{7,23},{8,24},{9,... | collective-permute-start | bytes 1179656 | tf_op jit(solution)/shard_map/ppermute | solution.py:423
  46.1 9.0 %collective-permute-start.5 = (bf16[608,256]{1,0:T(8,128)(2,1)S(1)}, bf16[608,256]{1,0:T(8,128)(2,1)S(1)}, u32[]{:S(2)}, u32[]{:S(2)}) collective-permute-start(bf16[608,256]{1,0:T(8,128)(2,1)S(1)} %collective-permute-done.3.refs_1_), channel_id=1, source_target_pairs={{0,6},{1,7},{2,0},{3,1},{4,2},{5,3},{6,4},{7,5},{8,14},{9,15},{10,... | collective-permute-start | bytes 933896 | tf_op jit(solution)/shard_map/ppermute | solution.py:423
  48.2 11.8 %collective-permute-start.11 = (bf16[256,1536]{1,0:T(8,128)(2,1)S(1)}, bf16[256,1536]{1,0:T(8,128)(2,1)S(1)}, u32[]{:S(2)}, u32[]{:S(2)}) collective-permute-start(bf16[256,1536]{1,0:T(8,128)(2,1)S(1)} %get-tuple-element.58), channel_id=1, source_target_pairs={{0,8},{1,9},{2,10},{3,11},{4,12},{5,13},{6,14},{7,15},{8,0},{9,1},... | collective-permute-start | bytes 2359304 | tf_op jit(solution)/shard_map/ppermute | solution.py:423
  49.1 16.1 %collective-permute-start.14 = (bf16[128,1536]{1,0:T(8,128)(2,1)S(1)}, bf16[128,1536]{1,0:T(8,128)(2,1)S(1)}, u32[]{:S(2)}, u32[]{:S(2)}) collective-permute-start(bf16[128,1536]{1,0:T(8,128)(2,1)S(1)} %get-tuple-element.62), channel_id=1, source_target_pairs={{0,16},{1,17},{2,18},{3,19},{4,20},{5,21},{6,22},{7,23},{8,24},{9,... | collective-permute-start | bytes 1179656 | tf_op jit(solution)/shard_map/ppermute | solution.py:423
  50.4 14.5 %collective-permute-start.10 = (bf16[128,768]{1,0:T(8,128)(2,1)S(1)}, bf16[128,768]{1,0:T(8,128)(2,1)S(1)}, u32[]{:S(2)}, u32[]{:S(2)}) collective-permute-start(bf16[128,768]{1,0:T(8,128)(2,1)S(1)} %act.4.refs_5_.refs_1_), channel_id=1, source_target_pairs={{0,16},{1,17},{2,18},{3,19},{4,20},{5,21},{6,22},{7,23},{8,24},{9,... | collective-permute-start | bytes 589832 | tf_op jit(solution)/shard_map/ppermute | solution.py:423
  59.9 12.5 %collective-permute-start.9 = (bf16[256,1536]{1,0:T(8,128)(2,1)S(1)}, bf16[256,1536]{1,0:T(8,128)(2,1)S(1)}, u32[]{:S(2)}, u32[]{:S(2)}) collective-permute-start(bf16[256,1536]{1,0:T(8,128)(2,1)S(1)} %get-tuple-element.57), channel_id=1, source_target_pairs={{0,8},{1,9},{2,10},{3,11},{4,12},{5,13},{6,14},{7,15},{8,0},{9,1},... | collective-permute-start | bytes 2359304 | tf_op jit(solution)/shard_map/ppermute | solution.py:423
  60.0 8.3 %copy-start.6 = (bf16[4,720,576]{1,2,0:T(8,128)(2,1)S(1)}, bf16[4,720,576]{1,2,0:T(8,128)(2,1)}, u32[]{:S(2)}) copy-start(bf16[4,720,576]{1,2,0:T(8,128)(2,1)} %param.18) | copy-start | bytes 9953284
  60.9 7.4 %collective-permute-start.12 = (bf16[128,768]{1,0:T(8,128)(2,1)S(1)}, bf16[128,768]{1,0:T(8,128)(2,1)S(1)}, u32[]{:S(2)}, u32[]{:S(2)}) collective-permute-start(bf16[128,768]{1,0:T(8,128)(2,1)S(1)} %act.4.refs_5_.refs_1_), channel_id=1, source_target_pairs={{0,8},{1,9},{2,10},{3,11},{4,12},{5,13},{6,14},{7,15},{8,0},{9,1},... | collective-permute-start | bytes 589832 | tf_op jit(solution)/shard_map/ppermute | solution.py:423
  64.9 3.3 %collective-permute-start.13 = (bf16[128,768]{1,0:T(8,128)(2,1)S(1)}, bf16[128,768]{1,0:T(8,128)(2,1)S(1)}, u32[]{:S(2)}, u32[]{:S(2)}) collective-permute-start(bf16[128,768]{1,0:T(8,128)(2,1)S(1)} %collective-permute-done.10.refs_2_), channel_id=1, source_target_pairs={{0,8},{1,9},{2,10},{3,11},{4,12},{5,13},{6,14},{7,15},{8,0},{9,1},... | collective-permute-start | bytes 589832 | tf_op jit(solution)/shard_map/ppermute | solution.py:423
  64.9 11.9 %collective-permute-start.16 = (bf16[128,1536]{1,0:T(8,128)(2,1)S(1)}, bf16[128,1536]{1,0:T(8,128)(2,1)S(1)}, u32[]{:S(2)}, u32[]{:S(2)}) collective-permute-start(bf16[128,1536]{1,0:T(8,128)(2,1)S(1)} %get-tuple-element.67), channel_id=1, source_target_pairs={{0,16},{1,17},{2,18},{3,19},{4,20},{5,21},{6,22},{7,23},{8,24},{9,... | collective-permute-start | bytes 1179656 | tf_op jit(solution)/shard_map/ppermute | solution.py:423
  66.4 14.6 %collective-permute-start.20 = (bf16[128,768]{1,0:T(8,128)(2,1)S(1)}, bf16[128,768]{1,0:T(8,128)(2,1)S(1)}, u32[]{:S(2)}, u32[]{:S(2)}) collective-permute-start(bf16[128,768]{1,0:T(8,128)(2,1)S(1)} %act.5.refs_7_.refs_1_), channel_id=1, source_target_pairs={{0,16},{1,17},{2,18},{3,19},{4,20},{5,21},{6,22},{7,23},{8,24},{9,... | collective-permute-start | bytes 589832 | tf_op jit(solution)/shard_map/ppermute | solution.py:423
  71.7 9.3 %collective-permute-start.27 = (bf16[288,256]{1,0:T(8,128)(2,1)S(1)}, bf16[288,256]{1,0:T(8,128)(2,1)S(1)}, u32[]{:S(2)}, u32[]{:S(2)}) collective-permute-start(bf16[288,256]{1,0:T(8,128)(2,1)S(1)} %get-tuple-element.75), channel_id=1, source_target_pairs={{0,1},{1,0},{2,3},{3,2},{4,5},{5,4},{6,7},{7,6},{8,9},{9,8},{10,11... | collective-permute-start | bytes 442376 | tf_op jit(solution)/shard_map/ppermute | solution.py:423
  78.1 6.8 %collective-permute-start.17 = (bf16[128,768]{1,0:T(8,128)(2,1)S(1)}, bf16[128,768]{1,0:T(8,128)(2,1)S(1)}, u32[]{:S(2)}, u32[]{:S(2)}) collective-permute-start(bf16[128,768]{1,0:T(8,128)(2,1)S(1)} %act.6.refs_7_.refs_1_), channel_id=1, source_target_pairs={{0,16},{1,17},{2,18},{3,19},{4,20},{5,21},{6,22},{7,23},{8,24},{9,... | collective-permute-start | bytes 589832 | tf_op jit(solution)/shard_map/ppermute | solution.py:423
  78.4 6.7 %collective-permute-start.21 = (bf16[128,768]{1,0:T(8,128)(2,1)S(1)}, bf16[128,768]{1,0:T(8,128)(2,1)S(1)}, u32[]{:S(2)}, u32[]{:S(2)}) collective-permute-start(bf16[128,768]{1,0:T(8,128)(2,1)S(1)} %act.5.refs_7_.refs_1_), channel_id=1, source_target_pairs={{0,8},{1,9},{2,10},{3,11},{4,12},{5,13},{6,14},{7,15},{8,0},{9,1},... | collective-permute-start | bytes 589832 | tf_op jit(solution)/shard_map/ppermute | solution.py:423
  81.0 4.1 %collective-permute-start.22 = (bf16[128,768]{1,0:T(8,128)(2,1)S(1)}, bf16[128,768]{1,0:T(8,128)(2,1)S(1)}, u32[]{:S(2)}, u32[]{:S(2)}) collective-permute-start(bf16[128,768]{1,0:T(8,128)(2,1)S(1)} %collective-permute-done.20.refs_2_), channel_id=1, source_target_pairs={{0,8},{1,9},{2,10},{3,11},{4,12},{5,13},{6,14},{7,15},{8,0},{9,1},... | collective-permute-start | bytes 589832 | tf_op jit(solution)/shard_map/ppermute | solution.py:423
  81.1 34.7 %collective-permute-start.28 = (bf16[288,256]{1,0:T(8,128)(2,1)S(1)}, bf16[288,256]{1,0:T(8,128)(2,1)S(1)}, u32[]{:S(2)}, u32[]{:S(2)}) collective-permute-start(bf16[288,256]{1,0:T(8,128)(2,1)S(1)} %add_convert_fusion.2), channel_id=1, source_target_pairs={{0,2},{1,3},{2,4},{3,5},{4,6},{5,7},{6,0},{7,1},{8,10},{9,11},{10,... | collective-permute-start | bytes 442376 | tf_op jit(solution)/shard_map/ppermute | solution.py:423
  81.3 7.9 %collective-permute-start.18 = (bf16[128,768]{1,0:T(8,128)(2,1)S(1)}, bf16[128,768]{1,0:T(8,128)(2,1)S(1)}, u32[]{:S(2)}, u32[]{:S(2)}) collective-permute-start(bf16[128,768]{1,0:T(8,128)(2,1)S(1)} %act.6.refs_7_.refs_1_), channel_id=1, source_target_pairs={{0,8},{1,9},{2,10},{3,11},{4,12},{5,13},{6,14},{7,15},{8,0},{9,1},... | collective-permute-start | bytes 589832 | tf_op jit(solution)/shard_map/ppermute | solution.py:423
  84.9 10.0 %collective-permute-start.15 = (bf16[128,1536]{1,0:T(8,128)(2,1)S(1)}, bf16[128,1536]{1,0:T(8,128)(2,1)S(1)}, u32[]{:S(2)}, u32[]{:S(2)}) collective-permute-start(bf16[128,1536]{1,0:T(8,128)(2,1)S(1)} %get-tuple-element.66), channel_id=1, source_target_pairs={{0,16},{1,17},{2,18},{3,19},{4,20},{5,21},{6,22},{7,23},{8,24},{9,... | collective-permute-start | bytes 1179656 | tf_op jit(solution)/shard_map/ppermute | solution.py:423
  85.2 4.1 %collective-permute-start.19 = (bf16[128,768]{1,0:T(8,128)(2,1)S(1)}, bf16[128,768]{1,0:T(8,128)(2,1)S(1)}, u32[]{:S(2)}, u32[]{:S(2)}) collective-permute-start(bf16[128,768]{1,0:T(8,128)(2,1)S(1)} %collective-permute-done.17.refs_2_), channel_id=1, source_target_pairs={{0,8},{1,9},{2,10},{3,11},{4,12},{5,13},{6,14},{7,15},{8,0},{9,1},... | collective-permute-start | bytes 589832 | tf_op jit(solution)/shard_map/ppermute | solution.py:423
  88.6 8.6 %collective-permute-start.29 = (bf16[288,256]{1,0:T(8,128)(2,1)S(1)}, bf16[288,256]{1,0:T(8,128)(2,1)S(1)}, u32[]{:S(2)}, u32[]{:S(2)}) collective-permute-start(bf16[288,256]{1,0:T(8,128)(2,1)S(1)} %get-tuple-element.76), channel_id=1, source_target_pairs={{0,1},{1,0},{2,3},{3,2},{4,5},{5,4},{6,7},{7,6},{8,9},{9,8},{10,11... | collective-permute-start | bytes 442376 | tf_op jit(solution)/shard_map/ppermute | solution.py:423
  96.1 5.7 %collective-permute-start.23 = (bf16[128,768]{1,0:T(8,128)(2,1)S(1)}, bf16[128,768]{1,0:T(8,128)(2,1)S(1)}, u32[]{:S(2)}, u32[]{:S(2)}) collective-permute-start(bf16[128,768]{1,0:T(8,128)(2,1)S(1)} %act.7.refs_1_.refs_7_), channel_id=1, source_target_pairs={{0,16},{1,17},{2,18},{3,19},{4,20},{5,21},{6,22},{7,23},{8,24},{9,... | collective-permute-start | bytes 589832 | tf_op jit(solution)/shard_map/ppermute | solution.py:423
  96.5 5.4 %collective-permute-start.31 = (bf16[288,256]{1,0:T(8,128)(2,1)S(1)}, bf16[288,256]{1,0:T(8,128)(2,1)S(1)}, u32[]{:S(2)}, u32[]{:S(2)}) collective-permute-start(bf16[288,256]{1,0:T(8,128)(2,1)S(1)} %get-tuple-element.77), channel_id=1, source_target_pairs={{0,1},{1,0},{2,3},{3,2},{4,5},{5,4},{6,7},{7,6},{8,9},{9,8},{10,11... | collective-permute-start | bytes 442376 | tf_op jit(solution)/shard_map/ppermute | solution.py:423
  97.3 18.4 %collective-permute-start.30 = (bf16[288,256]{1,0:T(8,128)(2,1)S(1)}, bf16[288,256]{1,0:T(8,128)(2,1)S(1)}, u32[]{:S(2)}, u32[]{:S(2)}) collective-permute-start(bf16[288,256]{1,0:T(8,128)(2,1)S(1)} %add_convert_fusion.1), channel_id=1, source_target_pairs={{0,4},{1,5},{2,6},{3,7},{4,0},{5,1},{6,2},{7,3},{8,12},{9,13},{10,... | collective-permute-start | bytes 442376 | tf_op jit(solution)/shard_map/ppermute | solution.py:423
  97.4 6.9 %collective-permute-start.24 = (bf16[128,768]{1,0:T(8,128)(2,1)S(1)}, bf16[128,768]{1,0:T(8,128)(2,1)S(1)}, u32[]{:S(2)}, u32[]{:S(2)}) collective-permute-start(bf16[128,768]{1,0:T(8,128)(2,1)S(1)} %act.7.refs_1_.refs_7_), channel_id=1, source_target_pairs={{0,8},{1,9},{2,10},{3,11},{4,12},{5,13},{6,14},{7,15},{8,0},{9,1},... | collective-permute-start | bytes 589832 | tf_op jit(solution)/shard_map/ppermute | solution.py:423
  101.9 2.4 %collective-permute-start.25 = (bf16[128,768]{1,0:T(8,128)(2,1)S(1)}, bf16[128,768]{1,0:T(8,128)(2,1)S(1)}, u32[]{:S(2)}, u32[]{:S(2)}) collective-permute-start(bf16[128,768]{1,0:T(8,128)(2,1)S(1)} %collective-permute-done.23.refs_2_), channel_id=1, source_target_pairs={{0,8},{1,9},{2,10},{3,11},{4,12},{5,13},{6,14},{7,15},{8,0},{9,1},... | collective-permute-start | bytes 589832 | tf_op jit(solution)/shard_map/ppermute | solution.py:423
  101.9 6.5 %copy-start.10 = (f32[4,288]{1,0:T(4,128)S(1)}, f32[4,288]{1,0:T(4,128)}, u32[]{:S(2)}) copy-start(f32[4,288]{1,0:T(4,128)} %get-tuple-element.55) | copy-start | bytes 13828
  101.9 22.2 %copy-start.8 = (f32[2304]{0:T(1024)S(1)}, f32[2304]{0:T(1024)}, u32[]{:S(2)}) copy-start(f32[2304]{0:T(1024)} %param.19) | copy-start | bytes 27652
  101.9 22.3 %copy-start.9 = (f32[16]{0:T(128)S(1)}, f32[16]{0:T(128)}, u32[]{:S(2)}) copy-start(f32[16]{0:T(128)} %param.21) | copy-start | bytes 196
  101.9 13.8 %collective-permute-start.32 = (bf16[288,256]{1,0:T(8,128)(2,1)S(1)}, bf16[288,256]{1,0:T(8,128)(2,1)S(1)}, u32[]{:S(2)}, u32[]{:S(2)}) collective-permute-start(bf16[288,256]{1,0:T(8,128)(2,1)S(1)} %add_convert_fusion), channel_id=1, source_target_pairs={{0,6},{1,7},{2,0},{3,1},{4,2},{5,3},{6,4},{7,5},{8,14},{9,15},{10,... | collective-permute-start | bytes 442376 | tf_op jit(solution)/shard_map/ppermute | solution.py:423
  104.3 23.3 %copy-start.1 = (bf16[2304,512]{1,0:T(8,128)(2,1)S(1)}, bf16[2304,512]{1,0:T(8,128)(2,1)}, u32[]{:S(2)}) copy-start(bf16[2304,512]{1,0:T(8,128)(2,1)} %refs_2_.1) | copy-start | bytes 7077892
  107.8 29.3 %copy-start.7 = (f32[256,288]{0,1:T(8,128)S(1)}, f32[256,288]{0,1:T(8,128)}, u32[]{:S(2)}) copy-start(f32[256,288]{0,1:T(8,128)} %param.11) | copy-start | bytes 884740
  107.8 8.0 %collective-permute-start.26 = (bf16[288,256]{1,0:T(8,128)(2,1)S(1)}, bf16[288,256]{1,0:T(8,128)(2,1)S(1)}, u32[]{:S(2)}, u32[]{:S(2)}) collective-permute-start(bf16[288,256]{1,0:T(8,128)(2,1)S(1)} %get-tuple-element.74), channel_id=1, source_target_pairs={{0,1},{1,0},{2,3},{3,2},{4,5},{5,4},{6,7},{7,6},{8,9},{9,8},{10,11... | collective-permute-start | bytes 442376 | tf_op jit(solution)/shard_map/ppermute | solution.py:423
  108.4 7.3 %collective-permute-start.8 = (f32[4,288]{1,0:T(4,128)S(1)}, f32[4,288]{1,0:T(4,128)S(1)}, u32[]{:S(2)}, u32[]{:S(2)}) collective-permute-start(f32[4,288]{1,0:T(4,128)S(1)} %copy-done.10), channel_id=1, source_target_pairs={{0,0},{1,1},{2,8},{3,9},{4,16},{5,17},{6,24},{7,25},{8,2},{9,3},{1... | collective-permute-start | bytes 13832 | tf_op jit(solution)/shard_map/ppermute | solution.py:423
  116.8 10.7 %all-to-all-start = ((f32[32,4,288]{2,1,0:T(4,128)}), f32[32,4,288]{2,1,0:T(4,128)S(1)}, u32[]{:S(2)}, u32[]{:S(2)}) async-start(f32[32,4,288]{2,1,0:T(4,128)} %get-tuple-element.78), calls=%async_computation | async-start | bytes 393216 | tf_op jit(solution)/shard_map/all_to_all | solution.py:516
  119.9 14.0 %collective-permute-start.33 = (bf16[288,256]{1,0:T(8,128)(2,1)S(1)}, bf16[288,256]{1,0:T(8,128)(2,1)S(1)}, u32[]{:S(2)}, u32[]{:S(2)}) collective-permute-start(bf16[288,256]{1,0:T(8,128)(2,1)S(1)} %get-tuple-element.80), channel_id=1, source_target_pairs={{0,0},{1,1},{2,8},{3,9},{4,16},{5,17},{6,24},{7,25},{8,2},{9,3},{1... | collective-permute-start | bytes 442376 | tf_op jit(solution)/shard_map/ppermute | solution.py:423
  133.9 9.3 %all-to-all-start.1 = ((f32[32,2,16]{2,1,0:T(2,128)}), f32[32,2,16]{2,1,0:T(2,128)S(1)}, u32[]{:S(2)}, u32[]{:S(2)}) async-start(f32[32,2,16]{2,1,0:T(2,128)} %get-tuple-element.83), calls=%async_computation.1 | async-start | bytes 65536 | tf_op jit(solution)/shard_map/all_to_all | solution.py:516

commit v16 on v15

--- a/solution.py
+++ b/solution.py
@@ -39,7 +39,7 @@
     block, tokens = x.shape
     v = x[...]
     wide = up_to(block)
-    g = jnp.concatenate([gain[...], jnp.zeros((1, wide - block), f32)], axis=1)
+    g = jnp.concatenate([gain[...].reshape(1, block), jnp.zeros((1, wide - block), f32)], axis=1)
     g = jnp.broadcast_to(g, (LANES, wide)).T[0:block, 0:1]
     out[0:block] = (v * g).astype(bf16)
     sq = jnp.sum(v * v, axis=0, keepdims=True)
@@ -428,7 +428,7 @@
 
     scal = jnp.stack([core, side, y]).astype(jnp.int32)
     sent, stream = prep_call(
-        skip_stream_arriving.T, premix_rmsnorm_gain[None], chosen_specialists.T, sequence_piece_tallies
+        skip_stream_arriving.T, premix_rmsnorm_gain, chosen_specialists.T, sequence_piece_tallies
     )
     wg, wu, wd = specialist_switch_weights, specialist_expand_weights, specialist_contract_weights
     if spread > 1:

time: 147 us -> 145 us (0.986)
  no operation moved by 1% of the time
where the time goes in v16:
time: 145 us; the launch traced here: 143 us
  waiting for transfers between devices  51.6 us (36%)
  Pallas kernels  46.1 us (32%)
  starting transfers between devices  37.9 us (26%)
  local copies, waits for them, and re-layouts  4.32 us (3%)
  other arithmetic  1.7 us (1%)
    ppermute x34, waiting for transfers between devices, send(): return lax.ppermute(value, ('dp', 'mp'), pairs)  43.1 us
    ppermute x34, starting transfers between devices, send(): return lax.ppermute(value, ('dp', 'mp'), pairs)  31.7 us
    pallas_call x4, Pallas kernels, partial_call(): pl.pallas_call(lambda *refs: partial_kernel(sides, len(feeds), *refs), gr...  19.4 us
    pallas_call x4, Pallas kernels, down_call(): pl.pallas_call(lambda *refs: down_kernel(sides, *refs), grid=(experts,),...  13.9 us
    all_to_all x2, waiting for transfers between devices, body(): exchange = lambda v: lax.all_to_all(v, ('dp', 'mp'), 0, 0, tiled=True)  8.51 us
    all_to_all x2, starting transfers between devices, body(): exchange = lambda v: lax.all_to_all(v, ('dp', 'mp'), 0, 0, tiled=True)  6.24 us
    pallas_call x4, Pallas kernels, act_call(): pl.pallas_call(lambda *refs: act_kernel(base, *refs), in_specs=[SMEM] + [...  4.95 us
    unnamed x22, local copies, waits for them, and re-layouts  4.05 us
  transfers between devices with their start and end apart: 36, of which 14 were waited for; matrix products, arithmetic and copies ran while one was open for 1% of the time, Pallas kernels for 30%

profile of v16, /device:TPU:4, one launch (start us, length us, event | category | flops | bytes accessed | tf_op | source)
XLA Modules:
  0.0 142.7 jit_solution(15870887508223328873)
XLA Ops:
  0.6 1.9 %prep.1 = (bf16[304,256]{1,0:T(8,128)(2,1)}, f32[4,288]{1,0:T(4,128)}) custom-call(s32[1,4]{1,0:T(1,128)} %tallies.1, f32[288,256]{1,0:T(8,128)} %bitcast.19, f32[288]{0:T(512)} %gain.1, s32[2,256]{1,0:T(2,128)} %bitcast.23), custom_call_target="tpu_custom_call" | custom-call | flops 88473 | bytes 132710 | tf_op jit(solution)/shard_map/prep/pallas_call | solution.py:75
  2.6 1.5 %collective-permute-start = (bf16[304,256]{1,0:T(8,128)(2,1)}, bf16[304,256]{1,0:T(8,128)(2,1)S(1)}, u32[]{:S(2)}, u32[]{:S(2)}) collective-permute-start(bf16[304,256]{1,0:T(8,128)(2,1)} %get-tuple-element.43), channel_id=1, source_target_pairs={{0,6},{1,7},{2,14},{3,15},{4,22},{5,23},{6,30},{7,31},{8,0},{9,1},... | collective-permute-start | bytes 466952 | tf_op jit(solution)/shard_map/ppermute | solution.py:423
  4.1 3.0 %collective-permute-start.1 = (bf16[304,256]{1,0:T(8,128)(2,1)}, bf16[304,256]{1,0:T(8,128)(2,1)S(1)}, u32[]{:S(2)}, u32[]{:S(2)}) collective-permute-start(bf16[304,256]{1,0:T(8,128)(2,1)} %get-tuple-element.43), channel_id=1, source_target_pairs={{0,7},{1,6},{2,15},{3,14},{4,23},{5,22},{6,31},{7,30},{8,1},{9,0},... | collective-permute-start | bytes 466952 | tf_op jit(solution)/shard_map/ppermute | solution.py:423
  7.2 3.8 %collective-permute-done.refs_0_ = bf16[304,256]{1,0:T(8,128)(2,1)S(1)} collective-permute-done((bf16[304,256]{1,0:T(8,128)(2,1)}, bf16[304,256]{1,0:T(8,128)(2,1)S(1)}, u32[]{:S(2)}, u32[]{:S(2)}) %collective-permute-start) | collective-permute-done | bytes 155680 | tf_op jit(solution)/shard_map/ppermute | solution.py:423
  11.0 4.3 %collective-permute-done.1.refs_1_ = bf16[304,256]{1,0:T(8,128)(2,1)S(1)} collective-permute-done((bf16[304,256]{1,0:T(8,128)(2,1)}, bf16[304,256]{1,0:T(8,128)(2,1)S(1)}, u32[]{:S(2)}, u32[]{:S(2)}) %collective-permute-start.1) | collective-permute-done | bytes 155680 | tf_op jit(solution)/shard_map/ppermute | solution.py:423
  15.3 5.9 %collective-permute-start.2 = (bf16[608,256]{1,0:T(8,128)(2,1)S(1)}, bf16[608,256]{1,0:T(8,128)(2,1)S(1)}, u32[]{:S(2)}, u32[]{:S(2)}) collective-permute-start(bf16[608,256]{1,0:T(8,128)(2,1)S(1)} %join.1.refs_1_), channel_id=1, source_target_pairs={{0,6},{1,7},{2,0},{3,1},{4,2},{5,3},{6,4},{7,5},{8,14},{9,15},{10,... | collective-permute-start | bytes 933896 | tf_op jit(solution)/shard_map/ppermute | solution.py:423
  21.2 2.0 %copy-done.2 = bf16[4,576,720]{2,1,0:T(8,128)(2,1)S(1)} copy-done((bf16[4,576,720]{2,1,0:T(8,128)(2,1)S(1)}, bf16[4,576,720]{2,1,0:T(8,128)(2,1)}, u32[]{:S(2)}) %copy-start.2) | copy-done | bytes 3317784
  23.2 2.0 %copy-done.4 = bf16[4,576,720]{2,1,0:T(8,128)(2,1)S(1)} copy-done((bf16[4,576,720]{2,1,0:T(8,128)(2,1)S(1)}, bf16[4,576,720]{2,1,0:T(8,128)(2,1)}, u32[]{:S(2)}) %copy-start.4) | copy-done | bytes 3317784
  25.3 4.9 %gate_up_partial.4 = (f32[256,1536]{1,0:T(8,128)S(1)}, bf16[256,1536]{1,0:T(8,128)(2,1)S(1)}, bf16[256,128]{1,0:T(8,128)(2,1)S(1)}) custom-call(s32[3]{0:T(128)S(1)} %pad_add_fusion.1.refs_0_, bf16[608,256]{1,0:T(8,128)(2,1)S(1)} %join.1.refs_1_, bf16[128,576]{1,0:T(8,128)(2,1)S(1)} %pad_add_fusion.refs_2_, bf16[4,576,720]{2,1,0:T(8,128)(2,1)S(1)} %copy-done.2, ...), custom_call_target="tpu_custom_call" | custom-call | flops 6794772480 | bytes 35979264 | tf_op jit(solution)/shard_map/gate_up_partial/pallas_call | solution.py:190
  30.3 4.9 %gate_up_partial.5 = (f32[256,1536]{1,0:T(8,128)S(1)}, bf16[256,1536]{1,0:T(8,128)(2,1)S(1)}, bf16[256,128]{1,0:T(8,128)(2,1)S(1)}) custom-call(s32[3]{0:T(128)S(1)} %pad_add_fusion.1.refs_0_, bf16[608,256]{1,0:T(8,128)(2,1)S(1)} %collective-permute-done.2.refs_1_, bf16[128,576]{1,0:T(8,128)(2,1)S(1)} %pad_add_fusion.refs_2_, ...), custom_call_target="tpu_custom_call" | custom-call | flops 6794772480 | bytes 35979264 | tf_op jit(solution)/shard_map/gate_up_partial/pallas_call | solution.py:190
  35.7 0.9 core_sum.4
  36.6 3.4 %collective-permute-done.3.refs_1_ = bf16[608,256]{1,0:T(8,128)(2,1)S(1)} collective-permute-done((bf16[608,256]{1,0:T(8,128)(2,1)S(1)}, bf16[608,256]{1,0:T(8,128)(2,1)S(1)}, u32[]{:S(2)}, u32[]{:S(2)}) %collective-permute-start.3) | collective-permute-done | bytes 311328 | tf_op jit(solution)/shard_map/ppermute | solution.py:423
  40.0 4.8 %gate_up_partial.6 = (f32[256,1536]{1,0:T(8,128)S(1)}, bf16[256,1536]{1,0:T(8,128)(2,1)S(1)}, bf16[256,128]{1,0:T(8,128)(2,1)S(1)}) custom-call(s32[3]{0:T(128)S(1)} %pad_add_fusion.1.refs_0_, bf16[608,256]{1,0:T(8,128)(2,1)S(1)} %collective-permute-done.3.refs_1_, bf16[128,576]{1,0:T(8,128)(2,1)S(1)} %pad_add_fusion.refs_2_, ...), custom_call_target="tpu_custom_call" | custom-call | flops 6794772480 | bytes 35979264 | tf_op jit(solution)/shard_map/gate_up_partial/pallas_call | solution.py:190
  44.8 2.1 %collective-permute-start.5 = (bf16[608,256]{1,0:T(8,128)(2,1)S(1)}, bf16[608,256]{1,0:T(8,128)(2,1)S(1)}, u32[]{:S(2)}, u32[]{:S(2)}) collective-permute-start(bf16[608,256]{1,0:T(8,128)(2,1)S(1)} %collective-permute-done.3.refs_1_), channel_id=1, source_target_pairs={{0,6},{1,7},{2,0},{3,1},{4,2},{5,3},{6,4},{7,5},{8,14},{9,15},{10,... | collective-permute-start | bytes 933896 | tf_op jit(solution)/shard_map/ppermute | solution.py:423
  47.0 0.9 core_sum.5
  47.9 1.2 act.4.refs_5_.refs_1_
  49.2 2.1 %collective-permute-start.10 = (bf16[128,768]{1,0:T(8,128)(2,1)S(1)}, bf16[128,768]{1,0:T(8,128)(2,1)S(1)}, u32[]{:S(2)}, u32[]{:S(2)}) collective-permute-start(bf16[128,768]{1,0:T(8,128)(2,1)S(1)} %act.4.refs_5_.refs_1_), channel_id=1, source_target_pairs={{0,16},{1,17},{2,18},{3,19},{4,20},{5,21},{6,22},{7,23},{8,24},{9,... | collective-permute-start | bytes 589832 | tf_op jit(solution)/shard_map/ppermute | solution.py:423
  51.3 2.6 %collective-permute-done.5.refs_1_ = bf16[608,256]{1,0:T(8,128)(2,1)S(1)} collective-permute-done((bf16[608,256]{1,0:T(8,128)(2,1)S(1)}, bf16[608,256]{1,0:T(8,128)(2,1)S(1)}, u32[]{:S(2)}, u32[]{:S(2)}) %collective-permute-start.5) | collective-permute-done | bytes 311328 | tf_op jit(solution)/shard_map/ppermute | solution.py:423
  53.8 4.8 %gate_up_partial.7 = (f32[256,1536]{1,0:T(8,128)S(1)}, bf16[256,1536]{1,0:T(8,128)(2,1)S(1)}, bf16[256,128]{1,0:T(8,128)(2,1)S(1)}) custom-call(s32[3]{0:T(128)S(1)} %pad_add_fusion.1.refs_0_, bf16[608,256]{1,0:T(8,128)(2,1)S(1)} %collective-permute-done.5.refs_1_, bf16[128,576]{1,0:T(8,128)(2,1)S(1)} %pad_add_fusion.refs_2_, ...), custom_call_target="tpu_custom_call" | custom-call | flops 6794772480 | bytes 35979264 | tf_op jit(solution)/shard_map/gate_up_partial/pallas_call | solution.py:190
  58.8 0.9 core_sum.6
  60.2 3.5 %collective-permute-done.10.refs_2_ = bf16[128,768]{1,0:T(8,128)(2,1)S(1)} collective-permute-done((bf16[128,768]{1,0:T(8,128)(2,1)S(1)}, bf16[128,768]{1,0:T(8,128)(2,1)S(1)}, u32[]{:S(2)}, u32[]{:S(2)}) %collective-permute-start.10) | collective-permute-done | bytes 196640 | tf_op jit(solution)/shard_map/ppermute | solution.py:423
  64.0 1.2 act.5.refs_7_.refs_1_
  65.2 1.8 %collective-permute-start.20 = (bf16[128,768]{1,0:T(8,128)(2,1)S(1)}, bf16[128,768]{1,0:T(8,128)(2,1)S(1)}, u32[]{:S(2)}, u32[]{:S(2)}) collective-permute-start(bf16[128,768]{1,0:T(8,128)(2,1)S(1)} %act.5.refs_7_.refs_1_), channel_id=1, source_target_pairs={{0,16},{1,17},{2,18},{3,19},{4,20},{5,21},{6,22},{7,23},{8,24},{9,... | collective-permute-start | bytes 589832 | tf_op jit(solution)/shard_map/ppermute | solution.py:423
  67.0 3.5 %down.4 = (bf16[288,256]{1,0:T(8,128)(2,1)S(1)}, bf16[288,256]{1,0:T(8,128)(2,1)S(1)}) custom-call(s32[3]{0:T(128)S(1)} %pad_add_fusion.1.refs_0_, bf16[128,768]{1,0:T(8,128)(2,1)S(1)} %act.4.refs_5_.refs_1_, bf16[128,768]{1,0:T(8,128)(2,1)S(1)} %collective-permute-done.10.refs_2_, bf16[128,768]{1,0:T(8,128)(2,1)S(1)} %collective-permute-done.12.refs_3_, ...), custom_call_target="tpu_custom_call" | custom-call | flops 3397386240 | bytes 14450688 | tf_op jit(solution)/shard_map/down/pallas_call | solution.py:306
  71.1 0.9 core_sum.7
  72.0 3.6 %collective-permute-done.16.refs_2_ = bf16[128,1536]{1,0:T(8,128)(2,1)S(1)} collective-permute-done((bf16[128,1536]{1,0:T(8,128)(2,1)S(1)}, bf16[128,1536]{1,0:T(8,128)(2,1)S(1)}, u32[]{:S(2)}, u32[]{:S(2)}) %collective-permute-start.16) | collective-permute-done | bytes 393248 | tf_op jit(solution)/shard_map/ppermute | solution.py:423
  75.6 1.2 act.6.refs_7_.refs_1_
  77.2 2.6 %collective-permute-done.20.refs_2_ = bf16[128,768]{1,0:T(8,128)(2,1)S(1)} collective-permute-done((bf16[128,768]{1,0:T(8,128)(2,1)S(1)}, bf16[128,768]{1,0:T(8,128)(2,1)S(1)}, u32[]{:S(2)}, u32[]{:S(2)}) %collective-permute-start.20) | collective-permute-done | bytes 196640 | tf_op jit(solution)/shard_map/ppermute | solution.py:423
  80.7 3.0 %collective-permute-done.17.refs_2_ = bf16[128,768]{1,0:T(8,128)(2,1)S(1)} collective-permute-done((bf16[128,768]{1,0:T(8,128)(2,1)S(1)}, bf16[128,768]{1,0:T(8,128)(2,1)S(1)}, u32[]{:S(2)}, u32[]{:S(2)}) %collective-permute-start.17) | collective-permute-done | bytes 196640 | tf_op jit(solution)/shard_map/ppermute | solution.py:423
  83.9 3.5 %down.5 = (bf16[288,256]{1,0:T(8,128)(2,1)S(1)}, bf16[288,256]{1,0:T(8,128)(2,1)S(1)}) custom-call(s32[3]{0:T(128)S(1)} %pad_add_fusion.1.refs_0_, bf16[128,768]{1,0:T(8,128)(2,1)S(1)} %act.5.refs_7_.refs_1_, bf16[128,768]{1,0:T(8,128)(2,1)S(1)} %collective-permute-done.20.refs_2_, bf16[128,768]{1,0:T(8,128)(2,1)S(1)} %collective-permute-done.21.refs_3_, ...), custom_call_target="tpu_custom_call" | custom-call | flops 3397386240 | bytes 14450688 | tf_op jit(solution)/shard_map/down/pallas_call | solution.py:306
  88.0 3.5 %down.6 = (bf16[288,256]{1,0:T(8,128)(2,1)S(1)}, bf16[288,256]{1,0:T(8,128)(2,1)S(1)}) custom-call(s32[3]{0:T(128)S(1)} %pad_add_fusion.1.refs_0_, bf16[128,768]{1,0:T(8,128)(2,1)S(1)} %act.6.refs_7_.refs_1_, bf16[128,768]{1,0:T(8,128)(2,1)S(1)} %collective-permute-done.17.refs_2_, bf16[128,768]{1,0:T(8,128)(2,1)S(1)} %collective-permute-done.18.refs_3_, ...), custom_call_target="tpu_custom_call" | custom-call | flops 3397386240 | bytes 14450688 | tf_op jit(solution)/shard_map/down/pallas_call | solution.py:306
  91.5 2.1 %collective-permute-done.15.refs_2_ = bf16[128,1536]{1,0:T(8,128)(2,1)S(1)} collective-permute-done((bf16[128,1536]{1,0:T(8,128)(2,1)S(1)}, bf16[128,1536]{1,0:T(8,128)(2,1)S(1)}, u32[]{:S(2)}, u32[]{:S(2)}) %collective-permute-start.15) | collective-permute-done | bytes 393248 | tf_op jit(solution)/shard_map/ppermute | solution.py:423
  93.6 1.2 act.7.refs_1_.refs_7_
  95.2 0.8 collective-permute-start.31
  96.2 4.4 %collective-permute-done.23.refs_2_ = bf16[128,768]{1,0:T(8,128)(2,1)S(1)} collective-permute-done((bf16[128,768]{1,0:T(8,128)(2,1)S(1)}, bf16[128,768]{1,0:T(8,128)(2,1)S(1)}, u32[]{:S(2)}, u32[]{:S(2)}) %collective-permute-start.23) | collective-permute-done | bytes 196640 | tf_op jit(solution)/shard_map/ppermute | solution.py:423
  100.7 2.3 %collective-permute-start.32 = (bf16[288,256]{1,0:T(8,128)(2,1)S(1)}, bf16[288,256]{1,0:T(8,128)(2,1)S(1)}, u32[]{:S(2)}, u32[]{:S(2)}) collective-permute-start(bf16[288,256]{1,0:T(8,128)(2,1)S(1)} %add_convert_fusion), channel_id=1, source_target_pairs={{0,6},{1,7},{2,0},{3,1},{4,2},{5,3},{6,4},{7,5},{8,14},{9,15},{10,... | collective-permute-start | bytes 442376 | tf_op jit(solution)/shard_map/ppermute | solution.py:423
  103.0 3.5 %down.7 = (bf16[288,256]{1,0:T(8,128)(2,1)S(1)}, bf16[288,256]{1,0:T(8,128)(2,1)S(1)}) custom-call(s32[3]{0:T(128)S(1)} %pad_add_fusion.1.refs_0_, bf16[128,768]{1,0:T(8,128)(2,1)S(1)} %act.7.refs_1_.refs_7_, bf16[128,768]{1,0:T(8,128)(2,1)S(1)} %collective-permute-done.23.refs_2_, bf16[128,768]{1,0:T(8,128)(2,1)S(1)} %collective-permute-done.24.refs_3_, ...), custom_call_target="tpu_custom_call" | custom-call | flops 3397386240 | bytes 14450688 | tf_op jit(solution)/shard_map/down/pallas_call | solution.py:306
  107.2 2.3 %collective-permute-start.8 = (f32[4,288]{1,0:T(4,128)S(1)}, f32[4,288]{1,0:T(4,128)S(1)}, u32[]{:S(2)}, u32[]{:S(2)}) collective-permute-start(f32[4,288]{1,0:T(4,128)S(1)} %copy-done.10), channel_id=1, source_target_pairs={{0,0},{1,1},{2,8},{3,9},{4,16},{5,17},{6,24},{7,25},{8,2},{9,3},{1... | collective-permute-start | bytes 13832 | tf_op jit(solution)/shard_map/ppermute | solution.py:423
  109.5 5.0 %collective-permute-done.8.stream = f32[4,288]{1,0:T(4,128)S(1)} collective-permute-done((f32[4,288]{1,0:T(4,128)S(1)}, f32[4,288]{1,0:T(4,128)S(1)}, u32[]{:S(2)}, u32[]{:S(2)}) %collective-permute-start.8) | collective-permute-done | bytes 4640 | tf_op jit(solution)/shard_map/ppermute | solution.py:423
  114.5 1.1 branch_total.1
  115.6 3.0 %all-to-all-start = ((f32[32,4,288]{2,1,0:T(4,128)}), f32[32,4,288]{2,1,0:T(4,128)S(1)}, u32[]{:S(2)}, u32[]{:S(2)}) async-start(f32[32,4,288]{2,1,0:T(4,128)} %get-tuple-element.78), calls=%async_computation | async-start | bytes 393216 | tf_op jit(solution)/shard_map/all_to_all | solution.py:516
  118.6 4.3 %collective-permute-start.33 = (bf16[288,256]{1,0:T(8,128)(2,1)S(1)}, bf16[288,256]{1,0:T(8,128)(2,1)S(1)}, u32[]{:S(2)}, u32[]{:S(2)}) collective-permute-start(bf16[288,256]{1,0:T(8,128)(2,1)S(1)} %get-tuple-element.80), channel_id=1, source_target_pairs={{0,0},{1,1},{2,8},{3,9},{4,16},{5,17},{6,24},{7,25},{8,2},{9,3},{1... | collective-permute-start | bytes 442376 | tf_op jit(solution)/shard_map/ppermute | solution.py:423
  123.1 3.2 %all-to-all-done.refs_0_ = f32[32,4,288]{2,1,0:T(4,128)S(1)} async-done(((f32[32,4,288]{2,1,0:T(4,128)}), f32[32,4,288]{2,1,0:T(4,128)S(1)}, u32[]{:S(2)}, u32[]{:S(2)}) %all-to-all-start) | async-done | bytes 147488 | tf_op jit(solution)/shard_map/all_to_all | solution.py:516
  126.3 1.4 %head.1 = (f32[16,512]{1,0:T(8,128)S(1)}, f32[32,2,16]{2,1,0:T(2,128)}) custom-call(f32[32,4,288]{2,1,0:T(4,128)S(1)} %all-to-all-done.refs_0_, f32[8,288]{1,0:T(8,128)S(1)} %reshape.12.refs_1_, bf16[2304,512]{1,0:T(8,128)(2,1)S(1)} %copy-done.1, f32[16,1]{1,0:T(8,128)S(1)} %copy.13.refs_3_), custom_call_target="tpu_custom_call" | custom-call | flops 11324620 | bytes 707788 | tf_op jit(solution)/shard_map/head/pallas_call | solution.py:380
  127.8 4.9 %collective-permute-done.33 = bf16[288,256]{1,0:T(8,128)(2,1)S(1)} collective-permute-done((bf16[288,256]{1,0:T(8,128)(2,1)S(1)}, bf16[288,256]{1,0:T(8,128)(2,1)S(1)}, u32[]{:S(2)}, u32[]{:S(2)}) %collective-permute-start.33) | collective-permute-done | bytes 147488 | tf_op jit(solution)/shard_map/ppermute | solution.py:423
  132.6 3.2 %all-to-all-start.1 = ((f32[32,2,16]{2,1,0:T(2,128)}), f32[32,2,16]{2,1,0:T(2,128)S(1)}, u32[]{:S(2)}, u32[]{:S(2)}) async-start(f32[32,2,16]{2,1,0:T(2,128)} %get-tuple-element.83), calls=%async_computation.1 | async-start | bytes 65536 | tf_op jit(solution)/shard_map/all_to_all | solution.py:516
  135.9 0.7 bitcast_add_fusion
  136.6 5.3 %all-to-all-done.1 = f32[32,2,16]{2,1,0:T(2,128)S(1)} async-done(((f32[32,2,16]{2,1,0:T(2,128)}), f32[32,2,16]{2,1,0:T(2,128)S(1)}, u32[]{:S(2)}, u32[]{:S(2)}) %all-to-all-start.1) | async-done | bytes 4128 | tf_op jit(solution)/shard_map/all_to_all | solution.py:516
  (80 shorter events, 6.9 us)
Async XLA Ops:
  0.6 6.4 %copy-start = (bf16[2304,4]{0,1:T(4,128)(2,1)S(1)}, bf16[2304,4]{0,1:T(4,128)(2,1)}, u32[]{:S(2)}) copy-start(bf16[2304,4]{0,1:T(4,128)(2,1)} %param.15) | copy-start | bytes 55300
  2.6 8.4 %collective-permute-start = (bf16[304,256]{1,0:T(8,128)(2,1)}, bf16[304,256]{1,0:T(8,128)(2,1)S(1)}, u32[]{:S(2)}, u32[]{:S(2)}) collective-permute-start(bf16[304,256]{1,0:T(8,128)(2,1)} %get-tuple-element.43), channel_id=1, source_target_pairs={{0,6},{1,7},{2,14},{3,15},{4,22},{5,23},{6,30},{7,31},{8,0},{9,1},... | collective-permute-start | bytes 466952 | tf_op jit(solution)/shard_map/ppermute | solution.py:423
  4.1 11.2 %collective-permute-start.1 = (bf16[304,256]{1,0:T(8,128)(2,1)}, bf16[304,256]{1,0:T(8,128)(2,1)S(1)}, u32[]{:S(2)}, u32[]{:S(2)}) collective-permute-start(bf16[304,256]{1,0:T(8,128)(2,1)} %get-tuple-element.43), channel_id=1, source_target_pairs={{0,7},{1,6},{2,15},{3,14},{4,23},{5,22},{6,31},{7,30},{8,1},{9,0},... | collective-permute-start | bytes 466952 | tf_op jit(solution)/shard_map/ppermute | solution.py:423
  15.3 14.9 %collective-permute-start.2 = (bf16[608,256]{1,0:T(8,128)(2,1)S(1)}, bf16[608,256]{1,0:T(8,128)(2,1)S(1)}, u32[]{:S(2)}, u32[]{:S(2)}) collective-permute-start(bf16[608,256]{1,0:T(8,128)(2,1)S(1)} %join.1.refs_1_), channel_id=1, source_target_pairs={{0,6},{1,7},{2,0},{3,1},{4,2},{5,3},{6,4},{7,5},{8,14},{9,15},{10,... | collective-permute-start | bytes 933896 | tf_op jit(solution)/shard_map/ppermute | solution.py:423
  21.2 2.0 %copy-start.2 = (bf16[4,576,720]{2,1,0:T(8,128)(2,1)S(1)}, bf16[4,576,720]{2,1,0:T(8,128)(2,1)}, u32[]{:S(2)}) copy-start(bf16[4,576,720]{2,1,0:T(8,128)(2,1)} %refs_3_.7) | copy-start | bytes 9953284
  23.2 2.0 %copy-start.4 = (bf16[4,576,720]{2,1,0:T(8,128)(2,1)S(1)}, bf16[4,576,720]{2,1,0:T(8,128)(2,1)}, u32[]{:S(2)}) copy-start(bf16[4,576,720]{2,1,0:T(8,128)(2,1)} %refs_4_.7) | copy-start | bytes 9953284
  25.2 5.1 %copy-start.3 = (bf16[4,576,720]{2,1,0:T(8,128)(2,1)S(1)}, bf16[4,576,720]{2,1,0:T(8,128)(2,1)}, u32[]{:S(2)}) copy-start(bf16[4,576,720]{2,1,0:T(8,128)(2,1)} %refs_3_.7) | copy-start | bytes 9953284
  25.3 5.1 %copy-start.5 = (bf16[4,576,720]{2,1,0:T(8,128)(2,1)S(1)}, bf16[4,576,720]{2,1,0:T(8,128)(2,1)}, u32[]{:S(2)}) copy-start(bf16[4,576,720]{2,1,0:T(8,128)(2,1)} %refs_4_.7) | copy-start | bytes 9953284
  30.2 5.5 %collective-permute-start.4 = (bf16[256,1536]{1,0:T(8,128)(2,1)S(1)}, bf16[256,1536]{1,0:T(8,128)(2,1)S(1)}, u32[]{:S(2)}, u32[]{:S(2)}) collective-permute-start(bf16[256,1536]{1,0:T(8,128)(2,1)S(1)} %get-tuple-element.45), channel_id=1, source_target_pairs={{0,8},{1,9},{2,10},{3,11},{4,12},{5,13},{6,14},{7,15},{8,0},{9,1},... | collective-permute-start | bytes 2359304 | tf_op jit(solution)/shard_map/ppermute | solution.py:423
  30.2 9.8 %collective-permute-start.3 = (bf16[608,256]{1,0:T(8,128)(2,1)S(1)}, bf16[608,256]{1,0:T(8,128)(2,1)S(1)}, u32[]{:S(2)}, u32[]{:S(2)}) collective-permute-start(bf16[608,256]{1,0:T(8,128)(2,1)S(1)} %collective-permute-done.2.refs_1_), channel_id=1, source_target_pairs={{0,6},{1,7},{2,0},{3,1},{4,2},{5,3},{6,4},{7,5},{8,14},{9,15},{10,... | collective-permute-start | bytes 933896 | tf_op jit(solution)/shard_map/ppermute | solution.py:423
  35.2 11.8 %collective-permute-start.7 = (bf16[256,1536]{1,0:T(8,128)(2,1)S(1)}, bf16[256,1536]{1,0:T(8,128)(2,1)S(1)}, u32[]{:S(2)}, u32[]{:S(2)}) collective-permute-start(bf16[256,1536]{1,0:T(8,128)(2,1)S(1)} %get-tuple-element.52), channel_id=1, source_target_pairs={{0,8},{1,9},{2,10},{3,11},{4,12},{5,13},{6,14},{7,15},{8,0},{9,1},... | collective-permute-start | bytes 2359304 | tf_op jit(solution)/shard_map/ppermute | solution.py:423
  36.5 11.4 %collective-permute-start.6 = (bf16[128,1536]{1,0:T(8,128)(2,1)S(1)}, bf16[128,1536]{1,0:T(8,128)(2,1)S(1)}, u32[]{:S(2)}, u32[]{:S(2)}) collective-permute-start(bf16[128,1536]{1,0:T(8,128)(2,1)S(1)} %get-tuple-element.50), channel_id=1, source_target_pairs={{0,16},{1,17},{2,18},{3,19},{4,20},{5,21},{6,22},{7,23},{8,24},{9,... | collective-permute-start | bytes 1179656 | tf_op jit(solution)/shard_map/ppermute | solution.py:423
  44.8 9.0 %collective-permute-start.5 = (bf16[608,256]{1,0:T(8,128)(2,1)S(1)}, bf16[608,256]{1,0:T(8,128)(2,1)S(1)}, u32[]{:S(2)}, u32[]{:S(2)}) collective-permute-start(bf16[608,256]{1,0:T(8,128)(2,1)S(1)} %collective-permute-done.3.refs_1_), channel_id=1, source_target_pairs={{0,6},{1,7},{2,0},{3,1},{4,2},{5,3},{6,4},{7,5},{8,14},{9,15},{10,... | collective-permute-start | bytes 933896 | tf_op jit(solution)/shard_map/ppermute | solution.py:423
  47.0 11.8 %collective-permute-start.11 = (bf16[256,1536]{1,0:T(8,128)(2,1)S(1)}, bf16[256,1536]{1,0:T(8,128)(2,1)S(1)}, u32[]{:S(2)}, u32[]{:S(2)}) collective-permute-start(bf16[256,1536]{1,0:T(8,128)(2,1)S(1)} %get-tuple-element.58), channel_id=1, source_target_pairs={{0,8},{1,9},{2,10},{3,11},{4,12},{5,13},{6,14},{7,15},{8,0},{9,1},... | collective-permute-start | bytes 2359304 | tf_op jit(solution)/shard_map/ppermute | solution.py:423
  47.9 16.1 %collective-permute-start.14 = (bf16[128,1536]{1,0:T(8,128)(2,1)S(1)}, bf16[128,1536]{1,0:T(8,128)(2,1)S(1)}, u32[]{:S(2)}, u32[]{:S(2)}) collective-permute-start(bf16[128,1536]{1,0:T(8,128)(2,1)S(1)} %get-tuple-element.62), channel_id=1, source_target_pairs={{0,16},{1,17},{2,18},{3,19},{4,20},{5,21},{6,22},{7,23},{8,24},{9,... | collective-permute-start | bytes 1179656 | tf_op jit(solution)/shard_map/ppermute | solution.py:423
  49.2 14.5 %collective-permute-start.10 = (bf16[128,768]{1,0:T(8,128)(2,1)S(1)}, bf16[128,768]{1,0:T(8,128)(2,1)S(1)}, u32[]{:S(2)}, u32[]{:S(2)}) collective-permute-start(bf16[128,768]{1,0:T(8,128)(2,1)S(1)} %act.4.refs_5_.refs_1_), channel_id=1, source_target_pairs={{0,16},{1,17},{2,18},{3,19},{4,20},{5,21},{6,22},{7,23},{8,24},{9,... | collective-permute-start | bytes 589832 | tf_op jit(solution)/shard_map/ppermute | solution.py:423
  58.6 12.5 %collective-permute-start.9 = (bf16[256,1536]{1,0:T(8,128)(2,1)S(1)}, bf16[256,1536]{1,0:T(8,128)(2,1)S(1)}, u32[]{:S(2)}, u32[]{:S(2)}) collective-permute-start(bf16[256,1536]{1,0:T(8,128)(2,1)S(1)} %get-tuple-element.57), channel_id=1, source_target_pairs={{0,8},{1,9},{2,10},{3,11},{4,12},{5,13},{6,14},{7,15},{8,0},{9,1},... | collective-permute-start | bytes 2359304 | tf_op jit(solution)/shard_map/ppermute | solution.py:423
  58.7 8.3 %copy-start.6 = (bf16[4,720,576]{1,2,0:T(8,128)(2,1)S(1)}, bf16[4,720,576]{1,2,0:T(8,128)(2,1)}, u32[]{:S(2)}) copy-start(bf16[4,720,576]{1,2,0:T(8,128)(2,1)} %param.18) | copy-start | bytes 9953284
  59.6 7.4 %collective-permute-start.12 = (bf16[128,768]{1,0:T(8,128)(2,1)S(1)}, bf16[128,768]{1,0:T(8,128)(2,1)S(1)}, u32[]{:S(2)}, u32[]{:S(2)}) collective-permute-start(bf16[128,768]{1,0:T(8,128)(2,1)S(1)} %act.4.refs_5_.refs_1_), channel_id=1, source_target_pairs={{0,8},{1,9},{2,10},{3,11},{4,12},{5,13},{6,14},{7,15},{8,0},{9,1},... | collective-permute-start | bytes 589832 | tf_op jit(solution)/shard_map/ppermute | solution.py:423
  63.7 3.3 %collective-permute-start.13 = (bf16[128,768]{1,0:T(8,128)(2,1)S(1)}, bf16[128,768]{1,0:T(8,128)(2,1)S(1)}, u32[]{:S(2)}, u32[]{:S(2)}) collective-permute-start(bf16[128,768]{1,0:T(8,128)(2,1)S(1)} %collective-permute-done.10.refs_2_), channel_id=1, source_target_pairs={{0,8},{1,9},{2,10},{3,11},{4,12},{5,13},{6,14},{7,15},{8,0},{9,1},... | collective-permute-start | bytes 589832 | tf_op jit(solution)/shard_map/ppermute | solution.py:423
  63.7 11.9 %collective-permute-start.16 = (bf16[128,1536]{1,0:T(8,128)(2,1)S(1)}, bf16[128,1536]{1,0:T(8,128)(2,1)S(1)}, u32[]{:S(2)}, u32[]{:S(2)}) collective-permute-start(bf16[128,1536]{1,0:T(8,128)(2,1)S(1)} %get-tuple-element.67), channel_id=1, source_target_pairs={{0,16},{1,17},{2,18},{3,19},{4,20},{5,21},{6,22},{7,23},{8,24},{9,... | collective-permute-start | bytes 1179656 | tf_op jit(solution)/shard_map/ppermute | solution.py:423
  65.2 14.6 %collective-permute-start.20 = (bf16[128,768]{1,0:T(8,128)(2,1)S(1)}, bf16[128,768]{1,0:T(8,128)(2,1)S(1)}, u32[]{:S(2)}, u32[]{:S(2)}) collective-permute-start(bf16[128,768]{1,0:T(8,128)(2,1)S(1)} %act.5.refs_7_.refs_1_), channel_id=1, source_target_pairs={{0,16},{1,17},{2,18},{3,19},{4,20},{5,21},{6,22},{7,23},{8,24},{9,... | collective-permute-start | bytes 589832 | tf_op jit(solution)/shard_map/ppermute | solution.py:423
  70.5 9.3 %collective-permute-start.27 = (bf16[288,256]{1,0:T(8,128)(2,1)S(1)}, bf16[288,256]{1,0:T(8,128)(2,1)S(1)}, u32[]{:S(2)}, u32[]{:S(2)}) collective-permute-start(bf16[288,256]{1,0:T(8,128)(2,1)S(1)} %get-tuple-element.75), channel_id=1, source_target_pairs={{0,1},{1,0},{2,3},{3,2},{4,5},{5,4},{6,7},{7,6},{8,9},{9,8},{10,11... | collective-permute-start | bytes 442376 | tf_op jit(solution)/shard_map/ppermute | solution.py:423
  76.8 6.8 %collective-permute-start.17 = (bf16[128,768]{1,0:T(8,128)(2,1)S(1)}, bf16[128,768]{1,0:T(8,128)(2,1)S(1)}, u32[]{:S(2)}, u32[]{:S(2)}) collective-permute-start(bf16[128,768]{1,0:T(8,128)(2,1)S(1)} %act.6.refs_7_.refs_1_), channel_id=1, source_target_pairs={{0,16},{1,17},{2,18},{3,19},{4,20},{5,21},{6,22},{7,23},{8,24},{9,... | collective-permute-start | bytes 589832 | tf_op jit(solution)/shard_map/ppermute | solution.py:423
  77.2 6.7 %collective-permute-start.21 = (bf16[128,768]{1,0:T(8,128)(2,1)S(1)}, bf16[128,768]{1,0:T(8,128)(2,1)S(1)}, u32[]{:S(2)}, u32[]{:S(2)}) collective-permute-start(bf16[128,768]{1,0:T(8,128)(2,1)S(1)} %act.5.refs_7_.refs_1_), channel_id=1, source_target_pairs={{0,8},{1,9},{2,10},{3,11},{4,12},{5,13},{6,14},{7,15},{8,0},{9,1},... | collective-permute-start | bytes 589832 | tf_op jit(solution)/shard_map/ppermute | solution.py:423
  79.8 4.1 %collective-permute-start.22 = (bf16[128,768]{1,0:T(8,128)(2,1)S(1)}, bf16[128,768]{1,0:T(8,128)(2,1)S(1)}, u32[]{:S(2)}, u32[]{:S(2)}) collective-permute-start(bf16[128,768]{1,0:T(8,128)(2,1)S(1)} %collective-permute-done.20.refs_2_), channel_id=1, source_target_pairs={{0,8},{1,9},{2,10},{3,11},{4,12},{5,13},{6,14},{7,15},{8,0},{9,1},... | collective-permute-start | bytes 589832 | tf_op jit(solution)/shard_map/ppermute | solution.py:423
  79.8 34.7 %collective-permute-start.28 = (bf16[288,256]{1,0:T(8,128)(2,1)S(1)}, bf16[288,256]{1,0:T(8,128)(2,1)S(1)}, u32[]{:S(2)}, u32[]{:S(2)}) collective-permute-start(bf16[288,256]{1,0:T(8,128)(2,1)S(1)} %add_convert_fusion.2), channel_id=1, source_target_pairs={{0,2},{1,3},{2,4},{3,5},{4,6},{5,7},{6,0},{7,1},{8,10},{9,11},{10,... | collective-permute-start | bytes 442376 | tf_op jit(solution)/shard_map/ppermute | solution.py:423
  80.1 8.0 %collective-permute-start.18 = (bf16[128,768]{1,0:T(8,128)(2,1)S(1)}, bf16[128,768]{1,0:T(8,128)(2,1)S(1)}, u32[]{:S(2)}, u32[]{:S(2)}) collective-permute-start(bf16[128,768]{1,0:T(8,128)(2,1)S(1)} %act.6.refs_7_.refs_1_), channel_id=1, source_target_pairs={{0,8},{1,9},{2,10},{3,11},{4,12},{5,13},{6,14},{7,15},{8,0},{9,1},... | collective-permute-start | bytes 589832 | tf_op jit(solution)/shard_map/ppermute | solution.py:423
  83.6 10.0 %collective-permute-start.15 = (bf16[128,1536]{1,0:T(8,128)(2,1)S(1)}, bf16[128,1536]{1,0:T(8,128)(2,1)S(1)}, u32[]{:S(2)}, u32[]{:S(2)}) collective-permute-start(bf16[128,1536]{1,0:T(8,128)(2,1)S(1)} %get-tuple-element.66), channel_id=1, source_target_pairs={{0,16},{1,17},{2,18},{3,19},{4,20},{5,21},{6,22},{7,23},{8,24},{9,... | collective-permute-start | bytes 1179656 | tf_op jit(solution)/shard_map/ppermute | solution.py:423
  83.9 4.1 %collective-permute-start.19 = (bf16[128,768]{1,0:T(8,128)(2,1)S(1)}, bf16[128,768]{1,0:T(8,128)(2,1)S(1)}, u32[]{:S(2)}, u32[]{:S(2)}) collective-permute-start(bf16[128,768]{1,0:T(8,128)(2,1)S(1)} %collective-permute-done.17.refs_2_), channel_id=1, source_target_pairs={{0,8},{1,9},{2,10},{3,11},{4,12},{5,13},{6,14},{7,15},{8,0},{9,1},... | collective-permute-start | bytes 589832 | tf_op jit(solution)/shard_map/ppermute | solution.py:423
  87.4 8.6 %collective-permute-start.29 = (bf16[288,256]{1,0:T(8,128)(2,1)S(1)}, bf16[288,256]{1,0:T(8,128)(2,1)S(1)}, u32[]{:S(2)}, u32[]{:S(2)}) collective-permute-start(bf16[288,256]{1,0:T(8,128)(2,1)S(1)} %get-tuple-element.76), channel_id=1, source_target_pairs={{0,1},{1,0},{2,3},{3,2},{4,5},{5,4},{6,7},{7,6},{8,9},{9,8},{10,11... | collective-permute-start | bytes 442376 | tf_op jit(solution)/shard_map/ppermute | solution.py:423
  94.9 5.7 %collective-permute-start.23 = (bf16[128,768]{1,0:T(8,128)(2,1)S(1)}, bf16[128,768]{1,0:T(8,128)(2,1)S(1)}, u32[]{:S(2)}, u32[]{:S(2)}) collective-permute-start(bf16[128,768]{1,0:T(8,128)(2,1)S(1)} %act.7.refs_1_.refs_7_), channel_id=1, source_target_pairs={{0,16},{1,17},{2,18},{3,19},{4,20},{5,21},{6,22},{7,23},{8,24},{9,... | collective-permute-start | bytes 589832 | tf_op jit(solution)/shard_map/ppermute | solution.py:423
  95.2 5.4 %collective-permute-start.31 = (bf16[288,256]{1,0:T(8,128)(2,1)S(1)}, bf16[288,256]{1,0:T(8,128)(2,1)S(1)}, u32[]{:S(2)}, u32[]{:S(2)}) collective-permute-start(bf16[288,256]{1,0:T(8,128)(2,1)S(1)} %get-tuple-element.77), channel_id=1, source_target_pairs={{0,1},{1,0},{2,3},{3,2},{4,5},{5,4},{6,7},{7,6},{8,9},{9,8},{10,11... | collective-permute-start | bytes 442376 | tf_op jit(solution)/shard_map/ppermute | solution.py:423
  96.1 18.4 %collective-permute-start.30 = (bf16[288,256]{1,0:T(8,128)(2,1)S(1)}, bf16[288,256]{1,0:T(8,128)(2,1)S(1)}, u32[]{:S(2)}, u32[]{:S(2)}) collective-permute-start(bf16[288,256]{1,0:T(8,128)(2,1)S(1)} %add_convert_fusion.1), channel_id=1, source_target_pairs={{0,4},{1,5},{2,6},{3,7},{4,0},{5,1},{6,2},{7,3},{8,12},{9,13},{10,... | collective-permute-start | bytes 442376 | tf_op jit(solution)/shard_map/ppermute | solution.py:423
  96.1 6.9 %collective-permute-start.24 = (bf16[128,768]{1,0:T(8,128)(2,1)S(1)}, bf16[128,768]{1,0:T(8,128)(2,1)S(1)}, u32[]{:S(2)}, u32[]{:S(2)}) collective-permute-start(bf16[128,768]{1,0:T(8,128)(2,1)S(1)} %act.7.refs_1_.refs_7_), channel_id=1, source_target_pairs={{0,8},{1,9},{2,10},{3,11},{4,12},{5,13},{6,14},{7,15},{8,0},{9,1},... | collective-permute-start | bytes 589832 | tf_op jit(solution)/shard_map/ppermute | solution.py:423
  100.6 2.4 %collective-permute-start.25 = (bf16[128,768]{1,0:T(8,128)(2,1)S(1)}, bf16[128,768]{1,0:T(8,128)(2,1)S(1)}, u32[]{:S(2)}, u32[]{:S(2)}) collective-permute-start(bf16[128,768]{1,0:T(8,128)(2,1)S(1)} %collective-permute-done.23.refs_2_), channel_id=1, source_target_pairs={{0,8},{1,9},{2,10},{3,11},{4,12},{5,13},{6,14},{7,15},{8,0},{9,1},... | collective-permute-start | bytes 589832 | tf_op jit(solution)/shard_map/ppermute | solution.py:423
  100.7 6.5 %copy-start.10 = (f32[4,288]{1,0:T(4,128)S(1)}, f32[4,288]{1,0:T(4,128)}, u32[]{:S(2)}) copy-start(f32[4,288]{1,0:T(4,128)} %get-tuple-element.55) | copy-start | bytes 13828
  100.7 22.2 %copy-start.8 = (f32[2304]{0:T(1024)S(1)}, f32[2304]{0:T(1024)}, u32[]{:S(2)}) copy-start(f32[2304]{0:T(1024)} %param.19) | copy-start | bytes 27652
  100.7 22.3 %copy-start.9 = (f32[16]{0:T(128)S(1)}, f32[16]{0:T(128)}, u32[]{:S(2)}) copy-start(f32[16]{0:T(128)} %param.21) | copy-start | bytes 196
  100.7 13.8 %collective-permute-start.32 = (bf16[288,256]{1,0:T(8,128)(2,1)S(1)}, bf16[288,256]{1,0:T(8,128)(2,1)S(1)}, u32[]{:S(2)}, u32[]{:S(2)}) collective-permute-start(bf16[288,256]{1,0:T(8,128)(2,1)S(1)} %add_convert_fusion), channel_id=1, source_target_pairs={{0,6},{1,7},{2,0},{3,1},{4,2},{5,3},{6,4},{7,5},{8,14},{9,15},{10,... | collective-permute-start | bytes 442376 | tf_op jit(solution)/shard_map/ppermute | solution.py:423
  103.0 23.3 %copy-start.1 = (bf16[2304,512]{1,0:T(8,128)(2,1)S(1)}, bf16[2304,512]{1,0:T(8,128)(2,1)}, u32[]{:S(2)}) copy-start(bf16[2304,512]{1,0:T(8,128)(2,1)} %refs_2_.1) | copy-start | bytes 7077892
  106.5 29.3 %copy-start.7 = (f32[256,288]{0,1:T(8,128)S(1)}, f32[256,288]{0,1:T(8,128)}, u32[]{:S(2)}) copy-start(f32[256,288]{0,1:T(8,128)} %param.11) | copy-start | bytes 884740
  106.5 8.0 %collective-permute-start.26 = (bf16[288,256]{1,0:T(8,128)(2,1)S(1)}, bf16[288,256]{1,0:T(8,128)(2,1)S(1)}, u32[]{:S(2)}, u32[]{:S(2)}) collective-permute-start(bf16[288,256]{1,0:T(8,128)(2,1)S(1)} %get-tuple-element.74), channel_id=1, source_target_pairs={{0,1},{1,0},{2,3},{3,2},{4,5},{5,4},{6,7},{7,6},{8,9},{9,8},{10,11... | collective-permute-start | bytes 442376 | tf_op jit(solution)/shard_map/ppermute | solution.py:423
  107.2 7.3 %collective-permute-start.8 = (f32[4,288]{1,0:T(4,128)S(1)}, f32[4,288]{1,0:T(4,128)S(1)}, u32[]{:S(2)}, u32[]{:S(2)}) collective-permute-start(f32[4,288]{1,0:T(4,128)S(1)} %copy-done.10), channel_id=1, source_target_pairs={{0,0},{1,1},{2,8},{3,9},{4,16},{5,17},{6,24},{7,25},{8,2},{9,3},{1... | collective-permute-start | bytes 13832 | tf_op jit(solution)/shard_map/ppermute | solution.py:423
  115.6 10.7 %all-to-all-start = ((f32[32,4,288]{2,1,0:T(4,128)}), f32[32,4,288]{2,1,0:T(4,128)S(1)}, u32[]{:S(2)}, u32[]{:S(2)}) async-start(f32[32,4,288]{2,1,0:T(4,128)} %get-tuple-element.78), calls=%async_computation | async-start | bytes 393216 | tf_op jit(solution)/shard_map/all_to_all | solution.py:516
  118.6 14.0 %collective-permute-start.33 = (bf16[288,256]{1,0:T(8,128)(2,1)S(1)}, bf16[288,256]{1,0:T(8,128)(2,1)S(1)}, u32[]{:S(2)}, u32[]{:S(2)}) collective-permute-start(bf16[288,256]{1,0:T(8,128)(2,1)S(1)} %get-tuple-element.80), channel_id=1, source_target_pairs={{0,0},{1,1},{2,8},{3,9},{4,16},{5,17},{6,24},{7,25},{8,2},{9,3},{1... | collective-permute-start | bytes 442376 | tf_op jit(solution)/shard_map/ppermute | solution.py:423
  132.6 9.3 %all-to-all-start.1 = ((f32[32,2,16]{2,1,0:T(2,128)}), f32[32,2,16]{2,1,0:T(2,128)S(1)}, u32[]{:S(2)}, u32[]{:S(2)}) async-start(f32[32,2,16]{2,1,0:T(2,128)} %get-tuple-element.83), calls=%async_computation.1 | async-start | bytes 65536 | tf_op jit(solution)/shard_map/all_to_all | solution.py:516
